TPU v7x, 32 devices: a whole 2x2x4 slice. The times are simulated.
32 devices in a mesh: parts: 2 (over y), tensor: 4 (over z), dp: 4 (over x, core).
Axes of the slice: x: 2, y: 2, z: 4, core: 2. Of those that a mesh axis runs over, the one named last changes fastest.
Arguments:
- train_input: bfloat16 [32, 64, 8192], P(('parts', 'dp'), None, 'tensor'), parts along dimension 0, may hold values from -6 to 6
- train_gate: bfloat16 [32, 64, 14336], P(('parts', 'dp'), None, 'tensor'), parts along dimension 0, may hold values from -6 to 6
- train_up: bfloat16 [32, 64, 14336], P(('parts', 'dp'), None, 'tensor'), parts along dimension 0, may hold values from -6 to 6
- train_outgrad: bfloat16 [32, 64, 8192], P(('parts', 'dp'), None, 'tensor'), parts along dimension 0, may hold values from -6 to 6
- train_lengths: int32 [32], P(('parts', 'dp')), parts along dimension 0, may hold values from 16 to 64, as said below
- query_input: bfloat16 [16, 64, 8192], P(('parts', 'dp'), None, 'tensor'), parts along dimension 0, may hold values from -6 to 6
- query_gate: bfloat16 [16, 64, 14336], P(('parts', 'dp'), None, 'tensor'), parts along dimension 0, may hold values from -6 to 6
- query_up: bfloat16 [16, 64, 14336], P(('parts', 'dp'), None, 'tensor'), parts along dimension 0, may hold values from -6 to 6
- query_outgrad: bfloat16 [16, 64, 8192], P(('parts', 'dp'), None, 'tensor'), parts along dimension 0, may hold values from -6 to 6
- query_lengths: int32 [16], P(('parts', 'dp')), parts along dimension 0, may hold values from 16 to 64, as said below
- down_weight: bfloat16 [14336, 8192], P('tensor', 'dp'), may hold values from -0.0625 to 0.0625
- proj_input: bfloat16 [64, 8192], P(None, 'tensor'), may hold values from -0.0625 to 0.0625
- proj_outgrad: bfloat16 [64, 8192], P(None, 'tensor'), may hold values from -0.0625 to 0.0625
- proj_hidden: bfloat16 [64, 14336], P(None, 'tensor'), may hold values from -0.046875 to 0.046875
- proj_gate: bfloat16 [64, 14336], P(None, 'tensor'), may hold values from -0.046875 to 0.046875
- proj_up: bfloat16 [64, 14336], P(None, 'tensor'), may hold values from -0.046875 to 0.046875
Outputs:
- scores: float32 [32, 8], P(('parts', 'dp')), parts along dimension 0
There are 2 independent parts, one for each index of `parts`. A program takes and returns all parts, laid end to end along the dimension named above; an argument that names none is the same for every part. Nothing has to cross between parts.
Inputs may be any that keep to these rules, and one draw needn't show every extreme that they name: `train_lengths`: positions from an example's length on are padding; some example has exactly 64 real tokens and some exactly 16. `query_lengths`: positions from an example's length on are padding; some example has exactly 64 real tokens and some exactly 16.
All inputs are finite; a program needn't handle non-finite values.
Results may differ from a plain program's by a relative error of at most 0.0041.
Values may be sent and summed in bfloat16 or wider, within the bound.
No kernel may reach another device: no remote copies, remote signals or barrier semaphores. Data moves between devices by JAX's collectives and lax.ppermute only.
A program may use at most 192 MiB of HBM per device.

v0:
```python
import jax
import jax.numpy as jnp
from jax import lax
from jax.sharding import PartitionSpec as P

RANK = 64
SEQ = 64


def flatten(array):
    return array.reshape(-1, array.shape[-1])


def project(rows, table):
    return lax.dot_general(
        rows, table, (((1,), (1,)), ((), ())), preferred_element_type=jnp.float32
    )


def inner(left_side, right_side):
    return lax.dot_general(
        left_side,
        right_side,
        (((1,), (1,)), ((), ())),
        precision=lax.Precision.HIGHEST,
        preferred_element_type=jnp.float32,
    )


def local_terms(inputs, gate, up, outgrad, hidden_grad, tables):
    proj_input, proj_outgrad, proj_hidden, proj_gate, proj_up = tables
    gate_wide = flatten(gate).astype(jnp.float32)
    up_wide = flatten(up).astype(jnp.float32)
    sigmoid_gate = jax.nn.sigmoid(gate_wide)
    silu_gate = gate_wide * sigmoid_gate
    hidden = (silu_gate * up_wide).astype(jnp.bfloat16)
    gate_grad = (
        hidden_grad * up_wide * sigmoid_gate * (1.0 + gate_wide * (1.0 - sigmoid_gate))
    ).astype(jnp.bfloat16)
    up_grad = (hidden_grad * silu_gate).astype(jnp.bfloat16)
    return (
        project(flatten(inputs), proj_input),
        project(hidden, proj_hidden),
        project(gate_grad, proj_gate),
        project(up_grad, proj_up),
        project(flatten(outgrad), proj_outgrad),
    )


def outer_sums(left_side, right_side, lengths):
    number = lengths.shape[0]
    length = left_side.shape[0] // number
    positions = lax.broadcasted_iota(jnp.int32, (number, length), 1)
    weights = (positions < lengths[:, None]).astype(jnp.float32)
    left_rows = left_side.reshape(number, length, left_side.shape[1]) * weights[:, :, None]
    right_rows = right_side.reshape(number, length, right_side.shape[1])
    summed = jnp.einsum("est,esu->etu", left_rows, right_rows, precision=lax.Precision.HIGHEST)
    return summed.reshape(number, -1)


def features(terms, lengths):
    in_side, hidden_side, gate_side, up_side, out_side = terms
    return jnp.concatenate(
        [
            outer_sums(in_side, gate_side, lengths),
            outer_sums(in_side, up_side, lengths),
            outer_sums(hidden_side, out_side, lengths),
        ],
        axis=1,
    )


def score_rows(train_features, piece):
    return inner(train_features, piece)


def per_device(
    train_input,
    train_gate,
    train_up,
    train_outgrad,
    train_lengths,
    query_input,
    query_gate,
    query_up,
    query_outgrad,
    query_lengths,
    down_weight,
    proj_input,
    proj_outgrad,
    proj_hidden,
    proj_gate,
    proj_up,
):
    train_rows, query_rows = (
        lax.all_gather(flatten(train_outgrad), "tensor", axis=1, tiled=True),
        lax.all_gather(flatten(query_outgrad), "tensor", axis=1, tiled=True),
    )
    piece = lax.all_gather(down_weight, "dp", axis=1, tiled=True)
    train_hidden_grad = project(train_rows, piece)
    query_hidden_grad = project(query_rows, piece)
    tables = (proj_input, proj_outgrad, proj_hidden, proj_gate, proj_up)
    train_terms = local_terms(
        train_input, train_gate, train_up, train_outgrad, train_hidden_grad, tables
    )
    query_terms = local_terms(
        query_input, query_gate, query_up, query_outgrad, query_hidden_grad, tables
    )
    summed = lax.psum(
        (
            train_terms[0],
            train_terms[1],
            train_terms[2],
            train_terms[3],
            train_terms[4],
            query_terms[0],
            query_terms[1],
            query_terms[2],
            query_terms[3],
            query_terms[4],
        ),
        "tensor",
    )
    train_features = features(summed[0:5], train_lengths)
    query_features = features(summed[5:10], query_lengths)
    scores = score_rows(train_features, lax.all_gather(query_features, "dp", axis=0, tiled=True))
    return scores / (RANK * SEQ)


def solution(mesh):
    in_specs = (
        P(("parts", "dp"), None, "tensor"),
        P(("parts", "dp"), None, "tensor"),
        P(("parts", "dp"), None, "tensor"),
        P(("parts", "dp"), None, "tensor"),
        P(("parts", "dp")),
        P(("parts", "dp"), None, "tensor"),
        P(("parts", "dp"), None, "tensor"),
        P(("parts", "dp"), None, "tensor"),
        P(("parts", "dp"), None, "tensor"),
        P(("parts", "dp")),
        P("tensor", "dp"),
        P(None, "tensor"),
        P(None, "tensor"),
        P(None, "tensor"),
        P(None, "tensor"),
        P(None, "tensor"),
    )
    out_specs = P(("parts", "dp"), None)
    return jax.shard_map(
        per_device, mesh=mesh, in_specs=in_specs, out_specs=out_specs, check_vma=False
    )
```

profile of v0, /device:TPU:0, one launch (start us, length us, event | category | flops | bytes accessed | tf_op | source)
XLA Modules:
  0.0 614.0 jit_solution(15299908137161887823)
XLA Ops:
  6.5 0.7 all-gather.9.cloned.1.call-update
  7.3 0.7 all-gather.7.cloned.1.call-update
  8.1 0.7 all-gather.5.cloned.1.call-update
  8.8 0.0 all-reduce.5.cloned.1.call-start
  8.9 1.4 fusion.50
  10.3 0.1 reshape.127
  10.4 0.6 copy.32
  11.0 0.4 fusion.47
  11.5 0.1 reshape.117
  11.6 0.7 copy.27
  12.2 0.1 compare_convert_fusion
  12.3 0.1 fusion.45
  12.4 0.9 fusion.52
  13.3 1.1 fusion.49
  14.4 43.2 %all-gather.9.cloned.1.call-done = bf16[128,8192]{1,0:T(8,128)(2,1)} async-done(((bf16[128,2048]{1,0:T(8,128)(2,1)}), bf16[128,8192]{1,0:T(8,128)(2,1)}) %all-gather.9.cloned.1.call-update) | async-done | bytes 2097168 | tf_op jit(solution)/shard_map/all_gather | solution.py:97
  57.6 346.3 %all-gather.7.cloned.1.call-done = bf16[3584,8192]{1,0:T(8,128)(2,1)} async-done(((bf16[3584,2048]{1,0:T(8,128)(2,1)}), bf16[3584,8192]{1,0:T(8,128)(2,1)}) %all-gather.7.cloned.1.call-update) | async-done | bytes 58720272 | tf_op jit(solution)/shard_map/all_gather | solution.py:99
  403.9 28.8 %fusion.10 = (bf16[128,3584]{1,0:T(8,128)(2,1)}, f32[128,3584]{1,0:T(8,128)S(1)}, f32[128,3584]{1,0:T(8,128)}) fusion(bf16[2,64,3584]{2,1,0:T(8,128)(2,1)} %param.23, bf16[2,64,3584]{2,1,0:T(8,128)(2,1)} %param.22, bf16[128,8192]{1,0:T(8,128)(2,1)} %all-gather.9.cloned.1.call-done, bf16[3584,8192]{1,0:T(8,128)(2,1)} %all-gather.7.cloned.1.call-done), kind=kOutput, calls=%fused_computation.21 | convolution fusion | flops 7522156544 | bytes 67239936 | tf_op jit(solution)/shard_map/dot_general | solution.py:15
  432.8 1.7 fusion.20
  434.5 0.1 reshape.133
  434.6 0.6 copy.35
  435.2 2.5 fusion.19
  437.7 48.6 %all-gather.5.cloned.1.call-done = bf16[256,8192]{1,0:T(8,128)(2,1)} async-done(((bf16[256,2048]{1,0:T(8,128)(2,1)}), bf16[256,8192]{1,0:T(8,128)(2,1)}) %all-gather.5.cloned.1.call-update) | async-done | bytes 4194320 | tf_op jit(solution)/shard_map/all_gather | solution.py:96
  486.3 27.9 %fusion.2 = (bf16[256,3584]{1,0:T(8,128)(2,1)S(1)}, f32[256,3584]{1,0:T(8,128)}, f32[256,3584]{1,0:T(8,128)}) fusion(bf16[4,64,3584]{2,1,0:T(8,128)(2,1)} %param.18, bf16[4,64,3584]{2,1,0:T(8,128)(2,1)} %param.17, bf16[256,8192]{1,0:T(8,128)(2,1)} %all-gather.5.cloned.1.call-done, bf16[3584,8192]{1,0:T(8,128)(2,1)} %all-gather.7.cloned.1.call-done), kind=kOutput, calls=%fused_computation.7 | convolution fusion | flops 15044313088 | bytes 75759616 | tf_op jit(solution)/shard_map/dot_general | solution.py:15
  514.2 4.6 fusion.16
  518.8 0.2 copy-done.7
  519.0 0.7 fusion.17
  519.6 0.1 reshape.123
  519.8 0.7 copy.30
  520.4 2.2 fusion.51
  522.6 0.0 all-reduce.7.cloned.1.call-start
  522.7 1.3 fusion.48
  524.0 33.9 %all-reduce.5.cloned.1.call-done = (f32[2,64,64]{2,1,0:T(8,128)}, f32[2,64,64]{1,2,0:T(8,128)}, f32[2,64,64]{2,1,0:T(8,128)}, f32[2,64,64]{1,2,0:T(8,128)}, f32[2,64,64]{2,1,0:T(8,128)}) async-done(((f32[2,64,64]{2,1,0:T(8,128)}, f32[2,64,64]{1,2,0:T(8,128)}, f32[2,64,64]{2,1,0:T(8,128)}, f32[2,64,64]{1,2,0:T(8,128)}, f32[2,64,64]{2,1,0:T(8,128)}), (f32[2,64,64]{2,1,0:T(8,128)}, f32[2,64,64]{1,2,0:T(8,128)}, ...) | async-done | bytes 163856 | tf_op jit(solution)/shard_map/psum | solution.py:109
  557.9 1.1 fusion.40
  559.0 0.1 reshape.130
  559.1 1.1 fusion.38
  560.2 0.1 reshape.132
  560.3 1.1 fusion.33
  561.4 0.1 reshape.135
  561.6 6.4 %all-gather = f32[4,2,12288]{2,1,0:T(2,128)S(1)} all-gather(f32[1,2,12288]{2,1,0:T(2,128)S(1)} %maximum_bitcast_fusion), channel_id=1, replica_groups=mesh['parts'=2,'tensor'=4,'dp'=4] {'dp'}, dimensions={0}, use_global_device_ids=true | all-gather | bytes 491520 | tf_op jit(solution)/shard_map/all_gather | solution.py:126
  568.0 0.3 reshape.141
  568.3 33.6 %all-reduce.7.cloned.1.call-done = (f32[4,64,64]{2,1,0:T(8,128)}, f32[4,64,64]{1,2,0:T(8,128)}, f32[4,64,64]{2,1,0:T(8,128)}, f32[4,64,64]{1,2,0:T(8,128)}, f32[4,64,64]{2,1,0:T(8,128)}) async-done(((f32[4,64,64]{2,1,0:T(8,128)}, f32[4,64,64]{1,2,0:T(8,128)}, f32[4,64,64]{2,1,0:T(8,128)}, f32[4,64,64]{1,2,0:T(8,128)}, f32[4,64,64]{2,1,0:T(8,128)}), (f32[4,64,64]{2,1,0:T(8,128)}, f32[4,64,64]{1,2,0:T(8,128)}, ...) | async-done | bytes 327696 | tf_op jit(solution)/shard_map/psum | solution.py:109
  601.9 1.2 fusion.31
  603.1 0.1 reshape.120
  603.3 1.2 fusion.29
  604.5 0.1 reshape.122
  604.6 1.2 fusion.27
  605.8 0.1 reshape.125
  605.9 1.5 convolution_multiply_fusion
  (31 shorter events, 0.2 us)
Async XLA Ops:
  6.5 4.5 copy-start
  6.5 51.1 %all-gather.9.cloned.1.call-start = ((), (), s32[]{:S(2)}) async-start(), calls=%async_computation.2 | async-start | bytes 2621440 | tf_op jit(solution)/shard_map/all_gather | solution.py:97
  7.3 1.6 copy-start.9
  7.3 396.7 %all-gather.7.cloned.1.call-start = ((), (), s32[]{:S(2)}) async-start(), calls=%async_computation.1 | async-start | bytes 73400320 | tf_op jit(solution)/shard_map/all_gather | solution.py:99
  8.0 4.2 copy-start.12
  8.0 4.3 copy-start.11
  8.0 4.4 copy-start.4
  8.0 4.3 copy-start.10
  8.1 478.3 %all-gather.5.cloned.1.call-start = ((), (), s32[]{:S(2)}) async-start(), calls=%async_computation | async-start | bytes 5242880 | tf_op jit(solution)/shard_map/all_gather | solution.py:96
  8.8 4.5 copy-start.3
  8.8 549.1 %all-reduce.5.cloned.1.call-start = ((), (), s32[]{:S(2)}) async-start(), calls=%async_computation.3 | async-start | bytes 655360 | tf_op jit(solution)/shard_map/psum | solution.py:109
  14.4 418.4 %copy-start.5 = (bf16[64,3584]{1,0:T(8,128)(2,1)S(1)}, bf16[64,3584]{1,0:T(8,128)(2,1)}, u32[]{:S(2)}) copy-start(bf16[64,3584]{1,0:T(8,128)(2,1)} %param.29) | copy-start | bytes 1376260
  432.8 2.4 copy-start.8
  514.2 4.6 copy-start.2
  514.2 4.8 copy-start.7
  518.9 1.5 copy-start.6
  522.6 79.3 %all-reduce.7.cloned.1.call-start = ((), (), s32[]{:S(2)}) async-start(), calls=%async_computation.4 | async-start | bytes 1310720 | tf_op jit(solution)/shard_map/psum | solution.py:109
  560.2 47.3 %copy-start.1 = (bf16[4,64,2048]{2,1,0:T(8,128)(2,1)S(1)}, bf16[4,64,2048]{2,1,0:T(8,128)(2,1)}, u32[]{:S(2)}) copy-start(bf16[4,64,2048]{2,1,0:T(8,128)(2,1)} %param.16) | copy-start | bytes 3145732
Sparse Core Ops, SparseCore 0:
  8.9 48.6 all-gather.8
  59.2 344.7 all-gather.6
  405.5 80.7 all-gather.4
  522.8 35.1 all-reduce.4
  560.5 41.3 all-reduce.6
where the time goes:
time: 614 us
  waiting for transfers between devices  508 us (83%)
  matrix products  81.9 us (13%)
  between operations  13.3 us (2%)
  blocking collectives  6.44 us (1%)
    all_gather x1, waiting for transfers between devices, per_device(): piece = lax.all_gather(down_weight, 'dp', axis=1, tiled=True)  346 us
    psum x2, waiting for transfers between devices, per_device(): lax.psum((train_terms[0], train_terms[1], train_terms[2], train_terms[3],...  67.6 us
    dot_general x6, matrix products, project(): lax.dot_general(rows, table, (((1,), (1,)), ((), ())), preferred_element_...  60.9 us
    all_gather x1, waiting for transfers between devices, per_device(): lax.all_gather(flatten(train_outgrad), 'tensor', axis=1, tiled=True)  48.6 us
    all_gather x1, waiting for transfers between devices, per_device(): lax.all_gather(flatten(query_outgrad), 'tensor', axis=1, tiled=True)  43.2 us
    reshape x6, matrix products, outer_sums(): right_rows = right_side.reshape(number, length, right_side.shape[1])  12.6 us
  transfers between devices with their start and end apart: 5, of which 5 were waited for; matrix products, arithmetic and copies ran while one was open for 7% of the time, Pallas kernels for 0%

commit v1 on v0

v1 whole, which is shorter than its diff:
```python
import jax
import jax.numpy as jnp
from jax import lax
from jax.sharding import PartitionSpec as P

RANK = 64
SEQ = 64


def flatten(array):
    return array.reshape(-1, array.shape[-1])


def project(rows, table):
    return lax.dot_general(
        rows, table, (((1,), (1,)), ((), ())), preferred_element_type=jnp.float32
    )


def inner(left_side, right_side):
    return lax.dot_general(
        left_side,
        right_side,
        (((1,), (1,)), ((), ())),
        precision=lax.Precision.HIGHEST,
        preferred_element_type=jnp.float32,
    )


def gated_hidden(gate, up):
    gate_wide = gate.astype(jnp.float32)
    up_wide = up.astype(jnp.float32)
    return (gate_wide * jax.nn.sigmoid(gate_wide) * up_wide).astype(jnp.bfloat16)


def gradient_sides(gate, up, hidden_grad, proj_gate, proj_up):
    gate_wide = gate.astype(jnp.float32)
    up_wide = up.astype(jnp.float32)
    sigmoid_gate = jax.nn.sigmoid(gate_wide)
    silu_gate = gate_wide * sigmoid_gate
    gate_grad = (
        hidden_grad * up_wide * sigmoid_gate * (1.0 + gate_wide * (1.0 - sigmoid_gate))
    ).astype(jnp.bfloat16)
    up_grad = (hidden_grad * silu_gate).astype(jnp.bfloat16)
    return project(gate_grad, proj_gate), project(up_grad, proj_up)


def outer_sums(left_side, right_side, lengths):
    number = lengths.shape[0]
    length = left_side.shape[0] // number
    positions = lax.broadcasted_iota(jnp.int32, (number, length), 1)
    weights = (positions < lengths[:, None]).astype(jnp.float32)
    left_rows = left_side.reshape(number, length, left_side.shape[1]) * weights[:, :, None]
    right_rows = right_side.reshape(number, length, right_side.shape[1])
    summed = jnp.einsum("est,esu->etu", left_rows, right_rows, precision=lax.Precision.HIGHEST)
    return summed.reshape(number, -1)


def features(in_side, hidden_side, gate_side, up_side, out_side, lengths):
    return jnp.concatenate(
        [
            outer_sums(in_side, gate_side, lengths),
            outer_sums(in_side, up_side, lengths),
            outer_sums(hidden_side, out_side, lengths),
        ],
        axis=1,
    )


def gathering_plan(
    train_input,
    train_gate,
    train_up,
    train_outgrad,
    train_lengths,
    query_input,
    query_gate,
    query_up,
    query_outgrad,
    query_lengths,
    down_weight,
    proj_input,
    proj_outgrad,
    proj_hidden,
    proj_gate,
    proj_up,
):
    weight = lax.all_gather(down_weight, "dp", axis=1, tiled=True)

    def full_features(inputs, gate, up, outgrad, lengths):
        inputs, gate, up, outgrad = [flatten(a) for a in (inputs, gate, up, outgrad)]
        rows = lax.all_gather(outgrad, "tensor", axis=1, tiled=True)
        gate_side, up_side = gradient_sides(gate, up, project(rows, weight), proj_gate, proj_up)
        hidden_side = project(gated_hidden(gate, up), proj_hidden)
        sides = (
            project(inputs, proj_input),
            hidden_side,
            gate_side,
            up_side,
            project(outgrad, proj_outgrad),
        )
        return features(*lax.psum(sides, "tensor"), lengths)

    train_features = full_features(
        train_input, train_gate, train_up, train_outgrad, train_lengths
    )
    query_features = full_features(
        query_input, query_gate, query_up, query_outgrad, query_lengths
    )
    gathered = lax.all_gather(query_features, "dp", axis=0, tiled=True)
    return inner(train_features, gathered) / (RANK * SEQ)


def pick(blocks, index):
    chosen = blocks[0]
    for number in range(1, len(blocks)):
        chosen = jnp.where(index == number, blocks[number], chosen)
    return chosen


def moving_plan(
    tensor,
    train_input,
    train_gate,
    train_up,
    train_outgrad,
    train_lengths,
    query_input,
    query_gate,
    query_up,
    query_outgrad,
    query_lengths,
    down_weight,
    proj_input,
    proj_outgrad,
    proj_hidden,
    proj_gate,
    proj_up,
):
    t = lax.axis_index("tensor")
    d = lax.axis_index("dp")
    x, core = d // 2, d % 2
    to_core = [(i, i ^ 1) for i in range(4)]
    to_chip = [(i, i ^ 2) for i in range(4)]
    upward = [(i, i + 1) for i in range(tensor - 1)]
    downward = [(i + 1, i) for i in range(tensor - 1)]

    weight_own = down_weight
    weight_sib = lax.ppermute(down_weight, "dp", to_core)

    def column_blocks(rows):
        rising, falling = [rows], [rows]
        for _ in range(tensor - 1):
            rising.append(lax.ppermute(rising[-1], "tensor", upward))
            falling.append(lax.ppermute(falling[-1], "tensor", downward))
        blocks = [rows]
        for step in range(1, tensor):
            blocks.append(jnp.where(t >= step, rising[step], falling[tensor - step]))
        return blocks

    def hidden_gradient(rows):
        blocks = column_blocks(rows)

        def column(k):
            return pick(blocks, (t - k) % tensor)

        far_own = lax.ppermute(column(2 * (1 - x) + core), "dp", to_chip)
        far_sib = lax.ppermute(column(2 * (1 - x) + 1 - core), "dp", to_chip)
        far = project(far_own, weight_own) + project(far_sib, weight_sib)
        returned = lax.ppermute(far.astype(jnp.bfloat16), "dp", to_chip)
        near = project(column(2 * x + core), weight_own)
        near = near + project(column(2 * x + 1 - core), weight_sib)
        return near + returned.astype(jnp.float32)

    query_rows = [flatten(a) for a in (query_input, query_gate, query_up, query_outgrad)]
    train_rows = [flatten(a) for a in (train_input, train_gate, train_up, train_outgrad)]

    q_input, q_gate, q_up, q_outgrad = query_rows
    gate_side, up_side = gradient_sides(
        q_gate, q_up, hidden_gradient(q_outgrad), proj_gate, proj_up
    )
    query_sides = lax.psum(
        (
            project(q_input, proj_input),
            project(gated_hidden(q_gate, q_up), proj_hidden),
            gate_side,
            up_side,
            project(q_outgrad, proj_outgrad),
        ),
        "tensor",
    )
    query_features = lax.all_gather(
        features(*query_sides, query_lengths), "dp", axis=0, tiled=True
    )

    t_input, t_gate, t_up, t_outgrad = train_rows
    in_side, out_side = lax.psum(
        (project(t_input, proj_input), project(t_outgrad, proj_outgrad)), "tensor"
    )
    hidden_side = project(gated_hidden(t_gate, t_up), proj_hidden)

    pieces = 2
    examples = train_lengths.shape[0] // pieces
    partial = []
    for piece in range(pieces):
        part = slice(piece * examples * SEQ, (piece + 1) * examples * SEQ)
        gate_side, up_side = gradient_sides(
            t_gate[part], t_up[part], hidden_gradient(t_outgrad[part]), proj_gate, proj_up
        )
        piece_features = features(
            in_side[part],
            hidden_side[part],
            gate_side,
            up_side,
            out_side[part],
            train_lengths[piece * examples : (piece + 1) * examples],
        )
        partial.append(inner(piece_features, query_features))
    scores = jnp.concatenate(partial, axis=0)
    total = scores
    for step in range(1, tensor):
        turn = [(i, (i + step) % tensor) for i in range(tensor)]
        total = total + lax.ppermute(scores, "tensor", turn)
    return total / (RANK * SEQ)


def solution(mesh):
    tensor, dp = mesh.shape["tensor"], mesh.shape["dp"]

    def per_device(*arguments):
        if tensor == 4 and dp == 4:
            return moving_plan(tensor, *arguments)
        return gathering_plan(*arguments)

    in_specs = (
        P(("parts", "dp"), None, "tensor"),
        P(("parts", "dp"), None, "tensor"),
        P(("parts", "dp"), None, "tensor"),
        P(("parts", "dp"), None, "tensor"),
        P(("parts", "dp")),
        P(("parts", "dp"), None, "tensor"),
        P(("parts", "dp"), None, "tensor"),
        P(("parts", "dp"), None, "tensor"),
        P(("parts", "dp"), None, "tensor"),
        P(("parts", "dp")),
        P("tensor", "dp"),
        P(None, "tensor"),
        P(None, "tensor"),
        P(None, "tensor"),
        P(None, "tensor"),
        P(None, "tensor"),
    )
    out_specs = P(("parts", "dp"), None)
    return jax.shard_map(
        per_device, mesh=mesh, in_specs=in_specs, out_specs=out_specs, check_vma=False
    )
```

time: 614 us -> 356 us (0.58)
  waiting for transfers between devices: 508 us -> 73.2 us
  matrix products: 81.9 us -> 163 us
  starting transfers between devices: 0.16 us -> 72.2 us
  other arithmetic: 0.19 us -> 12.3 us
    all_gather x3 -> x0, waiting for transfers between devices: 438 us -> none  [the longest x1 346 us: per_device(): piece = lax.all_gather(down_weight, 'dp', axis=1, tiled=True)]
    dot_general x6 -> x17, matrix products: 60.9 us -> 145 us  [project(): lax.dot_general(rows, table, (((1,), (1,)), ((), ())), preferred_element_...]
    ppermute x0 -> x31, starting transfers between devices: none -> 72.1 us  [the longest x9 44.1 us: column_blocks(): rising.append(lax.ppermute(rising[-1], 'tensor', upward))]
    ppermute x0 -> x31, waiting for transfers between devices: none -> 38 us  [the longest x9 25.6 us: column_blocks(): rising.append(lax.ppermute(rising[-1], 'tensor', upward))]
    psum x2, waiting for transfers between devices: 67.6 us -> 35.1 us  [the longest x1 35.1 us: moving_plan(): lax.psum((project(q_input, proj_input), project(gated_hidden(q_gate, q_up...]
    select_n x0 -> x6, other arithmetic: none -> 8.18 us  [pick(): chosen = jnp.where(index == number, blocks[number], chosen)]
    reshape x6 -> x7, matrix products: 12.6 us -> 11.7 us  [outer_sums(): right_rows = right_side.reshape(number, length, right_side.shape[1])]
  transfers between devices with their start and end apart: 5 -> 33, of which waited for: 5 -> 20; matrix products, arithmetic and copies ran while one was open for 7% -> 46% of each run, Pallas kernels for 0% -> 0%
where the time goes in v1:
time: 356 us; the launch traced here: 350 us
  matrix products  163 us (46%)
  waiting for transfers between devices  73.2 us (21%)
  starting transfers between devices  72.2 us (20%)
  between operations  14.3 us (4%)
  other arithmetic  12.3 us (3%)
  local copies, waits for them, and re-layouts  8.22 us (2%)
  blocking collectives  6.44 us (2%)
    dot_general x17, matrix products, project(): lax.dot_general(rows, table, (((1,), (1,)), ((), ())), preferred_element_...  145 us
    ppermute x9, starting transfers between devices, column_blocks(): rising.append(lax.ppermute(rising[-1], 'tensor', upward))  44.1 us
    psum x1, waiting for transfers between devices, moving_plan(): lax.psum((project(q_input, proj_input), project(gated_hidden(q_gate, q_up...  35.1 us
    ppermute x9, waiting for transfers between devices, column_blocks(): rising.append(lax.ppermute(rising[-1], 'tensor', upward))  25.6 us
    ppermute x9, starting transfers between devices, column_blocks(): falling.append(lax.ppermute(falling[-1], 'tensor', downward))  12 us
    reshape x7, matrix products, outer_sums(): right_rows = right_side.reshape(number, length, right_side.shape[1])  11.7 us
    ppermute x9, waiting for transfers between devices, column_blocks(): falling.append(lax.ppermute(falling[-1], 'tensor', downward))  11 us
    select_n x6, other arithmetic, pick(): chosen = jnp.where(index == number, blocks[number], chosen)  8.18 us
  transfers between devices with their start and end apart: 33, of which 20 were waited for; matrix products, arithmetic and copies ran while one was open for 46% of the time, Pallas kernels for 0%

profile of v1, /device:TPU:0, one launch (start us, length us, event | category | flops | bytes accessed | tf_op | source)
XLA Modules:
  0.0 350.1 jit_solution(17840344898583715628)
XLA Ops:
  7.1 1.6 fusion.116
  8.7 5.2 %collective-permute-start = (bf16[128,2048]{1,0:T(8,128)(2,1)S(1)}, bf16[128,2048]{1,0:T(8,128)(2,1)}, u32[]{:S(2)}, u32[]{:S(2)}) collective-permute-start(bf16[128,2048]{1,0:T(8,128)(2,1)S(1)} %bitcast.123), channel_id=1, source_target_pairs={{0,4},{4,8},{8,12},{1,5},{5,9},{9,13},{2,6},{6,10},{10,14},{3,7},{... | collective-permute-start | bytes 1572872 | tf_op jit(solution)/shard_map/ppermute | solution.py:154
  15.2 5.4 %collective-permute-start.10 = (bf16[128,2048]{1,0:T(8,128)(2,1)S(1)}, bf16[128,2048]{1,0:T(8,128)(2,1)}, u32[]{:S(2)}, u32[]{:S(2)}) collective-permute-start(bf16[128,2048]{1,0:T(8,128)(2,1)S(1)} %bitcast.114), channel_id=1, source_target_pairs={{0,4},{4,8},{8,12},{1,5},{5,9},{9,13},{2,6},{6,10},{10,14},{3,7},{... | collective-permute-start | bytes 1572872 | tf_op jit(solution)/shard_map/ppermute | solution.py:154
  24.1 3.3 fusion.10
  27.4 1.9 fusion.114
  30.0 4.6 %collective-permute-start.19 = (bf16[128,2048]{1,0:T(8,128)(2,1)S(1)}, bf16[128,2048]{1,0:T(8,128)(2,1)S(1)}, u32[]{:S(2)}, u32[]{:S(2)}) collective-permute-start(bf16[128,2048]{1,0:T(8,128)(2,1)S(1)} %bitcast.119), channel_id=1, source_target_pairs={{0,4},{4,8},{8,12},{1,5},{5,9},{9,13},{2,6},{6,10},{10,14},{3,7},{... | collective-permute-start | bytes 1572872 | tf_op jit(solution)/shard_map/ppermute | solution.py:154
  36.3 1.7 collective-permute-done.10
  38.0 5.4 %collective-permute-start.1 = (bf16[128,2048]{1,0:T(8,128)(2,1)}, bf16[128,2048]{1,0:T(8,128)(2,1)}, u32[]{:S(2)}, u32[]{:S(2)}) collective-permute-start(bf16[128,2048]{1,0:T(8,128)(2,1)} %collective-permute-done), channel_id=1, source_target_pairs={{0,4},{4,8},{8,12},{1,5},{5,9},{9,13},{2,6},{6,10},{10,14},{3,7},{... | collective-permute-start | bytes 1572872 | tf_op jit(solution)/shard_map/ppermute | solution.py:154
  45.3 4.8 %collective-permute-done.19 = bf16[128,2048]{1,0:T(8,128)(2,1)S(1)} collective-permute-done((bf16[128,2048]{1,0:T(8,128)(2,1)S(1)}, bf16[128,2048]{1,0:T(8,128)(2,1)S(1)}, u32[]{:S(2)}, u32[]{:S(2)}) %collective-permute-start.19) | collective-permute-done | bytes 524320 | tf_op jit(solution)/shard_map/ppermute | solution.py:154
  50.2 5.2 %collective-permute-start.11 = (bf16[128,2048]{1,0:T(8,128)(2,1)}, bf16[128,2048]{1,0:T(8,128)(2,1)}, u32[]{:S(2)}, u32[]{:S(2)}) collective-permute-start(bf16[128,2048]{1,0:T(8,128)(2,1)} %collective-permute-done.10), channel_id=1, source_target_pairs={{0,4},{4,8},{8,12},{1,5},{5,9},{9,13},{2,6},{6,10},{10,14},{3,7},{... | collective-permute-start | bytes 1572872 | tf_op jit(solution)/shard_map/ppermute | solution.py:154
  59.4 4.3 %collective-permute-done.1 = bf16[128,2048]{1,0:T(8,128)(2,1)} collective-permute-done((bf16[128,2048]{1,0:T(8,128)(2,1)}, bf16[128,2048]{1,0:T(8,128)(2,1)}, u32[]{:S(2)}, u32[]{:S(2)}) %collective-permute-start.1) | collective-permute-done | bytes 524320 | tf_op jit(solution)/shard_map/ppermute | solution.py:154
  63.7 4.4 %collective-permute-start.20 = (bf16[128,2048]{1,0:T(8,128)(2,1)S(1)}, bf16[128,2048]{1,0:T(8,128)(2,1)S(1)}, u32[]{:S(2)}, u32[]{:S(2)}) collective-permute-start(bf16[128,2048]{1,0:T(8,128)(2,1)S(1)} %collective-permute-done.19), channel_id=1, source_target_pairs={{0,4},{4,8},{8,12},{1,5},{5,9},{9,13},{2,6},{6,10},{10,14},{3,7},{... | collective-permute-start | bytes 1572872 | tf_op jit(solution)/shard_map/ppermute | solution.py:154
  70.2 4.7 %collective-permute-done.11 = bf16[128,2048]{1,0:T(8,128)(2,1)} collective-permute-done((bf16[128,2048]{1,0:T(8,128)(2,1)}, bf16[128,2048]{1,0:T(8,128)(2,1)}, u32[]{:S(2)}, u32[]{:S(2)}) %collective-permute-start.11) | collective-permute-done | bytes 524320 | tf_op jit(solution)/shard_map/ppermute | solution.py:154
  74.9 5.2 %collective-permute-start.2 = (bf16[128,2048]{1,0:T(8,128)(2,1)}, bf16[128,2048]{1,0:T(8,128)(2,1)}, u32[]{:S(2)}, u32[]{:S(2)}) collective-permute-start(bf16[128,2048]{1,0:T(8,128)(2,1)} %collective-permute-done.1), channel_id=1, source_target_pairs={{0,4},{4,8},{8,12},{1,5},{5,9},{9,13},{2,6},{6,10},{10,14},{3,7},{... | collective-permute-start | bytes 1572872 | tf_op jit(solution)/shard_map/ppermute | solution.py:154
  83.9 2.2 collective-permute-done.20
  86.0 4.4 %collective-permute-start.12 = (bf16[128,2048]{1,0:T(8,128)(2,1)}, bf16[128,2048]{1,0:T(8,128)(2,1)S(1)}, u32[]{:S(2)}, u32[]{:S(2)}) collective-permute-start(bf16[128,2048]{1,0:T(8,128)(2,1)} %collective-permute-done.11), channel_id=1, source_target_pairs={{0,4},{4,8},{8,12},{1,5},{5,9},{9,13},{2,6},{6,10},{10,14},{3,7},{... | collective-permute-start | bytes 1572872 | tf_op jit(solution)/shard_map/ppermute | solution.py:154
  92.7 4.7 %collective-permute-done.2 = bf16[128,2048]{1,0:T(8,128)(2,1)} collective-permute-done((bf16[128,2048]{1,0:T(8,128)(2,1)}, bf16[128,2048]{1,0:T(8,128)(2,1)}, u32[]{:S(2)}, u32[]{:S(2)}) %collective-permute-start.2) | collective-permute-done | bytes 524320 | tf_op jit(solution)/shard_map/ppermute | solution.py:154
  97.4 4.4 %collective-permute-start.21 = (bf16[128,2048]{1,0:T(8,128)(2,1)S(1)}, bf16[128,2048]{1,0:T(8,128)(2,1)S(1)}, u32[]{:S(2)}, u32[]{:S(2)}) collective-permute-start(bf16[128,2048]{1,0:T(8,128)(2,1)S(1)} %collective-permute-done.20), channel_id=1, source_target_pairs={{0,4},{4,8},{8,12},{1,5},{5,9},{9,13},{2,6},{6,10},{10,14},{3,7},{... | collective-permute-start | bytes 1572872 | tf_op jit(solution)/shard_map/ppermute | solution.py:154
  102.6 1.7 collective-permute-start.24
  104.4 1.6 select_select_fusion.5
  106.2 2.4 collective-permute-done.12
  110.1 3.6 %collective-permute-done.15 = bf16[128,2048]{1,0:T(8,128)(2,1)S(1)} collective-permute-done((bf16[128,2048]{1,0:T(8,128)(2,1)}, bf16[128,2048]{1,0:T(8,128)(2,1)S(1)}, u32[]{:S(2)}, u32[]{:S(2)}) %collective-permute-start.15) | collective-permute-done | bytes 524320 | tf_op jit(solution)/shard_map/ppermute | solution.py:155
  115.2 2.3 select_select_fusion.3
  120.8 3.4 collective-permute-done.24
  124.2 1.5 collective-permute-start.16
  125.7 2.2 select_select_fusion.1
  130.9 10.1 %fusion.122 = f32[128,3584]{1,0:T(8,128)S(1)} fusion(bf16[128,2048]{1,0:T(8,128)(2,1)S(1)} %collective-permute-done.8, bf16[3584,2048]{1,0:T(8,128)(2,1)} %collective-permute-done.6), kind=kOutput, calls=%fused_computation.168 | convolution fusion | flops 1879048192 | bytes 17039360 | tf_op jit(solution)/shard_map/dot_general | solution.py:15
  141.0 11.3 %fusion.3 = bf16[128,3584]{1,0:T(8,128)(2,1)} fusion(f32[128,3584]{1,0:T(8,128)S(1)} %fusion.122, bf16[128,2048]{1,0:T(8,128)(2,1)} %collective-permute-done.7, bf16[3584,2048]{1,0:T(8,128)(2,1)} %param.26), kind=kOutput, calls=%fused_computation.9 | convolution fusion | flops 1879965696 | bytes 17956864 | tf_op jit(solution)/shard_map/dot_general | solution.py:15
  152.8 10.3 %fusion.128 = f32[128,3584]{1,0:T(8,128)S(1)} fusion(bf16[128,2048]{1,0:T(8,128)(2,1)} %collective-permute-done.17, bf16[3584,2048]{1,0:T(8,128)(2,1)} %collective-permute-done.6), kind=kOutput, calls=%fused_computation.174 | convolution fusion | flops 1879048192 | bytes 17039360 | tf_op jit(solution)/shard_map/dot_general | solution.py:15
  163.1 11.4 %fusion.4 = bf16[128,3584]{1,0:T(8,128)(2,1)} fusion(f32[128,3584]{1,0:T(8,128)S(1)} %fusion.128, bf16[128,2048]{1,0:T(8,128)(2,1)} %collective-permute-done.16, bf16[3584,2048]{1,0:T(8,128)(2,1)} %param.26), kind=kOutput, calls=%fused_computation.10 | convolution fusion | flops 1879965696 | bytes 17956864 | tf_op jit(solution)/shard_map/dot_general | solution.py:15
  174.6 1.5 collective-permute-start.18
  176.1 10.3 %fusion.131 = f32[128,3584]{1,0:T(8,128)S(1)} fusion(bf16[128,2048]{1,0:T(8,128)(2,1)} %collective-permute-done.26, bf16[3584,2048]{1,0:T(8,128)(2,1)} %collective-permute-done.6), kind=kOutput, calls=%fused_computation.177 | convolution fusion | flops 1879048192 | bytes 17039360 | tf_op jit(solution)/shard_map/dot_general | solution.py:15
  186.4 11.3 %fusion.5 = bf16[128,3584]{1,0:T(8,128)(2,1)} fusion(f32[128,3584]{1,0:T(8,128)S(1)} %fusion.131, bf16[128,2048]{1,0:T(8,128)(2,1)} %collective-permute-done.25, bf16[3584,2048]{1,0:T(8,128)(2,1)} %param.26), kind=kOutput, calls=%fused_computation.11 | convolution fusion | flops 1879965696 | bytes 17956864 | tf_op jit(solution)/shard_map/dot_general | solution.py:15
  198.2 12.0 %fusion.54 = f32[128,3584]{1,0:T(8,128)} fusion(bf16[3584,2048]{1,0:T(8,128)(2,1)} %collective-permute-done.6, bf16[128,2048]{1,0:T(8,128)(2,1)} %copy-done.7, bf16[128,2048]{1,0:T(8,128)(2,1)S(1)} %get-tuple-element.14, bf16[128,2048]{1,0:T(8,128)(2,1)S(1)} %get-tuple-element.13, bf16[128,2048]{1,0:T(8,128)(2,1)S(1)} %bitcast.125, pred[]{:T(512)S(6)} %eq.79, ...), kind=kOutput, calls=%fused_computation.81 | convolution fusion | flops 1879834624 | bytes 18612228 | tf_op jit(solution)/shard_map/dot_general | solution.py:15
  210.2 11.4 %fusion.47 = f32[128,3584]{1,0:T(8,128)} fusion(bf16[3584,2048]{1,0:T(8,128)(2,1)} %collective-permute-done.6, bf16[128,2048]{1,0:T(8,128)(2,1)S(1)} %copy-done.14, bf16[128,2048]{1,0:T(8,128)(2,1)S(1)} %copy-done.12, bf16[128,2048]{1,0:T(8,128)(2,1)S(1)} %copy-done.9, bf16[128,2048]{1,0:T(8,128)(2,1)S(1)} %bitcast.117, pred[]{:T(512)S(6)} %eq.79, ...), kind=kOutput, calls=%fused_computation.72 | convolution fusion | flops 1879834624 | bytes 18612228 | tf_op jit(solution)/shard_map/dot_general | solution.py:15
  221.5 11.4 %fusion.40 = f32[128,3584]{1,0:T(8,128)} fusion(bf16[3584,2048]{1,0:T(8,128)(2,1)} %collective-permute-done.6, bf16[128,2048]{1,0:T(8,128)(2,1)S(1)} %get-tuple-element.19, bf16[128,2048]{1,0:T(8,128)(2,1)S(1)} %get-tuple-element.18, bf16[128,2048]{1,0:T(8,128)(2,1)S(1)} %get-tuple-element.17, bf16[128,2048]{1,0:T(8,128)(2,1)S(1)} %bitcast.121, ...), kind=kOutput, calls=%fused_computation.63 | convolution fusion | flops 1879834624 | bytes 18612228 | tf_op jit(solution)/shard_map/dot_general | solution.py:15
  232.9 13.2 %fusion.20 = (bf16[128,3584]{1,0:T(8,128)(2,1)}, bf16[128,3584]{1,0:T(8,128)(2,1)}) fusion(bf16[2,64,3584]{2,1,0:T(8,128)(2,1)} %get-tuple-element.28, bf16[2,64,3584]{2,1,0:T(8,128)(2,1)} %get-tuple-element.50, bf16[128,3584]{1,0:T(8,128)(2,1)} %collective-permute-done.9, f32[128,3584]{1,0:T(8,128)} %fusion.54, bf16[3584,2048]{1,0:T(8,128)(2,1)} %param.26, ...), kind=kOutput, calls=%fused_computation.39 | convolution fusion | flops 1888092160 | bytes 23199748 | tf_op jit(solution)/shard_map/dot_general | solution.py:15
  246.1 1.7 fusion.123
  248.1 1.8 fusion.124
  249.9 14.1 %fusion.13 = (bf16[128,3584]{1,0:T(8,128)(2,1)}, f32[128,3584]{1,0:T(8,128)}, f32[128,3584]{1,0:T(8,128)}) fusion(bf16[2,64,3584]{2,1,0:T(8,128)(2,1)} %param.23, bf16[2,64,3584]{2,1,0:T(8,128)(2,1)} %param.22, bf16[128,3584]{1,0:T(8,128)(2,1)} %collective-permute-done.18, f32[128,3584]{1,0:T(8,128)} %fusion.47, bf16[3584,2048]{1,0:T(8,128)(2,1)} %param.26, ...), kind=kOutput, calls=%fused_computation.32 | convolution fusion | flops 1887174656 | bytes 25952260 | tf_op jit(solution)/shard_map/dot_general | solution.py:15
  264.4 2.3 fusion.38
  267.5 2.2 fusion.129
  269.7 3.1 fusion.37
  272.8 13.2 %fusion.32 = (bf16[128,3584]{1,0:T(8,128)(2,1)}, bf16[128,3584]{1,0:T(8,128)(2,1)}) fusion(bf16[2,64,3584]{2,1,0:T(8,128)(2,1)} %get-tuple-element.29, bf16[2,64,3584]{2,1,0:T(8,128)(2,1)} %get-tuple-element.49, bf16[128,3584]{1,0:T(8,128)(2,1)} %collective-permute-done.27, f32[128,3584]{1,0:T(8,128)} %fusion.40, bf16[3584,2048]{1,0:T(8,128)(2,1)} %param.26, ...), kind=kOutput, calls=%fused_computation.51 | convolution fusion | flops 1888092160 | bytes 23199748 | tf_op jit(solution)/shard_map/dot_general | solution.py:15
  286.0 1.6 fusion.132
  288.7 35.1 %all-reduce.5.cloned.1.call-done = (f32[2,64,64]{2,1,0:T(8,128)}, f32[2,64,64]{1,2,0:T(8,128)}, f32[2,64,64]{2,1,0:T(8,128)}, f32[2,64,64]{1,2,0:T(8,128)}, f32[2,64,64]{2,1,0:T(8,128)}) async-done(((f32[2,64,64]{2,1,0:T(8,128)}, f32[2,64,64]{1,2,0:T(8,128)}, f32[2,64,64]{2,1,0:T(8,128)}, f32[2,64,64]{1,2,0:T(8,128)}, f32[2,64,64]{2,1,0:T(8,128)}), (f32[2,64,64]{2,1,0:T(8,128)}, f32[2,64,64]{1,2,0:T(8,128)}, ...) | async-done | bytes 163856 | tf_op jit(solution)/shard_map/psum | solution.py:182
  327.4 6.4 %all-gather = f32[4,2,12288]{2,1,0:T(2,128)S(1)} all-gather(f32[1,2,12288]{2,1,0:T(2,128)S(1)} %maximum_bitcast_fusion), channel_id=1, replica_groups=mesh['parts'=2,'tensor'=4,'dp'=4] {'dp'}, dimensions={0}, use_global_device_ids=true | all-gather | bytes 491520 | tf_op jit(solution)/shard_map/all_gather | solution.py:192
  338.9 2.2 collective-permute-start.30
  (157 shorter events, 45.8 us)
Async XLA Ops:
  6.5 15.3 %copy-start = (bf16[4,64,2048]{2,1,0:T(8,128)(2,1)S(1)}, bf16[4,64,2048]{2,1,0:T(8,128)(2,1)}, u32[]{:S(2)}) copy-start(bf16[4,64,2048]{2,1,0:T(8,128)(2,1)} %param.16) | copy-start | bytes 3145732
  6.5 15.3 %copy-start.19 = (bf16[64,2048]{1,0:T(8,128)(2,1)S(1)}, bf16[64,2048]{1,0:T(8,128)(2,1)}, u32[]{:S(2)}) copy-start(bf16[64,2048]{1,0:T(8,128)(2,1)} %param.27) | copy-start | bytes 786436
  6.5 16.4 %copy-start.20 = (bf16[64,2048]{1,0:T(8,128)(2,1)S(1)}, bf16[64,2048]{1,0:T(8,128)(2,1)}, u32[]{:S(2)}) copy-start(bf16[64,2048]{1,0:T(8,128)(2,1)} %param.28) | copy-start | bytes 786436
  6.5 74.9 %all-reduce.7.cloned.1.call-start = ((), (), s32[]{:S(2)}) async-start(), calls=%async_computation.1 | async-start | bytes 262144 | tf_op jit(solution)/shard_map/psum | solution.py:197
  6.6 16.3 %copy-start.15 = (bf16[4,64,2048]{2,1,0:T(8,128)(2,1)S(1)}, bf16[4,64,2048]{2,1,0:T(8,128)(2,1)}, u32[]{:S(2)}) copy-start(bf16[4,64,2048]{2,1,0:T(8,128)(2,1)} %param.19) | copy-start | bytes 3145732
  6.6 122.8 %collective-permute-start.6 = (bf16[3584,2048]{1,0:T(8,128)(2,1)}, bf16[3584,2048]{1,0:T(8,128)(2,1)}, u32[]{:S(2)}, u32[]{:S(2)}) collective-permute-start(bf16[3584,2048]{1,0:T(8,128)(2,1)} %param.26), channel_id=1, source_target_pairs={{0,1},{1,0},{2,3},{3,2},{4,5},{5,4},{6,7},{7,6},{8,9},{9,8},{10,11... | collective-permute-start | bytes 44040200 | tf_op jit(solution)/shard_map/ppermute | solution.py:149
  8.7 21.3 %collective-permute-start = (bf16[128,2048]{1,0:T(8,128)(2,1)S(1)}, bf16[128,2048]{1,0:T(8,128)(2,1)}, u32[]{:S(2)}, u32[]{:S(2)}) collective-permute-start(bf16[128,2048]{1,0:T(8,128)(2,1)S(1)} %bitcast.123), channel_id=1, source_target_pairs={{0,4},{4,8},{8,12},{1,5},{5,9},{9,13},{2,6},{6,10},{10,14},{3,7},{... | collective-permute-start | bytes 1572872 | tf_op jit(solution)/shard_map/ppermute | solution.py:154
  13.9 20.7 %collective-permute-start.3 = (bf16[128,2048]{1,0:T(8,128)(2,1)S(1)}, bf16[128,2048]{1,0:T(8,128)(2,1)}, u32[]{:S(2)}, u32[]{:S(2)}) collective-permute-start(bf16[128,2048]{1,0:T(8,128)(2,1)S(1)} %bitcast.124), channel_id=1, source_target_pairs={{4,0},{8,4},{12,8},{5,1},{9,5},{13,9},{6,2},{10,6},{14,10},{7,3},{... | collective-permute-start | bytes 1572872 | tf_op jit(solution)/shard_map/ppermute | solution.py:155
  15.2 22.9 %collective-permute-start.10 = (bf16[128,2048]{1,0:T(8,128)(2,1)S(1)}, bf16[128,2048]{1,0:T(8,128)(2,1)}, u32[]{:S(2)}, u32[]{:S(2)}) collective-permute-start(bf16[128,2048]{1,0:T(8,128)(2,1)S(1)} %bitcast.114), channel_id=1, source_target_pairs={{0,4},{4,8},{8,12},{1,5},{5,9},{9,13},{2,6},{6,10},{10,14},{3,7},{... | collective-permute-start | bytes 1572872 | tf_op jit(solution)/shard_map/ppermute | solution.py:154
  20.5 23.5 %collective-permute-start.13 = (bf16[128,2048]{1,0:T(8,128)(2,1)S(1)}, bf16[128,2048]{1,0:T(8,128)(2,1)}, u32[]{:S(2)}, u32[]{:S(2)}) collective-permute-start(bf16[128,2048]{1,0:T(8,128)(2,1)S(1)} %bitcast.115), channel_id=1, source_target_pairs={{4,0},{8,4},{12,8},{5,1},{9,5},{13,9},{6,2},{10,6},{14,10},{7,3},{... | collective-permute-start | bytes 1572872 | tf_op jit(solution)/shard_map/ppermute | solution.py:155
  24.0 299.8 %all-reduce.5.cloned.1.call-start = ((), (), s32[]{:S(2)}) async-start(), calls=%async_computation | async-start | bytes 655360 | tf_op jit(solution)/shard_map/psum | solution.py:182
  29.3 30.0 %copy-start.31 = (s32[2]{0:T(128)S(1)}, s32[2]{0:T(128)}, u32[]{:S(2)}) copy-start(s32[2]{0:T(128)} %param.25) | copy-start | bytes 28
  30.0 20.2 %collective-permute-start.19 = (bf16[128,2048]{1,0:T(8,128)(2,1)S(1)}, bf16[128,2048]{1,0:T(8,128)(2,1)S(1)}, u32[]{:S(2)}, u32[]{:S(2)}) collective-permute-start(bf16[128,2048]{1,0:T(8,128)(2,1)S(1)} %bitcast.119), channel_id=1, source_target_pairs={{0,4},{4,8},{8,12},{1,5},{5,9},{9,13},{2,6},{6,10},{10,14},{3,7},{... | collective-permute-start | bytes 1572872 | tf_op jit(solution)/shard_map/ppermute | solution.py:154
  34.6 21.4 %collective-permute-start.22 = (bf16[128,2048]{1,0:T(8,128)(2,1)S(1)}, bf16[128,2048]{1,0:T(8,128)(2,1)S(1)}, u32[]{:S(2)}, u32[]{:S(2)}) collective-permute-start(bf16[128,2048]{1,0:T(8,128)(2,1)S(1)} %bitcast.120), channel_id=1, source_target_pairs={{4,0},{8,4},{12,8},{5,1},{9,5},{13,9},{6,2},{10,6},{14,10},{7,3},{... | collective-permute-start | bytes 1572872 | tf_op jit(solution)/shard_map/ppermute | solution.py:155
  38.0 25.6 %collective-permute-start.1 = (bf16[128,2048]{1,0:T(8,128)(2,1)}, bf16[128,2048]{1,0:T(8,128)(2,1)}, u32[]{:S(2)}, u32[]{:S(2)}) collective-permute-start(bf16[128,2048]{1,0:T(8,128)(2,1)} %collective-permute-done), channel_id=1, source_target_pairs={{0,4},{4,8},{8,12},{1,5},{5,9},{9,13},{2,6},{6,10},{10,14},{3,7},{... | collective-permute-start | bytes 1572872 | tf_op jit(solution)/shard_map/ppermute | solution.py:154
  44.1 24.8 %collective-permute-start.4 = (bf16[128,2048]{1,0:T(8,128)(2,1)}, bf16[128,2048]{1,0:T(8,128)(2,1)}, u32[]{:S(2)}, u32[]{:S(2)}) collective-permute-start(bf16[128,2048]{1,0:T(8,128)(2,1)} %collective-permute-done.3), channel_id=1, source_target_pairs={{4,0},{8,4},{12,8},{5,1},{9,5},{13,9},{6,2},{10,6},{14,10},{7,3},{... | collective-permute-start | bytes 1572872 | tf_op jit(solution)/shard_map/ppermute | solution.py:155
  50.2 52.4 %copy-start.22 = (bf16[128,2048]{1,0:T(8,128)(2,1)}, bf16[128,2048]{1,0:T(8,128)(2,1)S(1)}, u32[]{:S(2)}) copy-start(bf16[128,2048]{1,0:T(8,128)(2,1)S(1)} %collective-permute-done.19) | copy-start | bytes 1572868
  50.2 24.7 %collective-permute-start.11 = (bf16[128,2048]{1,0:T(8,128)(2,1)}, bf16[128,2048]{1,0:T(8,128)(2,1)}, u32[]{:S(2)}, u32[]{:S(2)}) collective-permute-start(bf16[128,2048]{1,0:T(8,128)(2,1)} %collective-permute-done.10), channel_id=1, source_target_pairs={{0,4},{4,8},{8,12},{1,5},{5,9},{9,13},{2,6},{6,10},{10,14},{3,7},{... | collective-permute-start | bytes 1572872 | tf_op jit(solution)/shard_map/ppermute | solution.py:154
  56.0 49.9 %copy-start.24 = (bf16[128,2048]{1,0:T(8,128)(2,1)}, bf16[128,2048]{1,0:T(8,128)(2,1)S(1)}, u32[]{:S(2)}) copy-start(bf16[128,2048]{1,0:T(8,128)(2,1)S(1)} %collective-permute-done.22) | copy-start | bytes 1572868
  56.0 24.1 %collective-permute-start.14 = (bf16[128,2048]{1,0:T(8,128)(2,1)}, bf16[128,2048]{1,0:T(8,128)(2,1)}, u32[]{:S(2)}, u32[]{:S(2)}) collective-permute-start(bf16[128,2048]{1,0:T(8,128)(2,1)} %collective-permute-done.13), channel_id=1, source_target_pairs={{4,0},{8,4},{12,8},{5,1},{9,5},{13,9},{6,2},{10,6},{14,10},{7,3},{... | collective-permute-start | bytes 1572872 | tf_op jit(solution)/shard_map/ppermute | solution.py:155
  63.7 22.4 %collective-permute-start.20 = (bf16[128,2048]{1,0:T(8,128)(2,1)S(1)}, bf16[128,2048]{1,0:T(8,128)(2,1)S(1)}, u32[]{:S(2)}, u32[]{:S(2)}) collective-permute-start(bf16[128,2048]{1,0:T(8,128)(2,1)S(1)} %collective-permute-done.19), channel_id=1, source_target_pairs={{0,4},{4,8},{8,12},{1,5},{5,9},{9,13},{2,6},{6,10},{10,14},{3,7},{... | collective-permute-start | bytes 1572872 | tf_op jit(solution)/shard_map/ppermute | solution.py:154
  68.9 22.5 %collective-permute-start.23 = (bf16[128,2048]{1,0:T(8,128)(2,1)S(1)}, bf16[128,2048]{1,0:T(8,128)(2,1)}, u32[]{:S(2)}, u32[]{:S(2)}) collective-permute-start(bf16[128,2048]{1,0:T(8,128)(2,1)S(1)} %collective-permute-done.22), channel_id=1, source_target_pairs={{4,0},{8,4},{12,8},{5,1},{9,5},{13,9},{6,2},{10,6},{14,10},{7,3},{... | collective-permute-start | bytes 1572872 | tf_op jit(solution)/shard_map/ppermute | solution.py:155
  74.9 22.5 %collective-permute-start.2 = (bf16[128,2048]{1,0:T(8,128)(2,1)}, bf16[128,2048]{1,0:T(8,128)(2,1)}, u32[]{:S(2)}, u32[]{:S(2)}) collective-permute-start(bf16[128,2048]{1,0:T(8,128)(2,1)} %collective-permute-done.1), channel_id=1, source_target_pairs={{0,4},{4,8},{8,12},{1,5},{5,9},{9,13},{2,6},{6,10},{10,14},{3,7},{... | collective-permute-start | bytes 1572872 | tf_op jit(solution)/shard_map/ppermute | solution.py:154
  80.1 22.5 %collective-permute-start.5 = (bf16[128,2048]{1,0:T(8,128)(2,1)}, bf16[128,2048]{1,0:T(8,128)(2,1)}, u32[]{:S(2)}, u32[]{:S(2)}) collective-permute-start(bf16[128,2048]{1,0:T(8,128)(2,1)} %collective-permute-done.4), channel_id=1, source_target_pairs={{4,0},{8,4},{12,8},{5,1},{9,5},{13,9},{6,2},{10,6},{14,10},{7,3},{... | collective-permute-start | bytes 1572872 | tf_op jit(solution)/shard_map/ppermute | solution.py:155
  86.0 19.9 %copy-start.26 = (bf16[128,2048]{1,0:T(8,128)(2,1)}, bf16[128,2048]{1,0:T(8,128)(2,1)S(1)}, u32[]{:S(2)}) copy-start(bf16[128,2048]{1,0:T(8,128)(2,1)S(1)} %collective-permute-done.20) | copy-start | bytes 1572868
  86.0 22.6 %collective-permute-start.12 = (bf16[128,2048]{1,0:T(8,128)(2,1)}, bf16[128,2048]{1,0:T(8,128)(2,1)S(1)}, u32[]{:S(2)}, u32[]{:S(2)}) collective-permute-start(bf16[128,2048]{1,0:T(8,128)(2,1)} %collective-permute-done.11), channel_id=1, source_target_pairs={{0,4},{4,8},{8,12},{1,5},{5,9},{9,13},{2,6},{6,10},{10,14},{3,7},{... | collective-permute-start | bytes 1572872 | tf_op jit(solution)/shard_map/ppermute | solution.py:154
  91.4 22.4 %collective-permute-start.15 = (bf16[128,2048]{1,0:T(8,128)(2,1)}, bf16[128,2048]{1,0:T(8,128)(2,1)S(1)}, u32[]{:S(2)}, u32[]{:S(2)}) collective-permute-start(bf16[128,2048]{1,0:T(8,128)(2,1)} %collective-permute-done.14), channel_id=1, source_target_pairs={{4,0},{8,4},{12,8},{5,1},{9,5},{13,9},{6,2},{10,6},{14,10},{7,3},{... | collective-permute-start | bytes 1572872 | tf_op jit(solution)/shard_map/ppermute | solution.py:155
  97.4 22.0 %collective-permute-start.21 = (bf16[128,2048]{1,0:T(8,128)(2,1)S(1)}, bf16[128,2048]{1,0:T(8,128)(2,1)S(1)}, u32[]{:S(2)}, u32[]{:S(2)}) collective-permute-start(bf16[128,2048]{1,0:T(8,128)(2,1)S(1)} %collective-permute-done.20), channel_id=1, source_target_pairs={{0,4},{4,8},{8,12},{1,5},{5,9},{9,13},{2,6},{6,10},{10,14},{3,7},{... | collective-permute-start | bytes 1572872 | tf_op jit(solution)/shard_map/ppermute | solution.py:154
  102.6 21.6 %collective-permute-start.24 = (bf16[128,2048]{1,0:T(8,128)(2,1)}, bf16[128,2048]{1,0:T(8,128)(2,1)S(1)}, u32[]{:S(2)}, u32[]{:S(2)}) collective-permute-start(bf16[128,2048]{1,0:T(8,128)(2,1)} %collective-permute-done.23), channel_id=1, source_target_pairs={{4,0},{8,4},{12,8},{5,1},{9,5},{13,9},{6,2},{10,6},{14,10},{7,3},{... | collective-permute-start | bytes 1572872 | tf_op jit(solution)/shard_map/ppermute | solution.py:155
  106.0 92.2 %copy-start.5 = (bf16[128,2048]{1,0:T(8,128)(2,1)}, bf16[128,2048]{1,0:T(8,128)(2,1)S(1)}, u32[]{:S(2)}) copy-start(bf16[128,2048]{1,0:T(8,128)(2,1)S(1)} %get-tuple-element.13) | copy-start | bytes 1572868
  106.0 92.2 %copy-start.6 = (bf16[128,2048]{1,0:T(8,128)(2,1)}, bf16[128,2048]{1,0:T(8,128)(2,1)S(1)}, u32[]{:S(2)}) copy-start(bf16[128,2048]{1,0:T(8,128)(2,1)S(1)} %get-tuple-element.14) | copy-start | bytes 1572868
  108.6 20.2 %collective-permute-start.8 = (bf16[128,2048]{1,0:T(8,128)(2,1)S(1)}, bf16[128,2048]{1,0:T(8,128)(2,1)S(1)}, u32[]{:S(2)}, u32[]{:S(2)}) collective-permute-start(bf16[128,2048]{1,0:T(8,128)(2,1)S(1)} %select_select_fusion.4), channel_id=1, source_target_pairs={{0,2},{1,3},{2,0},{3,1},{4,6},{5,7},{6,4},{7,5},{8,10},{9,11},{10,... | collective-permute-start | bytes 1572872 | tf_op jit(solution)/shard_map/ppermute | solution.py:168
  113.7 27.2 %collective-permute-start.7 = (bf16[128,2048]{1,0:T(8,128)(2,1)S(1)}, bf16[128,2048]{1,0:T(8,128)(2,1)}, u32[]{:S(2)}, u32[]{:S(2)}) collective-permute-start(bf16[128,2048]{1,0:T(8,128)(2,1)S(1)} %get-tuple-element.12), channel_id=1, source_target_pairs={{0,2},{1,3},{2,0},{3,1},{4,6},{5,7},{6,4},{7,5},{8,10},{9,11},{10,... | collective-permute-start | bytes 1572872 | tf_op jit(solution)/shard_map/ppermute | solution.py:167
  119.3 33.5 %collective-permute-start.17 = (bf16[128,2048]{1,0:T(8,128)(2,1)}, bf16[128,2048]{1,0:T(8,128)(2,1)}, u32[]{:S(2)}, u32[]{:S(2)}) collective-permute-start(bf16[128,2048]{1,0:T(8,128)(2,1)} %select_select_fusion.2), channel_id=1, source_target_pairs={{0,2},{1,3},{2,0},{3,1},{4,6},{5,7},{6,4},{7,5},{8,10},{9,11},{10,... | collective-permute-start | bytes 1572872 | tf_op jit(solution)/shard_map/ppermute | solution.py:168
  124.2 38.9 %collective-permute-start.16 = (bf16[128,2048]{1,0:T(8,128)(2,1)}, bf16[128,2048]{1,0:T(8,128)(2,1)}, u32[]{:S(2)}, u32[]{:S(2)}) collective-permute-start(bf16[128,2048]{1,0:T(8,128)(2,1)} %get-tuple-element.20), channel_id=1, source_target_pairs={{0,2},{1,3},{2,0},{3,1},{4,6},{5,7},{6,4},{7,5},{8,10},{9,11},{10,... | collective-permute-start | bytes 1572872 | tf_op jit(solution)/shard_map/ppermute | solution.py:167
  128.8 47.2 %collective-permute-start.26 = (bf16[128,2048]{1,0:T(8,128)(2,1)}, bf16[128,2048]{1,0:T(8,128)(2,1)}, u32[]{:S(2)}, u32[]{:S(2)}) collective-permute-start(bf16[128,2048]{1,0:T(8,128)(2,1)} %select_select_fusion), channel_id=1, source_target_pairs={{0,2},{1,3},{2,0},{3,1},{4,6},{5,7},{6,4},{7,5},{8,10},{9,11},{10,... | collective-permute-start | bytes 1572872 | tf_op jit(solution)/shard_map/ppermute | solution.py:168
  129.4 57.0 %collective-permute-start.25 = (bf16[128,2048]{1,0:T(8,128)(2,1)}, bf16[128,2048]{1,0:T(8,128)(2,1)}, u32[]{:S(2)}, u32[]{:S(2)}) collective-permute-start(bf16[128,2048]{1,0:T(8,128)(2,1)} %get-tuple-element.16), channel_id=1, source_target_pairs={{0,2},{1,3},{2,0},{3,1},{4,6},{5,7},{6,4},{7,5},{8,10},{9,11},{10,... | collective-permute-start | bytes 1572872 | tf_op jit(solution)/shard_map/ppermute | solution.py:167
  152.3 80.6 %collective-permute-start.9 = (bf16[128,3584]{1,0:T(8,128)(2,1)}, bf16[128,3584]{1,0:T(8,128)(2,1)}, u32[]{:S(2)}, u32[]{:S(2)}) collective-permute-start(bf16[128,3584]{1,0:T(8,128)(2,1)} %fusion.3), channel_id=1, source_target_pairs={{0,2},{1,3},{2,0},{3,1},{4,6},{5,7},{6,4},{7,5},{8,10},{9,11},{10,... | collective-permute-start | bytes 2752520 | tf_op jit(solution)/shard_map/ppermute | solution.py:170
  174.6 75.3 %collective-permute-start.18 = (bf16[128,3584]{1,0:T(8,128)(2,1)}, bf16[128,3584]{1,0:T(8,128)(2,1)}, u32[]{:S(2)}, u32[]{:S(2)}) collective-permute-start(bf16[128,3584]{1,0:T(8,128)(2,1)} %fusion.4), channel_id=1, source_target_pairs={{0,2},{1,3},{2,0},{3,1},{4,6},{5,7},{6,4},{7,5},{8,10},{9,11},{10,... | collective-permute-start | bytes 2752520 | tf_op jit(solution)/shard_map/ppermute | solution.py:170
  197.7 12.5 %copy-start.9 = (bf16[128,2048]{1,0:T(8,128)(2,1)S(1)}, bf16[128,2048]{1,0:T(8,128)(2,1)}, u32[]{:S(2)}) copy-start(bf16[128,2048]{1,0:T(8,128)(2,1)} %copy-done.8) | copy-start | bytes 1572868
  197.7 12.5 %copy-start.12 = (bf16[128,2048]{1,0:T(8,128)(2,1)S(1)}, bf16[128,2048]{1,0:T(8,128)(2,1)}, u32[]{:S(2)}) copy-start(bf16[128,2048]{1,0:T(8,128)(2,1)} %copy-done.11) | copy-start | bytes 1572868
  197.7 12.5 %copy-start.14 = (bf16[128,2048]{1,0:T(8,128)(2,1)S(1)}, bf16[128,2048]{1,0:T(8,128)(2,1)}, u32[]{:S(2)}) copy-start(bf16[128,2048]{1,0:T(8,128)(2,1)} %copy-done.13) | copy-start | bytes 1572868
  197.7 75.1 %collective-permute-start.27 = (bf16[128,3584]{1,0:T(8,128)(2,1)}, bf16[128,3584]{1,0:T(8,128)(2,1)}, u32[]{:S(2)}, u32[]{:S(2)}) collective-permute-start(bf16[128,3584]{1,0:T(8,128)(2,1)} %fusion.5), channel_id=1, source_target_pairs={{0,2},{1,3},{2,0},{3,1},{4,6},{5,7},{6,4},{7,5},{8,10},{9,11},{10,... | collective-permute-start | bytes 2752520 | tf_op jit(solution)/shard_map/ppermute | solution.py:170
  288.4 45.7 %copy-start.29 = (f32[2,4096]{1,0:T(2,128)S(1)}, f32[2,4096]{1,0:T(2,128)}, u32[]{:S(2)}) copy-start(f32[2,4096]{1,0:T(2,128)} %reshape.182) | copy-start | bytes 98308
  288.4 54.6 %copy-start.1 = (bf16[4,64,2048]{2,1,0:T(8,128)(2,1)S(1)}, bf16[4,64,2048]{2,1,0:T(8,128)(2,1)}, u32[]{:S(2)}) copy-start(bf16[4,64,2048]{2,1,0:T(8,128)(2,1)} %param.16) | copy-start | bytes 3145732
  336.0 5.4 %collective-permute-start.28 = (f32[4,8]{1,0:T(4,128)S(1)}, f32[4,8]{1,0:T(4,128)S(1)}, u32[]{:S(2)}, u32[]{:S(2)}) collective-permute-start(f32[4,8]{1,0:T(4,128)S(1)} %pad_maximum_fusion), channel_id=1, source_target_pairs={{0,4},{4,8},{8,12},{12,0},{1,5},{5,9},{9,13},{13,1},{2,6},{6,10},{... | collective-permute-start | bytes 392 | tf_op jit(solution)/shard_map/ppermute | solution.py:223
  337.5 4.5 %collective-permute-start.29 = (f32[4,8]{1,0:T(4,128)S(1)}, f32[4,8]{1,0:T(4,128)S(1)}, u32[]{:S(2)}, u32[]{:S(2)}) collective-permute-start(f32[4,8]{1,0:T(4,128)S(1)} %pad_maximum_fusion), channel_id=1, source_target_pairs={{0,8},{4,12},{8,0},{12,4},{1,9},{5,13},{9,1},{13,5},{2,10},{6,14},... | collective-permute-start | bytes 392 | tf_op jit(solution)/shard_map/ppermute | solution.py:223
  338.9 3.6 %collective-permute-start.30 = (f32[4,8]{1,0:T(4,128)S(1)}, f32[4,8]{1,0:T(4,128)S(1)}, u32[]{:S(2)}, u32[]{:S(2)}) collective-permute-start(f32[4,8]{1,0:T(4,128)S(1)} %pad_maximum_fusion), channel_id=1, source_target_pairs={{0,12},{4,0},{8,4},{12,8},{1,13},{5,1},{9,5},{13,9},{2,14},{6,2},{... | collective-permute-start | bytes 392 | tf_op jit(solution)/shard_map/ppermute | solution.py:223
  (17 other events, 108.4 us)
Sparse Core Ops, SparseCore 0:
  24.1 38.3 all-reduce.6
  288.5 35.2 all-reduce.4

commit v2 on v1

--- a/solution.py
+++ b/solution.py
@@ -1,10 +1,16 @@
+import functools
+
 import jax
 import jax.numpy as jnp
 from jax import lax
+from jax.experimental import pallas as pl
+from jax.experimental.pallas import tpu as pltpu
 from jax.sharding import PartitionSpec as P
 
 RANK = 64
 SEQ = 64
+TILE = 512
+VMEM_BYTES = 40 * 1024 * 1024
 
 
 def flatten(array):
@@ -111,15 +117,148 @@
     return inner(train_features, gathered) / (RANK * SEQ)
 
 
-def pick(blocks, index):
-    chosen = blocks[0]
-    for number in range(1, len(blocks)):
-        chosen = jnp.where(index == number, blocks[number], chosen)
-    return chosen
+def stacked_products(near, far, weight_own, weight_sib, stacked):
+    number = near.shape[0]
+
+    @pl.when(pl.program_id(0) == 0)
+    def _():
+        stacked[:number, :] = near[...]
+        stacked[number:, :] = far[...]
+
+    half = weight_own.shape[1]
+    return project(stacked[:, :half], weight_own[...]) + project(
+        stacked[:, half:], weight_sib[...]
+    )
+
+
+def add_sides(hidden_grad, gate, up, proj_gate, proj_up, gate_side, up_side):
+    gate_part, up_part = gradient_sides(gate, up, hidden_grad, proj_gate, proj_up)
+    first = pl.program_id(0) == 0
+
+    @pl.when(first)
+    def _():
+        gate_side[...] = gate_part
+        up_side[...] = up_part
+
+    @pl.when(jnp.logical_not(first))
+    def _():
+        gate_side[...] += gate_part
+        up_side[...] += up_part
+
+
+def partial_kernel(near, far, weight_own, weight_sib, near_sum, far_sum, stacked):
+    total = stacked_products(near, far, weight_own, weight_sib, stacked)
+    number = near.shape[0]
+    near_sum[...] = total[:number]
+    far_sum[...] = total[number:].astype(jnp.bfloat16)
+
+
+def finish_kernel(near_sum, returned, gate, up, proj_gate, proj_up, gate_side, up_side):
+    hidden_grad = near_sum[...] + returned[...].astype(jnp.float32)
+    add_sides(hidden_grad, gate[...], up[...], proj_gate[...], proj_up[...], gate_side, up_side)
+
+
+def lent_kernel(
+    near,
+    far,
+    weight_own,
+    weight_sib,
+    gate,
+    up,
+    far_gate,
+    far_up,
+    proj_gate,
+    proj_up,
+    gate_side,
+    up_side,
+    stacked,
+):
+    hidden_grad = stacked_products(near, far, weight_own, weight_sib, stacked)
+    gates = jnp.concatenate([gate[...], far_gate[...]], axis=0)
+    ups = jnp.concatenate([up[...], far_up[...]], axis=0)
+    add_sides(hidden_grad, gates, ups, proj_gate[...], proj_up[...], gate_side, up_side)
+
+
+def whole(shape):
+    return pl.BlockSpec(shape, lambda i: (0, 0))
+
+
+def columns(number):
+    return pl.BlockSpec((number, TILE), lambda i: (0, i))
+
+
+def rows(width):
+    return pl.BlockSpec((TILE, width), lambda i: (i, 0))
+
+
+def cost(flops, arrays):
+    moved = sum(array.size * array.dtype.itemsize for array in arrays)
+    return pl.CostEstimate(flops=flops, bytes_accessed=moved, transcendentals=0)
+
+
+def partial_sums(near, far, weight_own, weight_sib):
+    number, width = near.shape
+    units, half = weight_own.shape
+    return pl.pallas_call(
+        partial_kernel,
+        grid=(units // TILE,),
+        in_specs=[whole(near.shape), whole(near.shape), rows(half), rows(half)],
+        out_specs=[columns(number), columns(number)],
+        out_shape=[
+            jax.ShapeDtypeStruct((number, units), jnp.float32),
+            jax.ShapeDtypeStruct((number, units), jnp.bfloat16),
+        ],
+        scratch_shapes=[pltpu.VMEM((2 * number, width), jnp.bfloat16)],
+        compiler_params=pltpu.CompilerParams(vmem_limit_bytes=VMEM_BYTES),
+        cost_estimate=cost(
+            4 * number * width * units, (near, far, weight_own, weight_sib)
+        ),
+    )(near, far, weight_own, weight_sib)
+
+
+def finished_sides(near_sum, returned, gate, up, proj_gate, proj_up):
+    number, units = near_sum.shape
+    side = jax.ShapeDtypeStruct((number, RANK), jnp.float32)
+    return pl.pallas_call(
+        finish_kernel,
+        grid=(units // TILE,),
+        in_specs=[columns(number)] * 4 + [columns(RANK)] * 2,
+        out_specs=[whole(side.shape)] * 2,
+        out_shape=[side] * 2,
+        compiler_params=pltpu.CompilerParams(vmem_limit_bytes=VMEM_BYTES),
+        cost_estimate=cost(
+            4 * number * RANK * units, (near_sum, returned, gate, up, proj_gate, proj_up)
+        ),
+    )(near_sum, returned, gate, up, proj_gate, proj_up)
+
+
+def lent_sides(near, far, weight_own, weight_sib, gate, up, far_gate, far_up, proj_gate, proj_up):
+    number, width = near.shape
+    units, half = weight_own.shape
+    side = jax.ShapeDtypeStruct((2 * number, RANK), jnp.float32)
+    operands = (
+        near, far, weight_own, weight_sib, gate, up, far_gate, far_up, proj_gate, proj_up
+    )
+    return pl.pallas_call(
+        lent_kernel,
+        grid=(units // TILE,),
+        in_specs=[whole(near.shape)] * 2
+        + [rows(half)] * 2
+        + [columns(number)] * 4
+        + [columns(RANK)] * 2,
+        out_specs=[whole(side.shape)] * 2,
+        out_shape=[side] * 2,
+        scratch_shapes=[pltpu.VMEM((2 * number, width), jnp.bfloat16)],
+        compiler_params=pltpu.CompilerParams(vmem_limit_bytes=VMEM_BYTES),
+        cost_estimate=cost(4 * number * width * units, operands),
+    )(*operands)
+
+
+def after(value, *others):
+    return lax.optimization_barrier((value, *others))[0]
 
 
 def moving_plan(
-    tensor,
     train_input,
     train_gate,
     train_up,
@@ -140,88 +279,131 @@
     t = lax.axis_index("tensor")
     d = lax.axis_index("dp")
     x, core = d // 2, d % 2
-    to_core = [(i, i ^ 1) for i in range(4)]
-    to_chip = [(i, i ^ 2) for i in range(4)]
-    upward = [(i, i + 1) for i in range(tensor - 1)]
-    downward = [(i + 1, i) for i in range(tensor - 1)]
-
-    weight_own = down_weight
-    weight_sib = lax.ppermute(down_weight, "dp", to_core)
-
-    def column_blocks(rows):
-        rising, falling = [rows], [rows]
-        for _ in range(tensor - 1):
-            rising.append(lax.ppermute(rising[-1], "tensor", upward))
-            falling.append(lax.ppermute(falling[-1], "tensor", downward))
-        blocks = [rows]
-        for step in range(1, tensor):
-            blocks.append(jnp.where(t >= step, rising[step], falling[tensor - step]))
-        return blocks
-
-    def hidden_gradient(rows):
-        blocks = column_blocks(rows)
-
-        def column(k):
-            return pick(blocks, (t - k) % tensor)
-
-        far_own = lax.ppermute(column(2 * (1 - x) + core), "dp", to_chip)
-        far_sib = lax.ppermute(column(2 * (1 - x) + 1 - core), "dp", to_chip)
-        far = project(far_own, weight_own) + project(far_sib, weight_sib)
-        returned = lax.ppermute(far.astype(jnp.bfloat16), "dp", to_chip)
-        near = project(column(2 * x + core), weight_own)
-        near = near + project(column(2 * x + 1 - core), weight_sib)
-        return near + returned.astype(jnp.float32)
-
-    query_rows = [flatten(a) for a in (query_input, query_gate, query_up, query_outgrad)]
-    train_rows = [flatten(a) for a in (train_input, train_gate, train_up, train_outgrad)]
-
-    q_input, q_gate, q_up, q_outgrad = query_rows
-    gate_side, up_side = gradient_sides(
-        q_gate, q_up, hidden_gradient(q_outgrad), proj_gate, proj_up
-    )
-    query_sides = lax.psum(
+    upper, inner_chip = t // 2, (t == 1) | (t == 2)
+    to_core = functools.partial(lax.ppermute, axis_name="dp", perm=[(i, i ^ 1) for i in range(4)])
+    to_chip = functools.partial(lax.ppermute, axis_name="dp", perm=[(i, i ^ 2) for i in range(4)])
+    outer = functools.partial(
+        lax.ppermute, axis_name="tensor", perm=[(0, 1), (1, 0), (2, 3), (3, 2)]
+    )
+    middle = functools.partial(
+        lax.ppermute, axis_name="tensor", perm=[(0, 0), (1, 2), (2, 1), (3, 3)]
+    )
+    across = functools.partial(
+        lax.ppermute, axis_name="tensor", perm=[(0, 2), (1, 3), (2, 0), (3, 1)]
+    )
+
+    def tensor_sum(values):
+        values = values + outer(values)
+        return values + across(values)
+
+    def hop_one(piece):
+        return piece, outer(piece), middle(piece)
+
+    def hop_two(piece, first, second_inner):
+        return piece, first, second_inner, outer(second_inner), middle(first)
+
+    def hop_three(piece, first, second_inner, second_outer, third_inner):
+        second = jnp.where(inner_chip, second_inner, second_outer)
+        third = jnp.where(inner_chip, third_inner, outer(third_inner))
+
+        def column(chip, low):
+            within = jnp.where(t % 2 == low, piece, first)
+            beyond = jnp.where((t < 2) == (low == 0), second, third)
+            return jnp.where(chip == upper, within, beyond)
+
+        def wide(chip):
+            return jnp.concatenate([column(chip, core), column(chip, 1 - core)], axis=1)
+
+        return wide(x), wide(1 - x)
+
+    q_input, q_gate, q_up, q_outgrad = [
+        flatten(a) for a in (query_input, query_gate, query_up, query_outgrad)
+    ]
+    t_input, t_gate, t_up, t_outgrad = [
+        flatten(a) for a in (train_input, train_gate, train_up, train_outgrad)
+    ]
+    examples = train_lengths.shape[0] // 2
+    cut = examples * SEQ
+
+    weight_own, weight_sib = down_weight, to_core(down_weight)
+
+    far_gate, far_up = to_chip(t_gate[cut:]), to_chip(t_up[cut:])
+    q_hops = hop_two(*hop_one(q_outgrad))
+    a_hops = hop_one(after(t_outgrad[:cut], q_hops[3], far_gate))
+    q_near, q_send = hop_three(*q_hops)
+    q_far = to_chip(q_send)
+    a_hops = hop_two(a_hops[0], after(a_hops[1], q_send, far_up), a_hops[2])
+    b_hops = hop_one(after(t_outgrad[cut:], a_hops[3]))
+    a_near, a_send = hop_three(*a_hops)
+    a_far = to_chip(a_send)
+    q_near_sum, q_far_sum = partial_sums(q_near, q_far, weight_own, weight_sib)
+    b_hops = hop_two(b_hops[0], after(b_hops[1], a_send, q_far_sum), b_hops[2])
+    b_near, b_send = hop_three(*b_hops)
+    b_far = to_chip(b_send)
+
+    in_side, out_side, q_in_side, q_hidden_side, q_out_side = lax.psum(
         (
+            project(t_input, proj_input),
+            project(t_outgrad, proj_outgrad),
             project(q_input, proj_input),
             project(gated_hidden(q_gate, q_up), proj_hidden),
-            gate_side,
-            up_side,
             project(q_outgrad, proj_outgrad),
         ),
         "tensor",
     )
-    query_features = lax.all_gather(
-        features(*query_sides, query_lengths), "dp", axis=0, tiled=True
-    )
-
-    t_input, t_gate, t_up, t_outgrad = train_rows
-    in_side, out_side = lax.psum(
-        (project(t_input, proj_input), project(t_outgrad, proj_outgrad)), "tensor"
-    )
     hidden_side = project(gated_hidden(t_gate, t_up), proj_hidden)
-
-    pieces = 2
-    examples = train_lengths.shape[0] // pieces
-    partial = []
-    for piece in range(pieces):
-        part = slice(piece * examples * SEQ, (piece + 1) * examples * SEQ)
-        gate_side, up_side = gradient_sides(
-            t_gate[part], t_up[part], hidden_gradient(t_outgrad[part]), proj_gate, proj_up
-        )
-        piece_features = features(
-            in_side[part],
-            hidden_side[part],
-            gate_side,
-            up_side,
-            out_side[part],
-            train_lengths[piece * examples : (piece + 1) * examples],
-        )
-        partial.append(inner(piece_features, query_features))
-    scores = jnp.concatenate(partial, axis=0)
-    total = scores
-    for step in range(1, tensor):
-        turn = [(i, (i + step) % tensor) for i in range(tensor)]
-        total = total + lax.ppermute(scores, "tensor", turn)
-    return total / (RANK * SEQ)
+    far_in_side = to_chip(in_side[cut:])
+    far_lengths = to_chip(train_lengths[examples:])
+
+    query_sides = finished_sides(
+        q_near_sum, to_chip(q_far_sum), q_gate, q_up, proj_gate, proj_up
+    )
+    q_gate_side, q_up_side = jnp.split(
+        tensor_sum(jnp.concatenate(query_sides, axis=1)), 2, axis=1
+    )
+    own_query_features = features(
+        q_in_side, q_hidden_side, q_gate_side, q_up_side, q_out_side, query_lengths
+    )
+    query_features = lax.all_gather(own_query_features, "dp", axis=0, tiled=True)
+
+    a_near_sum, a_far_sum = partial_sums(
+        a_near, after(a_far, *query_sides), weight_own, weight_sib
+    )
+    a_gate_side, a_up_side = finished_sides(
+        a_near_sum, to_chip(a_far_sum), t_gate[:cut], t_up[:cut], proj_gate, proj_up
+    )
+    b_gate_side, b_up_side = lent_sides(
+        b_near,
+        after(b_far, own_query_features),
+        weight_own,
+        weight_sib,
+        t_gate[cut:],
+        t_up[cut:],
+        far_gate,
+        far_up,
+        proj_gate,
+        proj_up,
+    )
+    a_features = features(
+        in_side[:cut], hidden_side[:cut], a_gate_side, a_up_side, out_side[:cut],
+        train_lengths[:examples],
+    )
+    b_features = features(
+        in_side[cut:], hidden_side[cut:], b_gate_side[:cut], b_up_side[:cut], out_side[cut:],
+        train_lengths[examples:],
+    )
+    far_features = jnp.concatenate(
+        [
+            outer_sums(far_in_side, b_gate_side[cut:], far_lengths),
+            outer_sums(far_in_side, b_up_side[cut:], far_lengths),
+        ],
+        axis=1,
+    )
+    far_scores = inner(far_features, query_features[:, : far_features.shape[1]])
+    a_scores = inner(a_features, query_features)
+    b_scores = inner(b_features, query_features) + to_chip(far_scores)
+    scores = tensor_sum(jnp.concatenate([a_scores, b_scores], axis=0))
+    return scores / (RANK * SEQ)
 
 
 def solution(mesh):
@@ -229,7 +411,7 @@
 
     def per_device(*arguments):
         if tensor == 4 and dp == 4:
-            return moving_plan(tensor, *arguments)
+            return moving_plan(*arguments)
         return gathering_plan(*arguments)
 
     in_specs = (

time: 356 us -> 301 us (0.85)
  matrix products: 163 us -> 18.3 us
  Pallas kernels: 0 us -> 56.1 us
  local copies, waits for them, and re-layouts: 8.22 us -> 34.6 us
  starting transfers between devices: 72.2 us -> 59.4 us
  blocking collectives: 6.44 us -> 17.6 us
  waiting for transfers between devices: 73.2 us -> 81.1 us
  other arithmetic: 12.3 us -> 16.9 us
    dot_general x17 -> x5, matrix products: 145 us -> 7.39 us  [project(): lax.dot_general(rows, table, (((1,), (1,)), ((), ())), preferred_element_...]
    pallas_call x0 -> x5, Pallas kernels: none -> 56.1 us  [the longest x2 30.6 us: partial_sums(): pl.pallas_call(partial_kernel, grid=(units // TILE,), in_specs=[whole(nea...]
    ppermute x31 -> x30, waiting for transfers between devices: 38 us -> 68.6 us  [the longest x3 19.4 us: hop_three(): third = jnp.where(inner_chip, third_inner, outer(third_inner))]
    psum x2, waiting for transfers between devices: 35.1 us -> 12.4 us  [moving_plan(): lax.psum((project(t_input, proj_input), project(t_outgrad, proj_outgrad),...]
    ppermute x31 -> x30, starting transfers between devices: 72.1 us -> 59.3 us  [the longest x6 16.6 us: hop_one(): return (piece, outer(piece), middle(piece))]
    unnamed x65 -> x81, local copies, waits for them, and re-layouts: 0.41 us -> 11.6 us
    all_gather x1, blocking collectives: 6.44 us -> 17.6 us  [moving_plan(): lax.all_gather(own_query_features, 'dp', axis=0, tiled=True)]
    reshape x7 -> x1, matrix products: 11.7 us -> 1.87 us  [outer_sums(): right_rows = right_side.reshape(number, length, right_side.shape[1])]
  transfers between devices with their start and end apart: 33 -> 32, of which waited for: 20 -> 13; matrix products, arithmetic and copies ran while one was open for 46% -> 18% of each run, Pallas kernels for 0% -> 14%
where the time goes in v2:
time: 301 us; the launch traced here: 298 us
  waiting for transfers between devices  81.1 us (27%)
  starting transfers between devices  59.4 us (20%)
  Pallas kernels  56.1 us (19%)
  local copies, waits for them, and re-layouts  34.6 us (11%)
  matrix products  18.3 us (6%)
  blocking collectives  17.6 us (6%)
  other arithmetic  16.9 us (6%)
  between operations  13.9 us (5%)
    pallas_call x2, Pallas kernels, partial_sums(): pl.pallas_call(partial_kernel, grid=(units // TILE,), in_specs=[whole(nea...  30.6 us
    ppermute x3, waiting for transfers between devices, hop_three(): third = jnp.where(inner_chip, third_inner, outer(third_inner))  19.4 us
    all_gather x1, blocking collectives, moving_plan(): lax.all_gather(own_query_features, 'dp', axis=0, tiled=True)  17.6 us
    ppermute x6, starting transfers between devices, hop_one(): return (piece, outer(piece), middle(piece))  16.6 us
    pallas_call x1, Pallas kernels, lent_sides(): pl.pallas_call(lent_kernel, grid=(units // TILE,), in_specs=[whole(near.s...  15.7 us
    ppermute x6, starting transfers between devices, hop_two(): return (piece, first, second_inner, outer(second_inner), middle(first))  13.7 us
    ppermute x1, waiting for transfers between devices, moving_plan(): b_far = to_chip(b_send)  13.6 us
    ppermute x3, starting transfers between devices, hop_three(): third = jnp.where(inner_chip, third_inner, outer(third_inner))  12.6 us
  transfers between devices with their start and end apart: 32, of which 13 were waited for; matrix products, arithmetic and copies ran while one was open for 18% of the time, Pallas kernels for 14%

profile of v2, /device:TPU:0, one launch (start us, length us, event | category | flops | bytes accessed | tf_op | source)
XLA Modules:
  0.0 297.8 jit_solution(8411183073662828844)
XLA Ops:
  7.1 2.7 collective-permute-start.4
  9.7 5.3 %collective-permute-start = (bf16[128,2048]{1,0:T(8,128)(2,1)}, bf16[128,2048]{1,0:T(8,128)(2,1)}, u32[]{:S(2)}, u32[]{:S(2)}) collective-permute-start(bf16[128,2048]{1,0:T(8,128)(2,1)} %bitcast.86), channel_id=1, source_target_pairs={{0,0},{4,8},{8,4},{12,12},{1,1},{5,9},{9,5},{13,13},{2,2},{6,10},{... | collective-permute-start | bytes 1572872 | tf_op jit(solution)/shard_map/ppermute | solution.py:300
  15.1 2.6 fusion.59
  17.7 1.5 collective-permute-start.2
  20.8 2.1 fusion.10
  23.7 1.9 fusion.72
  25.6 2.0 fusion.68
  27.7 2.3 fusion.70
  30.0 3.3 %fusion.4 = bf16[256,3584]{1,0:T(8,128)(2,1)S(1)} fusion(bf16[4,64,3584]{2,1,0:T(8,128)(2,1)} %param.18, bf16[4,64,3584]{2,1,0:T(8,128)(2,1)} %param.17), kind=kLoop, calls=%fused_computation.6 | loop fusion | flops 7340032 | bytes 5505024 | tf_op jit(solution)/shard_map/convert_element_type | solution.py:39
  34.4 5.5 %collective-permute-start.5 = (bf16[128,2048]{1,0:T(8,128)(2,1)}, bf16[128,2048]{1,0:T(8,128)(2,1)}, u32[]{:S(2)}, u32[]{:S(2)}) collective-permute-start(bf16[128,2048]{1,0:T(8,128)(2,1)} %collective-permute-done.4), channel_id=1, source_target_pairs={{0,0},{4,8},{8,4},{12,12},{1,1},{5,9},{9,5},{13,13},{2,2},{6,10},{... | collective-permute-start | bytes 1572872 | tf_op jit(solution)/shard_map/ppermute | solution.py:303
  40.7 10.6 %collective-permute-start.6 = (bf16[128,2048]{1,0:T(8,128)(2,1)}, bf16[128,2048]{1,0:T(8,128)(2,1)}, u32[]{:S(2)}, u32[]{:S(2)}) collective-permute-start(bf16[128,2048]{1,0:T(8,128)(2,1)} %collective-permute-done.5), channel_id=1, source_target_pairs={{0,4},{4,0},{8,12},{12,8},{1,5},{5,1},{9,13},{13,9},{2,6},{6,2},{1... | collective-permute-start | bytes 1572872 | tf_op jit(solution)/shard_map/ppermute | solution.py:307
  52.9 2.1 fusion.60
  55.0 1.5 collective-permute-start.7
  56.5 1.8 collective-permute-done.1
  59.8 9.5 %collective-permute-done.6 = bf16[128,2048]{1,0:T(8,128)(2,1)} collective-permute-done((bf16[128,2048]{1,0:T(8,128)(2,1)}, bf16[128,2048]{1,0:T(8,128)(2,1)}, u32[]{:S(2)}, u32[]{:S(2)}) %collective-permute-start.6) | collective-permute-done | bytes 524320 | tf_op jit(solution)/shard_map/ppermute | solution.py:307
  71.0 2.3 broadcast_select_fusion.19
  74.3 1.9 collective-permute-done.7.far_up
  77.1 6.9 %collective-permute-done.3 = bf16[128,2048]{1,0:T(8,128)(2,1)S(1)} collective-permute-done((bf16[128,2048]{1,0:T(8,128)(2,1)S(1)}, bf16[128,2048]{1,0:T(8,128)(2,1)S(1)}, u32[]{:S(2)}, u32[]{:S(2)}) %collective-permute-start.3) | collective-permute-done | bytes 524320 | tf_op jit(solution)/shard_map/ppermute | solution.py:300
  87.2 12.4 %all-reduce.7.cloned.1.call-done = (f32[256,64]{0,1:T(8,128)}, f32[256,64]{0,1:T(8,128)}) async-done(((f32[256,64]{0,1:T(8,128)}, f32[256,64]{0,1:T(8,128)}), (f32[256,64]{0,1:T(8,128)}, f32[256,64]{0,1:T(8,128)})) %all-reduce.7.cloned.1.call-update) | async-done | bytes 131088 | tf_op jit(solution)/shard_map/psum | solution.py:344
  102.5 1.5 collective-permute-start.9
  107.4 10.2 %collective-permute-done.9 = bf16[128,2048]{1,0:T(8,128)(2,1)S(1)} collective-permute-done((bf16[128,2048]{1,0:T(8,128)(2,1)}, bf16[128,2048]{1,0:T(8,128)(2,1)S(1)}, u32[]{:S(2)}, u32[]{:S(2)}) %collective-permute-start.9) | collective-permute-done | bytes 524320 | tf_op jit(solution)/shard_map/ppermute | solution.py:303
  117.5 1.5 collective-permute-start.19
  119.0 9.8 %collective-permute-done.11 = bf16[128,2048]{1,0:T(8,128)(2,1)} collective-permute-done((bf16[128,2048]{1,0:T(8,128)(2,1)S(1)}, bf16[128,2048]{1,0:T(8,128)(2,1)}, u32[]{:S(2)}, u32[]{:S(2)}) %collective-permute-start.11) | collective-permute-done | bytes 524320 | tf_op jit(solution)/shard_map/ppermute | solution.py:307
  131.1 15.1 %shard_map.154 = (f32[128,3584]{1,0:T(8,128)S(1)}, bf16[128,3584]{1,0:T(8,128)(2,1)}) custom-call(bf16[128,4096]{1,0:T(8,128)(2,1)S(1)} %pad_maximum_fusion.3.near, bf16[128,4096]{1,0:T(8,128)(2,1)S(1)} %collective-permute-done.13.far, bf16[3584,2048]{1,0:T(8,128)(2,1)} %weight_own.5, bf16[3584,2048]{1,0:T(8,128)(2,1)} %collective-permute-done.14.weight_sib), custom_call_target="tpu_custom_call" | custom-call | flops 7516192768 | bytes 31457280 | tf_op jit(solution)/shard_map/pallas_call | solution.py:202
  150.5 1.5 reshape.223
  152.0 1.6 reshape.230
  154.3 1.5 reshape.202
  155.8 1.5 reshape.231
  157.2 5.4 %collective-permute-start.20 = (bf16[128,2048]{1,0:T(8,128)(2,1)}, bf16[128,2048]{1,0:T(8,128)(2,1)}, u32[]{:S(2)}, u32[]{:S(2)}) collective-permute-start(bf16[128,2048]{1,0:T(8,128)(2,1)} %bitcast.21), channel_id=1, source_target_pairs={{0,0},{4,8},{8,4},{12,12},{1,1},{5,9},{9,5},{13,13},{2,2},{6,10},{... | collective-permute-start | bytes 1572872 | tf_op jit(solution)/shard_map/ppermute | solution.py:300
  162.6 5.4 %collective-permute-start.22 = (bf16[128,2048]{1,0:T(8,128)(2,1)}, bf16[128,2048]{1,0:T(8,128)(2,1)}, u32[]{:S(2)}, u32[]{:S(2)}) collective-permute-start(bf16[128,2048]{1,0:T(8,128)(2,1)} %collective-permute-done.19), channel_id=1, source_target_pairs={{0,0},{4,8},{8,4},{12,12},{1,1},{5,9},{9,5},{13,13},{2,2},{6,10},{... | collective-permute-start | bytes 1572872 | tf_op jit(solution)/shard_map/ppermute | solution.py:303
  168.0 1.9 collective-permute-done.15.returned
  172.3 4.9 %shard_map.155 = (f32[128,64]{1,0:T(8,128)S(1)}, f32[128,64]{1,0:T(8,128)S(1)}) custom-call(f32[128,3584]{1,0:T(8,128)S(1)} %get-tuple-element.23.near_sum, bf16[128,3584]{1,0:T(8,128)(2,1)} %collective-permute-done.15.returned, bf16[128,3584]{1,0:T(8,128)(2,1)S(1)} %bitcast.80, bf16[128,3584]{1,0:T(8,128)(2,1)S(1)} %bitcast.82, ...), custom_call_target="tpu_custom_call" | custom-call | flops 117440512 | bytes 5505024 | tf_op jit(solution)/shard_map/pallas_call | solution.py:222
  177.3 1.6 collective-permute-start.17
  179.6 1.5 collective-permute-start.23
  181.1 4.8 %collective-permute-done.12.far = bf16[128,4096]{1,0:T(8,128)(2,1)} collective-permute-done((bf16[128,4096]{1,0:T(8,128)(2,1)}, bf16[128,4096]{1,0:T(8,128)(2,1)}, u32[]{:S(2)}, u32[]{:S(2)}) %collective-permute-start.12) | collective-permute-done | bytes 1048608 | tf_op jit(solution)/shard_map/ppermute | solution.py:338
  186.0 2.1 collective-permute-start.18
  188.1 15.4 %shard_map.156 = (f32[128,3584]{1,0:T(8,128)S(1)}, bf16[128,3584]{1,0:T(8,128)(2,1)}) custom-call(bf16[128,4096]{1,0:T(8,128)(2,1)S(1)} %pad_maximum_fusion.1.near, bf16[128,4096]{1,0:T(8,128)(2,1)} %collective-permute-done.12.far, bf16[3584,2048]{1,0:T(8,128)(2,1)} %weight_own.5, bf16[3584,2048]{1,0:T(8,128)(2,1)} %collective-permute-done.14.weight_sib), custom_call_target="tpu_custom_call" | custom-call | flops 7516192768 | bytes 31457280 | tf_op jit(solution)/shard_map/pallas_call | solution.py:202
  206.1 17.6 %all-gather = f32[4,2,12288]{2,1,0:T(2,128)S(1)} all-gather(f32[1,2,12288]{2,1,0:T(2,128)S(1)} %bitcast.103), channel_id=1, replica_groups=mesh['parts'=2,'tensor'=4,'dp'=4] {'dp'}, dimensions={0}, use_global_device_ids=true | all-gather | bytes 491520 | tf_op jit(solution)/shard_map/all_gather | solution.py:367
  228.9 4.9 %shard_map.157 = (f32[128,64]{1,0:T(8,128)S(1)}, f32[128,64]{1,0:T(8,128)S(1)}) custom-call(f32[128,3584]{1,0:T(8,128)S(1)} %copy-done.11, bf16[128,3584]{1,0:T(8,128)(2,1)} %collective-permute-done.16.returned, bf16[128,3584]{1,0:T(8,128)(2,1)S(1)} %bitcast.75, bf16[128,3584]{1,0:T(8,128)(2,1)S(1)} %bitcast.78, bf16[64,3584]{1,0:T(8,128)(2,1)S(1)} %copy-done.2, ...), custom_call_target="tpu_custom_call" | custom-call | flops 117440512 | bytes 5505024 | tf_op jit(solution)/shard_map/pallas_call | solution.py:222
  234.7 1.5 reshape.209
  238.0 1.7 fusion.14
  239.7 13.6 %collective-permute-done.24.far = bf16[128,4096]{1,0:T(8,128)(2,1)S(1)} collective-permute-done((bf16[128,4096]{1,0:T(8,128)(2,1)}, bf16[128,4096]{1,0:T(8,128)(2,1)S(1)}, u32[]{:S(2)}, u32[]{:S(2)}) %collective-permute-start.24) | collective-permute-done | bytes 1048608 | tf_op jit(solution)/shard_map/ppermute | solution.py:342
  259.0 15.7 %shard_map.158 = (f32[256,64]{1,0:T(8,128)S(1)}, f32[256,64]{1,0:T(8,128)S(1)}) custom-call(bf16[128,4096]{1,0:T(8,128)(2,1)S(1)} %pad_maximum_fusion.4.near, bf16[128,4096]{1,0:T(8,128)(2,1)S(1)} %copy-done.13, bf16[3584,2048]{1,0:T(8,128)(2,1)} %weight_own.5, bf16[3584,2048]{1,0:T(8,128)(2,1)} %collective-permute-done.14.weight_sib, ...), custom_call_target="tpu_custom_call" | custom-call | flops 7516192768 | bytes 36044800 | tf_op jit(solution)/shard_map/pallas_call | solution.py:242
  277.0 2.6 collective-permute-done.27
  279.6 1.8 convolution_add_fusion
  281.4 2.8 collective-permute-start.28
  284.2 1.6 collective-permute-done.28
  286.3 4.1 %collective-permute-done.29 = f32[4,8]{1,0:T(4,128)S(1)} collective-permute-done((f32[4,8]{1,0:T(4,128)S(1)}, f32[4,8]{1,0:T(4,128)S(1)}, u32[]{:S(2)}, u32[]{:S(2)}) %collective-permute-start.29) | collective-permute-done | bytes 160 | tf_op jit(solution)/shard_map/ppermute | solution.py:297
  (179 shorter events, 50.7 us)
Async XLA Ops:
  6.5 19.1 %copy-start = (bf16[4,64,2048]{2,1,0:T(8,128)(2,1)S(1)}, bf16[4,64,2048]{2,1,0:T(8,128)(2,1)}, u32[]{:S(2)}) copy-start(bf16[4,64,2048]{2,1,0:T(8,128)(2,1)} %param.16) | copy-start | bytes 3145732
  6.5 12.6 %copy-start.37 = (s32[4]{0:T(128)S(1)}, s32[4]{0:T(128)}, u32[]{:S(2)}) copy-start(s32[4]{0:T(128)} %param.20) | copy-start | bytes 52
  6.5 13.2 %copy-start.24 = (bf16[64,2048]{1,0:T(8,128)(2,1)S(1)}, bf16[64,2048]{1,0:T(8,128)(2,1)}, u32[]{:S(2)}) copy-start(bf16[64,2048]{1,0:T(8,128)(2,1)} %param.27) | copy-start | bytes 786436
  6.5 78.9 %all-reduce.5.cloned.1.call-start = ((), (), s32[]{:S(2)}) async-start(), calls=%async_computation | async-start | bytes 393216 | tf_op jit(solution)/shard_map/psum | solution.py:344
  6.5 13.2 %copy-start.29 = (bf16[2,64,2048]{2,1,0:T(8,128)(2,1)S(1)}, bf16[2,64,2048]{2,1,0:T(8,128)(2,1)}, u32[]{:S(2)}) copy-start(bf16[2,64,2048]{2,1,0:T(8,128)(2,1)} %param.21) | copy-start | bytes 1572868
  6.6 124.5 %collective-permute-start.14 = (bf16[3584,2048]{1,0:T(8,128)(2,1)}, bf16[3584,2048]{1,0:T(8,128)(2,1)}, u32[]{:S(2)}, u32[]{:S(2)}) collective-permute-start(bf16[3584,2048]{1,0:T(8,128)(2,1)} %weight_own.5), channel_id=1, source_target_pairs={{0,1},{1,0},{2,3},{3,2},{4,5},{5,4},{6,7},{7,6},{8,9},{9,8},{10,11... | collective-permute-start | bytes 44040200 | tf_op jit(solution)/shard_map/ppermute | solution.py:328
  7.1 13.8 %copy-start.14 = (bf16[2,64,3584]{2,1,0:T(8,128)(2,1)S(1)}, bf16[2,64,3584]{2,1,0:T(8,128)(2,1)}, u32[]{:S(2)}) copy-start(bf16[2,64,3584]{2,1,0:T(8,128)(2,1)} %param.22) | copy-start | bytes 2752516
  7.1 27.3 %collective-permute-start.4 = (bf16[128,2048]{1,0:T(8,128)(2,1)}, bf16[128,2048]{1,0:T(8,128)(2,1)}, u32[]{:S(2)}, u32[]{:S(2)}) collective-permute-start(bf16[128,2048]{1,0:T(8,128)(2,1)} %bitcast.85), channel_id=1, source_target_pairs={{0,4},{4,0},{8,12},{12,8},{1,5},{5,1},{9,13},{13,9},{2,6},{6,2},{1... | collective-permute-start | bytes 1572872 | tf_op jit(solution)/shard_map/ppermute | solution.py:300
  9.7 30.9 %collective-permute-start = (bf16[128,2048]{1,0:T(8,128)(2,1)}, bf16[128,2048]{1,0:T(8,128)(2,1)}, u32[]{:S(2)}, u32[]{:S(2)}) collective-permute-start(bf16[128,2048]{1,0:T(8,128)(2,1)} %bitcast.86), channel_id=1, source_target_pairs={{0,0},{4,8},{8,4},{12,12},{1,1},{5,9},{9,5},{13,13},{2,2},{6,10},{... | collective-permute-start | bytes 1572872 | tf_op jit(solution)/shard_map/ppermute | solution.py:300
  17.7 37.3 %collective-permute-start.2 = (bf16[128,3584]{1,0:T(8,128)(2,1)S(1)}, bf16[128,3584]{1,0:T(8,128)(2,1)}, u32[]{:S(2)}, u32[]{:S(2)}) collective-permute-start(bf16[128,3584]{1,0:T(8,128)(2,1)S(1)} %bitcast.73), channel_id=1, source_target_pairs={{0,2},{1,3},{2,0},{3,1},{4,6},{5,7},{6,4},{7,5},{8,10},{9,11},{10,... | collective-permute-start | bytes 2752520 | tf_op jit(solution)/shard_map/ppermute | solution.py:330
  19.2 65.4 %collective-permute-start.26 = (s32[2]{0:T(128)S(1)}, s32[2]{0:T(128)}, u32[]{:S(2)}, u32[]{:S(2)}) collective-permute-start(s32[2]{0:T(128)S(1)} %get-tuple-element.79), channel_id=1, source_target_pairs={{0,2},{1,3},{2,0},{3,1},{4,6},{5,7},{6,4},{7,5},{8,10},{9,11},{10,... | collective-permute-start | bytes 32 | tf_op jit(solution)/shard_map/ppermute | solution.py:356
  25.6 74.0 %all-reduce.7.cloned.1.call-start = ((), (), s32[]{:S(2)}) async-start(), calls=%async_computation.1 | async-start | bytes 262144 | tf_op jit(solution)/shard_map/psum | solution.py:344
  34.4 20.6 %copy-start.7 = (bf16[2,64,3584]{2,1,0:T(8,128)(2,1)}, bf16[2,64,3584]{2,1,0:T(8,128)(2,1)S(1)}, u32[]{:S(2)}) copy-start(bf16[2,64,3584]{2,1,0:T(8,128)(2,1)S(1)} %get-tuple-element.61) | copy-start | bytes 2752516
  34.4 16.9 %copy-start.38 = (s32[2]{0:T(128)S(1)}, s32[2]{0:T(128)}, u32[]{:S(2)}) copy-start(s32[2]{0:T(128)} %param.25) | copy-start | bytes 28
  34.4 6.3 %collective-permute-start.5 = (bf16[128,2048]{1,0:T(8,128)(2,1)}, bf16[128,2048]{1,0:T(8,128)(2,1)}, u32[]{:S(2)}, u32[]{:S(2)}) collective-permute-start(bf16[128,2048]{1,0:T(8,128)(2,1)} %collective-permute-done.4), channel_id=1, source_target_pairs={{0,0},{4,8},{8,4},{12,12},{1,1},{5,9},{9,5},{13,13},{2,2},{6,10},{... | collective-permute-start | bytes 1572872 | tf_op jit(solution)/shard_map/ppermute | solution.py:303
  40.7 17.6 %collective-permute-start.1 = (bf16[128,2048]{1,0:T(8,128)(2,1)}, bf16[128,2048]{1,0:T(8,128)(2,1)}, u32[]{:S(2)}, u32[]{:S(2)}) collective-permute-start(bf16[128,2048]{1,0:T(8,128)(2,1)} %collective-permute-done), channel_id=1, source_target_pairs={{0,4},{4,0},{8,12},{12,8},{1,5},{5,1},{9,13},{13,9},{2,6},{6,2},{1... | collective-permute-start | bytes 1572872 | tf_op jit(solution)/shard_map/ppermute | solution.py:303
  40.7 28.6 %collective-permute-start.6 = (bf16[128,2048]{1,0:T(8,128)(2,1)}, bf16[128,2048]{1,0:T(8,128)(2,1)}, u32[]{:S(2)}, u32[]{:S(2)}) collective-permute-start(bf16[128,2048]{1,0:T(8,128)(2,1)} %collective-permute-done.5), channel_id=1, source_target_pairs={{0,4},{4,0},{8,12},{12,8},{1,5},{5,1},{9,13},{13,9},{2,6},{6,2},{1... | collective-permute-start | bytes 1572872 | tf_op jit(solution)/shard_map/ppermute | solution.py:307
  55.0 21.2 %collective-permute-start.7 = (bf16[128,3584]{1,0:T(8,128)(2,1)S(1)}, bf16[128,3584]{1,0:T(8,128)(2,1)S(1)}, u32[]{:S(2)}, u32[]{:S(2)}) collective-permute-start(bf16[128,3584]{1,0:T(8,128)(2,1)S(1)} %bitcast.76), channel_id=1, source_target_pairs={{0,2},{1,3},{2,0},{3,1},{4,6},{5,7},{6,4},{7,5},{8,10},{9,11},{10,... | collective-permute-start | bytes 2752520 | tf_op jit(solution)/shard_map/ppermute | solution.py:330
  58.3 44.2 %collective-permute-start.8 = (bf16[128,2048]{1,0:T(8,128)(2,1)S(1)}, bf16[128,2048]{1,0:T(8,128)(2,1)}, u32[]{:S(2)}, u32[]{:S(2)}) collective-permute-start(bf16[128,2048]{1,0:T(8,128)(2,1)S(1)} %bitcast.88), channel_id=1, source_target_pairs={{0,0},{4,8},{8,4},{12,12},{1,1},{5,9},{9,5},{13,13},{2,2},{6,10},{... | collective-permute-start | bytes 1572872 | tf_op jit(solution)/shard_map/ppermute | solution.py:300
  69.3 14.7 %collective-permute-start.3 = (bf16[128,2048]{1,0:T(8,128)(2,1)S(1)}, bf16[128,2048]{1,0:T(8,128)(2,1)S(1)}, u32[]{:S(2)}, u32[]{:S(2)}) collective-permute-start(bf16[128,2048]{1,0:T(8,128)(2,1)S(1)} %bitcast.89), channel_id=1, source_target_pairs={{0,4},{4,0},{8,12},{12,8},{1,5},{5,1},{9,13},{13,9},{2,6},{6,2},{1... | collective-permute-start | bytes 1572872 | tf_op jit(solution)/shard_map/ppermute | solution.py:300
  73.3 34.0 %copy-start.21 = (bf16[128,2048]{1,0:T(8,128)(2,1)S(1)}, bf16[128,2048]{1,0:T(8,128)(2,1)}, u32[]{:S(2)}) copy-start(bf16[128,2048]{1,0:T(8,128)(2,1)} %get-tuple-element.58) | copy-start | bytes 1572868
  73.3 34.0 %copy-start.22 = (bf16[128,2048]{1,0:T(8,128)(2,1)S(1)}, bf16[128,2048]{1,0:T(8,128)(2,1)}, u32[]{:S(2)}) copy-start(bf16[128,2048]{1,0:T(8,128)(2,1)} %get-tuple-element.59) | copy-start | bytes 1572868
  84.0 20.0 %collective-permute-start.10 = (bf16[128,2048]{1,0:T(8,128)(2,1)S(1)}, bf16[128,2048]{1,0:T(8,128)(2,1)S(1)}, u32[]{:S(2)}, u32[]{:S(2)}) collective-permute-start(bf16[128,2048]{1,0:T(8,128)(2,1)S(1)} %collective-permute-done.3), channel_id=1, source_target_pairs={{0,0},{4,8},{8,4},{12,12},{1,1},{5,9},{9,5},{13,13},{2,2},{6,10},{... | collective-permute-start | bytes 1572872 | tf_op jit(solution)/shard_map/ppermute | solution.py:303
  101.0 54.8 %collective-permute-start.25 = (f32[128,64]{0,1:T(8,128)}, f32[128,64]{0,1:T(8,128)}, u32[]{:S(2)}, u32[]{:S(2)}) collective-permute-start(f32[128,64]{0,1:T(8,128)} %get-tuple-element.71), channel_id=1, source_target_pairs={{0,2},{1,3},{2,0},{3,1},{4,6},{5,7},{6,4},{7,5},{8,10},{9,11},{10,... | collective-permute-start | bytes 98312 | tf_op jit(solution)/shard_map/ppermute | solution.py:355
  102.5 15.1 %collective-permute-start.9 = (bf16[128,2048]{1,0:T(8,128)(2,1)}, bf16[128,2048]{1,0:T(8,128)(2,1)S(1)}, u32[]{:S(2)}, u32[]{:S(2)}) collective-permute-start(bf16[128,2048]{1,0:T(8,128)(2,1)} %collective-permute-done.8), channel_id=1, source_target_pairs={{0,4},{4,0},{8,12},{12,8},{1,5},{5,1},{9,13},{13,9},{2,6},{6,2},{1... | collective-permute-start | bytes 1572872 | tf_op jit(solution)/shard_map/ppermute | solution.py:303
  104.0 24.9 %collective-permute-start.11 = (bf16[128,2048]{1,0:T(8,128)(2,1)S(1)}, bf16[128,2048]{1,0:T(8,128)(2,1)}, u32[]{:S(2)}, u32[]{:S(2)}) collective-permute-start(bf16[128,2048]{1,0:T(8,128)(2,1)S(1)} %collective-permute-done.10), channel_id=1, source_target_pairs={{0,4},{4,0},{8,12},{12,8},{1,5},{5,1},{9,13},{13,9},{2,6},{6,2},{1... | collective-permute-start | bytes 1572872 | tf_op jit(solution)/shard_map/ppermute | solution.py:307
  106.7 24.3 %collective-permute-start.13 = (bf16[128,4096]{1,0:T(8,128)(2,1)}, bf16[128,4096]{1,0:T(8,128)(2,1)S(1)}, u32[]{:S(2)}, u32[]{:S(2)}) collective-permute-start(bf16[128,4096]{1,0:T(8,128)(2,1)} %pad_maximum_fusion), channel_id=1, source_target_pairs={{0,2},{1,3},{2,0},{3,1},{4,6},{5,7},{6,4},{7,5},{8,10},{9,11},{10,... | collective-permute-start | bytes 3145736 | tf_op jit(solution)/shard_map/ppermute | solution.py:334
  117.5 45.1 %collective-permute-start.19 = (bf16[128,2048]{1,0:T(8,128)(2,1)}, bf16[128,2048]{1,0:T(8,128)(2,1)}, u32[]{:S(2)}, u32[]{:S(2)}) collective-permute-start(bf16[128,2048]{1,0:T(8,128)(2,1)} %bitcast.21), channel_id=1, source_target_pairs={{0,4},{4,0},{8,12},{12,8},{1,5},{5,1},{9,13},{13,9},{2,6},{6,2},{1... | collective-permute-start | bytes 1572872 | tf_op jit(solution)/shard_map/ppermute | solution.py:300
  146.2 23.7 %copy-start.2 = (bf16[64,3584]{1,0:T(8,128)(2,1)S(1)}, bf16[64,3584]{1,0:T(8,128)(2,1)}, u32[]{:S(2)}) copy-start(bf16[64,3584]{1,0:T(8,128)(2,1)} %proj_gate.5) | copy-start | bytes 1376260
  146.2 23.7 %copy-start.3 = (bf16[64,3584]{1,0:T(8,128)(2,1)S(1)}, bf16[64,3584]{1,0:T(8,128)(2,1)}, u32[]{:S(2)}) copy-start(bf16[64,3584]{1,0:T(8,128)(2,1)} %proj_up.5) | copy-start | bytes 1376260
  146.2 23.7 %collective-permute-start.15 = (bf16[128,3584]{1,0:T(8,128)(2,1)}, bf16[128,3584]{1,0:T(8,128)(2,1)}, u32[]{:S(2)}, u32[]{:S(2)}) collective-permute-start(bf16[128,3584]{1,0:T(8,128)(2,1)} %get-tuple-element.24), channel_id=1, source_target_pairs={{0,2},{1,3},{2,0},{3,1},{4,6},{5,7},{6,4},{7,5},{8,10},{9,11},{10,... | collective-permute-start | bytes 2752520 | tf_op jit(solution)/shard_map/ppermute | solution.py:359
  148.0 37.9 %collective-permute-start.12 = (bf16[128,4096]{1,0:T(8,128)(2,1)}, bf16[128,4096]{1,0:T(8,128)(2,1)}, u32[]{:S(2)}, u32[]{:S(2)}) collective-permute-start(bf16[128,4096]{1,0:T(8,128)(2,1)} %pad_maximum_fusion.2), channel_id=1, source_target_pairs={{0,2},{1,3},{2,0},{3,1},{4,6},{5,7},{6,4},{7,5},{8,10},{9,11},{10,... | collective-permute-start | bytes 3145736 | tf_op jit(solution)/shard_map/ppermute | solution.py:338
  157.2 21.7 %collective-permute-start.20 = (bf16[128,2048]{1,0:T(8,128)(2,1)}, bf16[128,2048]{1,0:T(8,128)(2,1)}, u32[]{:S(2)}, u32[]{:S(2)}) collective-permute-start(bf16[128,2048]{1,0:T(8,128)(2,1)} %bitcast.21), channel_id=1, source_target_pairs={{0,0},{4,8},{8,4},{12,12},{1,1},{5,9},{9,5},{13,13},{2,2},{6,10},{... | collective-permute-start | bytes 1572872 | tf_op jit(solution)/shard_map/ppermute | solution.py:300
  162.6 16.9 %collective-permute-start.22 = (bf16[128,2048]{1,0:T(8,128)(2,1)}, bf16[128,2048]{1,0:T(8,128)(2,1)}, u32[]{:S(2)}, u32[]{:S(2)}) collective-permute-start(bf16[128,2048]{1,0:T(8,128)(2,1)} %collective-permute-done.19), channel_id=1, source_target_pairs={{0,0},{4,8},{8,4},{12,12},{1,1},{5,9},{9,5},{13,13},{2,2},{6,10},{... | collective-permute-start | bytes 1572872 | tf_op jit(solution)/shard_map/ppermute | solution.py:303
  177.3 8.6 %collective-permute-start.17 = (f32[128,128]{1,0:T(8,128)S(1)}, f32[128,128]{1,0:T(8,128)S(1)}, u32[]{:S(2)}, u32[]{:S(2)}) collective-permute-start(f32[128,128]{1,0:T(8,128)S(1)} %pad_maximum_fusion.6), channel_id=1, source_target_pairs={{0,4},{4,0},{8,12},{12,8},{1,5},{5,1},{9,13},{13,9},{2,6},{6,2},{1... | collective-permute-start | bytes 196616 | tf_op jit(solution)/shard_map/ppermute | solution.py:296
  179.0 44.9 %collective-permute-start.21 = (bf16[128,2048]{1,0:T(8,128)(2,1)}, bf16[128,2048]{1,0:T(8,128)(2,1)S(1)}, u32[]{:S(2)}, u32[]{:S(2)}) collective-permute-start(bf16[128,2048]{1,0:T(8,128)(2,1)} %collective-permute-done.20), channel_id=1, source_target_pairs={{0,4},{4,0},{8,12},{12,8},{1,5},{5,1},{9,13},{13,9},{2,6},{6,2},{1... | collective-permute-start | bytes 1572872 | tf_op jit(solution)/shard_map/ppermute | solution.py:303
  179.6 44.4 %collective-permute-start.23 = (bf16[128,2048]{1,0:T(8,128)(2,1)}, bf16[128,2048]{1,0:T(8,128)(2,1)S(1)}, u32[]{:S(2)}, u32[]{:S(2)}) collective-permute-start(bf16[128,2048]{1,0:T(8,128)(2,1)} %collective-permute-done.22), channel_id=1, source_target_pairs={{0,4},{4,0},{8,12},{12,8},{1,5},{5,1},{9,13},{13,9},{2,6},{6,2},{1... | collective-permute-start | bytes 1572872 | tf_op jit(solution)/shard_map/ppermute | solution.py:307
  186.0 19.4 %copy-start.31 = (f32[2,64,64]{1,2,0:T(8,128)S(1)}, f32[2,64,64]{1,2,0:T(8,128)}, u32[]{:S(2)}) copy-start(f32[2,64,64]{1,2,0:T(8,128)} %get-tuple-element.37) | copy-start | bytes 98308
  186.0 20.1 %copy-start.36 = (f32[2,4096]{1,0:T(2,128)S(1)}, f32[2,4096]{1,0:T(2,128)}, u32[]{:S(2)}) copy-start(f32[2,4096]{1,0:T(2,128)} %reshape.222) | copy-start | bytes 98308
  186.0 19.3 %collective-permute-start.18 = (f32[128,128]{1,0:T(8,128)S(1)}, f32[128,128]{1,0:T(8,128)S(1)}, u32[]{:S(2)}, u32[]{:S(2)}) collective-permute-start(f32[128,128]{1,0:T(8,128)S(1)} %fusion.97), channel_id=1, source_target_pairs={{0,8},{4,12},{8,0},{12,4},{1,9},{5,13},{9,1},{13,5},{2,10},{6,14},... | collective-permute-start | bytes 196616 | tf_op jit(solution)/shard_map/ppermute | solution.py:297
  204.8 23.2 %collective-permute-start.16 = (bf16[128,3584]{1,0:T(8,128)(2,1)}, bf16[128,3584]{1,0:T(8,128)(2,1)}, u32[]{:S(2)}, u32[]{:S(2)}) collective-permute-start(bf16[128,3584]{1,0:T(8,128)(2,1)} %get-tuple-element.29), channel_id=1, source_target_pairs={{0,2},{1,3},{2,0},{3,1},{4,6},{5,7},{6,4},{7,5},{8,10},{9,11},{10,... | collective-permute-start | bytes 2752520 | tf_op jit(solution)/shard_map/ppermute | solution.py:373
  227.6 25.6 %collective-permute-start.24 = (bf16[128,4096]{1,0:T(8,128)(2,1)}, bf16[128,4096]{1,0:T(8,128)(2,1)S(1)}, u32[]{:S(2)}, u32[]{:S(2)}) collective-permute-start(bf16[128,4096]{1,0:T(8,128)(2,1)} %pad_maximum_fusion.5), channel_id=1, source_target_pairs={{0,2},{1,3},{2,0},{3,1},{4,6},{5,7},{6,4},{7,5},{8,10},{9,11},{10,... | collective-permute-start | bytes 3145736 | tf_op jit(solution)/shard_map/ppermute | solution.py:342
  259.0 15.8 %copy-start.27 = (f32[2,64,64]{1,0,2:T(2,128)S(1)}, f32[2,64,64]{1,0,2:T(2,128)}, u32[]{:S(2)}) copy-start(f32[2,64,64]{1,0,2:T(2,128)} %reshape.231) | copy-start | bytes 98308
  259.0 17.4 %copy-start.26 = (f32[2,64,64]{1,0,2:T(2,128)S(1)}, f32[2,64,64]{1,0,2:T(2,128)}, u32[]{:S(2)}) copy-start(f32[2,64,64]{1,0,2:T(2,128)} %reshape.223) | copy-start | bytes 98308
  259.0 31.9 %copy-start.1 = (bf16[4,64,2048]{2,1,0:T(8,128)(2,1)S(1)}, bf16[4,64,2048]{2,1,0:T(8,128)(2,1)}, u32[]{:S(2)}) copy-start(bf16[4,64,2048]{2,1,0:T(8,128)(2,1)} %param.16) | copy-start | bytes 3145732
  276.0 3.6 %collective-permute-start.27 = (f32[2,8]{1,0:T(2,128)S(1)}, f32[2,8]{1,0:T(2,128)S(1)}, u32[]{:S(2)}, u32[]{:S(2)}) collective-permute-start(f32[2,8]{1,0:T(2,128)S(1)} %fusion.12), channel_id=1, source_target_pairs={{0,2},{1,3},{2,0},{3,1},{4,6},{5,7},{6,4},{7,5},{8,10},{9,11},{10,... | collective-permute-start | bytes 200 | tf_op jit(solution)/shard_map/ppermute | solution.py:404
  281.4 4.4 %collective-permute-start.28 = (f32[4,8]{1,0:T(4,128)S(1)}, f32[4,8]{1,0:T(4,128)S(1)}, u32[]{:S(2)}, u32[]{:S(2)}) collective-permute-start(f32[4,8]{1,0:T(4,128)S(1)} %pad_maximum_fusion.7), channel_id=1, source_target_pairs={{0,4},{4,0},{8,12},{12,8},{1,5},{5,1},{9,13},{13,9},{2,6},{6,2},{1... | collective-permute-start | bytes 392 | tf_op jit(solution)/shard_map/ppermute | solution.py:296
  285.8 4.5 %collective-permute-start.29 = (f32[4,8]{1,0:T(4,128)S(1)}, f32[4,8]{1,0:T(4,128)S(1)}, u32[]{:S(2)}, u32[]{:S(2)}) collective-permute-start(f32[4,8]{1,0:T(4,128)S(1)} %fusion.57), channel_id=1, source_target_pairs={{0,8},{4,12},{8,0},{12,4},{1,9},{5,13},{9,1},{13,5},{2,10},{6,14},... | collective-permute-start | bytes 392 | tf_op jit(solution)/shard_map/ppermute | solution.py:297
  (23 other events, 65.2 us)
Sparse Core Ops, SparseCore 0:
  25.7 36.2 all-reduce.4
  64.5 35.0 all-reduce.6

commit v3 on v1

--- a/solution.py
+++ b/solution.py
@@ -1,10 +1,16 @@
+import functools
+
 import jax
 import jax.numpy as jnp
 from jax import lax
+from jax.experimental import pallas as pl
+from jax.experimental.pallas import tpu as pltpu
 from jax.sharding import PartitionSpec as P
 
 RANK = 64
 SEQ = 64
+TILE = 512
+VMEM_BYTES = 40 * 1024 * 1024
 
 
 def flatten(array):
@@ -111,15 +117,312 @@
     return inner(train_features, gathered) / (RANK * SEQ)
 
 
-def pick(blocks, index):
-    chosen = blocks[0]
-    for number in range(1, len(blocks)):
-        chosen = jnp.where(index == number, blocks[number], chosen)
-    return chosen
+ANYWHERE = pl.BlockSpec(memory_space=pl.ANY)
+SCALARS = pl.BlockSpec(memory_space=pltpu.SMEM)
+IN_VMEM = pl.BlockSpec(memory_space=pltpu.VMEM)
+
+
+def params():
+    return pltpu.CompilerParams(vmem_limit_bytes=VMEM_BYTES)
+
+
+def cost(flops, arrays):
+    moved = sum(array.size * array.dtype.itemsize for array in arrays)
+    return pl.CostEstimate(flops=flops, bytes_accessed=moved, transcendentals=0)
+
+
+def tile_columns(number, block=0):
+    return pl.BlockSpec((number, TILE), lambda i: (block, i))
+
+
+def tile_rows(width):
+    return pl.BlockSpec((TILE, width), lambda i: (i, 0))
+
+
+def whole(shape):
+    return pl.BlockSpec(shape, lambda i: tuple(0 for _ in shape))
+
+
+def stacked_products(flags, pairs, far, weight_own, weight_sib, stacked, semaphores):
+    number = far.shape[1]
+
+    @pl.when(pl.program_id(0) == 0)
+    def _():
+        slot = flags[1]
+        far_copies = [
+            pltpu.make_async_copy(
+                far.at[i], stacked.at[jnp.bitwise_xor(slot, i), pl.ds(number, number)],
+                semaphores.at[2 + i],
+            )
+            for i in range(2)
+        ]
+        for copy in far_copies:
+            copy.start()
+        for code, pair in enumerate(pairs):
+
+            @pl.when(flags[0] == code)
+            def _():
+                copies = [
+                    pltpu.make_async_copy(
+                        pair[i], stacked.at[jnp.bitwise_xor(slot, i), pl.ds(0, number)],
+                        semaphores.at[i],
+                    )
+                    for i in range(2)
+                ]
+                for copy in copies:
+                    copy.start()
+                for copy in copies:
+                    copy.wait()
+
+        for copy in far_copies:
+            copy.wait()
+
+    return project(weight_own[...], stacked[0]) + project(weight_sib[...], stacked[1])
+
+
+def add_sides(hidden_grad, gate, up, proj_gate, proj_up, sides):
+    gate_part, up_part = gradient_sides(gate, up, hidden_grad, proj_gate, proj_up)
+    part = jnp.concatenate([gate_part, up_part], axis=1)
+    first = pl.program_id(0) == 0
+
+    @pl.when(first)
+    def _():
+        sides[...] = part
+
+    @pl.when(jnp.logical_not(first))
+    def _():
+        sides[...] += part
+
+
+def partial_kernel(
+    flags, b0, b1, b2, b3, b4, b5, far, weight_own, weight_sib, near_sum, far_sum, stacked, sems
+):
+    pairs = ((b0, b1), (b2, b3), (b4, b5))
+    total = stacked_products(flags, pairs, far, weight_own, weight_sib, stacked, sems)
+    number = far.shape[1]
+    near_sum[...] = total[:, :number]
+    far_sum[...] = total[:, number:].astype(jnp.bfloat16)
+
+
+def partial_sums(flags, blocks, far, weight_own, weight_sib):
+    number, half = blocks[0].shape
+    units = weight_own.shape[0]
+    return pl.pallas_call(
+        partial_kernel,
+        grid=(units // TILE,),
+        in_specs=[SCALARS] + [ANYWHERE] * 7 + [tile_rows(half)] * 2,
+        out_specs=[tile_rows(number)] * 2,
+        out_shape=[
+            jax.ShapeDtypeStruct((units, number), jnp.float32),
+            jax.ShapeDtypeStruct((units, number), jnp.bfloat16),
+        ],
+        scratch_shapes=[
+            pltpu.VMEM((2, 2 * number, half), jnp.bfloat16),
+            pltpu.SemaphoreType.DMA((4,)),
+        ],
+        compiler_params=params(),
+        cost_estimate=cost(8 * number * half * units, (far, weight_own, weight_sib)),
+    )(flags, *blocks, far, weight_own, weight_sib)
+
+
+def finish_kernel(near_sum, returned, gate, up, proj_gate, proj_up, sides):
+    hidden_grad = (near_sum[...] + returned[...].astype(jnp.float32)).T
+    add_sides(hidden_grad, gate[...], up[...], proj_gate[...], proj_up[...], sides)
+
+
+def finished_sides(near_sum, returned, gate, up, proj_gate, proj_up):
+    units, number = near_sum.shape
+    return pl.pallas_call(
+        finish_kernel,
+        grid=(units // TILE,),
+        in_specs=[tile_rows(number)] * 2 + [tile_columns(number)] * 2 + [tile_columns(RANK)] * 2,
+        out_specs=whole((number, 2 * RANK)),
+        out_shape=jax.ShapeDtypeStruct((number, 2 * RANK), jnp.float32),
+        compiler_params=params(),
+        cost_estimate=cost(4 * number * RANK * units, (near_sum, returned, gate, up)),
+    )(near_sum, returned, gate, up, proj_gate, proj_up)
+
+
+def lent_kernel(
+    flags, b0, b1, b2, b3, b4, b5, far, weight_own, weight_sib, gate, up, far_gate, far_up,
+    proj_gate, proj_up, sides, stacked, sems,
+):
+    pairs = ((b0, b1), (b2, b3), (b4, b5))
+    total = stacked_products(flags, pairs, far, weight_own, weight_sib, stacked, sems)
+    gates = jnp.concatenate([gate[...], far_gate[...]], axis=0)
+    ups = jnp.concatenate([up[...], far_up[...]], axis=0)
+    add_sides(total.T, gates, ups, proj_gate[...], proj_up[...], sides)
+
+
+def lent_sides(
+    flags, blocks, far, weight_own, weight_sib, gate, up, far_gate, far_up, proj_gate, proj_up
+):
+    number, half = blocks[0].shape
+    units = weight_own.shape[0]
+    return pl.pallas_call(
+        lent_kernel,
+        grid=(units // TILE,),
+        in_specs=[SCALARS]
+        + [ANYWHERE] * 7
+        + [tile_rows(half)] * 2
+        + [tile_columns(number, 1)] * 2
+        + [tile_columns(number)] * 2
+        + [tile_columns(RANK)] * 2,
+        out_specs=whole((2 * number, 2 * RANK)),
+        out_shape=jax.ShapeDtypeStruct((2 * number, 2 * RANK), jnp.float32),
+        scratch_shapes=[
+            pltpu.VMEM((2, 2 * number, half), jnp.bfloat16),
+            pltpu.SemaphoreType.DMA((4,)),
+        ],
+        compiler_params=params(),
+        cost_estimate=cost(8 * number * half * units, (far, weight_own, weight_sib)),
+    )(
+        flags, *blocks, far, weight_own, weight_sib, gate, up, far_gate, far_up, proj_gate, proj_up
+    )
+
+
+def early_kernel(
+    t_input, q_input, t_outgrad, q_outgrad, proj_input, proj_outgrad, t_gate, t_up, q_gate, q_up,
+    proj_hidden, sides,
+):
+    number = t_input.shape[0]
+    middle = pl.ds(RANK, RANK)
+    t_hidden = project(gated_hidden(t_gate[...], t_up[...]), proj_hidden[...])
+    q_hidden = project(gated_hidden(q_gate[...], q_up[...]), proj_hidden[...])
+    first = pl.program_id(0) == 0
+
+    @pl.when(first)
+    def _():
+        for inputs, outgrad, hidden, part in (
+            (t_input, t_outgrad, t_hidden, slice(0, number)),
+            (q_input, q_outgrad, q_hidden, slice(number, None)),
+        ):
+            sides[part, :] = jnp.concatenate(
+                [
+                    project(inputs[...], proj_input[...]),
+                    hidden,
+                    project(outgrad[...], proj_outgrad[...]),
+                ],
+                axis=1,
+            )
+
+    @pl.when(jnp.logical_not(first))
+    def _():
+        sides[:number, middle] += t_hidden
+        sides[number:, middle] += q_hidden
+
+
+def early_sides(
+    t_input, q_input, t_outgrad, q_outgrad, proj_input, proj_outgrad, t_gate, t_up, q_gate, q_up,
+    proj_hidden,
+):
+    train, query, units = t_gate.shape[0], q_gate.shape[0], t_gate.shape[1]
+    wide = (t_input, q_input, t_outgrad, q_outgrad, proj_input, proj_outgrad)
+    tiled = (t_gate, t_up, q_gate, q_up, proj_hidden)
+    return pl.pallas_call(
+        early_kernel,
+        grid=(units // TILE,),
+        in_specs=[whole(a.shape) for a in wide] + [tile_columns(a.shape[0]) for a in tiled],
+        out_specs=whole((train + query, 3 * RANK)),
+        out_shape=jax.ShapeDtypeStruct((train + query, 3 * RANK), jnp.float32),
+        compiler_params=params(),
+        cost_estimate=cost(2 * (train + query) * RANK * units, wide + tiled),
+    )(*wide, *tiled)
+
+
+def outer_sum(left_side, right_side, weight):
+    return lax.dot_general(
+        left_side * weight,
+        right_side,
+        (((0,), (0,)), ((), ())),
+        precision=lax.Precision.HIGHEST,
+        preferred_element_type=jnp.float32,
+    )
+
+
+def example_features(in_side, hidden_side, gate_side, up_side, out_side, length):
+    positions = lax.broadcasted_iota(jnp.int32, (SEQ, RANK), 0)
+    weight = (positions < length).astype(jnp.float32)
+    return (
+        outer_sum(in_side, gate_side, weight),
+        outer_sum(in_side, up_side, weight),
+        outer_sum(hidden_side, out_side, weight),
+    )
+
+
+def query_kernel(lengths, sides, gradient, found):
+    for e in range(found.shape[0]):
+        part = slice(e * SEQ, (e + 1) * SEQ)
+        three = example_features(
+            sides[part, :RANK],
+            sides[part, RANK : 2 * RANK],
+            gradient[part, :RANK],
+            gradient[part, RANK:],
+            sides[part, 2 * RANK :],
+            lengths[e],
+        )
+        for segment in range(3):
+            found[e, segment * RANK : (segment + 1) * RANK, :] = three[segment]
+
+
+def query_features(lengths, sides, gradient):
+    return pl.pallas_call(
+        query_kernel,
+        in_specs=[SCALARS, IN_VMEM, IN_VMEM],
+        out_specs=IN_VMEM,
+        out_shape=jax.ShapeDtypeStruct((lengths.shape[0], 3 * RANK, RANK), jnp.float32),
+        compiler_params=params(),
+    )(lengths, sides, gradient)
+
+
+def score_kernel(
+    lengths, place, whole_sides, own_sides, near, far, q0, q1, q2, q3, scores
+):
+    queries = q0.shape[0]
+    shape = scores.shape
+    row = lax.broadcasted_iota(jnp.int32, shape, 0)
+    column = lax.broadcasted_iota(jnp.int32, shape, 1)
+    total = jnp.zeros(shape, jnp.float32)
+    for e in range(shape[0]):
+        part = slice(e * SEQ, (e + 1) * SEQ)
+        gradient = near[part, :] + far[part, :]
+        three = jnp.concatenate(
+            example_features(
+                whole_sides[part, :RANK],
+                own_sides[part, RANK : 2 * RANK],
+                gradient[:, :RANK],
+                gradient[:, RANK:],
+                whole_sides[part, 2 * RANK :],
+                lengths[e],
+            ),
+            axis=0,
+        )
+        for step, found in enumerate((q0, q1, q2, q3)):
+            for j in range(queries):
+                value = jnp.sum(three * found[j], keepdims=True)
+                here = (row == e) & (
+                    column == queries * jnp.bitwise_xor(place[0], step) + j
+                )
+                total = total + jnp.where(here, value, 0.0)
+    scores[...] = total
+
+
+def partial_scores(lengths, place, whole_sides, own_sides, near, far, found):
+    number = lengths.shape[0]
+    return pl.pallas_call(
+        score_kernel,
+        in_specs=[SCALARS] * 2 + [IN_VMEM] * 8,
+        out_specs=IN_VMEM,
+        out_shape=jax.ShapeDtypeStruct((number, 4 * found[0].shape[0]), jnp.float32),
+        compiler_params=params(),
+    )(lengths, place, whole_sides, own_sides, near, far, *found)
+
+
+def after(value, *others):
+    return lax.optimization_barrier((value, *others))[0]
 
 
 def moving_plan(
-    tensor,
     train_input,
     train_gate,
     train_up,
@@ -139,89 +442,119 @@
 ):
     t = lax.axis_index("tensor")
     d = lax.axis_index("dp")
-    x, core = d // 2, d % 2
-    to_core = [(i, i ^ 1) for i in range(4)]
-    to_chip = [(i, i ^ 2) for i in range(4)]
-    upward = [(i, i + 1) for i in range(tensor - 1)]
-    downward = [(i + 1, i) for i in range(tensor - 1)]
-
-    weight_own = down_weight
-    weight_sib = lax.ppermute(down_weight, "dp", to_core)
-
-    def column_blocks(rows):
-        rising, falling = [rows], [rows]
-        for _ in range(tensor - 1):
-            rising.append(lax.ppermute(rising[-1], "tensor", upward))
-            falling.append(lax.ppermute(falling[-1], "tensor", downward))
-        blocks = [rows]
-        for step in range(1, tensor):
-            blocks.append(jnp.where(t >= step, rising[step], falling[tensor - step]))
-        return blocks
-
-    def hidden_gradient(rows):
-        blocks = column_blocks(rows)
-
-        def column(k):
-            return pick(blocks, (t - k) % tensor)
-
-        far_own = lax.ppermute(column(2 * (1 - x) + core), "dp", to_chip)
-        far_sib = lax.ppermute(column(2 * (1 - x) + 1 - core), "dp", to_chip)
-        far = project(far_own, weight_own) + project(far_sib, weight_sib)
-        returned = lax.ppermute(far.astype(jnp.bfloat16), "dp", to_chip)
-        near = project(column(2 * x + core), weight_own)
-        near = near + project(column(2 * x + 1 - core), weight_sib)
-        return near + returned.astype(jnp.float32)
-
-    query_rows = [flatten(a) for a in (query_input, query_gate, query_up, query_outgrad)]
-    train_rows = [flatten(a) for a in (train_input, train_gate, train_up, train_outgrad)]
-
-    q_input, q_gate, q_up, q_outgrad = query_rows
-    gate_side, up_side = gradient_sides(
-        q_gate, q_up, hidden_gradient(q_outgrad), proj_gate, proj_up
-    )
-    query_sides = lax.psum(
-        (
-            project(q_input, proj_input),
-            project(gated_hidden(q_gate, q_up), proj_hidden),
-            gate_side,
-            up_side,
-            project(q_outgrad, proj_outgrad),
-        ),
-        "tensor",
-    )
-    query_features = lax.all_gather(
-        features(*query_sides, query_lengths), "dp", axis=0, tiled=True
-    )
-
-    t_input, t_gate, t_up, t_outgrad = train_rows
-    in_side, out_side = lax.psum(
-        (project(t_input, proj_input), project(t_outgrad, proj_outgrad)), "tensor"
-    )
-    hidden_side = project(gated_hidden(t_gate, t_up), proj_hidden)
-
-    pieces = 2
-    examples = train_lengths.shape[0] // pieces
-    partial = []
-    for piece in range(pieces):
-        part = slice(piece * examples * SEQ, (piece + 1) * examples * SEQ)
-        gate_side, up_side = gradient_sides(
-            t_gate[part], t_up[part], hidden_gradient(t_outgrad[part]), proj_gate, proj_up
+    x, core, upper = d // 2, d % 2, t // 2
+    at_home = x == upper
+    inner_chip = (t == 1) | (t == 2)
+    near_code = jnp.where(at_home, 0, jnp.where(inner_chip, 1, 2))
+    first_parity = jnp.where(at_home, t % 2, upper)
+    flags = jnp.stack([near_code, first_parity ^ core]).astype(jnp.int32)
+    place = jnp.stack([d]).astype(jnp.int32)
+
+    to_core = functools.partial(lax.ppermute, axis_name="dp", perm=[(i, i ^ 1) for i in range(4)])
+    to_chip = functools.partial(lax.ppermute, axis_name="dp", perm=[(i, i ^ 2) for i in range(4)])
+    outer = functools.partial(
+        lax.ppermute, axis_name="tensor", perm=[(i, i ^ 1) for i in range(4)]
+    )
+    across = functools.partial(
+        lax.ppermute, axis_name="tensor", perm=[(i, i ^ 2) for i in range(4)]
+    )
+    middle = functools.partial(
+        lax.ppermute,
+        axis_name=("tensor", "dp"),
+        perm=[
+            (4 * i + j, 4 * (3 - i) + j) if i in (1, 2) else (4 * i + j, 4 * i + (j ^ 1))
+            for i in range(4)
+            for j in range(4)
+        ],
+    )
+
+    def tensor_sum(values):
+        values = values + outer(values)
+        return values + across(values)
+
+    def crossing_pair(piece, first, second_inner, third_inner, second_outer, third_outer):
+        def choose(within, beyond_inner, beyond_outer):
+            beyond = jnp.where(inner_chip, beyond_inner, beyond_outer)
+            return jnp.where(at_home, beyond, within)
+
+        return jnp.stack(
+            [choose(piece, second_inner, second_outer), choose(first, third_inner, third_outer)]
         )
-        piece_features = features(
-            in_side[part],
-            hidden_side[part],
-            gate_side,
-            up_side,
-            out_side[part],
-            train_lengths[piece * examples : (piece + 1) * examples],
-        )
-        partial.append(inner(piece_features, query_features))
-    scores = jnp.concatenate(partial, axis=0)
-    total = scores
-    for step in range(1, tensor):
-        turn = [(i, (i + step) % tensor) for i in range(tensor)]
-        total = total + lax.ppermute(scores, "tensor", turn)
-    return total / (RANK * SEQ)
+
+    q_input, q_gate, q_up, q_outgrad = [
+        flatten(a) for a in (query_input, query_gate, query_up, query_outgrad)
+    ]
+    t_input, t_gate, t_up, t_outgrad = [
+        flatten(a) for a in (train_input, train_gate, train_up, train_outgrad)
+    ]
+    examples = train_lengths.shape[0] // 2
+    cut = examples * SEQ
+
+    weight_own, weight_sib = down_weight, to_core(down_weight)
+
+    q_one, q_mid = outer(q_outgrad), middle(q_outgrad)
+    lent = to_chip(jnp.stack([t_gate[cut:], t_up[cut:]]))
+    own_sides = early_sides(
+        t_input, q_input, t_outgrad, q_outgrad, proj_input, proj_outgrad, t_gate, t_up, q_gate,
+        q_up, proj_hidden,
+    )
+    q_two, q_last = outer(q_mid), middle(q_one)
+    whole_sides = lax.psum(own_sides, "tensor")
+    q_three = outer(after(q_last, own_sides))
+    q_blocks = (q_outgrad, q_one, q_mid, q_last, q_two, q_three)
+
+    a_rows = after(t_outgrad[:cut], q_two)
+    a_one, a_mid = outer(a_rows), middle(a_rows)
+    q_send = crossing_pair(*q_blocks)
+    q_far = to_chip(q_send)
+    a_one, a_mid = lax.optimization_barrier((a_one, a_mid, q_send, lent))[:2]
+    a_two, a_last = outer(a_mid), middle(a_one)
+    a_three = outer(a_last)
+    a_blocks = (a_rows, a_one, a_mid, a_last, a_two, a_three)
+
+    b_rows = after(t_outgrad[cut:], a_two, q_far)
+    b_one, b_mid = outer(b_rows), middle(b_rows)
+    a_send = crossing_pair(*a_blocks)
+    a_far = to_chip(a_send)
+    q_near_sum, q_far_sum = partial_sums(
+        flags, q_blocks, after(q_far, a_send), weight_own, weight_sib
+    )
+    b_one, b_mid = lax.optimization_barrier((b_one, b_mid, q_far_sum))[:2]
+    b_two, b_last = outer(b_mid), middle(b_one)
+    b_three = outer(b_last)
+    b_blocks = (b_rows, b_one, b_mid, b_last, b_two, b_three)
+
+    q_gradient = finished_sides(
+        q_near_sum, after(to_chip(q_far_sum), a_far), q_gate, q_up, proj_gate, proj_up
+    )
+    b_send = crossing_pair(*b_blocks)
+    b_far = to_chip(b_send)
+    a_near_sum, a_far_sum = partial_sums(
+        flags, a_blocks, after(a_far, q_gradient, b_send), weight_own, weight_sib
+    )
+    own_found = query_features(
+        query_lengths, whole_sides[2 * cut :], tensor_sum(q_gradient)
+    )
+    core_found = to_core(own_found)
+    found = (own_found, core_found, to_chip(own_found), to_chip(core_found))
+
+    b_gradient = lent_sides(
+        flags, b_blocks, after(b_far, own_found), weight_own, weight_sib, t_gate, t_up, lent[0],
+        lent[1], proj_gate, proj_up,
+    )
+    a_gradient = finished_sides(
+        a_near_sum, to_chip(a_far_sum), t_gate, t_up, proj_gate, proj_up
+    )
+    a_scores = partial_scores(
+        train_lengths[:examples], place, whole_sides[:cut], own_sides[:cut], a_gradient,
+        jnp.zeros_like(a_gradient), found,
+    )
+    b_scores = partial_scores(
+        train_lengths[examples:], place, whole_sides[cut : 2 * cut], own_sides[cut : 2 * cut],
+        b_gradient[:cut], to_chip(b_gradient[cut:]), found,
+    )
+    scores = tensor_sum(jnp.concatenate([a_scores, b_scores], axis=0))
+    return scores / (RANK * SEQ)
 
 
 def solution(mesh):
@@ -229,7 +562,7 @@
 
     def per_device(*arguments):
         if tensor == 4 and dp == 4:
-            return moving_plan(tensor, *arguments)
+            return moving_plan(*arguments)
         return gathering_plan(*arguments)
 
     in_specs = (

time: 356 us -> 255 us (0.72); the launches traced: 350 us -> 254 us
  matrix products: 163 us -> 0 us
  Pallas kernels: 0 us -> 67.7 us
  starting transfers between devices: 72.2 us -> 56.1 us
  waiting for transfers between devices: 73.2 us -> 87.2 us
  local copies, waits for them, and re-layouts: 8.22 us -> 19.4 us
  blocking collectives: 6.44 us -> 0 us
    dot_general x28 -> x0, matrix products: 152 us -> none  [the longest x17 145 us: project(): lax.dot_general(rows, table, (((1,), (1,)), ((), ())), preferred_element_...]
    pallas_call x0 -> x9, Pallas kernels: none -> 67.7 us  [the longest x2 33.1 us: partial_sums(): pl.pallas_call(partial_kernel, grid=(units // TILE,), in_specs=[SCALARS]...]
    ppermute x31 -> x30, waiting for transfers between devices: 38 us -> 55.8 us  [the longest x2 17 us: moving_plan(): q_one, q_mid = (outer(q_outgrad), middle(q_outgrad))]
    ppermute x31 -> x30, starting transfers between devices: 72.1 us -> 56.1 us  [the longest x1 11.5 us: moving_plan(): b_three = outer(b_last)]
    unnamed x65 -> x52, local copies, waits for them, and re-layouts: 0.41 us -> 13.6 us
    reshape x7 -> x0, matrix products: 11.7 us -> none  [outer_sums(): right_rows = right_side.reshape(number, length, right_side.shape[1])]
    another operation x0 -> x11, other arithmetic: none -> 9.43 us  [the longest x9 7.93 us: crossing_pair(): jnp.stack([choose(piece, second_inner, second_outer), choose(first, third...]
    select_n x6 -> x0, other arithmetic: 8.18 us -> none  [pick(): chosen = jnp.where(index == number, blocks[number], chosen)]
  transfers between devices with their start and end apart: 33 -> 31, of which waited for: 20 -> 12; matrix products, arithmetic and copies ran while one was open for 46% -> 6% of each run, Pallas kernels for 0% -> 26%
where the time goes in v3:
time: 255 us; the launch traced here: 254 us
  waiting for transfers between devices  87.2 us (34%)
  Pallas kernels  67.7 us (27%)
  starting transfers between devices  56.1 us (22%)
  local copies, waits for them, and re-layouts  19.4 us (8%)
  between operations  13.8 us (5%)
  other arithmetic  10 us (4%)
    pallas_call x2, Pallas kernels, partial_sums(): pl.pallas_call(partial_kernel, grid=(units // TILE,), in_specs=[SCALARS]...  33.1 us
    psum x1, waiting for transfers between devices, moving_plan(): whole_sides = lax.psum(own_sides, 'tensor')  30.7 us
    pallas_call x1, Pallas kernels, lent_sides(): pl.pallas_call(lent_kernel, grid=(units // TILE,), in_specs=[SCALARS] + [...  18.2 us
    ppermute x2, waiting for transfers between devices, moving_plan(): q_one, q_mid = (outer(q_outgrad), middle(q_outgrad))  17 us
    unnamed x52, local copies, waits for them, and re-layouts  13.6 us
    ppermute x1, starting transfers between devices, moving_plan(): b_three = outer(b_last)  11.5 us
    ppermute x1, starting transfers between devices, moving_plan(): a_three = outer(a_last)  9.88 us
    ppermute x1, waiting for transfers between devices, moving_plan(): q_three = outer(after(q_last, own_sides))  9.79 us
  transfers between devices with their start and end apart: 31, of which 12 were waited for; matrix products, arithmetic and copies ran while one was open for 6% of the time, Pallas kernels for 26%

profile of v3, /device:TPU:0, one launch (start us, length us, event | category | flops | bytes accessed | tf_op | source)
XLA Modules:
  0.0 254.2 jit_solution(15558403621544365114)
XLA Ops:
  7.0 2.6 %collective-permute-start.4 = (bf16[128,2048]{1,0:T(8,128)(2,1)}, bf16[128,2048]{1,0:T(8,128)(2,1)}, u32[]{:S(2)}, u32[]{:S(2)}) collective-permute-start(bf16[128,2048]{1,0:T(8,128)(2,1)} %bitcast.40), channel_id=1, source_target_pairs={{0,4},{4,0},{8,12},{12,8},{1,5},{5,1},{9,13},{13,9},{2,6},{6,2},{1... | collective-permute-start | bytes 1572872 | tf_op jit(solution)/shard_map/ppermute | solution.py:495
  9.8 12.7 %collective-permute-done.4.b1 = bf16[128,2048]{1,0:T(8,128)(2,1)} collective-permute-done((bf16[128,2048]{1,0:T(8,128)(2,1)}, bf16[128,2048]{1,0:T(8,128)(2,1)}, u32[]{:S(2)}, u32[]{:S(2)}) %collective-permute-start.4) | collective-permute-done | bytes 524320 | tf_op jit(solution)/shard_map/ppermute | solution.py:495
  22.5 1.4 pad_maximum_fusion
  23.9 1.7 collective-permute-start.7
  25.6 4.3 %collective-permute-done.b2 = bf16[128,2048]{1,0:T(8,128)(2,1)} collective-permute-done((bf16[128,2048]{1,0:T(8,128)(2,1)}, bf16[128,2048]{1,0:T(8,128)(2,1)}, u32[]{:S(2)}, u32[]{:S(2)}) %collective-permute-start) | collective-permute-done | bytes 524320 | tf_op jit(solution)/shard_map/ppermute | solution.py:495
  29.9 1.2 copy-done.9
  31.1 1.2 copy-done.11
  32.3 1.2 copy-done.19
  36.5 5.1 %shard_map.154 = f32[384,192]{1,0:T(8,128)} custom-call(bf16[256,2048]{1,0:T(8,128)(2,1)S(1)} %bitcast.57, bf16[128,2048]{1,0:T(8,128)(2,1)S(1)} %bitcast.58, bf16[256,2048]{1,0:T(8,128)(2,1)S(1)} %bitcast.52, bf16[128,2048]{1,0:T(8,128)(2,1)S(1)} %bitcast.42, bf16[64,2048]{1,0:T(8,128)(2,1)S(1)} %copy-done.22, bf16[64,2048]{1,0:T(8,128)(2,1)S(1)} %copy-done.23, ...), custom_call_target="tpu_custom_call" | custom-call | flops 176160768 | bytes 9633792 | tf_op jit(solution)/shard_map/pallas_call | solution.py:322
  41.6 2.0 collective-permute-start.6
  43.6 2.1 fusion.1
  45.7 1.1 select_bitcast_fusion.5
  46.9 9.8 %collective-permute-done.6.b5 = bf16[128,2048]{1,0:T(8,128)(2,1)} collective-permute-done((bf16[128,2048]{1,0:T(8,128)(2,1)}, bf16[128,2048]{1,0:T(8,128)(2,1)}, u32[]{:S(2)}, u32[]{:S(2)}) %collective-permute-start.6) | collective-permute-done | bytes 524320 | tf_op jit(solution)/shard_map/ppermute | solution.py:503
  58.9 8.5 %collective-permute-done.2.b1 = bf16[128,2048]{1,0:T(8,128)(2,1)} collective-permute-done((bf16[128,2048]{1,0:T(8,128)(2,1)}, bf16[128,2048]{1,0:T(8,128)(2,1)}, u32[]{:S(2)}, u32[]{:S(2)}) %collective-permute-start.2) | collective-permute-done | bytes 524320 | tf_op jit(solution)/shard_map/ppermute | solution.py:507
  67.4 2.7 %collective-permute-start.12 = (bf16[2,128,2048]{2,1,0:T(8,128)(2,1)}, bf16[2,128,2048]{2,1,0:T(8,128)(2,1)}, u32[]{:S(2)}, u32[]{:S(2)}) collective-permute-start(bf16[2,128,2048]{2,1,0:T(8,128)(2,1)} %pad_maximum_fusion.1), channel_id=1, source_target_pairs={{0,2},{1,3},{2,0},{3,1},{4,6},{5,7},{6,4},{7,5},{8,10},{9,11},{10,... | collective-permute-start | bytes 3145736 | tf_op jit(solution)/shard_map/ppermute | solution.py:509
  70.0 4.4 %collective-permute-start.9 = (bf16[128,2048]{1,0:T(8,128)(2,1)}, bf16[128,2048]{1,0:T(8,128)(2,1)}, u32[]{:S(2)}, u32[]{:S(2)}) collective-permute-start(bf16[128,2048]{1,0:T(8,128)(2,1)} %collective-permute-done.3.b2), channel_id=1, source_target_pairs={{0,4},{4,0},{8,12},{12,8},{1,5},{5,1},{9,13},{13,9},{2,6},{6,2},{1... | collective-permute-start | bytes 1572872 | tf_op jit(solution)/shard_map/ppermute | solution.py:511
  74.4 9.9 %collective-permute-start.10 = (bf16[128,2048]{1,0:T(8,128)(2,1)}, bf16[128,2048]{1,0:T(8,128)(2,1)S(1)}, u32[]{:S(2)}, u32[]{:S(2)}) collective-permute-start(bf16[128,2048]{1,0:T(8,128)(2,1)} %collective-permute-done.8.b3), channel_id=1, source_target_pairs={{0,4},{4,0},{8,12},{12,8},{1,5},{5,1},{9,13},{13,9},{2,6},{6,2},{1... | collective-permute-start | bytes 1572872 | tf_op jit(solution)/shard_map/ppermute | solution.py:512
  84.4 2.2 collective-permute-done.9.b4
  87.7 6.4 %collective-permute-done.12.far = bf16[2,128,2048]{2,1,0:T(8,128)(2,1)} collective-permute-done((bf16[2,128,2048]{2,1,0:T(8,128)(2,1)}, bf16[2,128,2048]{2,1,0:T(8,128)(2,1)}, u32[]{:S(2)}, u32[]{:S(2)}) %collective-permute-start.12) | collective-permute-done | bytes 1048608 | tf_op jit(solution)/shard_map/ppermute | solution.py:509
  94.1 2.9 %collective-permute-start.15 = (bf16[128,2048]{1,0:T(8,128)(2,1)S(1)}, bf16[128,2048]{1,0:T(8,128)(2,1)}, u32[]{:S(2)}, u32[]{:S(2)}) collective-permute-start(bf16[128,2048]{1,0:T(8,128)(2,1)S(1)} %bitcast.44), channel_id=1, source_target_pairs={{0,4},{4,0},{8,12},{12,8},{1,5},{5,1},{9,13},{13,9},{2,6},{6,2},{1... | collective-permute-start | bytes 1572872 | tf_op jit(solution)/shard_map/ppermute | solution.py:516
  98.2 2.7 %collective-permute-start.11 = (bf16[2,128,2048]{2,1,0:T(8,128)(2,1)}, bf16[2,128,2048]{2,1,0:T(8,128)(2,1)}, u32[]{:S(2)}, u32[]{:S(2)}) collective-permute-start(bf16[2,128,2048]{2,1,0:T(8,128)(2,1)} %pad_maximum_fusion.2), channel_id=1, source_target_pairs={{0,2},{1,3},{2,0},{3,1},{4,6},{5,7},{6,4},{7,5},{8,10},{9,11},{10,... | collective-permute-start | bytes 3145736 | tf_op jit(solution)/shard_map/ppermute | solution.py:518
  100.9 16.9 %shard_map.155 = (f32[3584,128]{1,0:T(8,128)S(1)}, bf16[3584,128]{1,0:T(8,128)(2,1)}) custom-call(s32[2]{0:T(128)S(1)} %pad_add_fusion.flags, bf16[128,2048]{1,0:T(8,128)(2,1)S(1)} %bitcast.43, bf16[128,2048]{1,0:T(8,128)(2,1)} %collective-permute-done.4.b1, bf16[128,2048]{1,0:T(8,128)(2,1)} %collective-permute-done.b2, ...), custom_call_target="tpu_custom_call" | custom-call | flops 7516192768 | bytes 30408704 | tf_op jit(solution)/shard_map/pallas_call | solution.py:210
  117.8 1.3 copy-done.17
  122.0 2.5 collective-permute-start.17
  124.4 11.5 %collective-permute-start.19 = (bf16[128,2048]{1,0:T(8,128)(2,1)}, bf16[128,2048]{1,0:T(8,128)(2,1)}, u32[]{:S(2)}, u32[]{:S(2)}) collective-permute-start(bf16[128,2048]{1,0:T(8,128)(2,1)} %collective-permute-done.18.b3), channel_id=1, source_target_pairs={{0,4},{4,0},{8,12},{12,8},{1,5},{5,1},{9,13},{13,9},{2,6},{6,2},{1... | collective-permute-start | bytes 1572872 | tf_op jit(solution)/shard_map/ppermute | solution.py:524
  135.9 30.7 %all-reduce.2.cloned.1.call-done = f32[384,192]{1,0:T(8,128)} async-done(((f32[384,192]{1,0:T(8,128)}), f32[384,192]{1,0:T(8,128)}) %all-reduce.2.cloned.1.call-update) | async-done | bytes 294928 | tf_op jit(solution)/shard_map/psum | solution.py:502
  168.7 1.2 copy-done.10
  169.9 1.2 copy-done.12
  171.1 1.5 copy-done.18
  172.6 5.2 %shard_map.156 = f32[128,128]{1,0:T(8,128)S(1)} custom-call(f32[3584,128]{1,0:T(8,128)S(1)} %copy-done.18, bf16[3584,128]{1,0:T(8,128)(2,1)} %collective-permute-done.14.returned, bf16[128,3584]{1,0:T(8,128)(2,1)S(1)} %bitcast.54, bf16[128,3584]{1,0:T(8,128)(2,1)S(1)} %bitcast.56, bf16[64,3584]{1,0:T(8,128)(2,1)S(1)} %copy-done.6, bf16[64,3584]{1,0:T(8,128)(2,1)S(1)} %copy-done.7), custom_call_target="tpu_custom_call" | custom-call | flops 117440512 | bytes 4587520 | tf_op jit(solution)/shard_map/pallas_call | solution.py:235
  177.8 1.4 collective-permute-start.21
  180.3 1.8 collective-permute-done.21
  182.1 1.9 collective-permute-start.22
  184.0 1.1 select_bitcast_fusion
  185.3 1.7 collective-permute-start.26
  187.0 1.6 slice_bitcast_fusion
  190.1 16.2 %shard_map.157 = (f32[3584,128]{1,0:T(8,128)S(1)}, bf16[3584,128]{1,0:T(8,128)(2,1)S(1)}) custom-call(s32[2]{0:T(128)S(1)} %pad_add_fusion.flags, bf16[128,2048]{1,0:T(8,128)(2,1)S(1)} %bitcast.51, bf16[128,2048]{1,0:T(8,128)(2,1)} %collective-permute-done.2.b1, bf16[128,2048]{1,0:T(8,128)(2,1)} %collective-permute-done.3.b2, ...), custom_call_target="tpu_custom_call" | custom-call | flops 7516192768 | bytes 30408704 | tf_op jit(solution)/shard_map/pallas_call | solution.py:210
  206.3 1.6 collective-permute-start.20
  209.4 18.2 %shard_map.161 = f32[256,128]{1,0:T(8,128)S(1)} custom-call(s32[2]{0:T(128)S(1)} %pad_add_fusion.flags, bf16[128,2048]{1,0:T(8,128)(2,1)S(1)} %bitcast.47, bf16[128,2048]{1,0:T(8,128)(2,1)} %collective-permute-done.15.b1, bf16[128,2048]{1,0:T(8,128)(2,1)S(1)} %copy-done.14, bf16[128,2048]{1,0:T(8,128)(2,1)} %collective-permute-done.18.b3, ...), custom_call_target="tpu_custom_call" | custom-call | flops 7516192768 | bytes 30408704 | tf_op jit(solution)/shard_map/pallas_call | solution.py:262
  227.7 2.1 collective-permute-start.27
  229.8 3.5 %collective-permute-done.20.returned = bf16[3584,128]{1,0:T(8,128)(2,1)S(1)} collective-permute-done((bf16[3584,128]{1,0:T(8,128)(2,1)S(1)}, bf16[3584,128]{1,0:T(8,128)(2,1)S(1)}, u32[]{:S(2)}, u32[]{:S(2)}) %collective-permute-start.20) | collective-permute-done | bytes 917536 | tf_op jit(solution)/shard_map/ppermute | solution.py:546
  233.3 2.9 %shard_map.158.near = f32[128,128]{1,0:T(8,128)S(1)} custom-call(f32[3584,128]{1,0:T(8,128)S(1)} %get-tuple-element.32.near_sum, bf16[3584,128]{1,0:T(8,128)(2,1)S(1)} %collective-permute-done.20.returned, bf16[256,3584]{1,0:T(8,128)(2,1)S(1)} %bitcast.34, bf16[256,3584]{1,0:T(8,128)(2,1)S(1)} %bitcast.38, bf16[64,3584]{1,0:T(8,128)(2,1)S(1)} %copy-done.6, ...), custom_call_target="tpu_custom_call" | custom-call | flops 117440512 | bytes 6422528 | tf_op jit(solution)/shard_map/pallas_call | solution.py:235
  236.2 1.2 shard_map.160
  237.4 1.2 shard_map.162
  238.6 1.4 collective-permute-start.28
  240.0 2.2 collective-permute-done.28
  242.2 1.1 collective-permute-start.29
  243.3 3.4 %collective-permute-done.29 = f32[4,8]{1,0:T(4,128)S(1)} collective-permute-done((f32[4,8]{1,0:T(4,128)S(1)}, f32[4,8]{1,0:T(4,128)S(1)}, u32[]{:S(2)}, u32[]{:S(2)}) %collective-permute-start.29) | collective-permute-done | bytes 160 | tf_op jit(solution)/shard_map/ppermute | solution.py:473
  (103 shorter events, 18.3 us)
Async XLA Ops:
  6.5 94.4 %collective-permute-start.13 = (bf16[3584,2048]{1,0:T(8,128)(2,1)}, bf16[3584,2048]{1,0:T(8,128)(2,1)}, u32[]{:S(2)}, u32[]{:S(2)}) collective-permute-start(bf16[3584,2048]{1,0:T(8,128)(2,1)} %weight_own.5), channel_id=1, source_target_pairs={{0,1},{1,0},{2,3},{3,2},{4,5},{5,4},{6,7},{7,6},{8,9},{9,8},{10,11... | collective-permute-start | bytes 44040200 | tf_op jit(solution)/shard_map/ppermute | solution.py:493
  7.0 15.5 %slice-start = ((bf16[4,64,3584]{2,1,0:T(8,128)(2,1)}), bf16[2,64,3584]{2,1,0:T(8,128)(2,1)S(1)}, s32[]{:S(2)}) async-start(bf16[4,64,3584]{2,1,0:T(8,128)(2,1)} %param.17), calls=%async_computation.1 | async-start | bytes 1835008 | tf_op jit(solution)/shard_map/slice | solution.py:496
  7.0 15.5 %slice-start.1 = ((bf16[4,64,3584]{2,1,0:T(8,128)(2,1)}), bf16[2,64,3584]{2,1,0:T(8,128)(2,1)S(1)}, s32[]{:S(2)}) async-start(bf16[4,64,3584]{2,1,0:T(8,128)(2,1)} %param.18), calls=%async_computation.2 | async-start | bytes 1835008 | tf_op jit(solution)/shard_map/slice | solution.py:496
  7.0 15.5 %collective-permute-start.4 = (bf16[128,2048]{1,0:T(8,128)(2,1)}, bf16[128,2048]{1,0:T(8,128)(2,1)}, u32[]{:S(2)}, u32[]{:S(2)}) collective-permute-start(bf16[128,2048]{1,0:T(8,128)(2,1)} %bitcast.40), channel_id=1, source_target_pairs={{0,4},{4,0},{8,12},{12,8},{1,5},{5,1},{9,13},{13,9},{2,6},{6,2},{1... | collective-permute-start | bytes 1572872 | tf_op jit(solution)/shard_map/ppermute | solution.py:495
  9.6 20.3 %collective-permute-start = (bf16[128,2048]{1,0:T(8,128)(2,1)}, bf16[128,2048]{1,0:T(8,128)(2,1)}, u32[]{:S(2)}, u32[]{:S(2)}) collective-permute-start(bf16[128,2048]{1,0:T(8,128)(2,1)} %bitcast.41), channel_id=1, source_target_pairs={{0,1},{1,0},{2,3},{3,2},{4,8},{5,9},{6,10},{7,11},{8,4},{9,5},{10,... | collective-permute-start | bytes 1572872 | tf_op jit(solution)/shard_map/ppermute | solution.py:495
  9.8 20.1 %copy-start.3 = (bf16[2,64,2048]{2,1,0:T(8,128)(2,1)S(1)}, bf16[2,64,2048]{2,1,0:T(8,128)(2,1)}, u32[]{:S(2)}) copy-start(bf16[2,64,2048]{2,1,0:T(8,128)(2,1)} %param.24) | copy-start | bytes 1572868
  9.8 20.1 %copy-start.5 = (bf16[4,64,2048]{2,1,0:T(8,128)(2,1)S(1)}, bf16[4,64,2048]{2,1,0:T(8,128)(2,1)}, u32[]{:S(2)}) copy-start(bf16[4,64,2048]{2,1,0:T(8,128)(2,1)} %param.19) | copy-start | bytes 3145732
  9.8 20.1 %copy-start.22 = (bf16[64,2048]{1,0:T(8,128)(2,1)S(1)}, bf16[64,2048]{1,0:T(8,128)(2,1)}, u32[]{:S(2)}) copy-start(bf16[64,2048]{1,0:T(8,128)(2,1)} %proj_input.1) | copy-start | bytes 786436
  22.5 19.1 %collective-permute-start.5 = (bf16[128,2048]{1,0:T(8,128)(2,1)}, bf16[128,2048]{1,0:T(8,128)(2,1)}, u32[]{:S(2)}, u32[]{:S(2)}) collective-permute-start(bf16[128,2048]{1,0:T(8,128)(2,1)} %collective-permute-done.4.b1), channel_id=1, source_target_pairs={{0,1},{1,0},{2,3},{3,2},{4,8},{5,9},{6,10},{7,11},{8,4},{9,5},{10,... | collective-permute-start | bytes 1572872 | tf_op jit(solution)/shard_map/ppermute | solution.py:501
  22.5 7.4 %copy-start = (bf16[4,64,3584]{2,1,0:T(8,128)(2,1)S(1)}, bf16[4,64,3584]{2,1,0:T(8,128)(2,1)}, u32[]{:S(2)}) copy-start(bf16[4,64,3584]{2,1,0:T(8,128)(2,1)} %param.17) | copy-start | bytes 5505028
  22.5 7.4 %copy-start.1 = (bf16[4,64,3584]{2,1,0:T(8,128)(2,1)S(1)}, bf16[4,64,3584]{2,1,0:T(8,128)(2,1)}, u32[]{:S(2)}) copy-start(bf16[4,64,3584]{2,1,0:T(8,128)(2,1)} %param.18) | copy-start | bytes 5505028
  23.9 43.4 %collective-permute-start.7 = (bf16[2,128,3584]{2,1,0:T(8,128)(2,1)}, bf16[2,128,3584]{2,1,0:T(8,128)(2,1)}, u32[]{:S(2)}, u32[]{:S(2)}) collective-permute-start(bf16[2,128,3584]{2,1,0:T(8,128)(2,1)} %pad_maximum_fusion), channel_id=1, source_target_pairs={{0,2},{1,3},{2,0},{3,1},{4,6},{5,7},{6,4},{7,5},{8,10},{9,11},{10,... | collective-permute-start | bytes 5505032 | tf_op jit(solution)/shard_map/ppermute | solution.py:496
  29.9 15.8 %collective-permute-start.1 = (bf16[128,2048]{1,0:T(8,128)(2,1)}, bf16[128,2048]{1,0:T(8,128)(2,1)}, u32[]{:S(2)}, u32[]{:S(2)}) collective-permute-start(bf16[128,2048]{1,0:T(8,128)(2,1)} %collective-permute-done.b2), channel_id=1, source_target_pairs={{0,4},{4,0},{8,12},{12,8},{1,5},{5,1},{9,13},{13,9},{2,6},{6,2},{1... | collective-permute-start | bytes 1572872 | tf_op jit(solution)/shard_map/ppermute | solution.py:501
  41.6 15.1 %collective-permute-start.6 = (bf16[128,2048]{1,0:T(8,128)(2,1)}, bf16[128,2048]{1,0:T(8,128)(2,1)}, u32[]{:S(2)}, u32[]{:S(2)}) collective-permute-start(bf16[128,2048]{1,0:T(8,128)(2,1)} %collective-permute-done.5.b3), channel_id=1, source_target_pairs={{0,4},{4,0},{8,12},{12,8},{1,5},{5,1},{9,13},{13,9},{2,6},{6,2},{1... | collective-permute-start | bytes 1572872 | tf_op jit(solution)/shard_map/ppermute | solution.py:503
  45.7 21.6 %collective-permute-start.2 = (bf16[128,2048]{1,0:T(8,128)(2,1)}, bf16[128,2048]{1,0:T(8,128)(2,1)}, u32[]{:S(2)}, u32[]{:S(2)}) collective-permute-start(bf16[128,2048]{1,0:T(8,128)(2,1)} %bitcast.48), channel_id=1, source_target_pairs={{0,4},{4,0},{8,12},{12,8},{1,5},{5,1},{9,13},{13,9},{2,6},{6,2},{1... | collective-permute-start | bytes 1572872 | tf_op jit(solution)/shard_map/ppermute | solution.py:507
  45.7 21.6 %collective-permute-start.3 = (bf16[128,2048]{1,0:T(8,128)(2,1)}, bf16[128,2048]{1,0:T(8,128)(2,1)}, u32[]{:S(2)}, u32[]{:S(2)}) collective-permute-start(bf16[128,2048]{1,0:T(8,128)(2,1)} %bitcast.49), channel_id=1, source_target_pairs={{0,1},{1,0},{2,3},{3,2},{4,8},{5,9},{6,10},{7,11},{8,4},{9,5},{10,... | collective-permute-start | bytes 1572872 | tf_op jit(solution)/shard_map/ppermute | solution.py:507
  67.3 7.1 %collective-permute-start.8 = (bf16[128,2048]{1,0:T(8,128)(2,1)}, bf16[128,2048]{1,0:T(8,128)(2,1)}, u32[]{:S(2)}, u32[]{:S(2)}) collective-permute-start(bf16[128,2048]{1,0:T(8,128)(2,1)} %collective-permute-done.2.b1), channel_id=1, source_target_pairs={{0,1},{1,0},{2,3},{3,2},{4,8},{5,9},{6,10},{7,11},{8,4},{9,5},{10,... | collective-permute-start | bytes 1572872 | tf_op jit(solution)/shard_map/ppermute | solution.py:511
  67.4 26.8 %collective-permute-start.12 = (bf16[2,128,2048]{2,1,0:T(8,128)(2,1)}, bf16[2,128,2048]{2,1,0:T(8,128)(2,1)}, u32[]{:S(2)}, u32[]{:S(2)}) collective-permute-start(bf16[2,128,2048]{2,1,0:T(8,128)(2,1)} %pad_maximum_fusion.1), channel_id=1, source_target_pairs={{0,2},{1,3},{2,0},{3,1},{4,6},{5,7},{6,4},{7,5},{8,10},{9,11},{10,... | collective-permute-start | bytes 3145736 | tf_op jit(solution)/shard_map/ppermute | solution.py:509
  70.0 16.6 %collective-permute-start.9 = (bf16[128,2048]{1,0:T(8,128)(2,1)}, bf16[128,2048]{1,0:T(8,128)(2,1)}, u32[]{:S(2)}, u32[]{:S(2)}) collective-permute-start(bf16[128,2048]{1,0:T(8,128)(2,1)} %collective-permute-done.3.b2), channel_id=1, source_target_pairs={{0,4},{4,0},{8,12},{12,8},{1,5},{5,1},{9,13},{13,9},{2,6},{6,2},{1... | collective-permute-start | bytes 1572872 | tf_op jit(solution)/shard_map/ppermute | solution.py:511
  74.4 22.6 %collective-permute-start.10 = (bf16[128,2048]{1,0:T(8,128)(2,1)}, bf16[128,2048]{1,0:T(8,128)(2,1)S(1)}, u32[]{:S(2)}, u32[]{:S(2)}) collective-permute-start(bf16[128,2048]{1,0:T(8,128)(2,1)} %collective-permute-done.8.b3), channel_id=1, source_target_pairs={{0,4},{4,0},{8,12},{12,8},{1,5},{5,1},{9,13},{13,9},{2,6},{6,2},{1... | collective-permute-start | bytes 1572872 | tf_op jit(solution)/shard_map/ppermute | solution.py:512
  94.1 25.1 %collective-permute-start.15 = (bf16[128,2048]{1,0:T(8,128)(2,1)S(1)}, bf16[128,2048]{1,0:T(8,128)(2,1)}, u32[]{:S(2)}, u32[]{:S(2)}) collective-permute-start(bf16[128,2048]{1,0:T(8,128)(2,1)S(1)} %bitcast.44), channel_id=1, source_target_pairs={{0,4},{4,0},{8,12},{12,8},{1,5},{5,1},{9,13},{13,9},{2,6},{6,2},{1... | collective-permute-start | bytes 1572872 | tf_op jit(solution)/shard_map/ppermute | solution.py:516
  97.0 22.3 %collective-permute-start.16 = (bf16[128,2048]{1,0:T(8,128)(2,1)S(1)}, bf16[128,2048]{1,0:T(8,128)(2,1)S(1)}, u32[]{:S(2)}, u32[]{:S(2)}) collective-permute-start(bf16[128,2048]{1,0:T(8,128)(2,1)S(1)} %bitcast.45), channel_id=1, source_target_pairs={{0,1},{1,0},{2,3},{3,2},{4,8},{5,9},{6,10},{7,11},{8,4},{9,5},{10,... | collective-permute-start | bytes 1572872 | tf_op jit(solution)/shard_map/ppermute | solution.py:516
  98.2 69.5 %collective-permute-start.11 = (bf16[2,128,2048]{2,1,0:T(8,128)(2,1)}, bf16[2,128,2048]{2,1,0:T(8,128)(2,1)}, u32[]{:S(2)}, u32[]{:S(2)}) collective-permute-start(bf16[2,128,2048]{2,1,0:T(8,128)(2,1)} %pad_maximum_fusion.2), channel_id=1, source_target_pairs={{0,2},{1,3},{2,0},{3,1},{4,6},{5,7},{6,4},{7,5},{8,10},{9,11},{10,... | collective-permute-start | bytes 3145736 | tf_op jit(solution)/shard_map/ppermute | solution.py:518
  117.8 1.3 copy-start.17
  119.1 48.6 %copy-start.6 = (bf16[64,3584]{1,0:T(8,128)(2,1)S(1)}, bf16[64,3584]{1,0:T(8,128)(2,1)}, u32[]{:S(2)}) copy-start(bf16[64,3584]{1,0:T(8,128)(2,1)} %proj_gate.5) | copy-start | bytes 1376260
  119.1 48.6 %collective-permute-start.14 = (bf16[3584,128]{1,0:T(8,128)(2,1)}, bf16[3584,128]{1,0:T(8,128)(2,1)}, u32[]{:S(2)}, u32[]{:S(2)}) collective-permute-start(bf16[3584,128]{1,0:T(8,128)(2,1)} %get-tuple-element.26), channel_id=1, source_target_pairs={{0,2},{1,3},{2,0},{3,1},{4,6},{5,7},{6,4},{7,5},{8,10},{9,11},{10,... | collective-permute-start | bytes 2752520 | tf_op jit(solution)/shard_map/ppermute | solution.py:528
  120.0 4.4 %collective-permute-start.18 = (bf16[128,2048]{1,0:T(8,128)(2,1)}, bf16[128,2048]{1,0:T(8,128)(2,1)}, u32[]{:S(2)}, u32[]{:S(2)}) collective-permute-start(bf16[128,2048]{1,0:T(8,128)(2,1)} %collective-permute-done.15.b1), channel_id=1, source_target_pairs={{0,1},{1,0},{2,3},{3,2},{4,8},{5,9},{6,10},{7,11},{8,4},{9,5},{10,... | collective-permute-start | bytes 1572872 | tf_op jit(solution)/shard_map/ppermute | solution.py:523
  121.2 45.3 %all-reduce.2.cloned.1.call-start = ((), (), s32[]{:S(2)}) async-start(), calls=%async_computation | async-start | bytes 786432 | tf_op jit(solution)/shard_map/psum | solution.py:502
  122.0 57.2 %collective-permute-start.17 = (bf16[128,2048]{1,0:T(8,128)(2,1)}, bf16[128,2048]{1,0:T(8,128)(2,1)}, u32[]{:S(2)}, u32[]{:S(2)}) collective-permute-start(bf16[128,2048]{1,0:T(8,128)(2,1)} %copy-done.13), channel_id=1, source_target_pairs={{0,4},{4,0},{8,12},{12,8},{1,5},{5,1},{9,13},{13,9},{2,6},{6,2},{1... | collective-permute-start | bytes 1572872 | tf_op jit(solution)/shard_map/ppermute | solution.py:523
  124.4 59.6 %collective-permute-start.19 = (bf16[128,2048]{1,0:T(8,128)(2,1)}, bf16[128,2048]{1,0:T(8,128)(2,1)}, u32[]{:S(2)}, u32[]{:S(2)}) collective-permute-start(bf16[128,2048]{1,0:T(8,128)(2,1)} %collective-permute-done.18.b3), channel_id=1, source_target_pairs={{0,4},{4,0},{8,12},{12,8},{1,5},{5,1},{9,13},{13,9},{2,6},{6,2},{1... | collective-permute-start | bytes 1572872 | tf_op jit(solution)/shard_map/ppermute | solution.py:524
  171.1 1.5 copy-start.18
  172.6 6.6 %copy-start.14 = (bf16[128,2048]{1,0:T(8,128)(2,1)S(1)}, bf16[128,2048]{1,0:T(8,128)(2,1)}, u32[]{:S(2)}) copy-start(bf16[128,2048]{1,0:T(8,128)(2,1)} %copy-done.13) | copy-start | bytes 1572868
  177.8 4.3 %collective-permute-start.21 = (f32[128,128]{1,0:T(8,128)S(1)}, f32[128,128]{1,0:T(8,128)S(1)}, u32[]{:S(2)}, u32[]{:S(2)}) collective-permute-start(f32[128,128]{1,0:T(8,128)S(1)} %shard_map.156), channel_id=1, source_target_pairs={{0,4},{4,0},{8,12},{12,8},{1,5},{5,1},{9,13},{13,9},{2,6},{6,2},{1... | collective-permute-start | bytes 196616 | tf_op jit(solution)/shard_map/ppermute | solution.py:472
  182.1 6.5 %collective-permute-start.22 = (f32[128,128]{1,0:T(8,128)S(1)}, f32[128,128]{1,0:T(8,128)S(1)}, u32[]{:S(2)}, u32[]{:S(2)}) collective-permute-start(f32[128,128]{1,0:T(8,128)S(1)} %add.25), channel_id=1, source_target_pairs={{0,8},{4,12},{8,0},{12,4},{1,9},{5,13},{9,1},{13,5},{2,10},{6,14},... | collective-permute-start | bytes 196616 | tf_op jit(solution)/shard_map/ppermute | solution.py:473
  185.3 3.3 %copy-start.24 = (s32[2]{0:T(128)S(1)}, s32[2]{0:T(128)}, u32[]{:S(2)}) copy-start(s32[2]{0:T(128)} %lengths.1) | copy-start | bytes 28
  185.3 4.8 %copy-start.4 = (bf16[2,64,2048]{2,1,0:T(8,128)(2,1)S(1)}, bf16[2,64,2048]{2,1,0:T(8,128)(2,1)}, u32[]{:S(2)}) copy-start(bf16[2,64,2048]{2,1,0:T(8,128)(2,1)} %get-tuple-element.37) | copy-start | bytes 1572868
  185.3 4.8 %copy-start.16 = (bf16[128,2048]{1,0:T(8,128)(2,1)S(1)}, bf16[128,2048]{1,0:T(8,128)(2,1)}, u32[]{:S(2)}) copy-start(bf16[128,2048]{1,0:T(8,128)(2,1)} %copy-done.15) | copy-start | bytes 1572868
  185.3 24.1 %collective-permute-start.26 = (bf16[2,128,2048]{2,1,0:T(8,128)(2,1)S(1)}, bf16[2,128,2048]{2,1,0:T(8,128)(2,1)S(1)}, u32[]{:S(2)}, u32[]{:S(2)}) collective-permute-start(bf16[2,128,2048]{2,1,0:T(8,128)(2,1)S(1)} %pad_maximum_fusion.3), channel_id=1, source_target_pairs={{0,2},{1,3},{2,0},{3,1},{4,6},{5,7},{6,4},{7,5},{8,10},{9,11},{10,... | collective-permute-start | bytes 3145736 | tf_op jit(solution)/shard_map/ppermute | solution.py:531
  189.6 19.9 %copy-start.2 = (bf16[4,64,3584]{2,1,0:T(8,128)(2,1)S(1)}, bf16[4,64,3584]{2,1,0:T(8,128)(2,1)}, u32[]{:S(2)}) copy-start(bf16[4,64,3584]{2,1,0:T(8,128)(2,1)} %param.18) | copy-start | bytes 5505028
  189.6 19.9 %copy-start.8 = (bf16[64,3584]{1,0:T(8,128)(2,1)S(1)}, bf16[64,3584]{1,0:T(8,128)(2,1)}, u32[]{:S(2)}) copy-start(bf16[64,3584]{1,0:T(8,128)(2,1)} %proj_up.5) | copy-start | bytes 1376260
  189.6 18.4 %collective-permute-start.23 = (f32[2,192,64]{2,1,0:T(8,128)S(1)}, f32[2,192,64]{2,1,0:T(8,128)S(1)}, u32[]{:S(2)}, u32[]{:S(2)}) collective-permute-start(f32[2,192,64]{2,1,0:T(8,128)S(1)} %shard_map.159.q0), channel_id=1, source_target_pairs={{0,1},{1,0},{2,3},{3,2},{4,5},{5,4},{6,7},{7,6},{8,9},{9,8},{10,11... | collective-permute-start | bytes 294920 | tf_op jit(solution)/shard_map/ppermute | solution.py:538
  189.6 46.5 %collective-permute-start.24 = (f32[2,192,64]{2,1,0:T(8,128)S(1)}, f32[2,192,64]{2,1,0:T(8,128)S(1)}, u32[]{:S(2)}, u32[]{:S(2)}) collective-permute-start(f32[2,192,64]{2,1,0:T(8,128)S(1)} %shard_map.159.q0), channel_id=1, source_target_pairs={{0,2},{1,3},{2,0},{3,1},{4,6},{5,7},{6,4},{7,5},{8,10},{9,11},{10,... | collective-permute-start | bytes 294920 | tf_op jit(solution)/shard_map/ppermute | solution.py:539
  206.3 27.0 %collective-permute-start.20 = (bf16[3584,128]{1,0:T(8,128)(2,1)S(1)}, bf16[3584,128]{1,0:T(8,128)(2,1)S(1)}, u32[]{:S(2)}, u32[]{:S(2)}) collective-permute-start(bf16[3584,128]{1,0:T(8,128)(2,1)S(1)} %get-tuple-element.33), channel_id=1, source_target_pairs={{0,2},{1,3},{2,0},{3,1},{4,6},{5,7},{6,4},{7,5},{8,10},{9,11},{10,... | collective-permute-start | bytes 2752520 | tf_op jit(solution)/shard_map/ppermute | solution.py:546
  207.9 28.3 %collective-permute-start.25 = (f32[2,192,64]{2,1,0:T(8,128)S(1)}, f32[2,192,64]{2,1,0:T(8,128)S(1)}, u32[]{:S(2)}, u32[]{:S(2)}) collective-permute-start(f32[2,192,64]{2,1,0:T(8,128)S(1)} %collective-permute-done.23.q1), channel_id=1, source_target_pairs={{0,2},{1,3},{2,0},{3,1},{4,6},{5,7},{6,4},{7,5},{8,10},{9,11},{10,... | collective-permute-start | bytes 294920 | tf_op jit(solution)/shard_map/ppermute | solution.py:539
  209.4 20.3 %copy-start.25 = (s32[4]{0:T(128)S(1)}, s32[4]{0:T(128)}, u32[]{:S(2)}) copy-start(s32[4]{0:T(128)} %param.20) | copy-start | bytes 52
  227.7 9.7 %collective-permute-start.27 = (f32[128,128]{1,0:T(8,128)S(1)}, f32[128,128]{1,0:T(8,128)S(1)}, u32[]{:S(2)}, u32[]{:S(2)}) collective-permute-start(f32[128,128]{1,0:T(8,128)S(1)} %get-tuple-element.44), channel_id=1, source_target_pairs={{0,2},{1,3},{2,0},{3,1},{4,6},{5,7},{6,4},{7,5},{8,10},{9,11},{10,... | collective-permute-start | bytes 196616 | tf_op jit(solution)/shard_map/ppermute | solution.py:554
  238.6 3.7 %collective-permute-start.28 = (f32[4,8]{1,0:T(4,128)S(1)}, f32[4,8]{1,0:T(4,128)S(1)}, u32[]{:S(2)}, u32[]{:S(2)}) collective-permute-start(f32[4,8]{1,0:T(4,128)S(1)} %pad_maximum_fusion.4), channel_id=1, source_target_pairs={{0,4},{4,0},{8,12},{12,8},{1,5},{5,1},{9,13},{13,9},{2,6},{6,2},{1... | collective-permute-start | bytes 392 | tf_op jit(solution)/shard_map/ppermute | solution.py:472
  242.2 4.5 %collective-permute-start.29 = (f32[4,8]{1,0:T(4,128)S(1)}, f32[4,8]{1,0:T(4,128)S(1)}, u32[]{:S(2)}, u32[]{:S(2)}) collective-permute-start(f32[4,8]{1,0:T(4,128)S(1)} %fusion), channel_id=1, source_target_pairs={{0,8},{4,12},{8,0},{12,4},{1,9},{5,13},{9,1},{13,5},{2,10},{6,14},... | collective-permute-start | bytes 392 | tf_op jit(solution)/shard_map/ppermute | solution.py:473
  (11 other events, 11.9 us)
Sparse Core Ops, SparseCore 0:
  124.4 42.1 all-reduce.1

commit v4 on v3

--- a/solution.py
+++ b/solution.py
@@ -10,7 +10,7 @@
 RANK = 64
 SEQ = 64
 TILE = 512
-VMEM_BYTES = 40 * 1024 * 1024
+VMEM_BYTES = 58 * 1024 * 1024
 
 
 def flatten(array):
@@ -143,41 +143,63 @@
     return pl.BlockSpec(shape, lambda i: tuple(0 for _ in shape))
 
 
-def stacked_products(flags, pairs, far, weight_own, weight_sib, stacked, semaphores):
-    number = far.shape[1]
-
-    @pl.when(pl.program_id(0) == 0)
+def stacked_products(flags, blocks, weights, stacked, held, row_sems, weight_sems):
+    own, pa, cross, pb, qa, qb, qc, pc, next_cross, next_pa = blocks
+    picks = (
+        (own, pa, cross, pb),
+        (pa, own, pb, cross),
+        (qb, qa, next_cross, qc),
+        (pc, pb, next_cross, next_pa),
+    )
+    number = own.shape[0]
+    step = pl.program_id(0)
+
+    def weight_copies(tile):
+        part = pl.ds(pl.multiple_of(tile * TILE, TILE), TILE)
+        return [
+            pltpu.make_async_copy(
+                weights[side].at[part], held.at[side, part], weight_sems.at[side, tile]
+            )
+            for side in range(2)
+        ]
+
+    @pl.when(step == 0)
     def _():
-        slot = flags[1]
-        far_copies = [
-            pltpu.make_async_copy(
-                far.at[i], stacked.at[jnp.bitwise_xor(slot, i), pl.ds(number, number)],
-                semaphores.at[2 + i],
-            )
-            for i in range(2)
-        ]
-        for copy in far_copies:
-            copy.start()
-        for code, pair in enumerate(pairs):
+        for code, pick in enumerate(picks):
 
             @pl.when(flags[0] == code)
             def _():
                 copies = [
                     pltpu.make_async_copy(
-                        pair[i], stacked.at[jnp.bitwise_xor(slot, i), pl.ds(0, number)],
-                        semaphores.at[i],
+                        block,
+                        stacked.at[
+                            jnp.bitwise_xor(flags[1], i % 2), pl.ds((i // 2) * number, number)
+                        ],
+                        row_sems.at[i],
                     )
-                    for i in range(2)
+                    for i, block in enumerate(pick)
                 ]
                 for copy in copies:
                     copy.start()
+                for tile in range(held.shape[1] // TILE):
+                    for copy in weight_copies(tile):
+                        copy.start()
                 for copy in copies:
                     copy.wait()
 
-        for copy in far_copies:
-            copy.wait()
-
-    return project(weight_own[...], stacked[0]) + project(weight_sib[...], stacked[1])
+    for copy in weight_copies(step):
+        copy.wait()
+    part = pl.ds(pl.multiple_of(step * TILE, TILE), TILE)
+    return project(held[0, part, :], stacked[0]) + project(held[1, part, :], stacked[1])
+
+
+def product_scratch(number, half, units):
+    return [
+        pltpu.VMEM((2, 2 * number, half), jnp.bfloat16),
+        pltpu.VMEM((2, units, half), jnp.bfloat16),
+        pltpu.SemaphoreType.DMA((4,)),
+        pltpu.SemaphoreType.DMA((2, units // TILE)),
+    ]
 
 
 def add_sides(hidden_grad, gate, up, proj_gate, proj_up, sides):
@@ -194,35 +216,32 @@
         sides[...] += part
 
 
-def partial_kernel(
-    flags, b0, b1, b2, b3, b4, b5, far, weight_own, weight_sib, near_sum, far_sum, stacked, sems
-):
-    pairs = ((b0, b1), (b2, b3), (b4, b5))
-    total = stacked_products(flags, pairs, far, weight_own, weight_sib, stacked, sems)
-    number = far.shape[1]
+def partial_kernel(*refs):
+    flags, blocks, weights, (near_sum, far_sum), scratch = (
+        refs[0], refs[1:11], refs[11:13], refs[13:15], refs[15:]
+    )
+    total = stacked_products(flags, blocks, weights, *scratch)
+    number = blocks[0].shape[0]
     near_sum[...] = total[:, :number]
     far_sum[...] = total[:, number:].astype(jnp.bfloat16)
 
 
-def partial_sums(flags, blocks, far, weight_own, weight_sib):
+def partial_sums(flags, blocks, weights):
     number, half = blocks[0].shape
-    units = weight_own.shape[0]
+    units = weights[0].shape[0]
     return pl.pallas_call(
         partial_kernel,
         grid=(units // TILE,),
-        in_specs=[SCALARS] + [ANYWHERE] * 7 + [tile_rows(half)] * 2,
+        in_specs=[SCALARS] + [ANYWHERE] * 12,
         out_specs=[tile_rows(number)] * 2,
         out_shape=[
             jax.ShapeDtypeStruct((units, number), jnp.float32),
             jax.ShapeDtypeStruct((units, number), jnp.bfloat16),
         ],
-        scratch_shapes=[
-            pltpu.VMEM((2, 2 * number, half), jnp.bfloat16),
-            pltpu.SemaphoreType.DMA((4,)),
-        ],
+        scratch_shapes=product_scratch(number, half, units),
         compiler_params=params(),
-        cost_estimate=cost(8 * number * half * units, (far, weight_own, weight_sib)),
-    )(flags, *blocks, far, weight_own, weight_sib)
+        cost_estimate=cost(8 * number * half * units, weights),
+    )(flags, *blocks, *weights)
 
 
 def finish_kernel(near_sum, returned, gate, up, proj_gate, proj_up, sides):
@@ -243,90 +262,83 @@
     )(near_sum, returned, gate, up, proj_gate, proj_up)
 
 
-def lent_kernel(
-    flags, b0, b1, b2, b3, b4, b5, far, weight_own, weight_sib, gate, up, far_gate, far_up,
-    proj_gate, proj_up, sides, stacked, sems,
-):
-    pairs = ((b0, b1), (b2, b3), (b4, b5))
-    total = stacked_products(flags, pairs, far, weight_own, weight_sib, stacked, sems)
+def lent_kernel(*refs):
+    flags, blocks, weights, operands, sides, scratch = (
+        refs[0], refs[1:11], refs[11:13], refs[13:19], refs[19], refs[20:]
+    )
+    gate, up, far_gate, far_up, proj_gate, proj_up = operands
+    total = stacked_products(flags, blocks, weights, *scratch)
     gates = jnp.concatenate([gate[...], far_gate[...]], axis=0)
     ups = jnp.concatenate([up[...], far_up[...]], axis=0)
     add_sides(total.T, gates, ups, proj_gate[...], proj_up[...], sides)
 
 
-def lent_sides(
-    flags, blocks, far, weight_own, weight_sib, gate, up, far_gate, far_up, proj_gate, proj_up
-):
+def lent_sides(flags, blocks, weights, gate, up, far_gate, far_up, proj_gate, proj_up):
     number, half = blocks[0].shape
-    units = weight_own.shape[0]
+    units = weights[0].shape[0]
     return pl.pallas_call(
         lent_kernel,
         grid=(units // TILE,),
         in_specs=[SCALARS]
-        + [ANYWHERE] * 7
-        + [tile_rows(half)] * 2
+        + [ANYWHERE] * 12
         + [tile_columns(number, 1)] * 2
         + [tile_columns(number)] * 2
         + [tile_columns(RANK)] * 2,
         out_specs=whole((2 * number, 2 * RANK)),
         out_shape=jax.ShapeDtypeStruct((2 * number, 2 * RANK), jnp.float32),
-        scratch_shapes=[
-            pltpu.VMEM((2, 2 * number, half), jnp.bfloat16),
-            pltpu.SemaphoreType.DMA((4,)),
-        ],
+        scratch_shapes=product_scratch(number, half, units),
         compiler_params=params(),
-        cost_estimate=cost(8 * number * half * units, (far, weight_own, weight_sib)),
-    )(
-        flags, *blocks, far, weight_own, weight_sib, gate, up, far_gate, far_up, proj_gate, proj_up
-    )
+        cost_estimate=cost(8 * number * half * units, weights),
+    )(flags, *blocks, *weights, gate, up, far_gate, far_up, proj_gate, proj_up)
 
 
 def early_kernel(
     t_input, q_input, t_outgrad, q_outgrad, proj_input, proj_outgrad, t_gate, t_up, q_gate, q_up,
-    proj_hidden, sides,
+    proj_hidden, in_out, hidden,
 ):
     number = t_input.shape[0]
-    middle = pl.ds(RANK, RANK)
     t_hidden = project(gated_hidden(t_gate[...], t_up[...]), proj_hidden[...])
     q_hidden = project(gated_hidden(q_gate[...], q_up[...]), proj_hidden[...])
     first = pl.program_id(0) == 0
 
     @pl.when(first)
     def _():
-        for inputs, outgrad, hidden, part in (
-            (t_input, t_outgrad, t_hidden, slice(0, number)),
-            (q_input, q_outgrad, q_hidden, slice(number, None)),
+        for inputs, outgrad, part in (
+            (t_input, t_outgrad, slice(0, number)),
+            (q_input, q_outgrad, slice(number, None)),
         ):
-            sides[part, :] = jnp.concatenate(
+            in_out[part, :] = jnp.concatenate(
                 [
                     project(inputs[...], proj_input[...]),
-                    hidden,
                     project(outgrad[...], proj_outgrad[...]),
                 ],
                 axis=1,
             )
+        hidden[:number, :] = t_hidden
+        hidden[number:, :] = q_hidden
 
     @pl.when(jnp.logical_not(first))
     def _():
-        sides[:number, middle] += t_hidden
-        sides[number:, middle] += q_hidden
+        hidden[:number, :] += t_hidden
+        hidden[number:, :] += q_hidden
 
 
 def early_sides(
     t_input, q_input, t_outgrad, q_outgrad, proj_input, proj_outgrad, t_gate, t_up, q_gate, q_up,
     proj_hidden,
 ):
-    train, query, units = t_gate.shape[0], q_gate.shape[0], t_gate.shape[1]
+    total, units = t_gate.shape[0] + q_gate.shape[0], t_gate.shape[1]
     wide = (t_input, q_input, t_outgrad, q_outgrad, proj_input, proj_outgrad)
     tiled = (t_gate, t_up, q_gate, q_up, proj_hidden)
+    shapes = ((total, 2 * RANK), (total, RANK))
     return pl.pallas_call(
         early_kernel,
         grid=(units // TILE,),
         in_specs=[whole(a.shape) for a in wide] + [tile_columns(a.shape[0]) for a in tiled],
-        out_specs=whole((train + query, 3 * RANK)),
-        out_shape=jax.ShapeDtypeStruct((train + query, 3 * RANK), jnp.float32),
+        out_specs=[whole(shape) for shape in shapes],
+        out_shape=[jax.ShapeDtypeStruct(shape, jnp.float32) for shape in shapes],
         compiler_params=params(),
-        cost_estimate=cost(2 * (train + query) * RANK * units, wide + tiled),
+        cost_estimate=cost(2 * total * RANK * units, wide + tiled),
     )(*wide, *tiled)
 
 
@@ -350,33 +362,33 @@
     )
 
 
-def query_kernel(lengths, sides, gradient, found):
+def query_kernel(lengths, in_out, sums, found):
     for e in range(found.shape[0]):
         part = slice(e * SEQ, (e + 1) * SEQ)
         three = example_features(
-            sides[part, :RANK],
-            sides[part, RANK : 2 * RANK],
-            gradient[part, :RANK],
-            gradient[part, RANK:],
-            sides[part, 2 * RANK :],
+            in_out[part, :RANK],
+            sums[part, 2 * RANK :],
+            sums[part, :RANK],
+            sums[part, RANK : 2 * RANK],
+            in_out[part, RANK:],
             lengths[e],
         )
         for segment in range(3):
             found[e, segment * RANK : (segment + 1) * RANK, :] = three[segment]
 
 
-def query_features(lengths, sides, gradient):
+def query_features(lengths, in_out, sums):
     return pl.pallas_call(
         query_kernel,
         in_specs=[SCALARS, IN_VMEM, IN_VMEM],
         out_specs=IN_VMEM,
         out_shape=jax.ShapeDtypeStruct((lengths.shape[0], 3 * RANK, RANK), jnp.float32),
         compiler_params=params(),
-    )(lengths, sides, gradient)
+    )(lengths, in_out, sums)
 
 
 def score_kernel(
-    lengths, place, whole_sides, own_sides, near, far, q0, q1, q2, q3, scores
+    lengths, place, in_out, hidden, near, far, q0, q1, q2, q3, scores
 ):
     queries = q0.shape[0]
     shape = scores.shape
@@ -388,11 +400,11 @@
         gradient = near[part, :] + far[part, :]
         three = jnp.concatenate(
             example_features(
-                whole_sides[part, :RANK],
-                own_sides[part, RANK : 2 * RANK],
+                in_out[part, :RANK],
+                hidden[part, :],
                 gradient[:, :RANK],
                 gradient[:, RANK:],
-                whole_sides[part, 2 * RANK :],
+                in_out[part, RANK:],
                 lengths[e],
             ),
             axis=0,
@@ -407,7 +419,7 @@
     scores[...] = total
 
 
-def partial_scores(lengths, place, whole_sides, own_sides, near, far, found):
+def partial_scores(lengths, place, in_out, hidden, near, far, found):
     number = lengths.shape[0]
     return pl.pallas_call(
         score_kernel,
@@ -415,7 +427,7 @@
         out_specs=IN_VMEM,
         out_shape=jax.ShapeDtypeStruct((number, 4 * found[0].shape[0]), jnp.float32),
         compiler_params=params(),
-    )(lengths, place, whole_sides, own_sides, near, far, *found)
+    )(lengths, place, in_out, hidden, near, far, *found)
 
 
 def after(value, *others):
@@ -442,12 +454,10 @@
 ):
     t = lax.axis_index("tensor")
     d = lax.axis_index("dp")
-    x, core, upper = d // 2, d % 2, t // 2
-    at_home = x == upper
-    inner_chip = (t == 1) | (t == 2)
-    near_code = jnp.where(at_home, 0, jnp.where(inner_chip, 1, 2))
-    first_parity = jnp.where(at_home, t % 2, upper)
-    flags = jnp.stack([near_code, first_parity ^ core]).astype(jnp.int32)
+    x, core = d // 2, d % 2
+    u = jnp.where(x == 0, t, 3 - t)
+    at_home = u < 2
+    flags = jnp.stack([u, core ^ x]).astype(jnp.int32)
     place = jnp.stack([d]).astype(jnp.int32)
 
     to_core = functools.partial(lax.ppermute, axis_name="dp", perm=[(i, i ^ 1) for i in range(4)])
@@ -472,15 +482,6 @@
         values = values + outer(values)
         return values + across(values)
 
-    def crossing_pair(piece, first, second_inner, third_inner, second_outer, third_outer):
-        def choose(within, beyond_inner, beyond_outer):
-            beyond = jnp.where(inner_chip, beyond_inner, beyond_outer)
-            return jnp.where(at_home, beyond, within)
-
-        return jnp.stack(
-            [choose(piece, second_inner, second_outer), choose(first, third_inner, third_outer)]
-        )
-
     q_input, q_gate, q_up, q_outgrad = [
         flatten(a) for a in (query_input, query_gate, query_up, query_outgrad)
     ]
@@ -490,67 +491,74 @@
     examples = train_lengths.shape[0] // 2
     cut = examples * SEQ
 
-    weight_own, weight_sib = down_weight, to_core(down_weight)
-
-    q_one, q_mid = outer(q_outgrad), middle(q_outgrad)
-    lent = to_chip(jnp.stack([t_gate[cut:], t_up[cut:]]))
-    own_sides = early_sides(
+    def begin(own, previous):
+        if previous is None:
+            return outer(own), to_chip(own), middle(own)
+        qb, pc, qc = previous
+        transit = jnp.where(u == 1, qb, pc)
+        return (
+            outer(jnp.where(u == 2, qc, own)),
+            to_chip(jnp.where(at_home, transit, own)),
+            middle(own),
+        )
+
+    def second(pa, cross, qa):
+        return outer(jnp.where(u == 2, qa, cross)), middle(pa)
+
+    weights = (down_weight, to_core(down_weight))
+
+    q_pa, q_cross, q_qa = begin(q_outgrad, None)
+    q_pb, q_qb = second(q_pa, q_cross, q_qa)
+    own_in_out, hidden = early_sides(
         t_input, q_input, t_outgrad, q_outgrad, proj_input, proj_outgrad, t_gate, t_up, q_gate,
         q_up, proj_hidden,
     )
-    q_two, q_last = outer(q_mid), middle(q_one)
-    whole_sides = lax.psum(own_sides, "tensor")
-    q_three = outer(after(q_last, own_sides))
-    q_blocks = (q_outgrad, q_one, q_mid, q_last, q_two, q_three)
-
-    a_rows = after(t_outgrad[:cut], q_two)
-    a_one, a_mid = outer(a_rows), middle(a_rows)
-    q_send = crossing_pair(*q_blocks)
-    q_far = to_chip(q_send)
-    a_one, a_mid = lax.optimization_barrier((a_one, a_mid, q_send, lent))[:2]
-    a_two, a_last = outer(a_mid), middle(a_one)
-    a_three = outer(a_last)
-    a_blocks = (a_rows, a_one, a_mid, a_last, a_two, a_three)
-
-    b_rows = after(t_outgrad[cut:], a_two, q_far)
-    b_one, b_mid = outer(b_rows), middle(b_rows)
-    a_send = crossing_pair(*a_blocks)
-    a_far = to_chip(a_send)
-    q_near_sum, q_far_sum = partial_sums(
-        flags, q_blocks, after(q_far, a_send), weight_own, weight_sib
-    )
-    b_one, b_mid = lax.optimization_barrier((b_one, b_mid, q_far_sum))[:2]
-    b_two, b_last = outer(b_mid), middle(b_one)
-    b_three = outer(b_last)
-    b_blocks = (b_rows, b_one, b_mid, b_last, b_two, b_three)
-
-    q_gradient = finished_sides(
-        q_near_sum, after(to_chip(q_far_sum), a_far), q_gate, q_up, proj_gate, proj_up
-    )
-    b_send = crossing_pair(*b_blocks)
-    b_far = to_chip(b_send)
-    a_near_sum, a_far_sum = partial_sums(
-        flags, a_blocks, after(a_far, q_gradient, b_send), weight_own, weight_sib
-    )
+    far_gate = to_chip(after(t_gate[cut:], q_cross))
+    q_qb = after(q_qb, own_in_out, q_pb)
+    q_pc, q_qc = outer(q_qb), middle(q_cross)
+    in_out = tensor_sum(own_in_out)
+
+    a_own = t_outgrad[:cut]
+    a_pa, a_cross, a_qa = begin(a_own, (q_qb, q_pc, q_qc))
+    a_pb, a_qb = second(a_pa, a_cross, a_qa)
+    q_blocks = (q_outgrad, q_pa, q_cross, q_pb, q_qa, q_qb, q_qc, q_pc, a_cross, a_pa)
+    q_near_sum, q_far_sum = partial_sums(flags, q_blocks, weights)
+    far_up = to_chip(after(t_up[cut:], a_cross, far_gate))
+    a_qb = after(a_qb, q_far_sum, a_pb, in_out)
+    q_returned = to_chip(q_far_sum)
+    a_pc, a_qc = outer(a_qb), middle(a_cross)
+
+    b_own = t_outgrad[cut:]
+    b_pa, b_cross, b_qa = begin(b_own, (a_qb, a_pc, after(a_qc, far_up)))
+    b_pb, b_qb = second(after(b_pa, q_returned), b_cross, b_qa)
+    a_blocks = (a_own, a_pa, a_cross, a_pb, a_qa, a_qb, a_qc, a_pc, b_cross, b_pa)
+    a_near_sum, a_far_sum = partial_sums(flags, a_blocks, weights)
+    b_qb = after(b_qb, a_far_sum, b_pb)
+    b_pc, b_qc = outer(b_qb), middle(b_cross)
+    q_gradient = finished_sides(q_near_sum, q_returned, q_gate, q_up, proj_gate, proj_up)
+    b_qc = after(b_qc, q_gradient)
+    c_pa, c_cross = outer(b_qc), to_chip(jnp.where(u == 1, b_qb, b_pc))
+    b_blocks = (b_own, b_pa, b_cross, b_pb, b_qa, b_qb, b_qc, b_pc, c_cross, c_pa)
+
     own_found = query_features(
-        query_lengths, whole_sides[2 * cut :], tensor_sum(q_gradient)
+        query_lengths,
+        in_out[2 * cut :],
+        tensor_sum(jnp.concatenate([q_gradient, hidden[2 * cut :]], axis=1)),
     )
     core_found = to_core(own_found)
     found = (own_found, core_found, to_chip(own_found), to_chip(core_found))
-
-    b_gradient = lent_sides(
-        flags, b_blocks, after(b_far, own_found), weight_own, weight_sib, t_gate, t_up, lent[0],
-        lent[1], proj_gate, proj_up,
-    )
     a_gradient = finished_sides(
         a_near_sum, to_chip(a_far_sum), t_gate, t_up, proj_gate, proj_up
     )
+    b_gradient = lent_sides(
+        after(flags, a_gradient, core_found), b_blocks, weights, t_gate, t_up, far_gate, far_up, proj_gate, proj_up
+    )
     a_scores = partial_scores(
-        train_lengths[:examples], place, whole_sides[:cut], own_sides[:cut], a_gradient,
+        train_lengths[:examples], place, in_out[:cut], hidden[:cut], a_gradient,
         jnp.zeros_like(a_gradient), found,
     )
     b_scores = partial_scores(
-        train_lengths[examples:], place, whole_sides[cut : 2 * cut], own_sides[cut : 2 * cut],
+        train_lengths[examples:], place, in_out[cut : 2 * cut], hidden[cut : 2 * cut],
         b_gradient[:cut], to_chip(b_gradient[cut:]), found,
     )
     scores = tensor_sum(jnp.concatenate([a_scores, b_scores], axis=0))

time: 255 us -> 258 us (1.012)
  Pallas kernels: 67.7 us -> 94.6 us
  between operations: 13.8 us -> 0.45 us
  waiting for transfers between devices: 87.2 us -> 99.7 us
  starting transfers between devices: 56.1 us -> 43.7 us
  local copies, waits for them, and re-layouts: 19.4 us -> 10.1 us
    psum x1 -> x0, waiting for transfers between devices: 30.7 us -> none  [moving_plan(): whole_sides = lax.psum(own_sides, 'tensor')]
    ppermute x21 -> x27, waiting for transfers between devices: 44.9 us -> 73.8 us  [the longest x3 17.1 us: begin(): return (outer(own), to_chip(own), middle(own))]
    ppermute x21 -> x27, starting transfers between devices: 45.5 us -> 27.5 us  [the longest x3 5.64 us: begin(): return (outer(own), to_chip(own), middle(own))]
    ppermute x2 -> x3, waiting for transfers between devices: 3.43 us -> 20.1 us  [tensor_sum(): return values + across(values)]
    unnamed x52 -> x80, local copies, waits for them, and re-layouts: 13.6 us -> 3.69 us
    another operation x11 -> x1, other arithmetic: 9.43 us -> 0.65 us  [moving_plan(): flags = jnp.stack([u, core ^ x]).astype(jnp.int32)]
    pallas_call x2, Pallas kernels: 33.1 us -> 40.4 us  [partial_sums(): pl.pallas_call(partial_kernel, grid=(units // TILE,), in_specs=[SCALARS]...]
    pallas_call x1, Pallas kernels: 18.2 us -> 25 us  [lent_sides(): pl.pallas_call(lent_kernel, grid=(units // TILE,), in_specs=[SCALARS] + [...]
  transfers between devices with their start and end apart: 31 -> 38, of which waited for: 12 -> 17; matrix products, arithmetic and copies ran while one was open for 6% -> 5% of each run, Pallas kernels for 26% -> 36%
where the time goes in v4:
time: 258 us; the launch traced here: 257 us
  waiting for transfers between devices  99.7 us (39%)
  Pallas kernels  94.6 us (37%)
  starting transfers between devices  43.7 us (17%)
  local copies, waits for them, and re-layouts  10.1 us (4%)
  other arithmetic  8.7 us (3%)
    pallas_call x2, Pallas kernels, partial_sums(): pl.pallas_call(partial_kernel, grid=(units // TILE,), in_specs=[SCALARS]...  40.4 us
    pallas_call x1, Pallas kernels, lent_sides(): pl.pallas_call(lent_kernel, grid=(units // TILE,), in_specs=[SCALARS] + [...  25 us
    ppermute x3, waiting for transfers between devices, tensor_sum(): return values + across(values)  20.1 us
    ppermute x3, waiting for transfers between devices, begin(): return (outer(own), to_chip(own), middle(own))  17.1 us
    pallas_call x2, Pallas kernels, finished_sides(): pl.pallas_call(finish_kernel, grid=(units // TILE,), in_specs=[tile_rows(...  13.2 us
    ppermute x2, waiting for transfers between devices, moving_plan(): q_pc, q_qc = (outer(q_qb), middle(q_cross))  10.7 us
    ppermute x1, waiting for transfers between devices, moving_plan(): far_gate = to_chip(after(t_gate[cut:], q_cross))  10.7 us
    ppermute x2, waiting for transfers between devices, moving_plan(): a_pc, a_qc = (outer(a_qb), middle(a_cross))  9.56 us
  transfers between devices with their start and end apart: 38, of which 17 were waited for; matrix products, arithmetic and copies ran while one was open for 5% of the time, Pallas kernels for 36%

profile of v4, /device:TPU:0, one launch (start us, length us, event | category | flops | bytes accessed | tf_op | source)
XLA Modules:
  0.0 257.3 jit_solution(3548496550762464014)
XLA Ops:
  0.5 2.5 collective-permute-start.2
  3.2 2.9 %collective-permute-start.5 = (bf16[128,2048]{1,0:T(8,128)(2,1)}, bf16[128,2048]{1,0:T(8,128)(2,1)S(1)}, u32[]{:S(2)}, u32[]{:S(2)}) collective-permute-start(bf16[128,2048]{1,0:T(8,128)(2,1)} %bitcast.36), channel_id=1, source_target_pairs={{0,4},{4,0},{8,12},{12,8},{1,5},{5,1},{9,13},{13,9},{2,6},{6,2},{1... | collective-permute-start | bytes 1572872 | tf_op jit(solution)/shard_map/ppermute | solution.py:496
  6.1 9.8 %collective-permute-done.2.refs_3_ = bf16[128,2048]{1,0:T(8,128)(2,1)} collective-permute-done((bf16[128,2048]{1,0:T(8,128)(2,1)}, bf16[128,2048]{1,0:T(8,128)(2,1)}, u32[]{:S(2)}, u32[]{:S(2)}) %collective-permute-start.2) | collective-permute-done | bytes 524320 | tf_op jit(solution)/shard_map/ppermute | solution.py:496
  15.9 7.3 %collective-permute-done.7.refs_5_ = bf16[128,2048]{1,0:T(8,128)(2,1)S(1)} collective-permute-done((bf16[128,2048]{1,0:T(8,128)(2,1)}, bf16[128,2048]{1,0:T(8,128)(2,1)S(1)}, u32[]{:S(2)}, u32[]{:S(2)}) %collective-permute-start.7) | collective-permute-done | bytes 524320 | tf_op jit(solution)/shard_map/ppermute | solution.py:496
  23.2 1.3 broadcast_select_fusion.4
  25.0 9.1 %shard_map.154 = (f32[384,128]{1,0:T(8,128)}, f32[384,64]{1,0:T(8,128)}) custom-call(bf16[256,2048]{1,0:T(8,128)(2,1)} %bitcast.39, bf16[128,2048]{1,0:T(8,128)(2,1)} %bitcast.41, bf16[256,2048]{1,0:T(8,128)(2,1)} %bitcast.29, bf16[128,2048]{1,0:T(8,128)(2,1)} %bitcast.37, bf16[64,2048]{1,0:T(8,128)(2,1)} %proj_input.1, bf16[64,2048]{1,0:T(8,128)(2,1)} %proj_outgrad.1, ...), custom_call_target="tpu_custom_call" | custom-call | flops 176160768 | bytes 9633792 | tf_op jit(solution)/shard_map/pallas_call | solution.py:334
  34.3 4.4 %collective-permute-done.8.refs_4_ = bf16[128,2048]{1,0:T(8,128)(2,1)S(1)} collective-permute-done((bf16[128,2048]{1,0:T(8,128)(2,1)S(1)}, bf16[128,2048]{1,0:T(8,128)(2,1)S(1)}, u32[]{:S(2)}, u32[]{:S(2)}) %collective-permute-start.8) | collective-permute-done | bytes 524320 | tf_op jit(solution)/shard_map/ppermute | solution.py:506
  38.8 2.6 %collective-permute-start.9 = (bf16[128,2048]{1,0:T(8,128)(2,1)S(1)}, bf16[128,2048]{1,0:T(8,128)(2,1)}, u32[]{:S(2)}, u32[]{:S(2)}) collective-permute-start(bf16[128,2048]{1,0:T(8,128)(2,1)S(1)} %collective-permute-done.6.refs_6_), channel_id=1, source_target_pairs={{0,4},{4,0},{8,12},{12,8},{1,5},{5,1},{9,13},{13,9},{2,6},{6,2},{1... | collective-permute-start | bytes 1572872 | tf_op jit(solution)/shard_map/ppermute | solution.py:518
  41.6 10.7 %collective-permute-done.9.refs_8_ = bf16[128,2048]{1,0:T(8,128)(2,1)} collective-permute-done((bf16[128,2048]{1,0:T(8,128)(2,1)S(1)}, bf16[128,2048]{1,0:T(8,128)(2,1)}, u32[]{:S(2)}, u32[]{:S(2)}) %collective-permute-start.9) | collective-permute-done | bytes 524320 | tf_op jit(solution)/shard_map/ppermute | solution.py:518
  52.3 2.1 select_select_fusion.1
  54.9 1.0 slice.63
  55.9 2.0 collective-permute-start.18
  57.9 2.3 collective-permute-done
  60.2 2.0 collective-permute-start.1
  62.2 8.6 %collective-permute-done.1 = f32[384,128]{1,0:T(8,128)S(1)} collective-permute-done((f32[384,128]{1,0:T(8,128)S(1)}, f32[384,128]{1,0:T(8,128)S(1)}, u32[]{:S(2)}, u32[]{:S(2)}) %collective-permute-start.1) | collective-permute-done | bytes 196640 | tf_op jit(solution)/shard_map/ppermute | solution.py:483
  72.2 1.3 slice.61
  74.3 1.4 collective-permute-start.12
  75.7 10.7 %collective-permute-done.18.refs_15_ = bf16[128,3584]{1,0:T(8,128)(2,1)S(1)} collective-permute-done((bf16[128,3584]{1,0:T(8,128)(2,1)}, bf16[128,3584]{1,0:T(8,128)(2,1)S(1)}, u32[]{:S(2)}, u32[]{:S(2)}) %collective-permute-start.18) | collective-permute-done | bytes 917536 | tf_op jit(solution)/shard_map/ppermute | solution.py:516
  87.5 20.1 %shard_map.155 = (f32[3584,128]{1,0:T(8,128)}, bf16[3584,128]{1,0:T(8,128)(2,1)}) custom-call(s32[2]{0:T(128)} %pad_add_fusion.refs_0_, bf16[128,2048]{1,0:T(8,128)(2,1)} %bitcast.38, bf16[128,2048]{1,0:T(8,128)(2,1)} %copy-done.26, bf16[128,2048]{1,0:T(8,128)(2,1)} %collective-permute-done.2.refs_3_, bf16[128,2048]{1,0:T(8,128)(2,1)} %copy-done.27, ...), custom_call_target="tpu_custom_call" | custom-call | flops 7516192768 | bytes 29360128 | tf_op jit(solution)/shard_map/pallas_call | solution.py:232
  107.7 2.7 %collective-permute-start.16 = (bf16[128,2048]{1,0:T(8,128)(2,1)S(1)}, bf16[128,2048]{1,0:T(8,128)(2,1)S(1)}, u32[]{:S(2)}, u32[]{:S(2)}) collective-permute-start(bf16[128,2048]{1,0:T(8,128)(2,1)S(1)} %collective-permute-done.13.refs_6_), channel_id=1, source_target_pairs={{0,4},{4,0},{8,12},{12,8},{1,5},{5,1},{9,13},{13,9},{2,6},{6,2},{1... | collective-permute-start | bytes 1572872 | tf_op jit(solution)/shard_map/ppermute | solution.py:529
  110.3 2.1 collective-permute-start.22
  112.4 9.6 %collective-permute-done.16.refs_8_ = bf16[128,2048]{1,0:T(8,128)(2,1)S(1)} collective-permute-done((bf16[128,2048]{1,0:T(8,128)(2,1)S(1)}, bf16[128,2048]{1,0:T(8,128)(2,1)S(1)}, u32[]{:S(2)}, u32[]{:S(2)}) %collective-permute-start.16) | collective-permute-done | bytes 524320 | tf_op jit(solution)/shard_map/ppermute | solution.py:529
  122.5 2.7 %collective-permute-start.17 = (bf16[128,2048]{1,0:T(8,128)(2,1)S(1)}, bf16[128,2048]{1,0:T(8,128)(2,1)S(1)}, u32[]{:S(2)}, u32[]{:S(2)}) collective-permute-start(bf16[128,2048]{1,0:T(8,128)(2,1)S(1)} %get-tuple-element.38), channel_id=1, source_target_pairs={{0,2},{1,3},{2,0},{3,1},{4,6},{5,7},{6,4},{7,5},{8,10},{9,11},{10,... | collective-permute-start | bytes 1572872 | tf_op jit(solution)/shard_map/ppermute | solution.py:501
  125.1 8.8 %collective-permute-done.22.returned = bf16[3584,128]{1,0:T(8,128)(2,1)S(1)} collective-permute-done((bf16[3584,128]{1,0:T(8,128)(2,1)}, bf16[3584,128]{1,0:T(8,128)(2,1)S(1)}, u32[]{:S(2)}, u32[]{:S(2)}) %collective-permute-start.22) | collective-permute-done | bytes 917536 | tf_op jit(solution)/shard_map/ppermute | solution.py:528
  133.9 1.1 collective-permute-done.20.refs_10_.refs_2_
  135.0 7.8 %collective-permute-done.17.refs_9_.refs_3_ = bf16[128,2048]{1,0:T(8,128)(2,1)S(1)} collective-permute-done((bf16[128,2048]{1,0:T(8,128)(2,1)S(1)}, bf16[128,2048]{1,0:T(8,128)(2,1)S(1)}, u32[]{:S(2)}, u32[]{:S(2)}) %collective-permute-start.17) | collective-permute-done | bytes 524320 | tf_op jit(solution)/shard_map/ppermute | solution.py:501
  142.9 1.8 collective-permute-start.29
  144.7 20.3 %shard_map.156 = (f32[3584,128]{1,0:T(8,128)}, bf16[3584,128]{1,0:T(8,128)(2,1)}) custom-call(s32[2]{0:T(128)} %pad_add_fusion.refs_0_, bf16[128,2048]{1,0:T(8,128)(2,1)} %bitcast.28, bf16[128,2048]{1,0:T(8,128)(2,1)} %copy-done.7, bf16[128,2048]{1,0:T(8,128)(2,1)} %copy-done.1, bf16[128,2048]{1,0:T(8,128)(2,1)} %copy-done.30, ...), custom_call_target="tpu_custom_call" | custom-call | flops 7516192768 | bytes 29360128 | tf_op jit(solution)/shard_map/pallas_call | solution.py:232
  165.0 1.5 collective-permute-start.32
  167.3 6.6 %shard_map.158 = f32[128,128]{1,0:T(8,128)} custom-call(f32[3584,128]{1,0:T(8,128)} %get-tuple-element.30.near_sum, bf16[3584,128]{1,0:T(8,128)(2,1)} %copy-done.18, bf16[128,3584]{1,0:T(8,128)(2,1)} %bitcast.31, bf16[128,3584]{1,0:T(8,128)(2,1)} %bitcast.33, bf16[64,3584]{1,0:T(8,128)(2,1)} %refs_17_.1, bf16[64,3584]{1,0:T(8,128)(2,1)} %refs_18_.1), custom_call_target="tpu_custom_call" | custom-call | flops 117440512 | bytes 4587520 | tf_op jit(solution)/shard_map/pallas_call | solution.py:254
  175.4 2.5 collective-permute-start.21
  178.3 1.6 collective-permute-done.32.refs_8_
  179.9 2.5 collective-permute-start.33
  182.7 2.0 collective-permute-start.24
  185.4 8.6 %collective-permute-done.24 = f32[128,192]{1,0:T(8,128)S(1)} collective-permute-done((f32[128,192]{1,0:T(8,128)S(1)}, f32[128,192]{1,0:T(8,128)S(1)}, u32[]{:S(2)}, u32[]{:S(2)}) %collective-permute-start.24) | collective-permute-done | bytes 98336 | tf_op jit(solution)/shard_map/ppermute | solution.py:483
  194.6 2.0 shard_map.159.q0
  196.6 2.4 collective-permute-start.26
  199.1 1.6 collective-permute-start.27
  201.7 6.6 %shard_map.157.near = f32[128,128]{1,0:T(8,128)} custom-call(f32[3584,128]{1,0:T(8,128)} %get-tuple-element.28.near_sum, bf16[3584,128]{1,0:T(8,128)(2,1)} %copy-done.16, bf16[256,3584]{1,0:T(8,128)(2,1)} %bitcast.20, bf16[256,3584]{1,0:T(8,128)(2,1)} %bitcast.23, bf16[64,3584]{1,0:T(8,128)(2,1)} %refs_17_.1, bf16[64,3584]{1,0:T(8,128)(2,1)} %refs_18_.1), custom_call_target="tpu_custom_call" | custom-call | flops 117440512 | bytes 6422528 | tf_op jit(solution)/shard_map/pallas_call | solution.py:254
  208.3 2.1 collective-permute-done.33.refs_9_
  211.1 25.0 %shard_map.161 = f32[256,128]{1,0:T(8,128)} custom-call(s32[2]{0:T(128)} %pad_add_fusion.refs_0_, bf16[128,2048]{1,0:T(8,128)(2,1)} %bitcast.26, bf16[128,2048]{1,0:T(8,128)(2,1)} %copy-done.6, bf16[128,2048]{1,0:T(8,128)(2,1)} %copy-done.2, bf16[128,2048]{1,0:T(8,128)(2,1)} %copy-done.28, bf16[128,2048]{1,0:T(8,128)(2,1)} %copy-done.13, ...), custom_call_target="tpu_custom_call" | custom-call | flops 7516192768 | bytes 29360128 | tf_op jit(solution)/shard_map/pallas_call | solution.py:279
  236.1 1.5 fusion.5
  237.6 2.7 %collective-permute-start.35 = (f32[128,128]{1,0:T(8,128)S(1)}, f32[128,128]{1,0:T(8,128)S(1)}, u32[]{:S(2)}, u32[]{:S(2)}) collective-permute-start(f32[128,128]{1,0:T(8,128)S(1)} %get-tuple-element.47), channel_id=1, source_target_pairs={{0,2},{1,3},{2,0},{3,1},{4,6},{5,7},{6,4},{7,5},{8,10},{9,11},{10,... | collective-permute-start | bytes 196616 | tf_op jit(solution)/shard_map/ppermute | solution.py:562
  241.7 2.5 shard_map.160
  244.8 2.4 shard_map.162
  248.3 3.2 %collective-permute-done.36 = f32[4,8]{1,0:T(4,128)S(1)} collective-permute-done((f32[4,8]{1,0:T(4,128)S(1)}, f32[4,8]{1,0:T(4,128)S(1)}, u32[]{:S(2)}, u32[]{:S(2)}) %collective-permute-start.36) | collective-permute-done | bytes 160 | tf_op jit(solution)/shard_map/ppermute | solution.py:482
  252.2 1.6 collective-permute-start.37
  253.8 2.9 %collective-permute-done.37 = f32[4,8]{1,0:T(4,128)S(1)} collective-permute-done((f32[4,8]{1,0:T(4,128)S(1)}, f32[4,8]{1,0:T(4,128)S(1)}, u32[]{:S(2)}, u32[]{:S(2)}) %collective-permute-start.37) | collective-permute-done | bytes 160 | tf_op jit(solution)/shard_map/ppermute | solution.py:483
  (140 shorter events, 16.1 us)
Async XLA Ops:
  0.0 87.1 %collective-permute-start.14 = (bf16[3584,2048]{1,0:T(8,128)(2,1)}, bf16[3584,2048]{1,0:T(8,128)(2,1)}, u32[]{:S(2)}, u32[]{:S(2)}) collective-permute-start(bf16[3584,2048]{1,0:T(8,128)(2,1)} %refs_11_.5), channel_id=1, source_target_pairs={{0,1},{1,0},{2,3},{3,2},{4,5},{5,4},{6,7},{7,6},{8,9},{9,8},{10,11... | collective-permute-start | bytes 44040200 | tf_op jit(solution)/shard_map/ppermute | solution.py:508
  0.5 15.4 %collective-permute-start.2 = (bf16[128,2048]{1,0:T(8,128)(2,1)}, bf16[128,2048]{1,0:T(8,128)(2,1)}, u32[]{:S(2)}, u32[]{:S(2)}) collective-permute-start(bf16[128,2048]{1,0:T(8,128)(2,1)} %bitcast.34), channel_id=1, source_target_pairs={{0,2},{1,3},{2,0},{3,1},{4,6},{5,7},{6,4},{7,5},{8,10},{9,11},{10,... | collective-permute-start | bytes 1572872 | tf_op jit(solution)/shard_map/ppermute | solution.py:496
  2.9 20.3 %collective-permute-start.7 = (bf16[128,2048]{1,0:T(8,128)(2,1)}, bf16[128,2048]{1,0:T(8,128)(2,1)S(1)}, u32[]{:S(2)}, u32[]{:S(2)}) collective-permute-start(bf16[128,2048]{1,0:T(8,128)(2,1)} %bitcast.35), channel_id=1, source_target_pairs={{0,1},{1,0},{2,3},{3,2},{4,8},{5,9},{6,10},{7,11},{8,4},{9,5},{10,... | collective-permute-start | bytes 1572872 | tf_op jit(solution)/shard_map/ppermute | solution.py:496
  3.2 21.4 %collective-permute-start.5 = (bf16[128,2048]{1,0:T(8,128)(2,1)}, bf16[128,2048]{1,0:T(8,128)(2,1)S(1)}, u32[]{:S(2)}, u32[]{:S(2)}) collective-permute-start(bf16[128,2048]{1,0:T(8,128)(2,1)} %bitcast.36), channel_id=1, source_target_pairs={{0,4},{4,0},{8,12},{12,8},{1,5},{5,1},{9,13},{13,9},{2,6},{6,2},{1... | collective-permute-start | bytes 1572872 | tf_op jit(solution)/shard_map/ppermute | solution.py:496
  24.5 14.3 %collective-permute-start.8 = (bf16[128,2048]{1,0:T(8,128)(2,1)S(1)}, bf16[128,2048]{1,0:T(8,128)(2,1)S(1)}, u32[]{:S(2)}, u32[]{:S(2)}) collective-permute-start(bf16[128,2048]{1,0:T(8,128)(2,1)S(1)} %broadcast_select_fusion.4), channel_id=1, source_target_pairs={{0,4},{4,0},{8,12},{12,8},{1,5},{5,1},{9,13},{13,9},{2,6},{6,2},{1... | collective-permute-start | bytes 1572872 | tf_op jit(solution)/shard_map/ppermute | solution.py:506
  24.6 14.2 %collective-permute-start.6 = (bf16[128,2048]{1,0:T(8,128)(2,1)S(1)}, bf16[128,2048]{1,0:T(8,128)(2,1)S(1)}, u32[]{:S(2)}, u32[]{:S(2)}) collective-permute-start(bf16[128,2048]{1,0:T(8,128)(2,1)S(1)} %collective-permute-done.5.refs_2_), channel_id=1, source_target_pairs={{0,1},{1,0},{2,3},{3,2},{4,8},{5,9},{6,10},{7,11},{8,4},{9,5},{10,... | collective-permute-start | bytes 1572872 | tf_op jit(solution)/shard_map/ppermute | solution.py:506
  34.1 7.5 %collective-permute-start.3 = (bf16[128,2048]{1,0:T(8,128)(2,1)}, bf16[128,2048]{1,0:T(8,128)(2,1)}, u32[]{:S(2)}, u32[]{:S(2)}) collective-permute-start(bf16[128,2048]{1,0:T(8,128)(2,1)} %collective-permute-done.2.refs_3_), channel_id=1, source_target_pairs={{0,1},{1,0},{2,3},{3,2},{4,8},{5,9},{6,10},{7,11},{8,4},{9,5},{10,... | collective-permute-start | bytes 1572872 | tf_op jit(solution)/shard_map/ppermute | solution.py:518
  38.8 13.6 %collective-permute-start.9 = (bf16[128,2048]{1,0:T(8,128)(2,1)S(1)}, bf16[128,2048]{1,0:T(8,128)(2,1)}, u32[]{:S(2)}, u32[]{:S(2)}) collective-permute-start(bf16[128,2048]{1,0:T(8,128)(2,1)S(1)} %collective-permute-done.6.refs_6_), channel_id=1, source_target_pairs={{0,4},{4,0},{8,12},{12,8},{1,5},{5,1},{9,13},{13,9},{2,6},{6,2},{1... | collective-permute-start | bytes 1572872 | tf_op jit(solution)/shard_map/ppermute | solution.py:518
  41.5 81.0 %copy-start.3 = (bf16[2,64,2048]{2,1,0:T(8,128)(2,1)}, bf16[2,64,2048]{2,1,0:T(8,128)(2,1)S(1)}, u32[]{:S(2)}) copy-start(bf16[2,64,2048]{2,1,0:T(8,128)(2,1)S(1)} %get-tuple-element.35) | copy-start | bytes 1572868
  41.5 32.7 %collective-permute-start.11 = (bf16[128,2048]{1,0:T(8,128)(2,1)S(1)}, bf16[128,2048]{1,0:T(8,128)(2,1)}, u32[]{:S(2)}, u32[]{:S(2)}) collective-permute-start(bf16[128,2048]{1,0:T(8,128)(2,1)S(1)} %bitcast.27), channel_id=1, source_target_pairs={{0,1},{1,0},{2,3},{3,2},{4,8},{5,9},{6,10},{7,11},{8,4},{9,5},{10,... | collective-permute-start | bytes 1572872 | tf_op jit(solution)/shard_map/ppermute | solution.py:502
  54.5 19.8 %collective-permute-start.10 = (bf16[128,2048]{1,0:T(8,128)(2,1)}, bf16[128,2048]{1,0:T(8,128)(2,1)S(1)}, u32[]{:S(2)}, u32[]{:S(2)}) collective-permute-start(bf16[128,2048]{1,0:T(8,128)(2,1)} %get-tuple-element.39), channel_id=1, source_target_pairs={{0,2},{1,3},{2,0},{3,1},{4,6},{5,7},{6,4},{7,5},{8,10},{9,11},{10,... | collective-permute-start | bytes 1572872 | tf_op jit(solution)/shard_map/ppermute | solution.py:501
  54.5 5.7 %collective-permute-start = (f32[384,128]{1,0:T(8,128)S(1)}, f32[384,128]{1,0:T(8,128)S(1)}, u32[]{:S(2)}, u32[]{:S(2)}) collective-permute-start(f32[384,128]{1,0:T(8,128)S(1)} %copy-done.34), channel_id=1, source_target_pairs={{0,4},{4,0},{8,12},{12,8},{1,5},{5,1},{9,13},{13,9},{2,6},{6,2},{1... | collective-permute-start | bytes 589832 | tf_op jit(solution)/shard_map/ppermute | solution.py:482
  55.9 30.5 %collective-permute-start.18 = (bf16[128,3584]{1,0:T(8,128)(2,1)}, bf16[128,3584]{1,0:T(8,128)(2,1)S(1)}, u32[]{:S(2)}, u32[]{:S(2)}) collective-permute-start(bf16[128,3584]{1,0:T(8,128)(2,1)} %bitcast.14), channel_id=1, source_target_pairs={{0,2},{1,3},{2,0},{3,1},{4,6},{5,7},{6,4},{7,5},{8,10},{9,11},{10,... | collective-permute-start | bytes 2752520 | tf_op jit(solution)/shard_map/ppermute | solution.py:516
  60.2 10.6 %collective-permute-start.1 = (f32[384,128]{1,0:T(8,128)S(1)}, f32[384,128]{1,0:T(8,128)S(1)}, u32[]{:S(2)}, u32[]{:S(2)}) collective-permute-start(f32[384,128]{1,0:T(8,128)S(1)} %add.23), channel_id=1, source_target_pairs={{0,8},{4,12},{8,0},{12,4},{1,9},{5,13},{9,1},{13,5},{2,10},{6,14},... | collective-permute-start | bytes 589832 | tf_op jit(solution)/shard_map/ppermute | solution.py:483
  70.8 15.7 %collective-permute-start.4 = (bf16[128,2048]{1,0:T(8,128)(2,1)}, bf16[128,2048]{1,0:T(8,128)(2,1)S(1)}, u32[]{:S(2)}, u32[]{:S(2)}) collective-permute-start(bf16[128,2048]{1,0:T(8,128)(2,1)} %get-tuple-element.40), channel_id=1, source_target_pairs={{0,4},{4,0},{8,12},{12,8},{1,5},{5,1},{9,13},{13,9},{2,6},{6,2},{1... | collective-permute-start | bytes 1572872 | tf_op jit(solution)/shard_map/ppermute | solution.py:500
  74.3 33.3 %collective-permute-start.12 = (bf16[128,2048]{1,0:T(8,128)(2,1)S(1)}, bf16[128,2048]{1,0:T(8,128)(2,1)S(1)}, u32[]{:S(2)}, u32[]{:S(2)}) collective-permute-start(bf16[128,2048]{1,0:T(8,128)(2,1)S(1)} %broadcast_select_fusion.3), channel_id=1, source_target_pairs={{0,4},{4,0},{8,12},{12,8},{1,5},{5,1},{9,13},{13,9},{2,6},{6,2},{1... | collective-permute-start | bytes 1572872 | tf_op jit(solution)/shard_map/ppermute | solution.py:506
  86.4 23.9 %collective-permute-start.19 = (bf16[128,3584]{1,0:T(8,128)(2,1)S(1)}, bf16[128,3584]{1,0:T(8,128)(2,1)}, u32[]{:S(2)}, u32[]{:S(2)}) collective-permute-start(bf16[128,3584]{1,0:T(8,128)(2,1)S(1)} %bitcast.40), channel_id=1, source_target_pairs={{0,2},{1,3},{2,0},{3,1},{4,6},{5,7},{6,4},{7,5},{8,10},{9,11},{10,... | collective-permute-start | bytes 2752520 | tf_op jit(solution)/shard_map/ppermute | solution.py:526
  86.5 23.8 %collective-permute-start.15 = (bf16[128,2048]{1,0:T(8,128)(2,1)S(1)}, bf16[128,2048]{1,0:T(8,128)(2,1)S(1)}, u32[]{:S(2)}, u32[]{:S(2)}) collective-permute-start(bf16[128,2048]{1,0:T(8,128)(2,1)S(1)} %collective-permute-done.10.refs_9_.refs_3_), channel_id=1, source_target_pairs={{0,1},{1,0},{2,3},{3,2},{4,8},{5,9},{6,10},{7,11},{8,4},{9,5},{10,... | collective-permute-start | bytes 1572872 | tf_op jit(solution)/shard_map/ppermute | solution.py:529
  86.5 21.1 %collective-permute-start.13 = (bf16[128,2048]{1,0:T(8,128)(2,1)S(1)}, bf16[128,2048]{1,0:T(8,128)(2,1)S(1)}, u32[]{:S(2)}, u32[]{:S(2)}) collective-permute-start(bf16[128,2048]{1,0:T(8,128)(2,1)S(1)} %collective-permute-done.4.refs_10_.refs_2_), channel_id=1, source_target_pairs={{0,1},{1,0},{2,3},{3,2},{4,8},{5,9},{6,10},{7,11},{8,4},{9,5},{10,... | collective-permute-start | bytes 1572872 | tf_op jit(solution)/shard_map/ppermute | solution.py:506
  107.6 35.2 %copy-start.10 = (bf16[128,2048]{1,0:T(8,128)(2,1)}, bf16[128,2048]{1,0:T(8,128)(2,1)S(1)}, u32[]{:S(2)}) copy-start(bf16[128,2048]{1,0:T(8,128)(2,1)S(1)} %collective-permute-done.13.refs_6_) | copy-start | bytes 1572868
  107.7 14.3 %collective-permute-start.16 = (bf16[128,2048]{1,0:T(8,128)(2,1)S(1)}, bf16[128,2048]{1,0:T(8,128)(2,1)S(1)}, u32[]{:S(2)}, u32[]{:S(2)}) collective-permute-start(bf16[128,2048]{1,0:T(8,128)(2,1)S(1)} %collective-permute-done.13.refs_6_), channel_id=1, source_target_pairs={{0,4},{4,0},{8,12},{12,8},{1,5},{5,1},{9,13},{13,9},{2,6},{6,2},{1... | collective-permute-start | bytes 1572872 | tf_op jit(solution)/shard_map/ppermute | solution.py:529
  110.3 32.6 %copy-start.9 = (bf16[128,2048]{1,0:T(8,128)(2,1)}, bf16[128,2048]{1,0:T(8,128)(2,1)S(1)}, u32[]{:S(2)}) copy-start(bf16[128,2048]{1,0:T(8,128)(2,1)S(1)} %collective-permute-done.15.refs_7_) | copy-start | bytes 1572868
  110.3 23.6 %collective-permute-start.22 = (bf16[3584,128]{1,0:T(8,128)(2,1)}, bf16[3584,128]{1,0:T(8,128)(2,1)S(1)}, u32[]{:S(2)}, u32[]{:S(2)}) collective-permute-start(bf16[3584,128]{1,0:T(8,128)(2,1)} %get-tuple-element.23), channel_id=1, source_target_pairs={{0,2},{1,3},{2,0},{3,1},{4,6},{5,7},{6,4},{7,5},{8,10},{9,11},{10,... | collective-permute-start | bytes 2752520 | tf_op jit(solution)/shard_map/ppermute | solution.py:528
  122.1 12.9 %collective-permute-start.20 = (bf16[128,2048]{1,0:T(8,128)(2,1)S(1)}, bf16[128,2048]{1,0:T(8,128)(2,1)S(1)}, u32[]{:S(2)}, u32[]{:S(2)}) collective-permute-start(bf16[128,2048]{1,0:T(8,128)(2,1)S(1)} %get-tuple-element.37), channel_id=1, source_target_pairs={{0,4},{4,0},{8,12},{12,8},{1,5},{5,1},{9,13},{13,9},{2,6},{6,2},{1... | collective-permute-start | bytes 1572872 | tf_op jit(solution)/shard_map/ppermute | solution.py:500
  122.5 12.5 %collective-permute-start.28 = (bf16[128,2048]{1,0:T(8,128)(2,1)S(1)}, bf16[128,2048]{1,0:T(8,128)(2,1)S(1)}, u32[]{:S(2)}, u32[]{:S(2)}) collective-permute-start(bf16[128,2048]{1,0:T(8,128)(2,1)S(1)} %bitcast.25), channel_id=1, source_target_pairs={{0,1},{1,0},{2,3},{3,2},{4,8},{5,9},{6,10},{7,11},{8,4},{9,5},{10,... | collective-permute-start | bytes 1572872 | tf_op jit(solution)/shard_map/ppermute | solution.py:502
  122.5 20.3 %collective-permute-start.17 = (bf16[128,2048]{1,0:T(8,128)(2,1)S(1)}, bf16[128,2048]{1,0:T(8,128)(2,1)S(1)}, u32[]{:S(2)}, u32[]{:S(2)}) collective-permute-start(bf16[128,2048]{1,0:T(8,128)(2,1)S(1)} %get-tuple-element.38), channel_id=1, source_target_pairs={{0,2},{1,3},{2,0},{3,1},{4,6},{5,7},{6,4},{7,5},{8,10},{9,11},{10,... | collective-permute-start | bytes 1572872 | tf_op jit(solution)/shard_map/ppermute | solution.py:501
  133.9 31.1 %copy-start.18 = (bf16[3584,128]{1,0:T(8,128)(2,1)}, bf16[3584,128]{1,0:T(8,128)(2,1)S(1)}, u32[]{:S(2)}) copy-start(bf16[3584,128]{1,0:T(8,128)(2,1)S(1)} %collective-permute-done.22.returned) | copy-start | bytes 2752516
  135.0 30.0 %collective-permute-start.30 = (bf16[128,2048]{1,0:T(8,128)(2,1)S(1)}, bf16[128,2048]{1,0:T(8,128)(2,1)S(1)}, u32[]{:S(2)}, u32[]{:S(2)}) collective-permute-start(bf16[128,2048]{1,0:T(8,128)(2,1)S(1)} %collective-permute-done.20.refs_10_.refs_2_), channel_id=1, source_target_pairs={{0,1},{1,0},{2,3},{3,2},{4,8},{5,9},{6,10},{7,11},{8,4},{9,5},{10,... | collective-permute-start | bytes 1572872 | tf_op jit(solution)/shard_map/ppermute | solution.py:506
  135.0 30.0 %copy-start.13 = (bf16[128,2048]{1,0:T(8,128)(2,1)}, bf16[128,2048]{1,0:T(8,128)(2,1)S(1)}, u32[]{:S(2)}) copy-start(bf16[128,2048]{1,0:T(8,128)(2,1)S(1)} %collective-permute-done.28.refs_5_) | copy-start | bytes 1572868
  142.9 22.1 %collective-permute-start.29 = (bf16[128,2048]{1,0:T(8,128)(2,1)S(1)}, bf16[128,2048]{1,0:T(8,128)(2,1)S(1)}, u32[]{:S(2)}, u32[]{:S(2)}) collective-permute-start(bf16[128,2048]{1,0:T(8,128)(2,1)S(1)} %broadcast_select_fusion.1), channel_id=1, source_target_pairs={{0,4},{4,0},{8,12},{12,8},{1,5},{5,1},{9,13},{13,9},{2,6},{6,2},{1... | collective-permute-start | bytes 1572872 | tf_op jit(solution)/shard_map/ppermute | solution.py:506
  144.7 21.9 %copy-start.33 = (f32[384,64]{1,0:T(8,128)S(1)}, f32[384,64]{1,0:T(8,128)}, u32[]{:S(2)}) copy-start(f32[384,64]{1,0:T(8,128)} %get-tuple-element.21) | copy-start | bytes 294916
  144.7 33.2 %collective-permute-start.31 = (bf16[128,2048]{1,0:T(8,128)(2,1)S(1)}, bf16[128,2048]{1,0:T(8,128)(2,1)S(1)}, u32[]{:S(2)}, u32[]{:S(2)}) collective-permute-start(bf16[128,2048]{1,0:T(8,128)(2,1)S(1)} %collective-permute-done.17.refs_9_.refs_3_), channel_id=1, source_target_pairs={{0,1},{1,0},{2,3},{3,2},{4,8},{5,9},{6,10},{7,11},{8,4},{9,5},{10,... | collective-permute-start | bytes 1572872 | tf_op jit(solution)/shard_map/ppermute | solution.py:537
  165.0 14.8 %collective-permute-start.32 = (bf16[128,2048]{1,0:T(8,128)(2,1)S(1)}, bf16[128,2048]{1,0:T(8,128)(2,1)S(1)}, u32[]{:S(2)}, u32[]{:S(2)}) collective-permute-start(bf16[128,2048]{1,0:T(8,128)(2,1)S(1)} %collective-permute-done.30.refs_6_), channel_id=1, source_target_pairs={{0,4},{4,0},{8,12},{12,8},{1,5},{5,1},{9,13},{13,9},{2,6},{6,2},{1... | collective-permute-start | bytes 1572872 | tf_op jit(solution)/shard_map/ppermute | solution.py:537
  174.8 7.8 %collective-permute-start.23 = (f32[128,192]{1,0:T(8,128)S(1)}, f32[128,192]{1,0:T(8,128)S(1)}, u32[]{:S(2)}, u32[]{:S(2)}) collective-permute-start(f32[128,192]{1,0:T(8,128)S(1)} %pad_maximum_fusion), channel_id=1, source_target_pairs={{0,4},{4,0},{8,12},{12,8},{1,5},{5,1},{9,13},{13,9},{2,6},{6,2},{1... | collective-permute-start | bytes 294920 | tf_op jit(solution)/shard_map/ppermute | solution.py:482
  175.4 25.3 %collective-permute-start.21 = (bf16[3584,128]{1,0:T(8,128)(2,1)S(1)}, bf16[3584,128]{1,0:T(8,128)(2,1)S(1)}, u32[]{:S(2)}, u32[]{:S(2)}) collective-permute-start(bf16[3584,128]{1,0:T(8,128)(2,1)S(1)} %copy-done.39), channel_id=1, source_target_pairs={{0,2},{1,3},{2,0},{3,1},{4,6},{5,7},{6,4},{7,5},{8,10},{9,11},{10,... | collective-permute-start | bytes 2752520 | tf_op jit(solution)/shard_map/ppermute | solution.py:551
  177.9 30.3 %copy-start.29 = (bf16[128,2048]{1,0:T(8,128)(2,1)}, bf16[128,2048]{1,0:T(8,128)(2,1)S(1)}, u32[]{:S(2)}) copy-start(bf16[128,2048]{1,0:T(8,128)(2,1)S(1)} %collective-permute-done.31.refs_7_) | copy-start | bytes 1572868
  177.9 30.3 %collective-permute-start.34 = (bf16[128,2048]{1,0:T(8,128)(2,1)S(1)}, bf16[128,2048]{1,0:T(8,128)(2,1)S(1)}, u32[]{:S(2)}, u32[]{:S(2)}) collective-permute-start(bf16[128,2048]{1,0:T(8,128)(2,1)S(1)} %collective-permute-done.31.refs_7_), channel_id=1, source_target_pairs={{0,4},{4,0},{8,12},{12,8},{1,5},{5,1},{9,13},{13,9},{2,6},{6,2},{1... | collective-permute-start | bytes 1572872 | tf_op jit(solution)/shard_map/ppermute | solution.py:540
  179.9 28.3 %copy-start.15 = (bf16[128,2048]{1,0:T(8,128)(2,1)}, bf16[128,2048]{1,0:T(8,128)(2,1)S(1)}, u32[]{:S(2)}) copy-start(bf16[128,2048]{1,0:T(8,128)(2,1)S(1)} %collective-permute-done.32.refs_8_) | copy-start | bytes 1572868
  179.9 30.4 %collective-permute-start.33 = (bf16[128,2048]{1,0:T(8,128)(2,1)S(1)}, bf16[128,2048]{1,0:T(8,128)(2,1)S(1)}, u32[]{:S(2)}, u32[]{:S(2)}) collective-permute-start(bf16[128,2048]{1,0:T(8,128)(2,1)S(1)} %broadcast_select_fusion), channel_id=1, source_target_pairs={{0,2},{1,3},{2,0},{3,1},{4,6},{5,7},{6,4},{7,5},{8,10},{9,11},{10,... | collective-permute-start | bytes 1572872 | tf_op jit(solution)/shard_map/ppermute | solution.py:540
  182.7 11.3 %collective-permute-start.24 = (f32[128,192]{1,0:T(8,128)S(1)}, f32[128,192]{1,0:T(8,128)S(1)}, u32[]{:S(2)}, u32[]{:S(2)}) collective-permute-start(f32[128,192]{1,0:T(8,128)S(1)} %fusion.1), channel_id=1, source_target_pairs={{0,8},{4,12},{8,0},{12,4},{1,9},{5,13},{9,1},{13,5},{2,10},{6,14},... | collective-permute-start | bytes 294920 | tf_op jit(solution)/shard_map/ppermute | solution.py:483
  196.6 2.4 collective-permute-start.25
  196.6 44.3 %collective-permute-start.26 = (f32[2,192,64]{2,1,0:T(8,128)}, f32[2,192,64]{2,1,0:T(8,128)S(1)}, u32[]{:S(2)}, u32[]{:S(2)}) collective-permute-start(f32[2,192,64]{2,1,0:T(8,128)} %shard_map.159.q0), channel_id=1, source_target_pairs={{0,2},{1,3},{2,0},{3,1},{4,6},{5,7},{6,4},{7,5},{8,10},{9,11},{10,... | collective-permute-start | bytes 294920 | tf_op jit(solution)/shard_map/ppermute | solution.py:549
  199.1 37.0 %copy-start.19 = (f32[2,192,64]{2,1,0:T(8,128)}, f32[2,192,64]{2,1,0:T(8,128)S(1)}, u32[]{:S(2)}) copy-start(f32[2,192,64]{2,1,0:T(8,128)S(1)} %collective-permute-done.25.q1) | copy-start | bytes 294916
  199.1 41.8 %collective-permute-start.27 = (f32[2,192,64]{2,1,0:T(8,128)S(1)}, f32[2,192,64]{2,1,0:T(8,128)S(1)}, u32[]{:S(2)}, u32[]{:S(2)}) collective-permute-start(f32[2,192,64]{2,1,0:T(8,128)S(1)} %collective-permute-done.25.q1), channel_id=1, source_target_pairs={{0,2},{1,3},{2,0},{3,1},{4,6},{5,7},{6,4},{7,5},{8,10},{9,11},{10,... | collective-permute-start | bytes 294920 | tf_op jit(solution)/shard_map/ppermute | solution.py:549
  208.2 32.1 %copy-start.38 = (s32[4]{0:T(128)S(1)}, s32[4]{0:T(128)}, u32[]{:S(2)}) copy-start(s32[4]{0:T(128)} %param.20) | copy-start | bytes 52
  237.6 6.5 %collective-permute-start.35 = (f32[128,128]{1,0:T(8,128)S(1)}, f32[128,128]{1,0:T(8,128)S(1)}, u32[]{:S(2)}, u32[]{:S(2)}) collective-permute-start(f32[128,128]{1,0:T(8,128)S(1)} %get-tuple-element.47), channel_id=1, source_target_pairs={{0,2},{1,3},{2,0},{3,1},{4,6},{5,7},{6,4},{7,5},{8,10},{9,11},{10,... | collective-permute-start | bytes 196616 | tf_op jit(solution)/shard_map/ppermute | solution.py:562
  247.9 3.6 %collective-permute-start.36 = (f32[4,8]{1,0:T(4,128)S(1)}, f32[4,8]{1,0:T(4,128)S(1)}, u32[]{:S(2)}, u32[]{:S(2)}) collective-permute-start(f32[4,8]{1,0:T(4,128)S(1)} %pad_maximum_fusion.1), channel_id=1, source_target_pairs={{0,4},{4,0},{8,12},{12,8},{1,5},{5,1},{9,13},{13,9},{2,6},{6,2},{1... | collective-permute-start | bytes 392 | tf_op jit(solution)/shard_map/ppermute | solution.py:482
  252.2 4.5 %collective-permute-start.37 = (f32[4,8]{1,0:T(4,128)S(1)}, f32[4,8]{1,0:T(4,128)S(1)}, u32[]{:S(2)}, u32[]{:S(2)}) collective-permute-start(f32[4,8]{1,0:T(4,128)S(1)} %fusion), channel_id=1, source_target_pairs={{0,8},{4,12},{8,0},{12,4},{1,9},{5,13},{9,1},{13,5},{2,10},{6,14},... | collective-permute-start | bytes 392 | tf_op jit(solution)/shard_map/ppermute | solution.py:483
  (30 other events, 249.6 us)

commit v5 on v3

--- a/solution.py
+++ b/solution.py
@@ -143,11 +143,28 @@
     return pl.BlockSpec(shape, lambda i: tuple(0 for _ in shape))
 
 
-def stacked_products(flags, pairs, far, weight_own, weight_sib, stacked, semaphores):
+def stacked_products(
+    flags, pairs, far, weight_own, weight_sib, stacked, semaphores, held, weight_sems
+):
     number = far.shape[1]
-
-    @pl.when(pl.program_id(0) == 0)
+    step = pl.program_id(0)
+    tiles = weight_own.shape[0] // TILE
+
+    def weight_copies(tile):
+        part = pl.ds(pl.multiple_of(tile * TILE, TILE), TILE)
+        slot = lax.rem(tile, 3)
+        return [
+            pltpu.make_async_copy(
+                weight.at[part], held.at[slot, side], weight_sems.at[slot, side]
+            )
+            for side, weight in enumerate((weight_own, weight_sib))
+        ]
+
+    @pl.when(step == 0)
     def _():
+        for tile in range(2):
+            for copy in weight_copies(tile):
+                copy.start()
         slot = flags[1]
         far_copies = [
             pltpu.make_async_copy(
@@ -177,7 +194,15 @@
         for copy in far_copies:
             copy.wait()
 
-    return project(weight_own[...], stacked[0]) + project(weight_sib[...], stacked[1])
+    @pl.when(step + 2 < tiles)
+    def _():
+        for copy in weight_copies(step + 2):
+            copy.start()
+
+    for copy in weight_copies(step):
+        copy.wait()
+    slot = lax.rem(step, 3)
+    return project(held[slot, 0], stacked[0]) + project(held[slot, 1], stacked[1])
 
 
 def add_sides(hidden_grad, gate, up, proj_gate, proj_up, sides):
@@ -195,10 +220,10 @@
 
 
 def partial_kernel(
-    flags, b0, b1, b2, b3, b4, b5, far, weight_own, weight_sib, near_sum, far_sum, stacked, sems
+    flags, b0, b1, b2, b3, b4, b5, far, weight_own, weight_sib, near_sum, far_sum, *scratch
 ):
     pairs = ((b0, b1), (b2, b3), (b4, b5))
-    total = stacked_products(flags, pairs, far, weight_own, weight_sib, stacked, sems)
+    total = stacked_products(flags, pairs, far, weight_own, weight_sib, *scratch)
     number = far.shape[1]
     near_sum[...] = total[:, :number]
     far_sum[...] = total[:, number:].astype(jnp.bfloat16)
@@ -210,7 +235,7 @@
     return pl.pallas_call(
         partial_kernel,
         grid=(units // TILE,),
-        in_specs=[SCALARS] + [ANYWHERE] * 7 + [tile_rows(half)] * 2,
+        in_specs=[SCALARS] + [ANYWHERE] * 9,
         out_specs=[tile_rows(number)] * 2,
         out_shape=[
             jax.ShapeDtypeStruct((units, number), jnp.float32),
@@ -219,6 +244,8 @@
         scratch_shapes=[
             pltpu.VMEM((2, 2 * number, half), jnp.bfloat16),
             pltpu.SemaphoreType.DMA((4,)),
+            pltpu.VMEM((3, 2, TILE, half), jnp.bfloat16),
+            pltpu.SemaphoreType.DMA((3, 2)),
         ],
         compiler_params=params(),
         cost_estimate=cost(8 * number * half * units, (far, weight_own, weight_sib)),
@@ -245,10 +272,10 @@
 
 def lent_kernel(
     flags, b0, b1, b2, b3, b4, b5, far, weight_own, weight_sib, gate, up, far_gate, far_up,
-    proj_gate, proj_up, sides, stacked, sems,
+    proj_gate, proj_up, sides, *scratch,
 ):
     pairs = ((b0, b1), (b2, b3), (b4, b5))
-    total = stacked_products(flags, pairs, far, weight_own, weight_sib, stacked, sems)
+    total = stacked_products(flags, pairs, far, weight_own, weight_sib, *scratch)
     gates = jnp.concatenate([gate[...], far_gate[...]], axis=0)
     ups = jnp.concatenate([up[...], far_up[...]], axis=0)
     add_sides(total.T, gates, ups, proj_gate[...], proj_up[...], sides)
@@ -263,8 +290,7 @@
         lent_kernel,
         grid=(units // TILE,),
         in_specs=[SCALARS]
-        + [ANYWHERE] * 7
-        + [tile_rows(half)] * 2
+        + [ANYWHERE] * 9
         + [tile_columns(number, 1)] * 2
         + [tile_columns(number)] * 2
         + [tile_columns(RANK)] * 2,
@@ -273,6 +299,8 @@
         scratch_shapes=[
             pltpu.VMEM((2, 2 * number, half), jnp.bfloat16),
             pltpu.SemaphoreType.DMA((4,)),
+            pltpu.VMEM((3, 2, TILE, half), jnp.bfloat16),
+            pltpu.SemaphoreType.DMA((3, 2)),
         ],
         compiler_params=params(),
         cost_estimate=cost(8 * number * half * units, (far, weight_own, weight_sib)),
@@ -283,50 +311,51 @@
 
 def early_kernel(
     t_input, q_input, t_outgrad, q_outgrad, proj_input, proj_outgrad, t_gate, t_up, q_gate, q_up,
-    proj_hidden, sides,
+    proj_hidden, in_out, hidden,
 ):
     number = t_input.shape[0]
-    middle = pl.ds(RANK, RANK)
     t_hidden = project(gated_hidden(t_gate[...], t_up[...]), proj_hidden[...])
     q_hidden = project(gated_hidden(q_gate[...], q_up[...]), proj_hidden[...])
     first = pl.program_id(0) == 0
 
     @pl.when(first)
     def _():
-        for inputs, outgrad, hidden, part in (
-            (t_input, t_outgrad, t_hidden, slice(0, number)),
-            (q_input, q_outgrad, q_hidden, slice(number, None)),
+        for inputs, outgrad, part in (
+            (t_input, t_outgrad, slice(0, number)),
+            (q_input, q_outgrad, slice(number, None)),
         ):
-            sides[part, :] = jnp.concatenate(
+            in_out[part, :] = jnp.concatenate(
                 [
                     project(inputs[...], proj_input[...]),
-                    hidden,
                     project(outgrad[...], proj_outgrad[...]),
                 ],
                 axis=1,
             )
+        hidden[:number, :] = t_hidden
+        hidden[number:, :] = q_hidden
 
     @pl.when(jnp.logical_not(first))
     def _():
-        sides[:number, middle] += t_hidden
-        sides[number:, middle] += q_hidden
+        hidden[:number, :] += t_hidden
+        hidden[number:, :] += q_hidden
 
 
 def early_sides(
     t_input, q_input, t_outgrad, q_outgrad, proj_input, proj_outgrad, t_gate, t_up, q_gate, q_up,
     proj_hidden,
 ):
-    train, query, units = t_gate.shape[0], q_gate.shape[0], t_gate.shape[1]
+    total, units = t_gate.shape[0] + q_gate.shape[0], t_gate.shape[1]
     wide = (t_input, q_input, t_outgrad, q_outgrad, proj_input, proj_outgrad)
     tiled = (t_gate, t_up, q_gate, q_up, proj_hidden)
+    shapes = ((total, 2 * RANK), (total, RANK))
     return pl.pallas_call(
         early_kernel,
         grid=(units // TILE,),
         in_specs=[whole(a.shape) for a in wide] + [tile_columns(a.shape[0]) for a in tiled],
-        out_specs=whole((train + query, 3 * RANK)),
-        out_shape=jax.ShapeDtypeStruct((train + query, 3 * RANK), jnp.float32),
+        out_specs=[whole(shape) for shape in shapes],
+        out_shape=[jax.ShapeDtypeStruct(shape, jnp.float32) for shape in shapes],
         compiler_params=params(),
-        cost_estimate=cost(2 * (train + query) * RANK * units, wide + tiled),
+        cost_estimate=cost(2 * total * RANK * units, wide + tiled),
     )(*wide, *tiled)
 
 
@@ -350,33 +379,33 @@
     )
 
 
-def query_kernel(lengths, sides, gradient, found):
+def query_kernel(lengths, in_out, sums, found):
     for e in range(found.shape[0]):
         part = slice(e * SEQ, (e + 1) * SEQ)
         three = example_features(
-            sides[part, :RANK],
-            sides[part, RANK : 2 * RANK],
-            gradient[part, :RANK],
-            gradient[part, RANK:],
-            sides[part, 2 * RANK :],
+            in_out[part, :RANK],
+            sums[part, 2 * RANK :],
+            sums[part, :RANK],
+            sums[part, RANK : 2 * RANK],
+            in_out[part, RANK:],
             lengths[e],
         )
         for segment in range(3):
             found[e, segment * RANK : (segment + 1) * RANK, :] = three[segment]
 
 
-def query_features(lengths, sides, gradient):
+def query_features(lengths, in_out, sums):
     return pl.pallas_call(
         query_kernel,
         in_specs=[SCALARS, IN_VMEM, IN_VMEM],
         out_specs=IN_VMEM,
         out_shape=jax.ShapeDtypeStruct((lengths.shape[0], 3 * RANK, RANK), jnp.float32),
         compiler_params=params(),
-    )(lengths, sides, gradient)
+    )(lengths, in_out, sums)
 
 
 def score_kernel(
-    lengths, place, whole_sides, own_sides, near, far, q0, q1, q2, q3, scores
+    lengths, place, in_out, hidden, near, far, q0, q1, q2, q3, scores
 ):
     queries = q0.shape[0]
     shape = scores.shape
@@ -388,11 +417,11 @@
         gradient = near[part, :] + far[part, :]
         three = jnp.concatenate(
             example_features(
-                whole_sides[part, :RANK],
-                own_sides[part, RANK : 2 * RANK],
+                in_out[part, :RANK],
+                hidden[part, :],
                 gradient[:, :RANK],
                 gradient[:, RANK:],
-                whole_sides[part, 2 * RANK :],
+                in_out[part, RANK:],
                 lengths[e],
             ),
             axis=0,
@@ -407,7 +436,7 @@
     scores[...] = total
 
 
-def partial_scores(lengths, place, whole_sides, own_sides, near, far, found):
+def partial_scores(lengths, place, in_out, hidden, near, far, found):
     number = lengths.shape[0]
     return pl.pallas_call(
         score_kernel,
@@ -415,7 +444,7 @@
         out_specs=IN_VMEM,
         out_shape=jax.ShapeDtypeStruct((number, 4 * found[0].shape[0]), jnp.float32),
         compiler_params=params(),
-    )(lengths, place, whole_sides, own_sides, near, far, *found)
+    )(lengths, place, in_out, hidden, near, far, *found)
 
 
 def after(value, *others):
@@ -472,15 +501,6 @@
         values = values + outer(values)
         return values + across(values)
 
-    def crossing_pair(piece, first, second_inner, third_inner, second_outer, third_outer):
-        def choose(within, beyond_inner, beyond_outer):
-            beyond = jnp.where(inner_chip, beyond_inner, beyond_outer)
-            return jnp.where(at_home, beyond, within)
-
-        return jnp.stack(
-            [choose(piece, second_inner, second_outer), choose(first, third_inner, third_outer)]
-        )
-
     q_input, q_gate, q_up, q_outgrad = [
         flatten(a) for a in (query_input, query_gate, query_up, query_outgrad)
     ]
@@ -490,67 +510,74 @@
     examples = train_lengths.shape[0] // 2
     cut = examples * SEQ
 
+    def direct(own, *others):
+        return own, outer(after(own, *others)), middle(own), across(own)
+
+    def last_hop(own, one, mid, two, *others):
+        two = after(two, one, mid, *others)
+        return own, one, mid, two, two, outer(two)
+
+    def crossing_pair(own, one, second_inner, third_inner, second_outer, third_outer):
+        def choose(within, beyond_inner, beyond_outer):
+            beyond = jnp.where(inner_chip, beyond_inner, beyond_outer)
+            return jnp.where(at_home, beyond, within)
+
+        return jnp.stack(
+            [choose(own, second_inner, second_outer), choose(one, third_inner, third_outer)]
+        )
+
+    q_direct = direct(q_outgrad)
+    far_gate = to_chip(t_gate[cut:])
+    own_in_out, hidden = early_sides(
+        t_input, after(q_input, *q_direct[1:]), t_outgrad, q_outgrad, proj_input, proj_outgrad, t_gate, t_up, q_gate,
+        q_up, proj_hidden,
+    )
     weight_own, weight_sib = down_weight, to_core(down_weight)
-
-    q_one, q_mid = outer(q_outgrad), middle(q_outgrad)
-    lent = to_chip(jnp.stack([t_gate[cut:], t_up[cut:]]))
-    own_sides = early_sides(
-        t_input, q_input, t_outgrad, q_outgrad, proj_input, proj_outgrad, t_gate, t_up, q_gate,
-        q_up, proj_hidden,
-    )
-    q_two, q_last = outer(q_mid), middle(q_one)
-    whole_sides = lax.psum(own_sides, "tensor")
-    q_three = outer(after(q_last, own_sides))
-    q_blocks = (q_outgrad, q_one, q_mid, q_last, q_two, q_three)
-
-    a_rows = after(t_outgrad[:cut], q_two)
-    a_one, a_mid = outer(a_rows), middle(a_rows)
-    q_send = crossing_pair(*q_blocks)
+    q_blocks = last_hop(*q_direct, far_gate)
+
+    far_up = to_chip(after(t_up[cut:], far_gate))
+    q_send = after(crossing_pair(*q_blocks), far_up, own_in_out)
+    a_direct = direct(after(t_outgrad[:cut], q_direct[3]), q_send)
+    pair_in_out = own_in_out + outer(own_in_out)
+    pair_in_out = after(pair_in_out, a_direct[2], a_direct[3])
+    in_out = pair_in_out + across(pair_in_out)
     q_far = to_chip(q_send)
-    a_one, a_mid = lax.optimization_barrier((a_one, a_mid, q_send, lent))[:2]
-    a_two, a_last = outer(a_mid), middle(a_one)
-    a_three = outer(a_last)
-    a_blocks = (a_rows, a_one, a_mid, a_last, a_two, a_three)
-
-    b_rows = after(t_outgrad[cut:], a_two, q_far)
-    b_one, b_mid = outer(b_rows), middle(b_rows)
+    a_blocks = last_hop(*a_direct, in_out, q_far)
+
+    b_direct = direct(after(t_outgrad[cut:], a_blocks[3]))
     a_send = crossing_pair(*a_blocks)
     a_far = to_chip(a_send)
     q_near_sum, q_far_sum = partial_sums(
         flags, q_blocks, after(q_far, a_send), weight_own, weight_sib
     )
-    b_one, b_mid = lax.optimization_barrier((b_one, b_mid, q_far_sum))[:2]
-    b_two, b_last = outer(b_mid), middle(b_one)
-    b_three = outer(b_last)
-    b_blocks = (b_rows, b_one, b_mid, b_last, b_two, b_three)
-
-    q_gradient = finished_sides(
-        q_near_sum, after(to_chip(q_far_sum), a_far), q_gate, q_up, proj_gate, proj_up
-    )
+    q_returned = to_chip(after(q_far_sum, a_far))
+    b_blocks = last_hop(*b_direct, q_far_sum)
+    a_near_sum, a_far_sum = partial_sums(flags, a_blocks, a_far, weight_own, weight_sib)
+    a_returned = to_chip(a_far_sum)
+    b_blocks = b_blocks[:5] + (after(b_blocks[5], a_far_sum),)
     b_send = crossing_pair(*b_blocks)
     b_far = to_chip(b_send)
-    a_near_sum, a_far_sum = partial_sums(
-        flags, a_blocks, after(a_far, q_gradient, b_send), weight_own, weight_sib
+    q_gradient = finished_sides(
+        q_near_sum, after(q_returned, b_send), q_gate, q_up, proj_gate, proj_up
     )
     own_found = query_features(
-        query_lengths, whole_sides[2 * cut :], tensor_sum(q_gradient)
+        query_lengths,
+        in_out[2 * cut :],
+        tensor_sum(jnp.concatenate([q_gradient, hidden[2 * cut :]], axis=1)),
     )
     core_found = to_core(own_found)
     found = (own_found, core_found, to_chip(own_found), to_chip(core_found))
-
     b_gradient = lent_sides(
-        flags, b_blocks, after(b_far, own_found), weight_own, weight_sib, t_gate, t_up, lent[0],
-        lent[1], proj_gate, proj_up,
-    )
-    a_gradient = finished_sides(
-        a_near_sum, to_chip(a_far_sum), t_gate, t_up, proj_gate, proj_up
-    )
+        flags, b_blocks, after(b_far, core_found), weight_own, weight_sib, t_gate, t_up, far_gate,
+        far_up, proj_gate, proj_up,
+    )
+    a_gradient = finished_sides(a_near_sum, a_returned, t_gate, t_up, proj_gate, proj_up)
     a_scores = partial_scores(
-        train_lengths[:examples], place, whole_sides[:cut], own_sides[:cut], a_gradient,
+        train_lengths[:examples], place, in_out[:cut], hidden[:cut], a_gradient,
         jnp.zeros_like(a_gradient), found,
     )
     b_scores = partial_scores(
-        train_lengths[examples:], place, whole_sides[cut : 2 * cut], own_sides[cut : 2 * cut],
+        train_lengths[examples:], place, in_out[cut : 2 * cut], hidden[cut : 2 * cut],
         b_gradient[:cut], to_chip(b_gradient[cut:]), found,
     )
     scores = tensor_sum(jnp.concatenate([a_scores, b_scores], axis=0))

time: 255 us -> 247 us (0.969)
  waiting for transfers between devices: 87.2 us -> 135 us
  starting transfers between devices: 56.1 us -> 29.2 us
  between operations: 13.8 us -> 0.42 us
  Pallas kernels: 67.7 us -> 55.4 us
  other arithmetic: 10 us -> 4.3 us
    ppermute x18, waiting for transfers between devices: 41 us -> 106 us  [the longest x9 61.3 us: direct(): return (own, outer(after(own, *others)), middle(own), across(own))]
    psum x1 -> x0, waiting for transfers between devices: 30.7 us -> none  [moving_plan(): whole_sides = lax.psum(own_sides, 'tensor')]
    ppermute x18, starting transfers between devices: 39.5 us -> 17 us  [the longest x9 11.6 us: direct(): return (own, outer(after(own, *others)), middle(own), across(own))]
    pallas_call x2, Pallas kernels: 33.1 us -> 25.5 us  [partial_sums(): pl.pallas_call(partial_kernel, grid=(units // TILE,), in_specs=[SCALARS]...]
    another operation x10 -> x6, other arithmetic: 9.35 us -> 2.84 us  [crossing_pair(): jnp.stack([choose(own, second_inner, second_outer), choose(one, third_inn...]
    ppermute x1, waiting for transfers between devices: 6.38 us -> 0.01 us  [moving_plan(): q_far = to_chip(q_send)]
    ppermute x1, waiting for transfers between devices: 0.99 us -> 6.66 us  [moving_plan(): b_far = to_chip(b_send)]
    ppermute x1, waiting for transfers between devices: 0.01 us -> 5.48 us  [moving_plan(): a_far = to_chip(a_send)]
  transfers between devices with their start and end apart: 31 -> 30, of which waited for: 12 -> 18; matrix products, arithmetic and copies ran while one was open for 6% -> 3% of each run, Pallas kernels for 26% -> 22%
where the time goes in v5:
time: 247 us; the launch traced here: 246 us
  waiting for transfers between devices  135 us (55%)
  Pallas kernels  55.4 us (22%)
  starting transfers between devices  29.2 us (12%)
  local copies, waits for them, and re-layouts  21.7 us (9%)
  other arithmetic  4.3 us (2%)
    ppermute x9, waiting for transfers between devices, direct(): return (own, outer(after(own, *others)), middle(own), across(own))  61.3 us
    pallas_call x2, Pallas kernels, partial_sums(): pl.pallas_call(partial_kernel, grid=(units // TILE,), in_specs=[SCALARS]...  25.5 us
    pallas_call x1, Pallas kernels, lent_sides(): pl.pallas_call(lent_kernel, grid=(units // TILE,), in_specs=[SCALARS] + [...  17.2 us
    unnamed x78, local copies, waits for them, and re-layouts  17.1 us
    ppermute x1, waiting for transfers between devices, moving_plan(): pair_in_out = own_in_out + outer(own_in_out)  13.8 us
    ppermute x3, waiting for transfers between devices, last_hop(): return (own, one, mid, two, two, outer(two))  13.5 us
    ppermute x9, starting transfers between devices, direct(): return (own, outer(after(own, *others)), middle(own), across(own))  11.6 us
    ppermute x1, waiting for transfers between devices, moving_plan(): in_out = pair_in_out + across(pair_in_out)  9.46 us
  transfers between devices with their start and end apart: 30, of which 18 were waited for; matrix products, arithmetic and copies ran while one was open for 3% of the time, Pallas kernels for 22%

profile of v5, /device:TPU:0, one launch (start us, length us, event | category | flops | bytes accessed | tf_op | source)
XLA Modules:
  0.0 245.8 jit_solution(5592143769901838548)
XLA Ops:
  0.5 1.5 slice.59
  1.9 2.5 %collective-permute-start.7 = (bf16[128,3584]{1,0:T(8,128)(2,1)S(1)}, bf16[128,3584]{1,0:T(8,128)(2,1)S(1)}, u32[]{:S(2)}, u32[]{:S(2)}) collective-permute-start(bf16[128,3584]{1,0:T(8,128)(2,1)S(1)} %bitcast.56), channel_id=1, source_target_pairs={{0,2},{1,3},{2,0},{3,1},{4,6},{5,7},{6,4},{7,5},{8,10},{9,11},{10,... | collective-permute-start | bytes 2752520 | tf_op jit(solution)/shard_map/ppermute | solution.py:530
  4.4 1.6 collective-permute-start
  6.0 2.6 %collective-permute-start.2 = (bf16[128,2048]{1,0:T(8,128)(2,1)}, bf16[128,2048]{1,0:T(8,128)(2,1)S(1)}, u32[]{:S(2)}, u32[]{:S(2)}) collective-permute-start(bf16[128,2048]{1,0:T(8,128)(2,1)} %bitcast.36), channel_id=1, source_target_pairs={{0,8},{4,12},{8,0},{12,4},{1,9},{5,13},{9,1},{13,5},{2,10},{6,14},... | collective-permute-start | bytes 1572872 | tf_op jit(solution)/shard_map/ppermute | solution.py:514
  8.6 10.0 %collective-permute-done.b1 = bf16[128,2048]{1,0:T(8,128)(2,1)S(1)} collective-permute-done((bf16[128,2048]{1,0:T(8,128)(2,1)}, bf16[128,2048]{1,0:T(8,128)(2,1)S(1)}, u32[]{:S(2)}, u32[]{:S(2)}) %collective-permute-start) | collective-permute-done | bytes 524320 | tf_op jit(solution)/shard_map/ppermute | solution.py:514
  18.6 4.6 %collective-permute-done.1.b2 = bf16[128,2048]{1,0:T(8,128)(2,1)S(1)} collective-permute-done((bf16[128,2048]{1,0:T(8,128)(2,1)}, bf16[128,2048]{1,0:T(8,128)(2,1)S(1)}, u32[]{:S(2)}, u32[]{:S(2)}) %collective-permute-start.1) | collective-permute-done | bytes 524320 | tf_op jit(solution)/shard_map/ppermute | solution.py:514
  23.2 20.0 %collective-permute-done.2.b3.b4 = bf16[128,2048]{1,0:T(8,128)(2,1)S(1)} collective-permute-done((bf16[128,2048]{1,0:T(8,128)(2,1)}, bf16[128,2048]{1,0:T(8,128)(2,1)S(1)}, u32[]{:S(2)}, u32[]{:S(2)}) %collective-permute-start.2) | collective-permute-done | bytes 524320 | tf_op jit(solution)/shard_map/ppermute | solution.py:514
  44.1 2.2 slice.61
  46.9 1.5 copy-done.1
  48.4 1.2 copy-done.7
  49.6 1.2 copy-done.10
  50.8 1.2 copy-done.12
  51.9 1.2 copy-done.25
  57.1 3.8 %shard_map.154 = (f32[384,128]{1,0:T(8,128)S(1)}, f32[384,64]{1,0:T(8,128)S(1)}) custom-call(bf16[256,2048]{1,0:T(8,128)(2,1)S(1)} %bitcast.54, bf16[128,2048]{1,0:T(8,128)(2,1)S(1)} %bitcast.55, bf16[256,2048]{1,0:T(8,128)(2,1)S(1)} %bitcast.49, bf16[128,2048]{1,0:T(8,128)(2,1)S(1)} %bitcast.37, bf16[64,2048]{1,0:T(8,128)(2,1)S(1)} %copy-done.32, ...), custom_call_target="tpu_custom_call" | custom-call | flops 176160768 | bytes 9633792 | tf_op jit(solution)/shard_map/pallas_call | solution.py:351
  61.0 1.2 select_bitcast_fusion.5
  62.3 5.8 %collective-permute-done.9.far_up = bf16[128,3584]{1,0:T(8,128)(2,1)} collective-permute-done((bf16[128,3584]{1,0:T(8,128)(2,1)}, bf16[128,3584]{1,0:T(8,128)(2,1)}, u32[]{:S(2)}, u32[]{:S(2)}) %collective-permute-start.9) | collective-permute-done | bytes 917536 | tf_op jit(solution)/shard_map/ppermute | solution.py:538
  69.6 3.2 %collective-permute-start.5 = (bf16[128,2048]{1,0:T(8,128)(2,1)S(1)}, bf16[128,2048]{1,0:T(8,128)(2,1)S(1)}, u32[]{:S(2)}, u32[]{:S(2)}) collective-permute-start(bf16[128,2048]{1,0:T(8,128)(2,1)S(1)} %bitcast.45), channel_id=1, source_target_pairs={{0,8},{4,12},{8,0},{12,4},{1,9},{5,13},{9,1},{13,5},{2,10},{6,14},... | collective-permute-start | bytes 1572872 | tf_op jit(solution)/shard_map/ppermute | solution.py:514
  72.8 13.8 %collective-permute-done.3 = f32[384,128]{1,0:T(8,128)S(1)} collective-permute-done((f32[384,128]{1,0:T(8,128)S(1)}, f32[384,128]{1,0:T(8,128)S(1)}, u32[]{:S(2)}, u32[]{:S(2)}) %collective-permute-start.3) | collective-permute-done | bytes 196640 | tf_op jit(solution)/shard_map/ppermute | solution.py:541
  86.6 2.5 %collective-permute-start.10 = (bf16[128,2048]{1,0:T(8,128)(2,1)S(1)}, bf16[128,2048]{1,0:T(8,128)(2,1)S(1)}, u32[]{:S(2)}, u32[]{:S(2)}) collective-permute-start(bf16[128,2048]{1,0:T(8,128)(2,1)S(1)} %bitcast.46), channel_id=1, source_target_pairs={{0,4},{4,0},{8,12},{12,8},{1,5},{5,1},{9,13},{13,9},{2,6},{6,2},{1... | collective-permute-start | bytes 1572872 | tf_op jit(solution)/shard_map/ppermute | solution.py:514
  89.1 15.8 %collective-permute-done.5.b3.b4 = bf16[128,2048]{1,0:T(8,128)(2,1)S(1)} collective-permute-done((bf16[128,2048]{1,0:T(8,128)(2,1)S(1)}, bf16[128,2048]{1,0:T(8,128)(2,1)S(1)}, u32[]{:S(2)}, u32[]{:S(2)}) %collective-permute-start.5) | collective-permute-done | bytes 524320 | tf_op jit(solution)/shard_map/ppermute | solution.py:514
  104.9 9.5 %collective-permute-done.6 = f32[384,128]{1,0:T(8,128)S(1)} collective-permute-done((f32[384,128]{1,0:T(8,128)S(1)}, f32[384,128]{1,0:T(8,128)S(1)}, u32[]{:S(2)}, u32[]{:S(2)}) %collective-permute-start.6) | collective-permute-done | bytes 196640 | tf_op jit(solution)/shard_map/ppermute | solution.py:543
  116.1 13.5 %collective-permute-done.12.b5 = bf16[128,2048]{1,0:T(8,128)(2,1)S(1)} collective-permute-done((bf16[128,2048]{1,0:T(8,128)(2,1)S(1)}, bf16[128,2048]{1,0:T(8,128)(2,1)S(1)}, u32[]{:S(2)}, u32[]{:S(2)}) %collective-permute-start.12) | collective-permute-done | bytes 524320 | tf_op jit(solution)/shard_map/ppermute | solution.py:518
  130.4 1.1 pad_maximum_fusion.1
  131.5 1.5 collective-permute-start.13
  133.1 1.7 collective-permute-start.18
  136.9 1.2 copy-done.27
  138.1 12.0 %shard_map.157 = (f32[3584,128]{1,0:T(8,128)S(1)}, bf16[3584,128]{1,0:T(8,128)(2,1)S(1)}) custom-call(s32[2]{0:T(128)S(1)} %pad_add_fusion.flags, bf16[128,2048]{1,0:T(8,128)(2,1)S(1)} %bitcast.38, bf16[128,2048]{1,0:T(8,128)(2,1)S(1)} %copy-done.15, bf16[128,2048]{1,0:T(8,128)(2,1)S(1)} %copy-done.18, bf16[128,2048]{1,0:T(8,128)(2,1)S(1)} %collective-permute-done.2.b3.b4, ...), custom_call_target="tpu_custom_call" | custom-call | flops 7516192768 | bytes 30408704 | tf_op jit(solution)/shard_map/pallas_call | solution.py:235
  150.2 5.5 %collective-permute-done.13.far = bf16[2,128,2048]{2,1,0:T(8,128)(2,1)} collective-permute-done((bf16[2,128,2048]{2,1,0:T(8,128)(2,1)}, bf16[2,128,2048]{2,1,0:T(8,128)(2,1)}, u32[]{:S(2)}, u32[]{:S(2)}) %collective-permute-start.13) | collective-permute-done | bytes 1048608 | tf_op jit(solution)/shard_map/ppermute | solution.py:549
  155.7 1.5 collective-permute-start.16
  157.2 11.0 %collective-permute-done.18.b3.b4 = bf16[128,2048]{1,0:T(8,128)(2,1)S(1)} collective-permute-done((bf16[128,2048]{1,0:T(8,128)(2,1)}, bf16[128,2048]{1,0:T(8,128)(2,1)S(1)}, u32[]{:S(2)}, u32[]{:S(2)}) %collective-permute-start.18) | collective-permute-done | bytes 524320 | tf_op jit(solution)/shard_map/ppermute | solution.py:514
  168.2 13.5 %shard_map.155 = (f32[3584,128]{1,0:T(8,128)S(1)}, bf16[3584,128]{1,0:T(8,128)(2,1)S(1)}) custom-call(s32[2]{0:T(128)S(1)} %pad_add_fusion.flags, bf16[128,2048]{1,0:T(8,128)(2,1)S(1)} %bitcast.48, bf16[128,2048]{1,0:T(8,128)(2,1)S(1)} %copy-done.22, bf16[128,2048]{1,0:T(8,128)(2,1)S(1)} %copy-done.20, bf16[128,2048]{1,0:T(8,128)(2,1)S(1)} %collective-permute-done.5.b3.b4, ...), custom_call_target="tpu_custom_call" | custom-call | flops 7516192768 | bytes 30408704 | tf_op jit(solution)/shard_map/pallas_call | solution.py:235
  183.5 2.9 %shard_map.158 = f32[128,128]{1,0:T(8,128)S(1)} custom-call(f32[3584,128]{1,0:T(8,128)S(1)} %get-tuple-element.39.near_sum, bf16[3584,128]{1,0:T(8,128)(2,1)S(1)} %collective-permute-done.16.returned, bf16[128,3584]{1,0:T(8,128)(2,1)S(1)} %bitcast.51, bf16[128,3584]{1,0:T(8,128)(2,1)S(1)} %bitcast.53, bf16[64,3584]{1,0:T(8,128)(2,1)S(1)} %copy-done.8, ...), custom_call_target="tpu_custom_call" | custom-call | flops 117440512 | bytes 4587520 | tf_op jit(solution)/shard_map/pallas_call | solution.py:262
  186.5 2.1 collective-permute-start.21
  188.5 3.1 %collective-permute-done.21 = f32[128,192]{1,0:T(8,128)S(1)} collective-permute-done((f32[128,192]{1,0:T(8,128)S(1)}, f32[128,192]{1,0:T(8,128)S(1)}, u32[]{:S(2)}, u32[]{:S(2)}) %collective-permute-start.21) | collective-permute-done | bytes 98336 | tf_op jit(solution)/shard_map/ppermute | solution.py:501
  191.6 1.7 collective-permute-start.22
  193.3 4.2 %collective-permute-done.22 = f32[128,192]{1,0:T(8,128)S(1)} collective-permute-done((f32[128,192]{1,0:T(8,128)S(1)}, f32[128,192]{1,0:T(8,128)S(1)}, u32[]{:S(2)}, u32[]{:S(2)}) %collective-permute-start.22) | collective-permute-done | bytes 98336 | tf_op jit(solution)/shard_map/ppermute | solution.py:502
  199.5 1.2 collective-permute-start.24
  201.5 6.7 %collective-permute-done.26.far = bf16[2,128,2048]{2,1,0:T(8,128)(2,1)S(1)} collective-permute-done((bf16[2,128,2048]{2,1,0:T(8,128)(2,1)S(1)}, bf16[2,128,2048]{2,1,0:T(8,128)(2,1)S(1)}, u32[]{:S(2)}, u32[]{:S(2)}) %collective-permute-start.26) | collective-permute-done | bytes 1048608 | tf_op jit(solution)/shard_map/ppermute | solution.py:559
  208.2 17.2 %shard_map.161 = f32[256,128]{1,0:T(8,128)S(1)} custom-call(s32[2]{0:T(128)S(1)} %pad_add_fusion.flags, bf16[128,2048]{1,0:T(8,128)(2,1)S(1)} %bitcast.43, bf16[128,2048]{1,0:T(8,128)(2,1)S(1)} %collective-permute-done.19.b1, bf16[128,2048]{1,0:T(8,128)(2,1)S(1)} %collective-permute-done.17.b2, bf16[128,2048]{1,0:T(8,128)(2,1)S(1)} %collective-permute-done.18.b3.b4, ...), custom_call_target="tpu_custom_call" | custom-call | flops 7516192768 | bytes 30408704 | tf_op jit(solution)/shard_map/pallas_call | solution.py:289
  226.1 1.8 collective-permute-done.15.returned
  227.8 2.9 %shard_map.156.near = f32[128,128]{1,0:T(8,128)S(1)} custom-call(f32[3584,128]{1,0:T(8,128)S(1)} %get-tuple-element.36.near_sum, bf16[3584,128]{1,0:T(8,128)(2,1)S(1)} %collective-permute-done.15.returned, bf16[256,3584]{1,0:T(8,128)(2,1)S(1)} %bitcast.30, bf16[256,3584]{1,0:T(8,128)(2,1)S(1)} %bitcast.33, bf16[64,3584]{1,0:T(8,128)(2,1)S(1)} %copy-done.8, ...), custom_call_target="tpu_custom_call" | custom-call | flops 117440512 | bytes 6422528 | tf_op jit(solution)/shard_map/pallas_call | solution.py:262
  230.7 1.4 collective-permute-done.24.q2
  232.0 2.7 %collective-permute-done.25.q3 = f32[2,192,64]{2,1,0:T(8,128)S(1)} collective-permute-done((f32[2,192,64]{2,1,0:T(8,128)S(1)}, f32[2,192,64]{2,1,0:T(8,128)S(1)}, u32[]{:S(2)}, u32[]{:S(2)}) %collective-permute-start.25) | collective-permute-done | bytes 98336 | tf_op jit(solution)/shard_map/ppermute | solution.py:569
  234.8 1.1 shard_map.160
  235.9 1.1 shard_map.162
  237.0 1.8 collective-permute-start.28
  238.8 1.9 collective-permute-done.28
  241.5 3.7 %collective-permute-done.29 = f32[4,8]{1,0:T(4,128)S(1)} collective-permute-done((f32[4,8]{1,0:T(4,128)S(1)}, f32[4,8]{1,0:T(4,128)S(1)}, u32[]{:S(2)}, u32[]{:S(2)}) %collective-permute-start.29) | collective-permute-done | bytes 160 | tf_op jit(solution)/shard_map/ppermute | solution.py:502
  (122 shorter events, 18.8 us)
Async XLA Ops:
  0.0 46.9 %copy-start = (bf16[4,64,3584]{2,1,0:T(8,128)(2,1)S(1)}, bf16[4,64,3584]{2,1,0:T(8,128)(2,1)}, u32[]{:S(2)}) copy-start(bf16[4,64,3584]{2,1,0:T(8,128)(2,1)} %param.17) | copy-start | bytes 5505028
  0.0 46.9 %copy-start.3 = (bf16[2,64,2048]{2,1,0:T(8,128)(2,1)S(1)}, bf16[2,64,2048]{2,1,0:T(8,128)(2,1)}, u32[]{:S(2)}) copy-start(bf16[2,64,2048]{2,1,0:T(8,128)(2,1)} %param.24) | copy-start | bytes 1572868
  0.0 134.8 %collective-permute-start.14 = (bf16[3584,2048]{1,0:T(8,128)(2,1)}, bf16[3584,2048]{1,0:T(8,128)(2,1)}, u32[]{:S(2)}, u32[]{:S(2)}) collective-permute-start(bf16[3584,2048]{1,0:T(8,128)(2,1)} %weight_own.5), channel_id=1, source_target_pairs={{0,1},{1,0},{2,3},{3,2},{4,5},{5,4},{6,7},{7,6},{8,9},{9,8},{10,11... | collective-permute-start | bytes 44040200 | tf_op jit(solution)/shard_map/ppermute | solution.py:535
  1.9 41.3 %collective-permute-start.7 = (bf16[128,3584]{1,0:T(8,128)(2,1)S(1)}, bf16[128,3584]{1,0:T(8,128)(2,1)S(1)}, u32[]{:S(2)}, u32[]{:S(2)}) collective-permute-start(bf16[128,3584]{1,0:T(8,128)(2,1)S(1)} %bitcast.56), channel_id=1, source_target_pairs={{0,2},{1,3},{2,0},{3,1},{4,6},{5,7},{6,4},{7,5},{8,10},{9,11},{10,... | collective-permute-start | bytes 2752520 | tf_op jit(solution)/shard_map/ppermute | solution.py:530
  4.4 14.2 %collective-permute-start = (bf16[128,2048]{1,0:T(8,128)(2,1)}, bf16[128,2048]{1,0:T(8,128)(2,1)S(1)}, u32[]{:S(2)}, u32[]{:S(2)}) collective-permute-start(bf16[128,2048]{1,0:T(8,128)(2,1)} %bitcast.34), channel_id=1, source_target_pairs={{0,4},{4,0},{8,12},{12,8},{1,5},{5,1},{9,13},{13,9},{2,6},{6,2},{1... | collective-permute-start | bytes 1572872 | tf_op jit(solution)/shard_map/ppermute | solution.py:514
  6.0 17.2 %collective-permute-start.1 = (bf16[128,2048]{1,0:T(8,128)(2,1)}, bf16[128,2048]{1,0:T(8,128)(2,1)S(1)}, u32[]{:S(2)}, u32[]{:S(2)}) collective-permute-start(bf16[128,2048]{1,0:T(8,128)(2,1)} %bitcast.35), channel_id=1, source_target_pairs={{0,1},{1,0},{2,3},{3,2},{4,8},{5,9},{6,10},{7,11},{8,4},{9,5},{10,... | collective-permute-start | bytes 1572872 | tf_op jit(solution)/shard_map/ppermute | solution.py:514
  6.0 37.2 %collective-permute-start.2 = (bf16[128,2048]{1,0:T(8,128)(2,1)}, bf16[128,2048]{1,0:T(8,128)(2,1)S(1)}, u32[]{:S(2)}, u32[]{:S(2)}) collective-permute-start(bf16[128,2048]{1,0:T(8,128)(2,1)} %bitcast.36), channel_id=1, source_target_pairs={{0,8},{4,12},{8,0},{12,4},{1,9},{5,13},{9,1},{13,5},{2,10},{6,14},... | collective-permute-start | bytes 1572872 | tf_op jit(solution)/shard_map/ppermute | solution.py:514
  18.6 42.4 %copy-start.14 = (bf16[128,2048]{1,0:T(8,128)(2,1)}, bf16[128,2048]{1,0:T(8,128)(2,1)S(1)}, u32[]{:S(2)}) copy-start(bf16[128,2048]{1,0:T(8,128)(2,1)S(1)} %collective-permute-done.b1) | copy-start | bytes 1572868
  23.2 20.0 %copy-start.16 = (bf16[128,2048]{1,0:T(8,128)(2,1)}, bf16[128,2048]{1,0:T(8,128)(2,1)S(1)}, u32[]{:S(2)}) copy-start(bf16[128,2048]{1,0:T(8,128)(2,1)S(1)} %collective-permute-done.1.b2) | copy-start | bytes 1572868
  44.1 16.8 %collective-permute-start.8 = (bf16[128,2048]{1,0:T(8,128)(2,1)S(1)}, bf16[128,2048]{1,0:T(8,128)(2,1)}, u32[]{:S(2)}, u32[]{:S(2)}) collective-permute-start(bf16[128,2048]{1,0:T(8,128)(2,1)S(1)} %collective-permute-done.2.b3.b4), channel_id=1, source_target_pairs={{0,4},{4,0},{8,12},{12,8},{1,5},{5,1},{9,13},{13,9},{2,6},{6,2},{1... | collective-permute-start | bytes 1572872 | tf_op jit(solution)/shard_map/ppermute | solution.py:518
  46.3 21.8 %collective-permute-start.9 = (bf16[128,3584]{1,0:T(8,128)(2,1)}, bf16[128,3584]{1,0:T(8,128)(2,1)}, u32[]{:S(2)}, u32[]{:S(2)}) collective-permute-start(bf16[128,3584]{1,0:T(8,128)(2,1)} %bitcast.15), channel_id=1, source_target_pairs={{0,2},{1,3},{2,0},{3,1},{4,6},{5,7},{6,4},{7,5},{8,10},{9,11},{10,... | collective-permute-start | bytes 2752520 | tf_op jit(solution)/shard_map/ppermute | solution.py:538
  57.1 3.9 %copy-start.17 = (bf16[128,2048]{1,0:T(8,128)(2,1)S(1)}, bf16[128,2048]{1,0:T(8,128)(2,1)}, u32[]{:S(2)}) copy-start(bf16[128,2048]{1,0:T(8,128)(2,1)} %copy-done.16) | copy-start | bytes 1572868
  68.1 47.0 %collective-permute-start.11 = (bf16[2,128,2048]{2,1,0:T(8,128)(2,1)S(1)}, bf16[2,128,2048]{2,1,0:T(8,128)(2,1)S(1)}, u32[]{:S(2)}, u32[]{:S(2)}) collective-permute-start(bf16[2,128,2048]{2,1,0:T(8,128)(2,1)S(1)} %pad_maximum_fusion), channel_id=1, source_target_pairs={{0,2},{1,3},{2,0},{3,1},{4,6},{5,7},{6,4},{7,5},{8,10},{9,11},{10,... | collective-permute-start | bytes 3145736 | tf_op jit(solution)/shard_map/ppermute | solution.py:544
  69.6 60.2 %copy-start.5 = (bf16[2,64,2048]{2,1,0:T(8,128)(2,1)}, bf16[2,64,2048]{2,1,0:T(8,128)(2,1)S(1)}, u32[]{:S(2)}) copy-start(bf16[2,64,2048]{2,1,0:T(8,128)(2,1)S(1)} %get-tuple-element.48) | copy-start | bytes 1572868
  69.6 19.5 %collective-permute-start.4 = (bf16[128,2048]{1,0:T(8,128)(2,1)S(1)}, bf16[128,2048]{1,0:T(8,128)(2,1)S(1)}, u32[]{:S(2)}, u32[]{:S(2)}) collective-permute-start(bf16[128,2048]{1,0:T(8,128)(2,1)S(1)} %bitcast.44), channel_id=1, source_target_pairs={{0,1},{1,0},{2,3},{3,2},{4,8},{5,9},{6,10},{7,11},{8,4},{9,5},{10,... | collective-permute-start | bytes 1572872 | tf_op jit(solution)/shard_map/ppermute | solution.py:514
  69.6 35.3 %collective-permute-start.5 = (bf16[128,2048]{1,0:T(8,128)(2,1)S(1)}, bf16[128,2048]{1,0:T(8,128)(2,1)S(1)}, u32[]{:S(2)}, u32[]{:S(2)}) collective-permute-start(bf16[128,2048]{1,0:T(8,128)(2,1)S(1)} %bitcast.45), channel_id=1, source_target_pairs={{0,8},{4,12},{8,0},{12,4},{1,9},{5,13},{9,1},{13,5},{2,10},{6,14},... | collective-permute-start | bytes 1572872 | tf_op jit(solution)/shard_map/ppermute | solution.py:514
  72.8 13.8 %collective-permute-start.3 = (f32[384,128]{1,0:T(8,128)S(1)}, f32[384,128]{1,0:T(8,128)S(1)}, u32[]{:S(2)}, u32[]{:S(2)}) collective-permute-start(f32[384,128]{1,0:T(8,128)S(1)} %get-tuple-element.27), channel_id=1, source_target_pairs={{0,4},{4,0},{8,12},{12,8},{1,5},{5,1},{9,13},{13,9},{2,6},{6,2},{1... | collective-permute-start | bytes 589832 | tf_op jit(solution)/shard_map/ppermute | solution.py:541
  86.6 28.5 %collective-permute-start.10 = (bf16[128,2048]{1,0:T(8,128)(2,1)S(1)}, bf16[128,2048]{1,0:T(8,128)(2,1)S(1)}, u32[]{:S(2)}, u32[]{:S(2)}) collective-permute-start(bf16[128,2048]{1,0:T(8,128)(2,1)S(1)} %bitcast.46), channel_id=1, source_target_pairs={{0,4},{4,0},{8,12},{12,8},{1,5},{5,1},{9,13},{13,9},{2,6},{6,2},{1... | collective-permute-start | bytes 1572872 | tf_op jit(solution)/shard_map/ppermute | solution.py:514
  89.1 40.7 %copy-start.19 = (bf16[128,2048]{1,0:T(8,128)(2,1)}, bf16[128,2048]{1,0:T(8,128)(2,1)S(1)}, u32[]{:S(2)}) copy-start(bf16[128,2048]{1,0:T(8,128)(2,1)S(1)} %collective-permute-done.4.b2) | copy-start | bytes 1572868
  104.9 9.5 %collective-permute-start.6 = (f32[384,128]{1,0:T(8,128)S(1)}, f32[384,128]{1,0:T(8,128)S(1)}, u32[]{:S(2)}, u32[]{:S(2)}) collective-permute-start(f32[384,128]{1,0:T(8,128)S(1)} %add.27), channel_id=1, source_target_pairs={{0,8},{4,12},{8,0},{12,4},{1,9},{5,13},{9,1},{13,5},{2,10},{6,14},... | collective-permute-start | bytes 589832 | tf_op jit(solution)/shard_map/ppermute | solution.py:543
  115.1 14.7 %copy-start.21 = (bf16[128,2048]{1,0:T(8,128)(2,1)}, bf16[128,2048]{1,0:T(8,128)(2,1)S(1)}, u32[]{:S(2)}) copy-start(bf16[128,2048]{1,0:T(8,128)(2,1)S(1)} %collective-permute-done.10.b1) | copy-start | bytes 1572868
  116.1 13.5 %collective-permute-start.12 = (bf16[128,2048]{1,0:T(8,128)(2,1)S(1)}, bf16[128,2048]{1,0:T(8,128)(2,1)S(1)}, u32[]{:S(2)}, u32[]{:S(2)}) collective-permute-start(bf16[128,2048]{1,0:T(8,128)(2,1)S(1)} %collective-permute-done.5.b3.b4), channel_id=1, source_target_pairs={{0,4},{4,0},{8,12},{12,8},{1,5},{5,1},{9,13},{13,9},{2,6},{6,2},{1... | collective-permute-start | bytes 1572872 | tf_op jit(solution)/shard_map/ppermute | solution.py:518
  131.5 24.2 %collective-permute-start.13 = (bf16[2,128,2048]{2,1,0:T(8,128)(2,1)}, bf16[2,128,2048]{2,1,0:T(8,128)(2,1)}, u32[]{:S(2)}, u32[]{:S(2)}) collective-permute-start(bf16[2,128,2048]{2,1,0:T(8,128)(2,1)} %pad_maximum_fusion.1), channel_id=1, source_target_pairs={{0,2},{1,3},{2,0},{3,1},{4,6},{5,7},{6,4},{7,5},{8,10},{9,11},{10,... | collective-permute-start | bytes 3145736 | tf_op jit(solution)/shard_map/ppermute | solution.py:549
  133.1 35.1 %copy-start.6 = (bf16[2,64,2048]{2,1,0:T(8,128)(2,1)S(1)}, bf16[2,64,2048]{2,1,0:T(8,128)(2,1)}, u32[]{:S(2)}) copy-start(bf16[2,64,2048]{2,1,0:T(8,128)(2,1)} %copy-done.5) | copy-start | bytes 1572868
  133.1 24.1 %collective-permute-start.17 = (bf16[128,2048]{1,0:T(8,128)(2,1)}, bf16[128,2048]{1,0:T(8,128)(2,1)S(1)}, u32[]{:S(2)}, u32[]{:S(2)}) collective-permute-start(bf16[128,2048]{1,0:T(8,128)(2,1)} %bitcast.39), channel_id=1, source_target_pairs={{0,1},{1,0},{2,3},{3,2},{4,8},{5,9},{6,10},{7,11},{8,4},{9,5},{10,... | collective-permute-start | bytes 1572872 | tf_op jit(solution)/shard_map/ppermute | solution.py:514
  133.1 35.0 %collective-permute-start.18 = (bf16[128,2048]{1,0:T(8,128)(2,1)}, bf16[128,2048]{1,0:T(8,128)(2,1)S(1)}, u32[]{:S(2)}, u32[]{:S(2)}) collective-permute-start(bf16[128,2048]{1,0:T(8,128)(2,1)} %bitcast.40), channel_id=1, source_target_pairs={{0,8},{4,12},{8,0},{12,4},{1,9},{5,13},{9,1},{13,5},{2,10},{6,14},... | collective-permute-start | bytes 1572872 | tf_op jit(solution)/shard_map/ppermute | solution.py:514
  134.8 33.3 %collective-permute-start.19 = (bf16[128,2048]{1,0:T(8,128)(2,1)}, bf16[128,2048]{1,0:T(8,128)(2,1)S(1)}, u32[]{:S(2)}, u32[]{:S(2)}) collective-permute-start(bf16[128,2048]{1,0:T(8,128)(2,1)} %bitcast.41), channel_id=1, source_target_pairs={{0,4},{4,0},{8,12},{12,8},{1,5},{5,1},{9,13},{13,9},{2,6},{6,2},{1... | collective-permute-start | bytes 1572872 | tf_op jit(solution)/shard_map/ppermute | solution.py:514
  138.1 30.0 %copy-start.20 = (bf16[128,2048]{1,0:T(8,128)(2,1)S(1)}, bf16[128,2048]{1,0:T(8,128)(2,1)}, u32[]{:S(2)}) copy-start(bf16[128,2048]{1,0:T(8,128)(2,1)} %copy-done.19) | copy-start | bytes 1572868
  138.1 30.0 %copy-start.22 = (bf16[128,2048]{1,0:T(8,128)(2,1)S(1)}, bf16[128,2048]{1,0:T(8,128)(2,1)}, u32[]{:S(2)}) copy-start(bf16[128,2048]{1,0:T(8,128)(2,1)} %copy-done.21) | copy-start | bytes 1572868
  138.1 30.0 %copy-start.24 = (bf16[128,2048]{1,0:T(8,128)(2,1)S(1)}, bf16[128,2048]{1,0:T(8,128)(2,1)}, u32[]{:S(2)}) copy-start(bf16[128,2048]{1,0:T(8,128)(2,1)} %copy-done.23) | copy-start | bytes 1572868
  155.7 26.0 %copy-start.4 = (bf16[2,64,2048]{2,1,0:T(8,128)(2,1)S(1)}, bf16[2,64,2048]{2,1,0:T(8,128)(2,1)}, u32[]{:S(2)}) copy-start(bf16[2,64,2048]{2,1,0:T(8,128)(2,1)} %get-tuple-element.47) | copy-start | bytes 1572868
  155.7 27.2 %collective-permute-start.16 = (bf16[3584,128]{1,0:T(8,128)(2,1)S(1)}, bf16[3584,128]{1,0:T(8,128)(2,1)S(1)}, u32[]{:S(2)}, u32[]{:S(2)}) collective-permute-start(bf16[3584,128]{1,0:T(8,128)(2,1)S(1)} %get-tuple-element.41), channel_id=1, source_target_pairs={{0,2},{1,3},{2,0},{3,1},{4,6},{5,7},{6,4},{7,5},{8,10},{9,11},{10,... | collective-permute-start | bytes 2752520 | tf_op jit(solution)/shard_map/ppermute | solution.py:553
  168.1 13.6 %collective-permute-start.20 = (bf16[128,2048]{1,0:T(8,128)(2,1)S(1)}, bf16[128,2048]{1,0:T(8,128)(2,1)S(1)}, u32[]{:S(2)}, u32[]{:S(2)}) collective-permute-start(bf16[128,2048]{1,0:T(8,128)(2,1)S(1)} %collective-permute-done.18.b3.b4), channel_id=1, source_target_pairs={{0,4},{4,0},{8,12},{12,8},{1,5},{5,1},{9,13},{13,9},{2,6},{6,2},{1... | collective-permute-start | bytes 1572872 | tf_op jit(solution)/shard_map/ppermute | solution.py:518
  182.0 26.2 %collective-permute-start.26 = (bf16[2,128,2048]{2,1,0:T(8,128)(2,1)S(1)}, bf16[2,128,2048]{2,1,0:T(8,128)(2,1)S(1)}, u32[]{:S(2)}, u32[]{:S(2)}) collective-permute-start(bf16[2,128,2048]{2,1,0:T(8,128)(2,1)S(1)} %pad_maximum_fusion.2), channel_id=1, source_target_pairs={{0,2},{1,3},{2,0},{3,1},{4,6},{5,7},{6,4},{7,5},{8,10},{9,11},{10,... | collective-permute-start | bytes 3145736 | tf_op jit(solution)/shard_map/ppermute | solution.py:559
  183.5 9.8 %copy-start.37 = (f32[384,128]{1,0:T(8,128)S(1)}, f32[384,128]{1,0:T(8,128)}, u32[]{:S(2)}) copy-start(f32[384,128]{1,0:T(8,128)} %add.28) | copy-start | bytes 589828
  183.5 14.1 %copy-start.36 = (s32[2]{0:T(128)S(1)}, s32[2]{0:T(128)}, u32[]{:S(2)}) copy-start(s32[2]{0:T(128)} %lengths.1) | copy-start | bytes 28
  183.5 24.6 %copy-start.29 = (bf16[128,3584]{1,0:T(8,128)(2,1)S(1)}, bf16[128,3584]{1,0:T(8,128)(2,1)}, u32[]{:S(2)}) copy-start(bf16[128,3584]{1,0:T(8,128)(2,1)} %copy-done.28) | copy-start | bytes 2752516
  186.4 21.7 %copy-start.2 = (bf16[4,64,3584]{2,1,0:T(8,128)(2,1)S(1)}, bf16[4,64,3584]{2,1,0:T(8,128)(2,1)}, u32[]{:S(2)}) copy-start(bf16[4,64,3584]{2,1,0:T(8,128)(2,1)} %param.18) | copy-start | bytes 5505028
  186.5 5.2 %collective-permute-start.21 = (f32[128,192]{1,0:T(8,128)S(1)}, f32[128,192]{1,0:T(8,128)S(1)}, u32[]{:S(2)}, u32[]{:S(2)}) collective-permute-start(f32[128,192]{1,0:T(8,128)S(1)} %pad_maximum_fusion.3), channel_id=1, source_target_pairs={{0,4},{4,0},{8,12},{12,8},{1,5},{5,1},{9,13},{13,9},{2,6},{6,2},{1... | collective-permute-start | bytes 294920 | tf_op jit(solution)/shard_map/ppermute | solution.py:501
  191.6 5.9 %collective-permute-start.22 = (f32[128,192]{1,0:T(8,128)S(1)}, f32[128,192]{1,0:T(8,128)S(1)}, u32[]{:S(2)}, u32[]{:S(2)}) collective-permute-start(f32[128,192]{1,0:T(8,128)S(1)} %fusion.1), channel_id=1, source_target_pairs={{0,8},{4,12},{8,0},{12,4},{1,9},{5,13},{9,1},{13,5},{2,10},{6,14},... | collective-permute-start | bytes 294920 | tf_op jit(solution)/shard_map/ppermute | solution.py:502
  198.5 27.5 %copy-start.38 = (s32[4]{0:T(128)S(1)}, s32[4]{0:T(128)}, u32[]{:S(2)}) copy-start(s32[4]{0:T(128)} %param.20) | copy-start | bytes 52
  198.5 2.2 collective-permute-start.23
  198.6 29.2 %collective-permute-start.15 = (bf16[3584,128]{1,0:T(8,128)(2,1)S(1)}, bf16[3584,128]{1,0:T(8,128)(2,1)S(1)}, u32[]{:S(2)}, u32[]{:S(2)}) collective-permute-start(bf16[3584,128]{1,0:T(8,128)(2,1)S(1)} %get-tuple-element.37), channel_id=1, source_target_pairs={{0,2},{1,3},{2,0},{3,1},{4,6},{5,7},{6,4},{7,5},{8,10},{9,11},{10,... | collective-permute-start | bytes 2752520 | tf_op jit(solution)/shard_map/ppermute | solution.py:556
  199.5 32.6 %collective-permute-start.24 = (f32[2,192,64]{2,1,0:T(8,128)S(1)}, f32[2,192,64]{2,1,0:T(8,128)S(1)}, u32[]{:S(2)}, u32[]{:S(2)}) collective-permute-start(f32[2,192,64]{2,1,0:T(8,128)S(1)} %shard_map.159.q0), channel_id=1, source_target_pairs={{0,2},{1,3},{2,0},{3,1},{4,6},{5,7},{6,4},{7,5},{8,10},{9,11},{10,... | collective-permute-start | bytes 294920 | tf_op jit(solution)/shard_map/ppermute | solution.py:569
  200.7 34.1 %collective-permute-start.25 = (f32[2,192,64]{2,1,0:T(8,128)S(1)}, f32[2,192,64]{2,1,0:T(8,128)S(1)}, u32[]{:S(2)}, u32[]{:S(2)}) collective-permute-start(f32[2,192,64]{2,1,0:T(8,128)S(1)} %collective-permute-done.23.q1), channel_id=1, source_target_pairs={{0,2},{1,3},{2,0},{3,1},{4,6},{5,7},{6,4},{7,5},{8,10},{9,11},{10,... | collective-permute-start | bytes 294920 | tf_op jit(solution)/shard_map/ppermute | solution.py:569
  225.4 10.5 %collective-permute-start.27 = (f32[128,128]{1,0:T(8,128)S(1)}, f32[128,128]{1,0:T(8,128)S(1)}, u32[]{:S(2)}, u32[]{:S(2)}) collective-permute-start(f32[128,128]{1,0:T(8,128)S(1)} %get-tuple-element.61), channel_id=1, source_target_pairs={{0,2},{1,3},{2,0},{3,1},{4,6},{5,7},{6,4},{7,5},{8,10},{9,11},{10,... | collective-permute-start | bytes 196616 | tf_op jit(solution)/shard_map/ppermute | solution.py:581
  237.0 3.7 %collective-permute-start.28 = (f32[4,8]{1,0:T(4,128)S(1)}, f32[4,8]{1,0:T(4,128)S(1)}, u32[]{:S(2)}, u32[]{:S(2)}) collective-permute-start(f32[4,8]{1,0:T(4,128)S(1)} %pad_maximum_fusion.4), channel_id=1, source_target_pairs={{0,4},{4,0},{8,12},{12,8},{1,5},{5,1},{9,13},{13,9},{2,6},{6,2},{1... | collective-permute-start | bytes 392 | tf_op jit(solution)/shard_map/ppermute | solution.py:501
  240.7 4.5 %collective-permute-start.29 = (f32[4,8]{1,0:T(4,128)S(1)}, f32[4,8]{1,0:T(4,128)S(1)}, u32[]{:S(2)}, u32[]{:S(2)}) collective-permute-start(f32[4,8]{1,0:T(4,128)S(1)} %fusion), channel_id=1, source_target_pairs={{0,8},{4,12},{8,0},{12,4},{1,9},{5,13},{9,1},{13,5},{2,10},{6,14},... | collective-permute-start | bytes 392 | tf_op jit(solution)/shard_map/ppermute | solution.py:502
  (21 other events, 24.1 us)

commit v6 on v5

--- a/solution.py
+++ b/solution.py
@@ -127,8 +127,7 @@
 
 
 def cost(flops, arrays):
-    moved = sum(array.size * array.dtype.itemsize for array in arrays)
-    return pl.CostEstimate(flops=flops, bytes_accessed=moved, transcendentals=0)
+    return pl.CostEstimate(flops=1024, bytes_accessed=1024, transcendentals=0)
 
 
 def tile_columns(number, block=0):
@@ -405,22 +404,22 @@
 
 
 def score_kernel(
-    lengths, place, in_out, hidden, near, far, q0, q1, q2, q3, scores
+    lengths, place, in_out, hidden, early, near, far, q0, q1, q2, q3, scores
 ):
     queries = q0.shape[0]
     shape = scores.shape
     row = lax.broadcasted_iota(jnp.int32, shape, 0)
     column = lax.broadcasted_iota(jnp.int32, shape, 1)
+    gradient = jnp.concatenate([early[...], near[...] + far[...]], axis=0)
     total = jnp.zeros(shape, jnp.float32)
     for e in range(shape[0]):
         part = slice(e * SEQ, (e + 1) * SEQ)
-        gradient = near[part, :] + far[part, :]
         three = jnp.concatenate(
             example_features(
                 in_out[part, :RANK],
                 hidden[part, :],
-                gradient[:, :RANK],
-                gradient[:, RANK:],
+                gradient[part, :RANK],
+                gradient[part, RANK:],
                 in_out[part, RANK:],
                 lengths[e],
             ),
@@ -436,15 +435,15 @@
     scores[...] = total
 
 
-def partial_scores(lengths, place, in_out, hidden, near, far, found):
+def partial_scores(lengths, place, in_out, hidden, early, near, far, found):
     number = lengths.shape[0]
     return pl.pallas_call(
         score_kernel,
-        in_specs=[SCALARS] * 2 + [IN_VMEM] * 8,
+        in_specs=[SCALARS] * 2 + [IN_VMEM] * 9,
         out_specs=IN_VMEM,
         out_shape=jax.ShapeDtypeStruct((number, 4 * found[0].shape[0]), jnp.float32),
         compiler_params=params(),
-    )(lengths, place, in_out, hidden, near, far, *found)
+    )(lengths, place, in_out, hidden, early, near, far, *found)
 
 
 def after(value, *others):
@@ -487,6 +486,9 @@
     across = functools.partial(
         lax.ppermute, axis_name="tensor", perm=[(i, i ^ 2) for i in range(4)]
     )
+    opposite = functools.partial(
+        lax.ppermute, axis_name="tensor", perm=[(i, 3 - i) for i in range(4)]
+    )
     middle = functools.partial(
         lax.ppermute,
         axis_name=("tensor", "dp"),
@@ -510,12 +512,12 @@
     examples = train_lengths.shape[0] // 2
     cut = examples * SEQ
 
-    def direct(own, *others):
-        return own, outer(after(own, *others)), middle(own), across(own)
-
-    def last_hop(own, one, mid, two, *others):
-        two = after(two, one, mid, *others)
-        return own, one, mid, two, two, outer(two)
+    def first_hops(own):
+        return own, outer(own), across(own)
+
+    def last_hops(own, one, two):
+        mid = middle(after(own, two))
+        return own, one, mid, two, two, outer(after(two, one))
 
     def crossing_pair(own, one, second_inner, third_inner, second_outer, third_outer):
         def choose(within, beyond_inner, beyond_outer):
@@ -526,37 +528,34 @@
             [choose(own, second_inner, second_outer), choose(one, third_inner, third_outer)]
         )
 
-    q_direct = direct(q_outgrad)
+    weight_own, weight_sib = down_weight, to_core(down_weight)
+    q_hops = first_hops(q_outgrad)
     far_gate = to_chip(t_gate[cut:])
+    q_blocks = last_hops(*q_hops)
     own_in_out, hidden = early_sides(
-        t_input, after(q_input, *q_direct[1:]), t_outgrad, q_outgrad, proj_input, proj_outgrad, t_gate, t_up, q_gate,
+        t_input, q_input, t_outgrad, q_outgrad, proj_input, proj_outgrad, t_gate, t_up, q_gate,
         q_up, proj_hidden,
     )
-    weight_own, weight_sib = down_weight, to_core(down_weight)
-    q_blocks = last_hop(*q_direct, far_gate)
-
+
+    a_hops = first_hops(after(t_outgrad[:cut], q_hops[2], far_gate))
     far_up = to_chip(after(t_up[cut:], far_gate))
-    q_send = after(crossing_pair(*q_blocks), far_up, own_in_out)
-    a_direct = direct(after(t_outgrad[:cut], q_direct[3]), q_send)
-    pair_in_out = own_in_out + outer(own_in_out)
-    pair_in_out = after(pair_in_out, a_direct[2], a_direct[3])
-    in_out = pair_in_out + across(pair_in_out)
+    q_send = after(crossing_pair(*q_blocks), far_up)
     q_far = to_chip(q_send)
-    a_blocks = last_hop(*a_direct, in_out, q_far)
-
-    b_direct = direct(after(t_outgrad[cut:], a_blocks[3]))
-    a_send = crossing_pair(*a_blocks)
+    a_blocks = last_hops(*a_hops[:2], after(a_hops[2], q_send))
+
+    b_hops = first_hops(after(t_outgrad[cut:], a_hops[2]))
+    a_send = crossing_pair(*a_blocks[:5], after(a_blocks[5], q_far, own_in_out))
     a_far = to_chip(a_send)
     q_near_sum, q_far_sum = partial_sums(
         flags, q_blocks, after(q_far, a_send), weight_own, weight_sib
     )
-    q_returned = to_chip(after(q_far_sum, a_far))
-    b_blocks = last_hop(*b_direct, q_far_sum)
+    q_returned = to_chip(q_far_sum)
+    b_blocks = last_hops(*b_hops[:2], after(b_hops[2], q_far_sum))
     a_near_sum, a_far_sum = partial_sums(flags, a_blocks, a_far, weight_own, weight_sib)
     a_returned = to_chip(a_far_sum)
-    b_blocks = b_blocks[:5] + (after(b_blocks[5], a_far_sum),)
-    b_send = crossing_pair(*b_blocks)
+    b_send = after(crossing_pair(*b_blocks), a_far_sum)
     b_far = to_chip(b_send)
+    in_out = tensor_sum(after(own_in_out, b_send))
     q_gradient = finished_sides(
         q_near_sum, after(q_returned, b_send), q_gate, q_up, proj_gate, proj_up
     )
@@ -568,19 +567,15 @@
     core_found = to_core(own_found)
     found = (own_found, core_found, to_chip(own_found), to_chip(core_found))
     b_gradient = lent_sides(
-        flags, b_blocks, after(b_far, core_found), weight_own, weight_sib, t_gate, t_up, far_gate,
+        flags, b_blocks, after(b_far, *found), weight_own, weight_sib, t_gate, t_up, far_gate,
         far_up, proj_gate, proj_up,
     )
     a_gradient = finished_sides(a_near_sum, a_returned, t_gate, t_up, proj_gate, proj_up)
-    a_scores = partial_scores(
-        train_lengths[:examples], place, in_out[:cut], hidden[:cut], a_gradient,
-        jnp.zeros_like(a_gradient), found,
-    )
-    b_scores = partial_scores(
-        train_lengths[examples:], place, in_out[cut : 2 * cut], hidden[cut : 2 * cut],
-        b_gradient[:cut], to_chip(b_gradient[cut:]), found,
-    )
-    scores = tensor_sum(jnp.concatenate([a_scores, b_scores], axis=0))
+    own_scores = partial_scores(
+        train_lengths, place, in_out[: 2 * cut], hidden[: 2 * cut], a_gradient, b_gradient[:cut],
+        to_chip(b_gradient[cut:]), found,
+    )
+    scores = own_scores + outer(own_scores) + across(own_scores) + opposite(own_scores)
     return scores / (RANK * SEQ)
 
 

time: 247 us -> 214 us (0.87)
  waiting for transfers between devices: 135 us -> 94.2 us
  starting transfers between devices: 29.2 us -> 41.9 us
  local copies, waits for them, and re-layouts: 21.7 us -> 18 us
    ppermute x15 -> x16, waiting for transfers between devices: 98.1 us -> 53.4 us  [the longest x6 34.8 us: first_hops(): return (own, outer(own), across(own))]
    ppermute x2, waiting for transfers between devices: 4.09 us -> 25 us  [moving_plan(): found = (own_found, core_found, to_chip(own_found), to_chip(core_found))]
    ppermute x15 -> x16, starting transfers between devices: 13.1 us -> 25.6 us  [the longest x6 17.7 us: first_hops(): return (own, outer(own), across(own))]
    ppermute x1, waiting for transfers between devices: 6.66 us -> 0.01 us  [moving_plan(): b_far = to_chip(b_send)]
    ppermute x1, waiting for transfers between devices: 5.8 us -> 0.01 us  [moving_plan(): far_up = to_chip(after(t_up[cut:], far_gate))]
    ppermute x1, waiting for transfers between devices: 5.48 us -> 1.2 us  [moving_plan(): a_far = to_chip(a_send)]
    unnamed x78 -> x82, local copies, waits for them, and re-layouts: 17.1 us -> 14.5 us
  transfers between devices with their start and end apart: 30 -> 31, of which waited for: 18 -> 19; matrix products, arithmetic and copies ran while one was open for 3% -> 3% of each run, Pallas kernels for 22% -> 26%
where the time goes in v6:
time: 214 us; the launch traced here: 213 us
  waiting for transfers between devices  94.2 us (44%)
  Pallas kernels  56.3 us (26%)
  starting transfers between devices  41.9 us (20%)
  local copies, waits for them, and re-layouts  18 us (8%)
  other arithmetic  2.54 us (1%)
    ppermute x6, waiting for transfers between devices, first_hops(): return (own, outer(own), across(own))  34.8 us
    pallas_call x2, Pallas kernels, partial_sums(): pl.pallas_call(partial_kernel, grid=(units // TILE,), in_specs=[SCALARS]...  25.7 us
    ppermute x2, waiting for transfers between devices, moving_plan(): found = (own_found, core_found, to_chip(own_found), to_chip(core_found))  25 us
    pallas_call x1, Pallas kernels, lent_sides(): pl.pallas_call(lent_kernel, grid=(units // TILE,), in_specs=[SCALARS] + [...  18.6 us
    ppermute x6, starting transfers between devices, first_hops(): return (own, outer(own), across(own))  17.7 us
    unnamed x82, local copies, waits for them, and re-layouts  14.5 us
    ppermute x3, waiting for transfers between devices, last_hops(): return (own, one, mid, two, two, outer(after(two, one)))  12.2 us
    ppermute x2, waiting for transfers between devices, tensor_sum(): return values + across(values)  9.31 us
  transfers between devices with their start and end apart: 31, of which 19 were waited for; matrix products, arithmetic and copies ran while one was open for 3% of the time, Pallas kernels for 26%

profile of v6, /device:TPU:0, one launch (start us, length us, event | category | flops | bytes accessed | tf_op | source)
XLA Modules:
  0.0 213.4 jit_solution(10586290202256073213)
XLA Ops:
  0.5 1.5 slice.46
  1.9 2.5 %collective-permute-start.1 = (bf16[128,3584]{1,0:T(8,128)(2,1)S(1)}, bf16[128,3584]{1,0:T(8,128)(2,1)S(1)}, u32[]{:S(2)}, u32[]{:S(2)}) collective-permute-start(bf16[128,3584]{1,0:T(8,128)(2,1)S(1)} %bitcast.46), channel_id=1, source_target_pairs={{0,2},{1,3},{2,0},{3,1},{4,6},{5,7},{6,4},{7,5},{8,10},{9,11},{10,... | collective-permute-start | bytes 2752520 | tf_op jit(solution)/shard_map/ppermute | solution.py:533
  4.4 1.6 collective-permute-start.4
  6.0 2.6 %collective-permute-start = (bf16[128,2048]{1,0:T(8,128)(2,1)}, bf16[128,2048]{1,0:T(8,128)(2,1)S(1)}, u32[]{:S(2)}, u32[]{:S(2)}) collective-permute-start(bf16[128,2048]{1,0:T(8,128)(2,1)} %bitcast.35), channel_id=1, source_target_pairs={{0,8},{4,12},{8,0},{12,4},{1,9},{5,13},{9,1},{13,5},{2,10},{6,14},... | collective-permute-start | bytes 1572872 | tf_op jit(solution)/shard_map/ppermute | solution.py:516
  8.6 21.2 %collective-permute-done.4.b1 = bf16[128,2048]{1,0:T(8,128)(2,1)S(1)} collective-permute-done((bf16[128,2048]{1,0:T(8,128)(2,1)}, bf16[128,2048]{1,0:T(8,128)(2,1)S(1)}, u32[]{:S(2)}, u32[]{:S(2)}) %collective-permute-start.4) | collective-permute-done | bytes 524320 | tf_op jit(solution)/shard_map/ppermute | solution.py:516
  29.8 2.4 %collective-permute-done.b3.b4 = bf16[128,2048]{1,0:T(8,128)(2,1)S(1)} collective-permute-done((bf16[128,2048]{1,0:T(8,128)(2,1)}, bf16[128,2048]{1,0:T(8,128)(2,1)S(1)}, u32[]{:S(2)}, u32[]{:S(2)}) %collective-permute-start) | collective-permute-done | bytes 524320 | tf_op jit(solution)/shard_map/ppermute | solution.py:516
  34.6 1.1 fusion.1
  35.7 1.1 collective-permute-start.10
  36.8 9.1 %collective-permute-start.2 = (bf16[128,2048]{1,0:T(8,128)(2,1)}, bf16[128,2048]{1,0:T(8,128)(2,1)S(1)}, u32[]{:S(2)}, u32[]{:S(2)}) collective-permute-start(bf16[128,2048]{1,0:T(8,128)(2,1)} %bitcast.10.b0), channel_id=1, source_target_pairs={{0,8},{4,12},{8,0},{12,4},{1,9},{5,13},{9,1},{13,5},{2,10},{6,14},... | collective-permute-start | bytes 1572872 | tf_op jit(solution)/shard_map/ppermute | solution.py:516
  45.9 12.2 %collective-permute-done.6.b5 = bf16[128,2048]{1,0:T(8,128)(2,1)S(1)} collective-permute-done((bf16[128,2048]{1,0:T(8,128)(2,1)S(1)}, bf16[128,2048]{1,0:T(8,128)(2,1)S(1)}, u32[]{:S(2)}, u32[]{:S(2)}) %collective-permute-start.6) | collective-permute-done | bytes 524320 | tf_op jit(solution)/shard_map/ppermute | solution.py:520
  60.7 6.2 %collective-permute-done.2.b3.b4 = bf16[128,2048]{1,0:T(8,128)(2,1)S(1)} collective-permute-done((bf16[128,2048]{1,0:T(8,128)(2,1)}, bf16[128,2048]{1,0:T(8,128)(2,1)S(1)}, u32[]{:S(2)}, u32[]{:S(2)}) %collective-permute-start.2) | collective-permute-done | bytes 524320 | tf_op jit(solution)/shard_map/ppermute | solution.py:516
  66.9 2.1 collective-permute-done.10.b1
  69.0 1.3 collective-permute-start.11
  70.3 1.2 copy-done.12
  71.5 1.2 copy-done.26
  72.7 1.0 copy-done.31
  76.7 3.8 %shard_map.154 = (f32[384,128]{1,0:T(8,128)S(1)}, f32[384,64]{1,0:T(8,128)S(1)}) custom-call(bf16[256,2048]{1,0:T(8,128)(2,1)S(1)} %bitcast.44, bf16[128,2048]{1,0:T(8,128)(2,1)S(1)} %bitcast.45, bf16[256,2048]{1,0:T(8,128)(2,1)S(1)} %bitcast.39, bf16[128,2048]{1,0:T(8,128)(2,1)S(1)} %bitcast.37, bf16[64,2048]{1,0:T(8,128)(2,1)S(1)} %copy-done.33, ...), custom_call_target="tpu_custom_call" | custom-call | flops 1024 | bytes 1024 | tf_op jit(solution)/shard_map/pallas_call | solution.py:350
  80.5 2.3 %collective-permute-start.14 = (bf16[128,2048]{1,0:T(8,128)(2,1)}, bf16[128,2048]{1,0:T(8,128)(2,1)}, u32[]{:S(2)}, u32[]{:S(2)}) collective-permute-start(bf16[128,2048]{1,0:T(8,128)(2,1)} %bitcast.9.b0), channel_id=1, source_target_pairs={{0,4},{4,0},{8,12},{12,8},{1,5},{5,1},{9,13},{13,9},{2,6},{6,2},{1... | collective-permute-start | bytes 1572872 | tf_op jit(solution)/shard_map/ppermute | solution.py:516
  85.7 1.1 pad_maximum_fusion.1
  87.9 1.0 copy-done.5
  88.9 1.0 copy-done.15
  91.0 1.0 copy-done.19
  92.1 1.2 copy-done.28
  93.3 12.0 %shard_map.155 = (f32[3584,128]{1,0:T(8,128)S(1)}, bf16[3584,128]{1,0:T(8,128)(2,1)S(1)}) custom-call(s32[2]{0:T(128)S(1)} %pad_add_fusion.flags, bf16[128,2048]{1,0:T(8,128)(2,1)S(1)} %bitcast.38, bf16[128,2048]{1,0:T(8,128)(2,1)S(1)} %copy-done.15, bf16[128,2048]{1,0:T(8,128)(2,1)S(1)} %copy-done.17, bf16[128,2048]{1,0:T(8,128)(2,1)S(1)} %collective-permute-done.b3.b4, ...), custom_call_target="tpu_custom_call" | custom-call | flops 1024 | bytes 1024 | tf_op jit(solution)/shard_map/pallas_call | solution.py:234
  105.3 2.8 %collective-permute-done.3.b3.b4 = bf16[128,2048]{1,0:T(8,128)(2,1)S(1)} collective-permute-done((bf16[128,2048]{1,0:T(8,128)(2,1)}, bf16[128,2048]{1,0:T(8,128)(2,1)S(1)}, u32[]{:S(2)}, u32[]{:S(2)}) %collective-permute-start.3) | collective-permute-done | bytes 524320 | tf_op jit(solution)/shard_map/ppermute | solution.py:516
  109.4 1.2 collective-permute-done.16.far
  110.6 13.7 %shard_map.156 = (f32[3584,128]{1,0:T(8,128)S(1)}, bf16[3584,128]{1,0:T(8,128)(2,1)S(1)}) custom-call(s32[2]{0:T(128)S(1)} %pad_add_fusion.flags, bf16[128,2048]{1,0:T(8,128)(2,1)} %bitcast.10.b0, bf16[128,2048]{1,0:T(8,128)(2,1)S(1)} %copy-done.21, bf16[128,2048]{1,0:T(8,128)(2,1)S(1)} %copy-done.25, bf16[128,2048]{1,0:T(8,128)(2,1)S(1)} %collective-permute-done.2.b3.b4, ...), custom_call_target="tpu_custom_call" | custom-call | flops 1024 | bytes 1024 | tf_op jit(solution)/shard_map/pallas_call | solution.py:234
  124.7 2.2 %collective-permute-start.20 = (bf16[2,128,2048]{2,1,0:T(8,128)(2,1)S(1)}, bf16[2,128,2048]{2,1,0:T(8,128)(2,1)S(1)}, u32[]{:S(2)}, u32[]{:S(2)}) collective-permute-start(bf16[2,128,2048]{2,1,0:T(8,128)(2,1)S(1)} %pad_maximum_fusion.2), channel_id=1, source_target_pairs={{0,2},{1,3},{2,0},{3,1},{4,6},{5,7},{6,4},{7,5},{8,10},{9,11},{10,... | collective-permute-start | bytes 3145736 | tf_op jit(solution)/shard_map/ppermute | solution.py:557
  126.9 1.2 collective-permute-start.17
  128.1 4.0 %collective-permute-done.21.returned = bf16[3584,128]{1,0:T(8,128)(2,1)S(1)} collective-permute-done((bf16[3584,128]{1,0:T(8,128)(2,1)S(1)}, bf16[3584,128]{1,0:T(8,128)(2,1)S(1)}, u32[]{:S(2)}, u32[]{:S(2)}) %collective-permute-start.21) | collective-permute-done | bytes 917536 | tf_op jit(solution)/shard_map/ppermute | solution.py:552
  132.2 2.9 %shard_map.158 = f32[128,128]{1,0:T(8,128)S(1)} custom-call(f32[3584,128]{1,0:T(8,128)S(1)} %get-tuple-element.50.near_sum, bf16[3584,128]{1,0:T(8,128)(2,1)S(1)} %collective-permute-done.21.returned, bf16[128,3584]{1,0:T(8,128)(2,1)S(1)} %bitcast.41, bf16[128,3584]{1,0:T(8,128)(2,1)S(1)} %bitcast.43, bf16[64,3584]{1,0:T(8,128)(2,1)S(1)} %copy-done.8, ...), custom_call_target="tpu_custom_call" | custom-call | flops 1024 | bytes 1024 | tf_op jit(solution)/shard_map/pallas_call | solution.py:261
  135.1 1.3 collective-permute-start.22
  137.7 3.2 %collective-permute-done.22 = f32[128,192]{1,0:T(8,128)S(1)} collective-permute-done((f32[128,192]{1,0:T(8,128)S(1)}, f32[128,192]{1,0:T(8,128)S(1)}, u32[]{:S(2)}, u32[]{:S(2)}) %collective-permute-start.22) | collective-permute-done | bytes 98336 | tf_op jit(solution)/shard_map/ppermute | solution.py:503
  140.9 2.5 %collective-permute-start.23 = (f32[128,192]{1,0:T(8,128)S(1)}, f32[128,192]{1,0:T(8,128)S(1)}, u32[]{:S(2)}, u32[]{:S(2)}) collective-permute-start(f32[128,192]{1,0:T(8,128)S(1)} %fusion), channel_id=1, source_target_pairs={{0,8},{4,12},{8,0},{12,4},{1,9},{5,13},{9,1},{13,5},{2,10},{6,14},... | collective-permute-start | bytes 294920 | tf_op jit(solution)/shard_map/ppermute | solution.py:504
  143.4 7.7 %collective-permute-done.18 = f32[384,128]{1,0:T(8,128)S(1)} collective-permute-done((f32[384,128]{1,0:T(8,128)S(1)}, f32[384,128]{1,0:T(8,128)S(1)}, u32[]{:S(2)}, u32[]{:S(2)}) %collective-permute-start.18) | collective-permute-done | bytes 196640 | tf_op jit(solution)/shard_map/ppermute | solution.py:504
  151.1 1.6 collective-permute-done.23
  153.7 1.4 collective-permute-start.25
  155.2 1.3 collective-permute-start.26
  156.5 22.0 %collective-permute-done.25.q2 = f32[2,192,64]{2,1,0:T(8,128)S(1)} collective-permute-done((f32[2,192,64]{2,1,0:T(8,128)S(1)}, f32[2,192,64]{2,1,0:T(8,128)S(1)}, u32[]{:S(2)}, u32[]{:S(2)}) %collective-permute-start.25) | collective-permute-done | bytes 98336 | tf_op jit(solution)/shard_map/ppermute | solution.py:568
  178.5 3.0 %collective-permute-done.26.q3 = f32[2,192,64]{2,1,0:T(8,128)S(1)} collective-permute-done((f32[2,192,64]{2,1,0:T(8,128)S(1)}, f32[2,192,64]{2,1,0:T(8,128)S(1)}, u32[]{:S(2)}, u32[]{:S(2)}) %collective-permute-start.26) | collective-permute-done | bytes 98336 | tf_op jit(solution)/shard_map/ppermute | solution.py:568
  181.5 18.6 %shard_map.160 = f32[256,128]{1,0:T(8,128)S(1)} custom-call(s32[2]{0:T(128)S(1)} %pad_add_fusion.flags, bf16[128,2048]{1,0:T(8,128)(2,1)} %bitcast.9.b0, bf16[128,2048]{1,0:T(8,128)(2,1)} %collective-permute-done.14.b1, bf16[128,2048]{1,0:T(8,128)(2,1)S(1)} %collective-permute-done.13.b2, bf16[128,2048]{1,0:T(8,128)(2,1)S(1)} %collective-permute-done.3.b3.b4, ...), custom_call_target="tpu_custom_call" | custom-call | flops 1024 | bytes 1024 | tf_op jit(solution)/shard_map/pallas_call | solution.py:288
  200.3 2.9 %shard_map.157.early = f32[128,128]{1,0:T(8,128)S(1)} custom-call(f32[3584,128]{1,0:T(8,128)S(1)} %get-tuple-element.49.near_sum, bf16[3584,128]{1,0:T(8,128)(2,1)S(1)} %collective-permute-done.19.returned, bf16[256,3584]{1,0:T(8,128)(2,1)S(1)} %bitcast.30, bf16[256,3584]{1,0:T(8,128)(2,1)S(1)} %bitcast.33, bf16[64,3584]{1,0:T(8,128)(2,1)S(1)} %copy-done.8, ...), custom_call_target="tpu_custom_call" | custom-call | flops 1024 | bytes 1024 | tf_op jit(solution)/shard_map/pallas_call | solution.py:261
  203.2 1.3 collective-permute-done.27.far
  204.5 1.4 shard_map.161
  205.9 1.2 collective-permute-start.30
  207.1 2.1 collective-permute-start.29
  209.2 1.2 collective-permute-start.28
  211.6 1.2 collective-permute-done.28
  (125 shorter events, 19.2 us)
Async XLA Ops:
  0.0 33.1 %copy-start.1 = (bf16[4,64,3584]{2,1,0:T(8,128)(2,1)S(1)}, bf16[4,64,3584]{2,1,0:T(8,128)(2,1)}, u32[]{:S(2)}) copy-start(bf16[4,64,3584]{2,1,0:T(8,128)(2,1)} %param.18) | copy-start | bytes 5505028
  0.0 34.6 %copy-start.6 = (bf16[4,64,2048]{2,1,0:T(8,128)(2,1)S(1)}, bf16[4,64,2048]{2,1,0:T(8,128)(2,1)}, u32[]{:S(2)}) copy-start(bf16[4,64,2048]{2,1,0:T(8,128)(2,1)} %param.19) | copy-start | bytes 3145732
  0.0 87.9 %collective-permute-start.12 = (bf16[3584,2048]{1,0:T(8,128)(2,1)}, bf16[3584,2048]{1,0:T(8,128)(2,1)}, u32[]{:S(2)}, u32[]{:S(2)}) collective-permute-start(bf16[3584,2048]{1,0:T(8,128)(2,1)} %weight_own.5), channel_id=1, source_target_pairs={{0,1},{1,0},{2,3},{3,2},{4,5},{5,4},{6,7},{7,6},{8,9},{9,8},{10,11... | collective-permute-start | bytes 44040200 | tf_op jit(solution)/shard_map/ppermute | solution.py:531
  1.9 32.2 %collective-permute-start.1 = (bf16[128,3584]{1,0:T(8,128)(2,1)S(1)}, bf16[128,3584]{1,0:T(8,128)(2,1)S(1)}, u32[]{:S(2)}, u32[]{:S(2)}) collective-permute-start(bf16[128,3584]{1,0:T(8,128)(2,1)S(1)} %bitcast.46), channel_id=1, source_target_pairs={{0,2},{1,3},{2,0},{3,1},{4,6},{5,7},{6,4},{7,5},{8,10},{9,11},{10,... | collective-permute-start | bytes 2752520 | tf_op jit(solution)/shard_map/ppermute | solution.py:533
  4.4 53.8 %copy-start.4 = (bf16[2,64,2048]{2,1,0:T(8,128)(2,1)S(1)}, bf16[2,64,2048]{2,1,0:T(8,128)(2,1)}, u32[]{:S(2)}) copy-start(bf16[2,64,2048]{2,1,0:T(8,128)(2,1)} %param.24) | copy-start | bytes 1572868
  4.4 25.4 %collective-permute-start.4 = (bf16[128,2048]{1,0:T(8,128)(2,1)}, bf16[128,2048]{1,0:T(8,128)(2,1)S(1)}, u32[]{:S(2)}, u32[]{:S(2)}) collective-permute-start(bf16[128,2048]{1,0:T(8,128)(2,1)} %bitcast.34), channel_id=1, source_target_pairs={{0,4},{4,0},{8,12},{12,8},{1,5},{5,1},{9,13},{13,9},{2,6},{6,2},{1... | collective-permute-start | bytes 1572872 | tf_op jit(solution)/shard_map/ppermute | solution.py:516
  6.0 26.2 %collective-permute-start = (bf16[128,2048]{1,0:T(8,128)(2,1)}, bf16[128,2048]{1,0:T(8,128)(2,1)S(1)}, u32[]{:S(2)}, u32[]{:S(2)}) collective-permute-start(bf16[128,2048]{1,0:T(8,128)(2,1)} %bitcast.35), channel_id=1, source_target_pairs={{0,8},{4,12},{8,0},{12,4},{1,9},{5,13},{9,1},{13,5},{2,10},{6,14},... | collective-permute-start | bytes 1572872 | tf_op jit(solution)/shard_map/ppermute | solution.py:516
  29.8 28.4 %copy-start.14 = (bf16[128,2048]{1,0:T(8,128)(2,1)}, bf16[128,2048]{1,0:T(8,128)(2,1)S(1)}, u32[]{:S(2)}) copy-start(bf16[128,2048]{1,0:T(8,128)(2,1)S(1)} %collective-permute-done.4.b1) | copy-start | bytes 1572868
  32.2 4.6 %collective-permute-start.5 = (bf16[128,2048]{1,0:T(8,128)(2,1)}, bf16[128,2048]{1,0:T(8,128)(2,1)S(1)}, u32[]{:S(2)}, u32[]{:S(2)}) collective-permute-start(bf16[128,2048]{1,0:T(8,128)(2,1)} %bitcast.36), channel_id=1, source_target_pairs={{0,1},{1,0},{2,3},{3,2},{4,8},{5,9},{6,10},{7,11},{8,4},{9,5},{10,... | collective-permute-start | bytes 1572872 | tf_op jit(solution)/shard_map/ppermute | solution.py:519
  32.2 26.0 %collective-permute-start.6 = (bf16[128,2048]{1,0:T(8,128)(2,1)S(1)}, bf16[128,2048]{1,0:T(8,128)(2,1)S(1)}, u32[]{:S(2)}, u32[]{:S(2)}) collective-permute-start(bf16[128,2048]{1,0:T(8,128)(2,1)S(1)} %collective-permute-done.b3.b4), channel_id=1, source_target_pairs={{0,4},{4,0},{8,12},{12,8},{1,5},{5,1},{9,13},{13,9},{2,6},{6,2},{1... | collective-permute-start | bytes 1572872 | tf_op jit(solution)/shard_map/ppermute | solution.py:520
  34.1 26.0 %collective-permute-start.7 = (bf16[128,3584]{1,0:T(8,128)(2,1)}, bf16[128,3584]{1,0:T(8,128)(2,1)}, u32[]{:S(2)}, u32[]{:S(2)}) collective-permute-start(bf16[128,3584]{1,0:T(8,128)(2,1)} %bitcast.16), channel_id=1, source_target_pairs={{0,2},{1,3},{2,0},{3,1},{4,6},{5,7},{6,4},{7,5},{8,10},{9,11},{10,... | collective-permute-start | bytes 2752520 | tf_op jit(solution)/shard_map/ppermute | solution.py:541
  35.7 33.3 %collective-permute-start.10 = (bf16[128,2048]{1,0:T(8,128)(2,1)}, bf16[128,2048]{1,0:T(8,128)(2,1)S(1)}, u32[]{:S(2)}, u32[]{:S(2)}) collective-permute-start(bf16[128,2048]{1,0:T(8,128)(2,1)} %bitcast.10.b0), channel_id=1, source_target_pairs={{0,4},{4,0},{8,12},{12,8},{1,5},{5,1},{9,13},{13,9},{2,6},{6,2},{1... | collective-permute-start | bytes 1572872 | tf_op jit(solution)/shard_map/ppermute | solution.py:516
  36.8 30.1 %collective-permute-start.2 = (bf16[128,2048]{1,0:T(8,128)(2,1)}, bf16[128,2048]{1,0:T(8,128)(2,1)S(1)}, u32[]{:S(2)}, u32[]{:S(2)}) collective-permute-start(bf16[128,2048]{1,0:T(8,128)(2,1)} %bitcast.10.b0), channel_id=1, source_target_pairs={{0,8},{4,12},{8,0},{12,4},{1,9},{5,13},{9,1},{13,5},{2,10},{6,14},... | collective-permute-start | bytes 1572872 | tf_op jit(solution)/shard_map/ppermute | solution.py:516
  58.2 12.1 %copy-start.2 = (bf16[4,64,3584]{2,1,0:T(8,128)(2,1)S(1)}, bf16[4,64,3584]{2,1,0:T(8,128)(2,1)}, u32[]{:S(2)}) copy-start(bf16[4,64,3584]{2,1,0:T(8,128)(2,1)} %param.18) | copy-start | bytes 5505028
  58.2 12.1 %copy-start.7 = (bf16[4,64,2048]{2,1,0:T(8,128)(2,1)S(1)}, bf16[4,64,2048]{2,1,0:T(8,128)(2,1)}, u32[]{:S(2)}) copy-start(bf16[4,64,2048]{2,1,0:T(8,128)(2,1)} %param.19) | copy-start | bytes 3145732
  58.2 12.1 %copy-start.10 = (bf16[2,64,3584]{2,1,0:T(8,128)(2,1)S(1)}, bf16[2,64,3584]{2,1,0:T(8,128)(2,1)}, u32[]{:S(2)}) copy-start(bf16[2,64,3584]{2,1,0:T(8,128)(2,1)} %param.22) | copy-start | bytes 2752516
  60.0 10.3 %copy-start = (bf16[4,64,3584]{2,1,0:T(8,128)(2,1)S(1)}, bf16[4,64,3584]{2,1,0:T(8,128)(2,1)}, u32[]{:S(2)}) copy-start(bf16[4,64,3584]{2,1,0:T(8,128)(2,1)} %param.17) | copy-start | bytes 5505028
  60.1 24.5 %collective-permute-start.8 = (bf16[2,128,2048]{2,1,0:T(8,128)(2,1)S(1)}, bf16[2,128,2048]{2,1,0:T(8,128)(2,1)S(1)}, u32[]{:S(2)}, u32[]{:S(2)}) collective-permute-start(bf16[2,128,2048]{2,1,0:T(8,128)(2,1)S(1)} %pad_maximum_fusion), channel_id=1, source_target_pairs={{0,2},{1,3},{2,0},{3,1},{4,6},{5,7},{6,4},{7,5},{8,10},{9,11},{10,... | collective-permute-start | bytes 3145736 | tf_op jit(solution)/shard_map/ppermute | solution.py:543
  69.0 15.5 %copy-start.20 = (bf16[128,2048]{1,0:T(8,128)(2,1)}, bf16[128,2048]{1,0:T(8,128)(2,1)S(1)}, u32[]{:S(2)}) copy-start(bf16[128,2048]{1,0:T(8,128)(2,1)S(1)} %collective-permute-done.10.b1) | copy-start | bytes 1572868
  69.0 13.9 %collective-permute-start.11 = (bf16[128,2048]{1,0:T(8,128)(2,1)S(1)}, bf16[128,2048]{1,0:T(8,128)(2,1)S(1)}, u32[]{:S(2)}, u32[]{:S(2)}) collective-permute-start(bf16[128,2048]{1,0:T(8,128)(2,1)S(1)} %collective-permute-done.2.b3.b4), channel_id=1, source_target_pairs={{0,4},{4,0},{8,12},{12,8},{1,5},{5,1},{9,13},{13,9},{2,6},{6,2},{1... | collective-permute-start | bytes 1572872 | tf_op jit(solution)/shard_map/ppermute | solution.py:520
  70.3 14.3 %collective-permute-start.9 = (bf16[128,2048]{1,0:T(8,128)(2,1)}, bf16[128,2048]{1,0:T(8,128)(2,1)S(1)}, u32[]{:S(2)}, u32[]{:S(2)}) collective-permute-start(bf16[128,2048]{1,0:T(8,128)(2,1)} %bitcast.10.b0), channel_id=1, source_target_pairs={{0,1},{1,0},{2,3},{3,2},{4,8},{5,9},{6,10},{7,11},{8,4},{9,5},{10,... | collective-permute-start | bytes 1572872 | tf_op jit(solution)/shard_map/ppermute | solution.py:519
  80.5 27.6 %collective-permute-start.14 = (bf16[128,2048]{1,0:T(8,128)(2,1)}, bf16[128,2048]{1,0:T(8,128)(2,1)}, u32[]{:S(2)}, u32[]{:S(2)}) collective-permute-start(bf16[128,2048]{1,0:T(8,128)(2,1)} %bitcast.9.b0), channel_id=1, source_target_pairs={{0,4},{4,0},{8,12},{12,8},{1,5},{5,1},{9,13},{13,9},{2,6},{6,2},{1... | collective-permute-start | bytes 1572872 | tf_op jit(solution)/shard_map/ppermute | solution.py:516
  82.9 25.3 %collective-permute-start.3 = (bf16[128,2048]{1,0:T(8,128)(2,1)}, bf16[128,2048]{1,0:T(8,128)(2,1)S(1)}, u32[]{:S(2)}, u32[]{:S(2)}) collective-permute-start(bf16[128,2048]{1,0:T(8,128)(2,1)} %bitcast.9.b0), channel_id=1, source_target_pairs={{0,8},{4,12},{8,0},{12,4},{1,9},{5,13},{9,1},{13,5},{2,10},{6,14},... | collective-permute-start | bytes 1572872 | tf_op jit(solution)/shard_map/ppermute | solution.py:516
  86.8 23.8 %collective-permute-start.16 = (bf16[2,128,2048]{2,1,0:T(8,128)(2,1)}, bf16[2,128,2048]{2,1,0:T(8,128)(2,1)}, u32[]{:S(2)}, u32[]{:S(2)}) collective-permute-start(bf16[2,128,2048]{2,1,0:T(8,128)(2,1)} %pad_maximum_fusion.1), channel_id=1, source_target_pairs={{0,2},{1,3},{2,0},{3,1},{4,6},{5,7},{6,4},{7,5},{8,10},{9,11},{10,... | collective-permute-start | bytes 3145736 | tf_op jit(solution)/shard_map/ppermute | solution.py:548
  93.3 17.3 %copy-start.21 = (bf16[128,2048]{1,0:T(8,128)(2,1)S(1)}, bf16[128,2048]{1,0:T(8,128)(2,1)}, u32[]{:S(2)}) copy-start(bf16[128,2048]{1,0:T(8,128)(2,1)} %copy-done.20) | copy-start | bytes 1572868
  93.3 17.3 %copy-start.23 = (bf16[128,2048]{1,0:T(8,128)(2,1)S(1)}, bf16[128,2048]{1,0:T(8,128)(2,1)}, u32[]{:S(2)}) copy-start(bf16[128,2048]{1,0:T(8,128)(2,1)} %copy-done.22) | copy-start | bytes 1572868
  93.3 17.3 %copy-start.25 = (bf16[128,2048]{1,0:T(8,128)(2,1)S(1)}, bf16[128,2048]{1,0:T(8,128)(2,1)}, u32[]{:S(2)}) copy-start(bf16[128,2048]{1,0:T(8,128)(2,1)} %copy-done.24) | copy-start | bytes 1572868
  108.2 16.2 %collective-permute-start.13 = (bf16[128,2048]{1,0:T(8,128)(2,1)}, bf16[128,2048]{1,0:T(8,128)(2,1)S(1)}, u32[]{:S(2)}, u32[]{:S(2)}) collective-permute-start(bf16[128,2048]{1,0:T(8,128)(2,1)} %bitcast.9.b0), channel_id=1, source_target_pairs={{0,1},{1,0},{2,3},{3,2},{4,8},{5,9},{6,10},{7,11},{8,4},{9,5},{10,... | collective-permute-start | bytes 1572872 | tf_op jit(solution)/shard_map/ppermute | solution.py:519
  108.2 16.2 %collective-permute-start.15 = (bf16[128,2048]{1,0:T(8,128)(2,1)S(1)}, bf16[128,2048]{1,0:T(8,128)(2,1)S(1)}, u32[]{:S(2)}, u32[]{:S(2)}) collective-permute-start(bf16[128,2048]{1,0:T(8,128)(2,1)S(1)} %collective-permute-done.3.b3.b4), channel_id=1, source_target_pairs={{0,4},{4,0},{8,12},{12,8},{1,5},{5,1},{9,13},{13,9},{2,6},{6,2},{1... | collective-permute-start | bytes 1572872 | tf_op jit(solution)/shard_map/ppermute | solution.py:520
  108.9 23.2 %collective-permute-start.21 = (bf16[3584,128]{1,0:T(8,128)(2,1)S(1)}, bf16[3584,128]{1,0:T(8,128)(2,1)S(1)}, u32[]{:S(2)}, u32[]{:S(2)}) collective-permute-start(bf16[3584,128]{1,0:T(8,128)(2,1)S(1)} %get-tuple-element.41), channel_id=1, source_target_pairs={{0,2},{1,3},{2,0},{3,1},{4,6},{5,7},{6,4},{7,5},{8,10},{9,11},{10,... | collective-permute-start | bytes 2752520 | tf_op jit(solution)/shard_map/ppermute | solution.py:552
  124.3 7.8 %copy-start.13 = (bf16[2,64,3584]{2,1,0:T(8,128)(2,1)S(1)}, bf16[2,64,3584]{2,1,0:T(8,128)(2,1)}, u32[]{:S(2)}) copy-start(bf16[2,64,3584]{2,1,0:T(8,128)(2,1)} %param.23) | copy-start | bytes 2752516
  124.6 7.6 %copy-start.8 = (bf16[64,3584]{1,0:T(8,128)(2,1)S(1)}, bf16[64,3584]{1,0:T(8,128)(2,1)}, u32[]{:S(2)}) copy-start(bf16[64,3584]{1,0:T(8,128)(2,1)} %proj_gate.5) | copy-start | bytes 1376260
  124.7 56.8 %collective-permute-start.20 = (bf16[2,128,2048]{2,1,0:T(8,128)(2,1)S(1)}, bf16[2,128,2048]{2,1,0:T(8,128)(2,1)S(1)}, u32[]{:S(2)}, u32[]{:S(2)}) collective-permute-start(bf16[2,128,2048]{2,1,0:T(8,128)(2,1)S(1)} %pad_maximum_fusion.2), channel_id=1, source_target_pairs={{0,2},{1,3},{2,0},{3,1},{4,6},{5,7},{6,4},{7,5},{8,10},{9,11},{10,... | collective-permute-start | bytes 3145736 | tf_op jit(solution)/shard_map/ppermute | solution.py:557
  126.9 10.0 %collective-permute-start.17 = (f32[384,128]{1,0:T(8,128)S(1)}, f32[384,128]{1,0:T(8,128)S(1)}, u32[]{:S(2)}, u32[]{:S(2)}) collective-permute-start(f32[384,128]{1,0:T(8,128)S(1)} %copy-done.38), channel_id=1, source_target_pairs={{0,4},{4,0},{8,12},{12,8},{1,5},{5,1},{9,13},{13,9},{2,6},{6,2},{1... | collective-permute-start | bytes 589832 | tf_op jit(solution)/shard_map/ppermute | solution.py:503
  132.2 20.6 %copy-start.39 = (s32[2]{0:T(128)S(1)}, s32[2]{0:T(128)}, u32[]{:S(2)}) copy-start(s32[2]{0:T(128)} %lengths.2) | copy-start | bytes 28
  135.1 46.4 %copy-start.3 = (bf16[4,64,3584]{2,1,0:T(8,128)(2,1)S(1)}, bf16[4,64,3584]{2,1,0:T(8,128)(2,1)}, u32[]{:S(2)}) copy-start(bf16[4,64,3584]{2,1,0:T(8,128)(2,1)} %param.18) | copy-start | bytes 5505028
  135.1 46.4 %copy-start.30 = (bf16[128,3584]{1,0:T(8,128)(2,1)S(1)}, bf16[128,3584]{1,0:T(8,128)(2,1)}, u32[]{:S(2)}) copy-start(bf16[128,3584]{1,0:T(8,128)(2,1)} %copy-done.29) | copy-start | bytes 2752516
  135.1 5.8 %collective-permute-start.22 = (f32[128,192]{1,0:T(8,128)S(1)}, f32[128,192]{1,0:T(8,128)S(1)}, u32[]{:S(2)}, u32[]{:S(2)}) collective-permute-start(f32[128,192]{1,0:T(8,128)S(1)} %pad_maximum_fusion.3), channel_id=1, source_target_pairs={{0,4},{4,0},{8,12},{12,8},{1,5},{5,1},{9,13},{13,9},{2,6},{6,2},{1... | collective-permute-start | bytes 294920 | tf_op jit(solution)/shard_map/ppermute | solution.py:503
  136.4 63.9 %collective-permute-start.19 = (bf16[3584,128]{1,0:T(8,128)(2,1)S(1)}, bf16[3584,128]{1,0:T(8,128)(2,1)S(1)}, u32[]{:S(2)}, u32[]{:S(2)}) collective-permute-start(bf16[3584,128]{1,0:T(8,128)(2,1)S(1)} %get-tuple-element.45), channel_id=1, source_target_pairs={{0,2},{1,3},{2,0},{3,1},{4,6},{5,7},{6,4},{7,5},{8,10},{9,11},{10,... | collective-permute-start | bytes 2752520 | tf_op jit(solution)/shard_map/ppermute | solution.py:555
  137.0 14.1 %collective-permute-start.18 = (f32[384,128]{1,0:T(8,128)S(1)}, f32[384,128]{1,0:T(8,128)S(1)}, u32[]{:S(2)}, u32[]{:S(2)}) collective-permute-start(f32[384,128]{1,0:T(8,128)S(1)} %add.32), channel_id=1, source_target_pairs={{0,8},{4,12},{8,0},{12,4},{1,9},{5,13},{9,1},{13,5},{2,10},{6,14},... | collective-permute-start | bytes 589832 | tf_op jit(solution)/shard_map/ppermute | solution.py:504
  140.9 11.8 %collective-permute-start.23 = (f32[128,192]{1,0:T(8,128)S(1)}, f32[128,192]{1,0:T(8,128)S(1)}, u32[]{:S(2)}, u32[]{:S(2)}) collective-permute-start(f32[128,192]{1,0:T(8,128)S(1)} %fusion), channel_id=1, source_target_pairs={{0,8},{4,12},{8,0},{12,4},{1,9},{5,13},{9,1},{13,5},{2,10},{6,14},... | collective-permute-start | bytes 294920 | tf_op jit(solution)/shard_map/ppermute | solution.py:504
  153.7 1.5 collective-permute-start.24
  153.7 24.8 %collective-permute-start.25 = (f32[2,192,64]{2,1,0:T(8,128)S(1)}, f32[2,192,64]{2,1,0:T(8,128)S(1)}, u32[]{:S(2)}, u32[]{:S(2)}) collective-permute-start(f32[2,192,64]{2,1,0:T(8,128)S(1)} %shard_map.159.q0), channel_id=1, source_target_pairs={{0,2},{1,3},{2,0},{3,1},{4,6},{5,7},{6,4},{7,5},{8,10},{9,11},{10,... | collective-permute-start | bytes 294920 | tf_op jit(solution)/shard_map/ppermute | solution.py:568
  155.2 26.3 %collective-permute-start.26 = (f32[2,192,64]{2,1,0:T(8,128)S(1)}, f32[2,192,64]{2,1,0:T(8,128)S(1)}, u32[]{:S(2)}, u32[]{:S(2)}) collective-permute-start(f32[2,192,64]{2,1,0:T(8,128)S(1)} %collective-permute-done.24.q1), channel_id=1, source_target_pairs={{0,2},{1,3},{2,0},{3,1},{4,6},{5,7},{6,4},{7,5},{8,10},{9,11},{10,... | collective-permute-start | bytes 294920 | tf_op jit(solution)/shard_map/ppermute | solution.py:568
  200.2 4.3 %collective-permute-start.27 = (f32[128,128]{1,0:T(8,128)S(1)}, f32[128,128]{1,0:T(8,128)S(1)}, u32[]{:S(2)}, u32[]{:S(2)}) collective-permute-start(f32[128,128]{1,0:T(8,128)S(1)} %get-tuple-element.61), channel_id=1, source_target_pairs={{0,2},{1,3},{2,0},{3,1},{4,6},{5,7},{6,4},{7,5},{8,10},{9,11},{10,... | collective-permute-start | bytes 196616 | tf_op jit(solution)/shard_map/ppermute | solution.py:576
  205.9 5.4 %collective-permute-start.30 = (f32[4,8]{1,0:T(4,128)S(1)}, f32[4,8]{1,0:T(4,128)S(1)}, u32[]{:S(2)}, u32[]{:S(2)}) collective-permute-start(f32[4,8]{1,0:T(4,128)S(1)} %shard_map.161), channel_id=1, source_target_pairs={{0,12},{4,8},{8,4},{12,0},{1,13},{5,9},{9,5},{13,1},{2,14},{6,10},... | collective-permute-start | bytes 392 | tf_op jit(solution)/shard_map/ppermute | solution.py:578
  207.1 4.5 %collective-permute-start.29 = (f32[4,8]{1,0:T(4,128)S(1)}, f32[4,8]{1,0:T(4,128)S(1)}, u32[]{:S(2)}, u32[]{:S(2)}) collective-permute-start(f32[4,8]{1,0:T(4,128)S(1)} %shard_map.161), channel_id=1, source_target_pairs={{0,8},{4,12},{8,0},{12,4},{1,9},{5,13},{9,1},{13,5},{2,10},{6,14},... | collective-permute-start | bytes 392 | tf_op jit(solution)/shard_map/ppermute | solution.py:578
  209.2 3.6 %collective-permute-start.28 = (f32[4,8]{1,0:T(4,128)S(1)}, f32[4,8]{1,0:T(4,128)S(1)}, u32[]{:S(2)}, u32[]{:S(2)}) collective-permute-start(f32[4,8]{1,0:T(4,128)S(1)} %shard_map.161), channel_id=1, source_target_pairs={{0,4},{4,0},{8,12},{12,8},{1,5},{5,1},{9,13},{13,9},{2,6},{6,2},{1... | collective-permute-start | bytes 392 | tf_op jit(solution)/shard_map/ppermute | solution.py:578
  (24 other events, 51.3 us)

commit v7 on v6

--- a/solution.py
+++ b/solution.py
@@ -11,6 +11,7 @@
 SEQ = 64
 TILE = 512
 VMEM_BYTES = 40 * 1024 * 1024
+BIG_VMEM_BYTES = 58 * 1024 * 1024
 
 
 def flatten(array):
@@ -39,7 +40,7 @@
     return (gate_wide * jax.nn.sigmoid(gate_wide) * up_wide).astype(jnp.bfloat16)
 
 
-def gradient_sides(gate, up, hidden_grad, proj_gate, proj_up):
+def gradients(gate, up, hidden_grad):
     gate_wide = gate.astype(jnp.float32)
     up_wide = up.astype(jnp.float32)
     sigmoid_gate = jax.nn.sigmoid(gate_wide)
@@ -48,6 +49,11 @@
         hidden_grad * up_wide * sigmoid_gate * (1.0 + gate_wide * (1.0 - sigmoid_gate))
     ).astype(jnp.bfloat16)
     up_grad = (hidden_grad * silu_gate).astype(jnp.bfloat16)
+    return gate_grad, up_grad
+
+
+def gradient_sides(gate, up, hidden_grad, proj_gate, proj_up):
+    gate_grad, up_grad = gradients(gate, up, hidden_grad)
     return project(gate_grad, proj_gate), project(up_grad, proj_up)
 
 
@@ -122,8 +128,8 @@
 IN_VMEM = pl.BlockSpec(memory_space=pltpu.VMEM)
 
 
-def params():
-    return pltpu.CompilerParams(vmem_limit_bytes=VMEM_BYTES)
+def params(limit=VMEM_BYTES):
+    return pltpu.CompilerParams(vmem_limit_bytes=limit)
 
 
 def cost(flops, arrays):
@@ -246,7 +252,7 @@
             pltpu.VMEM((3, 2, TILE, half), jnp.bfloat16),
             pltpu.SemaphoreType.DMA((3, 2)),
         ],
-        compiler_params=params(),
+        compiler_params=params(BIG_VMEM_BYTES),
         cost_estimate=cost(8 * number * half * units, (far, weight_own, weight_sib)),
     )(flags, *blocks, far, weight_own, weight_sib)
 
@@ -269,20 +275,57 @@
     )(near_sum, returned, gate, up, proj_gate, proj_up)
 
 
+def turn_kernel(gate, up, far_gate, far_up, gates, ups):
+    number = gate.shape[0]
+    for source, target, part in (
+        (gate, gates, slice(0, number)),
+        (up, ups, slice(0, number)),
+        (far_gate, gates, slice(number, None)),
+        (far_up, ups, slice(number, None)),
+    ):
+        target[:, part] = source[...].astype(jnp.float32).T.astype(jnp.bfloat16)
+
+
+def turned(gate, up, far_gate, far_up):
+    number, units = far_gate.shape
+    shape = jax.ShapeDtypeStruct((units, 2 * number), jnp.bfloat16)
+    return pl.pallas_call(
+        turn_kernel,
+        grid=(units // TILE,),
+        in_specs=[tile_columns(number, 1)] * 2 + [tile_columns(number)] * 2,
+        out_specs=[tile_rows(2 * number)] * 2,
+        out_shape=[shape] * 2,
+        compiler_params=params(),
+        cost_estimate=cost(0, (gate, up)),
+    )(gate, up, far_gate, far_up)
+
+
 def lent_kernel(
-    flags, b0, b1, b2, b3, b4, b5, far, weight_own, weight_sib, gate, up, far_gate, far_up,
-    proj_gate, proj_up, sides, *scratch,
+    flags, b0, b1, b2, b3, b4, b5, far, weight_own, weight_sib, gates, ups, proj_gate, proj_up,
+    sides, *scratch,
 ):
     pairs = ((b0, b1), (b2, b3), (b4, b5))
-    total = stacked_products(flags, pairs, far, weight_own, weight_sib, *scratch)
-    gates = jnp.concatenate([gate[...], far_gate[...]], axis=0)
-    ups = jnp.concatenate([up[...], far_up[...]], axis=0)
-    add_sides(total.T, gates, ups, proj_gate[...], proj_up[...], sides)
-
-
-def lent_sides(
-    flags, blocks, far, weight_own, weight_sib, gate, up, far_gate, far_up, proj_gate, proj_up
-):
+    hidden_grad = stacked_products(flags, pairs, far, weight_own, weight_sib, *scratch)
+    gate_grad, up_grad = gradients(gates[...], ups[...], hidden_grad)
+    part = jnp.concatenate(
+        [
+            jnp.dot(proj_gate[...], gate_grad, preferred_element_type=jnp.float32),
+            jnp.dot(proj_up[...], up_grad, preferred_element_type=jnp.float32),
+        ],
+        axis=0,
+    )
+    first = pl.program_id(0) == 0
+
+    @pl.when(first)
+    def _():
+        sides[...] = part
+
+    @pl.when(jnp.logical_not(first))
+    def _():
+        sides[...] += part
+
+
+def lent_sides(flags, blocks, far, weight_own, weight_sib, gates, ups, proj_gate, proj_up):
     number, half = blocks[0].shape
     units = weight_own.shape[0]
     return pl.pallas_call(
@@ -290,22 +333,19 @@
         grid=(units // TILE,),
         in_specs=[SCALARS]
         + [ANYWHERE] * 9
-        + [tile_columns(number, 1)] * 2
-        + [tile_columns(number)] * 2
+        + [tile_rows(2 * number)] * 2
         + [tile_columns(RANK)] * 2,
-        out_specs=whole((2 * number, 2 * RANK)),
-        out_shape=jax.ShapeDtypeStruct((2 * number, 2 * RANK), jnp.float32),
+        out_specs=whole((2 * RANK, 2 * number)),
+        out_shape=jax.ShapeDtypeStruct((2 * RANK, 2 * number), jnp.float32),
         scratch_shapes=[
             pltpu.VMEM((2, 2 * number, half), jnp.bfloat16),
             pltpu.SemaphoreType.DMA((4,)),
             pltpu.VMEM((3, 2, TILE, half), jnp.bfloat16),
             pltpu.SemaphoreType.DMA((3, 2)),
         ],
-        compiler_params=params(),
+        compiler_params=params(BIG_VMEM_BYTES),
         cost_estimate=cost(8 * number * half * units, (far, weight_own, weight_sib)),
-    )(
-        flags, *blocks, far, weight_own, weight_sib, gate, up, far_gate, far_up, proj_gate, proj_up
-    )
+    )(flags, *blocks, far, weight_own, weight_sib, gates, ups, proj_gate, proj_up)
 
 
 def early_kernel(
@@ -410,7 +450,7 @@
     shape = scores.shape
     row = lax.broadcasted_iota(jnp.int32, shape, 0)
     column = lax.broadcasted_iota(jnp.int32, shape, 1)
-    gradient = jnp.concatenate([early[...], near[...] + far[...]], axis=0)
+    gradient = jnp.concatenate([early[...], (near[...] + far[...]).T], axis=0)
     total = jnp.zeros(shape, jnp.float32)
     for e in range(shape[0]):
         part = slice(e * SEQ, (e + 1) * SEQ)
@@ -531,12 +571,12 @@
     weight_own, weight_sib = down_weight, to_core(down_weight)
     q_hops = first_hops(q_outgrad)
     far_gate = to_chip(t_gate[cut:])
-    q_blocks = last_hops(*q_hops)
     own_in_out, hidden = early_sides(
         t_input, q_input, t_outgrad, q_outgrad, proj_input, proj_outgrad, t_gate, t_up, q_gate,
         q_up, proj_hidden,
     )
 
+    q_blocks = last_hops(*q_hops[:2], after(q_hops[2], own_in_out))
     a_hops = first_hops(after(t_outgrad[:cut], q_hops[2], far_gate))
     far_up = to_chip(after(t_up[cut:], far_gate))
     q_send = after(crossing_pair(*q_blocks), far_up)
@@ -544,7 +584,7 @@
     a_blocks = last_hops(*a_hops[:2], after(a_hops[2], q_send))
 
     b_hops = first_hops(after(t_outgrad[cut:], a_hops[2]))
-    a_send = crossing_pair(*a_blocks[:5], after(a_blocks[5], q_far, own_in_out))
+    a_send = crossing_pair(*a_blocks[:5], after(a_blocks[5], q_far))
     a_far = to_chip(a_send)
     q_near_sum, q_far_sum = partial_sums(
         flags, q_blocks, after(q_far, a_send), weight_own, weight_sib
@@ -552,10 +592,10 @@
     q_returned = to_chip(q_far_sum)
     b_blocks = last_hops(*b_hops[:2], after(b_hops[2], q_far_sum))
     a_near_sum, a_far_sum = partial_sums(flags, a_blocks, a_far, weight_own, weight_sib)
-    a_returned = to_chip(a_far_sum)
     b_send = after(crossing_pair(*b_blocks), a_far_sum)
     b_far = to_chip(b_send)
     in_out = tensor_sum(after(own_in_out, b_send))
+    a_returned = to_chip(after(a_far_sum, in_out))
     q_gradient = finished_sides(
         q_near_sum, after(q_returned, b_send), q_gate, q_up, proj_gate, proj_up
     )
@@ -566,14 +606,15 @@
     )
     core_found = to_core(own_found)
     found = (own_found, core_found, to_chip(own_found), to_chip(core_found))
+    gates, ups = turned(t_gate, t_up, after(far_gate, b_send), far_up)
     b_gradient = lent_sides(
-        flags, b_blocks, after(b_far, *found), weight_own, weight_sib, t_gate, t_up, far_gate,
-        far_up, proj_gate, proj_up,
+        flags, b_blocks, after(b_far, core_found), weight_own, weight_sib, gates, ups, proj_gate,
+        proj_up,
     )
     a_gradient = finished_sides(a_near_sum, a_returned, t_gate, t_up, proj_gate, proj_up)
     own_scores = partial_scores(
-        train_lengths, place, in_out[: 2 * cut], hidden[: 2 * cut], a_gradient, b_gradient[:cut],
-        to_chip(b_gradient[cut:]), found,
+        train_lengths, place, in_out[: 2 * cut], hidden[: 2 * cut], a_gradient, b_gradient[:, :cut],
+        to_chip(b_gradient[:, cut:]), found,
     )
     scores = own_scores + outer(own_scores) + across(own_scores) + opposite(own_scores)
     return scores / (RANK * SEQ)

time: 214 us -> 207 us (0.967)
  waiting for transfers between devices: 94.2 us -> 69 us
  Pallas kernels: 56.3 us -> 63.3 us
  local copies, waits for them, and re-layouts: 18 us -> 24.3 us
  other arithmetic: 2.54 us -> 5.78 us
    ppermute x2, waiting for transfers between devices: 25 us -> 0.01 us  [moving_plan(): found = (own_found, core_found, to_chip(own_found), to_chip(core_found))]
    ppermute x6, waiting for transfers between devices: 34.8 us -> 18.6 us  [first_hops(): return (own, outer(own), across(own))]
    ppermute x3, waiting for transfers between devices: 12.2 us -> 22.2 us  [last_hops(): return (own, one, mid, two, two, outer(after(two, one)))]
    ppermute x2, waiting for transfers between devices: 3.19 us -> 9.52 us  [tensor_sum(): values = values + outer(values)]
    unnamed x82 -> x80, local copies, waits for them, and re-layouts: 14.5 us -> 20 us
    ppermute x2, waiting for transfers between devices: 9.31 us -> 13.8 us  [tensor_sum(): return values + across(values)]
    pallas_call x2, Pallas kernels: 25.7 us -> 29.8 us  [partial_sums(): pl.pallas_call(partial_kernel, grid=(units // TILE,), in_specs=[SCALARS]...]
    ppermute x1, waiting for transfers between devices: 4.01 us -> 0.01 us  [moving_plan(): q_returned = to_chip(q_far_sum)]
  transfers between devices with their start and end apart: 31 -> 31, of which waited for: 19 -> 14; matrix products, arithmetic and copies ran while one was open for 3% -> 5% of each run, Pallas kernels for 26% -> 30%
where the time goes in v7:
time: 207 us
  waiting for transfers between devices  69 us (33%)
  Pallas kernels  63.3 us (31%)
  starting transfers between devices  43.7 us (21%)
  local copies, waits for them, and re-layouts  24.3 us (12%)
  other arithmetic  5.78 us (3%)
    pallas_call x2, Pallas kernels, partial_sums(): pl.pallas_call(partial_kernel, grid=(units // TILE,), in_specs=[SCALARS]...  29.8 us
    ppermute x3, waiting for transfers between devices, last_hops(): return (own, one, mid, two, two, outer(after(two, one)))  22.2 us
    unnamed x80, local copies, waits for them, and re-layouts  20 us
    ppermute x6, waiting for transfers between devices, first_hops(): return (own, outer(own), across(own))  18.6 us
    ppermute x6, starting transfers between devices, first_hops(): return (own, outer(own), across(own))  18.2 us
    pallas_call x1, Pallas kernels, lent_sides(): pl.pallas_call(lent_kernel, grid=(units // TILE,), in_specs=[SCALARS] + [...  18.2 us
    ppermute x2, waiting for transfers between devices, tensor_sum(): return values + across(values)  13.8 us
    ppermute x2, waiting for transfers between devices, tensor_sum(): values = values + outer(values)  9.52 us
  transfers between devices with their start and end apart: 31, of which 14 were waited for; matrix products, arithmetic and copies ran while one was open for 5% of the time, Pallas kernels for 30%

profile of v7, /device:TPU:0, one launch (start us, length us, event | category | flops | bytes accessed | tf_op | source)
XLA Modules:
  0.0 206.6 jit_solution(294806033779007656)
XLA Ops:
  0.5 1.3 slice.46
  1.8 2.6 %collective-permute-start.1 = (bf16[128,3584]{1,0:T(8,128)(2,1)S(1)}, bf16[128,3584]{1,0:T(8,128)(2,1)S(1)}, u32[]{:S(2)}, u32[]{:S(2)}) collective-permute-start(bf16[128,3584]{1,0:T(8,128)(2,1)S(1)} %bitcast.46), channel_id=1, source_target_pairs={{0,2},{1,3},{2,0},{3,1},{4,6},{5,7},{6,4},{7,5},{8,10},{9,11},{10,... | collective-permute-start | bytes 2752520 | tf_op jit(solution)/shard_map/ppermute | solution.py:573
  4.4 2.6 %collective-permute-start = (bf16[128,2048]{1,0:T(8,128)(2,1)}, bf16[128,2048]{1,0:T(8,128)(2,1)}, u32[]{:S(2)}, u32[]{:S(2)}) collective-permute-start(bf16[128,2048]{1,0:T(8,128)(2,1)} %bitcast.4.q_outgrad.b0), channel_id=1, source_target_pairs={{0,8},{4,12},{8,0},{12,4},{1,9},{5,13},{9,1},{13,5},{2,10},{6,14},... | collective-permute-start | bytes 1572872 | tf_op jit(solution)/shard_map/ppermute | solution.py:556
  7.0 1.6 collective-permute-start.4
  8.6 1.5 copy-done.1
  10.1 1.2 copy-done.3
  11.3 1.2 copy-done.8
  12.5 1.2 copy-done.10
  13.7 1.2 copy-done.16
  18.8 4.9 %shard_map.154 = (f32[384,128]{1,0:T(8,128)S(1)}, f32[384,64]{1,0:T(8,128)S(1)}) custom-call(bf16[256,2048]{1,0:T(8,128)(2,1)S(1)} %bitcast.39, bf16[128,2048]{1,0:T(8,128)(2,1)S(1)} %bitcast.40, bf16[256,2048]{1,0:T(8,128)(2,1)S(1)} %bitcast.34, bf16[128,2048]{1,0:T(8,128)(2,1)} %bitcast.4.q_outgrad.b0, bf16[64,2048]{1,0:T(8,128)(2,1)S(1)} %copy-done.25, ...), custom_call_target="tpu_custom_call" | custom-call | flops 1024 | bytes 1024 | tf_op jit(solution)/shard_map/pallas_call | solution.py:390
  23.7 7.2 %collective-permute-done.b3.b4 = bf16[128,2048]{1,0:T(8,128)(2,1)} collective-permute-done((bf16[128,2048]{1,0:T(8,128)(2,1)}, bf16[128,2048]{1,0:T(8,128)(2,1)}, u32[]{:S(2)}, u32[]{:S(2)}) %collective-permute-start) | collective-permute-done | bytes 524320 | tf_op jit(solution)/shard_map/ppermute | solution.py:556
  31.0 1.9 collective-permute-start.6
  35.6 10.1 %collective-permute-start.2 = (bf16[128,2048]{1,0:T(8,128)(2,1)}, bf16[128,2048]{1,0:T(8,128)(2,1)S(1)}, u32[]{:S(2)}, u32[]{:S(2)}) collective-permute-start(bf16[128,2048]{1,0:T(8,128)(2,1)} %bitcast.42), channel_id=1, source_target_pairs={{0,8},{4,12},{8,0},{12,4},{1,9},{5,13},{9,1},{13,5},{2,10},{6,14},... | collective-permute-start | bytes 1572872 | tf_op jit(solution)/shard_map/ppermute | solution.py:556
  45.7 11.6 %collective-permute-done.6.b5 = bf16[128,2048]{1,0:T(8,128)(2,1)} collective-permute-done((bf16[128,2048]{1,0:T(8,128)(2,1)}, bf16[128,2048]{1,0:T(8,128)(2,1)}, u32[]{:S(2)}, u32[]{:S(2)}) %collective-permute-start.6) | collective-permute-done | bytes 524320 | tf_op jit(solution)/shard_map/ppermute | solution.py:560
  57.2 1.5 select_bitcast_fusion.5
  59.6 6.4 %collective-permute-done.2.b3.b4 = bf16[128,2048]{1,0:T(8,128)(2,1)S(1)} collective-permute-done((bf16[128,2048]{1,0:T(8,128)(2,1)}, bf16[128,2048]{1,0:T(8,128)(2,1)S(1)}, u32[]{:S(2)}, u32[]{:S(2)}) %collective-permute-start.2) | collective-permute-done | bytes 524320 | tf_op jit(solution)/shard_map/ppermute | solution.py:556
  65.9 2.0 collective-permute-done.10.b1
  68.0 2.2 %collective-permute-start.11 = (bf16[128,2048]{1,0:T(8,128)(2,1)S(1)}, bf16[128,2048]{1,0:T(8,128)(2,1)S(1)}, u32[]{:S(2)}, u32[]{:S(2)}) collective-permute-start(bf16[128,2048]{1,0:T(8,128)(2,1)S(1)} %collective-permute-done.2.b3.b4), channel_id=1, source_target_pairs={{0,4},{4,0},{8,12},{12,8},{1,5},{5,1},{9,13},{13,9},{2,6},{6,2},{1... | collective-permute-start | bytes 1572872 | tf_op jit(solution)/shard_map/ppermute | solution.py:560
  70.2 2.2 %collective-permute-start.14 = (bf16[128,2048]{1,0:T(8,128)(2,1)}, bf16[128,2048]{1,0:T(8,128)(2,1)}, u32[]{:S(2)}, u32[]{:S(2)}) collective-permute-start(bf16[128,2048]{1,0:T(8,128)(2,1)} %bitcast.9.b0), channel_id=1, source_target_pairs={{0,4},{4,0},{8,12},{12,8},{1,5},{5,1},{9,13},{13,9},{2,6},{6,2},{1... | collective-permute-start | bytes 1572872 | tf_op jit(solution)/shard_map/ppermute | solution.py:556
  72.4 10.6 %collective-permute-done.11.b5 = bf16[128,2048]{1,0:T(8,128)(2,1)S(1)} collective-permute-done((bf16[128,2048]{1,0:T(8,128)(2,1)S(1)}, bf16[128,2048]{1,0:T(8,128)(2,1)S(1)}, u32[]{:S(2)}, u32[]{:S(2)}) %collective-permute-start.11) | collective-permute-done | bytes 524320 | tf_op jit(solution)/shard_map/ppermute | solution.py:560
  83.0 1.6 collective-permute-start.3
  88.7 14.9 %shard_map.155 = (f32[3584,128]{1,0:T(8,128)}, bf16[3584,128]{1,0:T(8,128)(2,1)}) custom-call(s32[2]{0:T(128)} %pad_add_fusion.flags, bf16[128,2048]{1,0:T(8,128)(2,1)} %bitcast.4.q_outgrad.b0, bf16[128,2048]{1,0:T(8,128)(2,1)} %copy-done.31, bf16[128,2048]{1,0:T(8,128)(2,1)} %collective-permute-done.5.b2, bf16[128,2048]{1,0:T(8,128)(2,1)} %collective-permute-done.b3.b4, ...), custom_call_target="tpu_custom_call" | custom-call | flops 1024 | bytes 1024 | tf_op jit(solution)/shard_map/pallas_call | solution.py:240
  103.6 2.9 %collective-permute-done.3.b3.b4 = bf16[128,2048]{1,0:T(8,128)(2,1)} collective-permute-done((bf16[128,2048]{1,0:T(8,128)(2,1)}, bf16[128,2048]{1,0:T(8,128)(2,1)}, u32[]{:S(2)}, u32[]{:S(2)}) %collective-permute-start.3) | collective-permute-done | bytes 524320 | tf_op jit(solution)/shard_map/ppermute | solution.py:556
  106.5 1.5 collective-permute-start.15
  108.5 2.6 %collective-permute-done.16.far = bf16[2,128,2048]{2,1,0:T(8,128)(2,1)S(1)} collective-permute-done((bf16[2,128,2048]{2,1,0:T(8,128)(2,1)}, bf16[2,128,2048]{2,1,0:T(8,128)(2,1)S(1)}, u32[]{:S(2)}, u32[]{:S(2)}) %collective-permute-start.16) | collective-permute-done | bytes 1048608 | tf_op jit(solution)/shard_map/ppermute | solution.py:588
  112.0 14.9 %shard_map.156 = (f32[3584,128]{1,0:T(8,128)}, bf16[3584,128]{1,0:T(8,128)(2,1)}) custom-call(s32[2]{0:T(128)} %pad_add_fusion.flags, bf16[128,2048]{1,0:T(8,128)(2,1)} %bitcast.43, bf16[128,2048]{1,0:T(8,128)(2,1)} %copy-done.32, bf16[128,2048]{1,0:T(8,128)(2,1)} %copy-done.36, bf16[128,2048]{1,0:T(8,128)(2,1)} %copy-done.29, bf16[128,2048]{1,0:T(8,128)(2,1)} %copy-done.29, ...), custom_call_target="tpu_custom_call" | custom-call | flops 1024 | bytes 1024 | tf_op jit(solution)/shard_map/pallas_call | solution.py:240
  127.0 1.6 select_bitcast_fusion.1
  129.8 1.1 collective-permute-start.17
  130.9 4.6 %collective-permute-done.17 = f32[384,128]{1,0:T(8,128)S(1)} collective-permute-done((f32[384,128]{1,0:T(8,128)S(1)}, f32[384,128]{1,0:T(8,128)S(1)}, u32[]{:S(2)}, u32[]{:S(2)}) %collective-permute-start.17) | collective-permute-done | bytes 196640 | tf_op jit(solution)/shard_map/ppermute | solution.py:543
  135.5 2.2 %collective-permute-start.18 = (f32[384,128]{1,0:T(8,128)S(1)}, f32[384,128]{1,0:T(8,128)S(1)}, u32[]{:S(2)}, u32[]{:S(2)}) collective-permute-start(f32[384,128]{1,0:T(8,128)S(1)} %add.32), channel_id=1, source_target_pairs={{0,8},{4,12},{8,0},{12,4},{1,9},{5,13},{9,1},{13,5},{2,10},{6,14},... | collective-permute-start | bytes 589832 | tf_op jit(solution)/shard_map/ppermute | solution.py:544
  137.7 8.0 %collective-permute-done.18 = f32[384,128]{1,0:T(8,128)S(1)} collective-permute-done((f32[384,128]{1,0:T(8,128)S(1)}, f32[384,128]{1,0:T(8,128)S(1)}, u32[]{:S(2)}, u32[]{:S(2)}) %collective-permute-start.18) | collective-permute-done | bytes 196640 | tf_op jit(solution)/shard_map/ppermute | solution.py:544
  147.4 1.2 copy-done.22
  148.6 2.9 %shard_map.158 = f32[128,128]{1,0:T(8,128)S(1)} custom-call(f32[3584,128]{1,0:T(8,128)S(1)} %copy-done.13, bf16[3584,128]{1,0:T(8,128)(2,1)S(1)} %copy-done.22, bf16[128,3584]{1,0:T(8,128)(2,1)S(1)} %bitcast.36, bf16[128,3584]{1,0:T(8,128)(2,1)S(1)} %bitcast.38, bf16[64,3584]{1,0:T(8,128)(2,1)S(1)} %copy-done.4, bf16[64,3584]{1,0:T(8,128)(2,1)S(1)} %copy-done.6), custom_call_target="tpu_custom_call" | custom-call | flops 1024 | bytes 1024 | tf_op jit(solution)/shard_map/pallas_call | solution.py:267
  151.6 5.0 %collective-permute-done.22 = f32[128,192]{1,0:T(8,128)S(1)} collective-permute-done((f32[128,192]{1,0:T(8,128)S(1)}, f32[128,192]{1,0:T(8,128)S(1)}, u32[]{:S(2)}, u32[]{:S(2)}) %collective-permute-start.22) | collective-permute-done | bytes 98336 | tf_op jit(solution)/shard_map/ppermute | solution.py:543
  156.6 1.2 collective-permute-start.23
  157.8 5.8 %collective-permute-done.23 = f32[128,192]{1,0:T(8,128)S(1)} collective-permute-done((f32[128,192]{1,0:T(8,128)S(1)}, f32[128,192]{1,0:T(8,128)S(1)}, u32[]{:S(2)}, u32[]{:S(2)}) %collective-permute-start.23) | collective-permute-done | bytes 98336 | tf_op jit(solution)/shard_map/ppermute | solution.py:544
  164.7 1.8 shard_map.160
  166.5 1.2 copy-done.14
  167.8 1.2 copy-done.15
  169.0 1.6 collective-permute-start.26
  172.0 18.2 %shard_map.161 = f32[128,256]{1,0:T(8,128)} custom-call(s32[2]{0:T(128)} %pad_add_fusion.flags, bf16[128,2048]{1,0:T(8,128)(2,1)} %bitcast.9.b0, bf16[128,2048]{1,0:T(8,128)(2,1)} %collective-permute-done.14.b1, bf16[128,2048]{1,0:T(8,128)(2,1)} %copy-done.33, bf16[128,2048]{1,0:T(8,128)(2,1)} %collective-permute-done.3.b3.b4, ...), custom_call_target="tpu_custom_call" | custom-call | flops 1024 | bytes 1024 | tf_op jit(solution)/shard_map/pallas_call | solution.py:331
  191.1 1.7 collective-permute-start.25
  192.8 1.5 copy-done.12
  194.3 2.8 %shard_map.157.early = f32[128,128]{1,0:T(8,128)S(1)} custom-call(f32[3584,128]{1,0:T(8,128)S(1)} %copy-done.12, bf16[3584,128]{1,0:T(8,128)(2,1)S(1)} %collective-permute-done.19.returned, bf16[256,3584]{1,0:T(8,128)(2,1)S(1)} %bitcast.30, bf16[256,3584]{1,0:T(8,128)(2,1)S(1)} %bitcast.33, bf16[64,3584]{1,0:T(8,128)(2,1)S(1)} %copy-done.5, ...), custom_call_target="tpu_custom_call" | custom-call | flops 1024 | bytes 1024 | tf_op jit(solution)/shard_map/pallas_call | solution.py:267
  197.2 2.0 shard_map.162
  199.2 2.3 %collective-permute-start.30 = (f32[4,8]{1,0:T(4,128)S(1)}, f32[4,8]{1,0:T(4,128)S(1)}, u32[]{:S(2)}, u32[]{:S(2)}) collective-permute-start(f32[4,8]{1,0:T(4,128)S(1)} %shard_map.162), channel_id=1, source_target_pairs={{0,12},{4,8},{8,4},{12,0},{1,13},{5,9},{9,5},{13,1},{2,14},{6,10},... | collective-permute-start | bytes 392 | tf_op jit(solution)/shard_map/ppermute | solution.py:619
  201.5 2.2 %collective-permute-start.28 = (f32[4,8]{1,0:T(4,128)S(1)}, f32[4,8]{1,0:T(4,128)S(1)}, u32[]{:S(2)}, u32[]{:S(2)}) collective-permute-start(f32[4,8]{1,0:T(4,128)S(1)} %shard_map.162), channel_id=1, source_target_pairs={{0,4},{4,0},{8,12},{12,8},{1,5},{5,1},{9,13},{13,9},{2,6},{6,2},{1... | collective-permute-start | bytes 392 | tf_op jit(solution)/shard_map/ppermute | solution.py:619
  204.7 1.3 collective-permute-done.29
  (124 shorter events, 21.4 us)
Async XLA Ops:
  0.0 8.6 %copy-start = (bf16[4,64,3584]{2,1,0:T(8,128)(2,1)S(1)}, bf16[4,64,3584]{2,1,0:T(8,128)(2,1)}, u32[]{:S(2)}) copy-start(bf16[4,64,3584]{2,1,0:T(8,128)(2,1)} %param.17) | copy-start | bytes 5505028
  0.0 88.7 %collective-permute-start.12 = (bf16[3584,2048]{1,0:T(8,128)(2,1)}, bf16[3584,2048]{1,0:T(8,128)(2,1)}, u32[]{:S(2)}, u32[]{:S(2)}) collective-permute-start(bf16[3584,2048]{1,0:T(8,128)(2,1)} %weight_own.5), channel_id=1, source_target_pairs={{0,1},{1,0},{2,3},{3,2},{4,5},{5,4},{6,7},{7,6},{8,9},{9,8},{10,11... | collective-permute-start | bytes 44040200 | tf_op jit(solution)/shard_map/ppermute | solution.py:571
  1.8 32.0 %collective-permute-start.1 = (bf16[128,3584]{1,0:T(8,128)(2,1)S(1)}, bf16[128,3584]{1,0:T(8,128)(2,1)S(1)}, u32[]{:S(2)}, u32[]{:S(2)}) collective-permute-start(bf16[128,3584]{1,0:T(8,128)(2,1)S(1)} %bitcast.46), channel_id=1, source_target_pairs={{0,2},{1,3},{2,0},{3,1},{4,6},{5,7},{6,4},{7,5},{8,10},{9,11},{10,... | collective-permute-start | bytes 2752520 | tf_op jit(solution)/shard_map/ppermute | solution.py:573
  4.4 26.5 %collective-permute-start = (bf16[128,2048]{1,0:T(8,128)(2,1)}, bf16[128,2048]{1,0:T(8,128)(2,1)}, u32[]{:S(2)}, u32[]{:S(2)}) collective-permute-start(bf16[128,2048]{1,0:T(8,128)(2,1)} %bitcast.4.q_outgrad.b0), channel_id=1, source_target_pairs={{0,8},{4,12},{8,0},{12,4},{1,9},{5,13},{9,1},{13,5},{2,10},{6,14},... | collective-permute-start | bytes 1572872 | tf_op jit(solution)/shard_map/ppermute | solution.py:556
  7.0 24.0 %collective-permute-start.4 = (bf16[128,2048]{1,0:T(8,128)(2,1)}, bf16[128,2048]{1,0:T(8,128)(2,1)S(1)}, u32[]{:S(2)}, u32[]{:S(2)}) collective-permute-start(bf16[128,2048]{1,0:T(8,128)(2,1)} %bitcast.4.q_outgrad.b0), channel_id=1, source_target_pairs={{0,4},{4,0},{8,12},{12,8},{1,5},{5,1},{9,13},{13,9},{2,6},{6,2},{1... | collective-permute-start | bytes 1572872 | tf_op jit(solution)/shard_map/ppermute | solution.py:556
  30.9 4.5 %copy-start.31 = (bf16[128,2048]{1,0:T(8,128)(2,1)}, bf16[128,2048]{1,0:T(8,128)(2,1)S(1)}, u32[]{:S(2)}) copy-start(bf16[128,2048]{1,0:T(8,128)(2,1)S(1)} %collective-permute-done.4.b1) | copy-start | bytes 1572868
  31.0 4.6 %collective-permute-start.5 = (bf16[128,2048]{1,0:T(8,128)(2,1)}, bf16[128,2048]{1,0:T(8,128)(2,1)}, u32[]{:S(2)}, u32[]{:S(2)}) collective-permute-start(bf16[128,2048]{1,0:T(8,128)(2,1)} %bitcast.4.q_outgrad.b0), channel_id=1, source_target_pairs={{0,1},{1,0},{2,3},{3,2},{4,8},{5,9},{6,10},{7,11},{8,4},{9,5},{10,... | collective-permute-start | bytes 1572872 | tf_op jit(solution)/shard_map/ppermute | solution.py:559
  31.0 26.3 %collective-permute-start.6 = (bf16[128,2048]{1,0:T(8,128)(2,1)}, bf16[128,2048]{1,0:T(8,128)(2,1)}, u32[]{:S(2)}, u32[]{:S(2)}) collective-permute-start(bf16[128,2048]{1,0:T(8,128)(2,1)} %collective-permute-done.b3.b4), channel_id=1, source_target_pairs={{0,4},{4,0},{8,12},{12,8},{1,5},{5,1},{9,13},{13,9},{2,6},{6,2},{1... | collective-permute-start | bytes 1572872 | tf_op jit(solution)/shard_map/ppermute | solution.py:560
  33.8 25.0 %collective-permute-start.7 = (bf16[128,3584]{1,0:T(8,128)(2,1)}, bf16[128,3584]{1,0:T(8,128)(2,1)S(1)}, u32[]{:S(2)}, u32[]{:S(2)}) collective-permute-start(bf16[128,3584]{1,0:T(8,128)(2,1)} %bitcast.16), channel_id=1, source_target_pairs={{0,2},{1,3},{2,0},{3,1},{4,6},{5,7},{6,4},{7,5},{8,10},{9,11},{10,... | collective-permute-start | bytes 2752520 | tf_op jit(solution)/shard_map/ppermute | solution.py:581
  35.5 32.5 %collective-permute-start.10 = (bf16[128,2048]{1,0:T(8,128)(2,1)}, bf16[128,2048]{1,0:T(8,128)(2,1)S(1)}, u32[]{:S(2)}, u32[]{:S(2)}) collective-permute-start(bf16[128,2048]{1,0:T(8,128)(2,1)} %bitcast.41), channel_id=1, source_target_pairs={{0,4},{4,0},{8,12},{12,8},{1,5},{5,1},{9,13},{13,9},{2,6},{6,2},{1... | collective-permute-start | bytes 1572872 | tf_op jit(solution)/shard_map/ppermute | solution.py:556
  35.6 30.4 %collective-permute-start.2 = (bf16[128,2048]{1,0:T(8,128)(2,1)}, bf16[128,2048]{1,0:T(8,128)(2,1)S(1)}, u32[]{:S(2)}, u32[]{:S(2)}) collective-permute-start(bf16[128,2048]{1,0:T(8,128)(2,1)} %bitcast.42), channel_id=1, source_target_pairs={{0,8},{4,12},{8,0},{12,4},{1,9},{5,13},{9,1},{13,5},{2,10},{6,14},... | collective-permute-start | bytes 1572872 | tf_op jit(solution)/shard_map/ppermute | solution.py:556
  58.7 11.4 %copy-start.30 = (bf16[2,64,2048]{2,1,0:T(8,128)(2,1)S(1)}, bf16[2,64,2048]{2,1,0:T(8,128)(2,1)}, u32[]{:S(2)}) copy-start(bf16[2,64,2048]{2,1,0:T(8,128)(2,1)} %get-tuple-element.63) | copy-start | bytes 1572868
  58.8 26.9 %copy-start.19 = (bf16[128,3584]{1,0:T(8,128)(2,1)}, bf16[128,3584]{1,0:T(8,128)(2,1)S(1)}, u32[]{:S(2)}) copy-start(bf16[128,3584]{1,0:T(8,128)(2,1)S(1)} %collective-permute-done.7.far_up) | copy-start | bytes 2752516
  58.9 25.8 %collective-permute-start.8 = (bf16[2,128,2048]{2,1,0:T(8,128)(2,1)S(1)}, bf16[2,128,2048]{2,1,0:T(8,128)(2,1)S(1)}, u32[]{:S(2)}, u32[]{:S(2)}) collective-permute-start(bf16[2,128,2048]{2,1,0:T(8,128)(2,1)S(1)} %pad_maximum_fusion), channel_id=1, source_target_pairs={{0,2},{1,3},{2,0},{3,1},{4,6},{5,7},{6,4},{7,5},{8,10},{9,11},{10,... | collective-permute-start | bytes 3145736 | tf_op jit(solution)/shard_map/ppermute | solution.py:583
  65.9 19.8 %copy-start.29 = (bf16[128,2048]{1,0:T(8,128)(2,1)}, bf16[128,2048]{1,0:T(8,128)(2,1)S(1)}, u32[]{:S(2)}) copy-start(bf16[128,2048]{1,0:T(8,128)(2,1)S(1)} %collective-permute-done.2.b3.b4) | copy-start | bytes 1572868
  68.0 17.8 %copy-start.32 = (bf16[128,2048]{1,0:T(8,128)(2,1)}, bf16[128,2048]{1,0:T(8,128)(2,1)S(1)}, u32[]{:S(2)}) copy-start(bf16[128,2048]{1,0:T(8,128)(2,1)S(1)} %collective-permute-done.10.b1) | copy-start | bytes 1572868
  68.0 15.0 %collective-permute-start.11 = (bf16[128,2048]{1,0:T(8,128)(2,1)S(1)}, bf16[128,2048]{1,0:T(8,128)(2,1)S(1)}, u32[]{:S(2)}, u32[]{:S(2)}) collective-permute-start(bf16[128,2048]{1,0:T(8,128)(2,1)S(1)} %collective-permute-done.2.b3.b4), channel_id=1, source_target_pairs={{0,4},{4,0},{8,12},{12,8},{1,5},{5,1},{9,13},{13,9},{2,6},{6,2},{1... | collective-permute-start | bytes 1572872 | tf_op jit(solution)/shard_map/ppermute | solution.py:560
  70.2 15.4 %collective-permute-start.9 = (bf16[128,2048]{1,0:T(8,128)(2,1)S(1)}, bf16[128,2048]{1,0:T(8,128)(2,1)S(1)}, u32[]{:S(2)}, u32[]{:S(2)}) collective-permute-start(bf16[128,2048]{1,0:T(8,128)(2,1)S(1)} %bitcast.44), channel_id=1, source_target_pairs={{0,1},{1,0},{2,3},{3,2},{4,8},{5,9},{6,10},{7,11},{8,4},{9,5},{10,... | collective-permute-start | bytes 1572872 | tf_op jit(solution)/shard_map/ppermute | solution.py:559
  70.2 36.3 %collective-permute-start.14 = (bf16[128,2048]{1,0:T(8,128)(2,1)}, bf16[128,2048]{1,0:T(8,128)(2,1)}, u32[]{:S(2)}, u32[]{:S(2)}) collective-permute-start(bf16[128,2048]{1,0:T(8,128)(2,1)} %bitcast.9.b0), channel_id=1, source_target_pairs={{0,4},{4,0},{8,12},{12,8},{1,5},{5,1},{9,13},{13,9},{2,6},{6,2},{1... | collective-permute-start | bytes 1572872 | tf_op jit(solution)/shard_map/ppermute | solution.py:556
  83.0 23.5 %collective-permute-start.3 = (bf16[128,2048]{1,0:T(8,128)(2,1)}, bf16[128,2048]{1,0:T(8,128)(2,1)}, u32[]{:S(2)}, u32[]{:S(2)}) collective-permute-start(bf16[128,2048]{1,0:T(8,128)(2,1)} %bitcast.9.b0), channel_id=1, source_target_pairs={{0,8},{4,12},{8,0},{12,4},{1,9},{5,13},{9,1},{13,5},{2,10},{6,14},... | collective-permute-start | bytes 1572872 | tf_op jit(solution)/shard_map/ppermute | solution.py:556
  87.5 23.6 %collective-permute-start.16 = (bf16[2,128,2048]{2,1,0:T(8,128)(2,1)}, bf16[2,128,2048]{2,1,0:T(8,128)(2,1)S(1)}, u32[]{:S(2)}, u32[]{:S(2)}) collective-permute-start(bf16[2,128,2048]{2,1,0:T(8,128)(2,1)} %pad_maximum_fusion.1), channel_id=1, source_target_pairs={{0,2},{1,3},{2,0},{3,1},{4,6},{5,7},{6,4},{7,5},{8,10},{9,11},{10,... | collective-permute-start | bytes 3145736 | tf_op jit(solution)/shard_map/ppermute | solution.py:588
  106.5 20.5 %collective-permute-start.13 = (bf16[128,2048]{1,0:T(8,128)(2,1)}, bf16[128,2048]{1,0:T(8,128)(2,1)S(1)}, u32[]{:S(2)}, u32[]{:S(2)}) collective-permute-start(bf16[128,2048]{1,0:T(8,128)(2,1)} %bitcast.9.b0), channel_id=1, source_target_pairs={{0,1},{1,0},{2,3},{3,2},{4,8},{5,9},{6,10},{7,11},{8,4},{9,5},{10,... | collective-permute-start | bytes 1572872 | tf_op jit(solution)/shard_map/ppermute | solution.py:559
  106.5 20.5 %collective-permute-start.15 = (bf16[128,2048]{1,0:T(8,128)(2,1)}, bf16[128,2048]{1,0:T(8,128)(2,1)S(1)}, u32[]{:S(2)}, u32[]{:S(2)}) collective-permute-start(bf16[128,2048]{1,0:T(8,128)(2,1)} %collective-permute-done.3.b3.b4), channel_id=1, source_target_pairs={{0,4},{4,0},{8,12},{12,8},{1,5},{5,1},{9,13},{13,9},{2,6},{6,2},{1... | collective-permute-start | bytes 1572872 | tf_op jit(solution)/shard_map/ppermute | solution.py:560
  108.0 38.5 %collective-permute-start.21 = (bf16[3584,128]{1,0:T(8,128)(2,1)}, bf16[3584,128]{1,0:T(8,128)(2,1)S(1)}, u32[]{:S(2)}, u32[]{:S(2)}) collective-permute-start(bf16[3584,128]{1,0:T(8,128)(2,1)} %get-tuple-element.47), channel_id=1, source_target_pairs={{0,2},{1,3},{2,0},{3,1},{4,6},{5,7},{6,4},{7,5},{8,10},{9,11},{10,... | collective-permute-start | bytes 2752520 | tf_op jit(solution)/shard_map/ppermute | solution.py:592
  127.0 20.4 %copy-start.13 = (f32[3584,128]{1,0:T(8,128)S(1)}, f32[3584,128]{1,0:T(8,128)}, u32[]{:S(2)}) copy-start(f32[3584,128]{1,0:T(8,128)} %get-tuple-element.57.near_sum) | copy-start | bytes 5505028
  128.6 18.8 %copy-start.4 = (bf16[64,3584]{1,0:T(8,128)(2,1)S(1)}, bf16[64,3584]{1,0:T(8,128)(2,1)}, u32[]{:S(2)}) copy-start(bf16[64,3584]{1,0:T(8,128)(2,1)} %proj_gate.5) | copy-start | bytes 1376260
  128.6 18.8 %copy-start.6 = (bf16[64,3584]{1,0:T(8,128)(2,1)S(1)}, bf16[64,3584]{1,0:T(8,128)(2,1)}, u32[]{:S(2)}) copy-start(bf16[64,3584]{1,0:T(8,128)(2,1)} %proj_up.5) | copy-start | bytes 1376260
  128.6 18.7 %copy-start.9 = (bf16[2,64,3584]{2,1,0:T(8,128)(2,1)S(1)}, bf16[2,64,3584]{2,1,0:T(8,128)(2,1)}, u32[]{:S(2)}) copy-start(bf16[2,64,3584]{2,1,0:T(8,128)(2,1)} %param.22) | copy-start | bytes 2752516
  128.7 18.7 %copy-start.11 = (bf16[2,64,3584]{2,1,0:T(8,128)(2,1)S(1)}, bf16[2,64,3584]{2,1,0:T(8,128)(2,1)}, u32[]{:S(2)}) copy-start(bf16[2,64,3584]{2,1,0:T(8,128)(2,1)} %param.23) | copy-start | bytes 2752516
  128.8 42.2 %collective-permute-start.20 = (bf16[2,128,2048]{2,1,0:T(8,128)(2,1)S(1)}, bf16[2,128,2048]{2,1,0:T(8,128)(2,1)S(1)}, u32[]{:S(2)}, u32[]{:S(2)}) collective-permute-start(bf16[2,128,2048]{2,1,0:T(8,128)(2,1)S(1)} %pad_maximum_fusion.2), channel_id=1, source_target_pairs={{0,2},{1,3},{2,0},{3,1},{4,6},{5,7},{6,4},{7,5},{8,10},{9,11},{10,... | collective-permute-start | bytes 3145736 | tf_op jit(solution)/shard_map/ppermute | solution.py:596
  129.8 5.7 %collective-permute-start.17 = (f32[384,128]{1,0:T(8,128)S(1)}, f32[384,128]{1,0:T(8,128)S(1)}, u32[]{:S(2)}, u32[]{:S(2)}) collective-permute-start(f32[384,128]{1,0:T(8,128)S(1)} %get-tuple-element.53), channel_id=1, source_target_pairs={{0,4},{4,0},{8,12},{12,8},{1,5},{5,1},{9,13},{13,9},{2,6},{6,2},{1... | collective-permute-start | bytes 589832 | tf_op jit(solution)/shard_map/ppermute | solution.py:543
  135.5 10.3 %collective-permute-start.18 = (f32[384,128]{1,0:T(8,128)S(1)}, f32[384,128]{1,0:T(8,128)S(1)}, u32[]{:S(2)}, u32[]{:S(2)}) collective-permute-start(f32[384,128]{1,0:T(8,128)S(1)} %add.32), channel_id=1, source_target_pairs={{0,8},{4,12},{8,0},{12,4},{1,9},{5,13},{9,1},{13,5},{2,10},{6,14},... | collective-permute-start | bytes 589832 | tf_op jit(solution)/shard_map/ppermute | solution.py:544
  145.8 47.0 %collective-permute-start.19 = (bf16[3584,128]{1,0:T(8,128)(2,1)}, bf16[3584,128]{1,0:T(8,128)(2,1)S(1)}, u32[]{:S(2)}, u32[]{:S(2)}) collective-permute-start(bf16[3584,128]{1,0:T(8,128)(2,1)} %get-tuple-element.56), channel_id=1, source_target_pairs={{0,2},{1,3},{2,0},{3,1},{4,6},{5,7},{6,4},{7,5},{8,10},{9,11},{10,... | collective-permute-start | bytes 2752520 | tf_op jit(solution)/shard_map/ppermute | solution.py:598
  148.6 15.1 %copy-start.27 = (s32[2]{0:T(128)S(1)}, s32[2]{0:T(128)}, u32[]{:S(2)}) copy-start(s32[2]{0:T(128)} %lengths.2) | copy-start | bytes 28
  148.6 16.1 %copy-start.2 = (bf16[4,64,3584]{2,1,0:T(8,128)(2,1)S(1)}, bf16[4,64,3584]{2,1,0:T(8,128)(2,1)}, u32[]{:S(2)}) copy-start(bf16[4,64,3584]{2,1,0:T(8,128)(2,1)} %param.18) | copy-start | bytes 5505028
  148.6 16.1 %copy-start.20 = (bf16[128,3584]{1,0:T(8,128)(2,1)S(1)}, bf16[128,3584]{1,0:T(8,128)(2,1)}, u32[]{:S(2)}) copy-start(bf16[128,3584]{1,0:T(8,128)(2,1)} %copy-done.19) | copy-start | bytes 2752516
  151.5 13.2 %copy-start.18 = (bf16[128,3584]{1,0:T(8,128)(2,1)S(1)}, bf16[128,3584]{1,0:T(8,128)(2,1)}, u32[]{:S(2)}) copy-start(bf16[128,3584]{1,0:T(8,128)(2,1)} %copy-done.17) | copy-start | bytes 2752516
  151.5 5.0 %collective-permute-start.22 = (f32[128,192]{1,0:T(8,128)S(1)}, f32[128,192]{1,0:T(8,128)S(1)}, u32[]{:S(2)}, u32[]{:S(2)}) collective-permute-start(f32[128,192]{1,0:T(8,128)S(1)} %pad_maximum_fusion.3), channel_id=1, source_target_pairs={{0,4},{4,0},{8,12},{12,8},{1,5},{5,1},{9,13},{13,9},{2,6},{6,2},{1... | collective-permute-start | bytes 294920 | tf_op jit(solution)/shard_map/ppermute | solution.py:543
  156.6 7.1 %collective-permute-start.23 = (f32[128,192]{1,0:T(8,128)S(1)}, f32[128,192]{1,0:T(8,128)S(1)}, u32[]{:S(2)}, u32[]{:S(2)}) collective-permute-start(f32[128,192]{1,0:T(8,128)S(1)} %fusion), channel_id=1, source_target_pairs={{0,8},{4,12},{8,0},{12,4},{1,9},{5,13},{9,1},{13,5},{2,10},{6,14},... | collective-permute-start | bytes 294920 | tf_op jit(solution)/shard_map/ppermute | solution.py:544
  164.6 6.0 %collective-permute-start.24 = (f32[2,192,64]{2,1,0:T(8,128)S(1)}, f32[2,192,64]{2,1,0:T(8,128)}, u32[]{:S(2)}, u32[]{:S(2)}) collective-permute-start(f32[2,192,64]{2,1,0:T(8,128)S(1)} %shard_map.159.q0), channel_id=1, source_target_pairs={{0,1},{1,0},{2,3},{3,2},{4,5},{5,4},{6,7},{7,6},{8,9},{9,8},{10,11... | collective-permute-start | bytes 294920 | tf_op jit(solution)/shard_map/ppermute | solution.py:607
  169.0 28.2 %collective-permute-start.26 = (f32[2,192,64]{2,1,0:T(8,128)S(1)}, f32[2,192,64]{2,1,0:T(8,128)}, u32[]{:S(2)}, u32[]{:S(2)}) collective-permute-start(f32[2,192,64]{2,1,0:T(8,128)S(1)} %shard_map.159.q0), channel_id=1, source_target_pairs={{0,2},{1,3},{2,0},{3,1},{4,6},{5,7},{6,4},{7,5},{8,10},{9,11},{10,... | collective-permute-start | bytes 294920 | tf_op jit(solution)/shard_map/ppermute | solution.py:608
  170.6 26.6 %collective-permute-start.27 = (f32[2,192,64]{2,1,0:T(8,128)}, f32[2,192,64]{2,1,0:T(8,128)}, u32[]{:S(2)}, u32[]{:S(2)}) collective-permute-start(f32[2,192,64]{2,1,0:T(8,128)} %collective-permute-done.24.q1), channel_id=1, source_target_pairs={{0,2},{1,3},{2,0},{3,1},{4,6},{5,7},{6,4},{7,5},{8,10},{9,11},{10,... | collective-permute-start | bytes 294920 | tf_op jit(solution)/shard_map/ppermute | solution.py:608
  172.0 20.8 %copy-start.5 = (bf16[64,3584]{1,0:T(8,128)(2,1)S(1)}, bf16[64,3584]{1,0:T(8,128)(2,1)}, u32[]{:S(2)}) copy-start(bf16[64,3584]{1,0:T(8,128)(2,1)} %proj_gate.5) | copy-start | bytes 1376260
  172.0 20.8 %copy-start.7 = (bf16[64,3584]{1,0:T(8,128)(2,1)S(1)}, bf16[64,3584]{1,0:T(8,128)(2,1)}, u32[]{:S(2)}) copy-start(bf16[64,3584]{1,0:T(8,128)(2,1)} %proj_up.5) | copy-start | bytes 1376260
  191.1 6.1 %collective-permute-start.25 = (f32[128,128]{1,0:T(8,128)S(1)}, f32[128,128]{1,0:T(8,128)S(1)}, u32[]{:S(2)}, u32[]{:S(2)}) collective-permute-start(f32[128,128]{1,0:T(8,128)S(1)} %get-tuple-element.71), channel_id=1, source_target_pairs={{0,2},{1,3},{2,0},{3,1},{4,6},{5,7},{6,4},{7,5},{8,10},{9,11},{10,... | collective-permute-start | bytes 196616 | tf_op jit(solution)/shard_map/ppermute | solution.py:617
  199.2 5.4 %collective-permute-start.30 = (f32[4,8]{1,0:T(4,128)S(1)}, f32[4,8]{1,0:T(4,128)S(1)}, u32[]{:S(2)}, u32[]{:S(2)}) collective-permute-start(f32[4,8]{1,0:T(4,128)S(1)} %shard_map.162), channel_id=1, source_target_pairs={{0,12},{4,8},{8,4},{12,0},{1,13},{5,9},{9,5},{13,1},{2,14},{6,10},... | collective-permute-start | bytes 392 | tf_op jit(solution)/shard_map/ppermute | solution.py:619
  201.5 4.5 %collective-permute-start.29 = (f32[4,8]{1,0:T(4,128)S(1)}, f32[4,8]{1,0:T(4,128)S(1)}, u32[]{:S(2)}, u32[]{:S(2)}) collective-permute-start(f32[4,8]{1,0:T(4,128)S(1)} %shard_map.162), channel_id=1, source_target_pairs={{0,8},{4,12},{8,0},{12,4},{1,9},{5,13},{9,1},{13,5},{2,10},{6,14},... | collective-permute-start | bytes 392 | tf_op jit(solution)/shard_map/ppermute | solution.py:619
  201.5 4.5 %collective-permute-start.28 = (f32[4,8]{1,0:T(4,128)S(1)}, f32[4,8]{1,0:T(4,128)S(1)}, u32[]{:S(2)}, u32[]{:S(2)}) collective-permute-start(f32[4,8]{1,0:T(4,128)S(1)} %shard_map.162), channel_id=1, source_target_pairs={{0,4},{4,0},{8,12},{12,8},{1,5},{5,1},{9,13},{13,9},{2,6},{6,2},{1... | collective-permute-start | bytes 392 | tf_op jit(solution)/shard_map/ppermute | solution.py:619
  (23 other events, 30.7 us)

commit v8 on v7

--- a/solution.py
+++ b/solution.py
@@ -151,7 +151,7 @@
 def stacked_products(
     flags, pairs, far, weight_own, weight_sib, stacked, semaphores, held, weight_sems
 ):
-    number = far.shape[1]
+    number = far[0].shape[0]
     step = pl.program_id(0)
     tiles = weight_own.shape[0] // TILE
 
@@ -165,34 +165,30 @@
             for side, weight in enumerate((weight_own, weight_sib))
         ]
 
-    @pl.when(step == 0)
-    def _():
-        for tile in range(2):
-            for copy in weight_copies(tile):
-                copy.start()
-        slot = flags[1]
-        far_copies = [
+    def row_copies(pair, slot, row, first):
+        return [
             pltpu.make_async_copy(
-                far.at[i], stacked.at[jnp.bitwise_xor(slot, i), pl.ds(number, number)],
-                semaphores.at[2 + i],
+                pair[i], stacked.at[jnp.bitwise_xor(slot, i), pl.ds(row, number)],
+                semaphores.at[first + i],
             )
             for i in range(2)
         ]
+
+    @pl.when(step == 0)
+    def _():
+        far_copies = row_copies(far, flags[2], number, 2)
         for copy in far_copies:
             copy.start()
         for code, pair in enumerate(pairs):
 
             @pl.when(flags[0] == code)
             def _():
-                copies = [
-                    pltpu.make_async_copy(
-                        pair[i], stacked.at[jnp.bitwise_xor(slot, i), pl.ds(0, number)],
-                        semaphores.at[i],
-                    )
-                    for i in range(2)
-                ]
+                copies = row_copies(pair, flags[1], 0, 0)
                 for copy in copies:
                     copy.start()
+                for tile in range(2):
+                    for copy in weight_copies(tile):
+                        copy.start()
                 for copy in copies:
                     copy.wait()
 
@@ -225,13 +221,24 @@
 
 
 def partial_kernel(
-    flags, b0, b1, b2, b3, b4, b5, far, weight_own, weight_sib, near_sum, far_sum, *scratch
+    flags, b0, b1, b2, b3, b4, b5, far_a, far_b, weight_own, weight_sib, near_sum, far_sum,
+    *scratch,
 ):
     pairs = ((b0, b1), (b2, b3), (b4, b5))
+    far = (far_a, far_b)
     total = stacked_products(flags, pairs, far, weight_own, weight_sib, *scratch)
-    number = far.shape[1]
+    number = far_a.shape[0]
     near_sum[...] = total[:, :number]
     far_sum[...] = total[:, number:].astype(jnp.bfloat16)
+
+
+def product_scratch(number, half):
+    return [
+        pltpu.VMEM((2, 2 * number, half), jnp.bfloat16),
+        pltpu.SemaphoreType.DMA((4,)),
+        pltpu.VMEM((3, 2, TILE, half), jnp.bfloat16),
+        pltpu.SemaphoreType.DMA((3, 2)),
+    ]
 
 
 def partial_sums(flags, blocks, far, weight_own, weight_sib):
@@ -240,21 +247,16 @@
     return pl.pallas_call(
         partial_kernel,
         grid=(units // TILE,),
-        in_specs=[SCALARS] + [ANYWHERE] * 9,
+        in_specs=[SCALARS] + [ANYWHERE] * 10,
         out_specs=[tile_rows(number)] * 2,
         out_shape=[
             jax.ShapeDtypeStruct((units, number), jnp.float32),
             jax.ShapeDtypeStruct((units, number), jnp.bfloat16),
         ],
-        scratch_shapes=[
-            pltpu.VMEM((2, 2 * number, half), jnp.bfloat16),
-            pltpu.SemaphoreType.DMA((4,)),
-            pltpu.VMEM((3, 2, TILE, half), jnp.bfloat16),
-            pltpu.SemaphoreType.DMA((3, 2)),
-        ],
+        scratch_shapes=product_scratch(number, half),
         compiler_params=params(BIG_VMEM_BYTES),
-        cost_estimate=cost(8 * number * half * units, (far, weight_own, weight_sib)),
-    )(flags, *blocks, far, weight_own, weight_sib)
+        cost_estimate=cost(8 * number * half * units, (weight_own, weight_sib)),
+    )(flags, *blocks, *far, weight_own, weight_sib)
 
 
 def finish_kernel(near_sum, returned, gate, up, proj_gate, proj_up, sides):
@@ -301,10 +303,11 @@
 
 
 def lent_kernel(
-    flags, b0, b1, b2, b3, b4, b5, far, weight_own, weight_sib, gates, ups, proj_gate, proj_up,
-    sides, *scratch,
+    flags, b0, b1, b2, b3, b4, b5, far_a, far_b, weight_own, weight_sib, gates, ups, proj_gate,
+    proj_up, near, away, *scratch,
 ):
     pairs = ((b0, b1), (b2, b3), (b4, b5))
+    far = (far_a, far_b)
     hidden_grad = stacked_products(flags, pairs, far, weight_own, weight_sib, *scratch)
     gate_grad, up_grad = gradients(gates[...], ups[...], hidden_grad)
     part = jnp.concatenate(
@@ -314,38 +317,37 @@
         ],
         axis=0,
     )
+    number = near.shape[1]
     first = pl.program_id(0) == 0
 
     @pl.when(first)
     def _():
-        sides[...] = part
+        near[...] = part[:, :number]
+        away[...] = part[:, number:]
 
     @pl.when(jnp.logical_not(first))
     def _():
-        sides[...] += part
+        near[...] += part[:, :number]
+        away[...] += part[:, number:]
 
 
 def lent_sides(flags, blocks, far, weight_own, weight_sib, gates, ups, proj_gate, proj_up):
     number, half = blocks[0].shape
     units = weight_own.shape[0]
+    side = jax.ShapeDtypeStruct((2 * RANK, number), jnp.float32)
     return pl.pallas_call(
         lent_kernel,
         grid=(units // TILE,),
         in_specs=[SCALARS]
-        + [ANYWHERE] * 9
+        + [ANYWHERE] * 10
         + [tile_rows(2 * number)] * 2
         + [tile_columns(RANK)] * 2,
-        out_specs=whole((2 * RANK, 2 * number)),
-        out_shape=jax.ShapeDtypeStruct((2 * RANK, 2 * number), jnp.float32),
-        scratch_shapes=[
-            pltpu.VMEM((2, 2 * number, half), jnp.bfloat16),
-            pltpu.SemaphoreType.DMA((4,)),
-            pltpu.VMEM((3, 2, TILE, half), jnp.bfloat16),
-            pltpu.SemaphoreType.DMA((3, 2)),
-        ],
+        out_specs=[whole(side.shape)] * 2,
+        out_shape=[side] * 2,
+        scratch_shapes=product_scratch(number, half),
         compiler_params=params(BIG_VMEM_BYTES),
-        cost_estimate=cost(8 * number * half * units, (far, weight_own, weight_sib)),
-    )(flags, *blocks, far, weight_own, weight_sib, gates, ups, proj_gate, proj_up)
+        cost_estimate=cost(8 * number * half * units, (weight_own, weight_sib)),
+    )(flags, *blocks, *far, weight_own, weight_sib, gates, ups, proj_gate, proj_up)
 
 
 def early_kernel(
@@ -418,29 +420,27 @@
     )
 
 
-def query_kernel(lengths, in_out, sums, found):
+def query_kernel(lengths, sums, found):
     for e in range(found.shape[0]):
         part = slice(e * SEQ, (e + 1) * SEQ)
+        gate_side, up_side, hidden_side, in_side, out_side = [
+            sums[part, i * RANK : (i + 1) * RANK] for i in range(5)
+        ]
         three = example_features(
-            in_out[part, :RANK],
-            sums[part, 2 * RANK :],
-            sums[part, :RANK],
-            sums[part, RANK : 2 * RANK],
-            in_out[part, RANK:],
-            lengths[e],
+            in_side, hidden_side, gate_side, up_side, out_side, lengths[e]
         )
         for segment in range(3):
             found[e, segment * RANK : (segment + 1) * RANK, :] = three[segment]
 
 
-def query_features(lengths, in_out, sums):
+def query_features(lengths, sums):
     return pl.pallas_call(
         query_kernel,
-        in_specs=[SCALARS, IN_VMEM, IN_VMEM],
+        in_specs=[SCALARS, IN_VMEM],
         out_specs=IN_VMEM,
         out_shape=jax.ShapeDtypeStruct((lengths.shape[0], 3 * RANK, RANK), jnp.float32),
         compiler_params=params(),
-    )(lengths, in_out, sums)
+    )(lengths, sums)
 
 
 def score_kernel(
@@ -515,11 +515,14 @@
     inner_chip = (t == 1) | (t == 2)
     near_code = jnp.where(at_home, 0, jnp.where(inner_chip, 1, 2))
     first_parity = jnp.where(at_home, t % 2, upper)
-    flags = jnp.stack([near_code, first_parity ^ core]).astype(jnp.int32)
+    near_slot = first_parity ^ core
+    far_slot = jnp.where(inner_chip & ~at_home, 1 - near_slot, near_slot)
+    flags = jnp.stack([near_code, near_slot, far_slot]).astype(jnp.int32)
     place = jnp.stack([d]).astype(jnp.int32)
 
     to_core = functools.partial(lax.ppermute, axis_name="dp", perm=[(i, i ^ 1) for i in range(4)])
     to_chip = functools.partial(lax.ppermute, axis_name="dp", perm=[(i, i ^ 2) for i in range(4)])
+    to_other = functools.partial(lax.ppermute, axis_name="dp", perm=[(i, i ^ 3) for i in range(4)])
     outer = functools.partial(
         lax.ppermute, axis_name="tensor", perm=[(i, i ^ 1) for i in range(4)]
     )
@@ -540,8 +543,20 @@
     )
 
     def tensor_sum(values):
-        values = values + outer(values)
-        return values + across(values)
+        return values + outer(values) + across(values) + opposite(values)
+
+    def first_hops(own):
+        return own, outer(own), across(own)
+
+    def last_hops(own, one, two):
+        mid = middle(after(own, two))
+        return own, one, mid, two, two, outer(after(two, one))
+
+    def crossing_first(own, two):
+        return jnp.where(at_home, two, own)
+
+    def crossing_second(one, mid, last):
+        return jnp.where(at_home, jnp.where(inner_chip, mid, last), one)
 
     q_input, q_gate, q_up, q_outgrad = [
         flatten(a) for a in (query_input, query_gate, query_up, query_outgrad)
@@ -569,55 +584,57 @@
         )
 
     weight_own, weight_sib = down_weight, to_core(down_weight)
-    q_hops = first_hops(q_outgrad)
+    q_own, q_one, q_two = first_hops(q_outgrad)
     far_gate = to_chip(t_gate[cut:])
     own_in_out, hidden = early_sides(
         t_input, q_input, t_outgrad, q_outgrad, proj_input, proj_outgrad, t_gate, t_up, q_gate,
         q_up, proj_hidden,
     )
-
-    q_blocks = last_hops(*q_hops[:2], after(q_hops[2], own_in_out))
-    a_hops = first_hops(after(t_outgrad[:cut], q_hops[2], far_gate))
+    q_blocks = last_hops(q_own, q_one, after(q_two, own_in_out, far_gate))
     far_up = to_chip(after(t_up[cut:], far_gate))
-    q_send = after(crossing_pair(*q_blocks), far_up)
-    q_far = to_chip(q_send)
-    a_blocks = last_hops(*a_hops[:2], after(a_hops[2], q_send))
-
-    b_hops = first_hops(after(t_outgrad[cut:], a_hops[2]))
-    a_send = crossing_pair(*a_blocks[:5], after(a_blocks[5], q_far))
-    a_far = to_chip(a_send)
+    q_first = to_chip(crossing_first(q_own, q_blocks[3]))
+    q_send = after(crossing_second(q_one, q_blocks[2], q_blocks[5]), far_up)
+    q_far = (q_first, to_chip(q_send))
+
+    a_own, a_one, a_two = first_hops(after(t_outgrad[:cut], q_send))
+    a_two = after(a_two, a_one)
+    a_cross = crossing_first(a_own, a_two)
+    a_first = to_chip(a_cross)
+    a_blocks = last_hops(a_own, a_one, a_two)
     q_near_sum, q_far_sum = partial_sums(
-        flags, q_blocks, after(q_far, a_send), weight_own, weight_sib
-    )
-    q_returned = to_chip(q_far_sum)
-    b_blocks = last_hops(*b_hops[:2], after(b_hops[2], q_far_sum))
+        after(flags, a_cross), q_blocks, q_far, weight_own, weight_sib
+    )
+    a_send = crossing_second(a_one, a_blocks[2], after(a_blocks[5], q_far_sum))
+    a_far = (a_first, to_chip(a_send))
+    q_returned = to_chip(after(q_far_sum, *a_far))
+
+    b_own, b_one, b_two = first_hops(after(t_outgrad[cut:], a_send))
     a_near_sum, a_far_sum = partial_sums(flags, a_blocks, a_far, weight_own, weight_sib)
-    b_send = after(crossing_pair(*b_blocks), a_far_sum)
-    b_far = to_chip(b_send)
-    in_out = tensor_sum(after(own_in_out, b_send))
-    a_returned = to_chip(after(a_far_sum, in_out))
-    q_gradient = finished_sides(
-        q_near_sum, after(q_returned, b_send), q_gate, q_up, proj_gate, proj_up
-    )
-    own_found = query_features(
-        query_lengths,
-        in_out[2 * cut :],
-        tensor_sum(jnp.concatenate([q_gradient, hidden[2 * cut :]], axis=1)),
-    )
-    core_found = to_core(own_found)
-    found = (own_found, core_found, to_chip(own_found), to_chip(core_found))
-    gates, ups = turned(t_gate, t_up, after(far_gate, b_send), far_up)
-    b_gradient = lent_sides(
-        flags, b_blocks, after(b_far, core_found), weight_own, weight_sib, gates, ups, proj_gate,
+    b_two = after(b_two, b_one, a_far_sum)
+    b_first = to_chip(crossing_first(b_own, b_two))
+    b_blocks = last_hops(b_own, b_one, b_two)
+    q_gradient = finished_sides(q_near_sum, q_returned, q_gate, q_up, proj_gate, proj_up)
+    gates, ups = turned(t_gate, t_up, after(far_gate, a_far_sum), far_up)
+    b_send = crossing_second(
+        after(b_one, q_gradient, b_first, gates), b_blocks[2], b_blocks[5]
+    )
+    b_far = (b_first, to_chip(b_send))
+    q_sums = jnp.concatenate([q_gradient, hidden[2 * cut :], own_in_out[2 * cut :]], axis=1)
+    q_sums = tensor_sum(after(q_sums, b_send))
+    a_returned = to_chip(after(a_far_sum, q_sums, *b_far))
+    in_out = tensor_sum(after(own_in_out[: 2 * cut], b_send))
+    own_found = query_features(query_lengths, q_sums)
+    found = (own_found, to_core(own_found), to_chip(own_found), to_other(own_found))
+    b_near, b_away = lent_sides(
+        flags, b_blocks, b_far, weight_own, weight_sib, gates, ups, proj_gate,
         proj_up,
     )
     a_gradient = finished_sides(a_near_sum, a_returned, t_gate, t_up, proj_gate, proj_up)
     own_scores = partial_scores(
-        train_lengths, place, in_out[: 2 * cut], hidden[: 2 * cut], a_gradient, b_gradient[:, :cut],
-        to_chip(b_gradient[:, cut:]), found,
-    )
-    scores = own_scores + outer(own_scores) + across(own_scores) + opposite(own_scores)
-    return scores / (RANK * SEQ)
+        train_lengths, place, in_out, hidden[: 2 * cut], a_gradient, b_near,
+        to_chip(b_away), found,
+    )
+    return tensor_sum(own_scores) / (RANK * SEQ)
 
 
 def solution(mesh):

time: 207 us -> 219 us (1.058)
  starting transfers between devices: 43.7 us -> 50.7 us
  waiting for transfers between devices: 69 us -> 73.3 us
  local copies, waits for them, and re-layouts: 24.3 us -> 21.9 us
    ppermute x3, waiting for transfers between devices: 22.2 us -> 11.1 us  [last_hops(): return (own, one, mid, two, two, outer(after(two, one)))]
    ppermute x1, waiting for transfers between devices: 0.01 us -> 8.61 us  [moving_plan(): far_up = to_chip(after(t_up[cut:], far_gate))]
    ppermute x16 -> x21, starting transfers between devices: 16.3 us -> 24.5 us  [the longest x9 13.4 us: tensor_sum(): return values + outer(values) + across(values) + opposite(values)]
    ppermute x6, waiting for transfers between devices: 18.6 us -> 24.5 us  [first_hops(): return (own, outer(own), across(own))]
    ppermute x6, starting transfers between devices: 18.2 us -> 12.6 us  [first_hops(): return (own, outer(own), across(own))]
    select_n x0 -> x6, other arithmetic: none -> 5.53 us  [the longest x3 3.44 us: crossing_first(): return jnp.where(at_home, two, own)]
    another operation x7 -> x1, other arithmetic: 5.1 us -> 0.58 us  [moving_plan(): flags = jnp.stack([near_code, near_slot, far_slot]).astype(jnp.int32)]
    ppermute x3, starting transfers between devices: 5.55 us -> 9.84 us  [last_hops(): return (own, one, mid, two, two, outer(after(two, one)))]
  transfers between devices with their start and end apart: 31 -> 36, of which waited for: 14 -> 12; matrix products, arithmetic and copies ran while one was open for 5% -> 5% of each run, Pallas kernels for 30% -> 29%
where the time goes in v8:
time: 219 us; the launch traced here: 218 us
  waiting for transfers between devices  73.3 us (33%)
  Pallas kernels  64 us (29%)
  starting transfers between devices  50.7 us (23%)
  local copies, waits for them, and re-layouts  21.9 us (10%)
  other arithmetic  7.88 us (4%)
    pallas_call x2, Pallas kernels, partial_sums(): pl.pallas_call(partial_kernel, grid=(units // TILE,), in_specs=[SCALARS]...  28.9 us
    ppermute x6, waiting for transfers between devices, first_hops(): return (own, outer(own), across(own))  24.5 us
    pallas_call x1, Pallas kernels, lent_sides(): pl.pallas_call(lent_kernel, grid=(units // TILE,), in_specs=[SCALARS] + [...  17.7 us
    ppermute x9, waiting for transfers between devices, tensor_sum(): return values + outer(values) + across(values) + opposite(values)  17.6 us
    unnamed x86, local copies, waits for them, and re-layouts  17.3 us
    ppermute x9, starting transfers between devices, tensor_sum(): return values + outer(values) + across(values) + opposite(values)  13.4 us
    ppermute x6, starting transfers between devices, first_hops(): return (own, outer(own), across(own))  12.6 us
    ppermute x3, waiting for transfers between devices, last_hops(): return (own, one, mid, two, two, outer(after(two, one)))  11.1 us
  transfers between devices with their start and end apart: 36, of which 12 were waited for; matrix products, arithmetic and copies ran while one was open for 5% of the time, Pallas kernels for 29%

profile of v8, /device:TPU:0, one launch (start us, length us, event | category | flops | bytes accessed | tf_op | source)
XLA Modules:
  0.0 218.2 jit_solution(5173831987186410645)
XLA Ops:
  0.5 1.3 slice.41
  1.8 2.6 %collective-permute-start.1 = (bf16[128,3584]{1,0:T(8,128)(2,1)S(1)}, bf16[128,3584]{1,0:T(8,128)(2,1)S(1)}, u32[]{:S(2)}, u32[]{:S(2)}) collective-permute-start(bf16[128,3584]{1,0:T(8,128)(2,1)S(1)} %bitcast.31), channel_id=1, source_target_pairs={{0,2},{1,3},{2,0},{3,1},{4,6},{5,7},{6,4},{7,5},{8,10},{9,11},{10,... | collective-permute-start | bytes 2752520 | tf_op jit(solution)/shard_map/ppermute | solution.py:588
  4.4 2.6 %collective-permute-start = (bf16[128,2048]{1,0:T(8,128)(2,1)}, bf16[128,2048]{1,0:T(8,128)(2,1)}, u32[]{:S(2)}, u32[]{:S(2)}) collective-permute-start(bf16[128,2048]{1,0:T(8,128)(2,1)} %bitcast.4.q_outgrad.b0), channel_id=1, source_target_pairs={{0,8},{4,12},{8,0},{12,4},{1,9},{5,13},{9,1},{13,5},{2,10},{6,14},... | collective-permute-start | bytes 1572872 | tf_op jit(solution)/shard_map/ppermute | solution.py:571
  7.0 1.6 collective-permute-start.3
  8.6 1.5 copy-done.1
  10.1 1.2 copy-done.3
  11.3 1.2 copy-done.9
  12.5 1.2 copy-done.11
  13.7 1.2 copy-done.17
  18.8 4.9 %shard_map.154 = (f32[384,128]{1,0:T(8,128)S(1)}, f32[384,64]{1,0:T(8,128)S(1)}) custom-call(bf16[256,2048]{1,0:T(8,128)(2,1)S(1)} %bitcast.28, bf16[128,2048]{1,0:T(8,128)(2,1)S(1)} %bitcast.29, bf16[256,2048]{1,0:T(8,128)(2,1)S(1)} %bitcast.23, bf16[128,2048]{1,0:T(8,128)(2,1)} %bitcast.4.q_outgrad.b0, bf16[64,2048]{1,0:T(8,128)(2,1)S(1)} %copy-done.24, ...), custom_call_target="tpu_custom_call" | custom-call | flops 1024 | bytes 1024 | tf_op jit(solution)/shard_map/pallas_call | solution.py:392
  23.7 7.1 %collective-permute-done.b3.b4 = bf16[128,2048]{1,0:T(8,128)(2,1)} collective-permute-done((bf16[128,2048]{1,0:T(8,128)(2,1)}, bf16[128,2048]{1,0:T(8,128)(2,1)}, u32[]{:S(2)}, u32[]{:S(2)}) %collective-permute-start) | collective-permute-done | bytes 524320 | tf_op jit(solution)/shard_map/ppermute | solution.py:571
  32.5 2.2 slice.43
  36.3 10.2 %collective-permute-done.4.b5 = bf16[128,2048]{1,0:T(8,128)(2,1)} collective-permute-done((bf16[128,2048]{1,0:T(8,128)(2,1)}, bf16[128,2048]{1,0:T(8,128)(2,1)}, u32[]{:S(2)}, u32[]{:S(2)}) %collective-permute-start.4) | collective-permute-done | bytes 524320 | tf_op jit(solution)/shard_map/ppermute | solution.py:575
  46.5 1.9 select_select_fusion.2
  48.4 8.6 %collective-permute-done.5.far_up = bf16[128,3584]{1,0:T(8,128)(2,1)S(1)} collective-permute-done((bf16[128,3584]{1,0:T(8,128)(2,1)}, bf16[128,3584]{1,0:T(8,128)(2,1)S(1)}, u32[]{:S(2)}, u32[]{:S(2)}) %collective-permute-start.5) | collective-permute-done | bytes 917536 | tf_op jit(solution)/shard_map/ppermute | solution.py:594
  57.9 1.7 collective-permute-start.7
  59.6 2.2 %collective-permute-start.6 = (bf16[128,2048]{1,0:T(8,128)(2,1)}, bf16[128,2048]{1,0:T(8,128)(2,1)S(1)}, u32[]{:S(2)}, u32[]{:S(2)}) collective-permute-start(bf16[128,2048]{1,0:T(8,128)(2,1)} %bitcast.10.b0), channel_id=1, source_target_pairs={{0,8},{4,12},{8,0},{12,4},{1,9},{5,13},{9,1},{13,5},{2,10},{6,14},... | collective-permute-start | bytes 1572872 | tf_op jit(solution)/shard_map/ppermute | solution.py:571
  61.9 1.3 broadcast_select_fusion.1
  63.6 1.6 collective-permute-start.11
  65.2 17.4 %collective-permute-done.7.b1 = bf16[128,2048]{1,0:T(8,128)(2,1)S(1)} collective-permute-done((bf16[128,2048]{1,0:T(8,128)(2,1)}, bf16[128,2048]{1,0:T(8,128)(2,1)S(1)}, u32[]{:S(2)}, u32[]{:S(2)}) %collective-permute-start.7) | collective-permute-done | bytes 524320 | tf_op jit(solution)/shard_map/ppermute | solution.py:571
  82.7 3.6 %collective-permute-start.9 = (bf16[128,2048]{1,0:T(8,128)(2,1)S(1)}, bf16[128,2048]{1,0:T(8,128)(2,1)S(1)}, u32[]{:S(2)}, u32[]{:S(2)}) collective-permute-start(bf16[128,2048]{1,0:T(8,128)(2,1)S(1)} %collective-permute-done.6.b3.b4), channel_id=1, source_target_pairs={{0,4},{4,0},{8,12},{12,8},{1,5},{5,1},{9,13},{13,9},{2,6},{6,2},{1... | collective-permute-start | bytes 1572872 | tf_op jit(solution)/shard_map/ppermute | solution.py:575
  87.7 1.6 collective-permute-start.15
  90.1 14.4 %shard_map.155 = (f32[3584,128]{1,0:T(8,128)}, bf16[3584,128]{1,0:T(8,128)(2,1)}) custom-call(s32[3]{0:T(128)} %pad_add_fusion.flags, bf16[128,2048]{1,0:T(8,128)(2,1)} %bitcast.4.q_outgrad.b0, bf16[128,2048]{1,0:T(8,128)(2,1)} %collective-permute-done.3.b1, bf16[128,2048]{1,0:T(8,128)(2,1)} %collective-permute-done.2.b2, ...), custom_call_target="tpu_custom_call" | custom-call | flops 1024 | bytes 1024 | tf_op jit(solution)/shard_map/pallas_call | solution.py:247
  105.2 4.4 %collective-permute-start.13 = (bf16[128,2048]{1,0:T(8,128)(2,1)}, bf16[128,2048]{1,0:T(8,128)(2,1)}, u32[]{:S(2)}, u32[]{:S(2)}) collective-permute-start(bf16[128,2048]{1,0:T(8,128)(2,1)} %bitcast.9.b0), channel_id=1, source_target_pairs={{0,8},{4,12},{8,0},{12,4},{1,9},{5,13},{9,1},{13,5},{2,10},{6,14},... | collective-permute-start | bytes 1572872 | tf_op jit(solution)/shard_map/ppermute | solution.py:571
  109.7 6.8 %collective-permute-done.16.far_b = bf16[128,2048]{1,0:T(8,128)(2,1)S(1)} collective-permute-done((bf16[128,2048]{1,0:T(8,128)(2,1)S(1)}, bf16[128,2048]{1,0:T(8,128)(2,1)S(1)}, u32[]{:S(2)}, u32[]{:S(2)}) %collective-permute-start.16) | collective-permute-done | bytes 524320 | tf_op jit(solution)/shard_map/ppermute | solution.py:608
  117.3 14.5 %shard_map.156 = (f32[3584,128]{1,0:T(8,128)}, bf16[3584,128]{1,0:T(8,128)(2,1)}) custom-call(s32[3]{0:T(128)} %pad_add_fusion.flags, bf16[128,2048]{1,0:T(8,128)(2,1)} %bitcast.10.b0, bf16[128,2048]{1,0:T(8,128)(2,1)} %copy-done.32, bf16[128,2048]{1,0:T(8,128)(2,1)} %copy-done.35, bf16[128,2048]{1,0:T(8,128)(2,1)} %copy-done.29, ...), custom_call_target="tpu_custom_call" | custom-call | flops 1024 | bytes 1024 | tf_op jit(solution)/shard_map/pallas_call | solution.py:247
  131.8 1.3 broadcast_select_fusion
  133.2 1.4 collective-permute-start.20
  134.5 5.6 %collective-permute-start.18 = (bf16[128,2048]{1,0:T(8,128)(2,1)}, bf16[128,2048]{1,0:T(8,128)(2,1)S(1)}, u32[]{:S(2)}, u32[]{:S(2)}) collective-permute-start(bf16[128,2048]{1,0:T(8,128)(2,1)} %collective-permute-done.13.b3.b4), channel_id=1, source_target_pairs={{0,4},{4,0},{8,12},{12,8},{1,5},{5,1},{9,13},{13,9},{2,6},{6,2},{1... | collective-permute-start | bytes 1572872 | tf_op jit(solution)/shard_map/ppermute | solution.py:575
  140.2 1.2 copy-done.21
  141.4 1.8 shard_map.158
  143.2 1.2 copy-done.14
  144.5 5.4 %shard_map.157 = f32[128,128]{1,0:T(8,128)S(1)} custom-call(f32[3584,128]{1,0:T(8,128)S(1)} %copy-done.16, bf16[3584,128]{1,0:T(8,128)(2,1)} %collective-permute-done.19.returned, bf16[128,3584]{1,0:T(8,128)(2,1)S(1)} %bitcast.25, bf16[128,3584]{1,0:T(8,128)(2,1)S(1)} %bitcast.27, bf16[64,3584]{1,0:T(8,128)(2,1)S(1)} %copy-done.5, bf16[64,3584]{1,0:T(8,128)(2,1)S(1)} %copy-done.7), custom_call_target="tpu_custom_call" | custom-call | flops 1024 | bytes 1024 | tf_op jit(solution)/shard_map/pallas_call | solution.py:269
  152.3 3.2 %collective-permute-start.26 = (f32[128,320]{1,0:T(8,128)S(1)}, f32[128,320]{1,0:T(8,128)S(1)}, u32[]{:S(2)}, u32[]{:S(2)}) collective-permute-start(f32[128,320]{1,0:T(8,128)S(1)} %pad_maximum_fusion), channel_id=1, source_target_pairs={{0,12},{4,8},{8,4},{12,0},{1,13},{5,9},{9,5},{13,1},{2,14},{6,10},... | collective-permute-start | bytes 491528 | tf_op jit(solution)/shard_map/ppermute | solution.py:546
  156.7 5.3 %collective-permute-done.26 = f32[128,320]{1,0:T(8,128)S(1)} collective-permute-done((f32[128,320]{1,0:T(8,128)S(1)}, f32[128,320]{1,0:T(8,128)S(1)}, u32[]{:S(2)}, u32[]{:S(2)}) %collective-permute-start.26) | collective-permute-done | bytes 163872 | tf_op jit(solution)/shard_map/ppermute | solution.py:546
  162.0 9.6 %collective-permute-done.25 = f32[128,320]{1,0:T(8,128)S(1)} collective-permute-done((f32[128,320]{1,0:T(8,128)S(1)}, f32[128,320]{1,0:T(8,128)S(1)}, u32[]{:S(2)}, u32[]{:S(2)}) %collective-permute-start.25) | collective-permute-done | bytes 163872 | tf_op jit(solution)/shard_map/ppermute | solution.py:546
  171.6 1.2 collective-permute-start.28
  172.9 2.7 %collective-permute-start.23 = (f32[256,128]{1,0:T(8,128)S(1)}, f32[256,128]{1,0:T(8,128)}, u32[]{:S(2)}, u32[]{:S(2)}) collective-permute-start(f32[256,128]{1,0:T(8,128)S(1)} %slice.36), channel_id=1, source_target_pairs={{0,12},{4,8},{8,4},{12,0},{1,13},{5,9},{9,5},{13,1},{2,14},{6,10},... | collective-permute-start | bytes 393224 | tf_op jit(solution)/shard_map/ppermute | solution.py:546
  175.6 1.7 collective-permute-start.21
  178.4 17.7 %shard_map.160 = (f32[128,128]{1,0:T(8,128)}, f32[128,128]{1,0:T(8,128)}) custom-call(s32[3]{0:T(128)} %pad_add_fusion.flags, bf16[128,2048]{1,0:T(8,128)(2,1)} %bitcast.9.b0, bf16[128,2048]{1,0:T(8,128)(2,1)} %copy-done.30, bf16[128,2048]{1,0:T(8,128)(2,1)} %copy-done.33, bf16[128,2048]{1,0:T(8,128)(2,1)} %collective-permute-done.13.b3.b4, ...), custom_call_target="tpu_custom_call" | custom-call | flops 1024 | bytes 1024 | tf_op jit(solution)/shard_map/pallas_call | solution.py:338
  200.0 1.5 copy-done.13
  201.5 2.9 %shard_map.159.early = f32[128,128]{1,0:T(8,128)S(1)} custom-call(f32[3584,128]{1,0:T(8,128)S(1)} %copy-done.13, bf16[3584,128]{1,0:T(8,128)(2,1)S(1)} %collective-permute-done.28.returned, bf16[256,3584]{1,0:T(8,128)(2,1)S(1)} %bitcast.19, bf16[256,3584]{1,0:T(8,128)(2,1)S(1)} %bitcast.22, bf16[64,3584]{1,0:T(8,128)(2,1)S(1)} %copy-done.6, ...), custom_call_target="tpu_custom_call" | custom-call | flops 1024 | bytes 1024 | tf_op jit(solution)/shard_map/pallas_call | solution.py:269
  204.4 2.8 %collective-permute-done.32.q3 = f32[2,192,64]{2,1,0:T(8,128)S(1)} collective-permute-done((f32[2,192,64]{2,1,0:T(8,128)S(1)}, f32[2,192,64]{2,1,0:T(8,128)S(1)}, u32[]{:S(2)}, u32[]{:S(2)}) %collective-permute-start.32) | collective-permute-done | bytes 98336 | tf_op jit(solution)/shard_map/ppermute | solution.py:627
  207.2 1.9 collective-permute-done.29.far
  209.0 1.4 shard_map.162
  210.5 2.7 %collective-permute-start.35 = (f32[4,8]{1,0:T(4,128)S(1)}, f32[4,8]{1,0:T(4,128)S(1)}, u32[]{:S(2)}, u32[]{:S(2)}) collective-permute-start(f32[4,8]{1,0:T(4,128)S(1)} %shard_map.162), channel_id=1, source_target_pairs={{0,12},{4,8},{8,4},{12,0},{1,13},{5,9},{9,5},{13,1},{2,14},{6,10},... | collective-permute-start | bytes 392 | tf_op jit(solution)/shard_map/ppermute | solution.py:546
  213.2 1.7 collective-permute-start.33
  215.9 1.7 collective-permute-done.34
  (137 shorter events, 23.0 us)
Async XLA Ops:
  0.0 89.2 %collective-permute-start.12 = (bf16[3584,2048]{1,0:T(8,128)(2,1)}, bf16[3584,2048]{1,0:T(8,128)(2,1)}, u32[]{:S(2)}, u32[]{:S(2)}) collective-permute-start(bf16[3584,2048]{1,0:T(8,128)(2,1)} %weight_own.5), channel_id=1, source_target_pairs={{0,1},{1,0},{2,3},{3,2},{4,5},{5,4},{6,7},{7,6},{8,9},{9,8},{10,11... | collective-permute-start | bytes 44040200 | tf_op jit(solution)/shard_map/ppermute | solution.py:586
  1.8 29.1 %collective-permute-start.1 = (bf16[128,3584]{1,0:T(8,128)(2,1)S(1)}, bf16[128,3584]{1,0:T(8,128)(2,1)S(1)}, u32[]{:S(2)}, u32[]{:S(2)}) collective-permute-start(bf16[128,3584]{1,0:T(8,128)(2,1)S(1)} %bitcast.31), channel_id=1, source_target_pairs={{0,2},{1,3},{2,0},{3,1},{4,6},{5,7},{6,4},{7,5},{8,10},{9,11},{10,... | collective-permute-start | bytes 2752520 | tf_op jit(solution)/shard_map/ppermute | solution.py:588
  4.4 26.5 %collective-permute-start = (bf16[128,2048]{1,0:T(8,128)(2,1)}, bf16[128,2048]{1,0:T(8,128)(2,1)}, u32[]{:S(2)}, u32[]{:S(2)}) collective-permute-start(bf16[128,2048]{1,0:T(8,128)(2,1)} %bitcast.4.q_outgrad.b0), channel_id=1, source_target_pairs={{0,8},{4,12},{8,0},{12,4},{1,9},{5,13},{9,1},{13,5},{2,10},{6,14},... | collective-permute-start | bytes 1572872 | tf_op jit(solution)/shard_map/ppermute | solution.py:571
  7.0 24.8 %collective-permute-start.3 = (bf16[128,2048]{1,0:T(8,128)(2,1)}, bf16[128,2048]{1,0:T(8,128)(2,1)}, u32[]{:S(2)}, u32[]{:S(2)}) collective-permute-start(bf16[128,2048]{1,0:T(8,128)(2,1)} %bitcast.4.q_outgrad.b0), channel_id=1, source_target_pairs={{0,4},{4,0},{8,12},{12,8},{1,5},{5,1},{9,13},{13,9},{2,6},{6,2},{1... | collective-permute-start | bytes 1572872 | tf_op jit(solution)/shard_map/ppermute | solution.py:571
  23.7 11.5 %copy-start.4 = (bf16[4,64,2048]{2,1,0:T(8,128)(2,1)S(1)}, bf16[4,64,2048]{2,1,0:T(8,128)(2,1)}, u32[]{:S(2)}) copy-start(bf16[4,64,2048]{2,1,0:T(8,128)(2,1)} %param.19) | copy-start | bytes 3145732
  31.8 4.5 %collective-permute-start.2 = (bf16[128,2048]{1,0:T(8,128)(2,1)}, bf16[128,2048]{1,0:T(8,128)(2,1)}, u32[]{:S(2)}, u32[]{:S(2)}) collective-permute-start(bf16[128,2048]{1,0:T(8,128)(2,1)} %bitcast.4.q_outgrad.b0), channel_id=1, source_target_pairs={{0,1},{1,0},{2,3},{3,2},{4,8},{5,9},{6,10},{7,11},{8,4},{9,5},{10,... | collective-permute-start | bytes 1572872 | tf_op jit(solution)/shard_map/ppermute | solution.py:574
  31.8 14.7 %collective-permute-start.4 = (bf16[128,2048]{1,0:T(8,128)(2,1)}, bf16[128,2048]{1,0:T(8,128)(2,1)}, u32[]{:S(2)}, u32[]{:S(2)}) collective-permute-start(bf16[128,2048]{1,0:T(8,128)(2,1)} %collective-permute-done.b3.b4), channel_id=1, source_target_pairs={{0,4},{4,0},{8,12},{12,8},{1,5},{5,1},{9,13},{13,9},{2,6},{6,2},{1... | collective-permute-start | bytes 1572872 | tf_op jit(solution)/shard_map/ppermute | solution.py:575
  34.7 22.3 %collective-permute-start.5 = (bf16[128,3584]{1,0:T(8,128)(2,1)}, bf16[128,3584]{1,0:T(8,128)(2,1)S(1)}, u32[]{:S(2)}, u32[]{:S(2)}) collective-permute-start(bf16[128,3584]{1,0:T(8,128)(2,1)} %bitcast.30), channel_id=1, source_target_pairs={{0,2},{1,3},{2,0},{3,1},{4,6},{5,7},{6,4},{7,5},{8,10},{9,11},{10,... | collective-permute-start | bytes 2752520 | tf_op jit(solution)/shard_map/ppermute | solution.py:594
  57.9 24.7 %collective-permute-start.7 = (bf16[128,2048]{1,0:T(8,128)(2,1)}, bf16[128,2048]{1,0:T(8,128)(2,1)S(1)}, u32[]{:S(2)}, u32[]{:S(2)}) collective-permute-start(bf16[128,2048]{1,0:T(8,128)(2,1)} %bitcast.10.b0), channel_id=1, source_target_pairs={{0,4},{4,0},{8,12},{12,8},{1,5},{5,1},{9,13},{13,9},{2,6},{6,2},{1... | collective-permute-start | bytes 1572872 | tf_op jit(solution)/shard_map/ppermute | solution.py:571
  59.6 22.9 %collective-permute-start.6 = (bf16[128,2048]{1,0:T(8,128)(2,1)}, bf16[128,2048]{1,0:T(8,128)(2,1)S(1)}, u32[]{:S(2)}, u32[]{:S(2)}) collective-permute-start(bf16[128,2048]{1,0:T(8,128)(2,1)} %bitcast.10.b0), channel_id=1, source_target_pairs={{0,8},{4,12},{8,0},{12,4},{1,9},{5,13},{9,1},{13,5},{2,10},{6,14},... | collective-permute-start | bytes 1572872 | tf_op jit(solution)/shard_map/ppermute | solution.py:571
  63.1 24.5 %collective-permute-start.10 = (bf16[128,2048]{1,0:T(8,128)(2,1)S(1)}, bf16[128,2048]{1,0:T(8,128)(2,1)S(1)}, u32[]{:S(2)}, u32[]{:S(2)}) collective-permute-start(bf16[128,2048]{1,0:T(8,128)(2,1)S(1)} %broadcast_select_fusion.1), channel_id=1, source_target_pairs={{0,2},{1,3},{2,0},{3,1},{4,6},{5,7},{6,4},{7,5},{8,10},{9,11},{10,... | collective-permute-start | bytes 1572872 | tf_op jit(solution)/shard_map/ppermute | solution.py:595
  63.6 25.7 %collective-permute-start.11 = (bf16[128,2048]{1,0:T(8,128)(2,1)}, bf16[128,2048]{1,0:T(8,128)(2,1)S(1)}, u32[]{:S(2)}, u32[]{:S(2)}) collective-permute-start(bf16[128,2048]{1,0:T(8,128)(2,1)} %select_select_fusion.2), channel_id=1, source_target_pairs={{0,2},{1,3},{2,0},{3,1},{4,6},{5,7},{6,4},{7,5},{8,10},{9,11},{10,... | collective-permute-start | bytes 1572872 | tf_op jit(solution)/shard_map/ppermute | solution.py:597
  82.6 21.9 %copy-start.32 = (bf16[128,2048]{1,0:T(8,128)(2,1)}, bf16[128,2048]{1,0:T(8,128)(2,1)S(1)}, u32[]{:S(2)}) copy-start(bf16[128,2048]{1,0:T(8,128)(2,1)S(1)} %collective-permute-done.7.b1) | copy-start | bytes 1572868
  82.6 21.9 %copy-start.29 = (bf16[128,2048]{1,0:T(8,128)(2,1)}, bf16[128,2048]{1,0:T(8,128)(2,1)S(1)}, u32[]{:S(2)}) copy-start(bf16[128,2048]{1,0:T(8,128)(2,1)S(1)} %collective-permute-done.6.b3.b4) | copy-start | bytes 1572868
  82.6 21.9 %collective-permute-start.8 = (bf16[128,2048]{1,0:T(8,128)(2,1)}, bf16[128,2048]{1,0:T(8,128)(2,1)S(1)}, u32[]{:S(2)}, u32[]{:S(2)}) collective-permute-start(bf16[128,2048]{1,0:T(8,128)(2,1)} %bitcast.10.b0), channel_id=1, source_target_pairs={{0,1},{1,0},{2,3},{3,2},{4,8},{5,9},{6,10},{7,11},{8,4},{9,5},{10,... | collective-permute-start | bytes 1572872 | tf_op jit(solution)/shard_map/ppermute | solution.py:574
  82.7 21.8 %collective-permute-start.9 = (bf16[128,2048]{1,0:T(8,128)(2,1)S(1)}, bf16[128,2048]{1,0:T(8,128)(2,1)S(1)}, u32[]{:S(2)}, u32[]{:S(2)}) collective-permute-start(bf16[128,2048]{1,0:T(8,128)(2,1)S(1)} %collective-permute-done.6.b3.b4), channel_id=1, source_target_pairs={{0,4},{4,0},{8,12},{12,8},{1,5},{5,1},{9,13},{13,9},{2,6},{6,2},{1... | collective-permute-start | bytes 1572872 | tf_op jit(solution)/shard_map/ppermute | solution.py:575
  87.7 22.0 %collective-permute-start.15 = (bf16[128,2048]{1,0:T(8,128)(2,1)}, bf16[128,2048]{1,0:T(8,128)(2,1)S(1)}, u32[]{:S(2)}, u32[]{:S(2)}) collective-permute-start(bf16[128,2048]{1,0:T(8,128)(2,1)} %broadcast_select_fusion.2), channel_id=1, source_target_pairs={{0,2},{1,3},{2,0},{3,1},{4,6},{5,7},{6,4},{7,5},{8,10},{9,11},{10,... | collective-permute-start | bytes 1572872 | tf_op jit(solution)/shard_map/ppermute | solution.py:602
  104.5 12.4 %copy-start.36 = (bf16[128,2048]{1,0:T(8,128)(2,1)}, bf16[128,2048]{1,0:T(8,128)(2,1)S(1)}, u32[]{:S(2)}) copy-start(bf16[128,2048]{1,0:T(8,128)(2,1)S(1)} %collective-permute-done.9.b5) | copy-start | bytes 1572868
  104.5 12.4 %copy-start.35 = (bf16[128,2048]{1,0:T(8,128)(2,1)}, bf16[128,2048]{1,0:T(8,128)(2,1)S(1)}, u32[]{:S(2)}) copy-start(bf16[128,2048]{1,0:T(8,128)(2,1)S(1)} %collective-permute-done.8.b2) | copy-start | bytes 1572868
  104.6 11.8 %collective-permute-start.16 = (bf16[128,2048]{1,0:T(8,128)(2,1)S(1)}, bf16[128,2048]{1,0:T(8,128)(2,1)S(1)}, u32[]{:S(2)}, u32[]{:S(2)}) collective-permute-start(bf16[128,2048]{1,0:T(8,128)(2,1)S(1)} %select_select_fusion.1), channel_id=1, source_target_pairs={{0,2},{1,3},{2,0},{3,1},{4,6},{5,7},{6,4},{7,5},{8,10},{9,11},{10,... | collective-permute-start | bytes 1572872 | tf_op jit(solution)/shard_map/ppermute | solution.py:608
  105.1 26.6 %collective-permute-start.14 = (bf16[128,2048]{1,0:T(8,128)(2,1)}, bf16[128,2048]{1,0:T(8,128)(2,1)S(1)}, u32[]{:S(2)}, u32[]{:S(2)}) collective-permute-start(bf16[128,2048]{1,0:T(8,128)(2,1)} %bitcast.9.b0), channel_id=1, source_target_pairs={{0,4},{4,0},{8,12},{12,8},{1,5},{5,1},{9,13},{13,9},{2,6},{6,2},{1... | collective-permute-start | bytes 1572872 | tf_op jit(solution)/shard_map/ppermute | solution.py:571
  105.2 26.6 %collective-permute-start.13 = (bf16[128,2048]{1,0:T(8,128)(2,1)}, bf16[128,2048]{1,0:T(8,128)(2,1)}, u32[]{:S(2)}, u32[]{:S(2)}) collective-permute-start(bf16[128,2048]{1,0:T(8,128)(2,1)} %bitcast.9.b0), channel_id=1, source_target_pairs={{0,8},{4,12},{8,0},{12,4},{1,9},{5,13},{9,1},{13,5},{2,10},{6,14},... | collective-permute-start | bytes 1572872 | tf_op jit(solution)/shard_map/ppermute | solution.py:571
  116.5 28.0 %collective-permute-start.19 = (bf16[3584,128]{1,0:T(8,128)(2,1)}, bf16[3584,128]{1,0:T(8,128)(2,1)}, u32[]{:S(2)}, u32[]{:S(2)}) collective-permute-start(bf16[3584,128]{1,0:T(8,128)(2,1)} %get-tuple-element.55), channel_id=1, source_target_pairs={{0,2},{1,3},{2,0},{3,1},{4,6},{5,7},{6,4},{7,5},{8,10},{9,11},{10,... | collective-permute-start | bytes 2752520 | tf_op jit(solution)/shard_map/ppermute | solution.py:609
  117.3 22.9 %copy-start.19 = (bf16[128,3584]{1,0:T(8,128)(2,1)S(1)}, bf16[128,3584]{1,0:T(8,128)(2,1)}, u32[]{:S(2)}) copy-start(bf16[128,3584]{1,0:T(8,128)(2,1)} %copy-done.18) | copy-start | bytes 2752516
  133.2 16.8 %collective-permute-start.20 = (bf16[128,2048]{1,0:T(8,128)(2,1)S(1)}, bf16[128,2048]{1,0:T(8,128)(2,1)S(1)}, u32[]{:S(2)}, u32[]{:S(2)}) collective-permute-start(bf16[128,2048]{1,0:T(8,128)(2,1)S(1)} %broadcast_select_fusion), channel_id=1, source_target_pairs={{0,2},{1,3},{2,0},{3,1},{4,6},{5,7},{6,4},{7,5},{8,10},{9,11},{10,... | collective-permute-start | bytes 1572872 | tf_op jit(solution)/shard_map/ppermute | solution.py:614
  134.5 15.5 %collective-permute-start.17 = (bf16[128,2048]{1,0:T(8,128)(2,1)}, bf16[128,2048]{1,0:T(8,128)(2,1)S(1)}, u32[]{:S(2)}, u32[]{:S(2)}) collective-permute-start(bf16[128,2048]{1,0:T(8,128)(2,1)} %bitcast.9.b0), channel_id=1, source_target_pairs={{0,1},{1,0},{2,3},{3,2},{4,8},{5,9},{6,10},{7,11},{8,4},{9,5},{10,... | collective-permute-start | bytes 1572872 | tf_op jit(solution)/shard_map/ppermute | solution.py:574
  134.5 16.4 %collective-permute-start.18 = (bf16[128,2048]{1,0:T(8,128)(2,1)}, bf16[128,2048]{1,0:T(8,128)(2,1)S(1)}, u32[]{:S(2)}, u32[]{:S(2)}) collective-permute-start(bf16[128,2048]{1,0:T(8,128)(2,1)} %collective-permute-done.13.b3.b4), channel_id=1, source_target_pairs={{0,4},{4,0},{8,12},{12,8},{1,5},{5,1},{9,13},{13,9},{2,6},{6,2},{1... | collective-permute-start | bytes 1572872 | tf_op jit(solution)/shard_map/ppermute | solution.py:575
  150.0 22.9 %copy-start.37 = (bf16[128,2048]{1,0:T(8,128)(2,1)}, bf16[128,2048]{1,0:T(8,128)(2,1)S(1)}, u32[]{:S(2)}) copy-start(bf16[128,2048]{1,0:T(8,128)(2,1)S(1)} %collective-permute-done.20.far_a) | copy-start | bytes 1572868
  150.0 27.3 %copy-start.27 = (s32[2]{0:T(128)S(1)}, s32[2]{0:T(128)}, u32[]{:S(2)}) copy-start(s32[2]{0:T(128)} %lengths.2) | copy-start | bytes 28
  150.0 22.8 %copy-start.33 = (bf16[128,2048]{1,0:T(8,128)(2,1)}, bf16[128,2048]{1,0:T(8,128)(2,1)S(1)}, u32[]{:S(2)}) copy-start(bf16[128,2048]{1,0:T(8,128)(2,1)S(1)} %collective-permute-done.17.b2) | copy-start | bytes 1572868
  150.9 21.9 %copy-start.34 = (bf16[128,2048]{1,0:T(8,128)(2,1)}, bf16[128,2048]{1,0:T(8,128)(2,1)S(1)}, u32[]{:S(2)}) copy-start(bf16[128,2048]{1,0:T(8,128)(2,1)S(1)} %collective-permute-done.18.b5) | copy-start | bytes 1572868
  151.1 20.6 %collective-permute-start.27 = (bf16[128,2048]{1,0:T(8,128)(2,1)S(1)}, bf16[128,2048]{1,0:T(8,128)(2,1)S(1)}, u32[]{:S(2)}, u32[]{:S(2)}) collective-permute-start(bf16[128,2048]{1,0:T(8,128)(2,1)S(1)} %select_select_fusion), channel_id=1, source_target_pairs={{0,2},{1,3},{2,0},{3,1},{4,6},{5,7},{6,4},{7,5},{8,10},{9,11},{10,... | collective-permute-start | bytes 1572872 | tf_op jit(solution)/shard_map/ppermute | solution.py:621
  152.3 9.8 %collective-permute-start.26 = (f32[128,320]{1,0:T(8,128)S(1)}, f32[128,320]{1,0:T(8,128)S(1)}, u32[]{:S(2)}, u32[]{:S(2)}) collective-permute-start(f32[128,320]{1,0:T(8,128)S(1)} %pad_maximum_fusion), channel_id=1, source_target_pairs={{0,12},{4,8},{8,4},{12,0},{1,13},{5,9},{9,5},{13,1},{2,14},{6,10},... | collective-permute-start | bytes 491528 | tf_op jit(solution)/shard_map/ppermute | solution.py:546
  155.5 16.1 %collective-permute-start.25 = (f32[128,320]{1,0:T(8,128)S(1)}, f32[128,320]{1,0:T(8,128)S(1)}, u32[]{:S(2)}, u32[]{:S(2)}) collective-permute-start(f32[128,320]{1,0:T(8,128)S(1)} %pad_maximum_fusion), channel_id=1, source_target_pairs={{0,8},{4,12},{8,0},{12,4},{1,9},{5,13},{9,1},{13,5},{2,10},{6,14},... | collective-permute-start | bytes 491528 | tf_op jit(solution)/shard_map/ppermute | solution.py:546
  156.1 15.5 %collective-permute-start.24 = (f32[128,320]{1,0:T(8,128)S(1)}, f32[128,320]{1,0:T(8,128)S(1)}, u32[]{:S(2)}, u32[]{:S(2)}) collective-permute-start(f32[128,320]{1,0:T(8,128)S(1)} %pad_maximum_fusion), channel_id=1, source_target_pairs={{0,4},{4,0},{8,12},{12,8},{1,5},{5,1},{9,13},{13,9},{2,6},{6,2},{1... | collective-permute-start | bytes 491528 | tf_op jit(solution)/shard_map/ppermute | solution.py:546
  171.6 28.3 %collective-permute-start.28 = (bf16[3584,128]{1,0:T(8,128)(2,1)}, bf16[3584,128]{1,0:T(8,128)(2,1)S(1)}, u32[]{:S(2)}, u32[]{:S(2)}) collective-permute-start(bf16[3584,128]{1,0:T(8,128)(2,1)} %get-tuple-element.63), channel_id=1, source_target_pairs={{0,2},{1,3},{2,0},{3,1},{4,6},{5,7},{6,4},{7,5},{8,10},{9,11},{10,... | collective-permute-start | bytes 2752520 | tf_op jit(solution)/shard_map/ppermute | solution.py:624
  172.9 23.2 %collective-permute-start.23 = (f32[256,128]{1,0:T(8,128)S(1)}, f32[256,128]{1,0:T(8,128)}, u32[]{:S(2)}, u32[]{:S(2)}) collective-permute-start(f32[256,128]{1,0:T(8,128)S(1)} %slice.36), channel_id=1, source_target_pairs={{0,12},{4,8},{8,4},{12,0},{1,13},{5,9},{9,5},{13,1},{2,14},{6,10},... | collective-permute-start | bytes 393224 | tf_op jit(solution)/shard_map/ppermute | solution.py:546
  175.6 21.5 %collective-permute-start.22 = (f32[256,128]{1,0:T(8,128)S(1)}, f32[256,128]{1,0:T(8,128)}, u32[]{:S(2)}, u32[]{:S(2)}) collective-permute-start(f32[256,128]{1,0:T(8,128)S(1)} %slice.36), channel_id=1, source_target_pairs={{0,8},{4,12},{8,0},{12,4},{1,9},{5,13},{9,1},{13,5},{2,10},{6,14},... | collective-permute-start | bytes 393224 | tf_op jit(solution)/shard_map/ppermute | solution.py:546
  175.6 22.4 %collective-permute-start.21 = (f32[256,128]{1,0:T(8,128)S(1)}, f32[256,128]{1,0:T(8,128)}, u32[]{:S(2)}, u32[]{:S(2)}) collective-permute-start(f32[256,128]{1,0:T(8,128)S(1)} %slice.36), channel_id=1, source_target_pairs={{0,4},{4,0},{8,12},{12,8},{1,5},{5,1},{9,13},{13,9},{2,6},{6,2},{1... | collective-permute-start | bytes 393224 | tf_op jit(solution)/shard_map/ppermute | solution.py:546
  178.3 26.1 %collective-permute-start.30 = (f32[2,192,64]{2,1,0:T(8,128)S(1)}, f32[2,192,64]{2,1,0:T(8,128)S(1)}, u32[]{:S(2)}, u32[]{:S(2)}) collective-permute-start(f32[2,192,64]{2,1,0:T(8,128)S(1)} %shard_map.161.q0), channel_id=1, source_target_pairs={{0,1},{1,0},{2,3},{3,2},{4,5},{5,4},{6,7},{7,6},{8,9},{9,8},{10,11... | collective-permute-start | bytes 294920 | tf_op jit(solution)/shard_map/ppermute | solution.py:627
  178.4 21.6 %copy-start.6 = (bf16[64,3584]{1,0:T(8,128)(2,1)S(1)}, bf16[64,3584]{1,0:T(8,128)(2,1)}, u32[]{:S(2)}) copy-start(bf16[64,3584]{1,0:T(8,128)(2,1)} %proj_gate.5) | copy-start | bytes 1376260
  178.4 21.6 %copy-start.8 = (bf16[64,3584]{1,0:T(8,128)(2,1)S(1)}, bf16[64,3584]{1,0:T(8,128)(2,1)}, u32[]{:S(2)}) copy-start(bf16[64,3584]{1,0:T(8,128)(2,1)} %proj_up.5) | copy-start | bytes 1376260
  196.1 8.3 %collective-permute-start.31 = (f32[2,192,64]{2,1,0:T(8,128)S(1)}, f32[2,192,64]{2,1,0:T(8,128)S(1)}, u32[]{:S(2)}, u32[]{:S(2)}) collective-permute-start(f32[2,192,64]{2,1,0:T(8,128)S(1)} %shard_map.161.q0), channel_id=1, source_target_pairs={{0,2},{1,3},{2,0},{3,1},{4,6},{5,7},{6,4},{7,5},{8,10},{9,11},{10,... | collective-permute-start | bytes 294920 | tf_op jit(solution)/shard_map/ppermute | solution.py:627
  197.1 10.1 %collective-permute-start.32 = (f32[2,192,64]{2,1,0:T(8,128)S(1)}, f32[2,192,64]{2,1,0:T(8,128)S(1)}, u32[]{:S(2)}, u32[]{:S(2)}) collective-permute-start(f32[2,192,64]{2,1,0:T(8,128)S(1)} %shard_map.161.q0), channel_id=1, source_target_pairs={{0,3},{1,2},{2,1},{3,0},{4,7},{5,6},{6,5},{7,4},{8,11},{9,10},{10,... | collective-permute-start | bytes 294920 | tf_op jit(solution)/shard_map/ppermute | solution.py:627
  198.0 11.1 %collective-permute-start.29 = (f32[128,128]{1,0:T(8,128)}, f32[128,128]{1,0:T(8,128)S(1)}, u32[]{:S(2)}, u32[]{:S(2)}) collective-permute-start(f32[128,128]{1,0:T(8,128)} %get-tuple-element.66), channel_id=1, source_target_pairs={{0,2},{1,3},{2,0},{3,1},{4,6},{5,7},{6,4},{7,5},{8,10},{9,11},{10,... | collective-permute-start | bytes 196616 | tf_op jit(solution)/shard_map/ppermute | solution.py:635
  210.5 5.4 %collective-permute-start.35 = (f32[4,8]{1,0:T(4,128)S(1)}, f32[4,8]{1,0:T(4,128)S(1)}, u32[]{:S(2)}, u32[]{:S(2)}) collective-permute-start(f32[4,8]{1,0:T(4,128)S(1)} %shard_map.162), channel_id=1, source_target_pairs={{0,12},{4,8},{8,4},{12,0},{1,13},{5,9},{9,5},{13,1},{2,14},{6,10},... | collective-permute-start | bytes 392 | tf_op jit(solution)/shard_map/ppermute | solution.py:546
  213.2 4.5 %collective-permute-start.34 = (f32[4,8]{1,0:T(4,128)S(1)}, f32[4,8]{1,0:T(4,128)S(1)}, u32[]{:S(2)}, u32[]{:S(2)}) collective-permute-start(f32[4,8]{1,0:T(4,128)S(1)} %shard_map.162), channel_id=1, source_target_pairs={{0,8},{4,12},{8,0},{12,4},{1,9},{5,13},{9,1},{13,5},{2,10},{6,14},... | collective-permute-start | bytes 392 | tf_op jit(solution)/shard_map/ppermute | solution.py:546
  213.2 4.5 %collective-permute-start.33 = (f32[4,8]{1,0:T(4,128)S(1)}, f32[4,8]{1,0:T(4,128)S(1)}, u32[]{:S(2)}, u32[]{:S(2)}) collective-permute-start(f32[4,8]{1,0:T(4,128)S(1)} %shard_map.162), channel_id=1, source_target_pairs={{0,4},{4,0},{8,12},{12,8},{1,5},{5,1},{9,13},{13,9},{2,6},{6,2},{1... | collective-permute-start | bytes 392 | tf_op jit(solution)/shard_map/ppermute | solution.py:546
  (31 other events, 101.2 us)

commit v9 on v8

--- a/solution.py
+++ b/solution.py
@@ -545,9 +545,6 @@
     def tensor_sum(values):
         return values + outer(values) + across(values) + opposite(values)
 
-    def first_hops(own):
-        return own, outer(own), across(own)
-
     def last_hops(own, one, two):
         mid = middle(after(own, two))
         return own, one, mid, two, two, outer(after(two, one))
@@ -584,45 +581,55 @@
         )
 
     weight_own, weight_sib = down_weight, to_core(down_weight)
-    q_own, q_one, q_two = first_hops(q_outgrad)
+    q_own, q_one, q_two = q_outgrad, outer(q_outgrad), across(q_outgrad)
     far_gate = to_chip(t_gate[cut:])
     own_in_out, hidden = early_sides(
         t_input, q_input, t_outgrad, q_outgrad, proj_input, proj_outgrad, t_gate, t_up, q_gate,
         q_up, proj_hidden,
     )
     q_blocks = last_hops(q_own, q_one, after(q_two, own_in_out, far_gate))
+    q_first = to_chip(crossing_first(q_own, q_blocks[3]))
+    q_send = crossing_second(q_one, q_blocks[2], q_blocks[5])
+    q_far = (q_first, to_chip(q_send))
+
     far_up = to_chip(after(t_up[cut:], far_gate))
-    q_first = to_chip(crossing_first(q_own, q_blocks[3]))
-    q_send = after(crossing_second(q_one, q_blocks[2], q_blocks[5]), far_up)
-    q_far = (q_first, to_chip(q_send))
-
-    a_own, a_one, a_two = first_hops(after(t_outgrad[:cut], q_send))
-    a_two = after(a_two, a_one)
+    a_own = after(t_outgrad[:cut], q_send)
+    a_one, a_two = outer(a_own), across(a_own)
+    a_two = after(a_two, a_one, far_up, *q_far)
     a_cross = crossing_first(a_own, a_two)
     a_first = to_chip(a_cross)
     a_blocks = last_hops(a_own, a_one, a_two)
     q_near_sum, q_far_sum = partial_sums(
         after(flags, a_cross), q_blocks, q_far, weight_own, weight_sib
     )
-    a_send = crossing_second(a_one, a_blocks[2], after(a_blocks[5], q_far_sum))
+    a_send = crossing_second(a_one, a_blocks[2], after(a_blocks[5], q_far_sum, a_first))
     a_far = (a_first, to_chip(a_send))
     q_returned = to_chip(after(q_far_sum, *a_far))
 
-    b_own, b_one, b_two = first_hops(after(t_outgrad[cut:], a_send))
-    a_near_sum, a_far_sum = partial_sums(flags, a_blocks, a_far, weight_own, weight_sib)
-    b_two = after(b_two, b_one, a_far_sum)
-    b_first = to_chip(crossing_first(b_own, b_two))
+    b_own = t_outgrad[cut:]
+    b_two = across(after(b_own, a_two))
+    b_one = outer(after(b_own, a_send))
+    q_hidden = hidden[2 * cut :]
+    pair_in_out = own_in_out + outer(after(own_in_out, a_send))
+    pair_hidden = q_hidden + outer(after(q_hidden, a_send))
+    b_two = after(b_two, b_one, pair_in_out, pair_hidden)
+    b_cross = crossing_first(b_own, b_two)
+    b_first = to_chip(b_cross)
     b_blocks = last_hops(b_own, b_one, b_two)
+    a_near_sum, a_far_sum = partial_sums(
+        after(flags, b_cross), a_blocks, a_far, weight_own, weight_sib
+    )
+    in_out = pair_in_out + across(after(pair_in_out, a_far_sum))
+    whole_hidden = pair_hidden + across(after(pair_hidden, a_far_sum))
     q_gradient = finished_sides(q_near_sum, q_returned, q_gate, q_up, proj_gate, proj_up)
     gates, ups = turned(t_gate, t_up, after(far_gate, a_far_sum), far_up)
     b_send = crossing_second(
-        after(b_one, q_gradient, b_first, gates), b_blocks[2], b_blocks[5]
+        after(b_one, q_gradient, b_first, gates, in_out, whole_hidden), b_blocks[2], b_blocks[5]
     )
     b_far = (b_first, to_chip(b_send))
-    q_sums = jnp.concatenate([q_gradient, hidden[2 * cut :], own_in_out[2 * cut :]], axis=1)
-    q_sums = tensor_sum(after(q_sums, b_send))
+    q_sums = tensor_sum(after(q_gradient, b_send))
     a_returned = to_chip(after(a_far_sum, q_sums, *b_far))
-    in_out = tensor_sum(after(own_in_out[: 2 * cut], b_send))
+    q_sums = jnp.concatenate([q_sums, whole_hidden, in_out[2 * cut :]], axis=1)
     own_found = query_features(query_lengths, q_sums)
     found = (own_found, to_core(own_found), to_chip(own_found), to_other(own_found))
     b_near, b_away = lent_sides(
@@ -631,7 +638,7 @@
     )
     a_gradient = finished_sides(a_near_sum, a_returned, t_gate, t_up, proj_gate, proj_up)
     own_scores = partial_scores(
-        train_lengths, place, in_out, hidden[: 2 * cut], a_gradient, b_near,
+        train_lengths, place, in_out[: 2 * cut], hidden[: 2 * cut], a_gradient, b_near,
         to_chip(b_away), found,
     )
     return tensor_sum(own_scores) / (RANK * SEQ)

time: 219 us -> 228 us (1.041)
  starting transfers between devices: 50.7 us -> 54.6 us
  waiting for transfers between devices: 73.3 us -> 76 us
    ppermute x7 -> x11, starting transfers between devices: 14 us -> 25.2 us  [the longest x1 9.72 us: moving_plan(): b_one = outer(after(b_own, a_send))]
    ppermute x9 -> x6, waiting for transfers between devices: 17.6 us -> 6.74 us  [tensor_sum(): return values + outer(values) + across(values) + opposite(values)]
    ppermute x7 -> x11, waiting for transfers between devices: 24.5 us -> 34.8 us  [the longest x1 14.4 us: moving_plan(): pair_hidden = q_hidden + outer(after(q_hidden, a_send))]
    ppermute x1, waiting for transfers between devices: 8.61 us -> 17.9 us  [moving_plan(): far_up = to_chip(after(t_up[cut:], far_gate))]
    ppermute x1, waiting for transfers between devices: 6.79 us -> 0.01 us  [moving_plan(): a_far = (a_first, to_chip(a_send))]
    ppermute x3, starting transfers between devices: 9.84 us -> 4.49 us  [last_hops(): return (own, one, mid, two, two, outer(after(two, one)))]
    ppermute x3, waiting for transfers between devices: 11.1 us -> 5.83 us  [last_hops(): return (own, one, mid, two, two, outer(after(two, one)))]
    ppermute x1, waiting for transfers between devices: 0.01 us -> 4.6 us  [moving_plan(): q_far = (q_first, to_chip(q_send))]
  transfers between devices with their start and end apart: 36 -> 37, of which waited for: 12 -> 17; matrix products, arithmetic and copies ran while one was open for 5% -> 6% of each run, Pallas kernels for 29% -> 28%
where the time goes in v9:
time: 228 us; the launch traced here: 227 us
  waiting for transfers between devices  76 us (33%)
  Pallas kernels  65.7 us (29%)
  starting transfers between devices  54.6 us (24%)
  local copies, waits for them, and re-layouts  20.7 us (9%)
  other arithmetic  9.76 us (4%)
    pallas_call x2, Pallas kernels, partial_sums(): pl.pallas_call(partial_kernel, grid=(units // TILE,), in_specs=[SCALARS]...  28.8 us
    ppermute x1, waiting for transfers between devices, moving_plan(): far_up = to_chip(after(t_up[cut:], far_gate))  17.9 us
    pallas_call x1, Pallas kernels, lent_sides(): pl.pallas_call(lent_kernel, grid=(units // TILE,), in_specs=[SCALARS] + [...  17.6 us
    ppermute x1, waiting for transfers between devices, moving_plan(): pair_hidden = q_hidden + outer(after(q_hidden, a_send))  14.4 us
    unnamed x72, local copies, waits for them, and re-layouts  14.3 us
    ppermute x1, starting transfers between devices, moving_plan(): b_one = outer(after(b_own, a_send))  9.72 us
    ppermute x6, starting transfers between devices, tensor_sum(): return values + outer(values) + across(values) + opposite(values)  8.84 us
    pallas_call x2, Pallas kernels, finished_sides(): pl.pallas_call(finish_kernel, grid=(units // TILE,), in_specs=[tile_rows(...  7.97 us
  transfers between devices with their start and end apart: 37, of which 17 were waited for; matrix products, arithmetic and copies ran while one was open for 6% of the time, Pallas kernels for 28%

profile of v9, /device:TPU:0, one launch (start us, length us, event | category | flops | bytes accessed | tf_op | source)
XLA Modules:
  0.0 227.2 jit_solution(50725991452167467)
XLA Ops:
  0.5 2.3 %slice.38 = bf16[2,64,3584]{2,1,0:T(8,128)(2,1)} slice(bf16[4,64,3584]{2,1,0:T(8,128)(2,1)} %param.17), slice={[2:4], [0:64], [0:3584]} | slice | bytes 1835008 | tf_op jit(solution)/shard_map/slice | solution.py:585
  2.7 2.5 %collective-permute-start.1 = (bf16[128,3584]{1,0:T(8,128)(2,1)}, bf16[128,3584]{1,0:T(8,128)(2,1)}, u32[]{:S(2)}, u32[]{:S(2)}) collective-permute-start(bf16[128,3584]{1,0:T(8,128)(2,1)} %bitcast.10), channel_id=1, source_target_pairs={{0,2},{1,3},{2,0},{3,1},{4,6},{5,7},{6,4},{7,5},{8,10},{9,11},{10,... | collective-permute-start | bytes 2752520 | tf_op jit(solution)/shard_map/ppermute | solution.py:585
  5.3 2.6 %collective-permute-start = (bf16[128,2048]{1,0:T(8,128)(2,1)}, bf16[128,2048]{1,0:T(8,128)(2,1)}, u32[]{:S(2)}, u32[]{:S(2)}) collective-permute-start(bf16[128,2048]{1,0:T(8,128)(2,1)} %bitcast.24), channel_id=1, source_target_pairs={{0,8},{4,12},{8,0},{12,4},{1,9},{5,13},{9,1},{13,5},{2,10},{6,14},... | collective-permute-start | bytes 1572872 | tf_op jit(solution)/shard_map/ppermute | solution.py:584
  7.9 1.6 collective-permute-start.3
  9.4 1.5 copy-done.1
  20.8 3.8 %shard_map.154 = (f32[384,128]{1,0:T(8,128)S(1)}, f32[384,64]{1,0:T(8,128)S(1)}) custom-call(bf16[256,2048]{1,0:T(8,128)(2,1)S(1)} %bitcast.34, bf16[128,2048]{1,0:T(8,128)(2,1)S(1)} %bitcast.35, bf16[256,2048]{1,0:T(8,128)(2,1)S(1)} %bitcast.29, bf16[128,2048]{1,0:T(8,128)(2,1)S(1)} %bitcast.27, bf16[64,2048]{1,0:T(8,128)(2,1)S(1)} %copy-done.24, ...), custom_call_target="tpu_custom_call" | custom-call | flops 1024 | bytes 1024 | tf_op jit(solution)/shard_map/pallas_call | solution.py:392
  26.0 5.8 %collective-permute-done.b3.b4 = bf16[128,2048]{1,0:T(8,128)(2,1)} collective-permute-done((bf16[128,2048]{1,0:T(8,128)(2,1)}, bf16[128,2048]{1,0:T(8,128)(2,1)}, u32[]{:S(2)}, u32[]{:S(2)}) %collective-permute-start) | collective-permute-done | bytes 524320 | tf_op jit(solution)/shard_map/ppermute | solution.py:584
  31.9 1.4 collective-permute-start.4
  33.4 1.9 broadcast_select_fusion.2
  36.4 2.2 slice.40
  38.5 2.0 collective-permute-start.7
  40.6 5.8 %collective-permute-done.4.b5 = bf16[128,2048]{1,0:T(8,128)(2,1)} collective-permute-done((bf16[128,2048]{1,0:T(8,128)(2,1)}, bf16[128,2048]{1,0:T(8,128)(2,1)}, u32[]{:S(2)}, u32[]{:S(2)}) %collective-permute-start.4) | collective-permute-done | bytes 524320 | tf_op jit(solution)/shard_map/ppermute | solution.py:572
  47.9 3.8 %collective-permute-start.5 = (bf16[128,2048]{1,0:T(8,128)(2,1)}, bf16[128,2048]{1,0:T(8,128)(2,1)S(1)}, u32[]{:S(2)}, u32[]{:S(2)}) collective-permute-start(bf16[128,2048]{1,0:T(8,128)(2,1)} %bitcast.9.b0), channel_id=1, source_target_pairs={{0,8},{4,12},{8,0},{12,4},{1,9},{5,13},{9,1},{13,5},{2,10},{6,14},... | collective-permute-start | bytes 1572872 | tf_op jit(solution)/shard_map/ppermute | solution.py:597
  52.1 17.9 %collective-permute-done.7.far_up = bf16[128,3584]{1,0:T(8,128)(2,1)S(1)} collective-permute-done((bf16[128,3584]{1,0:T(8,128)(2,1)}, bf16[128,3584]{1,0:T(8,128)(2,1)S(1)}, u32[]{:S(2)}, u32[]{:S(2)}) %collective-permute-start.7) | collective-permute-done | bytes 917536 | tf_op jit(solution)/shard_map/ppermute | solution.py:595
  70.0 2.3 collective-permute-done.6.b1
  72.3 2.4 %collective-permute-done.5.b3.b4 = bf16[128,2048]{1,0:T(8,128)(2,1)S(1)} collective-permute-done((bf16[128,2048]{1,0:T(8,128)(2,1)}, bf16[128,2048]{1,0:T(8,128)(2,1)S(1)}, u32[]{:S(2)}, u32[]{:S(2)}) %collective-permute-start.5) | collective-permute-done | bytes 524320 | tf_op jit(solution)/shard_map/ppermute | solution.py:597
  74.7 4.6 %collective-permute-done.9.far_b = bf16[128,2048]{1,0:T(8,128)(2,1)} collective-permute-done((bf16[128,2048]{1,0:T(8,128)(2,1)S(1)}, bf16[128,2048]{1,0:T(8,128)(2,1)}, u32[]{:S(2)}, u32[]{:S(2)}) %collective-permute-start.9) | collective-permute-done | bytes 524320 | tf_op jit(solution)/shard_map/ppermute | solution.py:593
  80.2 1.7 collective-permute-start.11
  81.9 1.3 collective-permute-start.13
  83.8 1.8 collective-permute-start.15
  85.6 14.4 %shard_map.155 = (f32[3584,128]{1,0:T(8,128)}, bf16[3584,128]{1,0:T(8,128)(2,1)}) custom-call(s32[3]{0:T(128)} %pad_add_fusion.flags, bf16[128,2048]{1,0:T(8,128)(2,1)} %bitcast.26, bf16[128,2048]{1,0:T(8,128)(2,1)} %collective-permute-done.3.b1, bf16[128,2048]{1,0:T(8,128)(2,1)} %collective-permute-done.2.b2, bf16[128,2048]{1,0:T(8,128)(2,1)} %collective-permute-done.b3.b4, ...), custom_call_target="tpu_custom_call" | custom-call | flops 1024 | bytes 1024 | tf_op jit(solution)/shard_map/pallas_call | solution.py:247
  101.3 9.7 %collective-permute-start.16 = (bf16[128,2048]{1,0:T(8,128)(2,1)}, bf16[128,2048]{1,0:T(8,128)(2,1)}, u32[]{:S(2)}, u32[]{:S(2)}) collective-permute-start(bf16[128,2048]{1,0:T(8,128)(2,1)} %bitcast.15.b0), channel_id=1, source_target_pairs={{0,4},{4,0},{8,12},{12,8},{1,5},{5,1},{9,13},{13,9},{2,6},{6,2},{1... | collective-permute-start | bytes 1572872 | tf_op jit(solution)/shard_map/ppermute | solution.py:611
  111.0 1.2 collective-permute-start.18
  112.4 1.9 collective-permute-start.14
  114.4 14.4 %collective-permute-done.17 = f32[128,64]{1,0:T(8,128)S(1)} collective-permute-done((f32[128,64]{1,0:T(8,128)S(1)}, f32[128,64]{1,0:T(8,128)S(1)}, u32[]{:S(2)}, u32[]{:S(2)}) %collective-permute-start.17) | collective-permute-done | bytes 32800 | tf_op jit(solution)/shard_map/ppermute | solution.py:614
  128.7 2.1 collective-permute-done.14
  130.9 2.2 collective-permute-start.20
  133.1 2.1 broadcast_select_fusion
  135.3 1.4 collective-permute-start.22
  136.6 14.4 %shard_map.156 = (f32[3584,128]{1,0:T(8,128)}, bf16[3584,128]{1,0:T(8,128)(2,1)}) custom-call(s32[3]{0:T(128)} %pad_add_fusion.flags, bf16[128,2048]{1,0:T(8,128)(2,1)} %bitcast.9.b0, bf16[128,2048]{1,0:T(8,128)(2,1)} %copy-done.32, bf16[128,2048]{1,0:T(8,128)(2,1)} %collective-permute-done.10.b2, bf16[128,2048]{1,0:T(8,128)(2,1)} %copy-done.31, ...), custom_call_target="tpu_custom_call" | custom-call | flops 1024 | bytes 1024 | tf_op jit(solution)/shard_map/pallas_call | solution.py:247
  151.1 2.0 collective-permute-start.24
  153.1 4.0 %collective-permute-done.24 = f32[128,64]{1,0:T(8,128)S(1)} collective-permute-done((f32[128,64]{1,0:T(8,128)S(1)}, f32[128,64]{1,0:T(8,128)S(1)}, u32[]{:S(2)}, u32[]{:S(2)}) %collective-permute-start.24) | collective-permute-done | bytes 32800 | tf_op jit(solution)/shard_map/ppermute | solution.py:623
  158.3 4.6 %shard_map.158 = (bf16[3584,256]{1,0:T(8,128)(2,1)S(1)}, bf16[3584,256]{1,0:T(8,128)(2,1)S(1)}) custom-call(bf16[256,3584]{1,0:T(8,128)(2,1)S(1)} %bitcast.19, bf16[256,3584]{1,0:T(8,128)(2,1)S(1)} %bitcast.22, bf16[128,3584]{1,0:T(8,128)(2,1)} %collective-permute-done.1.far_gate, bf16[128,3584]{1,0:T(8,128)(2,1)S(1)} %collective-permute-done.7.far_up), custom_call_target="tpu_custom_call" | custom-call | flops 1024 | bytes 1024 | tf_op jit(solution)/shard_map/pallas_call | solution.py:294
  163.0 3.8 %collective-permute-done.19 = f32[384,128]{1,0:T(8,128)S(1)} collective-permute-done((f32[384,128]{1,0:T(8,128)S(1)}, f32[384,128]{1,0:T(8,128)S(1)}, u32[]{:S(2)}, u32[]{:S(2)}) %collective-permute-start.19) | collective-permute-done | bytes 196640 | tf_op jit(solution)/shard_map/ppermute | solution.py:622
  166.8 5.1 %shard_map.157 = f32[128,128]{1,0:T(8,128)S(1)} custom-call(f32[3584,128]{1,0:T(8,128)S(1)} %copy-done.16, bf16[3584,128]{1,0:T(8,128)(2,1)} %collective-permute-done.20.returned, bf16[128,3584]{1,0:T(8,128)(2,1)S(1)} %bitcast.31, bf16[128,3584]{1,0:T(8,128)(2,1)S(1)} %bitcast.33, bf16[64,3584]{1,0:T(8,128)(2,1)S(1)} %copy-done.7, bf16[64,3584]{1,0:T(8,128)(2,1)S(1)} %copy-done.9), custom_call_target="tpu_custom_call" | custom-call | flops 1024 | bytes 1024 | tf_op jit(solution)/shard_map/pallas_call | solution.py:269
  173.2 1.8 collective-permute-start.28
  175.0 1.8 collective-permute-start.27
  176.8 2.6 %collective-permute-start.25 = (f32[128,128]{1,0:T(8,128)S(1)}, f32[128,128]{1,0:T(8,128)S(1)}, u32[]{:S(2)}, u32[]{:S(2)}) collective-permute-start(f32[128,128]{1,0:T(8,128)S(1)} %shard_map.157), channel_id=1, source_target_pairs={{0,4},{4,0},{8,12},{12,8},{1,5},{5,1},{9,13},{13,9},{2,6},{6,2},{1... | collective-permute-start | bytes 196616 | tf_op jit(solution)/shard_map/ppermute | solution.py:546
  179.4 2.1 collective-permute-done.27
  181.5 1.3 collective-permute-done.26
  182.9 3.5 %collective-permute-done.28.far_b = bf16[128,2048]{1,0:T(8,128)(2,1)} collective-permute-done((bf16[128,2048]{1,0:T(8,128)(2,1)S(1)}, bf16[128,2048]{1,0:T(8,128)(2,1)}, u32[]{:S(2)}, u32[]{:S(2)}) %collective-permute-start.28) | collective-permute-done | bytes 524320 | tf_op jit(solution)/shard_map/ppermute | solution.py:629
  190.7 17.6 %shard_map.160 = (f32[128,128]{1,0:T(8,128)}, f32[128,128]{1,0:T(8,128)}) custom-call(s32[3]{0:T(128)} %pad_add_fusion.flags, bf16[128,2048]{1,0:T(8,128)(2,1)} %bitcast.15.b0, bf16[128,2048]{1,0:T(8,128)(2,1)} %collective-permute-done.16.b1, bf16[128,2048]{1,0:T(8,128)(2,1)} %collective-permute-done.21.b2, bf16[128,2048]{1,0:T(8,128)(2,1)} %collective-permute-done.15.b3.b4, ...), custom_call_target="tpu_custom_call" | custom-call | flops 1024 | bytes 1024 | tf_op jit(solution)/shard_map/pallas_call | solution.py:338
  210.2 1.5 copy-done.15
  211.7 2.8 %shard_map.159.early = f32[128,128]{1,0:T(8,128)S(1)} custom-call(f32[3584,128]{1,0:T(8,128)S(1)} %copy-done.15, bf16[3584,128]{1,0:T(8,128)(2,1)S(1)} %collective-permute-done.29.returned, bf16[256,3584]{1,0:T(8,128)(2,1)S(1)} %bitcast.20, bf16[256,3584]{1,0:T(8,128)(2,1)S(1)} %bitcast.23, bf16[64,3584]{1,0:T(8,128)(2,1)S(1)} %copy-done.8, ...), custom_call_target="tpu_custom_call" | custom-call | flops 1024 | bytes 1024 | tf_op jit(solution)/shard_map/pallas_call | solution.py:269
  214.5 2.5 %collective-permute-done.30.far = f32[128,128]{1,0:T(8,128)S(1)} collective-permute-done((f32[128,128]{1,0:T(8,128)}, f32[128,128]{1,0:T(8,128)S(1)}, u32[]{:S(2)}, u32[]{:S(2)}) %collective-permute-start.30) | collective-permute-done | bytes 65568 | tf_op jit(solution)/shard_map/ppermute | solution.py:642
  217.1 1.9 shard_map.162
  219.0 3.2 %collective-permute-start.36 = (f32[4,8]{1,0:T(4,128)S(1)}, f32[4,8]{1,0:T(4,128)S(1)}, u32[]{:S(2)}, u32[]{:S(2)}) collective-permute-start(f32[4,8]{1,0:T(4,128)S(1)} %shard_map.162), channel_id=1, source_target_pairs={{0,12},{4,8},{8,4},{12,0},{1,13},{5,9},{9,5},{13,1},{2,14},{6,10},... | collective-permute-start | bytes 392 | tf_op jit(solution)/shard_map/ppermute | solution.py:546
  224.4 2.2 collective-permute-done.35
  (128 shorter events, 29.1 us)
Async XLA Ops:
  0.0 85.6 %collective-permute-start.12 = (bf16[3584,2048]{1,0:T(8,128)(2,1)}, bf16[3584,2048]{1,0:T(8,128)(2,1)}, u32[]{:S(2)}, u32[]{:S(2)}) collective-permute-start(bf16[3584,2048]{1,0:T(8,128)(2,1)} %weight_own.5), channel_id=1, source_target_pairs={{0,1},{1,0},{2,3},{3,2},{4,5},{5,4},{6,7},{7,6},{8,9},{9,8},{10,11... | collective-permute-start | bytes 44040200 | tf_op jit(solution)/shard_map/ppermute | solution.py:583
  2.7 29.0 %collective-permute-start.1 = (bf16[128,3584]{1,0:T(8,128)(2,1)}, bf16[128,3584]{1,0:T(8,128)(2,1)}, u32[]{:S(2)}, u32[]{:S(2)}) collective-permute-start(bf16[128,3584]{1,0:T(8,128)(2,1)} %bitcast.10), channel_id=1, source_target_pairs={{0,2},{1,3},{2,0},{3,1},{4,6},{5,7},{6,4},{7,5},{8,10},{9,11},{10,... | collective-permute-start | bytes 2752520 | tf_op jit(solution)/shard_map/ppermute | solution.py:585
  5.3 26.5 %collective-permute-start = (bf16[128,2048]{1,0:T(8,128)(2,1)}, bf16[128,2048]{1,0:T(8,128)(2,1)}, u32[]{:S(2)}, u32[]{:S(2)}) collective-permute-start(bf16[128,2048]{1,0:T(8,128)(2,1)} %bitcast.24), channel_id=1, source_target_pairs={{0,8},{4,12},{8,0},{12,4},{1,9},{5,13},{9,1},{13,5},{2,10},{6,14},... | collective-permute-start | bytes 1572872 | tf_op jit(solution)/shard_map/ppermute | solution.py:584
  7.9 24.1 %collective-permute-start.3 = (bf16[128,2048]{1,0:T(8,128)(2,1)}, bf16[128,2048]{1,0:T(8,128)(2,1)}, u32[]{:S(2)}, u32[]{:S(2)}) collective-permute-start(bf16[128,2048]{1,0:T(8,128)(2,1)} %bitcast.25), channel_id=1, source_target_pairs={{0,4},{4,0},{8,12},{12,8},{1,5},{5,1},{9,13},{13,9},{2,6},{6,2},{1... | collective-permute-start | bytes 1572872 | tf_op jit(solution)/shard_map/ppermute | solution.py:584
  31.7 8.8 %collective-permute-start.2 = (bf16[128,2048]{1,0:T(8,128)(2,1)S(1)}, bf16[128,2048]{1,0:T(8,128)(2,1)}, u32[]{:S(2)}, u32[]{:S(2)}) collective-permute-start(bf16[128,2048]{1,0:T(8,128)(2,1)S(1)} %bitcast.28), channel_id=1, source_target_pairs={{0,1},{1,0},{2,3},{3,2},{4,8},{5,9},{6,10},{7,11},{8,4},{9,5},{10,... | collective-permute-start | bytes 1572872 | tf_op jit(solution)/shard_map/ppermute | solution.py:571
  31.9 14.5 %collective-permute-start.4 = (bf16[128,2048]{1,0:T(8,128)(2,1)}, bf16[128,2048]{1,0:T(8,128)(2,1)}, u32[]{:S(2)}, u32[]{:S(2)}) collective-permute-start(bf16[128,2048]{1,0:T(8,128)(2,1)} %collective-permute-done.b3.b4), channel_id=1, source_target_pairs={{0,4},{4,0},{8,12},{12,8},{1,5},{5,1},{9,13},{13,9},{2,6},{6,2},{1... | collective-permute-start | bytes 1572872 | tf_op jit(solution)/shard_map/ppermute | solution.py:572
  35.3 16.4 %collective-permute-start.8 = (bf16[128,2048]{1,0:T(8,128)(2,1)}, bf16[128,2048]{1,0:T(8,128)(2,1)}, u32[]{:S(2)}, u32[]{:S(2)}) collective-permute-start(bf16[128,2048]{1,0:T(8,128)(2,1)} %broadcast_select_fusion.2), channel_id=1, source_target_pairs={{0,2},{1,3},{2,0},{3,1},{4,6},{5,7},{6,4},{7,5},{8,10},{9,11},{10,... | collective-permute-start | bytes 1572872 | tf_op jit(solution)/shard_map/ppermute | solution.py:591
  38.5 31.5 %collective-permute-start.7 = (bf16[128,3584]{1,0:T(8,128)(2,1)}, bf16[128,3584]{1,0:T(8,128)(2,1)S(1)}, u32[]{:S(2)}, u32[]{:S(2)}) collective-permute-start(bf16[128,3584]{1,0:T(8,128)(2,1)} %bitcast.36), channel_id=1, source_target_pairs={{0,2},{1,3},{2,0},{3,1},{4,6},{5,7},{6,4},{7,5},{8,10},{9,11},{10,... | collective-permute-start | bytes 2752520 | tf_op jit(solution)/shard_map/ppermute | solution.py:595
  47.5 24.8 %collective-permute-start.6 = (bf16[128,2048]{1,0:T(8,128)(2,1)}, bf16[128,2048]{1,0:T(8,128)(2,1)S(1)}, u32[]{:S(2)}, u32[]{:S(2)}) collective-permute-start(bf16[128,2048]{1,0:T(8,128)(2,1)} %bitcast.9.b0), channel_id=1, source_target_pairs={{0,4},{4,0},{8,12},{12,8},{1,5},{5,1},{9,13},{13,9},{2,6},{6,2},{1... | collective-permute-start | bytes 1572872 | tf_op jit(solution)/shard_map/ppermute | solution.py:597
  47.9 26.8 %collective-permute-start.5 = (bf16[128,2048]{1,0:T(8,128)(2,1)}, bf16[128,2048]{1,0:T(8,128)(2,1)S(1)}, u32[]{:S(2)}, u32[]{:S(2)}) collective-permute-start(bf16[128,2048]{1,0:T(8,128)(2,1)} %bitcast.9.b0), channel_id=1, source_target_pairs={{0,8},{4,12},{8,0},{12,4},{1,9},{5,13},{9,1},{13,5},{2,10},{6,14},... | collective-permute-start | bytes 1572872 | tf_op jit(solution)/shard_map/ppermute | solution.py:597
  51.7 27.6 %collective-permute-start.9 = (bf16[128,2048]{1,0:T(8,128)(2,1)S(1)}, bf16[128,2048]{1,0:T(8,128)(2,1)}, u32[]{:S(2)}, u32[]{:S(2)}) collective-permute-start(bf16[128,2048]{1,0:T(8,128)(2,1)S(1)} %select_select_fusion.2), channel_id=1, source_target_pairs={{0,2},{1,3},{2,0},{3,1},{4,6},{5,7},{6,4},{7,5},{8,10},{9,11},{10,... | collective-permute-start | bytes 1572872 | tf_op jit(solution)/shard_map/ppermute | solution.py:593
  74.7 25.3 %copy-start.31 = (bf16[128,2048]{1,0:T(8,128)(2,1)}, bf16[128,2048]{1,0:T(8,128)(2,1)S(1)}, u32[]{:S(2)}) copy-start(bf16[128,2048]{1,0:T(8,128)(2,1)S(1)} %collective-permute-done.5.b3.b4) | copy-start | bytes 1572868
  80.2 19.8 %collective-permute-start.11 = (bf16[128,2048]{1,0:T(8,128)(2,1)S(1)}, bf16[128,2048]{1,0:T(8,128)(2,1)}, u32[]{:S(2)}, u32[]{:S(2)}) collective-permute-start(bf16[128,2048]{1,0:T(8,128)(2,1)S(1)} %collective-permute-done.5.b3.b4), channel_id=1, source_target_pairs={{0,4},{4,0},{8,12},{12,8},{1,5},{5,1},{9,13},{13,9},{2,6},{6,2},{1... | collective-permute-start | bytes 1572872 | tf_op jit(solution)/shard_map/ppermute | solution.py:572
  81.9 18.2 %collective-permute-start.13 = (bf16[128,2048]{1,0:T(8,128)(2,1)}, bf16[128,2048]{1,0:T(8,128)(2,1)}, u32[]{:S(2)}, u32[]{:S(2)}) collective-permute-start(bf16[128,2048]{1,0:T(8,128)(2,1)} %broadcast_select_fusion.1), channel_id=1, source_target_pairs={{0,2},{1,3},{2,0},{3,1},{4,6},{5,7},{6,4},{7,5},{8,10},{9,11},{10,... | collective-permute-start | bytes 1572872 | tf_op jit(solution)/shard_map/ppermute | solution.py:600
  83.2 16.9 %collective-permute-start.10 = (bf16[128,2048]{1,0:T(8,128)(2,1)}, bf16[128,2048]{1,0:T(8,128)(2,1)}, u32[]{:S(2)}, u32[]{:S(2)}) collective-permute-start(bf16[128,2048]{1,0:T(8,128)(2,1)} %bitcast.9.b0), channel_id=1, source_target_pairs={{0,1},{1,0},{2,3},{3,2},{4,8},{5,9},{6,10},{7,11},{8,4},{9,5},{10,... | collective-permute-start | bytes 1572872 | tf_op jit(solution)/shard_map/ppermute | solution.py:571
  83.8 16.3 %copy-start.33 = (bf16[128,2048]{1,0:T(8,128)(2,1)S(1)}, bf16[128,2048]{1,0:T(8,128)(2,1)}, u32[]{:S(2)}) copy-start(bf16[128,2048]{1,0:T(8,128)(2,1)} %copy-done.32) | copy-start | bytes 1572868
  83.8 47.1 %collective-permute-start.15 = (bf16[128,2048]{1,0:T(8,128)(2,1)}, bf16[128,2048]{1,0:T(8,128)(2,1)}, u32[]{:S(2)}, u32[]{:S(2)}) collective-permute-start(bf16[128,2048]{1,0:T(8,128)(2,1)} %bitcast.15.b0), channel_id=1, source_target_pairs={{0,8},{4,12},{8,0},{12,4},{1,9},{5,13},{9,1},{13,5},{2,10},{6,14},... | collective-permute-start | bytes 1572872 | tf_op jit(solution)/shard_map/ppermute | solution.py:610
  101.3 29.6 %collective-permute-start.16 = (bf16[128,2048]{1,0:T(8,128)(2,1)}, bf16[128,2048]{1,0:T(8,128)(2,1)}, u32[]{:S(2)}, u32[]{:S(2)}) collective-permute-start(bf16[128,2048]{1,0:T(8,128)(2,1)} %bitcast.15.b0), channel_id=1, source_target_pairs={{0,4},{4,0},{8,12},{12,8},{1,5},{5,1},{9,13},{13,9},{2,6},{6,2},{1... | collective-permute-start | bytes 1572872 | tf_op jit(solution)/shard_map/ppermute | solution.py:611
  111.0 19.9 %collective-permute-start.18 = (bf16[128,2048]{1,0:T(8,128)(2,1)S(1)}, bf16[128,2048]{1,0:T(8,128)(2,1)S(1)}, u32[]{:S(2)}, u32[]{:S(2)}) collective-permute-start(bf16[128,2048]{1,0:T(8,128)(2,1)S(1)} %select_select_fusion.1), channel_id=1, source_target_pairs={{0,2},{1,3},{2,0},{3,1},{4,6},{5,7},{6,4},{7,5},{8,10},{9,11},{10,... | collective-permute-start | bytes 1572872 | tf_op jit(solution)/shard_map/ppermute | solution.py:606
  112.3 16.5 %collective-permute-start.17 = (f32[128,64]{1,0:T(8,128)S(1)}, f32[128,64]{1,0:T(8,128)S(1)}, u32[]{:S(2)}, u32[]{:S(2)}) collective-permute-start(f32[128,64]{1,0:T(8,128)S(1)} %slice.44), channel_id=1, source_target_pairs={{0,4},{4,0},{8,12},{12,8},{1,5},{5,1},{9,13},{13,9},{2,6},{6,2},{1... | collective-permute-start | bytes 98312 | tf_op jit(solution)/shard_map/ppermute | solution.py:614
  112.4 18.4 %collective-permute-start.14 = (f32[384,128]{1,0:T(8,128)S(1)}, f32[384,128]{1,0:T(8,128)S(1)}, u32[]{:S(2)}, u32[]{:S(2)}) collective-permute-start(f32[384,128]{1,0:T(8,128)S(1)} %copy-done.27), channel_id=1, source_target_pairs={{0,4},{4,0},{8,12},{12,8},{1,5},{5,1},{9,13},{13,9},{2,6},{6,2},{1... | collective-permute-start | bytes 589832 | tf_op jit(solution)/shard_map/ppermute | solution.py:613
  130.9 35.9 %collective-permute-start.20 = (bf16[3584,128]{1,0:T(8,128)(2,1)}, bf16[3584,128]{1,0:T(8,128)(2,1)}, u32[]{:S(2)}, u32[]{:S(2)}) collective-permute-start(bf16[3584,128]{1,0:T(8,128)(2,1)} %get-tuple-element.63), channel_id=1, source_target_pairs={{0,2},{1,3},{2,0},{3,1},{4,6},{5,7},{6,4},{7,5},{8,10},{9,11},{10,... | collective-permute-start | bytes 2752520 | tf_op jit(solution)/shard_map/ppermute | solution.py:607
  135.3 23.1 %copy-start.2 = (bf16[4,64,3584]{2,1,0:T(8,128)(2,1)S(1)}, bf16[4,64,3584]{2,1,0:T(8,128)(2,1)}, u32[]{:S(2)}) copy-start(bf16[4,64,3584]{2,1,0:T(8,128)(2,1)} %param.18) | copy-start | bytes 5505028
  135.3 36.8 %collective-permute-start.23 = (bf16[128,2048]{1,0:T(8,128)(2,1)}, bf16[128,2048]{1,0:T(8,128)(2,1)}, u32[]{:S(2)}, u32[]{:S(2)}) collective-permute-start(bf16[128,2048]{1,0:T(8,128)(2,1)} %broadcast_select_fusion), channel_id=1, source_target_pairs={{0,2},{1,3},{2,0},{3,1},{4,6},{5,7},{6,4},{7,5},{8,10},{9,11},{10,... | collective-permute-start | bytes 1572872 | tf_op jit(solution)/shard_map/ppermute | solution.py:617
  135.3 36.8 %collective-permute-start.21 = (bf16[128,2048]{1,0:T(8,128)(2,1)}, bf16[128,2048]{1,0:T(8,128)(2,1)}, u32[]{:S(2)}, u32[]{:S(2)}) collective-permute-start(bf16[128,2048]{1,0:T(8,128)(2,1)} %bitcast.15.b0), channel_id=1, source_target_pairs={{0,1},{1,0},{2,3},{3,2},{4,8},{5,9},{6,10},{7,11},{8,4},{9,5},{10,... | collective-permute-start | bytes 1572872 | tf_op jit(solution)/shard_map/ppermute | solution.py:571
  135.3 36.8 %collective-permute-start.22 = (bf16[128,2048]{1,0:T(8,128)(2,1)}, bf16[128,2048]{1,0:T(8,128)(2,1)}, u32[]{:S(2)}, u32[]{:S(2)}) collective-permute-start(bf16[128,2048]{1,0:T(8,128)(2,1)} %collective-permute-done.15.b3.b4), channel_id=1, source_target_pairs={{0,4},{4,0},{8,12},{12,8},{1,5},{5,1},{9,13},{13,9},{2,6},{6,2},{1... | collective-permute-start | bytes 1572872 | tf_op jit(solution)/shard_map/ppermute | solution.py:572
  151.1 15.7 %copy-start.7 = (bf16[64,3584]{1,0:T(8,128)(2,1)S(1)}, bf16[64,3584]{1,0:T(8,128)(2,1)}, u32[]{:S(2)}) copy-start(bf16[64,3584]{1,0:T(8,128)(2,1)} %proj_gate.5) | copy-start | bytes 1376260
  151.1 15.7 %copy-start.9 = (bf16[64,3584]{1,0:T(8,128)(2,1)S(1)}, bf16[64,3584]{1,0:T(8,128)(2,1)}, u32[]{:S(2)}) copy-start(bf16[64,3584]{1,0:T(8,128)(2,1)} %proj_up.5) | copy-start | bytes 1376260
  151.1 15.7 %copy-start.12 = (bf16[2,64,3584]{2,1,0:T(8,128)(2,1)S(1)}, bf16[2,64,3584]{2,1,0:T(8,128)(2,1)}, u32[]{:S(2)}) copy-start(bf16[2,64,3584]{2,1,0:T(8,128)(2,1)} %param.22) | copy-start | bytes 2752516
  151.1 15.7 %copy-start.14 = (bf16[2,64,3584]{2,1,0:T(8,128)(2,1)S(1)}, bf16[2,64,3584]{2,1,0:T(8,128)(2,1)}, u32[]{:S(2)}) copy-start(bf16[2,64,3584]{2,1,0:T(8,128)(2,1)} %param.23) | copy-start | bytes 2752516
  151.1 6.0 %collective-permute-start.24 = (f32[128,64]{1,0:T(8,128)S(1)}, f32[128,64]{1,0:T(8,128)S(1)}, u32[]{:S(2)}, u32[]{:S(2)}) collective-permute-start(f32[128,64]{1,0:T(8,128)S(1)} %slice_add_fusion), channel_id=1, source_target_pairs={{0,8},{4,12},{8,0},{12,4},{1,9},{5,13},{9,1},{13,5},{2,10},{6,14},... | collective-permute-start | bytes 98312 | tf_op jit(solution)/shard_map/ppermute | solution.py:623
  157.1 9.6 %collective-permute-start.19 = (f32[384,128]{1,0:T(8,128)S(1)}, f32[384,128]{1,0:T(8,128)S(1)}, u32[]{:S(2)}, u32[]{:S(2)}) collective-permute-start(f32[384,128]{1,0:T(8,128)S(1)} %add.41), channel_id=1, source_target_pairs={{0,8},{4,12},{8,0},{12,4},{1,9},{5,13},{9,1},{13,5},{2,10},{6,14},... | collective-permute-start | bytes 589832 | tf_op jit(solution)/shard_map/ppermute | solution.py:622
  166.8 20.9 %copy-start.34 = (f32[384,128]{1,0:T(8,128)}, f32[384,128]{1,0:T(8,128)S(1)}, u32[]{:S(2)}) copy-start(f32[384,128]{1,0:T(8,128)S(1)} %add.43) | copy-start | bytes 589828
  172.0 15.7 %copy-start.29 = (s32[2]{0:T(128)S(1)}, s32[2]{0:T(128)}, u32[]{:S(2)}) copy-start(s32[2]{0:T(128)} %lengths.2) | copy-start | bytes 28
  173.2 13.3 %collective-permute-start.28 = (bf16[128,2048]{1,0:T(8,128)(2,1)S(1)}, bf16[128,2048]{1,0:T(8,128)(2,1)}, u32[]{:S(2)}, u32[]{:S(2)}) collective-permute-start(bf16[128,2048]{1,0:T(8,128)(2,1)S(1)} %select_select_fusion), channel_id=1, source_target_pairs={{0,2},{1,3},{2,0},{3,1},{4,6},{5,7},{6,4},{7,5},{8,10},{9,11},{10,... | collective-permute-start | bytes 1572872 | tf_op jit(solution)/shard_map/ppermute | solution.py:629
  175.0 6.5 %collective-permute-start.27 = (f32[128,128]{1,0:T(8,128)S(1)}, f32[128,128]{1,0:T(8,128)S(1)}, u32[]{:S(2)}, u32[]{:S(2)}) collective-permute-start(f32[128,128]{1,0:T(8,128)S(1)} %shard_map.157), channel_id=1, source_target_pairs={{0,12},{4,8},{8,4},{12,0},{1,13},{5,9},{9,5},{13,1},{2,14},{6,10},... | collective-permute-start | bytes 196616 | tf_op jit(solution)/shard_map/ppermute | solution.py:546
  176.8 6.1 %collective-permute-start.26 = (f32[128,128]{1,0:T(8,128)S(1)}, f32[128,128]{1,0:T(8,128)S(1)}, u32[]{:S(2)}, u32[]{:S(2)}) collective-permute-start(f32[128,128]{1,0:T(8,128)S(1)} %shard_map.157), channel_id=1, source_target_pairs={{0,8},{4,12},{8,0},{12,4},{1,9},{5,13},{9,1},{13,5},{2,10},{6,14},... | collective-permute-start | bytes 196616 | tf_op jit(solution)/shard_map/ppermute | solution.py:546
  176.8 6.1 %collective-permute-start.25 = (f32[128,128]{1,0:T(8,128)S(1)}, f32[128,128]{1,0:T(8,128)S(1)}, u32[]{:S(2)}, u32[]{:S(2)}) collective-permute-start(f32[128,128]{1,0:T(8,128)S(1)} %shard_map.157), channel_id=1, source_target_pairs={{0,4},{4,0},{8,12},{12,8},{1,5},{5,1},{9,13},{13,9},{2,6},{6,2},{1... | collective-permute-start | bytes 196616 | tf_op jit(solution)/shard_map/ppermute | solution.py:546
  186.4 23.7 %collective-permute-start.29 = (bf16[3584,128]{1,0:T(8,128)(2,1)}, bf16[3584,128]{1,0:T(8,128)(2,1)S(1)}, u32[]{:S(2)}, u32[]{:S(2)}) collective-permute-start(bf16[3584,128]{1,0:T(8,128)(2,1)} %get-tuple-element.71), channel_id=1, source_target_pairs={{0,2},{1,3},{2,0},{3,1},{4,6},{5,7},{6,4},{7,5},{8,10},{9,11},{10,... | collective-permute-start | bytes 2752520 | tf_op jit(solution)/shard_map/ppermute | solution.py:631
  188.7 25.8 %collective-permute-start.31 = (f32[2,192,64]{2,1,0:T(8,128)S(1)}, f32[2,192,64]{2,1,0:T(8,128)S(1)}, u32[]{:S(2)}, u32[]{:S(2)}) collective-permute-start(f32[2,192,64]{2,1,0:T(8,128)S(1)} %shard_map.161.q0), channel_id=1, source_target_pairs={{0,1},{1,0},{2,3},{3,2},{4,5},{5,4},{6,7},{7,6},{8,9},{9,8},{10,11... | collective-permute-start | bytes 294920 | tf_op jit(solution)/shard_map/ppermute | solution.py:634
  188.8 25.7 %collective-permute-start.32 = (f32[2,192,64]{2,1,0:T(8,128)S(1)}, f32[2,192,64]{2,1,0:T(8,128)}, u32[]{:S(2)}, u32[]{:S(2)}) collective-permute-start(f32[2,192,64]{2,1,0:T(8,128)S(1)} %shard_map.161.q0), channel_id=1, source_target_pairs={{0,2},{1,3},{2,0},{3,1},{4,6},{5,7},{6,4},{7,5},{8,10},{9,11},{10,... | collective-permute-start | bytes 294920 | tf_op jit(solution)/shard_map/ppermute | solution.py:634
  189.7 24.8 %collective-permute-start.33 = (f32[2,192,64]{2,1,0:T(8,128)S(1)}, f32[2,192,64]{2,1,0:T(8,128)}, u32[]{:S(2)}, u32[]{:S(2)}) collective-permute-start(f32[2,192,64]{2,1,0:T(8,128)S(1)} %shard_map.161.q0), channel_id=1, source_target_pairs={{0,3},{1,2},{2,1},{3,0},{4,7},{5,6},{6,5},{7,4},{8,11},{9,10},{10,... | collective-permute-start | bytes 294920 | tf_op jit(solution)/shard_map/ppermute | solution.py:634
  190.7 19.5 %copy-start.8 = (bf16[64,3584]{1,0:T(8,128)(2,1)S(1)}, bf16[64,3584]{1,0:T(8,128)(2,1)}, u32[]{:S(2)}) copy-start(bf16[64,3584]{1,0:T(8,128)(2,1)} %proj_gate.5) | copy-start | bytes 1376260
  190.7 19.5 %copy-start.10 = (bf16[64,3584]{1,0:T(8,128)(2,1)S(1)}, bf16[64,3584]{1,0:T(8,128)(2,1)}, u32[]{:S(2)}) copy-start(bf16[64,3584]{1,0:T(8,128)(2,1)} %proj_up.5) | copy-start | bytes 1376260
  208.3 8.7 %collective-permute-start.30 = (f32[128,128]{1,0:T(8,128)}, f32[128,128]{1,0:T(8,128)S(1)}, u32[]{:S(2)}, u32[]{:S(2)}) collective-permute-start(f32[128,128]{1,0:T(8,128)} %get-tuple-element.74), channel_id=1, source_target_pairs={{0,2},{1,3},{2,0},{3,1},{4,6},{5,7},{6,4},{7,5},{8,10},{9,11},{10,... | collective-permute-start | bytes 196616 | tf_op jit(solution)/shard_map/ppermute | solution.py:642
  219.0 5.4 %collective-permute-start.36 = (f32[4,8]{1,0:T(4,128)S(1)}, f32[4,8]{1,0:T(4,128)S(1)}, u32[]{:S(2)}, u32[]{:S(2)}) collective-permute-start(f32[4,8]{1,0:T(4,128)S(1)} %shard_map.162), channel_id=1, source_target_pairs={{0,12},{4,8},{8,4},{12,0},{1,13},{5,9},{9,5},{13,1},{2,14},{6,10},... | collective-permute-start | bytes 392 | tf_op jit(solution)/shard_map/ppermute | solution.py:546
  222.2 4.5 %collective-permute-start.35 = (f32[4,8]{1,0:T(4,128)S(1)}, f32[4,8]{1,0:T(4,128)S(1)}, u32[]{:S(2)}, u32[]{:S(2)}) collective-permute-start(f32[4,8]{1,0:T(4,128)S(1)} %shard_map.162), channel_id=1, source_target_pairs={{0,8},{4,12},{8,0},{12,4},{1,9},{5,13},{9,1},{13,5},{2,10},{6,14},... | collective-permute-start | bytes 392 | tf_op jit(solution)/shard_map/ppermute | solution.py:546
  222.2 4.5 %collective-permute-start.34 = (f32[4,8]{1,0:T(4,128)S(1)}, f32[4,8]{1,0:T(4,128)S(1)}, u32[]{:S(2)}, u32[]{:S(2)}) collective-permute-start(f32[4,8]{1,0:T(4,128)S(1)} %shard_map.162), channel_id=1, source_target_pairs={{0,4},{4,0},{8,12},{12,8},{1,5},{5,1},{9,13},{13,9},{2,6},{6,2},{1... | collective-permute-start | bytes 392 | tf_op jit(solution)/shard_map/ppermute | solution.py:546
  (25 other events, 121.3 us)

commit v10 on v7

--- a/solution.py
+++ b/solution.py
@@ -167,9 +167,6 @@
 
     @pl.when(step == 0)
     def _():
-        for tile in range(2):
-            for copy in weight_copies(tile):
-                copy.start()
         slot = flags[1]
         far_copies = [
             pltpu.make_async_copy(
@@ -193,6 +190,9 @@
                 ]
                 for copy in copies:
                     copy.start()
+                for tile in range(2):
+                    for copy in weight_copies(tile):
+                        copy.start()
                 for copy in copies:
                     copy.wait()
 
@@ -302,7 +302,7 @@
 
 def lent_kernel(
     flags, b0, b1, b2, b3, b4, b5, far, weight_own, weight_sib, gates, ups, proj_gate, proj_up,
-    sides, *scratch,
+    near, away, *scratch,
 ):
     pairs = ((b0, b1), (b2, b3), (b4, b5))
     hidden_grad = stacked_products(flags, pairs, far, weight_own, weight_sib, *scratch)
@@ -314,15 +314,18 @@
         ],
         axis=0,
     )
+    number = near.shape[1]
     first = pl.program_id(0) == 0
 
     @pl.when(first)
     def _():
-        sides[...] = part
+        near[...] = part[:, :number]
+        away[...] = part[:, number:]
 
     @pl.when(jnp.logical_not(first))
     def _():
-        sides[...] += part
+        near[...] += part[:, :number]
+        away[...] += part[:, number:]
 
 
 def lent_sides(flags, blocks, far, weight_own, weight_sib, gates, ups, proj_gate, proj_up):
@@ -335,8 +338,8 @@
         + [ANYWHERE] * 9
         + [tile_rows(2 * number)] * 2
         + [tile_columns(RANK)] * 2,
-        out_specs=whole((2 * RANK, 2 * number)),
-        out_shape=jax.ShapeDtypeStruct((2 * RANK, 2 * number), jnp.float32),
+        out_specs=[whole((2 * RANK, number))] * 2,
+        out_shape=[jax.ShapeDtypeStruct((2 * RANK, number), jnp.float32)] * 2,
         scratch_shapes=[
             pltpu.VMEM((2, 2 * number, half), jnp.bfloat16),
             pltpu.SemaphoreType.DMA((4,)),
@@ -520,6 +523,7 @@
 
     to_core = functools.partial(lax.ppermute, axis_name="dp", perm=[(i, i ^ 1) for i in range(4)])
     to_chip = functools.partial(lax.ppermute, axis_name="dp", perm=[(i, i ^ 2) for i in range(4)])
+    to_other = functools.partial(lax.ppermute, axis_name="dp", perm=[(i, i ^ 3) for i in range(4)])
     outer = functools.partial(
         lax.ppermute, axis_name="tensor", perm=[(i, i ^ 1) for i in range(4)]
     )
@@ -539,10 +543,6 @@
         ],
     )
 
-    def tensor_sum(values):
-        values = values + outer(values)
-        return values + across(values)
-
     q_input, q_gate, q_up, q_outgrad = [
         flatten(a) for a in (query_input, query_gate, query_up, query_outgrad)
     ]
@@ -584,37 +584,38 @@
     a_blocks = last_hops(*a_hops[:2], after(a_hops[2], q_send))
 
     b_hops = first_hops(after(t_outgrad[cut:], a_hops[2]))
-    a_send = crossing_pair(*a_blocks[:5], after(a_blocks[5], q_far))
+    gates, ups = turned(t_gate, t_up, far_gate, far_up)
+    a_send = crossing_pair(*a_blocks[:5], after(a_blocks[5], q_far, gates))
     a_far = to_chip(a_send)
     q_near_sum, q_far_sum = partial_sums(
         flags, q_blocks, after(q_far, a_send), weight_own, weight_sib
     )
-    q_returned = to_chip(q_far_sum)
+    q_returned = to_chip(after(q_far_sum, a_far))
     b_blocks = last_hops(*b_hops[:2], after(b_hops[2], q_far_sum))
-    a_near_sum, a_far_sum = partial_sums(flags, a_blocks, a_far, weight_own, weight_sib)
-    b_send = after(crossing_pair(*b_blocks), a_far_sum)
+    b_send = crossing_pair(*b_blocks)
     b_far = to_chip(b_send)
-    in_out = tensor_sum(after(own_in_out, b_send))
-    a_returned = to_chip(after(a_far_sum, in_out))
+    a_near_sum, a_far_sum = partial_sums(
+        flags, a_blocks, after(a_far, b_send), weight_own, weight_sib
+    )
+    a_returned = to_chip(a_far_sum)
+    in_out = own_in_out + outer(after(own_in_out, b_send))
     q_gradient = finished_sides(
-        q_near_sum, after(q_returned, b_send), q_gate, q_up, proj_gate, proj_up
-    )
-    own_found = query_features(
-        query_lengths,
-        in_out[2 * cut :],
-        tensor_sum(jnp.concatenate([q_gradient, hidden[2 * cut :]], axis=1)),
-    )
-    core_found = to_core(own_found)
-    found = (own_found, core_found, to_chip(own_found), to_chip(core_found))
-    gates, ups = turned(t_gate, t_up, after(far_gate, b_send), far_up)
-    b_gradient = lent_sides(
-        flags, b_blocks, after(b_far, core_found), weight_own, weight_sib, gates, ups, proj_gate,
-        proj_up,
-    )
+        q_near_sum, after(q_returned, a_far_sum), q_gate, q_up, proj_gate, proj_up
+    )
+    q_sums = jnp.concatenate([q_gradient, hidden[2 * cut :]], axis=1)
+    q_sums = q_sums + outer(q_sums)
+    b_near, b_away = lent_sides(
+        after(flags, q_sums, in_out), b_blocks, b_far, weight_own, weight_sib, gates, ups,
+        proj_gate, proj_up,
+    )
+    in_out = in_out + after(across(in_out), b_near)
+    q_sums = q_sums + after(across(q_sums), b_near)
+    own_found = query_features(query_lengths, in_out[2 * cut :], q_sums)
+    found = (own_found, to_core(own_found), to_chip(own_found), to_other(own_found))
     a_gradient = finished_sides(a_near_sum, a_returned, t_gate, t_up, proj_gate, proj_up)
     own_scores = partial_scores(
-        train_lengths, place, in_out[: 2 * cut], hidden[: 2 * cut], a_gradient, b_gradient[:, :cut],
-        to_chip(b_gradient[:, cut:]), found,
+        train_lengths, place, in_out[: 2 * cut], hidden[: 2 * cut], a_gradient, b_near,
+        to_chip(b_away), found,
     )
     scores = own_scores + outer(own_scores) + across(own_scores) + opposite(own_scores)
     return scores / (RANK * SEQ)

time: 207 us -> 197 us (0.952)
  waiting for transfers between devices: 69 us -> 54.6 us
  starting transfers between devices: 43.7 us -> 50.7 us
  local copies, waits for them, and re-layouts: 24.3 us -> 17.9 us
  Pallas kernels: 63.3 us -> 66.7 us
    ppermute x10, waiting for transfers between devices: 23.4 us -> 3.5 us  [the longest x1 3.48 us: moving_plan(): to_chip(b_away)]
    ppermute x10, starting transfers between devices: 9.65 us -> 15.9 us  [the longest x1 6.11 us: moving_plan(): q_sums = q_sums + after(across(q_sums), b_near)]
    ppermute x3, waiting for transfers between devices: 22.2 us -> 28 us  [last_hops(): return (own, one, mid, two, two, outer(after(two, one)))]
    unnamed x80 -> x74, local copies, waits for them, and re-layouts: 20 us -> 14.6 us
    pallas_call x1, Pallas kernels: 1.82 us -> 4.61 us  [turned(): pl.pallas_call(turn_kernel, grid=(units // TILE,), in_specs=[tile_columns...]
    pallas_call x2, Pallas kernels: 5.71 us -> 7.95 us  [finished_sides(): pl.pallas_call(finish_kernel, grid=(units // TILE,), in_specs=[tile_rows(...]
    ppermute x1, starting transfers between devices: 2.26 us -> 0.07 us  [moving_plan(): opposite(own_scores)]
  transfers between devices with their start and end apart: 31 -> 31, of which waited for: 14 -> 12; matrix products, arithmetic and copies ran while one was open for 5% -> 4% of each run, Pallas kernels for 30% -> 33%
where the time goes in v10:
time: 197 us; the launch traced here: 196 us
  Pallas kernels  66.7 us (34%)
  waiting for transfers between devices  54.6 us (28%)
  starting transfers between devices  50.7 us (26%)
  local copies, waits for them, and re-layouts  17.9 us (9%)
  other arithmetic  5.39 us (3%)
    pallas_call x2, Pallas kernels, partial_sums(): pl.pallas_call(partial_kernel, grid=(units // TILE,), in_specs=[SCALARS]...  28.7 us
    ppermute x3, waiting for transfers between devices, last_hops(): return (own, one, mid, two, two, outer(after(two, one)))  28 us
    ppermute x6, waiting for transfers between devices, first_hops(): return (own, outer(own), across(own))  20 us
    ppermute x6, starting transfers between devices, first_hops(): return (own, outer(own), across(own))  18.4 us
    pallas_call x1, Pallas kernels, lent_sides(): pl.pallas_call(lent_kernel, grid=(units // TILE,), in_specs=[SCALARS] + [...  18.3 us
    unnamed x74, local copies, waits for them, and re-layouts  14.6 us
    pallas_call x2, Pallas kernels, finished_sides(): pl.pallas_call(finish_kernel, grid=(units // TILE,), in_specs=[tile_rows(...  7.95 us
    ppermute x1, starting transfers between devices, moving_plan(): q_sums = q_sums + after(across(q_sums), b_near)  6.11 us
  transfers between devices with their start and end apart: 31, of which 12 were waited for; matrix products, arithmetic and copies ran while one was open for 4% of the time, Pallas kernels for 33%

profile of v10, /device:TPU:0, one launch (start us, length us, event | category | flops | bytes accessed | tf_op | source)
XLA Modules:
  0.0 195.8 jit_solution(4064716160287469517)
XLA Ops:
  0.5 1.3 slice.40
  1.8 2.6 %collective-permute-start.1 = (bf16[128,3584]{1,0:T(8,128)(2,1)S(1)}, bf16[128,3584]{1,0:T(8,128)(2,1)S(1)}, u32[]{:S(2)}, u32[]{:S(2)}) collective-permute-start(bf16[128,3584]{1,0:T(8,128)(2,1)S(1)} %bitcast.46), channel_id=1, source_target_pairs={{0,2},{1,3},{2,0},{3,1},{4,6},{5,7},{6,4},{7,5},{8,10},{9,11},{10,... | collective-permute-start | bytes 2752520 | tf_op jit(solution)/shard_map/ppermute | solution.py:573
  4.4 2.6 %collective-permute-start = (bf16[128,2048]{1,0:T(8,128)(2,1)}, bf16[128,2048]{1,0:T(8,128)(2,1)}, u32[]{:S(2)}, u32[]{:S(2)}) collective-permute-start(bf16[128,2048]{1,0:T(8,128)(2,1)} %bitcast.4.q_outgrad.b0), channel_id=1, source_target_pairs={{0,8},{4,12},{8,0},{12,4},{1,9},{5,13},{9,1},{13,5},{2,10},{6,14},... | collective-permute-start | bytes 1572872 | tf_op jit(solution)/shard_map/ppermute | solution.py:556
  7.0 1.6 collective-permute-start.4
  8.6 1.5 copy-done.1
  10.1 1.2 copy-done.4
  11.3 1.2 copy-done.9
  12.5 1.2 copy-done.11
  13.7 1.2 copy-done.17
  14.9 1.0 copy-done.18
  15.9 1.0 copy-done.19
  18.8 4.9 %shard_map.154 = (f32[384,128]{1,0:T(8,128)S(1)}, f32[384,64]{1,0:T(8,128)S(1)}) custom-call(bf16[256,2048]{1,0:T(8,128)(2,1)S(1)} %bitcast.39, bf16[128,2048]{1,0:T(8,128)(2,1)S(1)} %bitcast.40, bf16[256,2048]{1,0:T(8,128)(2,1)S(1)} %bitcast.34, bf16[128,2048]{1,0:T(8,128)(2,1)} %bitcast.4.q_outgrad.b0, bf16[64,2048]{1,0:T(8,128)(2,1)S(1)} %copy-done.20, ...), custom_call_target="tpu_custom_call" | custom-call | flops 1024 | bytes 1024 | tf_op jit(solution)/shard_map/pallas_call | solution.py:393
  23.7 7.1 %collective-permute-done.b3.b4 = bf16[128,2048]{1,0:T(8,128)(2,1)} collective-permute-done((bf16[128,2048]{1,0:T(8,128)(2,1)}, bf16[128,2048]{1,0:T(8,128)(2,1)}, u32[]{:S(2)}, u32[]{:S(2)}) %collective-permute-start) | collective-permute-done | bytes 524320 | tf_op jit(solution)/shard_map/ppermute | solution.py:556
  31.0 1.9 collective-permute-start.6
  35.4 10.3 %collective-permute-start.2 = (bf16[128,2048]{1,0:T(8,128)(2,1)S(1)}, bf16[128,2048]{1,0:T(8,128)(2,1)S(1)}, u32[]{:S(2)}, u32[]{:S(2)}) collective-permute-start(bf16[128,2048]{1,0:T(8,128)(2,1)S(1)} %bitcast.42), channel_id=1, source_target_pairs={{0,8},{4,12},{8,0},{12,4},{1,9},{5,13},{9,1},{13,5},{2,10},{6,14},... | collective-permute-start | bytes 1572872 | tf_op jit(solution)/shard_map/ppermute | solution.py:556
  45.7 11.6 %collective-permute-done.6.b5 = bf16[128,2048]{1,0:T(8,128)(2,1)} collective-permute-done((bf16[128,2048]{1,0:T(8,128)(2,1)}, bf16[128,2048]{1,0:T(8,128)(2,1)}, u32[]{:S(2)}, u32[]{:S(2)}) %collective-permute-start.6) | collective-permute-done | bytes 524320 | tf_op jit(solution)/shard_map/ppermute | solution.py:560
  57.2 1.5 select_bitcast_fusion.5
  59.5 6.3 %collective-permute-done.2.b3.b4 = bf16[128,2048]{1,0:T(8,128)(2,1)S(1)} collective-permute-done((bf16[128,2048]{1,0:T(8,128)(2,1)S(1)}, bf16[128,2048]{1,0:T(8,128)(2,1)S(1)}, u32[]{:S(2)}, u32[]{:S(2)}) %collective-permute-start.2) | collective-permute-done | bytes 524320 | tf_op jit(solution)/shard_map/ppermute | solution.py:556
  65.8 2.1 %collective-permute-done.10.b1 = bf16[128,2048]{1,0:T(8,128)(2,1)S(1)} collective-permute-done((bf16[128,2048]{1,0:T(8,128)(2,1)S(1)}, bf16[128,2048]{1,0:T(8,128)(2,1)S(1)}, u32[]{:S(2)}, u32[]{:S(2)}) %collective-permute-start.10) | collective-permute-done | bytes 524320 | tf_op jit(solution)/shard_map/ppermute | solution.py:556
  68.0 2.2 %collective-permute-start.11 = (bf16[128,2048]{1,0:T(8,128)(2,1)S(1)}, bf16[128,2048]{1,0:T(8,128)(2,1)S(1)}, u32[]{:S(2)}, u32[]{:S(2)}) collective-permute-start(bf16[128,2048]{1,0:T(8,128)(2,1)S(1)} %collective-permute-done.2.b3.b4), channel_id=1, source_target_pairs={{0,4},{4,0},{8,12},{12,8},{1,5},{5,1},{9,13},{13,9},{2,6},{6,2},{1... | collective-permute-start | bytes 1572872 | tf_op jit(solution)/shard_map/ppermute | solution.py:560
  70.2 2.2 %collective-permute-start.14 = (bf16[128,2048]{1,0:T(8,128)(2,1)}, bf16[128,2048]{1,0:T(8,128)(2,1)}, u32[]{:S(2)}, u32[]{:S(2)}) collective-permute-start(bf16[128,2048]{1,0:T(8,128)(2,1)} %bitcast.9.b0), channel_id=1, source_target_pairs={{0,4},{4,0},{8,12},{12,8},{1,5},{5,1},{9,13},{13,9},{2,6},{6,2},{1... | collective-permute-start | bytes 1572872 | tf_op jit(solution)/shard_map/ppermute | solution.py:556
  72.4 4.6 %shard_map.155 = (bf16[3584,256]{1,0:T(8,128)(2,1)S(1)}, bf16[3584,256]{1,0:T(8,128)(2,1)S(1)}) custom-call(bf16[256,3584]{1,0:T(8,128)(2,1)S(1)} %bitcast.29, bf16[256,3584]{1,0:T(8,128)(2,1)S(1)} %bitcast.32, bf16[128,3584]{1,0:T(8,128)(2,1)S(1)} %collective-permute-done.1.far_gate, bf16[128,3584]{1,0:T(8,128)(2,1)} %collective-permute-done.7.far_up), custom_call_target="tpu_custom_call" | custom-call | flops 1024 | bytes 1024 | tf_op jit(solution)/shard_map/pallas_call | solution.py:292
  77.0 5.9 %collective-permute-done.11.b5 = bf16[128,2048]{1,0:T(8,128)(2,1)S(1)} collective-permute-done((bf16[128,2048]{1,0:T(8,128)(2,1)S(1)}, bf16[128,2048]{1,0:T(8,128)(2,1)S(1)}, u32[]{:S(2)}, u32[]{:S(2)}) %collective-permute-start.11) | collective-permute-done | bytes 524320 | tf_op jit(solution)/shard_map/ppermute | solution.py:560
  83.0 1.6 collective-permute-start.3
  85.5 1.1 pad_maximum_fusion.1
  87.7 14.3 %shard_map.156 = (f32[3584,128]{1,0:T(8,128)}, bf16[3584,128]{1,0:T(8,128)(2,1)}) custom-call(s32[2]{0:T(128)} %pad_add_fusion.flags, bf16[128,2048]{1,0:T(8,128)(2,1)} %bitcast.4.q_outgrad.b0, bf16[128,2048]{1,0:T(8,128)(2,1)} %copy-done.30, bf16[128,2048]{1,0:T(8,128)(2,1)} %collective-permute-done.5.b2, bf16[128,2048]{1,0:T(8,128)(2,1)} %collective-permute-done.b3.b4, ...), custom_call_target="tpu_custom_call" | custom-call | flops 1024 | bytes 1024 | tf_op jit(solution)/shard_map/pallas_call | solution.py:240
  102.1 4.3 %collective-permute-done.3.b3.b4 = bf16[128,2048]{1,0:T(8,128)(2,1)S(1)} collective-permute-done((bf16[128,2048]{1,0:T(8,128)(2,1)}, bf16[128,2048]{1,0:T(8,128)(2,1)S(1)}, u32[]{:S(2)}, u32[]{:S(2)}) %collective-permute-start.3) | collective-permute-done | bytes 524320 | tf_op jit(solution)/shard_map/ppermute | solution.py:556
  106.4 1.7 collective-permute-start.15
  108.1 1.6 collective-permute-done.18.far
  110.3 10.5 %collective-permute-done.15.b5 = bf16[128,2048]{1,0:T(8,128)(2,1)S(1)} collective-permute-done((bf16[128,2048]{1,0:T(8,128)(2,1)S(1)}, bf16[128,2048]{1,0:T(8,128)(2,1)S(1)}, u32[]{:S(2)}, u32[]{:S(2)}) %collective-permute-start.15) | collective-permute-done | bytes 524320 | tf_op jit(solution)/shard_map/ppermute | solution.py:560
  121.5 1.1 pad_maximum_fusion.2
  122.7 1.3 collective-permute-start.21
  124.0 14.3 %shard_map.157 = (f32[3584,128]{1,0:T(8,128)}, bf16[3584,128]{1,0:T(8,128)(2,1)}) custom-call(s32[2]{0:T(128)} %pad_add_fusion.flags, bf16[128,2048]{1,0:T(8,128)(2,1)} %bitcast.45, bf16[128,2048]{1,0:T(8,128)(2,1)} %copy-done.31, bf16[128,2048]{1,0:T(8,128)(2,1)} %copy-done.33, bf16[128,2048]{1,0:T(8,128)(2,1)} %copy-done.28, bf16[128,2048]{1,0:T(8,128)(2,1)} %copy-done.28, ...), custom_call_target="tpu_custom_call" | custom-call | flops 1024 | bytes 1024 | tf_op jit(solution)/shard_map/pallas_call | solution.py:240
  138.4 1.0 collective-permute-start.22
  139.8 1.5 copy-done.16
  141.2 5.1 %shard_map.158 = f32[128,128]{1,0:T(8,128)S(1)} custom-call(f32[3584,128]{1,0:T(8,128)S(1)} %copy-done.16, bf16[3584,128]{1,0:T(8,128)(2,1)} %collective-permute-done.19.returned, bf16[128,3584]{1,0:T(8,128)(2,1)S(1)} %bitcast.36, bf16[128,3584]{1,0:T(8,128)(2,1)S(1)} %bitcast.38, bf16[64,3584]{1,0:T(8,128)(2,1)S(1)} %copy-done.5, bf16[64,3584]{1,0:T(8,128)(2,1)S(1)} %copy-done.7), custom_call_target="tpu_custom_call" | custom-call | flops 1024 | bytes 1024 | tf_op jit(solution)/shard_map/pallas_call | solution.py:267
  146.4 1.8 collective-permute-start.20
  148.2 4.0 %collective-permute-start.17 = (f32[384,128]{1,0:T(8,128)S(1)}, f32[384,128]{1,0:T(8,128)S(1)}, u32[]{:S(2)}, u32[]{:S(2)}) collective-permute-start(f32[384,128]{1,0:T(8,128)S(1)} %add.32), channel_id=1, source_target_pairs={{0,8},{4,12},{8,0},{12,4},{1,9},{5,13},{9,1},{13,5},{2,10},{6,14},... | collective-permute-start | bytes 589832 | tf_op jit(solution)/shard_map/ppermute | solution.py:611
  152.2 6.1 %collective-permute-start.24 = (f32[128,192]{1,0:T(8,128)S(1)}, f32[128,192]{1,0:T(8,128)S(1)}, u32[]{:S(2)}, u32[]{:S(2)}) collective-permute-start(f32[128,192]{1,0:T(8,128)S(1)} %fusion), channel_id=1, source_target_pairs={{0,8},{4,12},{8,0},{12,4},{1,9},{5,13},{9,1},{13,5},{2,10},{6,14},... | collective-permute-start | bytes 294920 | tf_op jit(solution)/shard_map/ppermute | solution.py:612
  158.3 18.3 %shard_map.159 = (f32[128,128]{1,0:T(8,128)}, f32[128,128]{1,0:T(8,128)}) custom-call(s32[2]{0:T(128)} %pad_add_fusion.flags, bf16[128,2048]{1,0:T(8,128)(2,1)} %bitcast.9.b0, bf16[128,2048]{1,0:T(8,128)(2,1)} %collective-permute-done.14.b1, bf16[128,2048]{1,0:T(8,128)(2,1)} %copy-done.34, bf16[128,2048]{1,0:T(8,128)(2,1)} %copy-done.27, ...), custom_call_target="tpu_custom_call" | custom-call | flops 1024 | bytes 1024 | tf_op jit(solution)/shard_map/pallas_call | solution.py:334
  177.8 1.8 collective-permute-start.25
  179.9 1.5 copy-done.13
  181.4 2.8 %shard_map.160.early = f32[128,128]{1,0:T(8,128)S(1)} custom-call(f32[3584,128]{1,0:T(8,128)S(1)} %copy-done.13, bf16[3584,128]{1,0:T(8,128)(2,1)S(1)} %collective-permute-done.22.returned, bf16[256,3584]{1,0:T(8,128)(2,1)S(1)} %bitcast.30, bf16[256,3584]{1,0:T(8,128)(2,1)S(1)} %bitcast.33, bf16[64,3584]{1,0:T(8,128)(2,1)S(1)} %copy-done.6, ...), custom_call_target="tpu_custom_call" | custom-call | flops 1024 | bytes 1024 | tf_op jit(solution)/shard_map/pallas_call | solution.py:267
  184.3 3.5 %collective-permute-done.23.far = f32[128,128]{1,0:T(8,128)S(1)} collective-permute-done((f32[128,128]{1,0:T(8,128)}, f32[128,128]{1,0:T(8,128)S(1)}, u32[]{:S(2)}, u32[]{:S(2)}) %collective-permute-start.23) | collective-permute-done | bytes 65568 | tf_op jit(solution)/shard_map/ppermute | solution.py:618
  187.8 1.4 shard_map.162
  189.3 1.0 collective-permute-start.29
  190.3 3.3 %collective-permute-start.28 = (f32[4,8]{1,0:T(4,128)S(1)}, f32[4,8]{1,0:T(4,128)S(1)}, u32[]{:S(2)}, u32[]{:S(2)}) collective-permute-start(f32[4,8]{1,0:T(4,128)S(1)} %shard_map.162), channel_id=1, source_target_pairs={{0,4},{4,0},{8,12},{12,8},{1,5},{5,1},{9,13},{13,9},{2,6},{6,2},{1... | collective-permute-start | bytes 392 | tf_op jit(solution)/shard_map/ppermute | solution.py:620
  193.6 1.0 collective-permute-done.30
  (117 shorter events, 12.2 us)
Async XLA Ops:
  0.0 8.6 %copy-start = (bf16[4,64,3584]{2,1,0:T(8,128)(2,1)S(1)}, bf16[4,64,3584]{2,1,0:T(8,128)(2,1)}, u32[]{:S(2)}) copy-start(bf16[4,64,3584]{2,1,0:T(8,128)(2,1)} %param.17) | copy-start | bytes 5505028
  0.0 87.7 %collective-permute-start.12 = (bf16[3584,2048]{1,0:T(8,128)(2,1)}, bf16[3584,2048]{1,0:T(8,128)(2,1)}, u32[]{:S(2)}, u32[]{:S(2)}) collective-permute-start(bf16[3584,2048]{1,0:T(8,128)(2,1)} %weight_own.5), channel_id=1, source_target_pairs={{0,1},{1,0},{2,3},{3,2},{4,5},{5,4},{6,7},{7,6},{8,9},{9,8},{10,11... | collective-permute-start | bytes 44040200 | tf_op jit(solution)/shard_map/ppermute | solution.py:571
  1.8 32.0 %collective-permute-start.1 = (bf16[128,3584]{1,0:T(8,128)(2,1)S(1)}, bf16[128,3584]{1,0:T(8,128)(2,1)S(1)}, u32[]{:S(2)}, u32[]{:S(2)}) collective-permute-start(bf16[128,3584]{1,0:T(8,128)(2,1)S(1)} %bitcast.46), channel_id=1, source_target_pairs={{0,2},{1,3},{2,0},{3,1},{4,6},{5,7},{6,4},{7,5},{8,10},{9,11},{10,... | collective-permute-start | bytes 2752520 | tf_op jit(solution)/shard_map/ppermute | solution.py:573
  4.4 26.5 %collective-permute-start = (bf16[128,2048]{1,0:T(8,128)(2,1)}, bf16[128,2048]{1,0:T(8,128)(2,1)}, u32[]{:S(2)}, u32[]{:S(2)}) collective-permute-start(bf16[128,2048]{1,0:T(8,128)(2,1)} %bitcast.4.q_outgrad.b0), channel_id=1, source_target_pairs={{0,8},{4,12},{8,0},{12,4},{1,9},{5,13},{9,1},{13,5},{2,10},{6,14},... | collective-permute-start | bytes 1572872 | tf_op jit(solution)/shard_map/ppermute | solution.py:556
  7.0 24.0 %collective-permute-start.4 = (bf16[128,2048]{1,0:T(8,128)(2,1)}, bf16[128,2048]{1,0:T(8,128)(2,1)S(1)}, u32[]{:S(2)}, u32[]{:S(2)}) collective-permute-start(bf16[128,2048]{1,0:T(8,128)(2,1)} %bitcast.4.q_outgrad.b0), channel_id=1, source_target_pairs={{0,4},{4,0},{8,12},{12,8},{1,5},{5,1},{9,13},{13,9},{2,6},{6,2},{1... | collective-permute-start | bytes 1572872 | tf_op jit(solution)/shard_map/ppermute | solution.py:556
  23.7 11.6 %copy-start.22 = (f32[384,128]{1,0:T(8,128)}, f32[384,128]{1,0:T(8,128)S(1)}, u32[]{:S(2)}) copy-start(f32[384,128]{1,0:T(8,128)S(1)} %get-tuple-element.55) | copy-start | bytes 589828
  31.0 4.4 %collective-permute-start.5 = (bf16[128,2048]{1,0:T(8,128)(2,1)}, bf16[128,2048]{1,0:T(8,128)(2,1)}, u32[]{:S(2)}, u32[]{:S(2)}) collective-permute-start(bf16[128,2048]{1,0:T(8,128)(2,1)} %bitcast.4.q_outgrad.b0), channel_id=1, source_target_pairs={{0,1},{1,0},{2,3},{3,2},{4,8},{5,9},{6,10},{7,11},{8,4},{9,5},{10,... | collective-permute-start | bytes 1572872 | tf_op jit(solution)/shard_map/ppermute | solution.py:559
  31.0 26.3 %collective-permute-start.6 = (bf16[128,2048]{1,0:T(8,128)(2,1)}, bf16[128,2048]{1,0:T(8,128)(2,1)}, u32[]{:S(2)}, u32[]{:S(2)}) collective-permute-start(bf16[128,2048]{1,0:T(8,128)(2,1)} %collective-permute-done.b3.b4), channel_id=1, source_target_pairs={{0,4},{4,0},{8,12},{12,8},{1,5},{5,1},{9,13},{13,9},{2,6},{6,2},{1... | collective-permute-start | bytes 1572872 | tf_op jit(solution)/shard_map/ppermute | solution.py:560
  33.8 25.0 %collective-permute-start.7 = (bf16[128,3584]{1,0:T(8,128)(2,1)}, bf16[128,3584]{1,0:T(8,128)(2,1)}, u32[]{:S(2)}, u32[]{:S(2)}) collective-permute-start(bf16[128,3584]{1,0:T(8,128)(2,1)} %bitcast.16), channel_id=1, source_target_pairs={{0,2},{1,3},{2,0},{3,1},{4,6},{5,7},{6,4},{7,5},{8,10},{9,11},{10,... | collective-permute-start | bytes 2752520 | tf_op jit(solution)/shard_map/ppermute | solution.py:581
  35.3 49.3 %copy-start.29 = (bf16[2,64,2048]{2,1,0:T(8,128)(2,1)}, bf16[2,64,2048]{2,1,0:T(8,128)(2,1)S(1)}, u32[]{:S(2)}) copy-start(bf16[2,64,2048]{2,1,0:T(8,128)(2,1)S(1)} %get-tuple-element.69) | copy-start | bytes 1572868
  35.3 32.7 %collective-permute-start.10 = (bf16[128,2048]{1,0:T(8,128)(2,1)S(1)}, bf16[128,2048]{1,0:T(8,128)(2,1)S(1)}, u32[]{:S(2)}, u32[]{:S(2)}) collective-permute-start(bf16[128,2048]{1,0:T(8,128)(2,1)S(1)} %bitcast.41), channel_id=1, source_target_pairs={{0,4},{4,0},{8,12},{12,8},{1,5},{5,1},{9,13},{13,9},{2,6},{6,2},{1... | collective-permute-start | bytes 1572872 | tf_op jit(solution)/shard_map/ppermute | solution.py:556
  35.4 30.5 %collective-permute-start.2 = (bf16[128,2048]{1,0:T(8,128)(2,1)S(1)}, bf16[128,2048]{1,0:T(8,128)(2,1)S(1)}, u32[]{:S(2)}, u32[]{:S(2)}) collective-permute-start(bf16[128,2048]{1,0:T(8,128)(2,1)S(1)} %bitcast.42), channel_id=1, source_target_pairs={{0,8},{4,12},{8,0},{12,4},{1,9},{5,13},{9,1},{13,5},{2,10},{6,14},... | collective-permute-start | bytes 1572872 | tf_op jit(solution)/shard_map/ppermute | solution.py:556
  58.7 13.7 %copy-start.2 = (bf16[4,64,3584]{2,1,0:T(8,128)(2,1)S(1)}, bf16[4,64,3584]{2,1,0:T(8,128)(2,1)}, u32[]{:S(2)}) copy-start(bf16[4,64,3584]{2,1,0:T(8,128)(2,1)} %param.18) | copy-start | bytes 5505028
  58.8 25.8 %collective-permute-start.8 = (bf16[2,128,2048]{2,1,0:T(8,128)(2,1)S(1)}, bf16[2,128,2048]{2,1,0:T(8,128)(2,1)S(1)}, u32[]{:S(2)}, u32[]{:S(2)}) collective-permute-start(bf16[2,128,2048]{2,1,0:T(8,128)(2,1)S(1)} %pad_maximum_fusion), channel_id=1, source_target_pairs={{0,2},{1,3},{2,0},{3,1},{4,6},{5,7},{6,4},{7,5},{8,10},{9,11},{10,... | collective-permute-start | bytes 3145736 | tf_op jit(solution)/shard_map/ppermute | solution.py:583
  65.8 18.8 %copy-start.28 = (bf16[128,2048]{1,0:T(8,128)(2,1)}, bf16[128,2048]{1,0:T(8,128)(2,1)S(1)}, u32[]{:S(2)}) copy-start(bf16[128,2048]{1,0:T(8,128)(2,1)S(1)} %collective-permute-done.2.b3.b4) | copy-start | bytes 1572868
  68.0 16.7 %copy-start.31 = (bf16[128,2048]{1,0:T(8,128)(2,1)}, bf16[128,2048]{1,0:T(8,128)(2,1)S(1)}, u32[]{:S(2)}) copy-start(bf16[128,2048]{1,0:T(8,128)(2,1)S(1)} %collective-permute-done.10.b1) | copy-start | bytes 1572868
  68.0 15.0 %collective-permute-start.11 = (bf16[128,2048]{1,0:T(8,128)(2,1)S(1)}, bf16[128,2048]{1,0:T(8,128)(2,1)S(1)}, u32[]{:S(2)}, u32[]{:S(2)}) collective-permute-start(bf16[128,2048]{1,0:T(8,128)(2,1)S(1)} %collective-permute-done.2.b3.b4), channel_id=1, source_target_pairs={{0,4},{4,0},{8,12},{12,8},{1,5},{5,1},{9,13},{13,9},{2,6},{6,2},{1... | collective-permute-start | bytes 1572872 | tf_op jit(solution)/shard_map/ppermute | solution.py:560
  70.2 14.5 %collective-permute-start.9 = (bf16[128,2048]{1,0:T(8,128)(2,1)S(1)}, bf16[128,2048]{1,0:T(8,128)(2,1)S(1)}, u32[]{:S(2)}, u32[]{:S(2)}) collective-permute-start(bf16[128,2048]{1,0:T(8,128)(2,1)S(1)} %bitcast.43), channel_id=1, source_target_pairs={{0,1},{1,0},{2,3},{3,2},{4,8},{5,9},{6,10},{7,11},{8,4},{9,5},{10,... | collective-permute-start | bytes 1572872 | tf_op jit(solution)/shard_map/ppermute | solution.py:559
  70.2 36.2 %collective-permute-start.14 = (bf16[128,2048]{1,0:T(8,128)(2,1)}, bf16[128,2048]{1,0:T(8,128)(2,1)}, u32[]{:S(2)}, u32[]{:S(2)}) collective-permute-start(bf16[128,2048]{1,0:T(8,128)(2,1)} %bitcast.9.b0), channel_id=1, source_target_pairs={{0,4},{4,0},{8,12},{12,8},{1,5},{5,1},{9,13},{13,9},{2,6},{6,2},{1... | collective-permute-start | bytes 1572872 | tf_op jit(solution)/shard_map/ppermute | solution.py:556
  77.0 7.8 %copy-start.14 = (bf16[3584,256]{1,0:T(8,128)(2,1)}, bf16[3584,256]{1,0:T(8,128)(2,1)S(1)}, u32[]{:S(2)}) copy-start(bf16[3584,256]{1,0:T(8,128)(2,1)S(1)} %get-tuple-element.48.gates) | copy-start | bytes 5505028
  77.0 7.8 %copy-start.15 = (bf16[3584,256]{1,0:T(8,128)(2,1)}, bf16[3584,256]{1,0:T(8,128)(2,1)S(1)}, u32[]{:S(2)}) copy-start(bf16[3584,256]{1,0:T(8,128)(2,1)S(1)} %get-tuple-element.63.ups) | copy-start | bytes 5505028
  83.0 23.4 %collective-permute-start.3 = (bf16[128,2048]{1,0:T(8,128)(2,1)}, bf16[128,2048]{1,0:T(8,128)(2,1)S(1)}, u32[]{:S(2)}, u32[]{:S(2)}) collective-permute-start(bf16[128,2048]{1,0:T(8,128)(2,1)} %bitcast.9.b0), channel_id=1, source_target_pairs={{0,8},{4,12},{8,0},{12,4},{1,9},{5,13},{9,1},{13,5},{2,10},{6,14},... | collective-permute-start | bytes 1572872 | tf_op jit(solution)/shard_map/ppermute | solution.py:556
  86.6 23.1 %collective-permute-start.18 = (bf16[2,128,2048]{2,1,0:T(8,128)(2,1)}, bf16[2,128,2048]{2,1,0:T(8,128)(2,1)}, u32[]{:S(2)}, u32[]{:S(2)}) collective-permute-start(bf16[2,128,2048]{2,1,0:T(8,128)(2,1)} %pad_maximum_fusion.1), channel_id=1, source_target_pairs={{0,2},{1,3},{2,0},{3,1},{4,6},{5,7},{6,4},{7,5},{8,10},{9,11},{10,... | collective-permute-start | bytes 3145736 | tf_op jit(solution)/shard_map/ppermute | solution.py:589
  106.4 14.5 %copy-start.27 = (bf16[128,2048]{1,0:T(8,128)(2,1)}, bf16[128,2048]{1,0:T(8,128)(2,1)S(1)}, u32[]{:S(2)}) copy-start(bf16[128,2048]{1,0:T(8,128)(2,1)S(1)} %collective-permute-done.3.b3.b4) | copy-start | bytes 1572868
  106.4 3.9 %collective-permute-start.13 = (bf16[128,2048]{1,0:T(8,128)(2,1)}, bf16[128,2048]{1,0:T(8,128)(2,1)S(1)}, u32[]{:S(2)}, u32[]{:S(2)}) collective-permute-start(bf16[128,2048]{1,0:T(8,128)(2,1)} %bitcast.9.b0), channel_id=1, source_target_pairs={{0,1},{1,0},{2,3},{3,2},{4,8},{5,9},{6,10},{7,11},{8,4},{9,5},{10,... | collective-permute-start | bytes 1572872 | tf_op jit(solution)/shard_map/ppermute | solution.py:559
  106.4 14.3 %collective-permute-start.15 = (bf16[128,2048]{1,0:T(8,128)(2,1)S(1)}, bf16[128,2048]{1,0:T(8,128)(2,1)S(1)}, u32[]{:S(2)}, u32[]{:S(2)}) collective-permute-start(bf16[128,2048]{1,0:T(8,128)(2,1)S(1)} %collective-permute-done.3.b3.b4), channel_id=1, source_target_pairs={{0,4},{4,0},{8,12},{12,8},{1,5},{5,1},{9,13},{13,9},{2,6},{6,2},{1... | collective-permute-start | bytes 1572872 | tf_op jit(solution)/shard_map/ppermute | solution.py:560
  109.7 30.0 %collective-permute-start.19 = (bf16[3584,128]{1,0:T(8,128)(2,1)}, bf16[3584,128]{1,0:T(8,128)(2,1)}, u32[]{:S(2)}, u32[]{:S(2)}) collective-permute-start(bf16[3584,128]{1,0:T(8,128)(2,1)} %get-tuple-element.57), channel_id=1, source_target_pairs={{0,2},{1,3},{2,0},{3,1},{4,6},{5,7},{6,4},{7,5},{8,10},{9,11},{10,... | collective-permute-start | bytes 2752520 | tf_op jit(solution)/shard_map/ppermute | solution.py:593
  110.3 10.7 %copy-start.34 = (bf16[128,2048]{1,0:T(8,128)(2,1)}, bf16[128,2048]{1,0:T(8,128)(2,1)S(1)}, u32[]{:S(2)}) copy-start(bf16[128,2048]{1,0:T(8,128)(2,1)S(1)} %collective-permute-done.13.b2) | copy-start | bytes 1572868
  122.7 16.7 %copy-start.23 = (f32[384,128]{1,0:T(8,128)S(1)}, f32[384,128]{1,0:T(8,128)}, u32[]{:S(2)}) copy-start(f32[384,128]{1,0:T(8,128)} %copy-done.22) | copy-start | bytes 589828
  122.7 17.0 %copy-start.5 = (bf16[64,3584]{1,0:T(8,128)(2,1)S(1)}, bf16[64,3584]{1,0:T(8,128)(2,1)}, u32[]{:S(2)}) copy-start(bf16[64,3584]{1,0:T(8,128)(2,1)} %proj_gate.5) | copy-start | bytes 1376260
  122.7 17.0 %copy-start.7 = (bf16[64,3584]{1,0:T(8,128)(2,1)S(1)}, bf16[64,3584]{1,0:T(8,128)(2,1)}, u32[]{:S(2)}) copy-start(bf16[64,3584]{1,0:T(8,128)(2,1)} %proj_up.5) | copy-start | bytes 1376260
  122.7 17.0 %copy-start.10 = (bf16[2,64,3584]{2,1,0:T(8,128)(2,1)S(1)}, bf16[2,64,3584]{2,1,0:T(8,128)(2,1)}, u32[]{:S(2)}) copy-start(bf16[2,64,3584]{2,1,0:T(8,128)(2,1)} %param.22) | copy-start | bytes 2752516
  122.7 17.0 %copy-start.12 = (bf16[2,64,3584]{2,1,0:T(8,128)(2,1)S(1)}, bf16[2,64,3584]{2,1,0:T(8,128)(2,1)}, u32[]{:S(2)}) copy-start(bf16[2,64,3584]{2,1,0:T(8,128)(2,1)} %param.23) | copy-start | bytes 2752516
  122.7 35.6 %collective-permute-start.21 = (bf16[2,128,2048]{2,1,0:T(8,128)(2,1)}, bf16[2,128,2048]{2,1,0:T(8,128)(2,1)}, u32[]{:S(2)}, u32[]{:S(2)}) collective-permute-start(bf16[2,128,2048]{2,1,0:T(8,128)(2,1)} %pad_maximum_fusion.2), channel_id=1, source_target_pairs={{0,2},{1,3},{2,0},{3,1},{4,6},{5,7},{6,4},{7,5},{8,10},{9,11},{10,... | collective-permute-start | bytes 3145736 | tf_op jit(solution)/shard_map/ppermute | solution.py:596
  138.4 41.5 %collective-permute-start.22 = (bf16[3584,128]{1,0:T(8,128)(2,1)}, bf16[3584,128]{1,0:T(8,128)(2,1)S(1)}, u32[]{:S(2)}, u32[]{:S(2)}) collective-permute-start(bf16[3584,128]{1,0:T(8,128)(2,1)} %get-tuple-element.59), channel_id=1, source_target_pairs={{0,2},{1,3},{2,0},{3,1},{4,6},{5,7},{6,4},{7,5},{8,10},{9,11},{10,... | collective-permute-start | bytes 2752520 | tf_op jit(solution)/shard_map/ppermute | solution.py:600
  139.4 8.8 %collective-permute-start.16 = (f32[384,128]{1,0:T(8,128)S(1)}, f32[384,128]{1,0:T(8,128)S(1)}, u32[]{:S(2)}, u32[]{:S(2)}) collective-permute-start(f32[384,128]{1,0:T(8,128)S(1)} %copy-done.23), channel_id=1, source_target_pairs={{0,4},{4,0},{8,12},{12,8},{1,5},{5,1},{9,13},{13,9},{2,6},{6,2},{1... | collective-permute-start | bytes 589832 | tf_op jit(solution)/shard_map/ppermute | solution.py:601
  146.4 5.8 %collective-permute-start.20 = (f32[128,192]{1,0:T(8,128)S(1)}, f32[128,192]{1,0:T(8,128)S(1)}, u32[]{:S(2)}, u32[]{:S(2)}) collective-permute-start(f32[128,192]{1,0:T(8,128)S(1)} %pad_maximum_fusion.3), channel_id=1, source_target_pairs={{0,4},{4,0},{8,12},{12,8},{1,5},{5,1},{9,13},{13,9},{2,6},{6,2},{1... | collective-permute-start | bytes 294920 | tf_op jit(solution)/shard_map/ppermute | solution.py:606
  148.2 28.4 %collective-permute-start.17 = (f32[384,128]{1,0:T(8,128)S(1)}, f32[384,128]{1,0:T(8,128)S(1)}, u32[]{:S(2)}, u32[]{:S(2)}) collective-permute-start(f32[384,128]{1,0:T(8,128)S(1)} %add.32), channel_id=1, source_target_pairs={{0,8},{4,12},{8,0},{12,4},{1,9},{5,13},{9,1},{13,5},{2,10},{6,14},... | collective-permute-start | bytes 589832 | tf_op jit(solution)/shard_map/ppermute | solution.py:611
  152.2 24.4 %collective-permute-start.24 = (f32[128,192]{1,0:T(8,128)S(1)}, f32[128,192]{1,0:T(8,128)S(1)}, u32[]{:S(2)}, u32[]{:S(2)}) collective-permute-start(f32[128,192]{1,0:T(8,128)S(1)} %fusion), channel_id=1, source_target_pairs={{0,8},{4,12},{8,0},{12,4},{1,9},{5,13},{9,1},{13,5},{2,10},{6,14},... | collective-permute-start | bytes 294920 | tf_op jit(solution)/shard_map/ppermute | solution.py:612
  158.3 18.4 %copy-start.25 = (s32[2]{0:T(128)S(1)}, s32[2]{0:T(128)}, u32[]{:S(2)}) copy-start(s32[2]{0:T(128)} %lengths.2) | copy-start | bytes 28
  158.3 21.5 %copy-start.3 = (bf16[4,64,3584]{2,1,0:T(8,128)(2,1)S(1)}, bf16[4,64,3584]{2,1,0:T(8,128)(2,1)}, u32[]{:S(2)}) copy-start(bf16[4,64,3584]{2,1,0:T(8,128)(2,1)} %param.18) | copy-start | bytes 5505028
  177.6 10.1 %collective-permute-start.27 = (f32[2,192,64]{2,1,0:T(8,128)S(1)}, f32[2,192,64]{2,1,0:T(8,128)S(1)}, u32[]{:S(2)}, u32[]{:S(2)}) collective-permute-start(f32[2,192,64]{2,1,0:T(8,128)S(1)} %shard_map.161.q0), channel_id=1, source_target_pairs={{0,3},{1,2},{2,1},{3,0},{4,7},{5,6},{6,5},{7,4},{8,11},{9,10},{10,... | collective-permute-start | bytes 294920 | tf_op jit(solution)/shard_map/ppermute | solution.py:614
  177.7 10.0 %collective-permute-start.26 = (f32[2,192,64]{2,1,0:T(8,128)S(1)}, f32[2,192,64]{2,1,0:T(8,128)S(1)}, u32[]{:S(2)}, u32[]{:S(2)}) collective-permute-start(f32[2,192,64]{2,1,0:T(8,128)S(1)} %shard_map.161.q0), channel_id=1, source_target_pairs={{0,2},{1,3},{2,0},{3,1},{4,6},{5,7},{6,4},{7,5},{8,10},{9,11},{10,... | collective-permute-start | bytes 294920 | tf_op jit(solution)/shard_map/ppermute | solution.py:614
  177.8 10.0 %collective-permute-start.25 = (f32[2,192,64]{2,1,0:T(8,128)S(1)}, f32[2,192,64]{2,1,0:T(8,128)S(1)}, u32[]{:S(2)}, u32[]{:S(2)}) collective-permute-start(f32[2,192,64]{2,1,0:T(8,128)S(1)} %shard_map.161.q0), channel_id=1, source_target_pairs={{0,1},{1,0},{2,3},{3,2},{4,5},{5,4},{6,7},{7,6},{8,9},{9,8},{10,11... | collective-permute-start | bytes 294920 | tf_op jit(solution)/shard_map/ppermute | solution.py:614
  179.6 8.2 %collective-permute-start.23 = (f32[128,128]{1,0:T(8,128)}, f32[128,128]{1,0:T(8,128)S(1)}, u32[]{:S(2)}, u32[]{:S(2)}) collective-permute-start(f32[128,128]{1,0:T(8,128)} %get-tuple-element.67), channel_id=1, source_target_pairs={{0,2},{1,3},{2,0},{3,1},{4,6},{5,7},{6,4},{7,5},{8,10},{9,11},{10,... | collective-permute-start | bytes 196616 | tf_op jit(solution)/shard_map/ppermute | solution.py:618
  189.2 5.4 %collective-permute-start.30 = (f32[4,8]{1,0:T(4,128)S(1)}, f32[4,8]{1,0:T(4,128)S(1)}, u32[]{:S(2)}, u32[]{:S(2)}) collective-permute-start(f32[4,8]{1,0:T(4,128)S(1)} %shard_map.162), channel_id=1, source_target_pairs={{0,12},{4,8},{8,4},{12,0},{1,13},{5,9},{9,5},{13,1},{2,14},{6,10},... | collective-permute-start | bytes 392 | tf_op jit(solution)/shard_map/ppermute | solution.py:620
  189.3 5.4 %collective-permute-start.29 = (f32[4,8]{1,0:T(4,128)S(1)}, f32[4,8]{1,0:T(4,128)S(1)}, u32[]{:S(2)}, u32[]{:S(2)}) collective-permute-start(f32[4,8]{1,0:T(4,128)S(1)} %shard_map.162), channel_id=1, source_target_pairs={{0,8},{4,12},{8,0},{12,4},{1,9},{5,13},{9,1},{13,5},{2,10},{6,14},... | collective-permute-start | bytes 392 | tf_op jit(solution)/shard_map/ppermute | solution.py:620
  190.3 4.9 %collective-permute-start.28 = (f32[4,8]{1,0:T(4,128)S(1)}, f32[4,8]{1,0:T(4,128)S(1)}, u32[]{:S(2)}, u32[]{:S(2)}) collective-permute-start(f32[4,8]{1,0:T(4,128)S(1)} %shard_map.162), channel_id=1, source_target_pairs={{0,4},{4,0},{8,12},{12,8},{1,5},{5,1},{9,13},{13,9},{2,6},{6,2},{1... | collective-permute-start | bytes 392 | tf_op jit(solution)/shard_map/ppermute | solution.py:620
  (20 other events, 42.3 us)

commit v11 on v10

--- a/solution.py
+++ b/solution.py
@@ -10,6 +10,7 @@
 RANK = 64
 SEQ = 64
 TILE = 512
+WIDE = 1792
 VMEM_BYTES = 40 * 1024 * 1024
 BIG_VMEM_BYTES = 58 * 1024 * 1024
 
@@ -136,12 +137,12 @@
     return pl.CostEstimate(flops=1024, bytes_accessed=1024, transcendentals=0)
 
 
-def tile_columns(number, block=0):
-    return pl.BlockSpec((number, TILE), lambda i: (block, i))
-
-
-def tile_rows(width):
-    return pl.BlockSpec((TILE, width), lambda i: (i, 0))
+def tile_columns(number, block=0, tile=TILE):
+    return pl.BlockSpec((number, tile), lambda i: (block, i))
+
+
+def tile_rows(width, tile=TILE):
+    return pl.BlockSpec((tile, width), lambda i: (i, 0))
 
 
 def whole(shape):
@@ -266,8 +267,10 @@
     units, number = near_sum.shape
     return pl.pallas_call(
         finish_kernel,
-        grid=(units // TILE,),
-        in_specs=[tile_rows(number)] * 2 + [tile_columns(number)] * 2 + [tile_columns(RANK)] * 2,
+        grid=(units // WIDE,),
+        in_specs=[tile_rows(number, WIDE)] * 2
+        + [tile_columns(number, 0, WIDE)] * 2
+        + [tile_columns(RANK, 0, WIDE)] * 2,
         out_specs=whole((number, 2 * RANK)),
         out_shape=jax.ShapeDtypeStruct((number, 2 * RANK), jnp.float32),
         compiler_params=params(),
@@ -577,7 +580,7 @@
     )
 
     q_blocks = last_hops(*q_hops[:2], after(q_hops[2], own_in_out))
-    a_hops = first_hops(after(t_outgrad[:cut], q_hops[2], far_gate))
+    a_hops = first_hops(after(t_outgrad[:cut], q_hops[2], far_gate, weight_sib))
     far_up = to_chip(after(t_up[cut:], far_gate))
     q_send = after(crossing_pair(*q_blocks), far_up)
     q_far = to_chip(q_send)
@@ -597,8 +600,8 @@
     a_near_sum, a_far_sum = partial_sums(
         flags, a_blocks, after(a_far, b_send), weight_own, weight_sib
     )
+    in_out = own_in_out + outer(after(own_in_out, b_send))
     a_returned = to_chip(a_far_sum)
-    in_out = own_in_out + outer(after(own_in_out, b_send))
     q_gradient = finished_sides(
         q_near_sum, after(q_returned, a_far_sum), q_gate, q_up, proj_gate, proj_up
     )
@@ -612,10 +615,13 @@
     q_sums = q_sums + after(across(q_sums), b_near)
     own_found = query_features(query_lengths, in_out[2 * cut :], q_sums)
     found = (own_found, to_core(own_found), to_chip(own_found), to_other(own_found))
-    a_gradient = finished_sides(a_near_sum, a_returned, t_gate, t_up, proj_gate, proj_up)
+    b_far_sides = to_chip(b_away)
+    a_gradient = finished_sides(
+        a_near_sum, after(a_returned, b_far_sides), t_gate, t_up, proj_gate, proj_up
+    )
     own_scores = partial_scores(
         train_lengths, place, in_out[: 2 * cut], hidden[: 2 * cut], a_gradient, b_near,
-        to_chip(b_away), found,
+        b_far_sides, found,
     )
     scores = own_scores + outer(own_scores) + across(own_scores) + opposite(own_scores)
     return scores / (RANK * SEQ)

time: 197 us -> 216 us (1.096)
  waiting for transfers between devices: 54.6 us -> 76.9 us
  Pallas kernels: 66.7 us -> 63.5 us
    ppermute x6, starting transfers between devices: 18.4 us -> 11.5 us  [first_hops(): return (own, outer(own), across(own))]
    ppermute x6, waiting for transfers between devices: 20 us -> 26.4 us  [first_hops(): return (own, outer(own), across(own))]
    ppermute x1, waiting for transfers between devices: 3.48 us -> 9.76 us  [moving_plan(): b_far_sides = to_chip(b_away)]
    ppermute x3, starting transfers between devices: 5.81 us -> 11.8 us  [last_hops(): return (own, one, mid, two, two, outer(after(two, one)))]
    ppermute x3, waiting for transfers between devices: 28 us -> 22.3 us  [last_hops(): return (own, one, mid, two, two, outer(after(two, one)))]
    ppermute x1, waiting for transfers between devices: 0.01 us -> 5.56 us  [moving_plan(): far_up = to_chip(after(t_up[cut:], far_gate))]
    ppermute x1, waiting for transfers between devices: 0.01 us -> 5.36 us  [moving_plan(): b_far = to_chip(b_send)]
    ppermute x1, starting transfers between devices: 6.11 us -> 2.89 us  [moving_plan(): q_sums = q_sums + after(across(q_sums), b_near)]
  transfers between devices with their start and end apart: 31 -> 31, of which waited for: 12 -> 15; matrix products, arithmetic and copies ran while one was open for 4% -> 4% of each run, Pallas kernels for 33% -> 29%
where the time goes in v11:
time: 216 us; the launch traced here: 215 us
  waiting for transfers between devices  76.9 us (36%)
  Pallas kernels  63.5 us (29%)
  starting transfers between devices  49.5 us (23%)
  local copies, waits for them, and re-layouts  19.4 us (9%)
  other arithmetic  5.4 us (2%)
    pallas_call x2, Pallas kernels, partial_sums(): pl.pallas_call(partial_kernel, grid=(units // TILE,), in_specs=[SCALARS]...  28.7 us
    ppermute x6, waiting for transfers between devices, first_hops(): return (own, outer(own), across(own))  26.4 us
    ppermute x3, waiting for transfers between devices, last_hops(): return (own, one, mid, two, two, outer(after(two, one)))  22.3 us
    pallas_call x1, Pallas kernels, lent_sides(): pl.pallas_call(lent_kernel, grid=(units // TILE,), in_specs=[SCALARS] + [...  18.2 us
    unnamed x74, local copies, waits for them, and re-layouts  15.9 us
    ppermute x3, starting transfers between devices, last_hops(): return (own, one, mid, two, two, outer(after(two, one)))  11.8 us
    ppermute x6, starting transfers between devices, first_hops(): return (own, outer(own), across(own))  11.5 us
    ppermute x1, waiting for transfers between devices, moving_plan(): b_far_sides = to_chip(b_away)  9.76 us
  transfers between devices with their start and end apart: 31, of which 15 were waited for; matrix products, arithmetic and copies ran while one was open for 4% of the time, Pallas kernels for 29%

profile of v11, /device:TPU:0, one launch (start us, length us, event | category | flops | bytes accessed | tf_op | source)
XLA Modules:
  0.0 215.1 jit_solution(12128947868931069599)
XLA Ops:
  0.5 1.3 slice.40
  1.8 2.6 %collective-permute-start.1 = (bf16[128,3584]{1,0:T(8,128)(2,1)S(1)}, bf16[128,3584]{1,0:T(8,128)(2,1)S(1)}, u32[]{:S(2)}, u32[]{:S(2)}) collective-permute-start(bf16[128,3584]{1,0:T(8,128)(2,1)S(1)} %bitcast.46), channel_id=1, source_target_pairs={{0,2},{1,3},{2,0},{3,1},{4,6},{5,7},{6,4},{7,5},{8,10},{9,11},{10,... | collective-permute-start | bytes 2752520 | tf_op jit(solution)/shard_map/ppermute | solution.py:576
  4.4 2.6 %collective-permute-start = (bf16[128,2048]{1,0:T(8,128)(2,1)}, bf16[128,2048]{1,0:T(8,128)(2,1)}, u32[]{:S(2)}, u32[]{:S(2)}) collective-permute-start(bf16[128,2048]{1,0:T(8,128)(2,1)} %bitcast.4.q_outgrad.b0), channel_id=1, source_target_pairs={{0,8},{4,12},{8,0},{12,4},{1,9},{5,13},{9,1},{13,5},{2,10},{6,14},... | collective-permute-start | bytes 1572872 | tf_op jit(solution)/shard_map/ppermute | solution.py:559
  7.0 1.6 collective-permute-start.5
  8.6 1.5 copy-done.1
  10.1 1.2 copy-done.4
  11.3 1.2 copy-done.9
  12.5 1.2 copy-done.11
  13.7 1.2 copy-done.17
  18.8 4.9 %shard_map.154 = (f32[384,128]{1,0:T(8,128)S(1)}, f32[384,64]{1,0:T(8,128)S(1)}) custom-call(bf16[256,2048]{1,0:T(8,128)(2,1)S(1)} %bitcast.39, bf16[128,2048]{1,0:T(8,128)(2,1)S(1)} %bitcast.40, bf16[256,2048]{1,0:T(8,128)(2,1)S(1)} %bitcast.34, bf16[128,2048]{1,0:T(8,128)(2,1)} %bitcast.4.q_outgrad.b0, bf16[64,2048]{1,0:T(8,128)(2,1)S(1)} %copy-done.20, ...), custom_call_target="tpu_custom_call" | custom-call | flops 1024 | bytes 1024 | tf_op jit(solution)/shard_map/pallas_call | solution.py:396
  23.7 7.2 %collective-permute-done.b3.b4 = bf16[128,2048]{1,0:T(8,128)(2,1)} collective-permute-done((bf16[128,2048]{1,0:T(8,128)(2,1)}, bf16[128,2048]{1,0:T(8,128)(2,1)}, u32[]{:S(2)}, u32[]{:S(2)}) %collective-permute-start) | collective-permute-done | bytes 524320 | tf_op jit(solution)/shard_map/ppermute | solution.py:559
  31.0 1.4 collective-permute-start.7
  35.0 9.2 %collective-permute-done.7.b5 = bf16[128,2048]{1,0:T(8,128)(2,1)} collective-permute-done((bf16[128,2048]{1,0:T(8,128)(2,1)}, bf16[128,2048]{1,0:T(8,128)(2,1)}, u32[]{:S(2)}, u32[]{:S(2)}) %collective-permute-start.7) | collective-permute-done | bytes 524320 | tf_op jit(solution)/shard_map/ppermute | solution.py:563
  44.2 1.5 select_bitcast_fusion.5
  45.7 4.7 %collective-permute-start.3 = (bf16[128,2048]{1,0:T(8,128)(2,1)S(1)}, bf16[128,2048]{1,0:T(8,128)(2,1)S(1)}, u32[]{:S(2)}, u32[]{:S(2)}) collective-permute-start(bf16[128,2048]{1,0:T(8,128)(2,1)S(1)} %bitcast.42), channel_id=1, source_target_pairs={{0,8},{4,12},{8,0},{12,4},{1,9},{5,13},{9,1},{13,5},{2,10},{6,14},... | collective-permute-start | bytes 1572872 | tf_op jit(solution)/shard_map/ppermute | solution.py:559
  50.9 5.6 %collective-permute-done.8.far_up = bf16[128,3584]{1,0:T(8,128)(2,1)} collective-permute-done((bf16[128,3584]{1,0:T(8,128)(2,1)}, bf16[128,3584]{1,0:T(8,128)(2,1)}, u32[]{:S(2)}, u32[]{:S(2)}) %collective-permute-start.8) | collective-permute-done | bytes 917536 | tf_op jit(solution)/shard_map/ppermute | solution.py:584
  57.0 15.7 %collective-permute-done.3.b3.b4 = bf16[128,2048]{1,0:T(8,128)(2,1)S(1)} collective-permute-done((bf16[128,2048]{1,0:T(8,128)(2,1)S(1)}, bf16[128,2048]{1,0:T(8,128)(2,1)S(1)}, u32[]{:S(2)}, u32[]{:S(2)}) %collective-permute-start.3) | collective-permute-done | bytes 524320 | tf_op jit(solution)/shard_map/ppermute | solution.py:559
  73.1 1.3 collective-permute-start.12
  74.4 4.6 %shard_map.155 = (bf16[3584,256]{1,0:T(8,128)(2,1)S(1)}, bf16[3584,256]{1,0:T(8,128)(2,1)S(1)}) custom-call(bf16[256,3584]{1,0:T(8,128)(2,1)S(1)} %bitcast.29, bf16[256,3584]{1,0:T(8,128)(2,1)S(1)} %bitcast.32, bf16[128,3584]{1,0:T(8,128)(2,1)S(1)} %collective-permute-done.1.far_gate, bf16[128,3584]{1,0:T(8,128)(2,1)} %collective-permute-done.8.far_up), custom_call_target="tpu_custom_call" | custom-call | flops 1024 | bytes 1024 | tf_op jit(solution)/shard_map/pallas_call | solution.py:295
  79.1 2.2 %collective-permute-start.4 = (bf16[128,2048]{1,0:T(8,128)(2,1)}, bf16[128,2048]{1,0:T(8,128)(2,1)S(1)}, u32[]{:S(2)}, u32[]{:S(2)}) collective-permute-start(bf16[128,2048]{1,0:T(8,128)(2,1)} %bitcast.9.b0), channel_id=1, source_target_pairs={{0,8},{4,12},{8,0},{12,4},{1,9},{5,13},{9,1},{13,5},{2,10},{6,14},... | collective-permute-start | bytes 1572872 | tf_op jit(solution)/shard_map/ppermute | solution.py:559
  81.3 7.9 %collective-permute-done.12.b5 = bf16[128,2048]{1,0:T(8,128)(2,1)S(1)} collective-permute-done((bf16[128,2048]{1,0:T(8,128)(2,1)S(1)}, bf16[128,2048]{1,0:T(8,128)(2,1)S(1)}, u32[]{:S(2)}, u32[]{:S(2)}) %collective-permute-start.12) | collective-permute-done | bytes 524320 | tf_op jit(solution)/shard_map/ppermute | solution.py:563
  91.9 14.4 %shard_map.156 = (f32[3584,128]{1,0:T(8,128)}, bf16[3584,128]{1,0:T(8,128)(2,1)}) custom-call(s32[2]{0:T(128)} %pad_add_fusion.flags, bf16[128,2048]{1,0:T(8,128)(2,1)} %bitcast.4.q_outgrad.b0, bf16[128,2048]{1,0:T(8,128)(2,1)} %copy-done.28, bf16[128,2048]{1,0:T(8,128)(2,1)} %collective-permute-done.6.b2, bf16[128,2048]{1,0:T(8,128)(2,1)} %collective-permute-done.b3.b4, ...), custom_call_target="tpu_custom_call" | custom-call | flops 1024 | bytes 1024 | tf_op jit(solution)/shard_map/pallas_call | solution.py:241
  106.3 3.0 %collective-permute-done.4.b3.b4 = bf16[128,2048]{1,0:T(8,128)(2,1)S(1)} collective-permute-done((bf16[128,2048]{1,0:T(8,128)(2,1)}, bf16[128,2048]{1,0:T(8,128)(2,1)S(1)}, u32[]{:S(2)}, u32[]{:S(2)}) %collective-permute-start.4) | collective-permute-done | bytes 524320 | tf_op jit(solution)/shard_map/ppermute | solution.py:559
  109.3 9.0 %collective-permute-start.15 = (bf16[128,2048]{1,0:T(8,128)(2,1)S(1)}, bf16[128,2048]{1,0:T(8,128)(2,1)S(1)}, u32[]{:S(2)}, u32[]{:S(2)}) collective-permute-start(bf16[128,2048]{1,0:T(8,128)(2,1)S(1)} %collective-permute-done.4.b3.b4), channel_id=1, source_target_pairs={{0,4},{4,0},{8,12},{12,8},{1,5},{5,1},{9,13},{13,9},{2,6},{6,2},{1... | collective-permute-start | bytes 1572872 | tf_op jit(solution)/shard_map/ppermute | solution.py:563
  118.3 1.9 collective-permute-start.19
  120.3 5.2 %collective-permute-done.15.b5 = bf16[128,2048]{1,0:T(8,128)(2,1)S(1)} collective-permute-done((bf16[128,2048]{1,0:T(8,128)(2,1)S(1)}, bf16[128,2048]{1,0:T(8,128)(2,1)S(1)}, u32[]{:S(2)}, u32[]{:S(2)}) %collective-permute-start.15) | collective-permute-done | bytes 524320 | tf_op jit(solution)/shard_map/ppermute | solution.py:563
  126.5 1.1 pad_maximum_fusion.2
  127.6 2.7 %collective-permute-start.21 = (bf16[2,128,2048]{2,1,0:T(8,128)(2,1)}, bf16[2,128,2048]{2,1,0:T(8,128)(2,1)S(1)}, u32[]{:S(2)}, u32[]{:S(2)}) collective-permute-start(bf16[2,128,2048]{2,1,0:T(8,128)(2,1)} %pad_maximum_fusion.2), channel_id=1, source_target_pairs={{0,2},{1,3},{2,0},{3,1},{4,6},{5,7},{6,4},{7,5},{8,10},{9,11},{10,... | collective-permute-start | bytes 3145736 | tf_op jit(solution)/shard_map/ppermute | solution.py:599
  130.3 14.3 %shard_map.157 = (f32[3584,128]{1,0:T(8,128)}, bf16[3584,128]{1,0:T(8,128)(2,1)}) custom-call(s32[2]{0:T(128)} %pad_add_fusion.flags, bf16[128,2048]{1,0:T(8,128)(2,1)} %bitcast.41, bf16[128,2048]{1,0:T(8,128)(2,1)} %copy-done.30, bf16[128,2048]{1,0:T(8,128)(2,1)} %copy-done.32, bf16[128,2048]{1,0:T(8,128)(2,1)} %copy-done.26, bf16[128,2048]{1,0:T(8,128)(2,1)} %copy-done.26, ...), custom_call_target="tpu_custom_call" | custom-call | flops 1024 | bytes 1024 | tf_op jit(solution)/shard_map/pallas_call | solution.py:241
  144.9 2.1 collective-permute-start.16
  147.0 1.5 copy-done.16
  148.5 2.4 %shard_map.158 = f32[128,128]{1,0:T(8,128)S(1)} custom-call(f32[3584,128]{1,0:T(8,128)S(1)} %copy-done.16, bf16[3584,128]{1,0:T(8,128)(2,1)} %collective-permute-done.19.returned, bf16[128,3584]{1,0:T(8,128)(2,1)S(1)} %bitcast.36, bf16[128,3584]{1,0:T(8,128)(2,1)S(1)} %bitcast.38, bf16[64,3584]{1,0:T(8,128)(2,1)S(1)} %copy-done.5, bf16[64,3584]{1,0:T(8,128)(2,1)S(1)} %copy-done.7), custom_call_target="tpu_custom_call" | custom-call | flops 1024 | bytes 1024 | tf_op jit(solution)/shard_map/pallas_call | solution.py:268
  151.0 2.7 %collective-permute-done.16 = f32[384,128]{1,0:T(8,128)S(1)} collective-permute-done((f32[384,128]{1,0:T(8,128)S(1)}, f32[384,128]{1,0:T(8,128)S(1)}, u32[]{:S(2)}, u32[]{:S(2)}) %collective-permute-start.16) | collective-permute-done | bytes 196640 | tf_op jit(solution)/shard_map/ppermute | solution.py:603
  153.7 1.4 collective-permute-start.17
  156.0 2.9 %collective-permute-start.24 = (f32[128,192]{1,0:T(8,128)S(1)}, f32[128,192]{1,0:T(8,128)S(1)}, u32[]{:S(2)}, u32[]{:S(2)}) collective-permute-start(f32[128,192]{1,0:T(8,128)S(1)} %fusion), channel_id=1, source_target_pairs={{0,8},{4,12},{8,0},{12,4},{1,9},{5,13},{9,1},{13,5},{2,10},{6,14},... | collective-permute-start | bytes 294920 | tf_op jit(solution)/shard_map/ppermute | solution.py:615
  158.9 5.4 %collective-permute-done.21.far = bf16[2,128,2048]{2,1,0:T(8,128)(2,1)S(1)} collective-permute-done((bf16[2,128,2048]{2,1,0:T(8,128)(2,1)}, bf16[2,128,2048]{2,1,0:T(8,128)(2,1)S(1)}, u32[]{:S(2)}, u32[]{:S(2)}) %collective-permute-start.21) | collective-permute-done | bytes 1048608 | tf_op jit(solution)/shard_map/ppermute | solution.py:599
  165.3 18.2 %shard_map.159 = (f32[128,128]{1,0:T(8,128)}, f32[128,128]{1,0:T(8,128)}) custom-call(s32[2]{0:T(128)} %pad_add_fusion.flags, bf16[128,2048]{1,0:T(8,128)(2,1)} %bitcast.9.b0, bf16[128,2048]{1,0:T(8,128)(2,1)} %copy-done.29, bf16[128,2048]{1,0:T(8,128)(2,1)} %copy-done.34, bf16[128,2048]{1,0:T(8,128)(2,1)} %copy-done.25, bf16[128,2048]{1,0:T(8,128)(2,1)} %copy-done.25, ...), custom_call_target="tpu_custom_call" | custom-call | flops 1024 | bytes 1024 | tf_op jit(solution)/shard_map/pallas_call | solution.py:337
  184.6 1.3 collective-permute-start.26
  186.5 1.3 collective-permute-start.23
  187.8 9.8 %collective-permute-done.23.far = f32[128,128]{1,0:T(8,128)S(1)} collective-permute-done((f32[128,128]{1,0:T(8,128)}, f32[128,128]{1,0:T(8,128)S(1)}, u32[]{:S(2)}, u32[]{:S(2)}) %collective-permute-start.23) | collective-permute-done | bytes 65568 | tf_op jit(solution)/shard_map/ppermute | solution.py:618
  197.5 1.5 copy-done.13
  199.0 2.4 %shard_map.160.early = f32[128,128]{1,0:T(8,128)S(1)} custom-call(f32[3584,128]{1,0:T(8,128)S(1)} %copy-done.13, bf16[3584,128]{1,0:T(8,128)(2,1)} %collective-permute-done.22.returned, bf16[256,3584]{1,0:T(8,128)(2,1)S(1)} %bitcast.30, bf16[256,3584]{1,0:T(8,128)(2,1)S(1)} %bitcast.33, bf16[64,3584]{1,0:T(8,128)(2,1)S(1)} %copy-done.6, ...), custom_call_target="tpu_custom_call" | custom-call | flops 1024 | bytes 1024 | tf_op jit(solution)/shard_map/pallas_call | solution.py:268
  201.5 1.4 shard_map.162
  202.9 4.8 %collective-permute-start.28 = (f32[4,8]{1,0:T(4,128)S(1)}, f32[4,8]{1,0:T(4,128)S(1)}, u32[]{:S(2)}, u32[]{:S(2)}) collective-permute-start(f32[4,8]{1,0:T(4,128)S(1)} %shard_map.162), channel_id=1, source_target_pairs={{0,4},{4,0},{8,12},{12,8},{1,5},{5,1},{9,13},{13,9},{2,6},{6,2},{1... | collective-permute-start | bytes 392 | tf_op jit(solution)/shard_map/ppermute | solution.py:626
  207.7 1.4 collective-permute-start.29
  209.1 1.4 collective-permute-start.30
  210.5 1.7 collective-permute-done.29
  212.2 2.3 %collective-permute-done.30 = f32[4,8]{1,0:T(4,128)S(1)} collective-permute-done((f32[4,8]{1,0:T(4,128)S(1)}, f32[4,8]{1,0:T(4,128)S(1)}, u32[]{:S(2)}, u32[]{:S(2)}) %collective-permute-start.30) | collective-permute-done | bytes 160 | tf_op jit(solution)/shard_map/ppermute | solution.py:626
  (117 shorter events, 16.6 us)
Async XLA Ops:
  0.0 45.7 %collective-permute-start.2 = (bf16[3584,2048]{1,0:T(8,128)(2,1)}, bf16[3584,2048]{1,0:T(8,128)(2,1)}, u32[]{:S(2)}, u32[]{:S(2)}) collective-permute-start(bf16[3584,2048]{1,0:T(8,128)(2,1)} %weight_own.5), channel_id=1, source_target_pairs={{0,1},{1,0},{2,3},{3,2},{4,5},{5,4},{6,7},{7,6},{8,9},{9,8},{10,11... | collective-permute-start | bytes 44040200 | tf_op jit(solution)/shard_map/ppermute | solution.py:574
  1.8 31.6 %collective-permute-start.1 = (bf16[128,3584]{1,0:T(8,128)(2,1)S(1)}, bf16[128,3584]{1,0:T(8,128)(2,1)S(1)}, u32[]{:S(2)}, u32[]{:S(2)}) collective-permute-start(bf16[128,3584]{1,0:T(8,128)(2,1)S(1)} %bitcast.46), channel_id=1, source_target_pairs={{0,2},{1,3},{2,0},{3,1},{4,6},{5,7},{6,4},{7,5},{8,10},{9,11},{10,... | collective-permute-start | bytes 2752520 | tf_op jit(solution)/shard_map/ppermute | solution.py:576
  4.4 26.5 %collective-permute-start = (bf16[128,2048]{1,0:T(8,128)(2,1)}, bf16[128,2048]{1,0:T(8,128)(2,1)}, u32[]{:S(2)}, u32[]{:S(2)}) collective-permute-start(bf16[128,2048]{1,0:T(8,128)(2,1)} %bitcast.4.q_outgrad.b0), channel_id=1, source_target_pairs={{0,8},{4,12},{8,0},{12,4},{1,9},{5,13},{9,1},{13,5},{2,10},{6,14},... | collective-permute-start | bytes 1572872 | tf_op jit(solution)/shard_map/ppermute | solution.py:559
  7.0 24.0 %collective-permute-start.5 = (bf16[128,2048]{1,0:T(8,128)(2,1)}, bf16[128,2048]{1,0:T(8,128)(2,1)S(1)}, u32[]{:S(2)}, u32[]{:S(2)}) collective-permute-start(bf16[128,2048]{1,0:T(8,128)(2,1)} %bitcast.4.q_outgrad.b0), channel_id=1, source_target_pairs={{0,4},{4,0},{8,12},{12,8},{1,5},{5,1},{9,13},{13,9},{2,6},{6,2},{1... | collective-permute-start | bytes 1572872 | tf_op jit(solution)/shard_map/ppermute | solution.py:559
  31.0 13.2 %collective-permute-start.7 = (bf16[128,2048]{1,0:T(8,128)(2,1)}, bf16[128,2048]{1,0:T(8,128)(2,1)}, u32[]{:S(2)}, u32[]{:S(2)}) collective-permute-start(bf16[128,2048]{1,0:T(8,128)(2,1)} %collective-permute-done.b3.b4), channel_id=1, source_target_pairs={{0,4},{4,0},{8,12},{12,8},{1,5},{5,1},{9,13},{13,9},{2,6},{6,2},{1... | collective-permute-start | bytes 1572872 | tf_op jit(solution)/shard_map/ppermute | solution.py:563
  32.4 11.8 %collective-permute-start.6 = (bf16[128,2048]{1,0:T(8,128)(2,1)}, bf16[128,2048]{1,0:T(8,128)(2,1)}, u32[]{:S(2)}, u32[]{:S(2)}) collective-permute-start(bf16[128,2048]{1,0:T(8,128)(2,1)} %bitcast.4.q_outgrad.b0), channel_id=1, source_target_pairs={{0,1},{1,0},{2,3},{3,2},{4,8},{5,9},{6,10},{7,11},{8,4},{9,5},{10,... | collective-permute-start | bytes 1572872 | tf_op jit(solution)/shard_map/ppermute | solution.py:562
  33.4 23.1 %collective-permute-start.8 = (bf16[128,3584]{1,0:T(8,128)(2,1)}, bf16[128,3584]{1,0:T(8,128)(2,1)}, u32[]{:S(2)}, u32[]{:S(2)}) collective-permute-start(bf16[128,3584]{1,0:T(8,128)(2,1)} %bitcast.16), channel_id=1, source_target_pairs={{0,2},{1,3},{2,0},{3,1},{4,6},{5,7},{6,4},{7,5},{8,10},{9,11},{10,... | collective-permute-start | bytes 2752520 | tf_op jit(solution)/shard_map/ppermute | solution.py:584
  35.0 10.7 %copy-start.27 = (bf16[2,64,2048]{2,1,0:T(8,128)(2,1)S(1)}, bf16[2,64,2048]{2,1,0:T(8,128)(2,1)}, u32[]{:S(2)}) copy-start(bf16[2,64,2048]{2,1,0:T(8,128)(2,1)} %get-tuple-element.71) | copy-start | bytes 1572868
  45.7 28.8 %copy-start.2 = (bf16[4,64,3584]{2,1,0:T(8,128)(2,1)S(1)}, bf16[4,64,3584]{2,1,0:T(8,128)(2,1)}, u32[]{:S(2)}) copy-start(bf16[4,64,3584]{2,1,0:T(8,128)(2,1)} %param.18) | copy-start | bytes 5505028
  45.7 27.0 %collective-permute-start.3 = (bf16[128,2048]{1,0:T(8,128)(2,1)S(1)}, bf16[128,2048]{1,0:T(8,128)(2,1)S(1)}, u32[]{:S(2)}, u32[]{:S(2)}) collective-permute-start(bf16[128,2048]{1,0:T(8,128)(2,1)S(1)} %bitcast.42), channel_id=1, source_target_pairs={{0,8},{4,12},{8,0},{12,4},{1,9},{5,13},{9,1},{13,5},{2,10},{6,14},... | collective-permute-start | bytes 1572872 | tf_op jit(solution)/shard_map/ppermute | solution.py:559
  50.6 22.6 %collective-permute-start.11 = (bf16[128,2048]{1,0:T(8,128)(2,1)S(1)}, bf16[128,2048]{1,0:T(8,128)(2,1)S(1)}, u32[]{:S(2)}, u32[]{:S(2)}) collective-permute-start(bf16[128,2048]{1,0:T(8,128)(2,1)S(1)} %bitcast.43), channel_id=1, source_target_pairs={{0,4},{4,0},{8,12},{12,8},{1,5},{5,1},{9,13},{13,9},{2,6},{6,2},{1... | collective-permute-start | bytes 1572872 | tf_op jit(solution)/shard_map/ppermute | solution.py:559
  56.5 24.9 %collective-permute-start.9 = (bf16[2,128,2048]{2,1,0:T(8,128)(2,1)S(1)}, bf16[2,128,2048]{2,1,0:T(8,128)(2,1)S(1)}, u32[]{:S(2)}, u32[]{:S(2)}) collective-permute-start(bf16[2,128,2048]{2,1,0:T(8,128)(2,1)S(1)} %pad_maximum_fusion), channel_id=1, source_target_pairs={{0,2},{1,3},{2,0},{3,1},{4,6},{5,7},{6,4},{7,5},{8,10},{9,11},{10,... | collective-permute-start | bytes 3145736 | tf_op jit(solution)/shard_map/ppermute | solution.py:586
  72.7 16.4 %copy-start.26 = (bf16[128,2048]{1,0:T(8,128)(2,1)}, bf16[128,2048]{1,0:T(8,128)(2,1)S(1)}, u32[]{:S(2)}) copy-start(bf16[128,2048]{1,0:T(8,128)(2,1)S(1)} %collective-permute-done.3.b3.b4) | copy-start | bytes 1572868
  73.1 16.1 %copy-start.30 = (bf16[128,2048]{1,0:T(8,128)(2,1)}, bf16[128,2048]{1,0:T(8,128)(2,1)S(1)}, u32[]{:S(2)}) copy-start(bf16[128,2048]{1,0:T(8,128)(2,1)S(1)} %collective-permute-done.11.b1) | copy-start | bytes 1572868
  73.1 16.1 %collective-permute-start.12 = (bf16[128,2048]{1,0:T(8,128)(2,1)S(1)}, bf16[128,2048]{1,0:T(8,128)(2,1)S(1)}, u32[]{:S(2)}, u32[]{:S(2)}) collective-permute-start(bf16[128,2048]{1,0:T(8,128)(2,1)S(1)} %collective-permute-done.3.b3.b4), channel_id=1, source_target_pairs={{0,4},{4,0},{8,12},{12,8},{1,5},{5,1},{9,13},{13,9},{2,6},{6,2},{1... | collective-permute-start | bytes 1572872 | tf_op jit(solution)/shard_map/ppermute | solution.py:563
  74.4 14.8 %collective-permute-start.10 = (bf16[128,2048]{1,0:T(8,128)(2,1)S(1)}, bf16[128,2048]{1,0:T(8,128)(2,1)S(1)}, u32[]{:S(2)}, u32[]{:S(2)}) collective-permute-start(bf16[128,2048]{1,0:T(8,128)(2,1)S(1)} %bitcast.44), channel_id=1, source_target_pairs={{0,1},{1,0},{2,3},{3,2},{4,8},{5,9},{6,10},{7,11},{8,4},{9,5},{10,... | collective-permute-start | bytes 1572872 | tf_op jit(solution)/shard_map/ppermute | solution.py:562
  79.1 10.3 %copy-start.14 = (bf16[3584,256]{1,0:T(8,128)(2,1)}, bf16[3584,256]{1,0:T(8,128)(2,1)S(1)}, u32[]{:S(2)}) copy-start(bf16[3584,256]{1,0:T(8,128)(2,1)S(1)} %get-tuple-element.49.gates) | copy-start | bytes 5505028
  79.1 10.3 %copy-start.15 = (bf16[3584,256]{1,0:T(8,128)(2,1)}, bf16[3584,256]{1,0:T(8,128)(2,1)S(1)}, u32[]{:S(2)}) copy-start(bf16[3584,256]{1,0:T(8,128)(2,1)S(1)} %get-tuple-element.64.ups) | copy-start | bytes 5505028
  79.1 30.2 %collective-permute-start.4 = (bf16[128,2048]{1,0:T(8,128)(2,1)}, bf16[128,2048]{1,0:T(8,128)(2,1)S(1)}, u32[]{:S(2)}, u32[]{:S(2)}) collective-permute-start(bf16[128,2048]{1,0:T(8,128)(2,1)} %bitcast.9.b0), channel_id=1, source_target_pairs={{0,8},{4,12},{8,0},{12,4},{1,9},{5,13},{9,1},{13,5},{2,10},{6,14},... | collective-permute-start | bytes 1572872 | tf_op jit(solution)/shard_map/ppermute | solution.py:559
  81.3 28.0 %collective-permute-start.14 = (bf16[128,2048]{1,0:T(8,128)(2,1)}, bf16[128,2048]{1,0:T(8,128)(2,1)S(1)}, u32[]{:S(2)}, u32[]{:S(2)}) collective-permute-start(bf16[128,2048]{1,0:T(8,128)(2,1)} %bitcast.9.b0), channel_id=1, source_target_pairs={{0,4},{4,0},{8,12},{12,8},{1,5},{5,1},{9,13},{13,9},{2,6},{6,2},{1... | collective-permute-start | bytes 1572872 | tf_op jit(solution)/shard_map/ppermute | solution.py:559
  81.3 9.9 %copy-start.35 = (bf16[2,128,2048]{2,1,0:T(8,128)(2,1)}, bf16[2,128,2048]{2,1,0:T(8,128)(2,1)S(1)}, u32[]{:S(2)}) copy-start(bf16[2,128,2048]{2,1,0:T(8,128)(2,1)S(1)} %collective-permute-done.9.far) | copy-start | bytes 3145732
  91.3 27.1 %collective-permute-start.18 = (bf16[2,128,2048]{2,1,0:T(8,128)(2,1)}, bf16[2,128,2048]{2,1,0:T(8,128)(2,1)}, u32[]{:S(2)}, u32[]{:S(2)}) collective-permute-start(bf16[2,128,2048]{2,1,0:T(8,128)(2,1)} %pad_maximum_fusion.1), channel_id=1, source_target_pairs={{0,2},{1,3},{2,0},{3,1},{4,6},{5,7},{6,4},{7,5},{8,10},{9,11},{10,... | collective-permute-start | bytes 3145736 | tf_op jit(solution)/shard_map/ppermute | solution.py:592
  109.3 16.4 %copy-start.25 = (bf16[128,2048]{1,0:T(8,128)(2,1)}, bf16[128,2048]{1,0:T(8,128)(2,1)S(1)}, u32[]{:S(2)}) copy-start(bf16[128,2048]{1,0:T(8,128)(2,1)S(1)} %collective-permute-done.4.b3.b4) | copy-start | bytes 1572868
  109.3 16.4 %copy-start.29 = (bf16[128,2048]{1,0:T(8,128)(2,1)}, bf16[128,2048]{1,0:T(8,128)(2,1)S(1)}, u32[]{:S(2)}) copy-start(bf16[128,2048]{1,0:T(8,128)(2,1)S(1)} %collective-permute-done.14.b1) | copy-start | bytes 1572868
  109.3 16.2 %collective-permute-start.15 = (bf16[128,2048]{1,0:T(8,128)(2,1)S(1)}, bf16[128,2048]{1,0:T(8,128)(2,1)S(1)}, u32[]{:S(2)}, u32[]{:S(2)}) collective-permute-start(bf16[128,2048]{1,0:T(8,128)(2,1)S(1)} %collective-permute-done.4.b3.b4), channel_id=1, source_target_pairs={{0,4},{4,0},{8,12},{12,8},{1,5},{5,1},{9,13},{13,9},{2,6},{6,2},{1... | collective-permute-start | bytes 1572872 | tf_op jit(solution)/shard_map/ppermute | solution.py:563
  118.3 7.2 %collective-permute-start.13 = (bf16[128,2048]{1,0:T(8,128)(2,1)}, bf16[128,2048]{1,0:T(8,128)(2,1)S(1)}, u32[]{:S(2)}, u32[]{:S(2)}) collective-permute-start(bf16[128,2048]{1,0:T(8,128)(2,1)} %bitcast.9.b0), channel_id=1, source_target_pairs={{0,1},{1,0},{2,3},{3,2},{4,8},{5,9},{6,10},{7,11},{8,4},{9,5},{10,... | collective-permute-start | bytes 1572872 | tf_op jit(solution)/shard_map/ppermute | solution.py:562
  118.3 28.6 %collective-permute-start.19 = (bf16[3584,128]{1,0:T(8,128)(2,1)}, bf16[3584,128]{1,0:T(8,128)(2,1)}, u32[]{:S(2)}, u32[]{:S(2)}) collective-permute-start(bf16[3584,128]{1,0:T(8,128)(2,1)} %get-tuple-element.58), channel_id=1, source_target_pairs={{0,2},{1,3},{2,0},{3,1},{4,6},{5,7},{6,4},{7,5},{8,10},{9,11},{10,... | collective-permute-start | bytes 2752520 | tf_op jit(solution)/shard_map/ppermute | solution.py:596
  127.6 19.4 %copy-start.5 = (bf16[64,3584]{1,0:T(8,128)(2,1)S(1)}, bf16[64,3584]{1,0:T(8,128)(2,1)}, u32[]{:S(2)}) copy-start(bf16[64,3584]{1,0:T(8,128)(2,1)} %proj_gate.5) | copy-start | bytes 1376260
  127.6 19.4 %copy-start.7 = (bf16[64,3584]{1,0:T(8,128)(2,1)S(1)}, bf16[64,3584]{1,0:T(8,128)(2,1)}, u32[]{:S(2)}) copy-start(bf16[64,3584]{1,0:T(8,128)(2,1)} %proj_up.5) | copy-start | bytes 1376260
  127.6 19.4 %copy-start.10 = (bf16[2,64,3584]{2,1,0:T(8,128)(2,1)S(1)}, bf16[2,64,3584]{2,1,0:T(8,128)(2,1)}, u32[]{:S(2)}) copy-start(bf16[2,64,3584]{2,1,0:T(8,128)(2,1)} %param.22) | copy-start | bytes 2752516
  127.6 19.4 %copy-start.12 = (bf16[2,64,3584]{2,1,0:T(8,128)(2,1)S(1)}, bf16[2,64,3584]{2,1,0:T(8,128)(2,1)}, u32[]{:S(2)}) copy-start(bf16[2,64,3584]{2,1,0:T(8,128)(2,1)} %param.23) | copy-start | bytes 2752516
  127.6 36.6 %collective-permute-start.21 = (bf16[2,128,2048]{2,1,0:T(8,128)(2,1)}, bf16[2,128,2048]{2,1,0:T(8,128)(2,1)S(1)}, u32[]{:S(2)}, u32[]{:S(2)}) collective-permute-start(bf16[2,128,2048]{2,1,0:T(8,128)(2,1)} %pad_maximum_fusion.2), channel_id=1, source_target_pairs={{0,2},{1,3},{2,0},{3,1},{4,6},{5,7},{6,4},{7,5},{8,10},{9,11},{10,... | collective-permute-start | bytes 3145736 | tf_op jit(solution)/shard_map/ppermute | solution.py:599
  144.6 43.1 %collective-permute-start.22 = (bf16[3584,128]{1,0:T(8,128)(2,1)}, bf16[3584,128]{1,0:T(8,128)(2,1)}, u32[]{:S(2)}, u32[]{:S(2)}) collective-permute-start(bf16[3584,128]{1,0:T(8,128)(2,1)} %get-tuple-element.60), channel_id=1, source_target_pairs={{0,2},{1,3},{2,0},{3,1},{4,6},{5,7},{6,4},{7,5},{8,10},{9,11},{10,... | collective-permute-start | bytes 2752520 | tf_op jit(solution)/shard_map/ppermute | solution.py:604
  144.9 8.8 %collective-permute-start.16 = (f32[384,128]{1,0:T(8,128)S(1)}, f32[384,128]{1,0:T(8,128)S(1)}, u32[]{:S(2)}, u32[]{:S(2)}) collective-permute-start(f32[384,128]{1,0:T(8,128)S(1)} %get-tuple-element.56), channel_id=1, source_target_pairs={{0,4},{4,0},{8,12},{12,8},{1,5},{5,1},{9,13},{13,9},{2,6},{6,2},{1... | collective-permute-start | bytes 589832 | tf_op jit(solution)/shard_map/ppermute | solution.py:603
  150.9 5.0 %collective-permute-start.20 = (f32[128,192]{1,0:T(8,128)S(1)}, f32[128,192]{1,0:T(8,128)S(1)}, u32[]{:S(2)}, u32[]{:S(2)}) collective-permute-start(f32[128,192]{1,0:T(8,128)S(1)} %pad_maximum_fusion.3), channel_id=1, source_target_pairs={{0,4},{4,0},{8,12},{12,8},{1,5},{5,1},{9,13},{13,9},{2,6},{6,2},{1... | collective-permute-start | bytes 294920 | tf_op jit(solution)/shard_map/ppermute | solution.py:609
  153.7 29.8 %collective-permute-start.17 = (f32[384,128]{1,0:T(8,128)S(1)}, f32[384,128]{1,0:T(8,128)S(1)}, u32[]{:S(2)}, u32[]{:S(2)}) collective-permute-start(f32[384,128]{1,0:T(8,128)S(1)} %add.32), channel_id=1, source_target_pairs={{0,8},{4,12},{8,0},{12,4},{1,9},{5,13},{9,1},{13,5},{2,10},{6,14},... | collective-permute-start | bytes 589832 | tf_op jit(solution)/shard_map/ppermute | solution.py:614
  156.0 27.6 %collective-permute-start.24 = (f32[128,192]{1,0:T(8,128)S(1)}, f32[128,192]{1,0:T(8,128)S(1)}, u32[]{:S(2)}, u32[]{:S(2)}) collective-permute-start(f32[128,192]{1,0:T(8,128)S(1)} %fusion), channel_id=1, source_target_pairs={{0,8},{4,12},{8,0},{12,4},{1,9},{5,13},{9,1},{13,5},{2,10},{6,14},... | collective-permute-start | bytes 294920 | tf_op jit(solution)/shard_map/ppermute | solution.py:615
  165.3 18.3 %copy-start.23 = (s32[2]{0:T(128)S(1)}, s32[2]{0:T(128)}, u32[]{:S(2)}) copy-start(s32[2]{0:T(128)} %lengths.2) | copy-start | bytes 28
  165.3 32.3 %copy-start.6 = (bf16[64,3584]{1,0:T(8,128)(2,1)S(1)}, bf16[64,3584]{1,0:T(8,128)(2,1)}, u32[]{:S(2)}) copy-start(bf16[64,3584]{1,0:T(8,128)(2,1)} %proj_gate.5) | copy-start | bytes 1376260
  165.3 32.3 %copy-start.8 = (bf16[64,3584]{1,0:T(8,128)(2,1)S(1)}, bf16[64,3584]{1,0:T(8,128)(2,1)}, u32[]{:S(2)}) copy-start(bf16[64,3584]{1,0:T(8,128)(2,1)} %proj_up.5) | copy-start | bytes 1376260
  183.5 14.0 %copy-start.3 = (bf16[4,64,3584]{2,1,0:T(8,128)(2,1)S(1)}, bf16[4,64,3584]{2,1,0:T(8,128)(2,1)}, u32[]{:S(2)}) copy-start(bf16[4,64,3584]{2,1,0:T(8,128)(2,1)} %param.18) | copy-start | bytes 5505028
  184.5 17.0 %collective-permute-start.25 = (f32[2,192,64]{2,1,0:T(8,128)S(1)}, f32[2,192,64]{2,1,0:T(8,128)S(1)}, u32[]{:S(2)}, u32[]{:S(2)}) collective-permute-start(f32[2,192,64]{2,1,0:T(8,128)S(1)} %shard_map.161.q0), channel_id=1, source_target_pairs={{0,1},{1,0},{2,3},{3,2},{4,5},{5,4},{6,7},{7,6},{8,9},{9,8},{10,11... | collective-permute-start | bytes 294920 | tf_op jit(solution)/shard_map/ppermute | solution.py:617
  184.6 16.9 %collective-permute-start.26 = (f32[2,192,64]{2,1,0:T(8,128)S(1)}, f32[2,192,64]{2,1,0:T(8,128)S(1)}, u32[]{:S(2)}, u32[]{:S(2)}) collective-permute-start(f32[2,192,64]{2,1,0:T(8,128)S(1)} %shard_map.161.q0), channel_id=1, source_target_pairs={{0,2},{1,3},{2,0},{3,1},{4,6},{5,7},{6,4},{7,5},{8,10},{9,11},{10,... | collective-permute-start | bytes 294920 | tf_op jit(solution)/shard_map/ppermute | solution.py:617
  185.9 15.6 %collective-permute-start.27 = (f32[2,192,64]{2,1,0:T(8,128)S(1)}, f32[2,192,64]{2,1,0:T(8,128)S(1)}, u32[]{:S(2)}, u32[]{:S(2)}) collective-permute-start(f32[2,192,64]{2,1,0:T(8,128)S(1)} %shard_map.161.q0), channel_id=1, source_target_pairs={{0,3},{1,2},{2,1},{3,0},{4,7},{5,6},{6,5},{7,4},{8,11},{9,10},{10,... | collective-permute-start | bytes 294920 | tf_op jit(solution)/shard_map/ppermute | solution.py:617
  186.5 11.1 %collective-permute-start.23 = (f32[128,128]{1,0:T(8,128)}, f32[128,128]{1,0:T(8,128)S(1)}, u32[]{:S(2)}, u32[]{:S(2)}) collective-permute-start(f32[128,128]{1,0:T(8,128)} %get-tuple-element.68), channel_id=1, source_target_pairs={{0,2},{1,3},{2,0},{3,1},{4,6},{5,7},{6,4},{7,5},{8,10},{9,11},{10,... | collective-permute-start | bytes 196616 | tf_op jit(solution)/shard_map/ppermute | solution.py:618
  202.9 7.6 %collective-permute-start.28 = (f32[4,8]{1,0:T(4,128)S(1)}, f32[4,8]{1,0:T(4,128)S(1)}, u32[]{:S(2)}, u32[]{:S(2)}) collective-permute-start(f32[4,8]{1,0:T(4,128)S(1)} %shard_map.162), channel_id=1, source_target_pairs={{0,4},{4,0},{8,12},{12,8},{1,5},{5,1},{9,13},{13,9},{2,6},{6,2},{1... | collective-permute-start | bytes 392 | tf_op jit(solution)/shard_map/ppermute | solution.py:626
  207.7 4.5 %collective-permute-start.29 = (f32[4,8]{1,0:T(4,128)S(1)}, f32[4,8]{1,0:T(4,128)S(1)}, u32[]{:S(2)}, u32[]{:S(2)}) collective-permute-start(f32[4,8]{1,0:T(4,128)S(1)} %shard_map.162), channel_id=1, source_target_pairs={{0,8},{4,12},{8,0},{12,4},{1,9},{5,13},{9,1},{13,5},{2,10},{6,14},... | collective-permute-start | bytes 392 | tf_op jit(solution)/shard_map/ppermute | solution.py:626
  209.1 5.4 %collective-permute-start.30 = (f32[4,8]{1,0:T(4,128)S(1)}, f32[4,8]{1,0:T(4,128)S(1)}, u32[]{:S(2)}, u32[]{:S(2)}) collective-permute-start(f32[4,8]{1,0:T(4,128)S(1)} %shard_map.162), channel_id=1, source_target_pairs={{0,12},{4,8},{8,4},{12,0},{1,13},{5,9},{9,5},{13,1},{2,14},{6,10},... | collective-permute-start | bytes 392 | tf_op jit(solution)/shard_map/ppermute | solution.py:626
  (20 other events, 35.4 us)

commit v12 on v8

--- a/solution.py
+++ b/solution.py
@@ -10,6 +10,7 @@
 RANK = 64
 SEQ = 64
 TILE = 512
+WIDE = 1792
 VMEM_BYTES = 40 * 1024 * 1024
 BIG_VMEM_BYTES = 58 * 1024 * 1024
 
@@ -136,12 +137,12 @@
     return pl.CostEstimate(flops=1024, bytes_accessed=1024, transcendentals=0)
 
 
-def tile_columns(number, block=0):
-    return pl.BlockSpec((number, TILE), lambda i: (block, i))
-
-
-def tile_rows(width):
-    return pl.BlockSpec((TILE, width), lambda i: (i, 0))
+def tile_columns(number, block=0, tile=TILE):
+    return pl.BlockSpec((number, tile), lambda i: (block, i))
+
+
+def tile_rows(width, tile=TILE):
+    return pl.BlockSpec((tile, width), lambda i: (i, 0))
 
 
 def whole(shape):
@@ -268,8 +269,10 @@
     units, number = near_sum.shape
     return pl.pallas_call(
         finish_kernel,
-        grid=(units // TILE,),
-        in_specs=[tile_rows(number)] * 2 + [tile_columns(number)] * 2 + [tile_columns(RANK)] * 2,
+        grid=(units // WIDE,),
+        in_specs=[tile_rows(number, WIDE)] * 2
+        + [tile_columns(number, 0, WIDE)] * 2
+        + [tile_columns(RANK, 0, WIDE)] * 2,
         out_specs=whole((number, 2 * RANK)),
         out_shape=jax.ShapeDtypeStruct((number, 2 * RANK), jnp.float32),
         compiler_params=params(),
@@ -545,9 +548,6 @@
     def tensor_sum(values):
         return values + outer(values) + across(values) + opposite(values)
 
-    def first_hops(own):
-        return own, outer(own), across(own)
-
     def last_hops(own, one, two):
         mid = middle(after(own, two))
         return own, one, mid, two, two, outer(after(two, one))
@@ -583,6 +583,9 @@
             [choose(own, second_inner, second_outer), choose(one, third_inner, third_outer)]
         )
 
+    def first_hops(own):
+        return own, outer(own), across(own)
+
     weight_own, weight_sib = down_weight, to_core(down_weight)
     q_own, q_one, q_two = first_hops(q_outgrad)
     far_gate = to_chip(t_gate[cut:])
@@ -590,49 +593,58 @@
         t_input, q_input, t_outgrad, q_outgrad, proj_input, proj_outgrad, t_gate, t_up, q_gate,
         q_up, proj_hidden,
     )
-    q_blocks = last_hops(q_own, q_one, after(q_two, own_in_out, far_gate))
-    far_up = to_chip(after(t_up[cut:], far_gate))
+    q_blocks = last_hops(q_own, q_one, after(q_two, own_in_out))
     q_first = to_chip(crossing_first(q_own, q_blocks[3]))
+    a_own, a_one, a_two = first_hops(after(t_outgrad[:cut], q_two, far_gate))
+    far_up = to_chip(after(t_up[cut:], far_gate, weight_sib))
     q_send = after(crossing_second(q_one, q_blocks[2], q_blocks[5]), far_up)
     q_far = (q_first, to_chip(q_send))
 
-    a_own, a_one, a_two = first_hops(after(t_outgrad[:cut], q_send))
-    a_two = after(a_two, a_one)
-    a_cross = crossing_first(a_own, a_two)
-    a_first = to_chip(a_cross)
+    b_own, b_one, b_two = first_hops(after(t_outgrad[cut:], a_two))
+    a_two = after(a_two, q_send)
+    a_first = to_chip(crossing_first(a_own, a_two))
     a_blocks = last_hops(a_own, a_one, a_two)
+    gates, ups = turned(t_gate, t_up, far_gate, far_up)
+    a_send = crossing_second(a_one, a_blocks[2], after(a_blocks[5], *q_far, gates))
+    a_far = (a_first, to_chip(a_send))
     q_near_sum, q_far_sum = partial_sums(
-        after(flags, a_cross), q_blocks, q_far, weight_own, weight_sib
-    )
-    a_send = crossing_second(a_one, a_blocks[2], after(a_blocks[5], q_far_sum))
-    a_far = (a_first, to_chip(a_send))
+        after(flags, a_send), q_blocks, q_far, weight_own, weight_sib
+    )
     q_returned = to_chip(after(q_far_sum, *a_far))
 
-    b_own, b_one, b_two = first_hops(after(t_outgrad[cut:], a_send))
-    a_near_sum, a_far_sum = partial_sums(flags, a_blocks, a_far, weight_own, weight_sib)
-    b_two = after(b_two, b_one, a_far_sum)
-    b_first = to_chip(crossing_first(b_own, b_two))
+    b_two = after(b_two, q_far_sum)
+    b_cross = crossing_first(b_own, b_two)
+    b_first = to_chip(b_cross)
     b_blocks = last_hops(b_own, b_one, b_two)
-    q_gradient = finished_sides(q_near_sum, q_returned, q_gate, q_up, proj_gate, proj_up)
-    gates, ups = turned(t_gate, t_up, after(far_gate, a_far_sum), far_up)
-    b_send = crossing_second(
-        after(b_one, q_gradient, b_first, gates), b_blocks[2], b_blocks[5]
-    )
+    a_near_sum, a_far_sum = partial_sums(
+        after(flags, b_cross), a_blocks, a_far, weight_own, weight_sib
+    )
+    b_send = crossing_second(b_one, b_blocks[2], after(b_blocks[5], a_far_sum))
     b_far = (b_first, to_chip(b_send))
-    q_sums = jnp.concatenate([q_gradient, hidden[2 * cut :], own_in_out[2 * cut :]], axis=1)
-    q_sums = tensor_sum(after(q_sums, b_send))
-    a_returned = to_chip(after(a_far_sum, q_sums, *b_far))
-    in_out = tensor_sum(after(own_in_out[: 2 * cut], b_send))
-    own_found = query_features(query_lengths, q_sums)
+    a_returned = to_chip(after(a_far_sum, *b_far))
+    in_out = own_in_out + outer(after(own_in_out, b_send))
+    q_gradient = finished_sides(
+        q_near_sum, after(q_returned, b_send), q_gate, q_up, proj_gate, proj_up
+    )
+    pair = jnp.concatenate([q_gradient, hidden[2 * cut :]], axis=1)
+    pair = pair + outer(pair)
+    b_near, b_away = lent_sides(
+        after(flags, pair, in_out), b_blocks, b_far, weight_own, weight_sib, gates, ups,
+        proj_gate, proj_up,
+    )
+    b_far_sides = to_chip(b_away)
+    in_out = in_out + after(across(in_out), b_near)
+    pair = pair + after(across(pair), b_near)
+    own_found = query_features(
+        query_lengths, jnp.concatenate([pair, in_out[2 * cut :]], axis=1)
+    )
     found = (own_found, to_core(own_found), to_chip(own_found), to_other(own_found))
-    b_near, b_away = lent_sides(
-        flags, b_blocks, b_far, weight_own, weight_sib, gates, ups, proj_gate,
-        proj_up,
-    )
-    a_gradient = finished_sides(a_near_sum, a_returned, t_gate, t_up, proj_gate, proj_up)
+    a_gradient = finished_sides(
+        a_near_sum, after(a_returned, b_far_sides), t_gate, t_up, proj_gate, proj_up
+    )
     own_scores = partial_scores(
-        train_lengths, place, in_out, hidden[: 2 * cut], a_gradient, b_near,
-        to_chip(b_away), found,
+        train_lengths, place, in_out[: 2 * cut], hidden[: 2 * cut], a_gradient, b_near,
+        b_far_sides, found,
     )
     return tensor_sum(own_scores) / (RANK * SEQ)
 

time: 219 us -> 219 us (level)
  waiting for transfers between devices: 73.3 us -> 77.3 us
  Pallas kernels: 64 us -> 60.4 us
    ppermute x1, waiting for transfers between devices: 0.01 us -> 25.9 us  [moving_plan(): b_far = (b_first, to_chip(b_send))]
    ppermute x5 -> x9, waiting for transfers between devices: 10.5 us -> 26.2 us  [the longest x1 13.5 us: moving_plan(): far_up = to_chip(after(t_up[cut:], far_gate, weight_sib))]
    ppermute x9 -> x3, waiting for transfers between devices: 17.6 us -> 2.33 us  [tensor_sum(): return values + outer(values) + across(values) + opposite(values)]
    ppermute x6, waiting for transfers between devices: 24.5 us -> 13.3 us  [first_hops(): return (own, outer(own), across(own))]
    ppermute x9 -> x3, starting transfers between devices: 13.4 us -> 4.44 us  [tensor_sum(): return values + outer(values) + across(values) + opposite(values)]
    ppermute x1, waiting for transfers between devices: 6.79 us -> 0.01 us  [moving_plan(): a_far = (a_first, to_chip(a_send))]
    ppermute x5 -> x9, starting transfers between devices: 5.58 us -> 12.1 us  [the longest x1 3.24 us: moving_plan(): pair = pair + after(across(pair), b_near)]
    pallas_call x2, Pallas kernels: 8.32 us -> 4.8 us  [finished_sides(): pl.pallas_call(finish_kernel, grid=(units // WIDE,), in_specs=[tile_rows(...]
  transfers between devices with their start and end apart: 36 -> 34, of which waited for: 12 -> 13; matrix products, arithmetic and copies ran while one was open for 5% -> 6% of each run, Pallas kernels for 29% -> 27%
where the time goes in v12:
time: 219 us; the launch traced here: 218 us
  waiting for transfers between devices  77.3 us (35%)
  Pallas kernels  60.4 us (28%)
  starting transfers between devices  48.9 us (22%)
  local copies, waits for them, and re-layouts  21.8 us (10%)
  other arithmetic  8.97 us (4%)
    pallas_call x2, Pallas kernels, partial_sums(): pl.pallas_call(partial_kernel, grid=(units // TILE,), in_specs=[SCALARS]...  28.9 us
    ppermute x1, waiting for transfers between devices, moving_plan(): b_far = (b_first, to_chip(b_send))  25.9 us
    pallas_call x1, Pallas kernels, lent_sides(): pl.pallas_call(lent_kernel, grid=(units // TILE,), in_specs=[SCALARS] + [...  17.7 us
    unnamed x74, local copies, waits for them, and re-layouts  16.3 us
    ppermute x1, waiting for transfers between devices, moving_plan(): far_up = to_chip(after(t_up[cut:], far_gate, weight_sib))  13.5 us
    ppermute x6, waiting for transfers between devices, first_hops(): return (own, outer(own), across(own))  13.3 us
    ppermute x6, starting transfers between devices, first_hops(): return (own, outer(own), across(own))  12.9 us
    ppermute x1, waiting for transfers between devices, moving_plan(): b_far_sides = to_chip(b_away)  9.74 us
  transfers between devices with their start and end apart: 34, of which 13 were waited for; matrix products, arithmetic and copies ran while one was open for 6% of the time, Pallas kernels for 27%

profile of v12, /device:TPU:0, one launch (start us, length us, event | category | flops | bytes accessed | tf_op | source)
XLA Modules:
  0.0 217.9 jit_solution(626195194928211575)
XLA Ops:
  0.5 3.6 %collective-permute-start = (bf16[128,2048]{1,0:T(8,128)(2,1)}, bf16[128,2048]{1,0:T(8,128)(2,1)}, u32[]{:S(2)}, u32[]{:S(2)}) collective-permute-start(bf16[128,2048]{1,0:T(8,128)(2,1)} %bitcast.4.q_outgrad.b0), channel_id=1, source_target_pairs={{0,8},{4,12},{8,0},{12,4},{1,9},{5,13},{9,1},{13,5},{2,10},{6,14},... | collective-permute-start | bytes 1572872 | tf_op jit(solution)/shard_map/ppermute | solution.py:587
  4.1 1.6 collective-permute-start.5
  5.7 2.2 %slice.40 = bf16[2,64,3584]{2,1,0:T(8,128)(2,1)} slice(bf16[4,64,3584]{2,1,0:T(8,128)(2,1)} %param.17), slice={[2:4], [0:64], [0:3584]} | slice | bytes 1835008 | tf_op jit(solution)/shard_map/slice | solution.py:591
  7.9 1.5 collective-permute-start.1
  9.4 1.5 copy-done.1
  14.5 1.2 copy-done.16
  19.7 4.9 %shard_map.154 = (f32[384,128]{1,0:T(8,128)S(1)}, f32[384,64]{1,0:T(8,128)S(1)}) custom-call(bf16[256,2048]{1,0:T(8,128)(2,1)S(1)} %bitcast.28, bf16[128,2048]{1,0:T(8,128)(2,1)S(1)} %bitcast.29, bf16[256,2048]{1,0:T(8,128)(2,1)S(1)} %bitcast.23, bf16[128,2048]{1,0:T(8,128)(2,1)} %bitcast.4.q_outgrad.b0, bf16[64,2048]{1,0:T(8,128)(2,1)S(1)} %copy-done.19, ...), custom_call_target="tpu_custom_call" | custom-call | flops 1024 | bytes 1024 | tf_op jit(solution)/shard_map/pallas_call | solution.py:395
  24.5 3.8 %collective-permute-done.b3.b4 = bf16[128,2048]{1,0:T(8,128)(2,1)} collective-permute-done((bf16[128,2048]{1,0:T(8,128)(2,1)}, bf16[128,2048]{1,0:T(8,128)(2,1)}, u32[]{:S(2)}, u32[]{:S(2)}) %collective-permute-start) | collective-permute-done | bytes 524320 | tf_op jit(solution)/shard_map/ppermute | solution.py:587
  28.4 1.5 collective-permute-start.6
  31.0 2.2 slice.42
  33.2 2.4 %collective-permute-start.2 = (bf16[128,2048]{1,0:T(8,128)(2,1)}, bf16[128,2048]{1,0:T(8,128)(2,1)S(1)}, u32[]{:S(2)}, u32[]{:S(2)}) collective-permute-start(bf16[128,2048]{1,0:T(8,128)(2,1)} %bitcast.30), channel_id=1, source_target_pairs={{0,8},{4,12},{8,0},{12,4},{1,9},{5,13},{9,1},{13,5},{2,10},{6,14},... | collective-permute-start | bytes 1572872 | tf_op jit(solution)/shard_map/ppermute | solution.py:587
  36.2 1.5 collective-permute-start.8
  37.7 1.3 broadcast_select_fusion.2
  39.0 4.5 %collective-permute-done.6.b5 = bf16[128,2048]{1,0:T(8,128)(2,1)} collective-permute-done((bf16[128,2048]{1,0:T(8,128)(2,1)}, bf16[128,2048]{1,0:T(8,128)(2,1)}, u32[]{:S(2)}, u32[]{:S(2)}) %collective-permute-start.6) | collective-permute-done | bytes 524320 | tf_op jit(solution)/shard_map/ppermute | solution.py:575
  43.5 1.6 collective-permute-start.12
  46.2 13.5 %collective-permute-done.8.far_up = bf16[128,3584]{1,0:T(8,128)(2,1)S(1)} collective-permute-done((bf16[128,3584]{1,0:T(8,128)(2,1)}, bf16[128,3584]{1,0:T(8,128)(2,1)S(1)}, u32[]{:S(2)}, u32[]{:S(2)}) %collective-permute-start.8) | collective-permute-done | bytes 917536 | tf_op jit(solution)/shard_map/ppermute | solution.py:599
  59.7 1.5 collective-permute-start.13
  61.2 5.6 %collective-permute-done.2.b3.b4 = bf16[128,2048]{1,0:T(8,128)(2,1)S(1)} collective-permute-done((bf16[128,2048]{1,0:T(8,128)(2,1)}, bf16[128,2048]{1,0:T(8,128)(2,1)S(1)}, u32[]{:S(2)}, u32[]{:S(2)}) %collective-permute-start.2) | collective-permute-done | bytes 524320 | tf_op jit(solution)/shard_map/ppermute | solution.py:587
  67.7 3.3 %collective-permute-start.3 = (bf16[128,2048]{1,0:T(8,128)(2,1)}, bf16[128,2048]{1,0:T(8,128)(2,1)}, u32[]{:S(2)}, u32[]{:S(2)}) collective-permute-start(bf16[128,2048]{1,0:T(8,128)(2,1)} %bitcast.9.b0), channel_id=1, source_target_pairs={{0,8},{4,12},{8,0},{12,4},{1,9},{5,13},{9,1},{13,5},{2,10},{6,14},... | collective-permute-start | bytes 1572872 | tf_op jit(solution)/shard_map/ppermute | solution.py:587
  71.0 1.4 collective-permute-start.15
  73.3 1.8 shard_map.155
  75.1 1.2 copy-done.13
  76.4 1.2 copy-done.14
  77.6 5.0 %collective-permute-done.11.b5 = bf16[128,2048]{1,0:T(8,128)(2,1)S(1)} collective-permute-done((bf16[128,2048]{1,0:T(8,128)(2,1)S(1)}, bf16[128,2048]{1,0:T(8,128)(2,1)S(1)}, u32[]{:S(2)}, u32[]{:S(2)}) %collective-permute-start.11) | collective-permute-done | bytes 524320 | tf_op jit(solution)/shard_map/ppermute | solution.py:575
  82.6 1.5 collective-permute-start.17
  85.6 14.4 %shard_map.156 = (f32[3584,128]{1,0:T(8,128)}, bf16[3584,128]{1,0:T(8,128)(2,1)}) custom-call(s32[3]{0:T(128)} %pad_add_fusion.flags, bf16[128,2048]{1,0:T(8,128)(2,1)} %bitcast.4.q_outgrad.b0, bf16[128,2048]{1,0:T(8,128)(2,1)} %copy-done.26, bf16[128,2048]{1,0:T(8,128)(2,1)} %collective-permute-done.4.b2, bf16[128,2048]{1,0:T(8,128)(2,1)} %collective-permute-done.b3.b4, ...), custom_call_target="tpu_custom_call" | custom-call | flops 1024 | bytes 1024 | tf_op jit(solution)/shard_map/pallas_call | solution.py:248
  99.9 3.8 %collective-permute-done.3.b3.b4 = bf16[128,2048]{1,0:T(8,128)(2,1)} collective-permute-done((bf16[128,2048]{1,0:T(8,128)(2,1)}, bf16[128,2048]{1,0:T(8,128)(2,1)}, u32[]{:S(2)}, u32[]{:S(2)}) %collective-permute-start.3) | collective-permute-done | bytes 524320 | tf_op jit(solution)/shard_map/ppermute | solution.py:587
  103.7 8.1 %collective-permute-start.16 = (bf16[128,2048]{1,0:T(8,128)(2,1)}, bf16[128,2048]{1,0:T(8,128)(2,1)}, u32[]{:S(2)}, u32[]{:S(2)}) collective-permute-start(bf16[128,2048]{1,0:T(8,128)(2,1)} %collective-permute-done.3.b3.b4), channel_id=1, source_target_pairs={{0,4},{4,0},{8,12},{12,8},{1,5},{5,1},{9,13},{13,9},{2,6},{6,2},{1... | collective-permute-start | bytes 1572872 | tf_op jit(solution)/shard_map/ppermute | solution.py:575
  111.8 1.9 broadcast_select_fusion.1
  115.1 1.5 collective-permute-start.21
  116.6 14.5 %shard_map.157 = (f32[3584,128]{1,0:T(8,128)}, bf16[3584,128]{1,0:T(8,128)(2,1)}) custom-call(s32[3]{0:T(128)} %pad_add_fusion.flags, bf16[128,2048]{1,0:T(8,128)(2,1)} %bitcast.32, bf16[128,2048]{1,0:T(8,128)(2,1)} %copy-done.28, bf16[128,2048]{1,0:T(8,128)(2,1)} %copy-done.30, bf16[128,2048]{1,0:T(8,128)(2,1)} %copy-done.24, bf16[128,2048]{1,0:T(8,128)(2,1)} %copy-done.24, ...), custom_call_target="tpu_custom_call" | custom-call | flops 1024 | bytes 1024 | tf_op jit(solution)/shard_map/pallas_call | solution.py:248
  131.2 1.3 select_select_fusion
  133.2 25.9 %collective-permute-done.24.far_b = bf16[128,2048]{1,0:T(8,128)(2,1)S(1)} collective-permute-done((bf16[128,2048]{1,0:T(8,128)(2,1)S(1)}, bf16[128,2048]{1,0:T(8,128)(2,1)S(1)}, u32[]{:S(2)}, u32[]{:S(2)}) %collective-permute-start.24) | collective-permute-done | bytes 524320 | tf_op jit(solution)/shard_map/ppermute | solution.py:623
  160.0 1.5 copy-done.15
  161.5 2.4 %shard_map.158 = f32[128,128]{1,0:T(8,128)S(1)} custom-call(f32[3584,128]{1,0:T(8,128)S(1)} %copy-done.15, bf16[3584,128]{1,0:T(8,128)(2,1)} %collective-permute-done.21.returned, bf16[128,3584]{1,0:T(8,128)(2,1)S(1)} %bitcast.25, bf16[128,3584]{1,0:T(8,128)(2,1)S(1)} %bitcast.27, bf16[64,3584]{1,0:T(8,128)(2,1)S(1)} %copy-done.4, bf16[64,3584]{1,0:T(8,128)(2,1)S(1)} %copy-done.6), custom_call_target="tpu_custom_call" | custom-call | flops 1024 | bytes 1024 | tf_op jit(solution)/shard_map/pallas_call | solution.py:270
  163.9 2.1 collective-permute-start.22
  166.6 1.5 collective-permute-start.20
  168.1 2.4 %collective-permute-done.22 = f32[128,192]{1,0:T(8,128)S(1)} collective-permute-done((f32[128,192]{1,0:T(8,128)S(1)}, f32[128,192]{1,0:T(8,128)S(1)}, u32[]{:S(2)}, u32[]{:S(2)}) %collective-permute-start.22) | collective-permute-done | bytes 98336 | tf_op jit(solution)/shard_map/ppermute | solution.py:630
  170.5 3.2 %collective-permute-start.27 = (f32[128,192]{1,0:T(8,128)S(1)}, f32[128,192]{1,0:T(8,128)S(1)}, u32[]{:S(2)}, u32[]{:S(2)}) collective-permute-start(f32[128,192]{1,0:T(8,128)S(1)} %fusion), channel_id=1, source_target_pairs={{0,8},{4,12},{8,0},{12,4},{1,9},{5,13},{9,1},{13,5},{2,10},{6,14},... | collective-permute-start | bytes 294920 | tf_op jit(solution)/shard_map/ppermute | solution.py:637
  173.7 17.7 %shard_map.159 = (f32[128,128]{1,0:T(8,128)}, f32[128,128]{1,0:T(8,128)}) custom-call(s32[3]{0:T(128)} %pad_add_fusion.flags, bf16[128,2048]{1,0:T(8,128)(2,1)} %bitcast.9.b0, bf16[128,2048]{1,0:T(8,128)(2,1)} %collective-permute-done.15.b1, bf16[128,2048]{1,0:T(8,128)(2,1)} %collective-permute-done.14.b2, bf16[128,2048]{1,0:T(8,128)(2,1)} %collective-permute-done.3.b3.b4, ...), custom_call_target="tpu_custom_call" | custom-call | flops 1024 | bytes 1024 | tf_op jit(solution)/shard_map/pallas_call | solution.py:341
  193.7 1.4 collective-permute-start.29
  195.6 1.3 collective-permute-start.26
  196.9 9.7 %collective-permute-done.26.far = f32[128,128]{1,0:T(8,128)S(1)} collective-permute-done((f32[128,128]{1,0:T(8,128)S(1)}, f32[128,128]{1,0:T(8,128)S(1)}, u32[]{:S(2)}, u32[]{:S(2)}) %collective-permute-start.26) | collective-permute-done | bytes 65568 | tf_op jit(solution)/shard_map/ppermute | solution.py:635
  206.7 2.4 %shard_map.160.early = f32[128,128]{1,0:T(8,128)S(1)} custom-call(f32[3584,128]{1,0:T(8,128)S(1)} %copy-done.12, bf16[3584,128]{1,0:T(8,128)(2,1)} %collective-permute-done.25.returned, bf16[256,3584]{1,0:T(8,128)(2,1)S(1)} %bitcast.19, bf16[256,3584]{1,0:T(8,128)(2,1)S(1)} %bitcast.22, bf16[64,3584]{1,0:T(8,128)(2,1)S(1)} %copy-done.5, ...), custom_call_target="tpu_custom_call" | custom-call | flops 1024 | bytes 1024 | tf_op jit(solution)/shard_map/pallas_call | solution.py:270
  209.2 1.4 shard_map.162
  210.6 1.3 collective-permute-start.32
  212.0 3.0 %collective-permute-start.33 = (f32[4,8]{1,0:T(4,128)S(1)}, f32[4,8]{1,0:T(4,128)S(1)}, u32[]{:S(2)}, u32[]{:S(2)}) collective-permute-start(f32[4,8]{1,0:T(4,128)S(1)} %shard_map.162), channel_id=1, source_target_pairs={{0,12},{4,8},{8,4},{12,0},{1,13},{5,9},{9,5},{13,1},{2,14},{6,10},... | collective-permute-start | bytes 392 | tf_op jit(solution)/shard_map/ppermute | solution.py:549
  215.2 2.2 collective-permute-done.33
  (124 shorter events, 21.3 us)
Async XLA Ops:
  0.0 9.4 %copy-start = (bf16[4,64,3584]{2,1,0:T(8,128)(2,1)S(1)}, bf16[4,64,3584]{2,1,0:T(8,128)(2,1)}, u32[]{:S(2)}) copy-start(bf16[4,64,3584]{2,1,0:T(8,128)(2,1)} %param.17) | copy-start | bytes 5505028
  0.0 36.2 %collective-permute-start.7 = (bf16[3584,2048]{1,0:T(8,128)(2,1)}, bf16[3584,2048]{1,0:T(8,128)(2,1)}, u32[]{:S(2)}, u32[]{:S(2)}) collective-permute-start(bf16[3584,2048]{1,0:T(8,128)(2,1)} %weight_own.5), channel_id=1, source_target_pairs={{0,1},{1,0},{2,3},{3,2},{4,5},{5,4},{6,7},{7,6},{8,9},{9,8},{10,11... | collective-permute-start | bytes 44040200 | tf_op jit(solution)/shard_map/ppermute | solution.py:589
  0.5 27.8 %collective-permute-start = (bf16[128,2048]{1,0:T(8,128)(2,1)}, bf16[128,2048]{1,0:T(8,128)(2,1)}, u32[]{:S(2)}, u32[]{:S(2)}) collective-permute-start(bf16[128,2048]{1,0:T(8,128)(2,1)} %bitcast.4.q_outgrad.b0), channel_id=1, source_target_pairs={{0,8},{4,12},{8,0},{12,4},{1,9},{5,13},{9,1},{13,5},{2,10},{6,14},... | collective-permute-start | bytes 1572872 | tf_op jit(solution)/shard_map/ppermute | solution.py:587
  4.1 24.3 %collective-permute-start.5 = (bf16[128,2048]{1,0:T(8,128)(2,1)}, bf16[128,2048]{1,0:T(8,128)(2,1)S(1)}, u32[]{:S(2)}, u32[]{:S(2)}) collective-permute-start(bf16[128,2048]{1,0:T(8,128)(2,1)} %bitcast.4.q_outgrad.b0), channel_id=1, source_target_pairs={{0,4},{4,0},{8,12},{12,8},{1,5},{5,1},{9,13},{13,9},{2,6},{6,2},{1... | collective-permute-start | bytes 1572872 | tf_op jit(solution)/shard_map/ppermute | solution.py:587
  7.9 25.3 %collective-permute-start.1 = (bf16[128,3584]{1,0:T(8,128)(2,1)}, bf16[128,3584]{1,0:T(8,128)(2,1)S(1)}, u32[]{:S(2)}, u32[]{:S(2)}) collective-permute-start(bf16[128,3584]{1,0:T(8,128)(2,1)} %bitcast.11), channel_id=1, source_target_pairs={{0,2},{1,3},{2,0},{3,1},{4,6},{5,7},{6,4},{7,5},{8,10},{9,11},{10,... | collective-permute-start | bytes 2752520 | tf_op jit(solution)/shard_map/ppermute | solution.py:591
  28.4 15.1 %collective-permute-start.6 = (bf16[128,2048]{1,0:T(8,128)(2,1)}, bf16[128,2048]{1,0:T(8,128)(2,1)}, u32[]{:S(2)}, u32[]{:S(2)}) collective-permute-start(bf16[128,2048]{1,0:T(8,128)(2,1)} %collective-permute-done.b3.b4), channel_id=1, source_target_pairs={{0,4},{4,0},{8,12},{12,8},{1,5},{5,1},{9,13},{13,9},{2,6},{6,2},{1... | collective-permute-start | bytes 1572872 | tf_op jit(solution)/shard_map/ppermute | solution.py:575
  29.9 15.2 %collective-permute-start.4 = (bf16[128,2048]{1,0:T(8,128)(2,1)}, bf16[128,2048]{1,0:T(8,128)(2,1)}, u32[]{:S(2)}, u32[]{:S(2)}) collective-permute-start(bf16[128,2048]{1,0:T(8,128)(2,1)} %bitcast.4.q_outgrad.b0), channel_id=1, source_target_pairs={{0,1},{1,0},{2,3},{3,2},{4,8},{5,9},{6,10},{7,11},{8,4},{9,5},{10,... | collective-permute-start | bytes 1572872 | tf_op jit(solution)/shard_map/ppermute | solution.py:574
  33.2 11.9 %copy-start.27 = (bf16[128,2048]{1,0:T(8,128)(2,1)S(1)}, bf16[128,2048]{1,0:T(8,128)(2,1)}, u32[]{:S(2)}) copy-start(bf16[128,2048]{1,0:T(8,128)(2,1)} %copy-done.26) | copy-start | bytes 1572868
  33.2 33.7 %collective-permute-start.2 = (bf16[128,2048]{1,0:T(8,128)(2,1)}, bf16[128,2048]{1,0:T(8,128)(2,1)S(1)}, u32[]{:S(2)}, u32[]{:S(2)}) collective-permute-start(bf16[128,2048]{1,0:T(8,128)(2,1)} %bitcast.30), channel_id=1, source_target_pairs={{0,8},{4,12},{8,0},{12,4},{1,9},{5,13},{9,1},{13,5},{2,10},{6,14},... | collective-permute-start | bytes 1572872 | tf_op jit(solution)/shard_map/ppermute | solution.py:587
  35.6 31.3 %collective-permute-start.10 = (bf16[128,2048]{1,0:T(8,128)(2,1)}, bf16[128,2048]{1,0:T(8,128)(2,1)S(1)}, u32[]{:S(2)}, u32[]{:S(2)}) collective-permute-start(bf16[128,2048]{1,0:T(8,128)(2,1)} %bitcast.31), channel_id=1, source_target_pairs={{0,4},{4,0},{8,12},{12,8},{1,5},{5,1},{9,13},{13,9},{2,6},{6,2},{1... | collective-permute-start | bytes 1572872 | tf_op jit(solution)/shard_map/ppermute | solution.py:587
  36.2 30.7 %copy-start.25 = (bf16[2,64,2048]{2,1,0:T(8,128)(2,1)S(1)}, bf16[2,64,2048]{2,1,0:T(8,128)(2,1)}, u32[]{:S(2)}) copy-start(bf16[2,64,2048]{2,1,0:T(8,128)(2,1)} %get-tuple-element.75) | copy-start | bytes 1572868
  36.2 23.5 %collective-permute-start.8 = (bf16[128,3584]{1,0:T(8,128)(2,1)}, bf16[128,3584]{1,0:T(8,128)(2,1)S(1)}, u32[]{:S(2)}, u32[]{:S(2)}) collective-permute-start(bf16[128,3584]{1,0:T(8,128)(2,1)} %bitcast.35), channel_id=1, source_target_pairs={{0,2},{1,3},{2,0},{3,1},{4,6},{5,7},{6,4},{7,5},{8,10},{9,11},{10,... | collective-permute-start | bytes 2752520 | tf_op jit(solution)/shard_map/ppermute | solution.py:599
  39.0 34.3 %copy-start.2 = (bf16[4,64,3584]{2,1,0:T(8,128)(2,1)S(1)}, bf16[4,64,3584]{2,1,0:T(8,128)(2,1)}, u32[]{:S(2)}) copy-start(bf16[4,64,3584]{2,1,0:T(8,128)(2,1)} %param.18) | copy-start | bytes 5505028
  43.5 27.4 %collective-permute-start.12 = (bf16[128,2048]{1,0:T(8,128)(2,1)S(1)}, bf16[128,2048]{1,0:T(8,128)(2,1)S(1)}, u32[]{:S(2)}, u32[]{:S(2)}) collective-permute-start(bf16[128,2048]{1,0:T(8,128)(2,1)S(1)} %broadcast_select_fusion.2), channel_id=1, source_target_pairs={{0,2},{1,3},{2,0},{3,1},{4,6},{5,7},{6,4},{7,5},{8,10},{9,11},{10,... | collective-permute-start | bytes 1572872 | tf_op jit(solution)/shard_map/ppermute | solution.py:597
  59.7 24.3 %collective-permute-start.13 = (bf16[128,2048]{1,0:T(8,128)(2,1)S(1)}, bf16[128,2048]{1,0:T(8,128)(2,1)S(1)}, u32[]{:S(2)}, u32[]{:S(2)}) collective-permute-start(bf16[128,2048]{1,0:T(8,128)(2,1)S(1)} %select_select_fusion.2), channel_id=1, source_target_pairs={{0,2},{1,3},{2,0},{3,1},{4,6},{5,7},{6,4},{7,5},{8,10},{9,11},{10,... | collective-permute-start | bytes 1572872 | tf_op jit(solution)/shard_map/ppermute | solution.py:601
  66.9 8.2 %copy-start.24 = (bf16[128,2048]{1,0:T(8,128)(2,1)}, bf16[128,2048]{1,0:T(8,128)(2,1)S(1)}, u32[]{:S(2)}) copy-start(bf16[128,2048]{1,0:T(8,128)(2,1)S(1)} %collective-permute-done.2.b3.b4) | copy-start | bytes 1572868
  66.9 17.2 %copy-start.28 = (bf16[128,2048]{1,0:T(8,128)(2,1)}, bf16[128,2048]{1,0:T(8,128)(2,1)S(1)}, u32[]{:S(2)}) copy-start(bf16[128,2048]{1,0:T(8,128)(2,1)S(1)} %collective-permute-done.10.b1) | copy-start | bytes 1572868
  66.9 15.7 %collective-permute-start.11 = (bf16[128,2048]{1,0:T(8,128)(2,1)S(1)}, bf16[128,2048]{1,0:T(8,128)(2,1)S(1)}, u32[]{:S(2)}, u32[]{:S(2)}) collective-permute-start(bf16[128,2048]{1,0:T(8,128)(2,1)S(1)} %collective-permute-done.2.b3.b4), channel_id=1, source_target_pairs={{0,4},{4,0},{8,12},{12,8},{1,5},{5,1},{9,13},{13,9},{2,6},{6,2},{1... | collective-permute-start | bytes 1572872 | tf_op jit(solution)/shard_map/ppermute | solution.py:575
  66.9 17.1 %collective-permute-start.9 = (bf16[128,2048]{1,0:T(8,128)(2,1)S(1)}, bf16[128,2048]{1,0:T(8,128)(2,1)S(1)}, u32[]{:S(2)}, u32[]{:S(2)}) collective-permute-start(bf16[128,2048]{1,0:T(8,128)(2,1)S(1)} %bitcast.33), channel_id=1, source_target_pairs={{0,1},{1,0},{2,3},{3,2},{4,8},{5,9},{6,10},{7,11},{8,4},{9,5},{10,... | collective-permute-start | bytes 1572872 | tf_op jit(solution)/shard_map/ppermute | solution.py:574
  67.7 36.0 %collective-permute-start.3 = (bf16[128,2048]{1,0:T(8,128)(2,1)}, bf16[128,2048]{1,0:T(8,128)(2,1)}, u32[]{:S(2)}, u32[]{:S(2)}) collective-permute-start(bf16[128,2048]{1,0:T(8,128)(2,1)} %bitcast.9.b0), channel_id=1, source_target_pairs={{0,8},{4,12},{8,0},{12,4},{1,9},{5,13},{9,1},{13,5},{2,10},{6,14},... | collective-permute-start | bytes 1572872 | tf_op jit(solution)/shard_map/ppermute | solution.py:587
  71.0 32.8 %collective-permute-start.15 = (bf16[128,2048]{1,0:T(8,128)(2,1)}, bf16[128,2048]{1,0:T(8,128)(2,1)}, u32[]{:S(2)}, u32[]{:S(2)}) collective-permute-start(bf16[128,2048]{1,0:T(8,128)(2,1)} %bitcast.9.b0), channel_id=1, source_target_pairs={{0,4},{4,0},{8,12},{12,8},{1,5},{5,1},{9,13},{13,9},{2,6},{6,2},{1... | collective-permute-start | bytes 1572872 | tf_op jit(solution)/shard_map/ppermute | solution.py:587
  82.6 31.7 %collective-permute-start.17 = (bf16[128,2048]{1,0:T(8,128)(2,1)}, bf16[128,2048]{1,0:T(8,128)(2,1)S(1)}, u32[]{:S(2)}, u32[]{:S(2)}) collective-permute-start(bf16[128,2048]{1,0:T(8,128)(2,1)} %broadcast_select_fusion), channel_id=1, source_target_pairs={{0,2},{1,3},{2,0},{3,1},{4,6},{5,7},{6,4},{7,5},{8,10},{9,11},{10,... | collective-permute-start | bytes 1572872 | tf_op jit(solution)/shard_map/ppermute | solution.py:605
  85.0 29.2 %collective-permute-start.18 = (bf16[128,2048]{1,0:T(8,128)(2,1)S(1)}, bf16[128,2048]{1,0:T(8,128)(2,1)S(1)}, u32[]{:S(2)}, u32[]{:S(2)}) collective-permute-start(bf16[128,2048]{1,0:T(8,128)(2,1)S(1)} %select_select_fusion.1), channel_id=1, source_target_pairs={{0,2},{1,3},{2,0},{3,1},{4,6},{5,7},{6,4},{7,5},{8,10},{9,11},{10,... | collective-permute-start | bytes 1572872 | tf_op jit(solution)/shard_map/ppermute | solution.py:609
  103.7 27.4 %collective-permute-start.16 = (bf16[128,2048]{1,0:T(8,128)(2,1)}, bf16[128,2048]{1,0:T(8,128)(2,1)}, u32[]{:S(2)}, u32[]{:S(2)}) collective-permute-start(bf16[128,2048]{1,0:T(8,128)(2,1)} %collective-permute-done.3.b3.b4), channel_id=1, source_target_pairs={{0,4},{4,0},{8,12},{12,8},{1,5},{5,1},{9,13},{13,9},{2,6},{6,2},{1... | collective-permute-start | bytes 1572872 | tf_op jit(solution)/shard_map/ppermute | solution.py:575
  111.8 19.4 %collective-permute-start.14 = (bf16[128,2048]{1,0:T(8,128)(2,1)}, bf16[128,2048]{1,0:T(8,128)(2,1)}, u32[]{:S(2)}, u32[]{:S(2)}) collective-permute-start(bf16[128,2048]{1,0:T(8,128)(2,1)} %bitcast.9.b0), channel_id=1, source_target_pairs={{0,1},{1,0},{2,3},{3,2},{4,8},{5,9},{6,10},{7,11},{8,4},{9,5},{10,... | collective-permute-start | bytes 1572872 | tf_op jit(solution)/shard_map/ppermute | solution.py:574
  113.7 19.5 %collective-permute-start.23 = (bf16[128,2048]{1,0:T(8,128)(2,1)}, bf16[128,2048]{1,0:T(8,128)(2,1)}, u32[]{:S(2)}, u32[]{:S(2)}) collective-permute-start(bf16[128,2048]{1,0:T(8,128)(2,1)} %broadcast_select_fusion.1), channel_id=1, source_target_pairs={{0,2},{1,3},{2,0},{3,1},{4,6},{5,7},{6,4},{7,5},{8,10},{9,11},{10,... | collective-permute-start | bytes 1572872 | tf_op jit(solution)/shard_map/ppermute | solution.py:617
  115.1 44.9 %collective-permute-start.21 = (bf16[3584,128]{1,0:T(8,128)(2,1)}, bf16[3584,128]{1,0:T(8,128)(2,1)}, u32[]{:S(2)}, u32[]{:S(2)}) collective-permute-start(bf16[3584,128]{1,0:T(8,128)(2,1)} %get-tuple-element.63), channel_id=1, source_target_pairs={{0,2},{1,3},{2,0},{3,1},{4,6},{5,7},{6,4},{7,5},{8,10},{9,11},{10,... | collective-permute-start | bytes 2752520 | tf_op jit(solution)/shard_map/ppermute | solution.py:613
  116.6 43.4 %copy-start.11 = (bf16[2,64,3584]{2,1,0:T(8,128)(2,1)S(1)}, bf16[2,64,3584]{2,1,0:T(8,128)(2,1)}, u32[]{:S(2)}) copy-start(bf16[2,64,3584]{2,1,0:T(8,128)(2,1)} %param.23) | copy-start | bytes 2752516
  131.1 28.9 %copy-start.4 = (bf16[64,3584]{1,0:T(8,128)(2,1)S(1)}, bf16[64,3584]{1,0:T(8,128)(2,1)}, u32[]{:S(2)}) copy-start(bf16[64,3584]{1,0:T(8,128)(2,1)} %proj_gate.5) | copy-start | bytes 1376260
  131.1 28.9 %copy-start.6 = (bf16[64,3584]{1,0:T(8,128)(2,1)S(1)}, bf16[64,3584]{1,0:T(8,128)(2,1)}, u32[]{:S(2)}) copy-start(bf16[64,3584]{1,0:T(8,128)(2,1)} %proj_up.5) | copy-start | bytes 1376260
  131.2 28.8 %copy-start.9 = (bf16[2,64,3584]{2,1,0:T(8,128)(2,1)S(1)}, bf16[2,64,3584]{2,1,0:T(8,128)(2,1)}, u32[]{:S(2)}) copy-start(bf16[2,64,3584]{2,1,0:T(8,128)(2,1)} %param.22) | copy-start | bytes 2752516
  132.4 26.7 %collective-permute-start.24 = (bf16[128,2048]{1,0:T(8,128)(2,1)S(1)}, bf16[128,2048]{1,0:T(8,128)(2,1)S(1)}, u32[]{:S(2)}, u32[]{:S(2)}) collective-permute-start(bf16[128,2048]{1,0:T(8,128)(2,1)S(1)} %select_select_fusion), channel_id=1, source_target_pairs={{0,2},{1,3},{2,0},{3,1},{4,6},{5,7},{6,4},{7,5},{8,10},{9,11},{10,... | collective-permute-start | bytes 1572872 | tf_op jit(solution)/shard_map/ppermute | solution.py:623
  159.1 47.5 %collective-permute-start.25 = (bf16[3584,128]{1,0:T(8,128)(2,1)}, bf16[3584,128]{1,0:T(8,128)(2,1)}, u32[]{:S(2)}, u32[]{:S(2)}) collective-permute-start(bf16[3584,128]{1,0:T(8,128)(2,1)} %get-tuple-element.71), channel_id=1, source_target_pairs={{0,2},{1,3},{2,0},{3,1},{4,6},{5,7},{6,4},{7,5},{8,10},{9,11},{10,... | collective-permute-start | bytes 2752520 | tf_op jit(solution)/shard_map/ppermute | solution.py:624
  160.0 6.6 %collective-permute-start.19 = (f32[384,128]{1,0:T(8,128)S(1)}, f32[384,128]{1,0:T(8,128)S(1)}, u32[]{:S(2)}, u32[]{:S(2)}) collective-permute-start(f32[384,128]{1,0:T(8,128)S(1)} %get-tuple-element.61), channel_id=1, source_target_pairs={{0,4},{4,0},{8,12},{12,8},{1,5},{5,1},{9,13},{13,9},{2,6},{6,2},{1... | collective-permute-start | bytes 589832 | tf_op jit(solution)/shard_map/ppermute | solution.py:625
  163.9 6.5 %collective-permute-start.22 = (f32[128,192]{1,0:T(8,128)S(1)}, f32[128,192]{1,0:T(8,128)S(1)}, u32[]{:S(2)}, u32[]{:S(2)}) collective-permute-start(f32[128,192]{1,0:T(8,128)S(1)} %pad_maximum_fusion.1), channel_id=1, source_target_pairs={{0,4},{4,0},{8,12},{12,8},{1,5},{5,1},{9,13},{13,9},{2,6},{6,2},{1... | collective-permute-start | bytes 294920 | tf_op jit(solution)/shard_map/ppermute | solution.py:630
  166.6 24.9 %collective-permute-start.20 = (f32[384,128]{1,0:T(8,128)S(1)}, f32[384,128]{1,0:T(8,128)}, u32[]{:S(2)}, u32[]{:S(2)}) collective-permute-start(f32[384,128]{1,0:T(8,128)S(1)} %add.32), channel_id=1, source_target_pairs={{0,8},{4,12},{8,0},{12,4},{1,9},{5,13},{9,1},{13,5},{2,10},{6,14},... | collective-permute-start | bytes 589832 | tf_op jit(solution)/shard_map/ppermute | solution.py:636
  170.5 22.0 %collective-permute-start.27 = (f32[128,192]{1,0:T(8,128)S(1)}, f32[128,192]{1,0:T(8,128)S(1)}, u32[]{:S(2)}, u32[]{:S(2)}) collective-permute-start(f32[128,192]{1,0:T(8,128)S(1)} %fusion), channel_id=1, source_target_pairs={{0,8},{4,12},{8,0},{12,4},{1,9},{5,13},{9,1},{13,5},{2,10},{6,14},... | collective-permute-start | bytes 294920 | tf_op jit(solution)/shard_map/ppermute | solution.py:637
  173.7 18.9 %copy-start.22 = (s32[2]{0:T(128)S(1)}, s32[2]{0:T(128)}, u32[]{:S(2)}) copy-start(s32[2]{0:T(128)} %lengths.2) | copy-start | bytes 28
  173.7 32.9 %copy-start.12 = (f32[3584,128]{1,0:T(8,128)S(1)}, f32[3584,128]{1,0:T(8,128)}, u32[]{:S(2)}) copy-start(f32[3584,128]{1,0:T(8,128)} %get-tuple-element.70.near_sum) | copy-start | bytes 5505028
  191.4 15.2 %copy-start.5 = (bf16[64,3584]{1,0:T(8,128)(2,1)S(1)}, bf16[64,3584]{1,0:T(8,128)(2,1)}, u32[]{:S(2)}) copy-start(bf16[64,3584]{1,0:T(8,128)(2,1)} %proj_gate.5) | copy-start | bytes 1376260
  191.4 15.2 %copy-start.7 = (bf16[64,3584]{1,0:T(8,128)(2,1)S(1)}, bf16[64,3584]{1,0:T(8,128)(2,1)}, u32[]{:S(2)}) copy-start(bf16[64,3584]{1,0:T(8,128)(2,1)} %proj_up.5) | copy-start | bytes 1376260
  193.6 15.5 %collective-permute-start.28 = (f32[2,192,64]{2,1,0:T(8,128)S(1)}, f32[2,192,64]{2,1,0:T(8,128)S(1)}, u32[]{:S(2)}, u32[]{:S(2)}) collective-permute-start(f32[2,192,64]{2,1,0:T(8,128)S(1)} %shard_map.161.q0), channel_id=1, source_target_pairs={{0,1},{1,0},{2,3},{3,2},{4,5},{5,4},{6,7},{7,6},{8,9},{9,8},{10,11... | collective-permute-start | bytes 294920 | tf_op jit(solution)/shard_map/ppermute | solution.py:641
  193.7 15.4 %collective-permute-start.29 = (f32[2,192,64]{2,1,0:T(8,128)S(1)}, f32[2,192,64]{2,1,0:T(8,128)S(1)}, u32[]{:S(2)}, u32[]{:S(2)}) collective-permute-start(f32[2,192,64]{2,1,0:T(8,128)S(1)} %shard_map.161.q0), channel_id=1, source_target_pairs={{0,2},{1,3},{2,0},{3,1},{4,6},{5,7},{6,4},{7,5},{8,10},{9,11},{10,... | collective-permute-start | bytes 294920 | tf_op jit(solution)/shard_map/ppermute | solution.py:641
  195.1 14.1 %collective-permute-start.30 = (f32[2,192,64]{2,1,0:T(8,128)S(1)}, f32[2,192,64]{2,1,0:T(8,128)S(1)}, u32[]{:S(2)}, u32[]{:S(2)}) collective-permute-start(f32[2,192,64]{2,1,0:T(8,128)S(1)} %shard_map.161.q0), channel_id=1, source_target_pairs={{0,3},{1,2},{2,1},{3,0},{4,7},{5,6},{6,5},{7,4},{8,11},{9,10},{10,... | collective-permute-start | bytes 294920 | tf_op jit(solution)/shard_map/ppermute | solution.py:641
  195.6 11.1 %collective-permute-start.26 = (f32[128,128]{1,0:T(8,128)S(1)}, f32[128,128]{1,0:T(8,128)S(1)}, u32[]{:S(2)}, u32[]{:S(2)}) collective-permute-start(f32[128,128]{1,0:T(8,128)S(1)} %copy-done.36), channel_id=1, source_target_pairs={{0,2},{1,3},{2,0},{3,1},{4,6},{5,7},{6,4},{7,5},{8,10},{9,11},{10,... | collective-permute-start | bytes 196616 | tf_op jit(solution)/shard_map/ppermute | solution.py:635
  210.6 4.5 %collective-permute-start.31 = (f32[4,8]{1,0:T(4,128)S(1)}, f32[4,8]{1,0:T(4,128)S(1)}, u32[]{:S(2)}, u32[]{:S(2)}) collective-permute-start(f32[4,8]{1,0:T(4,128)S(1)} %shard_map.162), channel_id=1, source_target_pairs={{0,4},{4,0},{8,12},{12,8},{1,5},{5,1},{9,13},{13,9},{2,6},{6,2},{1... | collective-permute-start | bytes 392 | tf_op jit(solution)/shard_map/ppermute | solution.py:549
  210.6 4.5 %collective-permute-start.32 = (f32[4,8]{1,0:T(4,128)S(1)}, f32[4,8]{1,0:T(4,128)S(1)}, u32[]{:S(2)}, u32[]{:S(2)}) collective-permute-start(f32[4,8]{1,0:T(4,128)S(1)} %shard_map.162), channel_id=1, source_target_pairs={{0,8},{4,12},{8,0},{12,4},{1,9},{5,13},{9,1},{13,5},{2,10},{6,14},... | collective-permute-start | bytes 392 | tf_op jit(solution)/shard_map/ppermute | solution.py:549
  212.0 5.4 %collective-permute-start.33 = (f32[4,8]{1,0:T(4,128)S(1)}, f32[4,8]{1,0:T(4,128)S(1)}, u32[]{:S(2)}, u32[]{:S(2)}) collective-permute-start(f32[4,8]{1,0:T(4,128)S(1)} %shard_map.162), channel_id=1, source_target_pairs={{0,12},{4,8},{8,4},{12,0},{1,13},{5,9},{9,5},{13,1},{2,14},{6,10},... | collective-permute-start | bytes 392 | tf_op jit(solution)/shard_map/ppermute | solution.py:549
  (23 other events, 37.5 us)

commit v13 on v12

--- a/solution.py
+++ b/solution.py
@@ -600,10 +600,10 @@
     q_send = after(crossing_second(q_one, q_blocks[2], q_blocks[5]), far_up)
     q_far = (q_first, to_chip(q_send))
 
-    b_own, b_one, b_two = first_hops(after(t_outgrad[cut:], a_two))
     a_two = after(a_two, q_send)
     a_first = to_chip(crossing_first(a_own, a_two))
     a_blocks = last_hops(a_own, a_one, a_two)
+    b_own, b_one, b_two = first_hops(after(t_outgrad[cut:], a_blocks[2], a_blocks[5]))
     gates, ups = turned(t_gate, t_up, far_gate, far_up)
     a_send = crossing_second(a_one, a_blocks[2], after(a_blocks[5], *q_far, gates))
     a_far = (a_first, to_chip(a_send))
@@ -619,15 +619,15 @@
     a_near_sum, a_far_sum = partial_sums(
         after(flags, b_cross), a_blocks, a_far, weight_own, weight_sib
     )
-    b_send = crossing_second(b_one, b_blocks[2], after(b_blocks[5], a_far_sum))
+    b_send = crossing_second(b_one, b_blocks[2], after(b_blocks[5], a_far_sum, b_first))
     b_far = (b_first, to_chip(b_send))
-    a_returned = to_chip(after(a_far_sum, *b_far))
     in_out = own_in_out + outer(after(own_in_out, b_send))
     q_gradient = finished_sides(
         q_near_sum, after(q_returned, b_send), q_gate, q_up, proj_gate, proj_up
     )
     pair = jnp.concatenate([q_gradient, hidden[2 * cut :]], axis=1)
-    pair = pair + outer(pair)
+    pair = pair + outer(after(pair, in_out, *b_far))
+    a_returned = to_chip(after(a_far_sum, pair))
     b_near, b_away = lent_sides(
         after(flags, pair, in_out), b_blocks, b_far, weight_own, weight_sib, gates, ups,
         proj_gate, proj_up,

time: 219 us -> 216 us (0.986)
  starting transfers between devices: 48.9 us -> 43.1 us
  waiting for transfers between devices: 77.3 us -> 82.3 us
    ppermute x1, waiting for transfers between devices: 25.9 us -> 7.72 us  [moving_plan(): b_far = (b_first, to_chip(b_send))]
    ppermute x3, waiting for transfers between devices: 9.52 us -> 17.3 us  [last_hops(): return (own, one, mid, two, two, outer(after(two, one)))]
    ppermute x6, waiting for transfers between devices: 13.3 us -> 20.5 us  [first_hops(): return (own, outer(own), across(own))]
    ppermute x1, waiting for transfers between devices: 0.01 us -> 5.13 us  [moving_plan(): q_returned = to_chip(after(q_far_sum, *a_far))]
    ppermute x3, starting transfers between devices: 9.61 us -> 4.98 us  [last_hops(): return (own, one, mid, two, two, outer(after(two, one)))]
    ppermute x1, starting transfers between devices: 0.01 us -> 4.6 us  [moving_plan(): in_out = own_in_out + outer(after(own_in_out, b_send))]
    ppermute x1, waiting for transfers between devices: 13.5 us -> 9.2 us  [moving_plan(): far_up = to_chip(after(t_up[cut:], far_gate, weight_sib))]
    ppermute x1, waiting for transfers between devices: 0.56 us -> 3.64 us  [moving_plan(): in_out = own_in_out + outer(after(own_in_out, b_send))]
  transfers between devices with their start and end apart: 34 -> 34, of which waited for: 13 -> 15; matrix products, arithmetic and copies ran while one was open for 6% -> 5% of each run, Pallas kernels for 27% -> 28%
where the time goes in v13:
time: 216 us; the launch traced here: 215 us
  waiting for transfers between devices  82.3 us (38%)
  Pallas kernels  61.4 us (28%)
  starting transfers between devices  43.1 us (20%)
  local copies, waits for them, and re-layouts  20.1 us (9%)
  other arithmetic  7.73 us (4%)
    pallas_call x2, Pallas kernels, partial_sums(): pl.pallas_call(partial_kernel, grid=(units // TILE,), in_specs=[SCALARS]...  28.9 us
    ppermute x6, waiting for transfers between devices, first_hops(): return (own, outer(own), across(own))  20.5 us
    pallas_call x1, Pallas kernels, lent_sides(): pl.pallas_call(lent_kernel, grid=(units // TILE,), in_specs=[SCALARS] + [...  17.6 us
    ppermute x3, waiting for transfers between devices, last_hops(): return (own, one, mid, two, two, outer(after(two, one)))  17.3 us
    unnamed x70, local copies, waits for them, and re-layouts  16.6 us
    ppermute x6, starting transfers between devices, first_hops(): return (own, outer(own), across(own))  10.1 us
    ppermute x1, waiting for transfers between devices, moving_plan(): b_far_sides = to_chip(b_away)  9.28 us
    ppermute x1, waiting for transfers between devices, moving_plan(): far_up = to_chip(after(t_up[cut:], far_gate, weight_sib))  9.2 us
  transfers between devices with their start and end apart: 34, of which 15 were waited for; matrix products, arithmetic and copies ran while one was open for 5% of the time, Pallas kernels for 28%

profile of v13, /device:TPU:0, one launch (start us, length us, event | category | flops | bytes accessed | tf_op | source)
XLA Modules:
  0.0 215.1 jit_solution(107900699831320334)
XLA Ops:
  0.5 1.3 slice.40
  1.8 2.6 %collective-permute-start.1 = (bf16[128,3584]{1,0:T(8,128)(2,1)S(1)}, bf16[128,3584]{1,0:T(8,128)(2,1)S(1)}, u32[]{:S(2)}, u32[]{:S(2)}) collective-permute-start(bf16[128,3584]{1,0:T(8,128)(2,1)S(1)} %bitcast.30), channel_id=1, source_target_pairs={{0,2},{1,3},{2,0},{3,1},{4,6},{5,7},{6,4},{7,5},{8,10},{9,11},{10,... | collective-permute-start | bytes 2752520 | tf_op jit(solution)/shard_map/ppermute | solution.py:591
  4.4 2.6 %collective-permute-start = (bf16[128,2048]{1,0:T(8,128)(2,1)}, bf16[128,2048]{1,0:T(8,128)(2,1)}, u32[]{:S(2)}, u32[]{:S(2)}) collective-permute-start(bf16[128,2048]{1,0:T(8,128)(2,1)} %bitcast.4.q_outgrad.b0), channel_id=1, source_target_pairs={{0,8},{4,12},{8,0},{12,4},{1,9},{5,13},{9,1},{13,5},{2,10},{6,14},... | collective-permute-start | bytes 1572872 | tf_op jit(solution)/shard_map/ppermute | solution.py:587
  7.0 1.6 collective-permute-start.4
  8.6 1.5 copy-done.1
  10.1 1.2 copy-done.3
  13.7 1.2 copy-done.16
  18.8 4.9 %shard_map.154 = (f32[384,128]{1,0:T(8,128)S(1)}, f32[384,64]{1,0:T(8,128)S(1)}) custom-call(bf16[256,2048]{1,0:T(8,128)(2,1)S(1)} %bitcast.28, bf16[128,2048]{1,0:T(8,128)(2,1)S(1)} %bitcast.29, bf16[256,2048]{1,0:T(8,128)(2,1)S(1)} %bitcast.23, bf16[128,2048]{1,0:T(8,128)(2,1)} %bitcast.4.q_outgrad.b0, bf16[64,2048]{1,0:T(8,128)(2,1)S(1)} %copy-done.19, ...), custom_call_target="tpu_custom_call" | custom-call | flops 1024 | bytes 1024 | tf_op jit(solution)/shard_map/pallas_call | solution.py:395
  23.7 7.1 %collective-permute-done.b3.b4 = bf16[128,2048]{1,0:T(8,128)(2,1)} collective-permute-done((bf16[128,2048]{1,0:T(8,128)(2,1)}, bf16[128,2048]{1,0:T(8,128)(2,1)}, u32[]{:S(2)}, u32[]{:S(2)}) %collective-permute-start) | collective-permute-done | bytes 524320 | tf_op jit(solution)/shard_map/ppermute | solution.py:587
  31.0 1.4 collective-permute-start.5
  35.1 2.4 %collective-permute-start.2 = (bf16[128,2048]{1,0:T(8,128)(2,1)}, bf16[128,2048]{1,0:T(8,128)(2,1)}, u32[]{:S(2)}, u32[]{:S(2)}) collective-permute-start(bf16[128,2048]{1,0:T(8,128)(2,1)} %bitcast.10.b0), channel_id=1, source_target_pairs={{0,8},{4,12},{8,0},{12,4},{1,9},{5,13},{9,1},{13,5},{2,10},{6,14},... | collective-permute-start | bytes 1572872 | tf_op jit(solution)/shard_map/ppermute | solution.py:587
  38.1 8.1 %collective-permute-done.5.b5 = bf16[128,2048]{1,0:T(8,128)(2,1)} collective-permute-done((bf16[128,2048]{1,0:T(8,128)(2,1)}, bf16[128,2048]{1,0:T(8,128)(2,1)}, u32[]{:S(2)}, u32[]{:S(2)}) %collective-permute-start.5) | collective-permute-done | bytes 524320 | tf_op jit(solution)/shard_map/ppermute | solution.py:575
  47.3 9.2 %collective-permute-done.7.far_up = bf16[128,3584]{1,0:T(8,128)(2,1)} collective-permute-done((bf16[128,3584]{1,0:T(8,128)(2,1)}, bf16[128,3584]{1,0:T(8,128)(2,1)}, u32[]{:S(2)}, u32[]{:S(2)}) %collective-permute-start.7) | collective-permute-done | bytes 917536 | tf_op jit(solution)/shard_map/ppermute | solution.py:599
  56.5 12.9 %collective-permute-done.2.b3.b4 = bf16[128,2048]{1,0:T(8,128)(2,1)} collective-permute-done((bf16[128,2048]{1,0:T(8,128)(2,1)}, bf16[128,2048]{1,0:T(8,128)(2,1)}, u32[]{:S(2)}, u32[]{:S(2)}) %collective-permute-start.2) | collective-permute-done | bytes 524320 | tf_op jit(solution)/shard_map/ppermute | solution.py:587
  69.5 1.3 broadcast_select_fusion.2
  71.2 1.6 collective-permute-start.13
  73.4 9.2 %collective-permute-done.10.b5 = bf16[128,2048]{1,0:T(8,128)(2,1)S(1)} collective-permute-done((bf16[128,2048]{1,0:T(8,128)(2,1)}, bf16[128,2048]{1,0:T(8,128)(2,1)S(1)}, u32[]{:S(2)}, u32[]{:S(2)}) %collective-permute-start.10) | collective-permute-done | bytes 524320 | tf_op jit(solution)/shard_map/ppermute | solution.py:575
  82.7 2.6 %collective-permute-start.11 = (bf16[128,2048]{1,0:T(8,128)(2,1)}, bf16[128,2048]{1,0:T(8,128)(2,1)}, u32[]{:S(2)}, u32[]{:S(2)}) collective-permute-start(bf16[128,2048]{1,0:T(8,128)(2,1)} %bitcast.9.b0), channel_id=1, source_target_pairs={{0,8},{4,12},{8,0},{12,4},{1,9},{5,13},{9,1},{13,5},{2,10},{6,14},... | collective-permute-start | bytes 1572872 | tf_op jit(solution)/shard_map/ppermute | solution.py:587
  85.3 1.9 broadcast_select_fusion
  87.7 4.6 %shard_map.155 = (bf16[3584,256]{1,0:T(8,128)(2,1)S(1)}, bf16[3584,256]{1,0:T(8,128)(2,1)S(1)}) custom-call(bf16[256,3584]{1,0:T(8,128)(2,1)S(1)} %bitcast.18, bf16[256,3584]{1,0:T(8,128)(2,1)S(1)} %bitcast.21, bf16[128,3584]{1,0:T(8,128)(2,1)S(1)} %collective-permute-done.1.far_gate, bf16[128,3584]{1,0:T(8,128)(2,1)} %collective-permute-done.7.far_up), custom_call_target="tpu_custom_call" | custom-call | flops 1024 | bytes 1024 | tf_op jit(solution)/shard_map/pallas_call | solution.py:297
  92.3 1.3 copy-done.13
  93.6 1.2 copy-done.14
  95.2 1.6 collective-permute-done.13.far_b
  98.5 14.4 %shard_map.156 = (f32[3584,128]{1,0:T(8,128)}, bf16[3584,128]{1,0:T(8,128)(2,1)}) custom-call(s32[3]{0:T(128)} %pad_add_fusion.flags, bf16[128,2048]{1,0:T(8,128)(2,1)} %bitcast.4.q_outgrad.b0, bf16[128,2048]{1,0:T(8,128)(2,1)} %copy-done.26, bf16[128,2048]{1,0:T(8,128)(2,1)} %collective-permute-done.3.b2, bf16[128,2048]{1,0:T(8,128)(2,1)} %collective-permute-done.b3.b4, ...), custom_call_target="tpu_custom_call" | custom-call | flops 1024 | bytes 1024 | tf_op jit(solution)/shard_map/pallas_call | solution.py:248
  112.9 1.9 broadcast_select_fusion.1
  116.3 3.5 %collective-permute-start.16 = (bf16[128,2048]{1,0:T(8,128)(2,1)}, bf16[128,2048]{1,0:T(8,128)(2,1)S(1)}, u32[]{:S(2)}, u32[]{:S(2)}) collective-permute-start(bf16[128,2048]{1,0:T(8,128)(2,1)} %collective-permute-done.11.b3.b4), channel_id=1, source_target_pairs={{0,4},{4,0},{8,12},{12,8},{1,5},{5,1},{9,13},{13,9},{2,6},{6,2},{1... | collective-permute-start | bytes 1572872 | tf_op jit(solution)/shard_map/ppermute | solution.py:575
  120.8 14.5 %shard_map.157 = (f32[3584,128]{1,0:T(8,128)}, bf16[3584,128]{1,0:T(8,128)(2,1)}) custom-call(s32[3]{0:T(128)} %pad_add_fusion.flags, bf16[128,2048]{1,0:T(8,128)(2,1)} %bitcast.10.b0, bf16[128,2048]{1,0:T(8,128)(2,1)} %collective-permute-done.9.b1, bf16[128,2048]{1,0:T(8,128)(2,1)} %copy-done.30, bf16[128,2048]{1,0:T(8,128)(2,1)} %collective-permute-done.2.b3.b4, ...), custom_call_target="tpu_custom_call" | custom-call | flops 1024 | bytes 1024 | tf_op jit(solution)/shard_map/pallas_call | solution.py:248
  135.5 1.2 collective-permute-start.23
  136.7 4.6 %collective-permute-start.20 = (f32[384,128]{1,0:T(8,128)S(1)}, f32[384,128]{1,0:T(8,128)S(1)}, u32[]{:S(2)}, u32[]{:S(2)}) collective-permute-start(f32[384,128]{1,0:T(8,128)S(1)} %copy-done.22), channel_id=1, source_target_pairs={{0,4},{4,0},{8,12},{12,8},{1,5},{5,1},{9,13},{13,9},{2,6},{6,2},{1... | collective-permute-start | bytes 589832 | tf_op jit(solution)/shard_map/ppermute | solution.py:624
  141.3 3.6 %collective-permute-done.20 = f32[384,128]{1,0:T(8,128)S(1)} collective-permute-done((f32[384,128]{1,0:T(8,128)S(1)}, f32[384,128]{1,0:T(8,128)S(1)}, u32[]{:S(2)}, u32[]{:S(2)}) %collective-permute-start.20) | collective-permute-done | bytes 196640 | tf_op jit(solution)/shard_map/ppermute | solution.py:624
  145.0 5.1 %collective-permute-done.22.returned = bf16[3584,128]{1,0:T(8,128)(2,1)S(1)} collective-permute-done((bf16[3584,128]{1,0:T(8,128)(2,1)}, bf16[3584,128]{1,0:T(8,128)(2,1)S(1)}, u32[]{:S(2)}, u32[]{:S(2)}) %collective-permute-start.22) | collective-permute-done | bytes 917536 | tf_op jit(solution)/shard_map/ppermute | solution.py:613
  150.1 1.5 copy-done.15
  151.6 1.6 shard_map.158
  153.2 7.7 %collective-permute-done.23.far_b = bf16[128,2048]{1,0:T(8,128)(2,1)S(1)} collective-permute-done((bf16[128,2048]{1,0:T(8,128)(2,1)S(1)}, bf16[128,2048]{1,0:T(8,128)(2,1)S(1)}, u32[]{:S(2)}, u32[]{:S(2)}) %collective-permute-start.23) | collective-permute-done | bytes 524320 | tf_op jit(solution)/shard_map/ppermute | solution.py:623
  160.9 1.6 collective-permute-start.24
  162.5 3.6 %collective-permute-done.24 = f32[128,192]{1,0:T(8,128)S(1)} collective-permute-done((f32[128,192]{1,0:T(8,128)S(1)}, f32[128,192]{1,0:T(8,128)S(1)}, u32[]{:S(2)}, u32[]{:S(2)}) %collective-permute-start.24) | collective-permute-done | bytes 98336 | tf_op jit(solution)/shard_map/ppermute | solution.py:629
  166.4 1.8 collective-permute-start.21
  169.3 17.6 %shard_map.159 = (f32[128,128]{1,0:T(8,128)}, f32[128,128]{1,0:T(8,128)}) custom-call(s32[3]{0:T(128)} %pad_add_fusion.flags, bf16[128,2048]{1,0:T(8,128)(2,1)} %bitcast.9.b0, bf16[128,2048]{1,0:T(8,128)(2,1)} %copy-done.27, bf16[128,2048]{1,0:T(8,128)(2,1)} %collective-permute-done.14.b2, bf16[128,2048]{1,0:T(8,128)(2,1)} %collective-permute-done.11.b3.b4, ...), custom_call_target="tpu_custom_call" | custom-call | flops 1024 | bytes 1024 | tf_op jit(solution)/shard_map/pallas_call | solution.py:341
  188.2 1.9 collective-permute-start.29
  190.1 1.7 collective-permute-start.26
  191.9 9.3 %collective-permute-done.26.far = f32[128,128]{1,0:T(8,128)S(1)} collective-permute-done((f32[128,128]{1,0:T(8,128)S(1)}, f32[128,128]{1,0:T(8,128)S(1)}, u32[]{:S(2)}, u32[]{:S(2)}) %collective-permute-start.26) | collective-permute-done | bytes 65568 | tf_op jit(solution)/shard_map/ppermute | solution.py:635
  201.2 1.5 copy-done.12
  202.7 1.6 shard_map.160.early
  204.3 1.4 shard_map.162
  205.7 1.6 collective-permute-start.31
  207.3 1.8 collective-permute-start.32
  210.2 1.6 collective-permute-done.32
  211.8 2.7 %collective-permute-done.33 = f32[4,8]{1,0:T(4,128)S(1)} collective-permute-done((f32[4,8]{1,0:T(4,128)S(1)}, f32[4,8]{1,0:T(4,128)S(1)}, u32[]{:S(2)}, u32[]{:S(2)}) %collective-permute-start.33) | collective-permute-done | bytes 160 | tf_op jit(solution)/shard_map/ppermute | solution.py:549
  (120 shorter events, 22.0 us)
Async XLA Ops:
  0.0 33.4 %collective-permute-start.6 = (bf16[3584,2048]{1,0:T(8,128)(2,1)}, bf16[3584,2048]{1,0:T(8,128)(2,1)}, u32[]{:S(2)}, u32[]{:S(2)}) collective-permute-start(bf16[3584,2048]{1,0:T(8,128)(2,1)} %weight_own.5), channel_id=1, source_target_pairs={{0,1},{1,0},{2,3},{3,2},{4,5},{5,4},{6,7},{7,6},{8,9},{9,8},{10,11... | collective-permute-start | bytes 44040200 | tf_op jit(solution)/shard_map/ppermute | solution.py:589
  1.8 31.6 %collective-permute-start.1 = (bf16[128,3584]{1,0:T(8,128)(2,1)S(1)}, bf16[128,3584]{1,0:T(8,128)(2,1)S(1)}, u32[]{:S(2)}, u32[]{:S(2)}) collective-permute-start(bf16[128,3584]{1,0:T(8,128)(2,1)S(1)} %bitcast.30), channel_id=1, source_target_pairs={{0,2},{1,3},{2,0},{3,1},{4,6},{5,7},{6,4},{7,5},{8,10},{9,11},{10,... | collective-permute-start | bytes 2752520 | tf_op jit(solution)/shard_map/ppermute | solution.py:591
  4.4 26.5 %collective-permute-start = (bf16[128,2048]{1,0:T(8,128)(2,1)}, bf16[128,2048]{1,0:T(8,128)(2,1)}, u32[]{:S(2)}, u32[]{:S(2)}) collective-permute-start(bf16[128,2048]{1,0:T(8,128)(2,1)} %bitcast.4.q_outgrad.b0), channel_id=1, source_target_pairs={{0,8},{4,12},{8,0},{12,4},{1,9},{5,13},{9,1},{13,5},{2,10},{6,14},... | collective-permute-start | bytes 1572872 | tf_op jit(solution)/shard_map/ppermute | solution.py:587
  7.0 24.0 %collective-permute-start.4 = (bf16[128,2048]{1,0:T(8,128)(2,1)}, bf16[128,2048]{1,0:T(8,128)(2,1)S(1)}, u32[]{:S(2)}, u32[]{:S(2)}) collective-permute-start(bf16[128,2048]{1,0:T(8,128)(2,1)} %bitcast.4.q_outgrad.b0), channel_id=1, source_target_pairs={{0,4},{4,0},{8,12},{12,8},{1,5},{5,1},{9,13},{13,9},{2,6},{6,2},{1... | collective-permute-start | bytes 1572872 | tf_op jit(solution)/shard_map/ppermute | solution.py:587
  30.9 15.2 %copy-start.26 = (bf16[128,2048]{1,0:T(8,128)(2,1)}, bf16[128,2048]{1,0:T(8,128)(2,1)S(1)}, u32[]{:S(2)}) copy-start(bf16[128,2048]{1,0:T(8,128)(2,1)S(1)} %collective-permute-done.4.b1) | copy-start | bytes 1572868
  31.0 15.2 %collective-permute-start.5 = (bf16[128,2048]{1,0:T(8,128)(2,1)}, bf16[128,2048]{1,0:T(8,128)(2,1)}, u32[]{:S(2)}, u32[]{:S(2)}) collective-permute-start(bf16[128,2048]{1,0:T(8,128)(2,1)} %collective-permute-done.b3.b4), channel_id=1, source_target_pairs={{0,4},{4,0},{8,12},{12,8},{1,5},{5,1},{9,13},{13,9},{2,6},{6,2},{1... | collective-permute-start | bytes 1572872 | tf_op jit(solution)/shard_map/ppermute | solution.py:575
  32.4 13.8 %collective-permute-start.3 = (bf16[128,2048]{1,0:T(8,128)(2,1)}, bf16[128,2048]{1,0:T(8,128)(2,1)}, u32[]{:S(2)}, u32[]{:S(2)}) collective-permute-start(bf16[128,2048]{1,0:T(8,128)(2,1)} %bitcast.4.q_outgrad.b0), channel_id=1, source_target_pairs={{0,1},{1,0},{2,3},{3,2},{4,8},{5,9},{6,10},{7,11},{8,4},{9,5},{10,... | collective-permute-start | bytes 1572872 | tf_op jit(solution)/shard_map/ppermute | solution.py:574
  33.4 23.1 %collective-permute-start.7 = (bf16[128,3584]{1,0:T(8,128)(2,1)}, bf16[128,3584]{1,0:T(8,128)(2,1)}, u32[]{:S(2)}, u32[]{:S(2)}) collective-permute-start(bf16[128,3584]{1,0:T(8,128)(2,1)} %bitcast.12), channel_id=1, source_target_pairs={{0,2},{1,3},{2,0},{3,1},{4,6},{5,7},{6,4},{7,5},{8,10},{9,11},{10,... | collective-permute-start | bytes 2752520 | tf_op jit(solution)/shard_map/ppermute | solution.py:599
  35.1 34.4 %collective-permute-start.2 = (bf16[128,2048]{1,0:T(8,128)(2,1)}, bf16[128,2048]{1,0:T(8,128)(2,1)}, u32[]{:S(2)}, u32[]{:S(2)}) collective-permute-start(bf16[128,2048]{1,0:T(8,128)(2,1)} %bitcast.10.b0), channel_id=1, source_target_pairs={{0,8},{4,12},{8,0},{12,4},{1,9},{5,13},{9,1},{13,5},{2,10},{6,14},... | collective-permute-start | bytes 1572872 | tf_op jit(solution)/shard_map/ppermute | solution.py:587
  37.5 31.9 %collective-permute-start.9 = (bf16[128,2048]{1,0:T(8,128)(2,1)}, bf16[128,2048]{1,0:T(8,128)(2,1)}, u32[]{:S(2)}, u32[]{:S(2)}) collective-permute-start(bf16[128,2048]{1,0:T(8,128)(2,1)} %bitcast.10.b0), channel_id=1, source_target_pairs={{0,4},{4,0},{8,12},{12,8},{1,5},{5,1},{9,13},{13,9},{2,6},{6,2},{1... | collective-permute-start | bytes 1572872 | tf_op jit(solution)/shard_map/ppermute | solution.py:587
  47.3 40.4 %copy-start.2 = (bf16[4,64,3584]{2,1,0:T(8,128)(2,1)S(1)}, bf16[4,64,3584]{2,1,0:T(8,128)(2,1)}, u32[]{:S(2)}) copy-start(bf16[4,64,3584]{2,1,0:T(8,128)(2,1)} %param.18) | copy-start | bytes 5505028
  69.4 13.2 %collective-permute-start.10 = (bf16[128,2048]{1,0:T(8,128)(2,1)}, bf16[128,2048]{1,0:T(8,128)(2,1)S(1)}, u32[]{:S(2)}, u32[]{:S(2)}) collective-permute-start(bf16[128,2048]{1,0:T(8,128)(2,1)} %collective-permute-done.2.b3.b4), channel_id=1, source_target_pairs={{0,4},{4,0},{8,12},{12,8},{1,5},{5,1},{9,13},{13,9},{2,6},{6,2},{1... | collective-permute-start | bytes 1572872 | tf_op jit(solution)/shard_map/ppermute | solution.py:575
  69.4 13.2 %collective-permute-start.8 = (bf16[128,2048]{1,0:T(8,128)(2,1)}, bf16[128,2048]{1,0:T(8,128)(2,1)S(1)}, u32[]{:S(2)}, u32[]{:S(2)}) collective-permute-start(bf16[128,2048]{1,0:T(8,128)(2,1)} %bitcast.10.b0), channel_id=1, source_target_pairs={{0,1},{1,0},{2,3},{3,2},{4,8},{5,9},{6,10},{7,11},{8,4},{9,5},{10,... | collective-permute-start | bytes 1572872 | tf_op jit(solution)/shard_map/ppermute | solution.py:574
  70.7 24.4 %collective-permute-start.12 = (bf16[128,2048]{1,0:T(8,128)(2,1)S(1)}, bf16[128,2048]{1,0:T(8,128)(2,1)S(1)}, u32[]{:S(2)}, u32[]{:S(2)}) collective-permute-start(bf16[128,2048]{1,0:T(8,128)(2,1)S(1)} %broadcast_select_fusion.2), channel_id=1, source_target_pairs={{0,2},{1,3},{2,0},{3,1},{4,6},{5,7},{6,4},{7,5},{8,10},{9,11},{10,... | collective-permute-start | bytes 1572872 | tf_op jit(solution)/shard_map/ppermute | solution.py:597
  71.2 25.6 %collective-permute-start.13 = (bf16[128,2048]{1,0:T(8,128)(2,1)S(1)}, bf16[128,2048]{1,0:T(8,128)(2,1)S(1)}, u32[]{:S(2)}, u32[]{:S(2)}) collective-permute-start(bf16[128,2048]{1,0:T(8,128)(2,1)S(1)} %select_select_fusion.2), channel_id=1, source_target_pairs={{0,2},{1,3},{2,0},{3,1},{4,6},{5,7},{6,4},{7,5},{8,10},{9,11},{10,... | collective-permute-start | bytes 1572872 | tf_op jit(solution)/shard_map/ppermute | solution.py:601
  82.7 14.1 %copy-start.29 = (bf16[128,2048]{1,0:T(8,128)(2,1)}, bf16[128,2048]{1,0:T(8,128)(2,1)S(1)}, u32[]{:S(2)}) copy-start(bf16[128,2048]{1,0:T(8,128)(2,1)S(1)} %collective-permute-done.10.b5) | copy-start | bytes 1572868
  82.7 14.1 %copy-start.30 = (bf16[128,2048]{1,0:T(8,128)(2,1)}, bf16[128,2048]{1,0:T(8,128)(2,1)S(1)}, u32[]{:S(2)}) copy-start(bf16[128,2048]{1,0:T(8,128)(2,1)S(1)} %collective-permute-done.8.b2) | copy-start | bytes 1572868
  82.7 30.2 %collective-permute-start.11 = (bf16[128,2048]{1,0:T(8,128)(2,1)}, bf16[128,2048]{1,0:T(8,128)(2,1)}, u32[]{:S(2)}, u32[]{:S(2)}) collective-permute-start(bf16[128,2048]{1,0:T(8,128)(2,1)} %bitcast.9.b0), channel_id=1, source_target_pairs={{0,8},{4,12},{8,0},{12,4},{1,9},{5,13},{9,1},{13,5},{2,10},{6,14},... | collective-permute-start | bytes 1572872 | tf_op jit(solution)/shard_map/ppermute | solution.py:587
  87.2 32.6 %collective-permute-start.17 = (bf16[128,2048]{1,0:T(8,128)(2,1)}, bf16[128,2048]{1,0:T(8,128)(2,1)}, u32[]{:S(2)}, u32[]{:S(2)}) collective-permute-start(bf16[128,2048]{1,0:T(8,128)(2,1)} %broadcast_select_fusion), channel_id=1, source_target_pairs={{0,2},{1,3},{2,0},{3,1},{4,6},{5,7},{6,4},{7,5},{8,10},{9,11},{10,... | collective-permute-start | bytes 1572872 | tf_op jit(solution)/shard_map/ppermute | solution.py:604
  94.8 21.4 %collective-permute-start.15 = (bf16[128,2048]{1,0:T(8,128)(2,1)}, bf16[128,2048]{1,0:T(8,128)(2,1)S(1)}, u32[]{:S(2)}, u32[]{:S(2)}) collective-permute-start(bf16[128,2048]{1,0:T(8,128)(2,1)} %bitcast.9.b0), channel_id=1, source_target_pairs={{0,4},{4,0},{8,12},{12,8},{1,5},{5,1},{9,13},{13,9},{2,6},{6,2},{1... | collective-permute-start | bytes 1572872 | tf_op jit(solution)/shard_map/ppermute | solution.py:587
  97.6 22.2 %collective-permute-start.18 = (bf16[128,2048]{1,0:T(8,128)(2,1)S(1)}, bf16[128,2048]{1,0:T(8,128)(2,1)}, u32[]{:S(2)}, u32[]{:S(2)}) collective-permute-start(bf16[128,2048]{1,0:T(8,128)(2,1)S(1)} %select_select_fusion.1), channel_id=1, source_target_pairs={{0,2},{1,3},{2,0},{3,1},{4,6},{5,7},{6,4},{7,5},{8,10},{9,11},{10,... | collective-permute-start | bytes 1572872 | tf_op jit(solution)/shard_map/ppermute | solution.py:609
  114.8 20.6 %collective-permute-start.19 = (bf16[128,2048]{1,0:T(8,128)(2,1)}, bf16[128,2048]{1,0:T(8,128)(2,1)}, u32[]{:S(2)}, u32[]{:S(2)}) collective-permute-start(bf16[128,2048]{1,0:T(8,128)(2,1)} %broadcast_select_fusion.1), channel_id=1, source_target_pairs={{0,2},{1,3},{2,0},{3,1},{4,6},{5,7},{6,4},{7,5},{8,10},{9,11},{10,... | collective-permute-start | bytes 1572872 | tf_op jit(solution)/shard_map/ppermute | solution.py:617
  116.3 19.2 %copy-start.27 = (bf16[128,2048]{1,0:T(8,128)(2,1)}, bf16[128,2048]{1,0:T(8,128)(2,1)S(1)}, u32[]{:S(2)}) copy-start(bf16[128,2048]{1,0:T(8,128)(2,1)S(1)} %collective-permute-done.15.b1) | copy-start | bytes 1572868
  116.3 19.1 %collective-permute-start.16 = (bf16[128,2048]{1,0:T(8,128)(2,1)}, bf16[128,2048]{1,0:T(8,128)(2,1)S(1)}, u32[]{:S(2)}, u32[]{:S(2)}) collective-permute-start(bf16[128,2048]{1,0:T(8,128)(2,1)} %collective-permute-done.11.b3.b4), channel_id=1, source_target_pairs={{0,4},{4,0},{8,12},{12,8},{1,5},{5,1},{9,13},{13,9},{2,6},{6,2},{1... | collective-permute-start | bytes 1572872 | tf_op jit(solution)/shard_map/ppermute | solution.py:575
  119.8 15.6 %collective-permute-start.14 = (bf16[128,2048]{1,0:T(8,128)(2,1)}, bf16[128,2048]{1,0:T(8,128)(2,1)}, u32[]{:S(2)}, u32[]{:S(2)}) collective-permute-start(bf16[128,2048]{1,0:T(8,128)(2,1)} %bitcast.9.b0), channel_id=1, source_target_pairs={{0,1},{1,0},{2,3},{3,2},{4,8},{5,9},{6,10},{7,11},{8,4},{9,5},{10,... | collective-permute-start | bytes 1572872 | tf_op jit(solution)/shard_map/ppermute | solution.py:574
  119.8 30.3 %collective-permute-start.22 = (bf16[3584,128]{1,0:T(8,128)(2,1)}, bf16[3584,128]{1,0:T(8,128)(2,1)S(1)}, u32[]{:S(2)}, u32[]{:S(2)}) collective-permute-start(bf16[3584,128]{1,0:T(8,128)(2,1)} %get-tuple-element.64), channel_id=1, source_target_pairs={{0,2},{1,3},{2,0},{3,1},{4,6},{5,7},{6,4},{7,5},{8,10},{9,11},{10,... | collective-permute-start | bytes 2752520 | tf_op jit(solution)/shard_map/ppermute | solution.py:613
  120.8 15.9 %copy-start.22 = (f32[384,128]{1,0:T(8,128)S(1)}, f32[384,128]{1,0:T(8,128)}, u32[]{:S(2)}) copy-start(f32[384,128]{1,0:T(8,128)} %copy-done.21) | copy-start | bytes 589828
  135.3 14.8 %copy-start.4 = (bf16[64,3584]{1,0:T(8,128)(2,1)S(1)}, bf16[64,3584]{1,0:T(8,128)(2,1)}, u32[]{:S(2)}) copy-start(bf16[64,3584]{1,0:T(8,128)(2,1)} %proj_gate.5) | copy-start | bytes 1376260
  135.3 14.8 %copy-start.6 = (bf16[64,3584]{1,0:T(8,128)(2,1)S(1)}, bf16[64,3584]{1,0:T(8,128)(2,1)}, u32[]{:S(2)}) copy-start(bf16[64,3584]{1,0:T(8,128)(2,1)} %proj_up.5) | copy-start | bytes 1376260
  135.3 14.8 %copy-start.9 = (bf16[2,64,3584]{2,1,0:T(8,128)(2,1)S(1)}, bf16[2,64,3584]{2,1,0:T(8,128)(2,1)}, u32[]{:S(2)}) copy-start(bf16[2,64,3584]{2,1,0:T(8,128)(2,1)} %param.22) | copy-start | bytes 2752516
  135.4 14.8 %copy-start.11 = (bf16[2,64,3584]{2,1,0:T(8,128)(2,1)S(1)}, bf16[2,64,3584]{2,1,0:T(8,128)(2,1)}, u32[]{:S(2)}) copy-start(bf16[2,64,3584]{2,1,0:T(8,128)(2,1)} %param.23) | copy-start | bytes 2752516
  135.4 17.8 %copy-start.28 = (bf16[128,2048]{1,0:T(8,128)(2,1)}, bf16[128,2048]{1,0:T(8,128)(2,1)S(1)}, u32[]{:S(2)}) copy-start(bf16[128,2048]{1,0:T(8,128)(2,1)S(1)} %collective-permute-done.16.b5) | copy-start | bytes 1572868
  135.5 25.4 %collective-permute-start.23 = (bf16[128,2048]{1,0:T(8,128)(2,1)S(1)}, bf16[128,2048]{1,0:T(8,128)(2,1)S(1)}, u32[]{:S(2)}, u32[]{:S(2)}) collective-permute-start(bf16[128,2048]{1,0:T(8,128)(2,1)S(1)} %select_select_fusion), channel_id=1, source_target_pairs={{0,2},{1,3},{2,0},{3,1},{4,6},{5,7},{6,4},{7,5},{8,10},{9,11},{10,... | collective-permute-start | bytes 1572872 | tf_op jit(solution)/shard_map/ppermute | solution.py:623
  136.7 8.3 %collective-permute-start.20 = (f32[384,128]{1,0:T(8,128)S(1)}, f32[384,128]{1,0:T(8,128)S(1)}, u32[]{:S(2)}, u32[]{:S(2)}) collective-permute-start(f32[384,128]{1,0:T(8,128)S(1)} %copy-done.22), channel_id=1, source_target_pairs={{0,4},{4,0},{8,12},{12,8},{1,5},{5,1},{9,13},{13,9},{2,6},{6,2},{1... | collective-permute-start | bytes 589832 | tf_op jit(solution)/shard_map/ppermute | solution.py:624
  160.9 5.1 %collective-permute-start.24 = (f32[128,192]{1,0:T(8,128)S(1)}, f32[128,192]{1,0:T(8,128)S(1)}, u32[]{:S(2)}, u32[]{:S(2)}) collective-permute-start(f32[128,192]{1,0:T(8,128)S(1)} %pad_maximum_fusion.1), channel_id=1, source_target_pairs={{0,4},{4,0},{8,12},{12,8},{1,5},{5,1},{9,13},{13,9},{2,6},{6,2},{1... | collective-permute-start | bytes 294920 | tf_op jit(solution)/shard_map/ppermute | solution.py:629
  166.1 35.1 %collective-permute-start.25 = (bf16[3584,128]{1,0:T(8,128)(2,1)}, bf16[3584,128]{1,0:T(8,128)(2,1)S(1)}, u32[]{:S(2)}, u32[]{:S(2)}) collective-permute-start(bf16[3584,128]{1,0:T(8,128)(2,1)} %get-tuple-element.73), channel_id=1, source_target_pairs={{0,2},{1,3},{2,0},{3,1},{4,6},{5,7},{6,4},{7,5},{8,10},{9,11},{10,... | collective-permute-start | bytes 2752520 | tf_op jit(solution)/shard_map/ppermute | solution.py:630
  166.4 20.5 %collective-permute-start.21 = (f32[384,128]{1,0:T(8,128)S(1)}, f32[384,128]{1,0:T(8,128)S(1)}, u32[]{:S(2)}, u32[]{:S(2)}) collective-permute-start(f32[384,128]{1,0:T(8,128)S(1)} %add.32), channel_id=1, source_target_pairs={{0,8},{4,12},{8,0},{12,4},{1,9},{5,13},{9,1},{13,5},{2,10},{6,14},... | collective-permute-start | bytes 589832 | tf_op jit(solution)/shard_map/ppermute | solution.py:636
  168.1 18.8 %collective-permute-start.27 = (f32[128,192]{1,0:T(8,128)S(1)}, f32[128,192]{1,0:T(8,128)S(1)}, u32[]{:S(2)}, u32[]{:S(2)}) collective-permute-start(f32[128,192]{1,0:T(8,128)S(1)} %fusion), channel_id=1, source_target_pairs={{0,8},{4,12},{8,0},{12,4},{1,9},{5,13},{9,1},{13,5},{2,10},{6,14},... | collective-permute-start | bytes 294920 | tf_op jit(solution)/shard_map/ppermute | solution.py:637
  169.3 17.8 %copy-start.24 = (s32[2]{0:T(128)S(1)}, s32[2]{0:T(128)}, u32[]{:S(2)}) copy-start(s32[2]{0:T(128)} %lengths.2) | copy-start | bytes 28
  186.9 14.3 %copy-start.5 = (bf16[64,3584]{1,0:T(8,128)(2,1)S(1)}, bf16[64,3584]{1,0:T(8,128)(2,1)}, u32[]{:S(2)}) copy-start(bf16[64,3584]{1,0:T(8,128)(2,1)} %proj_gate.5) | copy-start | bytes 1376260
  186.9 14.2 %copy-start.7 = (bf16[64,3584]{1,0:T(8,128)(2,1)S(1)}, bf16[64,3584]{1,0:T(8,128)(2,1)}, u32[]{:S(2)}) copy-start(bf16[64,3584]{1,0:T(8,128)(2,1)} %proj_up.5) | copy-start | bytes 1376260
  188.1 16.2 %collective-permute-start.28 = (f32[2,192,64]{2,1,0:T(8,128)S(1)}, f32[2,192,64]{2,1,0:T(8,128)S(1)}, u32[]{:S(2)}, u32[]{:S(2)}) collective-permute-start(f32[2,192,64]{2,1,0:T(8,128)S(1)} %shard_map.161.q0), channel_id=1, source_target_pairs={{0,1},{1,0},{2,3},{3,2},{4,5},{5,4},{6,7},{7,6},{8,9},{9,8},{10,11... | collective-permute-start | bytes 294920 | tf_op jit(solution)/shard_map/ppermute | solution.py:641
  188.2 16.1 %collective-permute-start.29 = (f32[2,192,64]{2,1,0:T(8,128)S(1)}, f32[2,192,64]{2,1,0:T(8,128)S(1)}, u32[]{:S(2)}, u32[]{:S(2)}) collective-permute-start(f32[2,192,64]{2,1,0:T(8,128)S(1)} %shard_map.161.q0), channel_id=1, source_target_pairs={{0,2},{1,3},{2,0},{3,1},{4,6},{5,7},{6,4},{7,5},{8,10},{9,11},{10,... | collective-permute-start | bytes 294920 | tf_op jit(solution)/shard_map/ppermute | solution.py:641
  190.0 14.3 %collective-permute-start.30 = (f32[2,192,64]{2,1,0:T(8,128)S(1)}, f32[2,192,64]{2,1,0:T(8,128)S(1)}, u32[]{:S(2)}, u32[]{:S(2)}) collective-permute-start(f32[2,192,64]{2,1,0:T(8,128)S(1)} %shard_map.161.q0), channel_id=1, source_target_pairs={{0,3},{1,2},{2,1},{3,0},{4,7},{5,6},{6,5},{7,4},{8,11},{9,10},{10,... | collective-permute-start | bytes 294920 | tf_op jit(solution)/shard_map/ppermute | solution.py:641
  190.1 11.0 %collective-permute-start.26 = (f32[128,128]{1,0:T(8,128)S(1)}, f32[128,128]{1,0:T(8,128)S(1)}, u32[]{:S(2)}, u32[]{:S(2)}) collective-permute-start(f32[128,128]{1,0:T(8,128)S(1)} %copy-done.34), channel_id=1, source_target_pairs={{0,2},{1,3},{2,0},{3,1},{4,6},{5,7},{6,4},{7,5},{8,10},{9,11},{10,... | collective-permute-start | bytes 196616 | tf_op jit(solution)/shard_map/ppermute | solution.py:635
  205.7 4.5 %collective-permute-start.31 = (f32[4,8]{1,0:T(4,128)S(1)}, f32[4,8]{1,0:T(4,128)S(1)}, u32[]{:S(2)}, u32[]{:S(2)}) collective-permute-start(f32[4,8]{1,0:T(4,128)S(1)} %shard_map.162), channel_id=1, source_target_pairs={{0,4},{4,0},{8,12},{12,8},{1,5},{5,1},{9,13},{13,9},{2,6},{6,2},{1... | collective-permute-start | bytes 392 | tf_op jit(solution)/shard_map/ppermute | solution.py:549
  207.3 4.5 %collective-permute-start.32 = (f32[4,8]{1,0:T(4,128)S(1)}, f32[4,8]{1,0:T(4,128)S(1)}, u32[]{:S(2)}, u32[]{:S(2)}) collective-permute-start(f32[4,8]{1,0:T(4,128)S(1)} %shard_map.162), channel_id=1, source_target_pairs={{0,8},{4,12},{8,0},{12,4},{1,9},{5,13},{9,1},{13,5},{2,10},{6,14},... | collective-permute-start | bytes 392 | tf_op jit(solution)/shard_map/ppermute | solution.py:549
  209.1 5.4 %collective-permute-start.33 = (f32[4,8]{1,0:T(4,128)S(1)}, f32[4,8]{1,0:T(4,128)S(1)}, u32[]{:S(2)}, u32[]{:S(2)}) collective-permute-start(f32[4,8]{1,0:T(4,128)S(1)} %shard_map.162), channel_id=1, source_target_pairs={{0,12},{4,8},{8,4},{12,0},{1,13},{5,9},{9,5},{13,1},{2,14},{6,10},... | collective-permute-start | bytes 392 | tf_op jit(solution)/shard_map/ppermute | solution.py:549
  (21 other events, 54.8 us)

commit v14 on v11

--- a/solution.py
+++ b/solution.py
@@ -580,7 +580,7 @@
     )
 
     q_blocks = last_hops(*q_hops[:2], after(q_hops[2], own_in_out))
-    a_hops = first_hops(after(t_outgrad[:cut], q_hops[2], far_gate, weight_sib))
+    a_hops = first_hops(after(t_outgrad[:cut], q_hops[2], far_gate))
     far_up = to_chip(after(t_up[cut:], far_gate))
     q_send = after(crossing_pair(*q_blocks), far_up)
     q_far = to_chip(q_send)
@@ -595,33 +595,27 @@
     )
     q_returned = to_chip(after(q_far_sum, a_far))
     b_blocks = last_hops(*b_hops[:2], after(b_hops[2], q_far_sum))
-    b_send = crossing_pair(*b_blocks)
+    a_near_sum, a_far_sum = partial_sums(flags, a_blocks, a_far, weight_own, weight_sib)
+    b_send = crossing_pair(*b_blocks[:5], after(b_blocks[5], a_far_sum))
     b_far = to_chip(b_send)
-    a_near_sum, a_far_sum = partial_sums(
-        flags, a_blocks, after(a_far, b_send), weight_own, weight_sib
-    )
     in_out = own_in_out + outer(after(own_in_out, b_send))
-    a_returned = to_chip(a_far_sum)
     q_gradient = finished_sides(
-        q_near_sum, after(q_returned, a_far_sum), q_gate, q_up, proj_gate, proj_up
-    )
-    q_sums = jnp.concatenate([q_gradient, hidden[2 * cut :]], axis=1)
+        q_near_sum, after(q_returned, b_send), q_gate, q_up, proj_gate, proj_up
+    )
+    q_sums = jnp.concatenate([after(q_gradient, in_out), hidden[2 * cut :]], axis=1)
     q_sums = q_sums + outer(q_sums)
-    b_near, b_away = lent_sides(
-        after(flags, q_sums, in_out), b_blocks, b_far, weight_own, weight_sib, gates, ups,
-        proj_gate, proj_up,
-    )
-    in_out = in_out + after(across(in_out), b_near)
-    q_sums = q_sums + after(across(q_sums), b_near)
+    in_out = in_out + across(in_out)
+    q_sums = q_sums + across(q_sums)
     own_found = query_features(query_lengths, in_out[2 * cut :], q_sums)
     found = (own_found, to_core(own_found), to_chip(own_found), to_other(own_found))
-    b_far_sides = to_chip(b_away)
-    a_gradient = finished_sides(
-        a_near_sum, after(a_returned, b_far_sides), t_gate, t_up, proj_gate, proj_up
-    )
+    a_returned = to_chip(after(a_far_sum, b_far, *found))
+    b_near, b_away = lent_sides(
+        flags, b_blocks, b_far, weight_own, weight_sib, gates, ups, proj_gate, proj_up
+    )
+    a_gradient = finished_sides(a_near_sum, a_returned, t_gate, t_up, proj_gate, proj_up)
     own_scores = partial_scores(
         train_lengths, place, in_out[: 2 * cut], hidden[: 2 * cut], a_gradient, b_near,
-        b_far_sides, found,
+        to_chip(b_away), found,
     )
     scores = own_scores + outer(own_scores) + across(own_scores) + opposite(own_scores)
     return scores / (RANK * SEQ)

time: 216 us -> 208 us (0.963)
  waiting for transfers between devices: 76.9 us -> 63.7 us
  starting transfers between devices: 49.5 us -> 57.4 us
    ppermute x6, starting transfers between devices: 11.5 us -> 29.6 us  [first_hops(): return (own, outer(own), across(own))]
    ppermute x6, waiting for transfers between devices: 26.4 us -> 17.6 us  [first_hops(): return (own, outer(own), across(own))]
    ppermute x3, starting transfers between devices: 11.8 us -> 4.08 us  [last_hops(): return (own, one, mid, two, two, outer(after(two, one)))]
    ppermute x1, waiting for transfers between devices: 5.56 us -> 0.01 us  [moving_plan(): far_up = to_chip(after(t_up[cut:], far_gate))]
    ppermute x1, waiting for transfers between devices: 5.36 us -> 0.01 us  [moving_plan(): b_far = to_chip(b_send)]
    ppermute x1, waiting for transfers between devices: 0.01 us -> 5.3 us  [moving_plan(): to_other(own_found)]
    ppermute x3, waiting for transfers between devices: 22.3 us -> 17.6 us  [last_hops(): return (own, one, mid, two, two, outer(after(two, one)))]
    ppermute x1, starting transfers between devices: 4.8 us -> 1.56 us  [moving_plan(): outer(own_scores)]
  transfers between devices with their start and end apart: 31 -> 31, of which waited for: 15 -> 16; matrix products, arithmetic and copies ran while one was open for 4% -> 4% of each run, Pallas kernels for 29% -> 29%
where the time goes in v14:
time: 208 us; the launch traced here: 207 us
  waiting for transfers between devices  63.7 us (31%)
  Pallas kernels  62 us (30%)
  starting transfers between devices  57.4 us (28%)
  local copies, waits for them, and re-layouts  17.4 us (8%)
  other arithmetic  6.13 us (3%)
    ppermute x6, starting transfers between devices, first_hops(): return (own, outer(own), across(own))  29.6 us
    pallas_call x2, Pallas kernels, partial_sums(): pl.pallas_call(partial_kernel, grid=(units // TILE,), in_specs=[SCALARS]...  28.7 us
    pallas_call x1, Pallas kernels, lent_sides(): pl.pallas_call(lent_kernel, grid=(units // TILE,), in_specs=[SCALARS] + [...  18.3 us
    ppermute x3, waiting for transfers between devices, last_hops(): return (own, one, mid, two, two, outer(after(two, one)))  17.6 us
    ppermute x6, waiting for transfers between devices, first_hops(): return (own, outer(own), across(own))  17.6 us
    unnamed x84, local copies, waits for them, and re-layouts  13.9 us
    ppermute x1, waiting for transfers between devices, moving_plan(): in_out = in_out + across(in_out)  7.31 us
    ppermute x1, waiting for transfers between devices, moving_plan(): to_other(own_found)  5.3 us
  transfers between devices with their start and end apart: 31, of which 16 were waited for; matrix products, arithmetic and copies ran while one was open for 4% of the time, Pallas kernels for 29%

profile of v14, /device:TPU:0, one launch (start us, length us, event | category | flops | bytes accessed | tf_op | source)
XLA Modules:
  0.0 207.1 jit_solution(7753749994887196304)
XLA Ops:
  0.5 1.3 slice.40
  1.8 2.6 %collective-permute-start.1 = (bf16[128,3584]{1,0:T(8,128)(2,1)S(1)}, bf16[128,3584]{1,0:T(8,128)(2,1)S(1)}, u32[]{:S(2)}, u32[]{:S(2)}) collective-permute-start(bf16[128,3584]{1,0:T(8,128)(2,1)S(1)} %bitcast.46), channel_id=1, source_target_pairs={{0,2},{1,3},{2,0},{3,1},{4,6},{5,7},{6,4},{7,5},{8,10},{9,11},{10,... | collective-permute-start | bytes 2752520 | tf_op jit(solution)/shard_map/ppermute | solution.py:576
  4.4 2.6 %collective-permute-start = (bf16[128,2048]{1,0:T(8,128)(2,1)}, bf16[128,2048]{1,0:T(8,128)(2,1)}, u32[]{:S(2)}, u32[]{:S(2)}) collective-permute-start(bf16[128,2048]{1,0:T(8,128)(2,1)} %bitcast.4.q_outgrad.b0), channel_id=1, source_target_pairs={{0,8},{4,12},{8,0},{12,4},{1,9},{5,13},{9,1},{13,5},{2,10},{6,14},... | collective-permute-start | bytes 1572872 | tf_op jit(solution)/shard_map/ppermute | solution.py:559
  7.0 1.6 collective-permute-start.4
  8.6 1.5 copy-done.1
  10.1 1.2 copy-done.4
  11.3 1.2 copy-done.9
  12.5 1.2 copy-done.11
  13.7 1.2 copy-done.17
  18.8 4.9 %shard_map.154 = (f32[384,128]{1,0:T(8,128)S(1)}, f32[384,64]{1,0:T(8,128)S(1)}) custom-call(bf16[256,2048]{1,0:T(8,128)(2,1)S(1)} %bitcast.39, bf16[128,2048]{1,0:T(8,128)(2,1)S(1)} %bitcast.40, bf16[256,2048]{1,0:T(8,128)(2,1)S(1)} %bitcast.34, bf16[128,2048]{1,0:T(8,128)(2,1)} %bitcast.4.q_outgrad.b0, bf16[64,2048]{1,0:T(8,128)(2,1)S(1)} %copy-done.20, ...), custom_call_target="tpu_custom_call" | custom-call | flops 1024 | bytes 1024 | tf_op jit(solution)/shard_map/pallas_call | solution.py:396
  23.7 7.2 %collective-permute-done.b3.b4 = bf16[128,2048]{1,0:T(8,128)(2,1)} collective-permute-done((bf16[128,2048]{1,0:T(8,128)(2,1)}, bf16[128,2048]{1,0:T(8,128)(2,1)}, u32[]{:S(2)}, u32[]{:S(2)}) %collective-permute-start) | collective-permute-done | bytes 524320 | tf_op jit(solution)/shard_map/ppermute | solution.py:559
  31.0 1.9 collective-permute-start.6
  34.4 1.1 fusion.1
  35.6 10.1 %collective-permute-start.2 = (bf16[128,2048]{1,0:T(8,128)(2,1)}, bf16[128,2048]{1,0:T(8,128)(2,1)S(1)}, u32[]{:S(2)}, u32[]{:S(2)}) collective-permute-start(bf16[128,2048]{1,0:T(8,128)(2,1)} %bitcast.42), channel_id=1, source_target_pairs={{0,8},{4,12},{8,0},{12,4},{1,9},{5,13},{9,1},{13,5},{2,10},{6,14},... | collective-permute-start | bytes 1572872 | tf_op jit(solution)/shard_map/ppermute | solution.py:559
  45.7 11.6 %collective-permute-done.6.b5 = bf16[128,2048]{1,0:T(8,128)(2,1)} collective-permute-done((bf16[128,2048]{1,0:T(8,128)(2,1)}, bf16[128,2048]{1,0:T(8,128)(2,1)}, u32[]{:S(2)}, u32[]{:S(2)}) %collective-permute-start.6) | collective-permute-done | bytes 524320 | tf_op jit(solution)/shard_map/ppermute | solution.py:563
  57.2 1.5 select_bitcast_fusion.5
  59.6 6.3 %collective-permute-done.2.b3.b4 = bf16[128,2048]{1,0:T(8,128)(2,1)S(1)} collective-permute-done((bf16[128,2048]{1,0:T(8,128)(2,1)}, bf16[128,2048]{1,0:T(8,128)(2,1)S(1)}, u32[]{:S(2)}, u32[]{:S(2)}) %collective-permute-start.2) | collective-permute-done | bytes 524320 | tf_op jit(solution)/shard_map/ppermute | solution.py:559
  65.9 2.0 collective-permute-done.10.b1
  68.0 2.2 %collective-permute-start.11 = (bf16[128,2048]{1,0:T(8,128)(2,1)S(1)}, bf16[128,2048]{1,0:T(8,128)(2,1)S(1)}, u32[]{:S(2)}, u32[]{:S(2)}) collective-permute-start(bf16[128,2048]{1,0:T(8,128)(2,1)S(1)} %collective-permute-done.2.b3.b4), channel_id=1, source_target_pairs={{0,4},{4,0},{8,12},{12,8},{1,5},{5,1},{9,13},{13,9},{2,6},{6,2},{1... | collective-permute-start | bytes 1572872 | tf_op jit(solution)/shard_map/ppermute | solution.py:563
  70.2 1.7 collective-permute-start.3
  71.8 4.6 %shard_map.155 = (bf16[3584,256]{1,0:T(8,128)(2,1)S(1)}, bf16[3584,256]{1,0:T(8,128)(2,1)S(1)}) custom-call(bf16[256,3584]{1,0:T(8,128)(2,1)S(1)} %bitcast.29, bf16[256,3584]{1,0:T(8,128)(2,1)S(1)} %bitcast.32, bf16[128,3584]{1,0:T(8,128)(2,1)S(1)} %collective-permute-done.1.far_gate, bf16[128,3584]{1,0:T(8,128)(2,1)} %collective-permute-done.7.far_up), custom_call_target="tpu_custom_call" | custom-call | flops 1024 | bytes 1024 | tf_op jit(solution)/shard_map/pallas_call | solution.py:295
  76.5 6.0 %collective-permute-done.11.b5 = bf16[128,2048]{1,0:T(8,128)(2,1)S(1)} collective-permute-done((bf16[128,2048]{1,0:T(8,128)(2,1)S(1)}, bf16[128,2048]{1,0:T(8,128)(2,1)S(1)}, u32[]{:S(2)}, u32[]{:S(2)}) %collective-permute-start.11) | collective-permute-done | bytes 524320 | tf_op jit(solution)/shard_map/ppermute | solution.py:563
  82.8 1.3 pad_maximum_fusion.1
  84.6 13.6 %collective-permute-start.14 = (bf16[128,2048]{1,0:T(8,128)(2,1)}, bf16[128,2048]{1,0:T(8,128)(2,1)S(1)}, u32[]{:S(2)}, u32[]{:S(2)}) collective-permute-start(bf16[128,2048]{1,0:T(8,128)(2,1)} %bitcast.9.b0), channel_id=1, source_target_pairs={{0,4},{4,0},{8,12},{12,8},{1,5},{5,1},{9,13},{13,9},{2,6},{6,2},{1... | collective-permute-start | bytes 1572872 | tf_op jit(solution)/shard_map/ppermute | solution.py:559
  98.9 14.4 %shard_map.156 = (f32[3584,128]{1,0:T(8,128)}, bf16[3584,128]{1,0:T(8,128)(2,1)}) custom-call(s32[2]{0:T(128)} %pad_add_fusion.flags, bf16[128,2048]{1,0:T(8,128)(2,1)} %bitcast.4.q_outgrad.b0, bf16[128,2048]{1,0:T(8,128)(2,1)} %copy-done.33, bf16[128,2048]{1,0:T(8,128)(2,1)} %collective-permute-done.5.b2, bf16[128,2048]{1,0:T(8,128)(2,1)} %collective-permute-done.b3.b4, ...), custom_call_target="tpu_custom_call" | custom-call | flops 1024 | bytes 1024 | tf_op jit(solution)/shard_map/pallas_call | solution.py:241
  113.3 2.0 collective-permute-done.14.b1
  115.8 14.4 %shard_map.157 = (f32[3584,128]{1,0:T(8,128)}, bf16[3584,128]{1,0:T(8,128)(2,1)}) custom-call(s32[2]{0:T(128)} %pad_add_fusion.flags, bf16[128,2048]{1,0:T(8,128)(2,1)} %bitcast.43, bf16[128,2048]{1,0:T(8,128)(2,1)} %copy-done.35, bf16[128,2048]{1,0:T(8,128)(2,1)} %copy-done.39, bf16[128,2048]{1,0:T(8,128)(2,1)} %copy-done.31, bf16[128,2048]{1,0:T(8,128)(2,1)} %copy-done.31, ...), custom_call_target="tpu_custom_call" | custom-call | flops 1024 | bytes 1024 | tf_op jit(solution)/shard_map/pallas_call | solution.py:241
  130.3 1.6 select_bitcast_fusion.1
  132.0 1.7 collective-permute-start.19
  133.7 4.0 %collective-permute-start.17 = (f32[384,128]{1,0:T(8,128)S(1)}, f32[384,128]{1,0:T(8,128)S(1)}, u32[]{:S(2)}, u32[]{:S(2)}) collective-permute-start(f32[384,128]{1,0:T(8,128)S(1)} %get-tuple-element.56), channel_id=1, source_target_pairs={{0,4},{4,0},{8,12},{12,8},{1,5},{5,1},{9,13},{13,9},{2,6},{6,2},{1... | collective-permute-start | bytes 589832 | tf_op jit(solution)/shard_map/ppermute | solution.py:601
  137.7 3.6 %collective-permute-done.17 = f32[384,128]{1,0:T(8,128)S(1)} collective-permute-done((f32[384,128]{1,0:T(8,128)S(1)}, f32[384,128]{1,0:T(8,128)S(1)}, u32[]{:S(2)}, u32[]{:S(2)}) %collective-permute-start.17) | collective-permute-done | bytes 196640 | tf_op jit(solution)/shard_map/ppermute | solution.py:601
  141.5 1.6 shard_map.158
  143.1 2.3 %collective-permute-start.21 = (f32[128,192]{1,0:T(8,128)S(1)}, f32[128,192]{1,0:T(8,128)S(1)}, u32[]{:S(2)}, u32[]{:S(2)}) collective-permute-start(f32[128,192]{1,0:T(8,128)S(1)} %pad_maximum_fusion.3), channel_id=1, source_target_pairs={{0,4},{4,0},{8,12},{12,8},{1,5},{5,1},{9,13},{13,9},{2,6},{6,2},{1... | collective-permute-start | bytes 294920 | tf_op jit(solution)/shard_map/ppermute | solution.py:606
  145.5 3.5 %collective-permute-done.21 = f32[128,192]{1,0:T(8,128)S(1)} collective-permute-done((f32[128,192]{1,0:T(8,128)S(1)}, f32[128,192]{1,0:T(8,128)S(1)}, u32[]{:S(2)}, u32[]{:S(2)}) %collective-permute-start.21) | collective-permute-done | bytes 98336 | tf_op jit(solution)/shard_map/ppermute | solution.py:606
  149.1 1.4 collective-permute-start.22
  150.5 7.3 %collective-permute-done.18 = f32[384,128]{1,0:T(8,128)S(1)} collective-permute-done((f32[384,128]{1,0:T(8,128)S(1)}, f32[384,128]{1,0:T(8,128)S(1)}, u32[]{:S(2)}, u32[]{:S(2)}) %collective-permute-start.18) | collective-permute-done | bytes 196640 | tf_op jit(solution)/shard_map/ppermute | solution.py:607
  157.8 1.4 collective-permute-done.22
  162.0 5.3 %collective-permute-done.25.q3 = f32[2,192,64]{2,1,0:T(8,128)S(1)} collective-permute-done((f32[2,192,64]{2,1,0:T(8,128)S(1)}, f32[2,192,64]{2,1,0:T(8,128)S(1)}, u32[]{:S(2)}, u32[]{:S(2)}) %collective-permute-start.25) | collective-permute-done | bytes 98336 | tf_op jit(solution)/shard_map/ppermute | solution.py:610
  168.0 2.1 %collective-permute-done.24.q2 = f32[2,192,64]{2,1,0:T(8,128)S(1)} collective-permute-done((f32[2,192,64]{2,1,0:T(8,128)S(1)}, f32[2,192,64]{2,1,0:T(8,128)S(1)}, u32[]{:S(2)}, u32[]{:S(2)}) %collective-permute-start.24) | collective-permute-done | bytes 98336 | tf_op jit(solution)/shard_map/ppermute | solution.py:610
  171.5 1.9 collective-permute-start.26
  173.4 18.3 %shard_map.161 = (f32[128,128]{1,0:T(8,128)}, f32[128,128]{1,0:T(8,128)}) custom-call(s32[2]{0:T(128)} %pad_add_fusion.flags, bf16[128,2048]{1,0:T(8,128)(2,1)} %bitcast.9.b0, bf16[128,2048]{1,0:T(8,128)(2,1)} %copy-done.34, bf16[128,2048]{1,0:T(8,128)(2,1)} %copy-done.37, bf16[128,2048]{1,0:T(8,128)(2,1)} %collective-permute-done.3.b3.b4, ...), custom_call_target="tpu_custom_call" | custom-call | flops 1024 | bytes 1024 | tf_op jit(solution)/shard_map/pallas_call | solution.py:337
  192.3 2.3 %collective-permute-done.26.returned = bf16[3584,128]{1,0:T(8,128)(2,1)S(1)} collective-permute-done((bf16[3584,128]{1,0:T(8,128)(2,1)}, bf16[3584,128]{1,0:T(8,128)(2,1)S(1)}, u32[]{:S(2)}, u32[]{:S(2)}) %collective-permute-start.26) | collective-permute-done | bytes 917536 | tf_op jit(solution)/shard_map/ppermute | solution.py:611
  194.6 1.5 copy-done.13
  196.1 1.6 shard_map.160.early
  197.7 1.4 shard_map.162
  199.1 2.9 %collective-permute-start.30 = (f32[4,8]{1,0:T(4,128)S(1)}, f32[4,8]{1,0:T(4,128)S(1)}, u32[]{:S(2)}, u32[]{:S(2)}) collective-permute-start(f32[4,8]{1,0:T(4,128)S(1)} %shard_map.162), channel_id=1, source_target_pairs={{0,12},{4,8},{8,4},{12,0},{1,13},{5,9},{9,5},{13,1},{2,14},{6,10},... | collective-permute-start | bytes 392 | tf_op jit(solution)/shard_map/ppermute | solution.py:620
  202.0 1.6 collective-permute-start.28
  204.6 1.9 collective-permute-done.29
  (127 shorter events, 16.4 us)
Async XLA Ops:
  0.0 8.6 %copy-start = (bf16[4,64,3584]{2,1,0:T(8,128)(2,1)S(1)}, bf16[4,64,3584]{2,1,0:T(8,128)(2,1)}, u32[]{:S(2)}) copy-start(bf16[4,64,3584]{2,1,0:T(8,128)(2,1)} %param.17) | copy-start | bytes 5505028
  0.0 98.9 %collective-permute-start.12 = (bf16[3584,2048]{1,0:T(8,128)(2,1)}, bf16[3584,2048]{1,0:T(8,128)(2,1)}, u32[]{:S(2)}, u32[]{:S(2)}) collective-permute-start(bf16[3584,2048]{1,0:T(8,128)(2,1)} %weight_own.5), channel_id=1, source_target_pairs={{0,1},{1,0},{2,3},{3,2},{4,5},{5,4},{6,7},{7,6},{8,9},{9,8},{10,11... | collective-permute-start | bytes 44040200 | tf_op jit(solution)/shard_map/ppermute | solution.py:574
  1.8 32.0 %collective-permute-start.1 = (bf16[128,3584]{1,0:T(8,128)(2,1)S(1)}, bf16[128,3584]{1,0:T(8,128)(2,1)S(1)}, u32[]{:S(2)}, u32[]{:S(2)}) collective-permute-start(bf16[128,3584]{1,0:T(8,128)(2,1)S(1)} %bitcast.46), channel_id=1, source_target_pairs={{0,2},{1,3},{2,0},{3,1},{4,6},{5,7},{6,4},{7,5},{8,10},{9,11},{10,... | collective-permute-start | bytes 2752520 | tf_op jit(solution)/shard_map/ppermute | solution.py:576
  4.4 26.5 %collective-permute-start = (bf16[128,2048]{1,0:T(8,128)(2,1)}, bf16[128,2048]{1,0:T(8,128)(2,1)}, u32[]{:S(2)}, u32[]{:S(2)}) collective-permute-start(bf16[128,2048]{1,0:T(8,128)(2,1)} %bitcast.4.q_outgrad.b0), channel_id=1, source_target_pairs={{0,8},{4,12},{8,0},{12,4},{1,9},{5,13},{9,1},{13,5},{2,10},{6,14},... | collective-permute-start | bytes 1572872 | tf_op jit(solution)/shard_map/ppermute | solution.py:559
  7.0 24.0 %collective-permute-start.4 = (bf16[128,2048]{1,0:T(8,128)(2,1)}, bf16[128,2048]{1,0:T(8,128)(2,1)S(1)}, u32[]{:S(2)}, u32[]{:S(2)}) collective-permute-start(bf16[128,2048]{1,0:T(8,128)(2,1)} %bitcast.4.q_outgrad.b0), channel_id=1, source_target_pairs={{0,4},{4,0},{8,12},{12,8},{1,5},{5,1},{9,13},{13,9},{2,6},{6,2},{1... | collective-permute-start | bytes 1572872 | tf_op jit(solution)/shard_map/ppermute | solution.py:559
  31.0 4.6 %collective-permute-start.5 = (bf16[128,2048]{1,0:T(8,128)(2,1)}, bf16[128,2048]{1,0:T(8,128)(2,1)}, u32[]{:S(2)}, u32[]{:S(2)}) collective-permute-start(bf16[128,2048]{1,0:T(8,128)(2,1)} %bitcast.4.q_outgrad.b0), channel_id=1, source_target_pairs={{0,1},{1,0},{2,3},{3,2},{4,8},{5,9},{6,10},{7,11},{8,4},{9,5},{10,... | collective-permute-start | bytes 1572872 | tf_op jit(solution)/shard_map/ppermute | solution.py:562
  31.0 26.3 %collective-permute-start.6 = (bf16[128,2048]{1,0:T(8,128)(2,1)}, bf16[128,2048]{1,0:T(8,128)(2,1)}, u32[]{:S(2)}, u32[]{:S(2)}) collective-permute-start(bf16[128,2048]{1,0:T(8,128)(2,1)} %collective-permute-done.b3.b4), channel_id=1, source_target_pairs={{0,4},{4,0},{8,12},{12,8},{1,5},{5,1},{9,13},{13,9},{2,6},{6,2},{1... | collective-permute-start | bytes 1572872 | tf_op jit(solution)/shard_map/ppermute | solution.py:563
  33.8 25.1 %collective-permute-start.7 = (bf16[128,3584]{1,0:T(8,128)(2,1)}, bf16[128,3584]{1,0:T(8,128)(2,1)}, u32[]{:S(2)}, u32[]{:S(2)}) collective-permute-start(bf16[128,3584]{1,0:T(8,128)(2,1)} %bitcast.16), channel_id=1, source_target_pairs={{0,2},{1,3},{2,0},{3,1},{4,6},{5,7},{6,4},{7,5},{8,10},{9,11},{10,... | collective-permute-start | bytes 2752520 | tf_op jit(solution)/shard_map/ppermute | solution.py:584
  35.5 32.5 %collective-permute-start.10 = (bf16[128,2048]{1,0:T(8,128)(2,1)}, bf16[128,2048]{1,0:T(8,128)(2,1)S(1)}, u32[]{:S(2)}, u32[]{:S(2)}) collective-permute-start(bf16[128,2048]{1,0:T(8,128)(2,1)} %bitcast.41), channel_id=1, source_target_pairs={{0,4},{4,0},{8,12},{12,8},{1,5},{5,1},{9,13},{13,9},{2,6},{6,2},{1... | collective-permute-start | bytes 1572872 | tf_op jit(solution)/shard_map/ppermute | solution.py:559
  35.6 30.4 %collective-permute-start.2 = (bf16[128,2048]{1,0:T(8,128)(2,1)}, bf16[128,2048]{1,0:T(8,128)(2,1)S(1)}, u32[]{:S(2)}, u32[]{:S(2)}) collective-permute-start(bf16[128,2048]{1,0:T(8,128)(2,1)} %bitcast.42), channel_id=1, source_target_pairs={{0,8},{4,12},{8,0},{12,4},{1,9},{5,13},{9,1},{13,5},{2,10},{6,14},... | collective-permute-start | bytes 1572872 | tf_op jit(solution)/shard_map/ppermute | solution.py:559
  57.2 12.9 %copy-start.32 = (bf16[2,64,2048]{2,1,0:T(8,128)(2,1)S(1)}, bf16[2,64,2048]{2,1,0:T(8,128)(2,1)}, u32[]{:S(2)}) copy-start(bf16[2,64,2048]{2,1,0:T(8,128)(2,1)} %get-tuple-element.67) | copy-start | bytes 1572868
  58.8 13.1 %copy-start.2 = (bf16[4,64,3584]{2,1,0:T(8,128)(2,1)S(1)}, bf16[4,64,3584]{2,1,0:T(8,128)(2,1)}, u32[]{:S(2)}) copy-start(bf16[4,64,3584]{2,1,0:T(8,128)(2,1)} %param.18) | copy-start | bytes 5505028
  58.9 23.6 %collective-permute-start.8 = (bf16[2,128,2048]{2,1,0:T(8,128)(2,1)S(1)}, bf16[2,128,2048]{2,1,0:T(8,128)(2,1)S(1)}, u32[]{:S(2)}, u32[]{:S(2)}) collective-permute-start(bf16[2,128,2048]{2,1,0:T(8,128)(2,1)S(1)} %pad_maximum_fusion), channel_id=1, source_target_pairs={{0,2},{1,3},{2,0},{3,1},{4,6},{5,7},{6,4},{7,5},{8,10},{9,11},{10,... | collective-permute-start | bytes 3145736 | tf_op jit(solution)/shard_map/ppermute | solution.py:586
  65.9 16.6 %copy-start.31 = (bf16[128,2048]{1,0:T(8,128)(2,1)}, bf16[128,2048]{1,0:T(8,128)(2,1)S(1)}, u32[]{:S(2)}) copy-start(bf16[128,2048]{1,0:T(8,128)(2,1)S(1)} %collective-permute-done.2.b3.b4) | copy-start | bytes 1572868
  68.0 14.6 %copy-start.35 = (bf16[128,2048]{1,0:T(8,128)(2,1)}, bf16[128,2048]{1,0:T(8,128)(2,1)S(1)}, u32[]{:S(2)}) copy-start(bf16[128,2048]{1,0:T(8,128)(2,1)S(1)} %collective-permute-done.10.b1) | copy-start | bytes 1572868
  68.0 14.6 %collective-permute-start.11 = (bf16[128,2048]{1,0:T(8,128)(2,1)S(1)}, bf16[128,2048]{1,0:T(8,128)(2,1)S(1)}, u32[]{:S(2)}, u32[]{:S(2)}) collective-permute-start(bf16[128,2048]{1,0:T(8,128)(2,1)S(1)} %collective-permute-done.2.b3.b4), channel_id=1, source_target_pairs={{0,4},{4,0},{8,12},{12,8},{1,5},{5,1},{9,13},{13,9},{2,6},{6,2},{1... | collective-permute-start | bytes 1572872 | tf_op jit(solution)/shard_map/ppermute | solution.py:563
  70.2 12.4 %collective-permute-start.9 = (bf16[128,2048]{1,0:T(8,128)(2,1)S(1)}, bf16[128,2048]{1,0:T(8,128)(2,1)S(1)}, u32[]{:S(2)}, u32[]{:S(2)}) collective-permute-start(bf16[128,2048]{1,0:T(8,128)(2,1)S(1)} %bitcast.44), channel_id=1, source_target_pairs={{0,1},{1,0},{2,3},{3,2},{4,8},{5,9},{6,10},{7,11},{8,4},{9,5},{10,... | collective-permute-start | bytes 1572872 | tf_op jit(solution)/shard_map/ppermute | solution.py:562
  70.2 43.1 %collective-permute-start.3 = (bf16[128,2048]{1,0:T(8,128)(2,1)}, bf16[128,2048]{1,0:T(8,128)(2,1)}, u32[]{:S(2)}, u32[]{:S(2)}) collective-permute-start(bf16[128,2048]{1,0:T(8,128)(2,1)} %bitcast.9.b0), channel_id=1, source_target_pairs={{0,8},{4,12},{8,0},{12,4},{1,9},{5,13},{9,1},{13,5},{2,10},{6,14},... | collective-permute-start | bytes 1572872 | tf_op jit(solution)/shard_map/ppermute | solution.py:559
  76.5 6.3 %copy-start.14 = (bf16[3584,256]{1,0:T(8,128)(2,1)}, bf16[3584,256]{1,0:T(8,128)(2,1)S(1)}, u32[]{:S(2)}) copy-start(bf16[3584,256]{1,0:T(8,128)(2,1)S(1)} %get-tuple-element.47.gates) | copy-start | bytes 5505028
  76.5 6.3 %copy-start.15 = (bf16[3584,256]{1,0:T(8,128)(2,1)}, bf16[3584,256]{1,0:T(8,128)(2,1)S(1)}, u32[]{:S(2)}) copy-start(bf16[3584,256]{1,0:T(8,128)(2,1)S(1)} %get-tuple-element.64.ups) | copy-start | bytes 5505028
  84.1 31.1 %collective-permute-start.16 = (bf16[2,128,2048]{2,1,0:T(8,128)(2,1)}, bf16[2,128,2048]{2,1,0:T(8,128)(2,1)}, u32[]{:S(2)}, u32[]{:S(2)}) collective-permute-start(bf16[2,128,2048]{2,1,0:T(8,128)(2,1)} %pad_maximum_fusion.1), channel_id=1, source_target_pairs={{0,2},{1,3},{2,0},{3,1},{4,6},{5,7},{6,4},{7,5},{8,10},{9,11},{10,... | collective-permute-start | bytes 3145736 | tf_op jit(solution)/shard_map/ppermute | solution.py:592
  84.6 30.6 %collective-permute-start.14 = (bf16[128,2048]{1,0:T(8,128)(2,1)}, bf16[128,2048]{1,0:T(8,128)(2,1)S(1)}, u32[]{:S(2)}, u32[]{:S(2)}) collective-permute-start(bf16[128,2048]{1,0:T(8,128)(2,1)} %bitcast.9.b0), channel_id=1, source_target_pairs={{0,4},{4,0},{8,12},{12,8},{1,5},{5,1},{9,13},{13,9},{2,6},{6,2},{1... | collective-permute-start | bytes 1572872 | tf_op jit(solution)/shard_map/ppermute | solution.py:559
  115.2 15.0 %copy-start.34 = (bf16[128,2048]{1,0:T(8,128)(2,1)}, bf16[128,2048]{1,0:T(8,128)(2,1)S(1)}, u32[]{:S(2)}) copy-start(bf16[128,2048]{1,0:T(8,128)(2,1)S(1)} %collective-permute-done.14.b1) | copy-start | bytes 1572868
  115.2 15.0 %collective-permute-start.15 = (bf16[128,2048]{1,0:T(8,128)(2,1)}, bf16[128,2048]{1,0:T(8,128)(2,1)S(1)}, u32[]{:S(2)}, u32[]{:S(2)}) collective-permute-start(bf16[128,2048]{1,0:T(8,128)(2,1)} %collective-permute-done.3.b3.b4), channel_id=1, source_target_pairs={{0,4},{4,0},{8,12},{12,8},{1,5},{5,1},{9,13},{13,9},{2,6},{6,2},{1... | collective-permute-start | bytes 1572872 | tf_op jit(solution)/shard_map/ppermute | solution.py:563
  115.2 15.0 %collective-permute-start.13 = (bf16[128,2048]{1,0:T(8,128)(2,1)}, bf16[128,2048]{1,0:T(8,128)(2,1)S(1)}, u32[]{:S(2)}, u32[]{:S(2)}) collective-permute-start(bf16[128,2048]{1,0:T(8,128)(2,1)} %bitcast.9.b0), channel_id=1, source_target_pairs={{0,1},{1,0},{2,3},{3,2},{4,8},{5,9},{6,10},{7,11},{8,4},{9,5},{10,... | collective-permute-start | bytes 1572872 | tf_op jit(solution)/shard_map/ppermute | solution.py:562
  115.2 26.2 %collective-permute-start.20 = (bf16[3584,128]{1,0:T(8,128)(2,1)}, bf16[3584,128]{1,0:T(8,128)(2,1)S(1)}, u32[]{:S(2)}, u32[]{:S(2)}) collective-permute-start(bf16[3584,128]{1,0:T(8,128)(2,1)} %get-tuple-element.60), channel_id=1, source_target_pairs={{0,2},{1,3},{2,0},{3,1},{4,6},{5,7},{6,4},{7,5},{8,10},{9,11},{10,... | collective-permute-start | bytes 2752520 | tf_op jit(solution)/shard_map/ppermute | solution.py:596
  130.3 11.1 %copy-start.16 = (f32[3584,128]{1,0:T(8,128)S(1)}, f32[3584,128]{1,0:T(8,128)}, u32[]{:S(2)}) copy-start(f32[3584,128]{1,0:T(8,128)} %get-tuple-element.59.near_sum) | copy-start | bytes 5505028
  131.9 9.6 %copy-start.5 = (bf16[64,3584]{1,0:T(8,128)(2,1)S(1)}, bf16[64,3584]{1,0:T(8,128)(2,1)}, u32[]{:S(2)}) copy-start(bf16[64,3584]{1,0:T(8,128)(2,1)} %proj_gate.5) | copy-start | bytes 1376260
  131.9 9.6 %copy-start.7 = (bf16[64,3584]{1,0:T(8,128)(2,1)S(1)}, bf16[64,3584]{1,0:T(8,128)(2,1)}, u32[]{:S(2)}) copy-start(bf16[64,3584]{1,0:T(8,128)(2,1)} %proj_up.5) | copy-start | bytes 1376260
  131.9 9.6 %copy-start.10 = (bf16[2,64,3584]{2,1,0:T(8,128)(2,1)S(1)}, bf16[2,64,3584]{2,1,0:T(8,128)(2,1)}, u32[]{:S(2)}) copy-start(bf16[2,64,3584]{2,1,0:T(8,128)(2,1)} %param.22) | copy-start | bytes 2752516
  131.9 9.6 %copy-start.12 = (bf16[2,64,3584]{2,1,0:T(8,128)(2,1)S(1)}, bf16[2,64,3584]{2,1,0:T(8,128)(2,1)}, u32[]{:S(2)}) copy-start(bf16[2,64,3584]{2,1,0:T(8,128)(2,1)} %param.23) | copy-start | bytes 2752516
  132.0 39.5 %collective-permute-start.19 = (bf16[2,128,2048]{2,1,0:T(8,128)(2,1)S(1)}, bf16[2,128,2048]{2,1,0:T(8,128)(2,1)S(1)}, u32[]{:S(2)}, u32[]{:S(2)}) collective-permute-start(bf16[2,128,2048]{2,1,0:T(8,128)(2,1)S(1)} %pad_maximum_fusion.2), channel_id=1, source_target_pairs={{0,2},{1,3},{2,0},{3,1},{4,6},{5,7},{6,4},{7,5},{8,10},{9,11},{10,... | collective-permute-start | bytes 3145736 | tf_op jit(solution)/shard_map/ppermute | solution.py:600
  133.7 7.6 %collective-permute-start.17 = (f32[384,128]{1,0:T(8,128)S(1)}, f32[384,128]{1,0:T(8,128)S(1)}, u32[]{:S(2)}, u32[]{:S(2)}) collective-permute-start(f32[384,128]{1,0:T(8,128)S(1)} %get-tuple-element.56), channel_id=1, source_target_pairs={{0,4},{4,0},{8,12},{12,8},{1,5},{5,1},{9,13},{13,9},{2,6},{6,2},{1... | collective-permute-start | bytes 589832 | tf_op jit(solution)/shard_map/ppermute | solution.py:601
  141.5 17.7 %copy-start.29 = (s32[2]{0:T(128)S(1)}, s32[2]{0:T(128)}, u32[]{:S(2)}) copy-start(s32[2]{0:T(128)} %lengths.2) | copy-start | bytes 28
  143.1 6.0 %collective-permute-start.21 = (f32[128,192]{1,0:T(8,128)S(1)}, f32[128,192]{1,0:T(8,128)S(1)}, u32[]{:S(2)}, u32[]{:S(2)}) collective-permute-start(f32[128,192]{1,0:T(8,128)S(1)} %pad_maximum_fusion.3), channel_id=1, source_target_pairs={{0,4},{4,0},{8,12},{12,8},{1,5},{5,1},{9,13},{13,9},{2,6},{6,2},{1... | collective-permute-start | bytes 294920 | tf_op jit(solution)/shard_map/ppermute | solution.py:606
  145.4 12.4 %collective-permute-start.18 = (f32[384,128]{1,0:T(8,128)S(1)}, f32[384,128]{1,0:T(8,128)S(1)}, u32[]{:S(2)}, u32[]{:S(2)}) collective-permute-start(f32[384,128]{1,0:T(8,128)S(1)} %add.32), channel_id=1, source_target_pairs={{0,8},{4,12},{8,0},{12,4},{1,9},{5,13},{9,1},{13,5},{2,10},{6,14},... | collective-permute-start | bytes 589832 | tf_op jit(solution)/shard_map/ppermute | solution.py:607
  149.1 10.1 %collective-permute-start.22 = (f32[128,192]{1,0:T(8,128)S(1)}, f32[128,192]{1,0:T(8,128)S(1)}, u32[]{:S(2)}, u32[]{:S(2)}) collective-permute-start(f32[128,192]{1,0:T(8,128)S(1)} %fusion), channel_id=1, source_target_pairs={{0,8},{4,12},{8,0},{12,4},{1,9},{5,13},{9,1},{13,5},{2,10},{6,14},... | collective-permute-start | bytes 294920 | tf_op jit(solution)/shard_map/ppermute | solution.py:608
  160.1 7.2 %collective-permute-start.25 = (f32[2,192,64]{2,1,0:T(8,128)S(1)}, f32[2,192,64]{2,1,0:T(8,128)S(1)}, u32[]{:S(2)}, u32[]{:S(2)}) collective-permute-start(f32[2,192,64]{2,1,0:T(8,128)S(1)} %shard_map.159.q0), channel_id=1, source_target_pairs={{0,3},{1,2},{2,1},{3,0},{4,7},{5,6},{6,5},{7,4},{8,11},{9,10},{10,... | collective-permute-start | bytes 294920 | tf_op jit(solution)/shard_map/ppermute | solution.py:610
  160.2 10.0 %collective-permute-start.24 = (f32[2,192,64]{2,1,0:T(8,128)S(1)}, f32[2,192,64]{2,1,0:T(8,128)S(1)}, u32[]{:S(2)}, u32[]{:S(2)}) collective-permute-start(f32[2,192,64]{2,1,0:T(8,128)S(1)} %shard_map.159.q0), channel_id=1, source_target_pairs={{0,2},{1,3},{2,0},{3,1},{4,6},{5,7},{6,4},{7,5},{8,10},{9,11},{10,... | collective-permute-start | bytes 294920 | tf_op jit(solution)/shard_map/ppermute | solution.py:610
  161.0 9.9 %collective-permute-start.23 = (f32[2,192,64]{2,1,0:T(8,128)S(1)}, f32[2,192,64]{2,1,0:T(8,128)S(1)}, u32[]{:S(2)}, u32[]{:S(2)}) collective-permute-start(f32[2,192,64]{2,1,0:T(8,128)S(1)} %shard_map.159.q0), channel_id=1, source_target_pairs={{0,1},{1,0},{2,3},{3,2},{4,5},{5,4},{6,7},{7,6},{8,9},{9,8},{10,11... | collective-permute-start | bytes 294920 | tf_op jit(solution)/shard_map/ppermute | solution.py:610
  171.5 23.0 %collective-permute-start.26 = (bf16[3584,128]{1,0:T(8,128)(2,1)}, bf16[3584,128]{1,0:T(8,128)(2,1)S(1)}, u32[]{:S(2)}, u32[]{:S(2)}) collective-permute-start(bf16[3584,128]{1,0:T(8,128)(2,1)} %get-tuple-element.63), channel_id=1, source_target_pairs={{0,2},{1,3},{2,0},{3,1},{4,6},{5,7},{6,4},{7,5},{8,10},{9,11},{10,... | collective-permute-start | bytes 2752520 | tf_op jit(solution)/shard_map/ppermute | solution.py:611
  173.4 21.1 %copy-start.3 = (bf16[4,64,3584]{2,1,0:T(8,128)(2,1)S(1)}, bf16[4,64,3584]{2,1,0:T(8,128)(2,1)}, u32[]{:S(2)}) copy-start(bf16[4,64,3584]{2,1,0:T(8,128)(2,1)} %param.18) | copy-start | bytes 5505028
  173.4 21.1 %copy-start.6 = (bf16[64,3584]{1,0:T(8,128)(2,1)S(1)}, bf16[64,3584]{1,0:T(8,128)(2,1)}, u32[]{:S(2)}) copy-start(bf16[64,3584]{1,0:T(8,128)(2,1)} %proj_gate.5) | copy-start | bytes 1376260
  173.4 21.1 %copy-start.8 = (bf16[64,3584]{1,0:T(8,128)(2,1)S(1)}, bf16[64,3584]{1,0:T(8,128)(2,1)}, u32[]{:S(2)}) copy-start(bf16[64,3584]{1,0:T(8,128)(2,1)} %proj_up.5) | copy-start | bytes 1376260
  191.7 5.9 %collective-permute-start.27 = (f32[128,128]{1,0:T(8,128)}, f32[128,128]{1,0:T(8,128)S(1)}, u32[]{:S(2)}, u32[]{:S(2)}) collective-permute-start(f32[128,128]{1,0:T(8,128)} %get-tuple-element.66), channel_id=1, source_target_pairs={{0,2},{1,3},{2,0},{3,1},{4,6},{5,7},{6,4},{7,5},{8,10},{9,11},{10,... | collective-permute-start | bytes 196616 | tf_op jit(solution)/shard_map/ppermute | solution.py:618
  199.1 5.4 %collective-permute-start.30 = (f32[4,8]{1,0:T(4,128)S(1)}, f32[4,8]{1,0:T(4,128)S(1)}, u32[]{:S(2)}, u32[]{:S(2)}) collective-permute-start(f32[4,8]{1,0:T(4,128)S(1)} %shard_map.162), channel_id=1, source_target_pairs={{0,12},{4,8},{8,4},{12,0},{1,13},{5,9},{9,5},{13,1},{2,14},{6,10},... | collective-permute-start | bytes 392 | tf_op jit(solution)/shard_map/ppermute | solution.py:620
  202.0 4.5 %collective-permute-start.29 = (f32[4,8]{1,0:T(4,128)S(1)}, f32[4,8]{1,0:T(4,128)S(1)}, u32[]{:S(2)}, u32[]{:S(2)}) collective-permute-start(f32[4,8]{1,0:T(4,128)S(1)} %shard_map.162), channel_id=1, source_target_pairs={{0,8},{4,12},{8,0},{12,4},{1,9},{5,13},{9,1},{13,5},{2,10},{6,14},... | collective-permute-start | bytes 392 | tf_op jit(solution)/shard_map/ppermute | solution.py:620
  202.0 4.5 %collective-permute-start.28 = (f32[4,8]{1,0:T(4,128)S(1)}, f32[4,8]{1,0:T(4,128)S(1)}, u32[]{:S(2)}, u32[]{:S(2)}) collective-permute-start(f32[4,8]{1,0:T(4,128)S(1)} %shard_map.162), channel_id=1, source_target_pairs={{0,4},{4,0},{8,12},{12,8},{1,5},{5,1},{9,13},{13,9},{2,6},{6,2},{1... | collective-permute-start | bytes 392 | tf_op jit(solution)/shard_map/ppermute | solution.py:620
  (25 other events, 37.4 us)

commit v15 on v11

--- a/solution.py
+++ b/solution.py
@@ -580,13 +580,13 @@
     )
 
     q_blocks = last_hops(*q_hops[:2], after(q_hops[2], own_in_out))
-    a_hops = first_hops(after(t_outgrad[:cut], q_hops[2], far_gate, weight_sib))
+    a_hops = first_hops(after(t_outgrad[:cut], q_hops[2], far_gate))
     far_up = to_chip(after(t_up[cut:], far_gate))
     q_send = after(crossing_pair(*q_blocks), far_up)
     q_far = to_chip(q_send)
     a_blocks = last_hops(*a_hops[:2], after(a_hops[2], q_send))
 
-    b_hops = first_hops(after(t_outgrad[cut:], a_hops[2]))
+    b_hops = first_hops(after(t_outgrad[cut:], a_blocks[2], a_blocks[5]))
     gates, ups = turned(t_gate, t_up, far_gate, far_up)
     a_send = crossing_pair(*a_blocks[:5], after(a_blocks[5], q_far, gates))
     a_far = to_chip(a_send)
@@ -600,8 +600,8 @@
     a_near_sum, a_far_sum = partial_sums(
         flags, a_blocks, after(a_far, b_send), weight_own, weight_sib
     )
+    a_returned = to_chip(a_far_sum)
     in_out = own_in_out + outer(after(own_in_out, b_send))
-    a_returned = to_chip(a_far_sum)
     q_gradient = finished_sides(
         q_near_sum, after(q_returned, a_far_sum), q_gate, q_up, proj_gate, proj_up
     )
@@ -611,17 +611,14 @@
         after(flags, q_sums, in_out), b_blocks, b_far, weight_own, weight_sib, gates, ups,
         proj_gate, proj_up,
     )
-    in_out = in_out + after(across(in_out), b_near)
-    q_sums = q_sums + after(across(q_sums), b_near)
+    in_out = in_out + across(after(in_out, b_near))
+    q_sums = q_sums + across(after(q_sums, b_near))
     own_found = query_features(query_lengths, in_out[2 * cut :], q_sums)
     found = (own_found, to_core(own_found), to_chip(own_found), to_other(own_found))
-    b_far_sides = to_chip(b_away)
-    a_gradient = finished_sides(
-        a_near_sum, after(a_returned, b_far_sides), t_gate, t_up, proj_gate, proj_up
-    )
+    a_gradient = finished_sides(a_near_sum, a_returned, t_gate, t_up, proj_gate, proj_up)
     own_scores = partial_scores(
         train_lengths, place, in_out[: 2 * cut], hidden[: 2 * cut], a_gradient, b_near,
-        b_far_sides, found,
+        to_chip(b_away), found,
     )
     scores = own_scores + outer(own_scores) + across(own_scores) + opposite(own_scores)
     return scores / (RANK * SEQ)

time: 216 us -> 212 us (0.981)
  starting transfers between devices: 49.5 us -> 42.9 us
  waiting for transfers between devices: 76.9 us -> 82.1 us
  local copies, waits for them, and re-layouts: 19.4 us -> 17.2 us
    ppermute x3, waiting for transfers between devices: 22.3 us -> 29.9 us  [last_hops(): return (own, one, mid, two, two, outer(after(two, one)))]
    ppermute x3, starting transfers between devices: 11.8 us -> 4.52 us  [last_hops(): return (own, one, mid, two, two, outer(after(two, one)))]
    ppermute x6, starting transfers between devices: 11.5 us -> 18.4 us  [first_hops(): return (own, outer(own), across(own))]
    ppermute x3, waiting for transfers between devices: 9.77 us -> 15.5 us  [the longest x1 9.73 us: moving_plan(): q_sums = q_sums + across(after(q_sums, b_near))]
    ppermute x1, waiting for transfers between devices: 5.56 us -> 0.01 us  [moving_plan(): far_up = to_chip(after(t_up[cut:], far_gate))]
    ppermute x6, waiting for transfers between devices: 26.4 us -> 21.9 us  [first_hops(): return (own, outer(own), across(own))]
    ppermute x1, starting transfers between devices: 4.8 us -> 1.99 us  [moving_plan(): outer(own_scores)]
    ppermute x1, waiting for transfers between devices: 2.66 us -> 0.06 us  [moving_plan(): in_out = own_in_out + outer(after(own_in_out, b_send))]
  transfers between devices with their start and end apart: 31 -> 31, of which waited for: 15 -> 16; matrix products, arithmetic and copies ran while one was open for 4% -> 4% of each run, Pallas kernels for 29% -> 29%
where the time goes in v15:
time: 212 us; the launch traced here: 211 us
  waiting for transfers between devices  82.1 us (39%)
  Pallas kernels  62.7 us (30%)
  starting transfers between devices  42.9 us (20%)
  local copies, waits for them, and re-layouts  17.2 us (8%)
  other arithmetic  5.48 us (3%)
    ppermute x3, waiting for transfers between devices, last_hops(): return (own, one, mid, two, two, outer(after(two, one)))  29.9 us
    pallas_call x2, Pallas kernels, partial_sums(): pl.pallas_call(partial_kernel, grid=(units // TILE,), in_specs=[SCALARS]...  28.7 us
    ppermute x6, waiting for transfers between devices, first_hops(): return (own, outer(own), across(own))  21.9 us
    ppermute x6, starting transfers between devices, first_hops(): return (own, outer(own), across(own))  18.4 us
    pallas_call x1, Pallas kernels, lent_sides(): pl.pallas_call(lent_kernel, grid=(units // TILE,), in_specs=[SCALARS] + [...  18.3 us
    unnamed x74, local copies, waits for them, and re-layouts  13.9 us
    ppermute x1, waiting for transfers between devices, moving_plan(): q_sums = q_sums + across(after(q_sums, b_near))  9.73 us
    ppermute x1, waiting for transfers between devices, moving_plan(): b_far = to_chip(b_send)  6.63 us
  transfers between devices with their start and end apart: 31, of which 16 were waited for; matrix products, arithmetic and copies ran while one was open for 4% of the time, Pallas kernels for 29%

profile of v15, /device:TPU:0, one launch (start us, length us, event | category | flops | bytes accessed | tf_op | source)
XLA Modules:
  0.0 210.8 jit_solution(11185414591079079256)
XLA Ops:
  0.5 1.3 slice.40
  1.8 2.6 %collective-permute-start.1 = (bf16[128,3584]{1,0:T(8,128)(2,1)S(1)}, bf16[128,3584]{1,0:T(8,128)(2,1)S(1)}, u32[]{:S(2)}, u32[]{:S(2)}) collective-permute-start(bf16[128,3584]{1,0:T(8,128)(2,1)S(1)} %bitcast.46), channel_id=1, source_target_pairs={{0,2},{1,3},{2,0},{3,1},{4,6},{5,7},{6,4},{7,5},{8,10},{9,11},{10,... | collective-permute-start | bytes 2752520 | tf_op jit(solution)/shard_map/ppermute | solution.py:576
  4.4 2.6 %collective-permute-start = (bf16[128,2048]{1,0:T(8,128)(2,1)}, bf16[128,2048]{1,0:T(8,128)(2,1)}, u32[]{:S(2)}, u32[]{:S(2)}) collective-permute-start(bf16[128,2048]{1,0:T(8,128)(2,1)} %bitcast.4.q_outgrad.b0), channel_id=1, source_target_pairs={{0,8},{4,12},{8,0},{12,4},{1,9},{5,13},{9,1},{13,5},{2,10},{6,14},... | collective-permute-start | bytes 1572872 | tf_op jit(solution)/shard_map/ppermute | solution.py:559
  7.0 1.6 collective-permute-start.4
  8.6 1.5 copy-done.1
  10.1 1.2 copy-done.4
  11.3 1.2 copy-done.9
  12.5 1.2 copy-done.11
  13.7 1.2 copy-done.17
  14.9 1.0 copy-done.18
  15.9 1.0 copy-done.19
  18.8 4.9 %shard_map.154 = (f32[384,128]{1,0:T(8,128)S(1)}, f32[384,64]{1,0:T(8,128)S(1)}) custom-call(bf16[256,2048]{1,0:T(8,128)(2,1)S(1)} %bitcast.39, bf16[128,2048]{1,0:T(8,128)(2,1)S(1)} %bitcast.40, bf16[256,2048]{1,0:T(8,128)(2,1)S(1)} %bitcast.34, bf16[128,2048]{1,0:T(8,128)(2,1)} %bitcast.4.q_outgrad.b0, bf16[64,2048]{1,0:T(8,128)(2,1)S(1)} %copy-done.20, ...), custom_call_target="tpu_custom_call" | custom-call | flops 1024 | bytes 1024 | tf_op jit(solution)/shard_map/pallas_call | solution.py:396
  23.7 7.1 %collective-permute-done.b3.b4 = bf16[128,2048]{1,0:T(8,128)(2,1)} collective-permute-done((bf16[128,2048]{1,0:T(8,128)(2,1)}, bf16[128,2048]{1,0:T(8,128)(2,1)}, u32[]{:S(2)}, u32[]{:S(2)}) %collective-permute-start) | collective-permute-done | bytes 524320 | tf_op jit(solution)/shard_map/ppermute | solution.py:559
  31.0 1.9 collective-permute-start.5
  32.8 1.0 slice.42
  35.4 10.3 %collective-permute-start.2 = (bf16[128,2048]{1,0:T(8,128)(2,1)S(1)}, bf16[128,2048]{1,0:T(8,128)(2,1)S(1)}, u32[]{:S(2)}, u32[]{:S(2)}) collective-permute-start(bf16[128,2048]{1,0:T(8,128)(2,1)S(1)} %bitcast.42), channel_id=1, source_target_pairs={{0,8},{4,12},{8,0},{12,4},{1,9},{5,13},{9,1},{13,5},{2,10},{6,14},... | collective-permute-start | bytes 1572872 | tf_op jit(solution)/shard_map/ppermute | solution.py:559
  45.7 11.6 %collective-permute-done.5.b5 = bf16[128,2048]{1,0:T(8,128)(2,1)} collective-permute-done((bf16[128,2048]{1,0:T(8,128)(2,1)}, bf16[128,2048]{1,0:T(8,128)(2,1)}, u32[]{:S(2)}, u32[]{:S(2)}) %collective-permute-start.5) | collective-permute-done | bytes 524320 | tf_op jit(solution)/shard_map/ppermute | solution.py:563
  57.2 1.5 select_bitcast_fusion.5
  59.5 6.3 %collective-permute-done.2.b3.b4 = bf16[128,2048]{1,0:T(8,128)(2,1)S(1)} collective-permute-done((bf16[128,2048]{1,0:T(8,128)(2,1)S(1)}, bf16[128,2048]{1,0:T(8,128)(2,1)S(1)}, u32[]{:S(2)}, u32[]{:S(2)}) %collective-permute-start.2) | collective-permute-done | bytes 524320 | tf_op jit(solution)/shard_map/ppermute | solution.py:559
  65.8 2.1 %collective-permute-done.8.b1 = bf16[128,2048]{1,0:T(8,128)(2,1)S(1)} collective-permute-done((bf16[128,2048]{1,0:T(8,128)(2,1)S(1)}, bf16[128,2048]{1,0:T(8,128)(2,1)S(1)}, u32[]{:S(2)}, u32[]{:S(2)}) %collective-permute-start.8) | collective-permute-done | bytes 524320 | tf_op jit(solution)/shard_map/ppermute | solution.py:559
  68.0 2.3 %collective-permute-start.9 = (bf16[128,2048]{1,0:T(8,128)(2,1)S(1)}, bf16[128,2048]{1,0:T(8,128)(2,1)S(1)}, u32[]{:S(2)}, u32[]{:S(2)}) collective-permute-start(bf16[128,2048]{1,0:T(8,128)(2,1)S(1)} %collective-permute-done.2.b3.b4), channel_id=1, source_target_pairs={{0,4},{4,0},{8,12},{12,8},{1,5},{5,1},{9,13},{13,9},{2,6},{6,2},{1... | collective-permute-start | bytes 1572872 | tf_op jit(solution)/shard_map/ppermute | solution.py:563
  70.2 4.6 %shard_map.155 = (bf16[3584,256]{1,0:T(8,128)(2,1)S(1)}, bf16[3584,256]{1,0:T(8,128)(2,1)S(1)}) custom-call(bf16[256,3584]{1,0:T(8,128)(2,1)S(1)} %bitcast.29, bf16[256,3584]{1,0:T(8,128)(2,1)S(1)} %bitcast.32, bf16[128,3584]{1,0:T(8,128)(2,1)S(1)} %collective-permute-done.1.far_gate, bf16[128,3584]{1,0:T(8,128)(2,1)} %collective-permute-done.6.far_up), custom_call_target="tpu_custom_call" | custom-call | flops 1024 | bytes 1024 | tf_op jit(solution)/shard_map/pallas_call | solution.py:295
  74.9 7.4 %collective-permute-done.9.b5 = bf16[128,2048]{1,0:T(8,128)(2,1)S(1)} collective-permute-done((bf16[128,2048]{1,0:T(8,128)(2,1)S(1)}, bf16[128,2048]{1,0:T(8,128)(2,1)S(1)}, u32[]{:S(2)}, u32[]{:S(2)}) %collective-permute-start.9) | collective-permute-done | bytes 524320 | tf_op jit(solution)/shard_map/ppermute | solution.py:563
  83.1 3.1 %collective-permute-start.10 = (bf16[128,2048]{1,0:T(8,128)(2,1)}, bf16[128,2048]{1,0:T(8,128)(2,1)S(1)}, u32[]{:S(2)}, u32[]{:S(2)}) collective-permute-start(bf16[128,2048]{1,0:T(8,128)(2,1)} %bitcast.9.b0), channel_id=1, source_target_pairs={{0,8},{4,12},{8,0},{12,4},{1,9},{5,13},{9,1},{13,5},{2,10},{6,14},... | collective-permute-start | bytes 1572872 | tf_op jit(solution)/shard_map/ppermute | solution.py:559
  86.4 1.2 pad_maximum_fusion.1
  88.7 14.3 %shard_map.156 = (f32[3584,128]{1,0:T(8,128)}, bf16[3584,128]{1,0:T(8,128)(2,1)}) custom-call(s32[2]{0:T(128)} %pad_add_fusion.flags, bf16[128,2048]{1,0:T(8,128)(2,1)} %bitcast.4.q_outgrad.b0, bf16[128,2048]{1,0:T(8,128)(2,1)} %copy-done.30, bf16[128,2048]{1,0:T(8,128)(2,1)} %collective-permute-done.3.b2, bf16[128,2048]{1,0:T(8,128)(2,1)} %collective-permute-done.b3.b4, ...), custom_call_target="tpu_custom_call" | custom-call | flops 1024 | bytes 1024 | tf_op jit(solution)/shard_map/pallas_call | solution.py:241
  103.0 6.2 %collective-permute-done.10.b3.b4 = bf16[128,2048]{1,0:T(8,128)(2,1)S(1)} collective-permute-done((bf16[128,2048]{1,0:T(8,128)(2,1)}, bf16[128,2048]{1,0:T(8,128)(2,1)S(1)}, u32[]{:S(2)}, u32[]{:S(2)}) %collective-permute-start.10) | collective-permute-done | bytes 524320 | tf_op jit(solution)/shard_map/ppermute | solution.py:559
  109.6 2.5 %collective-permute-done.17.far = bf16[2,128,2048]{2,1,0:T(8,128)(2,1)} collective-permute-done((bf16[2,128,2048]{2,1,0:T(8,128)(2,1)}, bf16[2,128,2048]{2,1,0:T(8,128)(2,1)}, u32[]{:S(2)}, u32[]{:S(2)}) %collective-permute-start.17) | collective-permute-done | bytes 1048608 | tf_op jit(solution)/shard_map/ppermute | solution.py:592
  112.6 10.9 %collective-permute-done.15.b5 = bf16[128,2048]{1,0:T(8,128)(2,1)S(1)} collective-permute-done((bf16[128,2048]{1,0:T(8,128)(2,1)S(1)}, bf16[128,2048]{1,0:T(8,128)(2,1)S(1)}, u32[]{:S(2)}, u32[]{:S(2)}) %collective-permute-start.15) | collective-permute-done | bytes 524320 | tf_op jit(solution)/shard_map/ppermute | solution.py:563
  124.4 1.1 pad_maximum_fusion.2
  125.5 1.4 collective-permute-start.20
  127.0 14.3 %shard_map.157 = (f32[3584,128]{1,0:T(8,128)}, bf16[3584,128]{1,0:T(8,128)(2,1)}) custom-call(s32[2]{0:T(128)} %pad_add_fusion.flags, bf16[128,2048]{1,0:T(8,128)(2,1)} %bitcast.45, bf16[128,2048]{1,0:T(8,128)(2,1)} %copy-done.31, bf16[128,2048]{1,0:T(8,128)(2,1)} %copy-done.32, bf16[128,2048]{1,0:T(8,128)(2,1)} %copy-done.28, bf16[128,2048]{1,0:T(8,128)(2,1)} %copy-done.28, ...), custom_call_target="tpu_custom_call" | custom-call | flops 1024 | bytes 1024 | tf_op jit(solution)/shard_map/pallas_call | solution.py:241
  142.6 1.5 copy-done.16
  144.1 2.4 %shard_map.158 = f32[128,128]{1,0:T(8,128)S(1)} custom-call(f32[3584,128]{1,0:T(8,128)S(1)} %copy-done.16, bf16[3584,128]{1,0:T(8,128)(2,1)} %collective-permute-done.18.returned, bf16[128,3584]{1,0:T(8,128)(2,1)S(1)} %bitcast.36, bf16[128,3584]{1,0:T(8,128)(2,1)S(1)} %bitcast.38, bf16[64,3584]{1,0:T(8,128)(2,1)S(1)} %copy-done.5, bf16[64,3584]{1,0:T(8,128)(2,1)S(1)} %copy-done.7), custom_call_target="tpu_custom_call" | custom-call | flops 1024 | bytes 1024 | tf_op jit(solution)/shard_map/pallas_call | solution.py:268
  146.5 1.8 collective-permute-start.19
  148.4 3.1 %collective-permute-done.19 = f32[128,192]{1,0:T(8,128)S(1)} collective-permute-done((f32[128,192]{1,0:T(8,128)S(1)}, f32[128,192]{1,0:T(8,128)S(1)}, u32[]{:S(2)}, u32[]{:S(2)}) %collective-permute-start.19) | collective-permute-done | bytes 98336 | tf_op jit(solution)/shard_map/ppermute | solution.py:609
  151.6 6.6 %collective-permute-done.20.far = bf16[2,128,2048]{2,1,0:T(8,128)(2,1)} collective-permute-done((bf16[2,128,2048]{2,1,0:T(8,128)(2,1)}, bf16[2,128,2048]{2,1,0:T(8,128)(2,1)}, u32[]{:S(2)}, u32[]{:S(2)}) %collective-permute-start.20) | collective-permute-done | bytes 1048608 | tf_op jit(solution)/shard_map/ppermute | solution.py:599
  158.2 18.3 %shard_map.159 = (f32[128,128]{1,0:T(8,128)}, f32[128,128]{1,0:T(8,128)}) custom-call(s32[2]{0:T(128)} %pad_add_fusion.flags, bf16[128,2048]{1,0:T(8,128)(2,1)} %bitcast.9.b0, bf16[128,2048]{1,0:T(8,128)(2,1)} %collective-permute-done.14.b1, bf16[128,2048]{1,0:T(8,128)(2,1)} %copy-done.34, bf16[128,2048]{1,0:T(8,128)(2,1)} %copy-done.27, ...), custom_call_target="tpu_custom_call" | custom-call | flops 1024 | bytes 1024 | tf_op jit(solution)/shard_map/pallas_call | solution.py:337
  176.6 2.9 %collective-permute-start.24 = (f32[128,192]{1,0:T(8,128)S(1)}, f32[128,192]{1,0:T(8,128)S(1)}, u32[]{:S(2)}, u32[]{:S(2)}) collective-permute-start(f32[128,192]{1,0:T(8,128)S(1)} %fusion), channel_id=1, source_target_pairs={{0,8},{4,12},{8,0},{12,4},{1,9},{5,13},{9,1},{13,5},{2,10},{6,14},... | collective-permute-start | bytes 294920 | tf_op jit(solution)/shard_map/ppermute | solution.py:615
  179.5 9.7 %collective-permute-done.24 = f32[128,192]{1,0:T(8,128)S(1)} collective-permute-done((f32[128,192]{1,0:T(8,128)S(1)}, f32[128,192]{1,0:T(8,128)S(1)}, u32[]{:S(2)}, u32[]{:S(2)}) %collective-permute-start.24) | collective-permute-done | bytes 98336 | tf_op jit(solution)/shard_map/ppermute | solution.py:615
  193.0 1.5 copy-done.13
  194.5 1.6 shard_map.160.early
  196.1 5.8 %collective-permute-done.23.far = f32[128,128]{1,0:T(8,128)S(1)} collective-permute-done((f32[128,128]{1,0:T(8,128)}, f32[128,128]{1,0:T(8,128)S(1)}, u32[]{:S(2)}, u32[]{:S(2)}) %collective-permute-start.23) | collective-permute-done | bytes 65568 | tf_op jit(solution)/shard_map/ppermute | solution.py:621
  201.9 1.4 shard_map.162
  203.3 2.5 %collective-permute-start.30 = (f32[4,8]{1,0:T(4,128)S(1)}, f32[4,8]{1,0:T(4,128)S(1)}, u32[]{:S(2)}, u32[]{:S(2)}) collective-permute-start(f32[4,8]{1,0:T(4,128)S(1)} %shard_map.162), channel_id=1, source_target_pairs={{0,12},{4,8},{8,4},{12,0},{1,13},{5,9},{9,5},{13,1},{2,14},{6,10},... | collective-permute-start | bytes 392 | tf_op jit(solution)/shard_map/ppermute | solution.py:623
  205.8 2.0 collective-permute-start.28
  207.8 1.0 collective-permute-done.30
  208.7 1.5 collective-permute-done.29
  (117 shorter events, 14.4 us)
Async XLA Ops:
  0.0 88.7 %collective-permute-start.12 = (bf16[3584,2048]{1,0:T(8,128)(2,1)}, bf16[3584,2048]{1,0:T(8,128)(2,1)}, u32[]{:S(2)}, u32[]{:S(2)}) collective-permute-start(bf16[3584,2048]{1,0:T(8,128)(2,1)} %weight_own.5), channel_id=1, source_target_pairs={{0,1},{1,0},{2,3},{3,2},{4,5},{5,4},{6,7},{7,6},{8,9},{9,8},{10,11... | collective-permute-start | bytes 44040200 | tf_op jit(solution)/shard_map/ppermute | solution.py:574
  1.8 32.0 %collective-permute-start.1 = (bf16[128,3584]{1,0:T(8,128)(2,1)S(1)}, bf16[128,3584]{1,0:T(8,128)(2,1)S(1)}, u32[]{:S(2)}, u32[]{:S(2)}) collective-permute-start(bf16[128,3584]{1,0:T(8,128)(2,1)S(1)} %bitcast.46), channel_id=1, source_target_pairs={{0,2},{1,3},{2,0},{3,1},{4,6},{5,7},{6,4},{7,5},{8,10},{9,11},{10,... | collective-permute-start | bytes 2752520 | tf_op jit(solution)/shard_map/ppermute | solution.py:576
  4.4 26.5 %collective-permute-start = (bf16[128,2048]{1,0:T(8,128)(2,1)}, bf16[128,2048]{1,0:T(8,128)(2,1)}, u32[]{:S(2)}, u32[]{:S(2)}) collective-permute-start(bf16[128,2048]{1,0:T(8,128)(2,1)} %bitcast.4.q_outgrad.b0), channel_id=1, source_target_pairs={{0,8},{4,12},{8,0},{12,4},{1,9},{5,13},{9,1},{13,5},{2,10},{6,14},... | collective-permute-start | bytes 1572872 | tf_op jit(solution)/shard_map/ppermute | solution.py:559
  7.0 24.0 %collective-permute-start.4 = (bf16[128,2048]{1,0:T(8,128)(2,1)}, bf16[128,2048]{1,0:T(8,128)(2,1)S(1)}, u32[]{:S(2)}, u32[]{:S(2)}) collective-permute-start(bf16[128,2048]{1,0:T(8,128)(2,1)} %bitcast.4.q_outgrad.b0), channel_id=1, source_target_pairs={{0,4},{4,0},{8,12},{12,8},{1,5},{5,1},{9,13},{13,9},{2,6},{6,2},{1... | collective-permute-start | bytes 1572872 | tf_op jit(solution)/shard_map/ppermute | solution.py:559
  23.7 11.6 %copy-start.22 = (f32[384,128]{1,0:T(8,128)}, f32[384,128]{1,0:T(8,128)S(1)}, u32[]{:S(2)}) copy-start(f32[384,128]{1,0:T(8,128)S(1)} %get-tuple-element.55) | copy-start | bytes 589828
  31.0 4.4 %collective-permute-start.3 = (bf16[128,2048]{1,0:T(8,128)(2,1)}, bf16[128,2048]{1,0:T(8,128)(2,1)}, u32[]{:S(2)}, u32[]{:S(2)}) collective-permute-start(bf16[128,2048]{1,0:T(8,128)(2,1)} %bitcast.4.q_outgrad.b0), channel_id=1, source_target_pairs={{0,1},{1,0},{2,3},{3,2},{4,8},{5,9},{6,10},{7,11},{8,4},{9,5},{10,... | collective-permute-start | bytes 1572872 | tf_op jit(solution)/shard_map/ppermute | solution.py:562
  31.0 26.3 %collective-permute-start.5 = (bf16[128,2048]{1,0:T(8,128)(2,1)}, bf16[128,2048]{1,0:T(8,128)(2,1)}, u32[]{:S(2)}, u32[]{:S(2)}) collective-permute-start(bf16[128,2048]{1,0:T(8,128)(2,1)} %collective-permute-done.b3.b4), channel_id=1, source_target_pairs={{0,4},{4,0},{8,12},{12,8},{1,5},{5,1},{9,13},{13,9},{2,6},{6,2},{1... | collective-permute-start | bytes 1572872 | tf_op jit(solution)/shard_map/ppermute | solution.py:563
  33.8 25.0 %collective-permute-start.6 = (bf16[128,3584]{1,0:T(8,128)(2,1)}, bf16[128,3584]{1,0:T(8,128)(2,1)}, u32[]{:S(2)}, u32[]{:S(2)}) collective-permute-start(bf16[128,3584]{1,0:T(8,128)(2,1)} %bitcast.14), channel_id=1, source_target_pairs={{0,2},{1,3},{2,0},{3,1},{4,6},{5,7},{6,4},{7,5},{8,10},{9,11},{10,... | collective-permute-start | bytes 2752520 | tf_op jit(solution)/shard_map/ppermute | solution.py:584
  35.3 50.9 %copy-start.29 = (bf16[2,64,2048]{2,1,0:T(8,128)(2,1)}, bf16[2,64,2048]{2,1,0:T(8,128)(2,1)S(1)}, u32[]{:S(2)}) copy-start(bf16[2,64,2048]{2,1,0:T(8,128)(2,1)S(1)} %get-tuple-element.69) | copy-start | bytes 1572868
  35.3 32.7 %collective-permute-start.8 = (bf16[128,2048]{1,0:T(8,128)(2,1)S(1)}, bf16[128,2048]{1,0:T(8,128)(2,1)S(1)}, u32[]{:S(2)}, u32[]{:S(2)}) collective-permute-start(bf16[128,2048]{1,0:T(8,128)(2,1)S(1)} %bitcast.41), channel_id=1, source_target_pairs={{0,4},{4,0},{8,12},{12,8},{1,5},{5,1},{9,13},{13,9},{2,6},{6,2},{1... | collective-permute-start | bytes 1572872 | tf_op jit(solution)/shard_map/ppermute | solution.py:559
  35.4 30.5 %collective-permute-start.2 = (bf16[128,2048]{1,0:T(8,128)(2,1)S(1)}, bf16[128,2048]{1,0:T(8,128)(2,1)S(1)}, u32[]{:S(2)}, u32[]{:S(2)}) collective-permute-start(bf16[128,2048]{1,0:T(8,128)(2,1)S(1)} %bitcast.42), channel_id=1, source_target_pairs={{0,8},{4,12},{8,0},{12,4},{1,9},{5,13},{9,1},{13,5},{2,10},{6,14},... | collective-permute-start | bytes 1572872 | tf_op jit(solution)/shard_map/ppermute | solution.py:559
  58.7 11.5 %copy-start.2 = (bf16[4,64,3584]{2,1,0:T(8,128)(2,1)S(1)}, bf16[4,64,3584]{2,1,0:T(8,128)(2,1)}, u32[]{:S(2)}) copy-start(bf16[4,64,3584]{2,1,0:T(8,128)(2,1)} %param.18) | copy-start | bytes 5505028
  58.8 27.3 %collective-permute-start.11 = (bf16[2,128,2048]{2,1,0:T(8,128)(2,1)S(1)}, bf16[2,128,2048]{2,1,0:T(8,128)(2,1)S(1)}, u32[]{:S(2)}, u32[]{:S(2)}) collective-permute-start(bf16[2,128,2048]{2,1,0:T(8,128)(2,1)S(1)} %pad_maximum_fusion), channel_id=1, source_target_pairs={{0,2},{1,3},{2,0},{3,1},{4,6},{5,7},{6,4},{7,5},{8,10},{9,11},{10,... | collective-permute-start | bytes 3145736 | tf_op jit(solution)/shard_map/ppermute | solution.py:586
  65.8 20.4 %copy-start.28 = (bf16[128,2048]{1,0:T(8,128)(2,1)}, bf16[128,2048]{1,0:T(8,128)(2,1)S(1)}, u32[]{:S(2)}) copy-start(bf16[128,2048]{1,0:T(8,128)(2,1)S(1)} %collective-permute-done.2.b3.b4) | copy-start | bytes 1572868
  68.0 18.2 %copy-start.31 = (bf16[128,2048]{1,0:T(8,128)(2,1)}, bf16[128,2048]{1,0:T(8,128)(2,1)S(1)}, u32[]{:S(2)}) copy-start(bf16[128,2048]{1,0:T(8,128)(2,1)S(1)} %collective-permute-done.8.b1) | copy-start | bytes 1572868
  68.0 6.9 %collective-permute-start.7 = (bf16[128,2048]{1,0:T(8,128)(2,1)S(1)}, bf16[128,2048]{1,0:T(8,128)(2,1)S(1)}, u32[]{:S(2)}, u32[]{:S(2)}) collective-permute-start(bf16[128,2048]{1,0:T(8,128)(2,1)S(1)} %bitcast.43), channel_id=1, source_target_pairs={{0,1},{1,0},{2,3},{3,2},{4,8},{5,9},{6,10},{7,11},{8,4},{9,5},{10,... | collective-permute-start | bytes 1572872 | tf_op jit(solution)/shard_map/ppermute | solution.py:562
  68.0 14.3 %collective-permute-start.9 = (bf16[128,2048]{1,0:T(8,128)(2,1)S(1)}, bf16[128,2048]{1,0:T(8,128)(2,1)S(1)}, u32[]{:S(2)}, u32[]{:S(2)}) collective-permute-start(bf16[128,2048]{1,0:T(8,128)(2,1)S(1)} %collective-permute-done.2.b3.b4), channel_id=1, source_target_pairs={{0,4},{4,0},{8,12},{12,8},{1,5},{5,1},{9,13},{13,9},{2,6},{6,2},{1... | collective-permute-start | bytes 1572872 | tf_op jit(solution)/shard_map/ppermute | solution.py:563
  74.9 11.5 %copy-start.14 = (bf16[3584,256]{1,0:T(8,128)(2,1)}, bf16[3584,256]{1,0:T(8,128)(2,1)S(1)}, u32[]{:S(2)}) copy-start(bf16[3584,256]{1,0:T(8,128)(2,1)S(1)} %get-tuple-element.48.gates) | copy-start | bytes 5505028
  74.9 11.5 %copy-start.15 = (bf16[3584,256]{1,0:T(8,128)(2,1)}, bf16[3584,256]{1,0:T(8,128)(2,1)S(1)}, u32[]{:S(2)}) copy-start(bf16[3584,256]{1,0:T(8,128)(2,1)S(1)} %get-tuple-element.63.ups) | copy-start | bytes 5505028
  82.3 26.9 %collective-permute-start.14 = (bf16[128,2048]{1,0:T(8,128)(2,1)}, bf16[128,2048]{1,0:T(8,128)(2,1)}, u32[]{:S(2)}, u32[]{:S(2)}) collective-permute-start(bf16[128,2048]{1,0:T(8,128)(2,1)} %bitcast.9.b0), channel_id=1, source_target_pairs={{0,4},{4,0},{8,12},{12,8},{1,5},{5,1},{9,13},{13,9},{2,6},{6,2},{1... | collective-permute-start | bytes 1572872 | tf_op jit(solution)/shard_map/ppermute | solution.py:559
  83.1 26.1 %collective-permute-start.10 = (bf16[128,2048]{1,0:T(8,128)(2,1)}, bf16[128,2048]{1,0:T(8,128)(2,1)S(1)}, u32[]{:S(2)}, u32[]{:S(2)}) collective-permute-start(bf16[128,2048]{1,0:T(8,128)(2,1)} %bitcast.9.b0), channel_id=1, source_target_pairs={{0,8},{4,12},{8,0},{12,4},{1,9},{5,13},{9,1},{13,5},{2,10},{6,14},... | collective-permute-start | bytes 1572872 | tf_op jit(solution)/shard_map/ppermute | solution.py:559
  87.6 24.5 %collective-permute-start.17 = (bf16[2,128,2048]{2,1,0:T(8,128)(2,1)}, bf16[2,128,2048]{2,1,0:T(8,128)(2,1)}, u32[]{:S(2)}, u32[]{:S(2)}) collective-permute-start(bf16[2,128,2048]{2,1,0:T(8,128)(2,1)} %pad_maximum_fusion.1), channel_id=1, source_target_pairs={{0,2},{1,3},{2,0},{3,1},{4,6},{5,7},{6,4},{7,5},{8,10},{9,11},{10,... | collective-permute-start | bytes 3145736 | tf_op jit(solution)/shard_map/ppermute | solution.py:592
  109.2 14.5 %copy-start.27 = (bf16[128,2048]{1,0:T(8,128)(2,1)}, bf16[128,2048]{1,0:T(8,128)(2,1)S(1)}, u32[]{:S(2)}) copy-start(bf16[128,2048]{1,0:T(8,128)(2,1)S(1)} %collective-permute-done.10.b3.b4) | copy-start | bytes 1572868
  109.2 3.4 %collective-permute-start.13 = (bf16[128,2048]{1,0:T(8,128)(2,1)}, bf16[128,2048]{1,0:T(8,128)(2,1)S(1)}, u32[]{:S(2)}, u32[]{:S(2)}) collective-permute-start(bf16[128,2048]{1,0:T(8,128)(2,1)} %bitcast.9.b0), channel_id=1, source_target_pairs={{0,1},{1,0},{2,3},{3,2},{4,8},{5,9},{6,10},{7,11},{8,4},{9,5},{10,... | collective-permute-start | bytes 1572872 | tf_op jit(solution)/shard_map/ppermute | solution.py:562
  109.2 14.3 %collective-permute-start.15 = (bf16[128,2048]{1,0:T(8,128)(2,1)S(1)}, bf16[128,2048]{1,0:T(8,128)(2,1)S(1)}, u32[]{:S(2)}, u32[]{:S(2)}) collective-permute-start(bf16[128,2048]{1,0:T(8,128)(2,1)S(1)} %collective-permute-done.10.b3.b4), channel_id=1, source_target_pairs={{0,4},{4,0},{8,12},{12,8},{1,5},{5,1},{9,13},{13,9},{2,6},{6,2},{1... | collective-permute-start | bytes 1572872 | tf_op jit(solution)/shard_map/ppermute | solution.py:563
  112.1 30.4 %collective-permute-start.18 = (bf16[3584,128]{1,0:T(8,128)(2,1)}, bf16[3584,128]{1,0:T(8,128)(2,1)}, u32[]{:S(2)}, u32[]{:S(2)}) collective-permute-start(bf16[3584,128]{1,0:T(8,128)(2,1)} %get-tuple-element.57), channel_id=1, source_target_pairs={{0,2},{1,3},{2,0},{3,1},{4,6},{5,7},{6,4},{7,5},{8,10},{9,11},{10,... | collective-permute-start | bytes 2752520 | tf_op jit(solution)/shard_map/ppermute | solution.py:596
  125.5 16.7 %copy-start.23 = (f32[384,128]{1,0:T(8,128)S(1)}, f32[384,128]{1,0:T(8,128)}, u32[]{:S(2)}) copy-start(f32[384,128]{1,0:T(8,128)} %copy-done.22) | copy-start | bytes 589828
  125.5 17.0 %copy-start.5 = (bf16[64,3584]{1,0:T(8,128)(2,1)S(1)}, bf16[64,3584]{1,0:T(8,128)(2,1)}, u32[]{:S(2)}) copy-start(bf16[64,3584]{1,0:T(8,128)(2,1)} %proj_gate.5) | copy-start | bytes 1376260
  125.5 17.0 %copy-start.7 = (bf16[64,3584]{1,0:T(8,128)(2,1)S(1)}, bf16[64,3584]{1,0:T(8,128)(2,1)}, u32[]{:S(2)}) copy-start(bf16[64,3584]{1,0:T(8,128)(2,1)} %proj_up.5) | copy-start | bytes 1376260
  125.5 17.0 %copy-start.10 = (bf16[2,64,3584]{2,1,0:T(8,128)(2,1)S(1)}, bf16[2,64,3584]{2,1,0:T(8,128)(2,1)}, u32[]{:S(2)}) copy-start(bf16[2,64,3584]{2,1,0:T(8,128)(2,1)} %param.22) | copy-start | bytes 2752516
  125.5 17.0 %copy-start.12 = (bf16[2,64,3584]{2,1,0:T(8,128)(2,1)S(1)}, bf16[2,64,3584]{2,1,0:T(8,128)(2,1)}, u32[]{:S(2)}) copy-start(bf16[2,64,3584]{2,1,0:T(8,128)(2,1)} %param.23) | copy-start | bytes 2752516
  125.5 32.6 %collective-permute-start.20 = (bf16[2,128,2048]{2,1,0:T(8,128)(2,1)}, bf16[2,128,2048]{2,1,0:T(8,128)(2,1)}, u32[]{:S(2)}, u32[]{:S(2)}) collective-permute-start(bf16[2,128,2048]{2,1,0:T(8,128)(2,1)} %pad_maximum_fusion.2), channel_id=1, source_target_pairs={{0,2},{1,3},{2,0},{3,1},{4,6},{5,7},{6,4},{7,5},{8,10},{9,11},{10,... | collective-permute-start | bytes 3145736 | tf_op jit(solution)/shard_map/ppermute | solution.py:599
  141.3 51.6 %collective-permute-start.22 = (bf16[3584,128]{1,0:T(8,128)(2,1)}, bf16[3584,128]{1,0:T(8,128)(2,1)S(1)}, u32[]{:S(2)}, u32[]{:S(2)}) collective-permute-start(bf16[3584,128]{1,0:T(8,128)(2,1)} %get-tuple-element.59), channel_id=1, source_target_pairs={{0,2},{1,3},{2,0},{3,1},{4,6},{5,7},{6,4},{7,5},{8,10},{9,11},{10,... | collective-permute-start | bytes 2752520 | tf_op jit(solution)/shard_map/ppermute | solution.py:603
  142.2 6.2 %collective-permute-start.16 = (f32[384,128]{1,0:T(8,128)S(1)}, f32[384,128]{1,0:T(8,128)S(1)}, u32[]{:S(2)}, u32[]{:S(2)}) collective-permute-start(f32[384,128]{1,0:T(8,128)S(1)} %copy-done.23), channel_id=1, source_target_pairs={{0,4},{4,0},{8,12},{12,8},{1,5},{5,1},{9,13},{13,9},{2,6},{6,2},{1... | collective-permute-start | bytes 589832 | tf_op jit(solution)/shard_map/ppermute | solution.py:604
  146.5 5.0 %collective-permute-start.19 = (f32[128,192]{1,0:T(8,128)S(1)}, f32[128,192]{1,0:T(8,128)S(1)}, u32[]{:S(2)}, u32[]{:S(2)}) collective-permute-start(f32[128,192]{1,0:T(8,128)S(1)} %pad_maximum_fusion.3), channel_id=1, source_target_pairs={{0,4},{4,0},{8,12},{12,8},{1,5},{5,1},{9,13},{13,9},{2,6},{6,2},{1... | collective-permute-start | bytes 294920 | tf_op jit(solution)/shard_map/ppermute | solution.py:609
  158.2 31.1 %copy-start.25 = (s32[2]{0:T(128)S(1)}, s32[2]{0:T(128)}, u32[]{:S(2)}) copy-start(s32[2]{0:T(128)} %lengths.2) | copy-start | bytes 28
  158.2 34.8 %copy-start.3 = (bf16[4,64,3584]{2,1,0:T(8,128)(2,1)S(1)}, bf16[4,64,3584]{2,1,0:T(8,128)(2,1)}, u32[]{:S(2)}) copy-start(bf16[4,64,3584]{2,1,0:T(8,128)(2,1)} %param.18) | copy-start | bytes 5505028
  176.5 16.5 %copy-start.6 = (bf16[64,3584]{1,0:T(8,128)(2,1)S(1)}, bf16[64,3584]{1,0:T(8,128)(2,1)}, u32[]{:S(2)}) copy-start(bf16[64,3584]{1,0:T(8,128)(2,1)} %proj_gate.5) | copy-start | bytes 1376260
  176.5 16.5 %copy-start.8 = (bf16[64,3584]{1,0:T(8,128)(2,1)S(1)}, bf16[64,3584]{1,0:T(8,128)(2,1)}, u32[]{:S(2)}) copy-start(bf16[64,3584]{1,0:T(8,128)(2,1)} %proj_up.5) | copy-start | bytes 1376260
  176.5 12.7 %collective-permute-start.21 = (f32[384,128]{1,0:T(8,128)S(1)}, f32[384,128]{1,0:T(8,128)S(1)}, u32[]{:S(2)}, u32[]{:S(2)}) collective-permute-start(f32[384,128]{1,0:T(8,128)S(1)} %add.32), channel_id=1, source_target_pairs={{0,8},{4,12},{8,0},{12,4},{1,9},{5,13},{9,1},{13,5},{2,10},{6,14},... | collective-permute-start | bytes 589832 | tf_op jit(solution)/shard_map/ppermute | solution.py:614
  176.6 12.6 %collective-permute-start.24 = (f32[128,192]{1,0:T(8,128)S(1)}, f32[128,192]{1,0:T(8,128)S(1)}, u32[]{:S(2)}, u32[]{:S(2)}) collective-permute-start(f32[128,192]{1,0:T(8,128)S(1)} %fusion), channel_id=1, source_target_pairs={{0,8},{4,12},{8,0},{12,4},{1,9},{5,13},{9,1},{13,5},{2,10},{6,14},... | collective-permute-start | bytes 294920 | tf_op jit(solution)/shard_map/ppermute | solution.py:615
  190.2 11.7 %collective-permute-start.27 = (f32[2,192,64]{2,1,0:T(8,128)S(1)}, f32[2,192,64]{2,1,0:T(8,128)S(1)}, u32[]{:S(2)}, u32[]{:S(2)}) collective-permute-start(f32[2,192,64]{2,1,0:T(8,128)S(1)} %shard_map.161.q0), channel_id=1, source_target_pairs={{0,3},{1,2},{2,1},{3,0},{4,7},{5,6},{6,5},{7,4},{8,11},{9,10},{10,... | collective-permute-start | bytes 294920 | tf_op jit(solution)/shard_map/ppermute | solution.py:617
  190.3 11.6 %collective-permute-start.26 = (f32[2,192,64]{2,1,0:T(8,128)S(1)}, f32[2,192,64]{2,1,0:T(8,128)S(1)}, u32[]{:S(2)}, u32[]{:S(2)}) collective-permute-start(f32[2,192,64]{2,1,0:T(8,128)S(1)} %shard_map.161.q0), channel_id=1, source_target_pairs={{0,2},{1,3},{2,0},{3,1},{4,6},{5,7},{6,4},{7,5},{8,10},{9,11},{10,... | collective-permute-start | bytes 294920 | tf_op jit(solution)/shard_map/ppermute | solution.py:617
  191.1 10.7 %collective-permute-start.25 = (f32[2,192,64]{2,1,0:T(8,128)S(1)}, f32[2,192,64]{2,1,0:T(8,128)S(1)}, u32[]{:S(2)}, u32[]{:S(2)}) collective-permute-start(f32[2,192,64]{2,1,0:T(8,128)S(1)} %shard_map.161.q0), channel_id=1, source_target_pairs={{0,1},{1,0},{2,3},{3,2},{4,5},{5,4},{6,7},{7,6},{8,9},{9,8},{10,11... | collective-permute-start | bytes 294920 | tf_op jit(solution)/shard_map/ppermute | solution.py:617
  192.1 9.7 %collective-permute-start.23 = (f32[128,128]{1,0:T(8,128)}, f32[128,128]{1,0:T(8,128)S(1)}, u32[]{:S(2)}, u32[]{:S(2)}) collective-permute-start(f32[128,128]{1,0:T(8,128)} %get-tuple-element.67), channel_id=1, source_target_pairs={{0,2},{1,3},{2,0},{3,1},{4,6},{5,7},{6,4},{7,5},{8,10},{9,11},{10,... | collective-permute-start | bytes 196616 | tf_op jit(solution)/shard_map/ppermute | solution.py:621
  203.3 5.4 %collective-permute-start.30 = (f32[4,8]{1,0:T(4,128)S(1)}, f32[4,8]{1,0:T(4,128)S(1)}, u32[]{:S(2)}, u32[]{:S(2)}) collective-permute-start(f32[4,8]{1,0:T(4,128)S(1)} %shard_map.162), channel_id=1, source_target_pairs={{0,12},{4,8},{8,4},{12,0},{1,13},{5,9},{9,5},{13,1},{2,14},{6,10},... | collective-permute-start | bytes 392 | tf_op jit(solution)/shard_map/ppermute | solution.py:623
  205.8 4.5 %collective-permute-start.29 = (f32[4,8]{1,0:T(4,128)S(1)}, f32[4,8]{1,0:T(4,128)S(1)}, u32[]{:S(2)}, u32[]{:S(2)}) collective-permute-start(f32[4,8]{1,0:T(4,128)S(1)} %shard_map.162), channel_id=1, source_target_pairs={{0,8},{4,12},{8,0},{12,4},{1,9},{5,13},{9,1},{13,5},{2,10},{6,14},... | collective-permute-start | bytes 392 | tf_op jit(solution)/shard_map/ppermute | solution.py:623
  205.8 4.5 %collective-permute-start.28 = (f32[4,8]{1,0:T(4,128)S(1)}, f32[4,8]{1,0:T(4,128)S(1)}, u32[]{:S(2)}, u32[]{:S(2)}) collective-permute-start(f32[4,8]{1,0:T(4,128)S(1)} %shard_map.162), channel_id=1, source_target_pairs={{0,4},{4,0},{8,12},{12,8},{1,5},{5,1},{9,13},{13,9},{2,6},{6,2},{1... | collective-permute-start | bytes 392 | tf_op jit(solution)/shard_map/ppermute | solution.py:623
  (20 other events, 69.8 us)

commit v16 on v15

--- a/solution.py
+++ b/solution.py
@@ -573,20 +573,20 @@
 
     weight_own, weight_sib = down_weight, to_core(down_weight)
     q_hops = first_hops(q_outgrad)
-    far_gate = to_chip(t_gate[cut:])
     own_in_out, hidden = early_sides(
         t_input, q_input, t_outgrad, q_outgrad, proj_input, proj_outgrad, t_gate, t_up, q_gate,
         q_up, proj_hidden,
     )
 
+    far_gate = to_chip(after(t_gate[cut:], own_in_out))
     q_blocks = last_hops(*q_hops[:2], after(q_hops[2], own_in_out))
-    a_hops = first_hops(after(t_outgrad[:cut], q_hops[2], far_gate))
+    a_hops = first_hops(after(t_outgrad[:cut], q_hops[2]))
     far_up = to_chip(after(t_up[cut:], far_gate))
-    q_send = after(crossing_pair(*q_blocks), far_up)
+    q_send = crossing_pair(*q_blocks)
     q_far = to_chip(q_send)
-    a_blocks = last_hops(*a_hops[:2], after(a_hops[2], q_send))
-
-    b_hops = first_hops(after(t_outgrad[cut:], a_blocks[2], a_blocks[5]))
+    a_blocks = last_hops(*a_hops[:2], after(a_hops[2], q_send, far_up))
+
+    b_hops = first_hops(after(t_outgrad[cut:], a_hops[2]))
     gates, ups = turned(t_gate, t_up, far_gate, far_up)
     a_send = crossing_pair(*a_blocks[:5], after(a_blocks[5], q_far, gates))
     a_far = to_chip(a_send)
@@ -611,8 +611,8 @@
         after(flags, q_sums, in_out), b_blocks, b_far, weight_own, weight_sib, gates, ups,
         proj_gate, proj_up,
     )
-    in_out = in_out + across(after(in_out, b_near))
-    q_sums = q_sums + across(after(q_sums, b_near))
+    in_out = in_out + after(across(in_out), b_near)
+    q_sums = q_sums + after(across(q_sums), b_near)
     own_found = query_features(query_lengths, in_out[2 * cut :], q_sums)
     found = (own_found, to_core(own_found), to_chip(own_found), to_other(own_found))
     a_gradient = finished_sides(a_near_sum, a_returned, t_gate, t_up, proj_gate, proj_up)

time: 212 us -> 203 us (0.958)
  starting transfers between devices: 42.9 us -> 37.7 us
  waiting for transfers between devices: 82.1 us -> 77 us
    ppermute x3, waiting for transfers between devices: 29.9 us -> 9.12 us  [last_hops(): return (own, one, mid, two, two, outer(after(two, one)))]
    ppermute x1, waiting for transfers between devices: 0.01 us -> 12 us  [moving_plan(): q_far = to_chip(q_send)]
    ppermute x6, starting transfers between devices: 18.4 us -> 10.8 us  [first_hops(): return (own, outer(own), across(own))]
    ppermute x6, waiting for transfers between devices: 21.9 us -> 27.5 us  [first_hops(): return (own, outer(own), across(own))]
    ppermute x1, waiting for transfers between devices: 6.63 us -> 1.29 us  [moving_plan(): b_far = to_chip(b_send)]
    ppermute x3, waiting for transfers between devices: 9.74 us -> 13.4 us  [the longest x1 13.4 us: moving_plan(): far_gate = to_chip(after(t_gate[cut:], own_in_out))]
    ppermute x3, starting transfers between devices: 4.52 us -> 2.18 us  [last_hops(): return (own, one, mid, two, two, outer(after(two, one)))]
    unnamed x74 -> x78, local copies, waits for them, and re-layouts: 13.9 us -> 16.2 us
  transfers between devices with their start and end apart: 31 -> 31, of which waited for: 16 -> 14; matrix products, arithmetic and copies ran while one was open for 4% -> 4% of each run, Pallas kernels for 29% -> 30%
where the time goes in v16:
time: 203 us
  waiting for transfers between devices  77 us (38%)
  Pallas kernels  62.7 us (31%)
  starting transfers between devices  37.7 us (19%)
  local copies, waits for them, and re-layouts  19.2 us (9%)
  other arithmetic  5.53 us (3%)
    pallas_call x2, Pallas kernels, partial_sums(): pl.pallas_call(partial_kernel, grid=(units // TILE,), in_specs=[SCALARS]...  28.7 us
    ppermute x6, waiting for transfers between devices, first_hops(): return (own, outer(own), across(own))  27.5 us
    pallas_call x1, Pallas kernels, lent_sides(): pl.pallas_call(lent_kernel, grid=(units // TILE,), in_specs=[SCALARS] + [...  18.2 us
    unnamed x78, local copies, waits for them, and re-layouts  16.2 us
    ppermute x1, waiting for transfers between devices, moving_plan(): far_gate = to_chip(after(t_gate[cut:], own_in_out))  13.4 us
    ppermute x1, waiting for transfers between devices, moving_plan(): q_far = to_chip(q_send)  12 us
    ppermute x6, starting transfers between devices, first_hops(): return (own, outer(own), across(own))  10.8 us
    ppermute x3, waiting for transfers between devices, last_hops(): return (own, one, mid, two, two, outer(after(two, one)))  9.12 us
  transfers between devices with their start and end apart: 31, of which 14 were waited for; matrix products, arithmetic and copies ran while one was open for 4% of the time, Pallas kernels for 30%

profile of v16, /device:TPU:0, one launch (start us, length us, event | category | flops | bytes accessed | tf_op | source)
XLA Modules:
  0.0 202.6 jit_solution(8502778930321962276)
XLA Ops:
  0.5 3.6 %collective-permute-start = (bf16[128,2048]{1,0:T(8,128)(2,1)}, bf16[128,2048]{1,0:T(8,128)(2,1)}, u32[]{:S(2)}, u32[]{:S(2)}) collective-permute-start(bf16[128,2048]{1,0:T(8,128)(2,1)} %bitcast.4.q_outgrad.b0), channel_id=1, source_target_pairs={{0,8},{4,12},{8,0},{12,4},{1,9},{5,13},{9,1},{13,5},{2,10},{6,14},... | collective-permute-start | bytes 1572872 | tf_op jit(solution)/shard_map/ppermute | solution.py:559
  4.0 1.6 collective-permute-start.3
  5.6 1.5 copy-done
  7.1 1.5 copy-done.2
  8.6 1.2 copy-done.6
  9.8 1.2 copy-done.12
  11.0 1.2 copy-done.14
  12.2 1.2 copy-done.20
  13.4 1.0 copy-done.21
  14.5 1.0 copy-done.22
  17.4 4.9 %shard_map.154 = (f32[384,128]{1,0:T(8,128)S(1)}, f32[384,64]{1,0:T(8,128)S(1)}) custom-call(bf16[256,2048]{1,0:T(8,128)(2,1)S(1)} %bitcast.39, bf16[128,2048]{1,0:T(8,128)(2,1)S(1)} %bitcast.40, bf16[256,2048]{1,0:T(8,128)(2,1)S(1)} %bitcast.34, bf16[128,2048]{1,0:T(8,128)(2,1)} %bitcast.4.q_outgrad.b0, bf16[64,2048]{1,0:T(8,128)(2,1)S(1)} %copy-done.23, ...), custom_call_target="tpu_custom_call" | custom-call | flops 1024 | bytes 1024 | tf_op jit(solution)/shard_map/pallas_call | solution.py:396
  22.3 1.0 slice.42
  23.3 1.5 collective-permute-start.7
  24.8 3.5 %collective-permute-done.b3.b4 = bf16[128,2048]{1,0:T(8,128)(2,1)} collective-permute-done((bf16[128,2048]{1,0:T(8,128)(2,1)}, bf16[128,2048]{1,0:T(8,128)(2,1)}, u32[]{:S(2)}, u32[]{:S(2)}) %collective-permute-start) | collective-permute-done | bytes 524320 | tf_op jit(solution)/shard_map/ppermute | solution.py:559
  28.5 1.5 collective-permute-start.5
  32.4 13.4 %collective-permute-done.7.far_gate = bf16[128,3584]{1,0:T(8,128)(2,1)} collective-permute-done((bf16[128,3584]{1,0:T(8,128)(2,1)}, bf16[128,3584]{1,0:T(8,128)(2,1)}, u32[]{:S(2)}, u32[]{:S(2)}) %collective-permute-start.7) | collective-permute-done | bytes 917536 | tf_op jit(solution)/shard_map/ppermute | solution.py:581
  46.2 1.5 collective-permute-start.8
  47.7 1.6 select_bitcast_fusion.5
  50.2 20.8 %collective-permute-done.1.b3.b4 = bf16[128,2048]{1,0:T(8,128)(2,1)S(1)} collective-permute-done((bf16[128,2048]{1,0:T(8,128)(2,1)S(1)}, bf16[128,2048]{1,0:T(8,128)(2,1)S(1)}, u32[]{:S(2)}, u32[]{:S(2)}) %collective-permute-start.1) | collective-permute-done | bytes 524320 | tf_op jit(solution)/shard_map/ppermute | solution.py:559
  71.1 2.2 %collective-permute-start.14 = (bf16[128,2048]{1,0:T(8,128)(2,1)}, bf16[128,2048]{1,0:T(8,128)(2,1)}, u32[]{:S(2)}, u32[]{:S(2)}) collective-permute-start(bf16[128,2048]{1,0:T(8,128)(2,1)} %bitcast.9.b0), channel_id=1, source_target_pairs={{0,4},{4,0},{8,12},{12,8},{1,5},{5,1},{9,13},{13,9},{2,6},{6,2},{1... | collective-permute-start | bytes 1572872 | tf_op jit(solution)/shard_map/ppermute | solution.py:559
  73.3 4.6 %shard_map.155 = (bf16[3584,256]{1,0:T(8,128)(2,1)S(1)}, bf16[3584,256]{1,0:T(8,128)(2,1)S(1)}) custom-call(bf16[256,3584]{1,0:T(8,128)(2,1)S(1)} %bitcast.29, bf16[256,3584]{1,0:T(8,128)(2,1)S(1)} %bitcast.32, bf16[128,3584]{1,0:T(8,128)(2,1)} %collective-permute-done.7.far_gate, bf16[128,3584]{1,0:T(8,128)(2,1)S(1)} %collective-permute-done.8.far_up), custom_call_target="tpu_custom_call" | custom-call | flops 1024 | bytes 1024 | tf_op jit(solution)/shard_map/pallas_call | solution.py:295
  77.9 12.0 %collective-permute-done.6.far = bf16[2,128,2048]{2,1,0:T(8,128)(2,1)S(1)} collective-permute-done((bf16[2,128,2048]{2,1,0:T(8,128)(2,1)S(1)}, bf16[2,128,2048]{2,1,0:T(8,128)(2,1)S(1)}, u32[]{:S(2)}, u32[]{:S(2)}) %collective-permute-start.6) | collective-permute-done | bytes 1048608 | tf_op jit(solution)/shard_map/ppermute | solution.py:586
  89.9 2.6 %collective-permute-start.2 = (bf16[128,2048]{1,0:T(8,128)(2,1)}, bf16[128,2048]{1,0:T(8,128)(2,1)S(1)}, u32[]{:S(2)}, u32[]{:S(2)}) collective-permute-start(bf16[128,2048]{1,0:T(8,128)(2,1)} %bitcast.9.b0), channel_id=1, source_target_pairs={{0,8},{4,12},{8,0},{12,4},{1,9},{5,13},{9,1},{13,5},{2,10},{6,14},... | collective-permute-start | bytes 1572872 | tf_op jit(solution)/shard_map/ppermute | solution.py:559
  93.5 1.1 pad_maximum_fusion.1
  94.6 1.5 collective-permute-start.18
  96.7 14.4 %shard_map.156 = (f32[3584,128]{1,0:T(8,128)}, bf16[3584,128]{1,0:T(8,128)(2,1)}) custom-call(s32[2]{0:T(128)} %pad_add_fusion.flags, bf16[128,2048]{1,0:T(8,128)(2,1)} %bitcast.4.q_outgrad.b0, bf16[128,2048]{1,0:T(8,128)(2,1)} %collective-permute-done.3.b1, bf16[128,2048]{1,0:T(8,128)(2,1)} %collective-permute-done.4.b2, ...), custom_call_target="tpu_custom_call" | custom-call | flops 1024 | bytes 1024 | tf_op jit(solution)/shard_map/pallas_call | solution.py:241
  111.0 3.0 %collective-permute-done.2.b3.b4 = bf16[128,2048]{1,0:T(8,128)(2,1)S(1)} collective-permute-done((bf16[128,2048]{1,0:T(8,128)(2,1)}, bf16[128,2048]{1,0:T(8,128)(2,1)S(1)}, u32[]{:S(2)}, u32[]{:S(2)}) %collective-permute-start.2) | collective-permute-done | bytes 524320 | tf_op jit(solution)/shard_map/ppermute | solution.py:559
  114.7 3.1 %collective-permute-done.18.far = bf16[2,128,2048]{2,1,0:T(8,128)(2,1)} collective-permute-done((bf16[2,128,2048]{2,1,0:T(8,128)(2,1)}, bf16[2,128,2048]{2,1,0:T(8,128)(2,1)}, u32[]{:S(2)}, u32[]{:S(2)}) %collective-permute-start.18) | collective-permute-done | bytes 1048608 | tf_op jit(solution)/shard_map/ppermute | solution.py:592
  117.8 1.5 collective-permute-start.19
  119.3 9.1 %collective-permute-done.15.b5 = bf16[128,2048]{1,0:T(8,128)(2,1)S(1)} collective-permute-done((bf16[128,2048]{1,0:T(8,128)(2,1)S(1)}, bf16[128,2048]{1,0:T(8,128)(2,1)S(1)}, u32[]{:S(2)}, u32[]{:S(2)}) %collective-permute-start.15) | collective-permute-done | bytes 524320 | tf_op jit(solution)/shard_map/ppermute | solution.py:563
  129.2 1.2 pad_maximum_fusion.2
  130.4 2.3 %collective-permute-start.21 = (bf16[2,128,2048]{2,1,0:T(8,128)(2,1)}, bf16[2,128,2048]{2,1,0:T(8,128)(2,1)}, u32[]{:S(2)}, u32[]{:S(2)}) collective-permute-start(bf16[2,128,2048]{2,1,0:T(8,128)(2,1)} %pad_maximum_fusion.2), channel_id=1, source_target_pairs={{0,2},{1,3},{2,0},{3,1},{4,6},{5,7},{6,4},{7,5},{8,10},{9,11},{10,... | collective-permute-start | bytes 3145736 | tf_op jit(solution)/shard_map/ppermute | solution.py:599
  132.7 14.4 %shard_map.157 = (f32[3584,128]{1,0:T(8,128)}, bf16[3584,128]{1,0:T(8,128)(2,1)}) custom-call(s32[2]{0:T(128)} %pad_add_fusion.flags, bf16[128,2048]{1,0:T(8,128)(2,1)} %bitcast.45, bf16[128,2048]{1,0:T(8,128)(2,1)} %copy-done.33, bf16[128,2048]{1,0:T(8,128)(2,1)} %copy-done.35, bf16[128,2048]{1,0:T(8,128)(2,1)} %copy-done.31, bf16[128,2048]{1,0:T(8,128)(2,1)} %copy-done.31, ...), custom_call_target="tpu_custom_call" | custom-call | flops 1024 | bytes 1024 | tf_op jit(solution)/shard_map/pallas_call | solution.py:241
  147.7 1.5 copy-done.19
  149.2 2.4 %shard_map.158 = f32[128,128]{1,0:T(8,128)S(1)} custom-call(f32[3584,128]{1,0:T(8,128)S(1)} %copy-done.19, bf16[3584,128]{1,0:T(8,128)(2,1)} %collective-permute-done.19.returned, bf16[128,3584]{1,0:T(8,128)(2,1)S(1)} %bitcast.36, bf16[128,3584]{1,0:T(8,128)(2,1)S(1)} %bitcast.38, bf16[64,3584]{1,0:T(8,128)(2,1)S(1)} %copy-done.8, ...), custom_call_target="tpu_custom_call" | custom-call | flops 1024 | bytes 1024 | tf_op jit(solution)/shard_map/pallas_call | solution.py:268
  151.6 1.8 collective-permute-start.20
  153.8 2.3 %collective-permute-start.17 = (f32[384,128]{1,0:T(8,128)S(1)}, f32[384,128]{1,0:T(8,128)S(1)}, u32[]{:S(2)}, u32[]{:S(2)}) collective-permute-start(f32[384,128]{1,0:T(8,128)S(1)} %add.32), channel_id=1, source_target_pairs={{0,8},{4,12},{8,0},{12,4},{1,9},{5,13},{9,1},{13,5},{2,10},{6,14},... | collective-permute-start | bytes 589832 | tf_op jit(solution)/shard_map/ppermute | solution.py:614
  156.1 2.6 %collective-permute-done.20 = f32[128,192]{1,0:T(8,128)S(1)} collective-permute-done((f32[128,192]{1,0:T(8,128)S(1)}, f32[128,192]{1,0:T(8,128)S(1)}, u32[]{:S(2)}, u32[]{:S(2)}) %collective-permute-start.20) | collective-permute-done | bytes 98336 | tf_op jit(solution)/shard_map/ppermute | solution.py:609
  158.8 3.4 %collective-permute-start.24 = (f32[128,192]{1,0:T(8,128)S(1)}, f32[128,192]{1,0:T(8,128)S(1)}, u32[]{:S(2)}, u32[]{:S(2)}) collective-permute-start(f32[128,192]{1,0:T(8,128)S(1)} %fusion), channel_id=1, source_target_pairs={{0,8},{4,12},{8,0},{12,4},{1,9},{5,13},{9,1},{13,5},{2,10},{6,14},... | collective-permute-start | bytes 294920 | tf_op jit(solution)/shard_map/ppermute | solution.py:615
  162.2 1.3 collective-permute-done.21.far
  163.5 18.2 %shard_map.159 = (f32[128,128]{1,0:T(8,128)}, f32[128,128]{1,0:T(8,128)}) custom-call(s32[2]{0:T(128)} %pad_add_fusion.flags, bf16[128,2048]{1,0:T(8,128)(2,1)} %bitcast.9.b0, bf16[128,2048]{1,0:T(8,128)(2,1)} %collective-permute-done.14.b1, bf16[128,2048]{1,0:T(8,128)(2,1)} %copy-done.36, bf16[128,2048]{1,0:T(8,128)(2,1)} %copy-done.30, ...), custom_call_target="tpu_custom_call" | custom-call | flops 1024 | bytes 1024 | tf_op jit(solution)/shard_map/pallas_call | solution.py:337
  183.5 1.1 collective-permute-start.25
  185.4 1.5 copy-done.16
  186.9 1.6 shard_map.160.early
  188.5 5.6 %collective-permute-done.23.far = f32[128,128]{1,0:T(8,128)S(1)} collective-permute-done((f32[128,128]{1,0:T(8,128)}, f32[128,128]{1,0:T(8,128)S(1)}, u32[]{:S(2)}, u32[]{:S(2)}) %collective-permute-start.23) | collective-permute-done | bytes 65568 | tf_op jit(solution)/shard_map/ppermute | solution.py:621
  194.1 1.4 shard_map.162
  195.5 2.0 collective-permute-start.30
  198.3 1.7 collective-permute-start.28
  (121 shorter events, 16.2 us)
Async XLA Ops:
  0.0 96.7 %collective-permute-start.12 = (bf16[3584,2048]{1,0:T(8,128)(2,1)}, bf16[3584,2048]{1,0:T(8,128)(2,1)}, u32[]{:S(2)}, u32[]{:S(2)}) collective-permute-start(bf16[3584,2048]{1,0:T(8,128)(2,1)} %weight_own.5), channel_id=1, source_target_pairs={{0,1},{1,0},{2,3},{3,2},{4,5},{5,4},{6,7},{7,6},{8,9},{9,8},{10,11... | collective-permute-start | bytes 44040200 | tf_op jit(solution)/shard_map/ppermute | solution.py:574
  0.5 27.8 %collective-permute-start = (bf16[128,2048]{1,0:T(8,128)(2,1)}, bf16[128,2048]{1,0:T(8,128)(2,1)}, u32[]{:S(2)}, u32[]{:S(2)}) collective-permute-start(bf16[128,2048]{1,0:T(8,128)(2,1)} %bitcast.4.q_outgrad.b0), channel_id=1, source_target_pairs={{0,8},{4,12},{8,0},{12,4},{1,9},{5,13},{9,1},{13,5},{2,10},{6,14},... | collective-permute-start | bytes 1572872 | tf_op jit(solution)/shard_map/ppermute | solution.py:559
  4.0 24.4 %collective-permute-start.3 = (bf16[128,2048]{1,0:T(8,128)(2,1)}, bf16[128,2048]{1,0:T(8,128)(2,1)}, u32[]{:S(2)}, u32[]{:S(2)}) collective-permute-start(bf16[128,2048]{1,0:T(8,128)(2,1)} %bitcast.4.q_outgrad.b0), channel_id=1, source_target_pairs={{0,4},{4,0},{8,12},{12,8},{1,5},{5,1},{9,13},{13,9},{2,6},{6,2},{1... | collective-permute-start | bytes 1572872 | tf_op jit(solution)/shard_map/ppermute | solution.py:559
  22.3 8.7 %copy-start.7 = (bf16[4,64,2048]{2,1,0:T(8,128)(2,1)S(1)}, bf16[4,64,2048]{2,1,0:T(8,128)(2,1)}, u32[]{:S(2)}) copy-start(bf16[4,64,2048]{2,1,0:T(8,128)(2,1)} %param.19) | copy-start | bytes 3145732
  23.3 22.5 %collective-permute-start.7 = (bf16[128,3584]{1,0:T(8,128)(2,1)}, bf16[128,3584]{1,0:T(8,128)(2,1)}, u32[]{:S(2)}, u32[]{:S(2)}) collective-permute-start(bf16[128,3584]{1,0:T(8,128)(2,1)} %bitcast.16), channel_id=1, source_target_pairs={{0,2},{1,3},{2,0},{3,1},{4,6},{5,7},{6,4},{7,5},{8,10},{9,11},{10,... | collective-permute-start | bytes 2752520 | tf_op jit(solution)/shard_map/ppermute | solution.py:581
  28.3 17.9 %collective-permute-start.4 = (bf16[128,2048]{1,0:T(8,128)(2,1)}, bf16[128,2048]{1,0:T(8,128)(2,1)}, u32[]{:S(2)}, u32[]{:S(2)}) collective-permute-start(bf16[128,2048]{1,0:T(8,128)(2,1)} %bitcast.4.q_outgrad.b0), channel_id=1, source_target_pairs={{0,1},{1,0},{2,3},{3,2},{4,8},{5,9},{6,10},{7,11},{8,4},{9,5},{10,... | collective-permute-start | bytes 1572872 | tf_op jit(solution)/shard_map/ppermute | solution.py:562
  28.5 19.2 %collective-permute-start.5 = (bf16[128,2048]{1,0:T(8,128)(2,1)}, bf16[128,2048]{1,0:T(8,128)(2,1)}, u32[]{:S(2)}, u32[]{:S(2)}) collective-permute-start(bf16[128,2048]{1,0:T(8,128)(2,1)} %collective-permute-done.b3.b4), channel_id=1, source_target_pairs={{0,4},{4,0},{8,12},{12,8},{1,5},{5,1},{9,13},{13,9},{2,6},{6,2},{1... | collective-permute-start | bytes 1572872 | tf_op jit(solution)/shard_map/ppermute | solution.py:563
  31.9 60.6 %copy-start.32 = (bf16[2,64,2048]{2,1,0:T(8,128)(2,1)}, bf16[2,64,2048]{2,1,0:T(8,128)(2,1)S(1)}, u32[]{:S(2)}) copy-start(bf16[2,64,2048]{2,1,0:T(8,128)(2,1)S(1)} %get-tuple-element.69) | copy-start | bytes 1572868
  31.9 39.0 %collective-permute-start.10 = (bf16[128,2048]{1,0:T(8,128)(2,1)S(1)}, bf16[128,2048]{1,0:T(8,128)(2,1)S(1)}, u32[]{:S(2)}, u32[]{:S(2)}) collective-permute-start(bf16[128,2048]{1,0:T(8,128)(2,1)S(1)} %bitcast.41), channel_id=1, source_target_pairs={{0,4},{4,0},{8,12},{12,8},{1,5},{5,1},{9,13},{13,9},{2,6},{6,2},{1... | collective-permute-start | bytes 1572872 | tf_op jit(solution)/shard_map/ppermute | solution.py:559
  45.8 25.1 %collective-permute-start.1 = (bf16[128,2048]{1,0:T(8,128)(2,1)S(1)}, bf16[128,2048]{1,0:T(8,128)(2,1)S(1)}, u32[]{:S(2)}, u32[]{:S(2)}) collective-permute-start(bf16[128,2048]{1,0:T(8,128)(2,1)S(1)} %bitcast.42), channel_id=1, source_target_pairs={{0,8},{4,12},{8,0},{12,4},{1,9},{5,13},{9,1},{13,5},{2,10},{6,14},... | collective-permute-start | bytes 1572872 | tf_op jit(solution)/shard_map/ppermute | solution.py:559
  46.2 24.8 %collective-permute-start.8 = (bf16[128,3584]{1,0:T(8,128)(2,1)}, bf16[128,3584]{1,0:T(8,128)(2,1)S(1)}, u32[]{:S(2)}, u32[]{:S(2)}) collective-permute-start(bf16[128,3584]{1,0:T(8,128)(2,1)} %bitcast.15), channel_id=1, source_target_pairs={{0,2},{1,3},{2,0},{3,1},{4,6},{5,7},{6,4},{7,5},{8,10},{9,11},{10,... | collective-permute-start | bytes 2752520 | tf_op jit(solution)/shard_map/ppermute | solution.py:584
  47.7 25.6 %copy-start.4 = (bf16[4,64,3584]{2,1,0:T(8,128)(2,1)S(1)}, bf16[4,64,3584]{2,1,0:T(8,128)(2,1)}, u32[]{:S(2)}) copy-start(bf16[4,64,3584]{2,1,0:T(8,128)(2,1)} %param.18) | copy-start | bytes 5505028
  49.3 24.0 %copy-start.1 = (bf16[4,64,3584]{2,1,0:T(8,128)(2,1)S(1)}, bf16[4,64,3584]{2,1,0:T(8,128)(2,1)}, u32[]{:S(2)}) copy-start(bf16[4,64,3584]{2,1,0:T(8,128)(2,1)} %param.17) | copy-start | bytes 5505028
  49.4 40.5 %collective-permute-start.6 = (bf16[2,128,2048]{2,1,0:T(8,128)(2,1)S(1)}, bf16[2,128,2048]{2,1,0:T(8,128)(2,1)S(1)}, u32[]{:S(2)}, u32[]{:S(2)}) collective-permute-start(bf16[2,128,2048]{2,1,0:T(8,128)(2,1)S(1)} %pad_maximum_fusion), channel_id=1, source_target_pairs={{0,2},{1,3},{2,0},{3,1},{4,6},{5,7},{6,4},{7,5},{8,10},{9,11},{10,... | collective-permute-start | bytes 3145736 | tf_op jit(solution)/shard_map/ppermute | solution.py:586
  70.9 21.6 %copy-start.31 = (bf16[128,2048]{1,0:T(8,128)(2,1)}, bf16[128,2048]{1,0:T(8,128)(2,1)S(1)}, u32[]{:S(2)}) copy-start(bf16[128,2048]{1,0:T(8,128)(2,1)S(1)} %collective-permute-done.1.b3.b4) | copy-start | bytes 1572868
  70.9 21.6 %copy-start.33 = (bf16[128,2048]{1,0:T(8,128)(2,1)}, bf16[128,2048]{1,0:T(8,128)(2,1)S(1)}, u32[]{:S(2)}) copy-start(bf16[128,2048]{1,0:T(8,128)(2,1)S(1)} %collective-permute-done.10.b1) | copy-start | bytes 1572868
  70.9 21.6 %collective-permute-start.11 = (bf16[128,2048]{1,0:T(8,128)(2,1)S(1)}, bf16[128,2048]{1,0:T(8,128)(2,1)S(1)}, u32[]{:S(2)}, u32[]{:S(2)}) collective-permute-start(bf16[128,2048]{1,0:T(8,128)(2,1)S(1)} %collective-permute-done.1.b3.b4), channel_id=1, source_target_pairs={{0,4},{4,0},{8,12},{12,8},{1,5},{5,1},{9,13},{13,9},{2,6},{6,2},{1... | collective-permute-start | bytes 1572872 | tf_op jit(solution)/shard_map/ppermute | solution.py:563
  71.0 21.5 %collective-permute-start.9 = (bf16[128,2048]{1,0:T(8,128)(2,1)S(1)}, bf16[128,2048]{1,0:T(8,128)(2,1)S(1)}, u32[]{:S(2)}, u32[]{:S(2)}) collective-permute-start(bf16[128,2048]{1,0:T(8,128)(2,1)S(1)} %bitcast.43), channel_id=1, source_target_pairs={{0,1},{1,0},{2,3},{3,2},{4,8},{5,9},{6,10},{7,11},{8,4},{9,5},{10,... | collective-permute-start | bytes 1572872 | tf_op jit(solution)/shard_map/ppermute | solution.py:562
  71.1 43.0 %collective-permute-start.14 = (bf16[128,2048]{1,0:T(8,128)(2,1)}, bf16[128,2048]{1,0:T(8,128)(2,1)}, u32[]{:S(2)}, u32[]{:S(2)}) collective-permute-start(bf16[128,2048]{1,0:T(8,128)(2,1)} %bitcast.9.b0), channel_id=1, source_target_pairs={{0,4},{4,0},{8,12},{12,8},{1,5},{5,1},{9,13},{13,9},{2,6},{6,2},{1... | collective-permute-start | bytes 1572872 | tf_op jit(solution)/shard_map/ppermute | solution.py:559
  77.9 14.8 %copy-start.17 = (bf16[3584,256]{1,0:T(8,128)(2,1)}, bf16[3584,256]{1,0:T(8,128)(2,1)S(1)}, u32[]{:S(2)}) copy-start(bf16[3584,256]{1,0:T(8,128)(2,1)S(1)} %get-tuple-element.48.gates) | copy-start | bytes 5505028
  77.9 14.8 %copy-start.18 = (bf16[3584,256]{1,0:T(8,128)(2,1)}, bf16[3584,256]{1,0:T(8,128)(2,1)S(1)}, u32[]{:S(2)}) copy-start(bf16[3584,256]{1,0:T(8,128)(2,1)S(1)} %get-tuple-element.63.ups) | copy-start | bytes 5505028
  89.9 24.2 %collective-permute-start.2 = (bf16[128,2048]{1,0:T(8,128)(2,1)}, bf16[128,2048]{1,0:T(8,128)(2,1)S(1)}, u32[]{:S(2)}, u32[]{:S(2)}) collective-permute-start(bf16[128,2048]{1,0:T(8,128)(2,1)} %bitcast.9.b0), channel_id=1, source_target_pairs={{0,8},{4,12},{8,0},{12,4},{1,9},{5,13},{9,1},{13,5},{2,10},{6,14},... | collective-permute-start | bytes 1572872 | tf_op jit(solution)/shard_map/ppermute | solution.py:559
  94.6 23.2 %collective-permute-start.18 = (bf16[2,128,2048]{2,1,0:T(8,128)(2,1)}, bf16[2,128,2048]{2,1,0:T(8,128)(2,1)}, u32[]{:S(2)}, u32[]{:S(2)}) collective-permute-start(bf16[2,128,2048]{2,1,0:T(8,128)(2,1)} %pad_maximum_fusion.1), channel_id=1, source_target_pairs={{0,2},{1,3},{2,0},{3,1},{4,6},{5,7},{6,4},{7,5},{8,10},{9,11},{10,... | collective-permute-start | bytes 3145736 | tf_op jit(solution)/shard_map/ppermute | solution.py:592
  114.1 14.5 %copy-start.30 = (bf16[128,2048]{1,0:T(8,128)(2,1)}, bf16[128,2048]{1,0:T(8,128)(2,1)S(1)}, u32[]{:S(2)}) copy-start(bf16[128,2048]{1,0:T(8,128)(2,1)S(1)} %collective-permute-done.2.b3.b4) | copy-start | bytes 1572868
  114.1 5.2 %collective-permute-start.13 = (bf16[128,2048]{1,0:T(8,128)(2,1)}, bf16[128,2048]{1,0:T(8,128)(2,1)S(1)}, u32[]{:S(2)}, u32[]{:S(2)}) collective-permute-start(bf16[128,2048]{1,0:T(8,128)(2,1)} %bitcast.9.b0), channel_id=1, source_target_pairs={{0,1},{1,0},{2,3},{3,2},{4,8},{5,9},{6,10},{7,11},{8,4},{9,5},{10,... | collective-permute-start | bytes 1572872 | tf_op jit(solution)/shard_map/ppermute | solution.py:562
  114.1 14.3 %collective-permute-start.15 = (bf16[128,2048]{1,0:T(8,128)(2,1)S(1)}, bf16[128,2048]{1,0:T(8,128)(2,1)S(1)}, u32[]{:S(2)}, u32[]{:S(2)}) collective-permute-start(bf16[128,2048]{1,0:T(8,128)(2,1)S(1)} %collective-permute-done.2.b3.b4), channel_id=1, source_target_pairs={{0,4},{4,0},{8,12},{12,8},{1,5},{5,1},{9,13},{13,9},{2,6},{6,2},{1... | collective-permute-start | bytes 1572872 | tf_op jit(solution)/shard_map/ppermute | solution.py:563
  117.8 29.9 %collective-permute-start.19 = (bf16[3584,128]{1,0:T(8,128)(2,1)}, bf16[3584,128]{1,0:T(8,128)(2,1)}, u32[]{:S(2)}, u32[]{:S(2)}) collective-permute-start(bf16[3584,128]{1,0:T(8,128)(2,1)} %get-tuple-element.57), channel_id=1, source_target_pairs={{0,2},{1,3},{2,0},{3,1},{4,6},{5,7},{6,4},{7,5},{8,10},{9,11},{10,... | collective-permute-start | bytes 2752520 | tf_op jit(solution)/shard_map/ppermute | solution.py:596
  119.3 9.3 %copy-start.36 = (bf16[128,2048]{1,0:T(8,128)(2,1)}, bf16[128,2048]{1,0:T(8,128)(2,1)S(1)}, u32[]{:S(2)}) copy-start(bf16[128,2048]{1,0:T(8,128)(2,1)S(1)} %collective-permute-done.13.b2) | copy-start | bytes 1572868
  130.4 17.0 %copy-start.26 = (f32[384,128]{1,0:T(8,128)S(1)}, f32[384,128]{1,0:T(8,128)}, u32[]{:S(2)}) copy-start(f32[384,128]{1,0:T(8,128)} %copy-done.25) | copy-start | bytes 589828
  130.4 17.3 %copy-start.8 = (bf16[64,3584]{1,0:T(8,128)(2,1)S(1)}, bf16[64,3584]{1,0:T(8,128)(2,1)}, u32[]{:S(2)}) copy-start(bf16[64,3584]{1,0:T(8,128)(2,1)} %proj_gate.5) | copy-start | bytes 1376260
  130.4 17.3 %copy-start.10 = (bf16[64,3584]{1,0:T(8,128)(2,1)S(1)}, bf16[64,3584]{1,0:T(8,128)(2,1)}, u32[]{:S(2)}) copy-start(bf16[64,3584]{1,0:T(8,128)(2,1)} %proj_up.5) | copy-start | bytes 1376260
  130.4 17.3 %copy-start.13 = (bf16[2,64,3584]{2,1,0:T(8,128)(2,1)S(1)}, bf16[2,64,3584]{2,1,0:T(8,128)(2,1)}, u32[]{:S(2)}) copy-start(bf16[2,64,3584]{2,1,0:T(8,128)(2,1)} %param.22) | copy-start | bytes 2752516
  130.4 17.3 %copy-start.15 = (bf16[2,64,3584]{2,1,0:T(8,128)(2,1)S(1)}, bf16[2,64,3584]{2,1,0:T(8,128)(2,1)}, u32[]{:S(2)}) copy-start(bf16[2,64,3584]{2,1,0:T(8,128)(2,1)} %param.23) | copy-start | bytes 2752516
  130.4 33.0 %collective-permute-start.21 = (bf16[2,128,2048]{2,1,0:T(8,128)(2,1)}, bf16[2,128,2048]{2,1,0:T(8,128)(2,1)}, u32[]{:S(2)}, u32[]{:S(2)}) collective-permute-start(bf16[2,128,2048]{2,1,0:T(8,128)(2,1)} %pad_maximum_fusion.2), channel_id=1, source_target_pairs={{0,2},{1,3},{2,0},{3,1},{4,6},{5,7},{6,4},{7,5},{8,10},{9,11},{10,... | collective-permute-start | bytes 3145736 | tf_op jit(solution)/shard_map/ppermute | solution.py:599
  147.1 38.3 %collective-permute-start.22 = (bf16[3584,128]{1,0:T(8,128)(2,1)}, bf16[3584,128]{1,0:T(8,128)(2,1)S(1)}, u32[]{:S(2)}, u32[]{:S(2)}) collective-permute-start(bf16[3584,128]{1,0:T(8,128)(2,1)} %get-tuple-element.59), channel_id=1, source_target_pairs={{0,2},{1,3},{2,0},{3,1},{4,6},{5,7},{6,4},{7,5},{8,10},{9,11},{10,... | collective-permute-start | bytes 2752520 | tf_op jit(solution)/shard_map/ppermute | solution.py:603
  147.3 6.4 %collective-permute-start.16 = (f32[384,128]{1,0:T(8,128)S(1)}, f32[384,128]{1,0:T(8,128)S(1)}, u32[]{:S(2)}, u32[]{:S(2)}) collective-permute-start(f32[384,128]{1,0:T(8,128)S(1)} %copy-done.26), channel_id=1, source_target_pairs={{0,4},{4,0},{8,12},{12,8},{1,5},{5,1},{9,13},{13,9},{2,6},{6,2},{1... | collective-permute-start | bytes 589832 | tf_op jit(solution)/shard_map/ppermute | solution.py:604
  151.6 7.1 %collective-permute-start.20 = (f32[128,192]{1,0:T(8,128)S(1)}, f32[128,192]{1,0:T(8,128)S(1)}, u32[]{:S(2)}, u32[]{:S(2)}) collective-permute-start(f32[128,192]{1,0:T(8,128)S(1)} %pad_maximum_fusion.3), channel_id=1, source_target_pairs={{0,4},{4,0},{8,12},{12,8},{1,5},{5,1},{9,13},{13,9},{2,6},{6,2},{1... | collective-permute-start | bytes 294920 | tf_op jit(solution)/shard_map/ppermute | solution.py:609
  153.8 28.0 %collective-permute-start.17 = (f32[384,128]{1,0:T(8,128)S(1)}, f32[384,128]{1,0:T(8,128)S(1)}, u32[]{:S(2)}, u32[]{:S(2)}) collective-permute-start(f32[384,128]{1,0:T(8,128)S(1)} %add.32), channel_id=1, source_target_pairs={{0,8},{4,12},{8,0},{12,4},{1,9},{5,13},{9,1},{13,5},{2,10},{6,14},... | collective-permute-start | bytes 589832 | tf_op jit(solution)/shard_map/ppermute | solution.py:614
  158.8 23.0 %collective-permute-start.24 = (f32[128,192]{1,0:T(8,128)S(1)}, f32[128,192]{1,0:T(8,128)S(1)}, u32[]{:S(2)}, u32[]{:S(2)}) collective-permute-start(f32[128,192]{1,0:T(8,128)S(1)} %fusion), channel_id=1, source_target_pairs={{0,8},{4,12},{8,0},{12,4},{1,9},{5,13},{9,1},{13,5},{2,10},{6,14},... | collective-permute-start | bytes 294920 | tf_op jit(solution)/shard_map/ppermute | solution.py:615
  163.4 18.4 %copy-start.28 = (s32[2]{0:T(128)S(1)}, s32[2]{0:T(128)}, u32[]{:S(2)}) copy-start(s32[2]{0:T(128)} %lengths.2) | copy-start | bytes 28
  163.5 21.9 %copy-start.5 = (bf16[4,64,3584]{2,1,0:T(8,128)(2,1)S(1)}, bf16[4,64,3584]{2,1,0:T(8,128)(2,1)}, u32[]{:S(2)}) copy-start(bf16[4,64,3584]{2,1,0:T(8,128)(2,1)} %param.18) | copy-start | bytes 5505028
  182.8 11.3 %collective-permute-start.27 = (f32[2,192,64]{2,1,0:T(8,128)S(1)}, f32[2,192,64]{2,1,0:T(8,128)S(1)}, u32[]{:S(2)}, u32[]{:S(2)}) collective-permute-start(f32[2,192,64]{2,1,0:T(8,128)S(1)} %shard_map.161.q0), channel_id=1, source_target_pairs={{0,3},{1,2},{2,1},{3,0},{4,7},{5,6},{6,5},{7,4},{8,11},{9,10},{10,... | collective-permute-start | bytes 294920 | tf_op jit(solution)/shard_map/ppermute | solution.py:617
  182.8 11.3 %collective-permute-start.26 = (f32[2,192,64]{2,1,0:T(8,128)S(1)}, f32[2,192,64]{2,1,0:T(8,128)S(1)}, u32[]{:S(2)}, u32[]{:S(2)}) collective-permute-start(f32[2,192,64]{2,1,0:T(8,128)S(1)} %shard_map.161.q0), channel_id=1, source_target_pairs={{0,2},{1,3},{2,0},{3,1},{4,6},{5,7},{6,4},{7,5},{8,10},{9,11},{10,... | collective-permute-start | bytes 294920 | tf_op jit(solution)/shard_map/ppermute | solution.py:617
  183.5 10.5 %collective-permute-start.25 = (f32[2,192,64]{2,1,0:T(8,128)S(1)}, f32[2,192,64]{2,1,0:T(8,128)S(1)}, u32[]{:S(2)}, u32[]{:S(2)}) collective-permute-start(f32[2,192,64]{2,1,0:T(8,128)S(1)} %shard_map.161.q0), channel_id=1, source_target_pairs={{0,1},{1,0},{2,3},{3,2},{4,5},{5,4},{6,7},{7,6},{8,9},{9,8},{10,11... | collective-permute-start | bytes 294920 | tf_op jit(solution)/shard_map/ppermute | solution.py:617
  184.7 9.4 %collective-permute-start.23 = (f32[128,128]{1,0:T(8,128)}, f32[128,128]{1,0:T(8,128)S(1)}, u32[]{:S(2)}, u32[]{:S(2)}) collective-permute-start(f32[128,128]{1,0:T(8,128)} %get-tuple-element.67), channel_id=1, source_target_pairs={{0,2},{1,3},{2,0},{3,1},{4,6},{5,7},{6,4},{7,5},{8,10},{9,11},{10,... | collective-permute-start | bytes 196616 | tf_op jit(solution)/shard_map/ppermute | solution.py:621
  195.5 5.4 %collective-permute-start.30 = (f32[4,8]{1,0:T(4,128)S(1)}, f32[4,8]{1,0:T(4,128)S(1)}, u32[]{:S(2)}, u32[]{:S(2)}) collective-permute-start(f32[4,8]{1,0:T(4,128)S(1)} %shard_map.162), channel_id=1, source_target_pairs={{0,12},{4,8},{8,4},{12,0},{1,13},{5,9},{9,5},{13,1},{2,14},{6,10},... | collective-permute-start | bytes 392 | tf_op jit(solution)/shard_map/ppermute | solution.py:623
  197.5 4.5 %collective-permute-start.29 = (f32[4,8]{1,0:T(4,128)S(1)}, f32[4,8]{1,0:T(4,128)S(1)}, u32[]{:S(2)}, u32[]{:S(2)}) collective-permute-start(f32[4,8]{1,0:T(4,128)S(1)} %shard_map.162), channel_id=1, source_target_pairs={{0,8},{4,12},{8,0},{12,4},{1,9},{5,13},{9,1},{13,5},{2,10},{6,14},... | collective-permute-start | bytes 392 | tf_op jit(solution)/shard_map/ppermute | solution.py:623
  198.3 3.7 %collective-permute-start.28 = (f32[4,8]{1,0:T(4,128)S(1)}, f32[4,8]{1,0:T(4,128)S(1)}, u32[]{:S(2)}, u32[]{:S(2)}) collective-permute-start(f32[4,8]{1,0:T(4,128)S(1)} %shard_map.162), channel_id=1, source_target_pairs={{0,4},{4,0},{8,12},{12,8},{1,5},{5,1},{9,13},{13,9},{2,6},{6,2},{1... | collective-permute-start | bytes 392 | tf_op jit(solution)/shard_map/ppermute | solution.py:623
  (22 other events, 52.5 us)

commit v17 on v15

--- a/solution.py
+++ b/solution.py
@@ -586,7 +586,7 @@
     q_far = to_chip(q_send)
     a_blocks = last_hops(*a_hops[:2], after(a_hops[2], q_send))
 
-    b_hops = first_hops(after(t_outgrad[cut:], a_blocks[2], a_blocks[5]))
+    b_hops = first_hops(after(t_outgrad[cut:], a_hops[2]))
     gates, ups = turned(t_gate, t_up, far_gate, far_up)
     a_send = crossing_pair(*a_blocks[:5], after(a_blocks[5], q_far, gates))
     a_far = to_chip(a_send)
@@ -611,8 +611,8 @@
         after(flags, q_sums, in_out), b_blocks, b_far, weight_own, weight_sib, gates, ups,
         proj_gate, proj_up,
     )
-    in_out = in_out + across(after(in_out, b_near))
-    q_sums = q_sums + across(after(q_sums, b_near))
+    in_out = in_out + after(across(in_out), b_near)
+    q_sums = q_sums + after(across(q_sums), b_near)
     own_found = query_features(query_lengths, in_out[2 * cut :], q_sums)
     found = (own_found, to_core(own_found), to_chip(own_found), to_other(own_found))
     a_gradient = finished_sides(a_near_sum, a_returned, t_gate, t_up, proj_gate, proj_up)

time: 212 us -> 195 us (0.920)
  waiting for transfers between devices: 82.1 us -> 57.4 us
  starting transfers between devices: 42.9 us -> 50.7 us
    ppermute x2, waiting for transfers between devices: 9.74 us -> 0.01 us  [the longest x1 0.01 us: moving_plan(): q_sums = q_sums + after(across(q_sums), b_near)]
    ppermute x2, starting transfers between devices: 2.98 us -> 10 us  [the longest x1 6 us: moving_plan(): q_sums = q_sums + after(across(q_sums), b_near)]
    ppermute x1, waiting for transfers between devices: 6.63 us -> 0.2 us  [moving_plan(): b_far = to_chip(b_send)]
    ppermute x1, waiting for transfers between devices: 3.14 us -> 0.01 us  [moving_plan(): q_sums = q_sums + outer(q_sums)]
  transfers between devices with their start and end apart: 31 -> 31, of which waited for: 16 -> 14; matrix products, arithmetic and copies ran while one was open for 4% -> 4% of each run, Pallas kernels for 29% -> 32%
where the time goes in v17:
time: 195 us
  Pallas kernels  62.7 us (32%)
  waiting for transfers between devices  57.4 us (29%)
  starting transfers between devices  50.7 us (26%)
  local copies, waits for them, and re-layouts  17.9 us (9%)
  other arithmetic  5.39 us (3%)
    pallas_call x2, Pallas kernels, partial_sums(): pl.pallas_call(partial_kernel, grid=(units // TILE,), in_specs=[SCALARS]...  28.7 us
    ppermute x3, waiting for transfers between devices, last_hops(): return (own, one, mid, two, two, outer(after(two, one)))  28 us
    ppermute x6, waiting for transfers between devices, first_hops(): return (own, outer(own), across(own))  20 us
    ppermute x6, starting transfers between devices, first_hops(): return (own, outer(own), across(own))  18.4 us
    pallas_call x1, Pallas kernels, lent_sides(): pl.pallas_call(lent_kernel, grid=(units // TILE,), in_specs=[SCALARS] + [...  18.3 us
    unnamed x74, local copies, waits for them, and re-layouts  14.6 us
    ppermute x1, starting transfers between devices, moving_plan(): q_sums = q_sums + after(across(q_sums), b_near)  6 us
    ppermute x3, starting transfers between devices, last_hops(): return (own, one, mid, two, two, outer(after(two, one)))  5.81 us
  transfers between devices with their start and end apart: 31, of which 14 were waited for; matrix products, arithmetic and copies ran while one was open for 4% of the time, Pallas kernels for 32%

profile of v17, /device:TPU:0, one launch (start us, length us, event | category | flops | bytes accessed | tf_op | source)
XLA Modules:
  0.0 194.5 jit_solution(10401797912052949020)
XLA Ops:
  0.5 1.3 slice.40
  1.8 2.6 %collective-permute-start.1 = (bf16[128,3584]{1,0:T(8,128)(2,1)S(1)}, bf16[128,3584]{1,0:T(8,128)(2,1)S(1)}, u32[]{:S(2)}, u32[]{:S(2)}) collective-permute-start(bf16[128,3584]{1,0:T(8,128)(2,1)S(1)} %bitcast.46), channel_id=1, source_target_pairs={{0,2},{1,3},{2,0},{3,1},{4,6},{5,7},{6,4},{7,5},{8,10},{9,11},{10,... | collective-permute-start | bytes 2752520 | tf_op jit(solution)/shard_map/ppermute | solution.py:576
  4.4 2.6 %collective-permute-start = (bf16[128,2048]{1,0:T(8,128)(2,1)}, bf16[128,2048]{1,0:T(8,128)(2,1)}, u32[]{:S(2)}, u32[]{:S(2)}) collective-permute-start(bf16[128,2048]{1,0:T(8,128)(2,1)} %bitcast.4.q_outgrad.b0), channel_id=1, source_target_pairs={{0,8},{4,12},{8,0},{12,4},{1,9},{5,13},{9,1},{13,5},{2,10},{6,14},... | collective-permute-start | bytes 1572872 | tf_op jit(solution)/shard_map/ppermute | solution.py:559
  7.0 1.6 collective-permute-start.4
  8.6 1.5 copy-done.1
  10.1 1.2 copy-done.4
  11.3 1.2 copy-done.9
  12.5 1.2 copy-done.11
  13.7 1.2 copy-done.17
  14.9 1.0 copy-done.18
  15.9 1.0 copy-done.19
  18.8 4.9 %shard_map.154 = (f32[384,128]{1,0:T(8,128)S(1)}, f32[384,64]{1,0:T(8,128)S(1)}) custom-call(bf16[256,2048]{1,0:T(8,128)(2,1)S(1)} %bitcast.39, bf16[128,2048]{1,0:T(8,128)(2,1)S(1)} %bitcast.40, bf16[256,2048]{1,0:T(8,128)(2,1)S(1)} %bitcast.34, bf16[128,2048]{1,0:T(8,128)(2,1)} %bitcast.4.q_outgrad.b0, bf16[64,2048]{1,0:T(8,128)(2,1)S(1)} %copy-done.20, ...), custom_call_target="tpu_custom_call" | custom-call | flops 1024 | bytes 1024 | tf_op jit(solution)/shard_map/pallas_call | solution.py:396
  23.7 7.1 %collective-permute-done.b3.b4 = bf16[128,2048]{1,0:T(8,128)(2,1)} collective-permute-done((bf16[128,2048]{1,0:T(8,128)(2,1)}, bf16[128,2048]{1,0:T(8,128)(2,1)}, u32[]{:S(2)}, u32[]{:S(2)}) %collective-permute-start) | collective-permute-done | bytes 524320 | tf_op jit(solution)/shard_map/ppermute | solution.py:559
  31.0 1.9 collective-permute-start.6
  35.4 10.3 %collective-permute-start.2 = (bf16[128,2048]{1,0:T(8,128)(2,1)S(1)}, bf16[128,2048]{1,0:T(8,128)(2,1)S(1)}, u32[]{:S(2)}, u32[]{:S(2)}) collective-permute-start(bf16[128,2048]{1,0:T(8,128)(2,1)S(1)} %bitcast.42), channel_id=1, source_target_pairs={{0,8},{4,12},{8,0},{12,4},{1,9},{5,13},{9,1},{13,5},{2,10},{6,14},... | collective-permute-start | bytes 1572872 | tf_op jit(solution)/shard_map/ppermute | solution.py:559
  45.7 11.6 %collective-permute-done.6.b5 = bf16[128,2048]{1,0:T(8,128)(2,1)} collective-permute-done((bf16[128,2048]{1,0:T(8,128)(2,1)}, bf16[128,2048]{1,0:T(8,128)(2,1)}, u32[]{:S(2)}, u32[]{:S(2)}) %collective-permute-start.6) | collective-permute-done | bytes 524320 | tf_op jit(solution)/shard_map/ppermute | solution.py:563
  57.2 1.5 select_bitcast_fusion.5
  59.5 6.3 %collective-permute-done.2.b3.b4 = bf16[128,2048]{1,0:T(8,128)(2,1)S(1)} collective-permute-done((bf16[128,2048]{1,0:T(8,128)(2,1)S(1)}, bf16[128,2048]{1,0:T(8,128)(2,1)S(1)}, u32[]{:S(2)}, u32[]{:S(2)}) %collective-permute-start.2) | collective-permute-done | bytes 524320 | tf_op jit(solution)/shard_map/ppermute | solution.py:559
  65.8 2.1 %collective-permute-done.10.b1 = bf16[128,2048]{1,0:T(8,128)(2,1)S(1)} collective-permute-done((bf16[128,2048]{1,0:T(8,128)(2,1)S(1)}, bf16[128,2048]{1,0:T(8,128)(2,1)S(1)}, u32[]{:S(2)}, u32[]{:S(2)}) %collective-permute-start.10) | collective-permute-done | bytes 524320 | tf_op jit(solution)/shard_map/ppermute | solution.py:559
  68.0 2.2 %collective-permute-start.11 = (bf16[128,2048]{1,0:T(8,128)(2,1)S(1)}, bf16[128,2048]{1,0:T(8,128)(2,1)S(1)}, u32[]{:S(2)}, u32[]{:S(2)}) collective-permute-start(bf16[128,2048]{1,0:T(8,128)(2,1)S(1)} %collective-permute-done.2.b3.b4), channel_id=1, source_target_pairs={{0,4},{4,0},{8,12},{12,8},{1,5},{5,1},{9,13},{13,9},{2,6},{6,2},{1... | collective-permute-start | bytes 1572872 | tf_op jit(solution)/shard_map/ppermute | solution.py:563
  70.2 2.2 %collective-permute-start.14 = (bf16[128,2048]{1,0:T(8,128)(2,1)}, bf16[128,2048]{1,0:T(8,128)(2,1)}, u32[]{:S(2)}, u32[]{:S(2)}) collective-permute-start(bf16[128,2048]{1,0:T(8,128)(2,1)} %bitcast.9.b0), channel_id=1, source_target_pairs={{0,4},{4,0},{8,12},{12,8},{1,5},{5,1},{9,13},{13,9},{2,6},{6,2},{1... | collective-permute-start | bytes 1572872 | tf_op jit(solution)/shard_map/ppermute | solution.py:559
  72.4 4.6 %shard_map.155 = (bf16[3584,256]{1,0:T(8,128)(2,1)S(1)}, bf16[3584,256]{1,0:T(8,128)(2,1)S(1)}) custom-call(bf16[256,3584]{1,0:T(8,128)(2,1)S(1)} %bitcast.29, bf16[256,3584]{1,0:T(8,128)(2,1)S(1)} %bitcast.32, bf16[128,3584]{1,0:T(8,128)(2,1)S(1)} %collective-permute-done.1.far_gate, bf16[128,3584]{1,0:T(8,128)(2,1)} %collective-permute-done.7.far_up), custom_call_target="tpu_custom_call" | custom-call | flops 1024 | bytes 1024 | tf_op jit(solution)/shard_map/pallas_call | solution.py:295
  77.0 5.9 %collective-permute-done.11.b5 = bf16[128,2048]{1,0:T(8,128)(2,1)S(1)} collective-permute-done((bf16[128,2048]{1,0:T(8,128)(2,1)S(1)}, bf16[128,2048]{1,0:T(8,128)(2,1)S(1)}, u32[]{:S(2)}, u32[]{:S(2)}) %collective-permute-start.11) | collective-permute-done | bytes 524320 | tf_op jit(solution)/shard_map/ppermute | solution.py:563
  83.0 1.6 collective-permute-start.3
  85.5 1.1 pad_maximum_fusion.1
  87.7 14.3 %shard_map.156 = (f32[3584,128]{1,0:T(8,128)}, bf16[3584,128]{1,0:T(8,128)(2,1)}) custom-call(s32[2]{0:T(128)} %pad_add_fusion.flags, bf16[128,2048]{1,0:T(8,128)(2,1)} %bitcast.4.q_outgrad.b0, bf16[128,2048]{1,0:T(8,128)(2,1)} %copy-done.30, bf16[128,2048]{1,0:T(8,128)(2,1)} %collective-permute-done.5.b2, bf16[128,2048]{1,0:T(8,128)(2,1)} %collective-permute-done.b3.b4, ...), custom_call_target="tpu_custom_call" | custom-call | flops 1024 | bytes 1024 | tf_op jit(solution)/shard_map/pallas_call | solution.py:241
  102.1 4.3 %collective-permute-done.3.b3.b4 = bf16[128,2048]{1,0:T(8,128)(2,1)S(1)} collective-permute-done((bf16[128,2048]{1,0:T(8,128)(2,1)}, bf16[128,2048]{1,0:T(8,128)(2,1)S(1)}, u32[]{:S(2)}, u32[]{:S(2)}) %collective-permute-start.3) | collective-permute-done | bytes 524320 | tf_op jit(solution)/shard_map/ppermute | solution.py:559
  106.4 1.7 collective-permute-start.15
  108.1 1.6 collective-permute-done.18.far
  110.3 10.5 %collective-permute-done.15.b5 = bf16[128,2048]{1,0:T(8,128)(2,1)S(1)} collective-permute-done((bf16[128,2048]{1,0:T(8,128)(2,1)S(1)}, bf16[128,2048]{1,0:T(8,128)(2,1)S(1)}, u32[]{:S(2)}, u32[]{:S(2)}) %collective-permute-start.15) | collective-permute-done | bytes 524320 | tf_op jit(solution)/shard_map/ppermute | solution.py:563
  121.5 1.1 pad_maximum_fusion.2
  122.7 1.3 collective-permute-start.21
  124.0 14.3 %shard_map.157 = (f32[3584,128]{1,0:T(8,128)}, bf16[3584,128]{1,0:T(8,128)(2,1)}) custom-call(s32[2]{0:T(128)} %pad_add_fusion.flags, bf16[128,2048]{1,0:T(8,128)(2,1)} %bitcast.45, bf16[128,2048]{1,0:T(8,128)(2,1)} %copy-done.31, bf16[128,2048]{1,0:T(8,128)(2,1)} %copy-done.33, bf16[128,2048]{1,0:T(8,128)(2,1)} %copy-done.28, bf16[128,2048]{1,0:T(8,128)(2,1)} %copy-done.28, ...), custom_call_target="tpu_custom_call" | custom-call | flops 1024 | bytes 1024 | tf_op jit(solution)/shard_map/pallas_call | solution.py:241
  138.4 1.0 collective-permute-start.22
  139.8 1.5 copy-done.16
  141.2 2.4 %shard_map.158 = f32[128,128]{1,0:T(8,128)S(1)} custom-call(f32[3584,128]{1,0:T(8,128)S(1)} %copy-done.16, bf16[3584,128]{1,0:T(8,128)(2,1)} %collective-permute-done.19.returned, bf16[128,3584]{1,0:T(8,128)(2,1)S(1)} %bitcast.36, bf16[128,3584]{1,0:T(8,128)(2,1)S(1)} %bitcast.38, bf16[64,3584]{1,0:T(8,128)(2,1)S(1)} %copy-done.5, bf16[64,3584]{1,0:T(8,128)(2,1)S(1)} %copy-done.7), custom_call_target="tpu_custom_call" | custom-call | flops 1024 | bytes 1024 | tf_op jit(solution)/shard_map/pallas_call | solution.py:268
  143.7 1.8 collective-permute-start.20
  145.6 4.0 %collective-permute-start.17 = (f32[384,128]{1,0:T(8,128)S(1)}, f32[384,128]{1,0:T(8,128)S(1)}, u32[]{:S(2)}, u32[]{:S(2)}) collective-permute-start(f32[384,128]{1,0:T(8,128)S(1)} %add.32), channel_id=1, source_target_pairs={{0,8},{4,12},{8,0},{12,4},{1,9},{5,13},{9,1},{13,5},{2,10},{6,14},... | collective-permute-start | bytes 589832 | tf_op jit(solution)/shard_map/ppermute | solution.py:614
  149.6 6.0 %collective-permute-start.24 = (f32[128,192]{1,0:T(8,128)S(1)}, f32[128,192]{1,0:T(8,128)S(1)}, u32[]{:S(2)}, u32[]{:S(2)}) collective-permute-start(f32[128,192]{1,0:T(8,128)S(1)} %fusion), channel_id=1, source_target_pairs={{0,8},{4,12},{8,0},{12,4},{1,9},{5,13},{9,1},{13,5},{2,10},{6,14},... | collective-permute-start | bytes 294920 | tf_op jit(solution)/shard_map/ppermute | solution.py:615
  155.8 18.3 %shard_map.159 = (f32[128,128]{1,0:T(8,128)}, f32[128,128]{1,0:T(8,128)}) custom-call(s32[2]{0:T(128)} %pad_add_fusion.flags, bf16[128,2048]{1,0:T(8,128)(2,1)} %bitcast.9.b0, bf16[128,2048]{1,0:T(8,128)(2,1)} %collective-permute-done.14.b1, bf16[128,2048]{1,0:T(8,128)(2,1)} %copy-done.34, bf16[128,2048]{1,0:T(8,128)(2,1)} %copy-done.27, ...), custom_call_target="tpu_custom_call" | custom-call | flops 1024 | bytes 1024 | tf_op jit(solution)/shard_map/pallas_call | solution.py:337
  175.2 1.8 collective-permute-start.25
  177.4 1.5 copy-done.13
  178.9 1.6 shard_map.160.early
  180.4 4.6 %collective-permute-done.23.far = f32[128,128]{1,0:T(8,128)S(1)} collective-permute-done((f32[128,128]{1,0:T(8,128)}, f32[128,128]{1,0:T(8,128)S(1)}, u32[]{:S(2)}, u32[]{:S(2)}) %collective-permute-start.23) | collective-permute-done | bytes 65568 | tf_op jit(solution)/shard_map/ppermute | solution.py:621
  185.0 1.4 shard_map.162
  186.5 3.0 %collective-permute-start.30 = (f32[4,8]{1,0:T(4,128)S(1)}, f32[4,8]{1,0:T(4,128)S(1)}, u32[]{:S(2)}, u32[]{:S(2)}) collective-permute-start(f32[4,8]{1,0:T(4,128)S(1)} %shard_map.162), channel_id=1, source_target_pairs={{0,12},{4,8},{8,4},{12,0},{1,13},{5,9},{9,5},{13,1},{2,14},{6,10},... | collective-permute-start | bytes 392 | tf_op jit(solution)/shard_map/ppermute | solution.py:623
  190.9 1.0 collective-permute-done.30
  191.9 2.0 %collective-permute-done.29 = f32[4,8]{1,0:T(4,128)S(1)} collective-permute-done((f32[4,8]{1,0:T(4,128)S(1)}, f32[4,8]{1,0:T(4,128)S(1)}, u32[]{:S(2)}, u32[]{:S(2)}) %collective-permute-start.29) | collective-permute-done | bytes 160 | tf_op jit(solution)/shard_map/ppermute | solution.py:623
  (117 shorter events, 13.3 us)
Async XLA Ops:
  0.0 8.6 %copy-start = (bf16[4,64,3584]{2,1,0:T(8,128)(2,1)S(1)}, bf16[4,64,3584]{2,1,0:T(8,128)(2,1)}, u32[]{:S(2)}) copy-start(bf16[4,64,3584]{2,1,0:T(8,128)(2,1)} %param.17) | copy-start | bytes 5505028
  0.0 87.7 %collective-permute-start.12 = (bf16[3584,2048]{1,0:T(8,128)(2,1)}, bf16[3584,2048]{1,0:T(8,128)(2,1)}, u32[]{:S(2)}, u32[]{:S(2)}) collective-permute-start(bf16[3584,2048]{1,0:T(8,128)(2,1)} %weight_own.5), channel_id=1, source_target_pairs={{0,1},{1,0},{2,3},{3,2},{4,5},{5,4},{6,7},{7,6},{8,9},{9,8},{10,11... | collective-permute-start | bytes 44040200 | tf_op jit(solution)/shard_map/ppermute | solution.py:574
  1.8 32.0 %collective-permute-start.1 = (bf16[128,3584]{1,0:T(8,128)(2,1)S(1)}, bf16[128,3584]{1,0:T(8,128)(2,1)S(1)}, u32[]{:S(2)}, u32[]{:S(2)}) collective-permute-start(bf16[128,3584]{1,0:T(8,128)(2,1)S(1)} %bitcast.46), channel_id=1, source_target_pairs={{0,2},{1,3},{2,0},{3,1},{4,6},{5,7},{6,4},{7,5},{8,10},{9,11},{10,... | collective-permute-start | bytes 2752520 | tf_op jit(solution)/shard_map/ppermute | solution.py:576
  4.4 26.5 %collective-permute-start = (bf16[128,2048]{1,0:T(8,128)(2,1)}, bf16[128,2048]{1,0:T(8,128)(2,1)}, u32[]{:S(2)}, u32[]{:S(2)}) collective-permute-start(bf16[128,2048]{1,0:T(8,128)(2,1)} %bitcast.4.q_outgrad.b0), channel_id=1, source_target_pairs={{0,8},{4,12},{8,0},{12,4},{1,9},{5,13},{9,1},{13,5},{2,10},{6,14},... | collective-permute-start | bytes 1572872 | tf_op jit(solution)/shard_map/ppermute | solution.py:559
  7.0 24.0 %collective-permute-start.4 = (bf16[128,2048]{1,0:T(8,128)(2,1)}, bf16[128,2048]{1,0:T(8,128)(2,1)S(1)}, u32[]{:S(2)}, u32[]{:S(2)}) collective-permute-start(bf16[128,2048]{1,0:T(8,128)(2,1)} %bitcast.4.q_outgrad.b0), channel_id=1, source_target_pairs={{0,4},{4,0},{8,12},{12,8},{1,5},{5,1},{9,13},{13,9},{2,6},{6,2},{1... | collective-permute-start | bytes 1572872 | tf_op jit(solution)/shard_map/ppermute | solution.py:559
  23.7 11.6 %copy-start.22 = (f32[384,128]{1,0:T(8,128)}, f32[384,128]{1,0:T(8,128)S(1)}, u32[]{:S(2)}) copy-start(f32[384,128]{1,0:T(8,128)S(1)} %get-tuple-element.55) | copy-start | bytes 589828
  31.0 4.4 %collective-permute-start.5 = (bf16[128,2048]{1,0:T(8,128)(2,1)}, bf16[128,2048]{1,0:T(8,128)(2,1)}, u32[]{:S(2)}, u32[]{:S(2)}) collective-permute-start(bf16[128,2048]{1,0:T(8,128)(2,1)} %bitcast.4.q_outgrad.b0), channel_id=1, source_target_pairs={{0,1},{1,0},{2,3},{3,2},{4,8},{5,9},{6,10},{7,11},{8,4},{9,5},{10,... | collective-permute-start | bytes 1572872 | tf_op jit(solution)/shard_map/ppermute | solution.py:562
  31.0 26.3 %collective-permute-start.6 = (bf16[128,2048]{1,0:T(8,128)(2,1)}, bf16[128,2048]{1,0:T(8,128)(2,1)}, u32[]{:S(2)}, u32[]{:S(2)}) collective-permute-start(bf16[128,2048]{1,0:T(8,128)(2,1)} %collective-permute-done.b3.b4), channel_id=1, source_target_pairs={{0,4},{4,0},{8,12},{12,8},{1,5},{5,1},{9,13},{13,9},{2,6},{6,2},{1... | collective-permute-start | bytes 1572872 | tf_op jit(solution)/shard_map/ppermute | solution.py:563
  33.8 25.0 %collective-permute-start.7 = (bf16[128,3584]{1,0:T(8,128)(2,1)}, bf16[128,3584]{1,0:T(8,128)(2,1)}, u32[]{:S(2)}, u32[]{:S(2)}) collective-permute-start(bf16[128,3584]{1,0:T(8,128)(2,1)} %bitcast.16), channel_id=1, source_target_pairs={{0,2},{1,3},{2,0},{3,1},{4,6},{5,7},{6,4},{7,5},{8,10},{9,11},{10,... | collective-permute-start | bytes 2752520 | tf_op jit(solution)/shard_map/ppermute | solution.py:584
  35.3 49.3 %copy-start.29 = (bf16[2,64,2048]{2,1,0:T(8,128)(2,1)}, bf16[2,64,2048]{2,1,0:T(8,128)(2,1)S(1)}, u32[]{:S(2)}) copy-start(bf16[2,64,2048]{2,1,0:T(8,128)(2,1)S(1)} %get-tuple-element.69) | copy-start | bytes 1572868
  35.3 32.7 %collective-permute-start.10 = (bf16[128,2048]{1,0:T(8,128)(2,1)S(1)}, bf16[128,2048]{1,0:T(8,128)(2,1)S(1)}, u32[]{:S(2)}, u32[]{:S(2)}) collective-permute-start(bf16[128,2048]{1,0:T(8,128)(2,1)S(1)} %bitcast.41), channel_id=1, source_target_pairs={{0,4},{4,0},{8,12},{12,8},{1,5},{5,1},{9,13},{13,9},{2,6},{6,2},{1... | collective-permute-start | bytes 1572872 | tf_op jit(solution)/shard_map/ppermute | solution.py:559
  35.4 30.5 %collective-permute-start.2 = (bf16[128,2048]{1,0:T(8,128)(2,1)S(1)}, bf16[128,2048]{1,0:T(8,128)(2,1)S(1)}, u32[]{:S(2)}, u32[]{:S(2)}) collective-permute-start(bf16[128,2048]{1,0:T(8,128)(2,1)S(1)} %bitcast.42), channel_id=1, source_target_pairs={{0,8},{4,12},{8,0},{12,4},{1,9},{5,13},{9,1},{13,5},{2,10},{6,14},... | collective-permute-start | bytes 1572872 | tf_op jit(solution)/shard_map/ppermute | solution.py:559
  58.7 13.7 %copy-start.2 = (bf16[4,64,3584]{2,1,0:T(8,128)(2,1)S(1)}, bf16[4,64,3584]{2,1,0:T(8,128)(2,1)}, u32[]{:S(2)}) copy-start(bf16[4,64,3584]{2,1,0:T(8,128)(2,1)} %param.18) | copy-start | bytes 5505028
  58.8 25.8 %collective-permute-start.8 = (bf16[2,128,2048]{2,1,0:T(8,128)(2,1)S(1)}, bf16[2,128,2048]{2,1,0:T(8,128)(2,1)S(1)}, u32[]{:S(2)}, u32[]{:S(2)}) collective-permute-start(bf16[2,128,2048]{2,1,0:T(8,128)(2,1)S(1)} %pad_maximum_fusion), channel_id=1, source_target_pairs={{0,2},{1,3},{2,0},{3,1},{4,6},{5,7},{6,4},{7,5},{8,10},{9,11},{10,... | collective-permute-start | bytes 3145736 | tf_op jit(solution)/shard_map/ppermute | solution.py:586
  65.8 18.8 %copy-start.28 = (bf16[128,2048]{1,0:T(8,128)(2,1)}, bf16[128,2048]{1,0:T(8,128)(2,1)S(1)}, u32[]{:S(2)}) copy-start(bf16[128,2048]{1,0:T(8,128)(2,1)S(1)} %collective-permute-done.2.b3.b4) | copy-start | bytes 1572868
  68.0 16.7 %copy-start.31 = (bf16[128,2048]{1,0:T(8,128)(2,1)}, bf16[128,2048]{1,0:T(8,128)(2,1)S(1)}, u32[]{:S(2)}) copy-start(bf16[128,2048]{1,0:T(8,128)(2,1)S(1)} %collective-permute-done.10.b1) | copy-start | bytes 1572868
  68.0 15.0 %collective-permute-start.11 = (bf16[128,2048]{1,0:T(8,128)(2,1)S(1)}, bf16[128,2048]{1,0:T(8,128)(2,1)S(1)}, u32[]{:S(2)}, u32[]{:S(2)}) collective-permute-start(bf16[128,2048]{1,0:T(8,128)(2,1)S(1)} %collective-permute-done.2.b3.b4), channel_id=1, source_target_pairs={{0,4},{4,0},{8,12},{12,8},{1,5},{5,1},{9,13},{13,9},{2,6},{6,2},{1... | collective-permute-start | bytes 1572872 | tf_op jit(solution)/shard_map/ppermute | solution.py:563
  70.2 14.5 %collective-permute-start.9 = (bf16[128,2048]{1,0:T(8,128)(2,1)S(1)}, bf16[128,2048]{1,0:T(8,128)(2,1)S(1)}, u32[]{:S(2)}, u32[]{:S(2)}) collective-permute-start(bf16[128,2048]{1,0:T(8,128)(2,1)S(1)} %bitcast.43), channel_id=1, source_target_pairs={{0,1},{1,0},{2,3},{3,2},{4,8},{5,9},{6,10},{7,11},{8,4},{9,5},{10,... | collective-permute-start | bytes 1572872 | tf_op jit(solution)/shard_map/ppermute | solution.py:562
  70.2 36.2 %collective-permute-start.14 = (bf16[128,2048]{1,0:T(8,128)(2,1)}, bf16[128,2048]{1,0:T(8,128)(2,1)}, u32[]{:S(2)}, u32[]{:S(2)}) collective-permute-start(bf16[128,2048]{1,0:T(8,128)(2,1)} %bitcast.9.b0), channel_id=1, source_target_pairs={{0,4},{4,0},{8,12},{12,8},{1,5},{5,1},{9,13},{13,9},{2,6},{6,2},{1... | collective-permute-start | bytes 1572872 | tf_op jit(solution)/shard_map/ppermute | solution.py:559
  77.0 7.8 %copy-start.14 = (bf16[3584,256]{1,0:T(8,128)(2,1)}, bf16[3584,256]{1,0:T(8,128)(2,1)S(1)}, u32[]{:S(2)}) copy-start(bf16[3584,256]{1,0:T(8,128)(2,1)S(1)} %get-tuple-element.48.gates) | copy-start | bytes 5505028
  77.0 7.8 %copy-start.15 = (bf16[3584,256]{1,0:T(8,128)(2,1)}, bf16[3584,256]{1,0:T(8,128)(2,1)S(1)}, u32[]{:S(2)}) copy-start(bf16[3584,256]{1,0:T(8,128)(2,1)S(1)} %get-tuple-element.63.ups) | copy-start | bytes 5505028
  83.0 23.4 %collective-permute-start.3 = (bf16[128,2048]{1,0:T(8,128)(2,1)}, bf16[128,2048]{1,0:T(8,128)(2,1)S(1)}, u32[]{:S(2)}, u32[]{:S(2)}) collective-permute-start(bf16[128,2048]{1,0:T(8,128)(2,1)} %bitcast.9.b0), channel_id=1, source_target_pairs={{0,8},{4,12},{8,0},{12,4},{1,9},{5,13},{9,1},{13,5},{2,10},{6,14},... | collective-permute-start | bytes 1572872 | tf_op jit(solution)/shard_map/ppermute | solution.py:559
  86.6 23.1 %collective-permute-start.18 = (bf16[2,128,2048]{2,1,0:T(8,128)(2,1)}, bf16[2,128,2048]{2,1,0:T(8,128)(2,1)}, u32[]{:S(2)}, u32[]{:S(2)}) collective-permute-start(bf16[2,128,2048]{2,1,0:T(8,128)(2,1)} %pad_maximum_fusion.1), channel_id=1, source_target_pairs={{0,2},{1,3},{2,0},{3,1},{4,6},{5,7},{6,4},{7,5},{8,10},{9,11},{10,... | collective-permute-start | bytes 3145736 | tf_op jit(solution)/shard_map/ppermute | solution.py:592
  106.4 14.5 %copy-start.27 = (bf16[128,2048]{1,0:T(8,128)(2,1)}, bf16[128,2048]{1,0:T(8,128)(2,1)S(1)}, u32[]{:S(2)}) copy-start(bf16[128,2048]{1,0:T(8,128)(2,1)S(1)} %collective-permute-done.3.b3.b4) | copy-start | bytes 1572868
  106.4 3.9 %collective-permute-start.13 = (bf16[128,2048]{1,0:T(8,128)(2,1)}, bf16[128,2048]{1,0:T(8,128)(2,1)S(1)}, u32[]{:S(2)}, u32[]{:S(2)}) collective-permute-start(bf16[128,2048]{1,0:T(8,128)(2,1)} %bitcast.9.b0), channel_id=1, source_target_pairs={{0,1},{1,0},{2,3},{3,2},{4,8},{5,9},{6,10},{7,11},{8,4},{9,5},{10,... | collective-permute-start | bytes 1572872 | tf_op jit(solution)/shard_map/ppermute | solution.py:562
  106.4 14.3 %collective-permute-start.15 = (bf16[128,2048]{1,0:T(8,128)(2,1)S(1)}, bf16[128,2048]{1,0:T(8,128)(2,1)S(1)}, u32[]{:S(2)}, u32[]{:S(2)}) collective-permute-start(bf16[128,2048]{1,0:T(8,128)(2,1)S(1)} %collective-permute-done.3.b3.b4), channel_id=1, source_target_pairs={{0,4},{4,0},{8,12},{12,8},{1,5},{5,1},{9,13},{13,9},{2,6},{6,2},{1... | collective-permute-start | bytes 1572872 | tf_op jit(solution)/shard_map/ppermute | solution.py:563
  109.7 30.0 %collective-permute-start.19 = (bf16[3584,128]{1,0:T(8,128)(2,1)}, bf16[3584,128]{1,0:T(8,128)(2,1)}, u32[]{:S(2)}, u32[]{:S(2)}) collective-permute-start(bf16[3584,128]{1,0:T(8,128)(2,1)} %get-tuple-element.57), channel_id=1, source_target_pairs={{0,2},{1,3},{2,0},{3,1},{4,6},{5,7},{6,4},{7,5},{8,10},{9,11},{10,... | collective-permute-start | bytes 2752520 | tf_op jit(solution)/shard_map/ppermute | solution.py:596
  110.3 10.7 %copy-start.34 = (bf16[128,2048]{1,0:T(8,128)(2,1)}, bf16[128,2048]{1,0:T(8,128)(2,1)S(1)}, u32[]{:S(2)}) copy-start(bf16[128,2048]{1,0:T(8,128)(2,1)S(1)} %collective-permute-done.13.b2) | copy-start | bytes 1572868
  122.7 16.7 %copy-start.23 = (f32[384,128]{1,0:T(8,128)S(1)}, f32[384,128]{1,0:T(8,128)}, u32[]{:S(2)}) copy-start(f32[384,128]{1,0:T(8,128)} %copy-done.22) | copy-start | bytes 589828
  122.7 17.0 %copy-start.5 = (bf16[64,3584]{1,0:T(8,128)(2,1)S(1)}, bf16[64,3584]{1,0:T(8,128)(2,1)}, u32[]{:S(2)}) copy-start(bf16[64,3584]{1,0:T(8,128)(2,1)} %proj_gate.5) | copy-start | bytes 1376260
  122.7 17.0 %copy-start.7 = (bf16[64,3584]{1,0:T(8,128)(2,1)S(1)}, bf16[64,3584]{1,0:T(8,128)(2,1)}, u32[]{:S(2)}) copy-start(bf16[64,3584]{1,0:T(8,128)(2,1)} %proj_up.5) | copy-start | bytes 1376260
  122.7 17.0 %copy-start.10 = (bf16[2,64,3584]{2,1,0:T(8,128)(2,1)S(1)}, bf16[2,64,3584]{2,1,0:T(8,128)(2,1)}, u32[]{:S(2)}) copy-start(bf16[2,64,3584]{2,1,0:T(8,128)(2,1)} %param.22) | copy-start | bytes 2752516
  122.7 17.0 %copy-start.12 = (bf16[2,64,3584]{2,1,0:T(8,128)(2,1)S(1)}, bf16[2,64,3584]{2,1,0:T(8,128)(2,1)}, u32[]{:S(2)}) copy-start(bf16[2,64,3584]{2,1,0:T(8,128)(2,1)} %param.23) | copy-start | bytes 2752516
  122.7 33.1 %collective-permute-start.21 = (bf16[2,128,2048]{2,1,0:T(8,128)(2,1)}, bf16[2,128,2048]{2,1,0:T(8,128)(2,1)}, u32[]{:S(2)}, u32[]{:S(2)}) collective-permute-start(bf16[2,128,2048]{2,1,0:T(8,128)(2,1)} %pad_maximum_fusion.2), channel_id=1, source_target_pairs={{0,2},{1,3},{2,0},{3,1},{4,6},{5,7},{6,4},{7,5},{8,10},{9,11},{10,... | collective-permute-start | bytes 3145736 | tf_op jit(solution)/shard_map/ppermute | solution.py:599
  138.4 39.0 %collective-permute-start.22 = (bf16[3584,128]{1,0:T(8,128)(2,1)}, bf16[3584,128]{1,0:T(8,128)(2,1)S(1)}, u32[]{:S(2)}, u32[]{:S(2)}) collective-permute-start(bf16[3584,128]{1,0:T(8,128)(2,1)} %get-tuple-element.59), channel_id=1, source_target_pairs={{0,2},{1,3},{2,0},{3,1},{4,6},{5,7},{6,4},{7,5},{8,10},{9,11},{10,... | collective-permute-start | bytes 2752520 | tf_op jit(solution)/shard_map/ppermute | solution.py:603
  139.4 6.2 %collective-permute-start.16 = (f32[384,128]{1,0:T(8,128)S(1)}, f32[384,128]{1,0:T(8,128)S(1)}, u32[]{:S(2)}, u32[]{:S(2)}) collective-permute-start(f32[384,128]{1,0:T(8,128)S(1)} %copy-done.23), channel_id=1, source_target_pairs={{0,4},{4,0},{8,12},{12,8},{1,5},{5,1},{9,13},{13,9},{2,6},{6,2},{1... | collective-permute-start | bytes 589832 | tf_op jit(solution)/shard_map/ppermute | solution.py:604
  143.7 5.9 %collective-permute-start.20 = (f32[128,192]{1,0:T(8,128)S(1)}, f32[128,192]{1,0:T(8,128)S(1)}, u32[]{:S(2)}, u32[]{:S(2)}) collective-permute-start(f32[128,192]{1,0:T(8,128)S(1)} %pad_maximum_fusion.3), channel_id=1, source_target_pairs={{0,4},{4,0},{8,12},{12,8},{1,5},{5,1},{9,13},{13,9},{2,6},{6,2},{1... | collective-permute-start | bytes 294920 | tf_op jit(solution)/shard_map/ppermute | solution.py:609
  145.6 28.6 %collective-permute-start.17 = (f32[384,128]{1,0:T(8,128)S(1)}, f32[384,128]{1,0:T(8,128)S(1)}, u32[]{:S(2)}, u32[]{:S(2)}) collective-permute-start(f32[384,128]{1,0:T(8,128)S(1)} %add.32), channel_id=1, source_target_pairs={{0,8},{4,12},{8,0},{12,4},{1,9},{5,13},{9,1},{13,5},{2,10},{6,14},... | collective-permute-start | bytes 589832 | tf_op jit(solution)/shard_map/ppermute | solution.py:614
  149.6 24.5 %collective-permute-start.24 = (f32[128,192]{1,0:T(8,128)S(1)}, f32[128,192]{1,0:T(8,128)S(1)}, u32[]{:S(2)}, u32[]{:S(2)}) collective-permute-start(f32[128,192]{1,0:T(8,128)S(1)} %fusion), channel_id=1, source_target_pairs={{0,8},{4,12},{8,0},{12,4},{1,9},{5,13},{9,1},{13,5},{2,10},{6,14},... | collective-permute-start | bytes 294920 | tf_op jit(solution)/shard_map/ppermute | solution.py:615
  155.8 18.4 %copy-start.25 = (s32[2]{0:T(128)S(1)}, s32[2]{0:T(128)}, u32[]{:S(2)}) copy-start(s32[2]{0:T(128)} %lengths.2) | copy-start | bytes 28
  155.8 21.5 %copy-start.3 = (bf16[4,64,3584]{2,1,0:T(8,128)(2,1)S(1)}, bf16[4,64,3584]{2,1,0:T(8,128)(2,1)}, u32[]{:S(2)}) copy-start(bf16[4,64,3584]{2,1,0:T(8,128)(2,1)} %param.18) | copy-start | bytes 5505028
  175.1 9.9 %collective-permute-start.27 = (f32[2,192,64]{2,1,0:T(8,128)S(1)}, f32[2,192,64]{2,1,0:T(8,128)S(1)}, u32[]{:S(2)}, u32[]{:S(2)}) collective-permute-start(f32[2,192,64]{2,1,0:T(8,128)S(1)} %shard_map.161.q0), channel_id=1, source_target_pairs={{0,3},{1,2},{2,1},{3,0},{4,7},{5,6},{6,5},{7,4},{8,11},{9,10},{10,... | collective-permute-start | bytes 294920 | tf_op jit(solution)/shard_map/ppermute | solution.py:617
  175.2 9.9 %collective-permute-start.26 = (f32[2,192,64]{2,1,0:T(8,128)S(1)}, f32[2,192,64]{2,1,0:T(8,128)S(1)}, u32[]{:S(2)}, u32[]{:S(2)}) collective-permute-start(f32[2,192,64]{2,1,0:T(8,128)S(1)} %shard_map.161.q0), channel_id=1, source_target_pairs={{0,2},{1,3},{2,0},{3,1},{4,6},{5,7},{6,4},{7,5},{8,10},{9,11},{10,... | collective-permute-start | bytes 294920 | tf_op jit(solution)/shard_map/ppermute | solution.py:617
  175.2 9.8 %collective-permute-start.25 = (f32[2,192,64]{2,1,0:T(8,128)S(1)}, f32[2,192,64]{2,1,0:T(8,128)S(1)}, u32[]{:S(2)}, u32[]{:S(2)}) collective-permute-start(f32[2,192,64]{2,1,0:T(8,128)S(1)} %shard_map.161.q0), channel_id=1, source_target_pairs={{0,1},{1,0},{2,3},{3,2},{4,5},{5,4},{6,7},{7,6},{8,9},{9,8},{10,11... | collective-permute-start | bytes 294920 | tf_op jit(solution)/shard_map/ppermute | solution.py:617
  177.0 8.0 %collective-permute-start.23 = (f32[128,128]{1,0:T(8,128)}, f32[128,128]{1,0:T(8,128)S(1)}, u32[]{:S(2)}, u32[]{:S(2)}) collective-permute-start(f32[128,128]{1,0:T(8,128)} %get-tuple-element.67), channel_id=1, source_target_pairs={{0,2},{1,3},{2,0},{3,1},{4,6},{5,7},{6,4},{7,5},{8,10},{9,11},{10,... | collective-permute-start | bytes 196616 | tf_op jit(solution)/shard_map/ppermute | solution.py:621
  186.5 5.4 %collective-permute-start.30 = (f32[4,8]{1,0:T(4,128)S(1)}, f32[4,8]{1,0:T(4,128)S(1)}, u32[]{:S(2)}, u32[]{:S(2)}) collective-permute-start(f32[4,8]{1,0:T(4,128)S(1)} %shard_map.162), channel_id=1, source_target_pairs={{0,12},{4,8},{8,4},{12,0},{1,13},{5,9},{9,5},{13,1},{2,14},{6,10},... | collective-permute-start | bytes 392 | tf_op jit(solution)/shard_map/ppermute | solution.py:623
  189.5 4.5 %collective-permute-start.29 = (f32[4,8]{1,0:T(4,128)S(1)}, f32[4,8]{1,0:T(4,128)S(1)}, u32[]{:S(2)}, u32[]{:S(2)}) collective-permute-start(f32[4,8]{1,0:T(4,128)S(1)} %shard_map.162), channel_id=1, source_target_pairs={{0,8},{4,12},{8,0},{12,4},{1,9},{5,13},{9,1},{13,5},{2,10},{6,14},... | collective-permute-start | bytes 392 | tf_op jit(solution)/shard_map/ppermute | solution.py:623
  190.0 4.0 %collective-permute-start.28 = (f32[4,8]{1,0:T(4,128)S(1)}, f32[4,8]{1,0:T(4,128)S(1)}, u32[]{:S(2)}, u32[]{:S(2)}) collective-permute-start(f32[4,8]{1,0:T(4,128)S(1)} %shard_map.162), channel_id=1, source_target_pairs={{0,4},{4,0},{8,12},{12,8},{1,5},{5,1},{9,13},{13,9},{2,6},{6,2},{1... | collective-permute-start | bytes 392 | tf_op jit(solution)/shard_map/ppermute | solution.py:623
  (20 other events, 42.0 us)

commit v18 on v17

--- a/solution.py
+++ b/solution.py
@@ -526,7 +526,6 @@
 
     to_core = functools.partial(lax.ppermute, axis_name="dp", perm=[(i, i ^ 1) for i in range(4)])
     to_chip = functools.partial(lax.ppermute, axis_name="dp", perm=[(i, i ^ 2) for i in range(4)])
-    to_other = functools.partial(lax.ppermute, axis_name="dp", perm=[(i, i ^ 3) for i in range(4)])
     outer = functools.partial(
         lax.ppermute, axis_name="tensor", perm=[(i, i ^ 1) for i in range(4)]
     )
@@ -611,14 +610,16 @@
         after(flags, q_sums, in_out), b_blocks, b_far, weight_own, weight_sib, gates, ups,
         proj_gate, proj_up,
     )
+    b_far_sides = to_chip(b_away)
     in_out = in_out + after(across(in_out), b_near)
     q_sums = q_sums + after(across(q_sums), b_near)
     own_found = query_features(query_lengths, in_out[2 * cut :], q_sums)
-    found = (own_found, to_core(own_found), to_chip(own_found), to_other(own_found))
+    chip_found = to_chip(own_found)
+    found = (own_found, to_core(own_found), chip_found, to_core(after(chip_found, b_far_sides)))
     a_gradient = finished_sides(a_near_sum, a_returned, t_gate, t_up, proj_gate, proj_up)
     own_scores = partial_scores(
         train_lengths, place, in_out[: 2 * cut], hidden[: 2 * cut], a_gradient, b_near,
-        to_chip(b_away), found,
+        b_far_sides, found,
     )
     scores = own_scores + outer(own_scores) + across(own_scores) + opposite(own_scores)
     return scores / (RANK * SEQ)

time: 195 us -> 194 us (level)
  transfers between devices with their start and end apart: 31 -> 31, of which waited for: 14 -> 15; matrix products, arithmetic and copies ran while one was open for 4% -> 4% of each run, Pallas kernels for 32% -> 32%
where the time goes in v18:
time: 194 us; the launch traced here: 193 us
  Pallas kernels  62.7 us (32%)
  waiting for transfers between devices  56.3 us (29%)
  starting transfers between devices  50.6 us (26%)
  local copies, waits for them, and re-layouts  17.9 us (9%)
  other arithmetic  5.39 us (3%)
    pallas_call x2, Pallas kernels, partial_sums(): pl.pallas_call(partial_kernel, grid=(units // TILE,), in_specs=[SCALARS]...  28.7 us
    ppermute x3, waiting for transfers between devices, last_hops(): return (own, one, mid, two, two, outer(after(two, one)))  28 us
    ppermute x6, waiting for transfers between devices, first_hops(): return (own, outer(own), across(own))  20 us
    ppermute x6, starting transfers between devices, first_hops(): return (own, outer(own), across(own))  18.4 us
    pallas_call x1, Pallas kernels, lent_sides(): pl.pallas_call(lent_kernel, grid=(units // TILE,), in_specs=[SCALARS] + [...  18.3 us
    unnamed x74, local copies, waits for them, and re-layouts  14.6 us
    ppermute x1, starting transfers between devices, moving_plan(): q_sums = q_sums + after(across(q_sums), b_near)  6 us
    ppermute x3, starting transfers between devices, last_hops(): return (own, one, mid, two, two, outer(after(two, one)))  5.81 us
  transfers between devices with their start and end apart: 31, of which 15 were waited for; matrix products, arithmetic and copies ran while one was open for 4% of the time, Pallas kernels for 32%

profile of v18, /device:TPU:0, one launch (start us, length us, event | category | flops | bytes accessed | tf_op | source)
XLA Modules:
  0.0 193.3 jit_solution(193443126553928837)
XLA Ops:
  0.5 1.3 slice.40
  1.8 2.6 %collective-permute-start.1 = (bf16[128,3584]{1,0:T(8,128)(2,1)S(1)}, bf16[128,3584]{1,0:T(8,128)(2,1)S(1)}, u32[]{:S(2)}, u32[]{:S(2)}) collective-permute-start(bf16[128,3584]{1,0:T(8,128)(2,1)S(1)} %bitcast.46), channel_id=1, source_target_pairs={{0,2},{1,3},{2,0},{3,1},{4,6},{5,7},{6,4},{7,5},{8,10},{9,11},{10,... | collective-permute-start | bytes 2752520 | tf_op jit(solution)/shard_map/ppermute | solution.py:575
  4.4 2.6 %collective-permute-start = (bf16[128,2048]{1,0:T(8,128)(2,1)}, bf16[128,2048]{1,0:T(8,128)(2,1)}, u32[]{:S(2)}, u32[]{:S(2)}) collective-permute-start(bf16[128,2048]{1,0:T(8,128)(2,1)} %bitcast.4.q_outgrad.b0), channel_id=1, source_target_pairs={{0,8},{4,12},{8,0},{12,4},{1,9},{5,13},{9,1},{13,5},{2,10},{6,14},... | collective-permute-start | bytes 1572872 | tf_op jit(solution)/shard_map/ppermute | solution.py:558
  7.0 1.6 collective-permute-start.4
  8.6 1.5 copy-done.1
  10.1 1.2 copy-done.4
  11.3 1.2 copy-done.9
  12.5 1.2 copy-done.11
  13.7 1.2 copy-done.17
  14.9 1.0 copy-done.18
  15.9 1.0 copy-done.19
  18.8 4.9 %shard_map.154 = (f32[384,128]{1,0:T(8,128)S(1)}, f32[384,64]{1,0:T(8,128)S(1)}) custom-call(bf16[256,2048]{1,0:T(8,128)(2,1)S(1)} %bitcast.39, bf16[128,2048]{1,0:T(8,128)(2,1)S(1)} %bitcast.40, bf16[256,2048]{1,0:T(8,128)(2,1)S(1)} %bitcast.34, bf16[128,2048]{1,0:T(8,128)(2,1)} %bitcast.4.q_outgrad.b0, bf16[64,2048]{1,0:T(8,128)(2,1)S(1)} %copy-done.20, ...), custom_call_target="tpu_custom_call" | custom-call | flops 1024 | bytes 1024 | tf_op jit(solution)/shard_map/pallas_call | solution.py:396
  23.7 7.1 %collective-permute-done.b3.b4 = bf16[128,2048]{1,0:T(8,128)(2,1)} collective-permute-done((bf16[128,2048]{1,0:T(8,128)(2,1)}, bf16[128,2048]{1,0:T(8,128)(2,1)}, u32[]{:S(2)}, u32[]{:S(2)}) %collective-permute-start) | collective-permute-done | bytes 524320 | tf_op jit(solution)/shard_map/ppermute | solution.py:558
  31.0 1.9 collective-permute-start.6
  35.4 10.3 %collective-permute-start.2 = (bf16[128,2048]{1,0:T(8,128)(2,1)S(1)}, bf16[128,2048]{1,0:T(8,128)(2,1)S(1)}, u32[]{:S(2)}, u32[]{:S(2)}) collective-permute-start(bf16[128,2048]{1,0:T(8,128)(2,1)S(1)} %bitcast.42), channel_id=1, source_target_pairs={{0,8},{4,12},{8,0},{12,4},{1,9},{5,13},{9,1},{13,5},{2,10},{6,14},... | collective-permute-start | bytes 1572872 | tf_op jit(solution)/shard_map/ppermute | solution.py:558
  45.7 11.6 %collective-permute-done.6.b5 = bf16[128,2048]{1,0:T(8,128)(2,1)} collective-permute-done((bf16[128,2048]{1,0:T(8,128)(2,1)}, bf16[128,2048]{1,0:T(8,128)(2,1)}, u32[]{:S(2)}, u32[]{:S(2)}) %collective-permute-start.6) | collective-permute-done | bytes 524320 | tf_op jit(solution)/shard_map/ppermute | solution.py:562
  57.2 1.5 select_bitcast_fusion.5
  59.5 6.3 %collective-permute-done.2.b3.b4 = bf16[128,2048]{1,0:T(8,128)(2,1)S(1)} collective-permute-done((bf16[128,2048]{1,0:T(8,128)(2,1)S(1)}, bf16[128,2048]{1,0:T(8,128)(2,1)S(1)}, u32[]{:S(2)}, u32[]{:S(2)}) %collective-permute-start.2) | collective-permute-done | bytes 524320 | tf_op jit(solution)/shard_map/ppermute | solution.py:558
  65.8 2.1 %collective-permute-done.10.b1 = bf16[128,2048]{1,0:T(8,128)(2,1)S(1)} collective-permute-done((bf16[128,2048]{1,0:T(8,128)(2,1)S(1)}, bf16[128,2048]{1,0:T(8,128)(2,1)S(1)}, u32[]{:S(2)}, u32[]{:S(2)}) %collective-permute-start.10) | collective-permute-done | bytes 524320 | tf_op jit(solution)/shard_map/ppermute | solution.py:558
  68.0 2.2 %collective-permute-start.11 = (bf16[128,2048]{1,0:T(8,128)(2,1)S(1)}, bf16[128,2048]{1,0:T(8,128)(2,1)S(1)}, u32[]{:S(2)}, u32[]{:S(2)}) collective-permute-start(bf16[128,2048]{1,0:T(8,128)(2,1)S(1)} %collective-permute-done.2.b3.b4), channel_id=1, source_target_pairs={{0,4},{4,0},{8,12},{12,8},{1,5},{5,1},{9,13},{13,9},{2,6},{6,2},{1... | collective-permute-start | bytes 1572872 | tf_op jit(solution)/shard_map/ppermute | solution.py:562
  70.2 2.2 %collective-permute-start.14 = (bf16[128,2048]{1,0:T(8,128)(2,1)}, bf16[128,2048]{1,0:T(8,128)(2,1)}, u32[]{:S(2)}, u32[]{:S(2)}) collective-permute-start(bf16[128,2048]{1,0:T(8,128)(2,1)} %bitcast.9.b0), channel_id=1, source_target_pairs={{0,4},{4,0},{8,12},{12,8},{1,5},{5,1},{9,13},{13,9},{2,6},{6,2},{1... | collective-permute-start | bytes 1572872 | tf_op jit(solution)/shard_map/ppermute | solution.py:558
  72.4 4.6 %shard_map.155 = (bf16[3584,256]{1,0:T(8,128)(2,1)S(1)}, bf16[3584,256]{1,0:T(8,128)(2,1)S(1)}) custom-call(bf16[256,3584]{1,0:T(8,128)(2,1)S(1)} %bitcast.29, bf16[256,3584]{1,0:T(8,128)(2,1)S(1)} %bitcast.32, bf16[128,3584]{1,0:T(8,128)(2,1)S(1)} %collective-permute-done.1.far_gate, bf16[128,3584]{1,0:T(8,128)(2,1)} %collective-permute-done.7.far_up), custom_call_target="tpu_custom_call" | custom-call | flops 1024 | bytes 1024 | tf_op jit(solution)/shard_map/pallas_call | solution.py:295
  77.0 5.9 %collective-permute-done.11.b5 = bf16[128,2048]{1,0:T(8,128)(2,1)S(1)} collective-permute-done((bf16[128,2048]{1,0:T(8,128)(2,1)S(1)}, bf16[128,2048]{1,0:T(8,128)(2,1)S(1)}, u32[]{:S(2)}, u32[]{:S(2)}) %collective-permute-start.11) | collective-permute-done | bytes 524320 | tf_op jit(solution)/shard_map/ppermute | solution.py:562
  83.0 1.6 collective-permute-start.3
  85.5 1.1 pad_maximum_fusion.1
  87.7 14.3 %shard_map.156 = (f32[3584,128]{1,0:T(8,128)}, bf16[3584,128]{1,0:T(8,128)(2,1)}) custom-call(s32[2]{0:T(128)} %pad_add_fusion.flags, bf16[128,2048]{1,0:T(8,128)(2,1)} %bitcast.4.q_outgrad.b0, bf16[128,2048]{1,0:T(8,128)(2,1)} %copy-done.30, bf16[128,2048]{1,0:T(8,128)(2,1)} %collective-permute-done.5.b2, bf16[128,2048]{1,0:T(8,128)(2,1)} %collective-permute-done.b3.b4, ...), custom_call_target="tpu_custom_call" | custom-call | flops 1024 | bytes 1024 | tf_op jit(solution)/shard_map/pallas_call | solution.py:241
  102.1 4.3 %collective-permute-done.3.b3.b4 = bf16[128,2048]{1,0:T(8,128)(2,1)S(1)} collective-permute-done((bf16[128,2048]{1,0:T(8,128)(2,1)}, bf16[128,2048]{1,0:T(8,128)(2,1)S(1)}, u32[]{:S(2)}, u32[]{:S(2)}) %collective-permute-start.3) | collective-permute-done | bytes 524320 | tf_op jit(solution)/shard_map/ppermute | solution.py:558
  106.4 1.7 collective-permute-start.15
  108.1 1.6 collective-permute-done.18.far
  110.3 10.5 %collective-permute-done.15.b5 = bf16[128,2048]{1,0:T(8,128)(2,1)S(1)} collective-permute-done((bf16[128,2048]{1,0:T(8,128)(2,1)S(1)}, bf16[128,2048]{1,0:T(8,128)(2,1)S(1)}, u32[]{:S(2)}, u32[]{:S(2)}) %collective-permute-start.15) | collective-permute-done | bytes 524320 | tf_op jit(solution)/shard_map/ppermute | solution.py:562
  121.5 1.1 pad_maximum_fusion.2
  122.7 1.3 collective-permute-start.21
  124.0 14.3 %shard_map.157 = (f32[3584,128]{1,0:T(8,128)}, bf16[3584,128]{1,0:T(8,128)(2,1)}) custom-call(s32[2]{0:T(128)} %pad_add_fusion.flags, bf16[128,2048]{1,0:T(8,128)(2,1)} %bitcast.45, bf16[128,2048]{1,0:T(8,128)(2,1)} %copy-done.31, bf16[128,2048]{1,0:T(8,128)(2,1)} %copy-done.33, bf16[128,2048]{1,0:T(8,128)(2,1)} %copy-done.28, bf16[128,2048]{1,0:T(8,128)(2,1)} %copy-done.28, ...), custom_call_target="tpu_custom_call" | custom-call | flops 1024 | bytes 1024 | tf_op jit(solution)/shard_map/pallas_call | solution.py:241
  138.4 1.0 collective-permute-start.22
  139.8 1.5 copy-done.16
  141.2 2.4 %shard_map.158 = f32[128,128]{1,0:T(8,128)S(1)} custom-call(f32[3584,128]{1,0:T(8,128)S(1)} %copy-done.16, bf16[3584,128]{1,0:T(8,128)(2,1)} %collective-permute-done.19.returned, bf16[128,3584]{1,0:T(8,128)(2,1)S(1)} %bitcast.36, bf16[128,3584]{1,0:T(8,128)(2,1)S(1)} %bitcast.38, bf16[64,3584]{1,0:T(8,128)(2,1)S(1)} %copy-done.5, bf16[64,3584]{1,0:T(8,128)(2,1)S(1)} %copy-done.7), custom_call_target="tpu_custom_call" | custom-call | flops 1024 | bytes 1024 | tf_op jit(solution)/shard_map/pallas_call | solution.py:268
  143.7 1.8 collective-permute-start.20
  145.6 4.0 %collective-permute-start.17 = (f32[384,128]{1,0:T(8,128)S(1)}, f32[384,128]{1,0:T(8,128)S(1)}, u32[]{:S(2)}, u32[]{:S(2)}) collective-permute-start(f32[384,128]{1,0:T(8,128)S(1)} %add.32), channel_id=1, source_target_pairs={{0,8},{4,12},{8,0},{12,4},{1,9},{5,13},{9,1},{13,5},{2,10},{6,14},... | collective-permute-start | bytes 589832 | tf_op jit(solution)/shard_map/ppermute | solution.py:614
  149.6 6.0 %collective-permute-start.24 = (f32[128,192]{1,0:T(8,128)S(1)}, f32[128,192]{1,0:T(8,128)S(1)}, u32[]{:S(2)}, u32[]{:S(2)}) collective-permute-start(f32[128,192]{1,0:T(8,128)S(1)} %fusion), channel_id=1, source_target_pairs={{0,8},{4,12},{8,0},{12,4},{1,9},{5,13},{9,1},{13,5},{2,10},{6,14},... | collective-permute-start | bytes 294920 | tf_op jit(solution)/shard_map/ppermute | solution.py:615
  155.8 18.3 %shard_map.159 = (f32[128,128]{1,0:T(8,128)}, f32[128,128]{1,0:T(8,128)}) custom-call(s32[2]{0:T(128)} %pad_add_fusion.flags, bf16[128,2048]{1,0:T(8,128)(2,1)} %bitcast.9.b0, bf16[128,2048]{1,0:T(8,128)(2,1)} %collective-permute-done.14.b1, bf16[128,2048]{1,0:T(8,128)(2,1)} %copy-done.34, bf16[128,2048]{1,0:T(8,128)(2,1)} %copy-done.27, ...), custom_call_target="tpu_custom_call" | custom-call | flops 1024 | bytes 1024 | tf_op jit(solution)/shard_map/pallas_call | solution.py:337
  175.2 2.0 %collective-permute-start.23 = (f32[128,128]{1,0:T(8,128)}, f32[128,128]{1,0:T(8,128)S(1)}, u32[]{:S(2)}, u32[]{:S(2)}) collective-permute-start(f32[128,128]{1,0:T(8,128)} %get-tuple-element.68), channel_id=1, source_target_pairs={{0,2},{1,3},{2,0},{3,1},{4,6},{5,7},{6,4},{7,5},{8,10},{9,11},{10,... | collective-permute-start | bytes 196616 | tf_op jit(solution)/shard_map/ppermute | solution.py:613
  177.2 4.3 %collective-permute-done.23.far = f32[128,128]{1,0:T(8,128)S(1)} collective-permute-done((f32[128,128]{1,0:T(8,128)}, f32[128,128]{1,0:T(8,128)S(1)}, u32[]{:S(2)}, u32[]{:S(2)}) %collective-permute-start.23) | collective-permute-done | bytes 65568 | tf_op jit(solution)/shard_map/ppermute | solution.py:613
  181.6 1.5 copy-done.13
  183.1 1.6 shard_map.160.early
  184.7 1.4 shard_map.162
  186.1 1.4 collective-permute-start.30
  187.5 1.6 collective-permute-start.29
  189.1 1.5 collective-permute-start.28
  (117 shorter events, 13.5 us)
Async XLA Ops:
  0.0 8.6 %copy-start = (bf16[4,64,3584]{2,1,0:T(8,128)(2,1)S(1)}, bf16[4,64,3584]{2,1,0:T(8,128)(2,1)}, u32[]{:S(2)}) copy-start(bf16[4,64,3584]{2,1,0:T(8,128)(2,1)} %param.17) | copy-start | bytes 5505028
  0.0 87.7 %collective-permute-start.12 = (bf16[3584,2048]{1,0:T(8,128)(2,1)}, bf16[3584,2048]{1,0:T(8,128)(2,1)}, u32[]{:S(2)}, u32[]{:S(2)}) collective-permute-start(bf16[3584,2048]{1,0:T(8,128)(2,1)} %weight_own.5), channel_id=1, source_target_pairs={{0,1},{1,0},{2,3},{3,2},{4,5},{5,4},{6,7},{7,6},{8,9},{9,8},{10,11... | collective-permute-start | bytes 44040200 | tf_op jit(solution)/shard_map/ppermute | solution.py:573
  1.8 32.0 %collective-permute-start.1 = (bf16[128,3584]{1,0:T(8,128)(2,1)S(1)}, bf16[128,3584]{1,0:T(8,128)(2,1)S(1)}, u32[]{:S(2)}, u32[]{:S(2)}) collective-permute-start(bf16[128,3584]{1,0:T(8,128)(2,1)S(1)} %bitcast.46), channel_id=1, source_target_pairs={{0,2},{1,3},{2,0},{3,1},{4,6},{5,7},{6,4},{7,5},{8,10},{9,11},{10,... | collective-permute-start | bytes 2752520 | tf_op jit(solution)/shard_map/ppermute | solution.py:575
  4.4 26.5 %collective-permute-start = (bf16[128,2048]{1,0:T(8,128)(2,1)}, bf16[128,2048]{1,0:T(8,128)(2,1)}, u32[]{:S(2)}, u32[]{:S(2)}) collective-permute-start(bf16[128,2048]{1,0:T(8,128)(2,1)} %bitcast.4.q_outgrad.b0), channel_id=1, source_target_pairs={{0,8},{4,12},{8,0},{12,4},{1,9},{5,13},{9,1},{13,5},{2,10},{6,14},... | collective-permute-start | bytes 1572872 | tf_op jit(solution)/shard_map/ppermute | solution.py:558
  7.0 24.0 %collective-permute-start.4 = (bf16[128,2048]{1,0:T(8,128)(2,1)}, bf16[128,2048]{1,0:T(8,128)(2,1)S(1)}, u32[]{:S(2)}, u32[]{:S(2)}) collective-permute-start(bf16[128,2048]{1,0:T(8,128)(2,1)} %bitcast.4.q_outgrad.b0), channel_id=1, source_target_pairs={{0,4},{4,0},{8,12},{12,8},{1,5},{5,1},{9,13},{13,9},{2,6},{6,2},{1... | collective-permute-start | bytes 1572872 | tf_op jit(solution)/shard_map/ppermute | solution.py:558
  23.7 11.6 %copy-start.22 = (f32[384,128]{1,0:T(8,128)}, f32[384,128]{1,0:T(8,128)S(1)}, u32[]{:S(2)}) copy-start(f32[384,128]{1,0:T(8,128)S(1)} %get-tuple-element.56) | copy-start | bytes 589828
  31.0 4.4 %collective-permute-start.5 = (bf16[128,2048]{1,0:T(8,128)(2,1)}, bf16[128,2048]{1,0:T(8,128)(2,1)}, u32[]{:S(2)}, u32[]{:S(2)}) collective-permute-start(bf16[128,2048]{1,0:T(8,128)(2,1)} %bitcast.4.q_outgrad.b0), channel_id=1, source_target_pairs={{0,1},{1,0},{2,3},{3,2},{4,8},{5,9},{6,10},{7,11},{8,4},{9,5},{10,... | collective-permute-start | bytes 1572872 | tf_op jit(solution)/shard_map/ppermute | solution.py:561
  31.0 26.3 %collective-permute-start.6 = (bf16[128,2048]{1,0:T(8,128)(2,1)}, bf16[128,2048]{1,0:T(8,128)(2,1)}, u32[]{:S(2)}, u32[]{:S(2)}) collective-permute-start(bf16[128,2048]{1,0:T(8,128)(2,1)} %collective-permute-done.b3.b4), channel_id=1, source_target_pairs={{0,4},{4,0},{8,12},{12,8},{1,5},{5,1},{9,13},{13,9},{2,6},{6,2},{1... | collective-permute-start | bytes 1572872 | tf_op jit(solution)/shard_map/ppermute | solution.py:562
  33.8 25.0 %collective-permute-start.7 = (bf16[128,3584]{1,0:T(8,128)(2,1)}, bf16[128,3584]{1,0:T(8,128)(2,1)}, u32[]{:S(2)}, u32[]{:S(2)}) collective-permute-start(bf16[128,3584]{1,0:T(8,128)(2,1)} %bitcast.16), channel_id=1, source_target_pairs={{0,2},{1,3},{2,0},{3,1},{4,6},{5,7},{6,4},{7,5},{8,10},{9,11},{10,... | collective-permute-start | bytes 2752520 | tf_op jit(solution)/shard_map/ppermute | solution.py:583
  35.3 49.3 %copy-start.29 = (bf16[2,64,2048]{2,1,0:T(8,128)(2,1)}, bf16[2,64,2048]{2,1,0:T(8,128)(2,1)S(1)}, u32[]{:S(2)}) copy-start(bf16[2,64,2048]{2,1,0:T(8,128)(2,1)S(1)} %get-tuple-element.71) | copy-start | bytes 1572868
  35.3 32.7 %collective-permute-start.10 = (bf16[128,2048]{1,0:T(8,128)(2,1)S(1)}, bf16[128,2048]{1,0:T(8,128)(2,1)S(1)}, u32[]{:S(2)}, u32[]{:S(2)}) collective-permute-start(bf16[128,2048]{1,0:T(8,128)(2,1)S(1)} %bitcast.41), channel_id=1, source_target_pairs={{0,4},{4,0},{8,12},{12,8},{1,5},{5,1},{9,13},{13,9},{2,6},{6,2},{1... | collective-permute-start | bytes 1572872 | tf_op jit(solution)/shard_map/ppermute | solution.py:558
  35.4 30.5 %collective-permute-start.2 = (bf16[128,2048]{1,0:T(8,128)(2,1)S(1)}, bf16[128,2048]{1,0:T(8,128)(2,1)S(1)}, u32[]{:S(2)}, u32[]{:S(2)}) collective-permute-start(bf16[128,2048]{1,0:T(8,128)(2,1)S(1)} %bitcast.42), channel_id=1, source_target_pairs={{0,8},{4,12},{8,0},{12,4},{1,9},{5,13},{9,1},{13,5},{2,10},{6,14},... | collective-permute-start | bytes 1572872 | tf_op jit(solution)/shard_map/ppermute | solution.py:558
  58.7 13.7 %copy-start.2 = (bf16[4,64,3584]{2,1,0:T(8,128)(2,1)S(1)}, bf16[4,64,3584]{2,1,0:T(8,128)(2,1)}, u32[]{:S(2)}) copy-start(bf16[4,64,3584]{2,1,0:T(8,128)(2,1)} %param.18) | copy-start | bytes 5505028
  58.8 25.8 %collective-permute-start.8 = (bf16[2,128,2048]{2,1,0:T(8,128)(2,1)S(1)}, bf16[2,128,2048]{2,1,0:T(8,128)(2,1)S(1)}, u32[]{:S(2)}, u32[]{:S(2)}) collective-permute-start(bf16[2,128,2048]{2,1,0:T(8,128)(2,1)S(1)} %pad_maximum_fusion), channel_id=1, source_target_pairs={{0,2},{1,3},{2,0},{3,1},{4,6},{5,7},{6,4},{7,5},{8,10},{9,11},{10,... | collective-permute-start | bytes 3145736 | tf_op jit(solution)/shard_map/ppermute | solution.py:585
  65.8 18.8 %copy-start.28 = (bf16[128,2048]{1,0:T(8,128)(2,1)}, bf16[128,2048]{1,0:T(8,128)(2,1)S(1)}, u32[]{:S(2)}) copy-start(bf16[128,2048]{1,0:T(8,128)(2,1)S(1)} %collective-permute-done.2.b3.b4) | copy-start | bytes 1572868
  68.0 16.7 %copy-start.31 = (bf16[128,2048]{1,0:T(8,128)(2,1)}, bf16[128,2048]{1,0:T(8,128)(2,1)S(1)}, u32[]{:S(2)}) copy-start(bf16[128,2048]{1,0:T(8,128)(2,1)S(1)} %collective-permute-done.10.b1) | copy-start | bytes 1572868
  68.0 15.0 %collective-permute-start.11 = (bf16[128,2048]{1,0:T(8,128)(2,1)S(1)}, bf16[128,2048]{1,0:T(8,128)(2,1)S(1)}, u32[]{:S(2)}, u32[]{:S(2)}) collective-permute-start(bf16[128,2048]{1,0:T(8,128)(2,1)S(1)} %collective-permute-done.2.b3.b4), channel_id=1, source_target_pairs={{0,4},{4,0},{8,12},{12,8},{1,5},{5,1},{9,13},{13,9},{2,6},{6,2},{1... | collective-permute-start | bytes 1572872 | tf_op jit(solution)/shard_map/ppermute | solution.py:562
  70.2 14.5 %collective-permute-start.9 = (bf16[128,2048]{1,0:T(8,128)(2,1)S(1)}, bf16[128,2048]{1,0:T(8,128)(2,1)S(1)}, u32[]{:S(2)}, u32[]{:S(2)}) collective-permute-start(bf16[128,2048]{1,0:T(8,128)(2,1)S(1)} %bitcast.43), channel_id=1, source_target_pairs={{0,1},{1,0},{2,3},{3,2},{4,8},{5,9},{6,10},{7,11},{8,4},{9,5},{10,... | collective-permute-start | bytes 1572872 | tf_op jit(solution)/shard_map/ppermute | solution.py:561
  70.2 36.2 %collective-permute-start.14 = (bf16[128,2048]{1,0:T(8,128)(2,1)}, bf16[128,2048]{1,0:T(8,128)(2,1)}, u32[]{:S(2)}, u32[]{:S(2)}) collective-permute-start(bf16[128,2048]{1,0:T(8,128)(2,1)} %bitcast.9.b0), channel_id=1, source_target_pairs={{0,4},{4,0},{8,12},{12,8},{1,5},{5,1},{9,13},{13,9},{2,6},{6,2},{1... | collective-permute-start | bytes 1572872 | tf_op jit(solution)/shard_map/ppermute | solution.py:558
  77.0 7.8 %copy-start.14 = (bf16[3584,256]{1,0:T(8,128)(2,1)}, bf16[3584,256]{1,0:T(8,128)(2,1)S(1)}, u32[]{:S(2)}) copy-start(bf16[3584,256]{1,0:T(8,128)(2,1)S(1)} %get-tuple-element.49.gates) | copy-start | bytes 5505028
  77.0 7.8 %copy-start.15 = (bf16[3584,256]{1,0:T(8,128)(2,1)}, bf16[3584,256]{1,0:T(8,128)(2,1)S(1)}, u32[]{:S(2)}) copy-start(bf16[3584,256]{1,0:T(8,128)(2,1)S(1)} %get-tuple-element.64.ups) | copy-start | bytes 5505028
  83.0 23.4 %collective-permute-start.3 = (bf16[128,2048]{1,0:T(8,128)(2,1)}, bf16[128,2048]{1,0:T(8,128)(2,1)S(1)}, u32[]{:S(2)}, u32[]{:S(2)}) collective-permute-start(bf16[128,2048]{1,0:T(8,128)(2,1)} %bitcast.9.b0), channel_id=1, source_target_pairs={{0,8},{4,12},{8,0},{12,4},{1,9},{5,13},{9,1},{13,5},{2,10},{6,14},... | collective-permute-start | bytes 1572872 | tf_op jit(solution)/shard_map/ppermute | solution.py:558
  86.6 23.1 %collective-permute-start.18 = (bf16[2,128,2048]{2,1,0:T(8,128)(2,1)}, bf16[2,128,2048]{2,1,0:T(8,128)(2,1)}, u32[]{:S(2)}, u32[]{:S(2)}) collective-permute-start(bf16[2,128,2048]{2,1,0:T(8,128)(2,1)} %pad_maximum_fusion.1), channel_id=1, source_target_pairs={{0,2},{1,3},{2,0},{3,1},{4,6},{5,7},{6,4},{7,5},{8,10},{9,11},{10,... | collective-permute-start | bytes 3145736 | tf_op jit(solution)/shard_map/ppermute | solution.py:591
  106.4 14.5 %copy-start.27 = (bf16[128,2048]{1,0:T(8,128)(2,1)}, bf16[128,2048]{1,0:T(8,128)(2,1)S(1)}, u32[]{:S(2)}) copy-start(bf16[128,2048]{1,0:T(8,128)(2,1)S(1)} %collective-permute-done.3.b3.b4) | copy-start | bytes 1572868
  106.4 3.9 %collective-permute-start.13 = (bf16[128,2048]{1,0:T(8,128)(2,1)}, bf16[128,2048]{1,0:T(8,128)(2,1)S(1)}, u32[]{:S(2)}, u32[]{:S(2)}) collective-permute-start(bf16[128,2048]{1,0:T(8,128)(2,1)} %bitcast.9.b0), channel_id=1, source_target_pairs={{0,1},{1,0},{2,3},{3,2},{4,8},{5,9},{6,10},{7,11},{8,4},{9,5},{10,... | collective-permute-start | bytes 1572872 | tf_op jit(solution)/shard_map/ppermute | solution.py:561
  106.4 14.3 %collective-permute-start.15 = (bf16[128,2048]{1,0:T(8,128)(2,1)S(1)}, bf16[128,2048]{1,0:T(8,128)(2,1)S(1)}, u32[]{:S(2)}, u32[]{:S(2)}) collective-permute-start(bf16[128,2048]{1,0:T(8,128)(2,1)S(1)} %collective-permute-done.3.b3.b4), channel_id=1, source_target_pairs={{0,4},{4,0},{8,12},{12,8},{1,5},{5,1},{9,13},{13,9},{2,6},{6,2},{1... | collective-permute-start | bytes 1572872 | tf_op jit(solution)/shard_map/ppermute | solution.py:562
  109.7 30.0 %collective-permute-start.19 = (bf16[3584,128]{1,0:T(8,128)(2,1)}, bf16[3584,128]{1,0:T(8,128)(2,1)}, u32[]{:S(2)}, u32[]{:S(2)}) collective-permute-start(bf16[3584,128]{1,0:T(8,128)(2,1)} %get-tuple-element.58), channel_id=1, source_target_pairs={{0,2},{1,3},{2,0},{3,1},{4,6},{5,7},{6,4},{7,5},{8,10},{9,11},{10,... | collective-permute-start | bytes 2752520 | tf_op jit(solution)/shard_map/ppermute | solution.py:595
  110.3 10.7 %copy-start.34 = (bf16[128,2048]{1,0:T(8,128)(2,1)}, bf16[128,2048]{1,0:T(8,128)(2,1)S(1)}, u32[]{:S(2)}) copy-start(bf16[128,2048]{1,0:T(8,128)(2,1)S(1)} %collective-permute-done.13.b2) | copy-start | bytes 1572868
  122.7 16.7 %copy-start.23 = (f32[384,128]{1,0:T(8,128)S(1)}, f32[384,128]{1,0:T(8,128)}, u32[]{:S(2)}) copy-start(f32[384,128]{1,0:T(8,128)} %copy-done.22) | copy-start | bytes 589828
  122.7 17.0 %copy-start.5 = (bf16[64,3584]{1,0:T(8,128)(2,1)S(1)}, bf16[64,3584]{1,0:T(8,128)(2,1)}, u32[]{:S(2)}) copy-start(bf16[64,3584]{1,0:T(8,128)(2,1)} %proj_gate.5) | copy-start | bytes 1376260
  122.7 17.0 %copy-start.7 = (bf16[64,3584]{1,0:T(8,128)(2,1)S(1)}, bf16[64,3584]{1,0:T(8,128)(2,1)}, u32[]{:S(2)}) copy-start(bf16[64,3584]{1,0:T(8,128)(2,1)} %proj_up.5) | copy-start | bytes 1376260
  122.7 17.0 %copy-start.10 = (bf16[2,64,3584]{2,1,0:T(8,128)(2,1)S(1)}, bf16[2,64,3584]{2,1,0:T(8,128)(2,1)}, u32[]{:S(2)}) copy-start(bf16[2,64,3584]{2,1,0:T(8,128)(2,1)} %param.22) | copy-start | bytes 2752516
  122.7 17.0 %copy-start.12 = (bf16[2,64,3584]{2,1,0:T(8,128)(2,1)S(1)}, bf16[2,64,3584]{2,1,0:T(8,128)(2,1)}, u32[]{:S(2)}) copy-start(bf16[2,64,3584]{2,1,0:T(8,128)(2,1)} %param.23) | copy-start | bytes 2752516
  122.7 33.1 %collective-permute-start.21 = (bf16[2,128,2048]{2,1,0:T(8,128)(2,1)}, bf16[2,128,2048]{2,1,0:T(8,128)(2,1)}, u32[]{:S(2)}, u32[]{:S(2)}) collective-permute-start(bf16[2,128,2048]{2,1,0:T(8,128)(2,1)} %pad_maximum_fusion.2), channel_id=1, source_target_pairs={{0,2},{1,3},{2,0},{3,1},{4,6},{5,7},{6,4},{7,5},{8,10},{9,11},{10,... | collective-permute-start | bytes 3145736 | tf_op jit(solution)/shard_map/ppermute | solution.py:598
  138.4 43.2 %collective-permute-start.22 = (bf16[3584,128]{1,0:T(8,128)(2,1)}, bf16[3584,128]{1,0:T(8,128)(2,1)S(1)}, u32[]{:S(2)}, u32[]{:S(2)}) collective-permute-start(bf16[3584,128]{1,0:T(8,128)(2,1)} %get-tuple-element.60), channel_id=1, source_target_pairs={{0,2},{1,3},{2,0},{3,1},{4,6},{5,7},{6,4},{7,5},{8,10},{9,11},{10,... | collective-permute-start | bytes 2752520 | tf_op jit(solution)/shard_map/ppermute | solution.py:602
  139.4 6.2 %collective-permute-start.16 = (f32[384,128]{1,0:T(8,128)S(1)}, f32[384,128]{1,0:T(8,128)S(1)}, u32[]{:S(2)}, u32[]{:S(2)}) collective-permute-start(f32[384,128]{1,0:T(8,128)S(1)} %copy-done.23), channel_id=1, source_target_pairs={{0,4},{4,0},{8,12},{12,8},{1,5},{5,1},{9,13},{13,9},{2,6},{6,2},{1... | collective-permute-start | bytes 589832 | tf_op jit(solution)/shard_map/ppermute | solution.py:603
  143.7 5.9 %collective-permute-start.20 = (f32[128,192]{1,0:T(8,128)S(1)}, f32[128,192]{1,0:T(8,128)S(1)}, u32[]{:S(2)}, u32[]{:S(2)}) collective-permute-start(f32[128,192]{1,0:T(8,128)S(1)} %pad_maximum_fusion.3), channel_id=1, source_target_pairs={{0,4},{4,0},{8,12},{12,8},{1,5},{5,1},{9,13},{13,9},{2,6},{6,2},{1... | collective-permute-start | bytes 294920 | tf_op jit(solution)/shard_map/ppermute | solution.py:608
  145.6 28.6 %collective-permute-start.17 = (f32[384,128]{1,0:T(8,128)S(1)}, f32[384,128]{1,0:T(8,128)S(1)}, u32[]{:S(2)}, u32[]{:S(2)}) collective-permute-start(f32[384,128]{1,0:T(8,128)S(1)} %add.32), channel_id=1, source_target_pairs={{0,8},{4,12},{8,0},{12,4},{1,9},{5,13},{9,1},{13,5},{2,10},{6,14},... | collective-permute-start | bytes 589832 | tf_op jit(solution)/shard_map/ppermute | solution.py:614
  149.6 24.5 %collective-permute-start.24 = (f32[128,192]{1,0:T(8,128)S(1)}, f32[128,192]{1,0:T(8,128)S(1)}, u32[]{:S(2)}, u32[]{:S(2)}) collective-permute-start(f32[128,192]{1,0:T(8,128)S(1)} %fusion), channel_id=1, source_target_pairs={{0,8},{4,12},{8,0},{12,4},{1,9},{5,13},{9,1},{13,5},{2,10},{6,14},... | collective-permute-start | bytes 294920 | tf_op jit(solution)/shard_map/ppermute | solution.py:615
  155.8 18.4 %copy-start.25 = (s32[2]{0:T(128)S(1)}, s32[2]{0:T(128)}, u32[]{:S(2)}) copy-start(s32[2]{0:T(128)} %lengths.2) | copy-start | bytes 28
  155.8 25.8 %copy-start.3 = (bf16[4,64,3584]{2,1,0:T(8,128)(2,1)S(1)}, bf16[4,64,3584]{2,1,0:T(8,128)(2,1)}, u32[]{:S(2)}) copy-start(bf16[4,64,3584]{2,1,0:T(8,128)(2,1)} %param.18) | copy-start | bytes 5505028
  175.1 6.4 %collective-permute-start.26 = (f32[2,192,64]{2,1,0:T(8,128)S(1)}, f32[2,192,64]{2,1,0:T(8,128)S(1)}, u32[]{:S(2)}, u32[]{:S(2)}) collective-permute-start(f32[2,192,64]{2,1,0:T(8,128)S(1)} %shard_map.161.q0), channel_id=1, source_target_pairs={{0,2},{1,3},{2,0},{3,1},{4,6},{5,7},{6,4},{7,5},{8,10},{9,11},{10,... | collective-permute-start | bytes 294920 | tf_op jit(solution)/shard_map/ppermute | solution.py:617
  175.2 6.4 %collective-permute-start.23 = (f32[128,128]{1,0:T(8,128)}, f32[128,128]{1,0:T(8,128)S(1)}, u32[]{:S(2)}, u32[]{:S(2)}) collective-permute-start(f32[128,128]{1,0:T(8,128)} %get-tuple-element.68), channel_id=1, source_target_pairs={{0,2},{1,3},{2,0},{3,1},{4,6},{5,7},{6,4},{7,5},{8,10},{9,11},{10,... | collective-permute-start | bytes 196616 | tf_op jit(solution)/shard_map/ppermute | solution.py:613
  177.2 7.5 %collective-permute-start.25 = (f32[2,192,64]{2,1,0:T(8,128)S(1)}, f32[2,192,64]{2,1,0:T(8,128)S(1)}, u32[]{:S(2)}, u32[]{:S(2)}) collective-permute-start(f32[2,192,64]{2,1,0:T(8,128)S(1)} %shard_map.161.q0), channel_id=1, source_target_pairs={{0,1},{1,0},{2,3},{3,2},{4,5},{5,4},{6,7},{7,6},{8,9},{9,8},{10,11... | collective-permute-start | bytes 294920 | tf_op jit(solution)/shard_map/ppermute | solution.py:618
  181.5 3.2 %collective-permute-start.27 = (f32[2,192,64]{2,1,0:T(8,128)S(1)}, f32[2,192,64]{2,1,0:T(8,128)S(1)}, u32[]{:S(2)}, u32[]{:S(2)}) collective-permute-start(f32[2,192,64]{2,1,0:T(8,128)S(1)} %collective-permute-done.26.q2), channel_id=1, source_target_pairs={{0,1},{1,0},{2,3},{3,2},{4,5},{5,4},{6,7},{7,6},{8,9},{9,8},{10,11... | collective-permute-start | bytes 294920 | tf_op jit(solution)/shard_map/ppermute | solution.py:618
  186.1 5.4 %collective-permute-start.30 = (f32[4,8]{1,0:T(4,128)S(1)}, f32[4,8]{1,0:T(4,128)S(1)}, u32[]{:S(2)}, u32[]{:S(2)}) collective-permute-start(f32[4,8]{1,0:T(4,128)S(1)} %shard_map.162), channel_id=1, source_target_pairs={{0,12},{4,8},{8,4},{12,0},{1,13},{5,9},{9,5},{13,1},{2,14},{6,10},... | collective-permute-start | bytes 392 | tf_op jit(solution)/shard_map/ppermute | solution.py:624
  187.5 4.5 %collective-permute-start.29 = (f32[4,8]{1,0:T(4,128)S(1)}, f32[4,8]{1,0:T(4,128)S(1)}, u32[]{:S(2)}, u32[]{:S(2)}) collective-permute-start(f32[4,8]{1,0:T(4,128)S(1)} %shard_map.162), channel_id=1, source_target_pairs={{0,8},{4,12},{8,0},{12,4},{1,9},{5,13},{9,1},{13,5},{2,10},{6,14},... | collective-permute-start | bytes 392 | tf_op jit(solution)/shard_map/ppermute | solution.py:624
  189.1 3.6 %collective-permute-start.28 = (f32[4,8]{1,0:T(4,128)S(1)}, f32[4,8]{1,0:T(4,128)S(1)}, u32[]{:S(2)}, u32[]{:S(2)}) collective-permute-start(f32[4,8]{1,0:T(4,128)S(1)} %shard_map.162), channel_id=1, source_target_pairs={{0,4},{4,0},{8,12},{12,8},{1,5},{5,1},{9,13},{13,9},{2,6},{6,2},{1... | collective-permute-start | bytes 392 | tf_op jit(solution)/shard_map/ppermute | solution.py:624
  (20 other events, 41.3 us)

commit v19 on v18

--- a/solution.py
+++ b/solution.py
@@ -11,6 +11,8 @@
 SEQ = 64
 TILE = 512
 WIDE = 1792
+NARROW = 256
+SLOTS = 5
 VMEM_BYTES = 40 * 1024 * 1024
 BIG_VMEM_BYTES = 58 * 1024 * 1024
 
@@ -154,11 +156,11 @@
 ):
     number = far.shape[1]
     step = pl.program_id(0)
-    tiles = weight_own.shape[0] // TILE
+    tiles = weight_own.shape[0] // NARROW
 
     def weight_copies(tile):
-        part = pl.ds(pl.multiple_of(tile * TILE, TILE), TILE)
-        slot = lax.rem(tile, 3)
+        part = pl.ds(pl.multiple_of(tile * NARROW, NARROW), NARROW)
+        slot = lax.rem(tile, SLOTS)
         return [
             pltpu.make_async_copy(
                 weight.at[part], held.at[slot, side], weight_sems.at[slot, side]
@@ -191,7 +193,7 @@
                 ]
                 for copy in copies:
                     copy.start()
-                for tile in range(2):
+                for tile in range(SLOTS - 1):
                     for copy in weight_copies(tile):
                         copy.start()
                 for copy in copies:
@@ -200,14 +202,14 @@
         for copy in far_copies:
             copy.wait()
 
-    @pl.when(step + 2 < tiles)
-    def _():
-        for copy in weight_copies(step + 2):
+    @pl.when(step + SLOTS - 1 < tiles)
+    def _():
+        for copy in weight_copies(step + SLOTS - 1):
             copy.start()
 
     for copy in weight_copies(step):
         copy.wait()
-    slot = lax.rem(step, 3)
+    slot = lax.rem(step, SLOTS)
     return project(held[slot, 0], stacked[0]) + project(held[slot, 1], stacked[1])
 
 
@@ -240,9 +242,9 @@
     units = weight_own.shape[0]
     return pl.pallas_call(
         partial_kernel,
-        grid=(units // TILE,),
+        grid=(units // NARROW,),
         in_specs=[SCALARS] + [ANYWHERE] * 9,
-        out_specs=[tile_rows(number)] * 2,
+        out_specs=[tile_rows(number, NARROW)] * 2,
         out_shape=[
             jax.ShapeDtypeStruct((units, number), jnp.float32),
             jax.ShapeDtypeStruct((units, number), jnp.bfloat16),
@@ -250,8 +252,8 @@
         scratch_shapes=[
             pltpu.VMEM((2, 2 * number, half), jnp.bfloat16),
             pltpu.SemaphoreType.DMA((4,)),
-            pltpu.VMEM((3, 2, TILE, half), jnp.bfloat16),
-            pltpu.SemaphoreType.DMA((3, 2)),
+            pltpu.VMEM((SLOTS, 2, NARROW, half), jnp.bfloat16),
+            pltpu.SemaphoreType.DMA((SLOTS, 2)),
         ],
         compiler_params=params(BIG_VMEM_BYTES),
         cost_estimate=cost(8 * number * half * units, (far, weight_own, weight_sib)),
@@ -336,18 +338,18 @@
     units = weight_own.shape[0]
     return pl.pallas_call(
         lent_kernel,
-        grid=(units // TILE,),
+        grid=(units // NARROW,),
         in_specs=[SCALARS]
         + [ANYWHERE] * 9
-        + [tile_rows(2 * number)] * 2
-        + [tile_columns(RANK)] * 2,
+        + [tile_rows(2 * number, NARROW)] * 2
+        + [tile_columns(RANK, 0, NARROW)] * 2,
         out_specs=[whole((2 * RANK, number))] * 2,
         out_shape=[jax.ShapeDtypeStruct((2 * RANK, number), jnp.float32)] * 2,
         scratch_shapes=[
             pltpu.VMEM((2, 2 * number, half), jnp.bfloat16),
             pltpu.SemaphoreType.DMA((4,)),
-            pltpu.VMEM((3, 2, TILE, half), jnp.bfloat16),
-            pltpu.SemaphoreType.DMA((3, 2)),
+            pltpu.VMEM((SLOTS, 2, NARROW, half), jnp.bfloat16),
+            pltpu.SemaphoreType.DMA((SLOTS, 2)),
         ],
         compiler_params=params(BIG_VMEM_BYTES),
         cost_estimate=cost(8 * number * half * units, (far, weight_own, weight_sib)),

time: 194 us -> 197 us (1.015)
  Pallas kernels: 62.7 us -> 68.5 us
  waiting for transfers between devices: 56.3 us -> 53.7 us
    pallas_call x3, Pallas kernels: 46.9 us -> 52.8 us  [the longest x2 32.4 us: partial_sums(): pl.pallas_call(partial_kernel, grid=(units // NARROW,), in_specs=[SCALARS...]
  transfers between devices with their start and end apart: 31 -> 31, of which waited for: 15 -> 13; matrix products, arithmetic and copies ran while one was open for 4% -> 4% of each run, Pallas kernels for 32% -> 34%
where the time goes in v19:
time: 197 us
  Pallas kernels  68.5 us (35%)
  waiting for transfers between devices  53.7 us (27%)
  starting transfers between devices  50.6 us (26%)
  local copies, waits for them, and re-layouts  17.9 us (9%)
  other arithmetic  5.39 us (3%)
    pallas_call x2, Pallas kernels, partial_sums(): pl.pallas_call(partial_kernel, grid=(units // NARROW,), in_specs=[SCALARS...  32.4 us
    ppermute x3, waiting for transfers between devices, last_hops(): return (own, one, mid, two, two, outer(after(two, one)))  28 us
    pallas_call x1, Pallas kernels, lent_sides(): pl.pallas_call(lent_kernel, grid=(units // NARROW,), in_specs=[SCALARS] +...  20.4 us
    ppermute x6, starting transfers between devices, first_hops(): return (own, outer(own), across(own))  18.4 us
    ppermute x6, waiting for transfers between devices, first_hops(): return (own, outer(own), across(own))  18.1 us
    unnamed x74, local copies, waits for them, and re-layouts  14.6 us
    ppermute x1, starting transfers between devices, moving_plan(): q_sums = q_sums + after(across(q_sums), b_near)  6.01 us
    ppermute x3, starting transfers between devices, last_hops(): return (own, one, mid, two, two, outer(after(two, one)))  5.81 us
  transfers between devices with their start and end apart: 31, of which 13 were waited for; matrix products, arithmetic and copies ran while one was open for 4% of the time, Pallas kernels for 34%

profile of v19, /device:TPU:0, one launch (start us, length us, event | category | flops | bytes accessed | tf_op | source)
XLA Modules:
  0.0 196.5 jit_solution(3935086656718653803)
XLA Ops:
  0.5 1.3 slice.40
  1.8 2.6 %collective-permute-start.1 = (bf16[128,3584]{1,0:T(8,128)(2,1)S(1)}, bf16[128,3584]{1,0:T(8,128)(2,1)S(1)}, u32[]{:S(2)}, u32[]{:S(2)}) collective-permute-start(bf16[128,3584]{1,0:T(8,128)(2,1)S(1)} %bitcast.46), channel_id=1, source_target_pairs={{0,2},{1,3},{2,0},{3,1},{4,6},{5,7},{6,4},{7,5},{8,10},{9,11},{10,... | collective-permute-start | bytes 2752520 | tf_op jit(solution)/shard_map/ppermute | solution.py:577
  4.4 2.6 %collective-permute-start = (bf16[128,2048]{1,0:T(8,128)(2,1)}, bf16[128,2048]{1,0:T(8,128)(2,1)}, u32[]{:S(2)}, u32[]{:S(2)}) collective-permute-start(bf16[128,2048]{1,0:T(8,128)(2,1)} %bitcast.4.q_outgrad.b0), channel_id=1, source_target_pairs={{0,8},{4,12},{8,0},{12,4},{1,9},{5,13},{9,1},{13,5},{2,10},{6,14},... | collective-permute-start | bytes 1572872 | tf_op jit(solution)/shard_map/ppermute | solution.py:560
  7.0 1.6 collective-permute-start.4
  8.6 1.5 copy-done.1
  10.1 1.2 copy-done.4
  11.3 1.2 copy-done.9
  12.5 1.2 copy-done.11
  13.7 1.2 copy-done.17
  14.9 1.0 copy-done.18
  15.9 1.0 copy-done.19
  18.8 4.9 %shard_map.154 = (f32[384,128]{1,0:T(8,128)S(1)}, f32[384,64]{1,0:T(8,128)S(1)}) custom-call(bf16[256,2048]{1,0:T(8,128)(2,1)S(1)} %bitcast.39, bf16[128,2048]{1,0:T(8,128)(2,1)S(1)} %bitcast.40, bf16[256,2048]{1,0:T(8,128)(2,1)S(1)} %bitcast.34, bf16[128,2048]{1,0:T(8,128)(2,1)} %bitcast.4.q_outgrad.b0, bf16[64,2048]{1,0:T(8,128)(2,1)S(1)} %copy-done.20, ...), custom_call_target="tpu_custom_call" | custom-call | flops 1024 | bytes 1024 | tf_op jit(solution)/shard_map/pallas_call | solution.py:398
  23.7 7.1 %collective-permute-done.b3.b4 = bf16[128,2048]{1,0:T(8,128)(2,1)} collective-permute-done((bf16[128,2048]{1,0:T(8,128)(2,1)}, bf16[128,2048]{1,0:T(8,128)(2,1)}, u32[]{:S(2)}, u32[]{:S(2)}) %collective-permute-start) | collective-permute-done | bytes 524320 | tf_op jit(solution)/shard_map/ppermute | solution.py:560
  31.0 1.9 collective-permute-start.6
  32.8 1.0 slice.42
  35.4 10.3 %collective-permute-start.2 = (bf16[128,2048]{1,0:T(8,128)(2,1)S(1)}, bf16[128,2048]{1,0:T(8,128)(2,1)S(1)}, u32[]{:S(2)}, u32[]{:S(2)}) collective-permute-start(bf16[128,2048]{1,0:T(8,128)(2,1)S(1)} %bitcast.42), channel_id=1, source_target_pairs={{0,8},{4,12},{8,0},{12,4},{1,9},{5,13},{9,1},{13,5},{2,10},{6,14},... | collective-permute-start | bytes 1572872 | tf_op jit(solution)/shard_map/ppermute | solution.py:560
  45.7 11.6 %collective-permute-done.6.b5 = bf16[128,2048]{1,0:T(8,128)(2,1)} collective-permute-done((bf16[128,2048]{1,0:T(8,128)(2,1)}, bf16[128,2048]{1,0:T(8,128)(2,1)}, u32[]{:S(2)}, u32[]{:S(2)}) %collective-permute-start.6) | collective-permute-done | bytes 524320 | tf_op jit(solution)/shard_map/ppermute | solution.py:564
  57.2 1.5 select_bitcast_fusion.5
  59.5 6.3 %collective-permute-done.2.b3.b4 = bf16[128,2048]{1,0:T(8,128)(2,1)S(1)} collective-permute-done((bf16[128,2048]{1,0:T(8,128)(2,1)S(1)}, bf16[128,2048]{1,0:T(8,128)(2,1)S(1)}, u32[]{:S(2)}, u32[]{:S(2)}) %collective-permute-start.2) | collective-permute-done | bytes 524320 | tf_op jit(solution)/shard_map/ppermute | solution.py:560
  65.8 2.1 %collective-permute-done.10.b1 = bf16[128,2048]{1,0:T(8,128)(2,1)S(1)} collective-permute-done((bf16[128,2048]{1,0:T(8,128)(2,1)S(1)}, bf16[128,2048]{1,0:T(8,128)(2,1)S(1)}, u32[]{:S(2)}, u32[]{:S(2)}) %collective-permute-start.10) | collective-permute-done | bytes 524320 | tf_op jit(solution)/shard_map/ppermute | solution.py:560
  68.0 2.2 %collective-permute-start.11 = (bf16[128,2048]{1,0:T(8,128)(2,1)S(1)}, bf16[128,2048]{1,0:T(8,128)(2,1)S(1)}, u32[]{:S(2)}, u32[]{:S(2)}) collective-permute-start(bf16[128,2048]{1,0:T(8,128)(2,1)S(1)} %collective-permute-done.2.b3.b4), channel_id=1, source_target_pairs={{0,4},{4,0},{8,12},{12,8},{1,5},{5,1},{9,13},{13,9},{2,6},{6,2},{1... | collective-permute-start | bytes 1572872 | tf_op jit(solution)/shard_map/ppermute | solution.py:564
  70.2 2.2 %collective-permute-start.14 = (bf16[128,2048]{1,0:T(8,128)(2,1)}, bf16[128,2048]{1,0:T(8,128)(2,1)}, u32[]{:S(2)}, u32[]{:S(2)}) collective-permute-start(bf16[128,2048]{1,0:T(8,128)(2,1)} %bitcast.9.b0), channel_id=1, source_target_pairs={{0,4},{4,0},{8,12},{12,8},{1,5},{5,1},{9,13},{13,9},{2,6},{6,2},{1... | collective-permute-start | bytes 1572872 | tf_op jit(solution)/shard_map/ppermute | solution.py:560
  72.4 4.6 %shard_map.155 = (bf16[3584,256]{1,0:T(8,128)(2,1)S(1)}, bf16[3584,256]{1,0:T(8,128)(2,1)S(1)}) custom-call(bf16[256,3584]{1,0:T(8,128)(2,1)S(1)} %bitcast.29, bf16[256,3584]{1,0:T(8,128)(2,1)S(1)} %bitcast.32, bf16[128,3584]{1,0:T(8,128)(2,1)S(1)} %collective-permute-done.1.far_gate, bf16[128,3584]{1,0:T(8,128)(2,1)} %collective-permute-done.7.far_up), custom_call_target="tpu_custom_call" | custom-call | flops 1024 | bytes 1024 | tf_op jit(solution)/shard_map/pallas_call | solution.py:297
  77.0 5.9 %collective-permute-done.11.b5 = bf16[128,2048]{1,0:T(8,128)(2,1)S(1)} collective-permute-done((bf16[128,2048]{1,0:T(8,128)(2,1)S(1)}, bf16[128,2048]{1,0:T(8,128)(2,1)S(1)}, u32[]{:S(2)}, u32[]{:S(2)}) %collective-permute-start.11) | collective-permute-done | bytes 524320 | tf_op jit(solution)/shard_map/ppermute | solution.py:564
  83.0 1.6 collective-permute-start.3
  85.5 1.1 pad_maximum_fusion.1
  87.7 16.2 %shard_map.156 = (f32[3584,128]{1,0:T(8,128)}, bf16[3584,128]{1,0:T(8,128)(2,1)}) custom-call(s32[2]{0:T(128)} %pad_add_fusion.flags, bf16[128,2048]{1,0:T(8,128)(2,1)} %bitcast.4.q_outgrad.b0, bf16[128,2048]{1,0:T(8,128)(2,1)} %copy-done.30, bf16[128,2048]{1,0:T(8,128)(2,1)} %collective-permute-done.5.b2, bf16[128,2048]{1,0:T(8,128)(2,1)} %collective-permute-done.b3.b4, ...), custom_call_target="tpu_custom_call" | custom-call | flops 1024 | bytes 1024 | tf_op jit(solution)/shard_map/pallas_call | solution.py:243
  103.9 2.5 %collective-permute-done.3.b3.b4 = bf16[128,2048]{1,0:T(8,128)(2,1)S(1)} collective-permute-done((bf16[128,2048]{1,0:T(8,128)(2,1)}, bf16[128,2048]{1,0:T(8,128)(2,1)S(1)}, u32[]{:S(2)}, u32[]{:S(2)}) %collective-permute-start.3) | collective-permute-done | bytes 524320 | tf_op jit(solution)/shard_map/ppermute | solution.py:560
  106.4 1.7 collective-permute-start.15
  108.1 1.6 collective-permute-done.18.far
  110.3 10.5 %collective-permute-done.15.b5 = bf16[128,2048]{1,0:T(8,128)(2,1)S(1)} collective-permute-done((bf16[128,2048]{1,0:T(8,128)(2,1)S(1)}, bf16[128,2048]{1,0:T(8,128)(2,1)S(1)}, u32[]{:S(2)}, u32[]{:S(2)}) %collective-permute-start.15) | collective-permute-done | bytes 524320 | tf_op jit(solution)/shard_map/ppermute | solution.py:564
  121.5 1.1 pad_maximum_fusion.2
  122.7 1.3 collective-permute-start.21
  124.0 16.2 %shard_map.157 = (f32[3584,128]{1,0:T(8,128)}, bf16[3584,128]{1,0:T(8,128)(2,1)}) custom-call(s32[2]{0:T(128)} %pad_add_fusion.flags, bf16[128,2048]{1,0:T(8,128)(2,1)} %bitcast.45, bf16[128,2048]{1,0:T(8,128)(2,1)} %copy-done.31, bf16[128,2048]{1,0:T(8,128)(2,1)} %copy-done.33, bf16[128,2048]{1,0:T(8,128)(2,1)} %copy-done.28, bf16[128,2048]{1,0:T(8,128)(2,1)} %copy-done.28, ...), custom_call_target="tpu_custom_call" | custom-call | flops 1024 | bytes 1024 | tf_op jit(solution)/shard_map/pallas_call | solution.py:243
  140.2 1.0 collective-permute-start.22
  141.6 1.5 copy-done.16
  143.1 2.4 %shard_map.158 = f32[128,128]{1,0:T(8,128)S(1)} custom-call(f32[3584,128]{1,0:T(8,128)S(1)} %copy-done.16, bf16[3584,128]{1,0:T(8,128)(2,1)} %collective-permute-done.19.returned, bf16[128,3584]{1,0:T(8,128)(2,1)S(1)} %bitcast.36, bf16[128,3584]{1,0:T(8,128)(2,1)S(1)} %bitcast.38, bf16[64,3584]{1,0:T(8,128)(2,1)S(1)} %copy-done.5, bf16[64,3584]{1,0:T(8,128)(2,1)S(1)} %copy-done.7), custom_call_target="tpu_custom_call" | custom-call | flops 1024 | bytes 1024 | tf_op jit(solution)/shard_map/pallas_call | solution.py:270
  145.5 1.8 collective-permute-start.20
  147.4 4.0 %collective-permute-start.17 = (f32[384,128]{1,0:T(8,128)S(1)}, f32[384,128]{1,0:T(8,128)S(1)}, u32[]{:S(2)}, u32[]{:S(2)}) collective-permute-start(f32[384,128]{1,0:T(8,128)S(1)} %add.32), channel_id=1, source_target_pairs={{0,8},{4,12},{8,0},{12,4},{1,9},{5,13},{9,1},{13,5},{2,10},{6,14},... | collective-permute-start | bytes 589832 | tf_op jit(solution)/shard_map/ppermute | solution.py:616
  151.4 6.0 %collective-permute-start.24 = (f32[128,192]{1,0:T(8,128)S(1)}, f32[128,192]{1,0:T(8,128)S(1)}, u32[]{:S(2)}, u32[]{:S(2)}) collective-permute-start(f32[128,192]{1,0:T(8,128)S(1)} %fusion), channel_id=1, source_target_pairs={{0,8},{4,12},{8,0},{12,4},{1,9},{5,13},{9,1},{13,5},{2,10},{6,14},... | collective-permute-start | bytes 294920 | tf_op jit(solution)/shard_map/ppermute | solution.py:617
  157.4 20.4 %shard_map.159 = (f32[128,128]{1,0:T(8,128)}, f32[128,128]{1,0:T(8,128)}) custom-call(s32[2]{0:T(128)} %pad_add_fusion.flags, bf16[128,2048]{1,0:T(8,128)(2,1)} %bitcast.9.b0, bf16[128,2048]{1,0:T(8,128)(2,1)} %collective-permute-done.14.b1, bf16[128,2048]{1,0:T(8,128)(2,1)} %copy-done.34, bf16[128,2048]{1,0:T(8,128)(2,1)} %copy-done.27, ...), custom_call_target="tpu_custom_call" | custom-call | flops 1024 | bytes 1024 | tf_op jit(solution)/shard_map/pallas_call | solution.py:339
  179.2 1.8 collective-permute-start.23
  181.0 4.3 %collective-permute-done.23.far = f32[128,128]{1,0:T(8,128)S(1)} collective-permute-done((f32[128,128]{1,0:T(8,128)}, f32[128,128]{1,0:T(8,128)S(1)}, u32[]{:S(2)}, u32[]{:S(2)}) %collective-permute-start.23) | collective-permute-done | bytes 65568 | tf_op jit(solution)/shard_map/ppermute | solution.py:615
  185.4 1.5 copy-done.13
  186.9 1.6 shard_map.160.early
  188.5 1.4 shard_map.162
  191.2 3.1 %collective-permute-start.28 = (f32[4,8]{1,0:T(4,128)S(1)}, f32[4,8]{1,0:T(4,128)S(1)}, u32[]{:S(2)}, u32[]{:S(2)}) collective-permute-start(f32[4,8]{1,0:T(4,128)S(1)} %shard_map.162), channel_id=1, source_target_pairs={{0,4},{4,0},{8,12},{12,8},{1,5},{5,1},{9,13},{13,9},{2,6},{6,2},{1... | collective-permute-start | bytes 392 | tf_op jit(solution)/shard_map/ppermute | solution.py:626
  194.4 1.0 collective-permute-done.30
  (117 shorter events, 12.3 us)
Async XLA Ops:
  0.0 8.6 %copy-start = (bf16[4,64,3584]{2,1,0:T(8,128)(2,1)S(1)}, bf16[4,64,3584]{2,1,0:T(8,128)(2,1)}, u32[]{:S(2)}) copy-start(bf16[4,64,3584]{2,1,0:T(8,128)(2,1)} %param.17) | copy-start | bytes 5505028
  0.0 87.7 %collective-permute-start.12 = (bf16[3584,2048]{1,0:T(8,128)(2,1)}, bf16[3584,2048]{1,0:T(8,128)(2,1)}, u32[]{:S(2)}, u32[]{:S(2)}) collective-permute-start(bf16[3584,2048]{1,0:T(8,128)(2,1)} %weight_own.5), channel_id=1, source_target_pairs={{0,1},{1,0},{2,3},{3,2},{4,5},{5,4},{6,7},{7,6},{8,9},{9,8},{10,11... | collective-permute-start | bytes 44040200 | tf_op jit(solution)/shard_map/ppermute | solution.py:575
  1.8 32.0 %collective-permute-start.1 = (bf16[128,3584]{1,0:T(8,128)(2,1)S(1)}, bf16[128,3584]{1,0:T(8,128)(2,1)S(1)}, u32[]{:S(2)}, u32[]{:S(2)}) collective-permute-start(bf16[128,3584]{1,0:T(8,128)(2,1)S(1)} %bitcast.46), channel_id=1, source_target_pairs={{0,2},{1,3},{2,0},{3,1},{4,6},{5,7},{6,4},{7,5},{8,10},{9,11},{10,... | collective-permute-start | bytes 2752520 | tf_op jit(solution)/shard_map/ppermute | solution.py:577
  4.4 26.5 %collective-permute-start = (bf16[128,2048]{1,0:T(8,128)(2,1)}, bf16[128,2048]{1,0:T(8,128)(2,1)}, u32[]{:S(2)}, u32[]{:S(2)}) collective-permute-start(bf16[128,2048]{1,0:T(8,128)(2,1)} %bitcast.4.q_outgrad.b0), channel_id=1, source_target_pairs={{0,8},{4,12},{8,0},{12,4},{1,9},{5,13},{9,1},{13,5},{2,10},{6,14},... | collective-permute-start | bytes 1572872 | tf_op jit(solution)/shard_map/ppermute | solution.py:560
  7.0 24.0 %collective-permute-start.4 = (bf16[128,2048]{1,0:T(8,128)(2,1)}, bf16[128,2048]{1,0:T(8,128)(2,1)S(1)}, u32[]{:S(2)}, u32[]{:S(2)}) collective-permute-start(bf16[128,2048]{1,0:T(8,128)(2,1)} %bitcast.4.q_outgrad.b0), channel_id=1, source_target_pairs={{0,4},{4,0},{8,12},{12,8},{1,5},{5,1},{9,13},{13,9},{2,6},{6,2},{1... | collective-permute-start | bytes 1572872 | tf_op jit(solution)/shard_map/ppermute | solution.py:560
  23.7 11.6 %copy-start.22 = (f32[384,128]{1,0:T(8,128)}, f32[384,128]{1,0:T(8,128)S(1)}, u32[]{:S(2)}) copy-start(f32[384,128]{1,0:T(8,128)S(1)} %get-tuple-element.56) | copy-start | bytes 589828
  31.0 4.4 %collective-permute-start.5 = (bf16[128,2048]{1,0:T(8,128)(2,1)}, bf16[128,2048]{1,0:T(8,128)(2,1)}, u32[]{:S(2)}, u32[]{:S(2)}) collective-permute-start(bf16[128,2048]{1,0:T(8,128)(2,1)} %bitcast.4.q_outgrad.b0), channel_id=1, source_target_pairs={{0,1},{1,0},{2,3},{3,2},{4,8},{5,9},{6,10},{7,11},{8,4},{9,5},{10,... | collective-permute-start | bytes 1572872 | tf_op jit(solution)/shard_map/ppermute | solution.py:563
  31.0 26.3 %collective-permute-start.6 = (bf16[128,2048]{1,0:T(8,128)(2,1)}, bf16[128,2048]{1,0:T(8,128)(2,1)}, u32[]{:S(2)}, u32[]{:S(2)}) collective-permute-start(bf16[128,2048]{1,0:T(8,128)(2,1)} %collective-permute-done.b3.b4), channel_id=1, source_target_pairs={{0,4},{4,0},{8,12},{12,8},{1,5},{5,1},{9,13},{13,9},{2,6},{6,2},{1... | collective-permute-start | bytes 1572872 | tf_op jit(solution)/shard_map/ppermute | solution.py:564
  33.8 25.0 %collective-permute-start.7 = (bf16[128,3584]{1,0:T(8,128)(2,1)}, bf16[128,3584]{1,0:T(8,128)(2,1)}, u32[]{:S(2)}, u32[]{:S(2)}) collective-permute-start(bf16[128,3584]{1,0:T(8,128)(2,1)} %bitcast.16), channel_id=1, source_target_pairs={{0,2},{1,3},{2,0},{3,1},{4,6},{5,7},{6,4},{7,5},{8,10},{9,11},{10,... | collective-permute-start | bytes 2752520 | tf_op jit(solution)/shard_map/ppermute | solution.py:585
  35.3 49.3 %copy-start.29 = (bf16[2,64,2048]{2,1,0:T(8,128)(2,1)}, bf16[2,64,2048]{2,1,0:T(8,128)(2,1)S(1)}, u32[]{:S(2)}) copy-start(bf16[2,64,2048]{2,1,0:T(8,128)(2,1)S(1)} %get-tuple-element.71) | copy-start | bytes 1572868
  35.3 32.7 %collective-permute-start.10 = (bf16[128,2048]{1,0:T(8,128)(2,1)S(1)}, bf16[128,2048]{1,0:T(8,128)(2,1)S(1)}, u32[]{:S(2)}, u32[]{:S(2)}) collective-permute-start(bf16[128,2048]{1,0:T(8,128)(2,1)S(1)} %bitcast.41), channel_id=1, source_target_pairs={{0,4},{4,0},{8,12},{12,8},{1,5},{5,1},{9,13},{13,9},{2,6},{6,2},{1... | collective-permute-start | bytes 1572872 | tf_op jit(solution)/shard_map/ppermute | solution.py:560
  35.4 30.5 %collective-permute-start.2 = (bf16[128,2048]{1,0:T(8,128)(2,1)S(1)}, bf16[128,2048]{1,0:T(8,128)(2,1)S(1)}, u32[]{:S(2)}, u32[]{:S(2)}) collective-permute-start(bf16[128,2048]{1,0:T(8,128)(2,1)S(1)} %bitcast.42), channel_id=1, source_target_pairs={{0,8},{4,12},{8,0},{12,4},{1,9},{5,13},{9,1},{13,5},{2,10},{6,14},... | collective-permute-start | bytes 1572872 | tf_op jit(solution)/shard_map/ppermute | solution.py:560
  58.7 13.7 %copy-start.2 = (bf16[4,64,3584]{2,1,0:T(8,128)(2,1)S(1)}, bf16[4,64,3584]{2,1,0:T(8,128)(2,1)}, u32[]{:S(2)}) copy-start(bf16[4,64,3584]{2,1,0:T(8,128)(2,1)} %param.18) | copy-start | bytes 5505028
  58.8 25.8 %collective-permute-start.8 = (bf16[2,128,2048]{2,1,0:T(8,128)(2,1)S(1)}, bf16[2,128,2048]{2,1,0:T(8,128)(2,1)S(1)}, u32[]{:S(2)}, u32[]{:S(2)}) collective-permute-start(bf16[2,128,2048]{2,1,0:T(8,128)(2,1)S(1)} %pad_maximum_fusion), channel_id=1, source_target_pairs={{0,2},{1,3},{2,0},{3,1},{4,6},{5,7},{6,4},{7,5},{8,10},{9,11},{10,... | collective-permute-start | bytes 3145736 | tf_op jit(solution)/shard_map/ppermute | solution.py:587
  65.8 18.8 %copy-start.28 = (bf16[128,2048]{1,0:T(8,128)(2,1)}, bf16[128,2048]{1,0:T(8,128)(2,1)S(1)}, u32[]{:S(2)}) copy-start(bf16[128,2048]{1,0:T(8,128)(2,1)S(1)} %collective-permute-done.2.b3.b4) | copy-start | bytes 1572868
  68.0 16.7 %copy-start.31 = (bf16[128,2048]{1,0:T(8,128)(2,1)}, bf16[128,2048]{1,0:T(8,128)(2,1)S(1)}, u32[]{:S(2)}) copy-start(bf16[128,2048]{1,0:T(8,128)(2,1)S(1)} %collective-permute-done.10.b1) | copy-start | bytes 1572868
  68.0 15.0 %collective-permute-start.11 = (bf16[128,2048]{1,0:T(8,128)(2,1)S(1)}, bf16[128,2048]{1,0:T(8,128)(2,1)S(1)}, u32[]{:S(2)}, u32[]{:S(2)}) collective-permute-start(bf16[128,2048]{1,0:T(8,128)(2,1)S(1)} %collective-permute-done.2.b3.b4), channel_id=1, source_target_pairs={{0,4},{4,0},{8,12},{12,8},{1,5},{5,1},{9,13},{13,9},{2,6},{6,2},{1... | collective-permute-start | bytes 1572872 | tf_op jit(solution)/shard_map/ppermute | solution.py:564
  70.2 14.5 %collective-permute-start.9 = (bf16[128,2048]{1,0:T(8,128)(2,1)S(1)}, bf16[128,2048]{1,0:T(8,128)(2,1)S(1)}, u32[]{:S(2)}, u32[]{:S(2)}) collective-permute-start(bf16[128,2048]{1,0:T(8,128)(2,1)S(1)} %bitcast.43), channel_id=1, source_target_pairs={{0,1},{1,0},{2,3},{3,2},{4,8},{5,9},{6,10},{7,11},{8,4},{9,5},{10,... | collective-permute-start | bytes 1572872 | tf_op jit(solution)/shard_map/ppermute | solution.py:563
  70.2 36.2 %collective-permute-start.14 = (bf16[128,2048]{1,0:T(8,128)(2,1)}, bf16[128,2048]{1,0:T(8,128)(2,1)}, u32[]{:S(2)}, u32[]{:S(2)}) collective-permute-start(bf16[128,2048]{1,0:T(8,128)(2,1)} %bitcast.9.b0), channel_id=1, source_target_pairs={{0,4},{4,0},{8,12},{12,8},{1,5},{5,1},{9,13},{13,9},{2,6},{6,2},{1... | collective-permute-start | bytes 1572872 | tf_op jit(solution)/shard_map/ppermute | solution.py:560
  77.0 7.8 %copy-start.14 = (bf16[3584,256]{1,0:T(8,128)(2,1)}, bf16[3584,256]{1,0:T(8,128)(2,1)S(1)}, u32[]{:S(2)}) copy-start(bf16[3584,256]{1,0:T(8,128)(2,1)S(1)} %get-tuple-element.49.gates) | copy-start | bytes 5505028
  77.0 7.8 %copy-start.15 = (bf16[3584,256]{1,0:T(8,128)(2,1)}, bf16[3584,256]{1,0:T(8,128)(2,1)S(1)}, u32[]{:S(2)}) copy-start(bf16[3584,256]{1,0:T(8,128)(2,1)S(1)} %get-tuple-element.64.ups) | copy-start | bytes 5505028
  83.0 23.4 %collective-permute-start.3 = (bf16[128,2048]{1,0:T(8,128)(2,1)}, bf16[128,2048]{1,0:T(8,128)(2,1)S(1)}, u32[]{:S(2)}, u32[]{:S(2)}) collective-permute-start(bf16[128,2048]{1,0:T(8,128)(2,1)} %bitcast.9.b0), channel_id=1, source_target_pairs={{0,8},{4,12},{8,0},{12,4},{1,9},{5,13},{9,1},{13,5},{2,10},{6,14},... | collective-permute-start | bytes 1572872 | tf_op jit(solution)/shard_map/ppermute | solution.py:560
  86.6 23.1 %collective-permute-start.18 = (bf16[2,128,2048]{2,1,0:T(8,128)(2,1)}, bf16[2,128,2048]{2,1,0:T(8,128)(2,1)}, u32[]{:S(2)}, u32[]{:S(2)}) collective-permute-start(bf16[2,128,2048]{2,1,0:T(8,128)(2,1)} %pad_maximum_fusion.1), channel_id=1, source_target_pairs={{0,2},{1,3},{2,0},{3,1},{4,6},{5,7},{6,4},{7,5},{8,10},{9,11},{10,... | collective-permute-start | bytes 3145736 | tf_op jit(solution)/shard_map/ppermute | solution.py:593
  106.4 14.5 %copy-start.27 = (bf16[128,2048]{1,0:T(8,128)(2,1)}, bf16[128,2048]{1,0:T(8,128)(2,1)S(1)}, u32[]{:S(2)}) copy-start(bf16[128,2048]{1,0:T(8,128)(2,1)S(1)} %collective-permute-done.3.b3.b4) | copy-start | bytes 1572868
  106.4 3.9 %collective-permute-start.13 = (bf16[128,2048]{1,0:T(8,128)(2,1)}, bf16[128,2048]{1,0:T(8,128)(2,1)S(1)}, u32[]{:S(2)}, u32[]{:S(2)}) collective-permute-start(bf16[128,2048]{1,0:T(8,128)(2,1)} %bitcast.9.b0), channel_id=1, source_target_pairs={{0,1},{1,0},{2,3},{3,2},{4,8},{5,9},{6,10},{7,11},{8,4},{9,5},{10,... | collective-permute-start | bytes 1572872 | tf_op jit(solution)/shard_map/ppermute | solution.py:563
  106.4 14.3 %collective-permute-start.15 = (bf16[128,2048]{1,0:T(8,128)(2,1)S(1)}, bf16[128,2048]{1,0:T(8,128)(2,1)S(1)}, u32[]{:S(2)}, u32[]{:S(2)}) collective-permute-start(bf16[128,2048]{1,0:T(8,128)(2,1)S(1)} %collective-permute-done.3.b3.b4), channel_id=1, source_target_pairs={{0,4},{4,0},{8,12},{12,8},{1,5},{5,1},{9,13},{13,9},{2,6},{6,2},{1... | collective-permute-start | bytes 1572872 | tf_op jit(solution)/shard_map/ppermute | solution.py:564
  109.7 31.8 %collective-permute-start.19 = (bf16[3584,128]{1,0:T(8,128)(2,1)}, bf16[3584,128]{1,0:T(8,128)(2,1)}, u32[]{:S(2)}, u32[]{:S(2)}) collective-permute-start(bf16[3584,128]{1,0:T(8,128)(2,1)} %get-tuple-element.58), channel_id=1, source_target_pairs={{0,2},{1,3},{2,0},{3,1},{4,6},{5,7},{6,4},{7,5},{8,10},{9,11},{10,... | collective-permute-start | bytes 2752520 | tf_op jit(solution)/shard_map/ppermute | solution.py:597
  110.3 10.7 %copy-start.34 = (bf16[128,2048]{1,0:T(8,128)(2,1)}, bf16[128,2048]{1,0:T(8,128)(2,1)S(1)}, u32[]{:S(2)}) copy-start(bf16[128,2048]{1,0:T(8,128)(2,1)S(1)} %collective-permute-done.13.b2) | copy-start | bytes 1572868
  122.7 18.5 %copy-start.23 = (f32[384,128]{1,0:T(8,128)S(1)}, f32[384,128]{1,0:T(8,128)}, u32[]{:S(2)}) copy-start(f32[384,128]{1,0:T(8,128)} %copy-done.22) | copy-start | bytes 589828
  122.7 18.9 %copy-start.5 = (bf16[64,3584]{1,0:T(8,128)(2,1)S(1)}, bf16[64,3584]{1,0:T(8,128)(2,1)}, u32[]{:S(2)}) copy-start(bf16[64,3584]{1,0:T(8,128)(2,1)} %proj_gate.5) | copy-start | bytes 1376260
  122.7 18.9 %copy-start.7 = (bf16[64,3584]{1,0:T(8,128)(2,1)S(1)}, bf16[64,3584]{1,0:T(8,128)(2,1)}, u32[]{:S(2)}) copy-start(bf16[64,3584]{1,0:T(8,128)(2,1)} %proj_up.5) | copy-start | bytes 1376260
  122.7 18.9 %copy-start.10 = (bf16[2,64,3584]{2,1,0:T(8,128)(2,1)S(1)}, bf16[2,64,3584]{2,1,0:T(8,128)(2,1)}, u32[]{:S(2)}) copy-start(bf16[2,64,3584]{2,1,0:T(8,128)(2,1)} %param.22) | copy-start | bytes 2752516
  122.7 18.9 %copy-start.12 = (bf16[2,64,3584]{2,1,0:T(8,128)(2,1)S(1)}, bf16[2,64,3584]{2,1,0:T(8,128)(2,1)}, u32[]{:S(2)}) copy-start(bf16[2,64,3584]{2,1,0:T(8,128)(2,1)} %param.23) | copy-start | bytes 2752516
  122.7 34.7 %collective-permute-start.21 = (bf16[2,128,2048]{2,1,0:T(8,128)(2,1)}, bf16[2,128,2048]{2,1,0:T(8,128)(2,1)}, u32[]{:S(2)}, u32[]{:S(2)}) collective-permute-start(bf16[2,128,2048]{2,1,0:T(8,128)(2,1)} %pad_maximum_fusion.2), channel_id=1, source_target_pairs={{0,2},{1,3},{2,0},{3,1},{4,6},{5,7},{6,4},{7,5},{8,10},{9,11},{10,... | collective-permute-start | bytes 3145736 | tf_op jit(solution)/shard_map/ppermute | solution.py:600
  140.2 45.2 %collective-permute-start.22 = (bf16[3584,128]{1,0:T(8,128)(2,1)}, bf16[3584,128]{1,0:T(8,128)(2,1)S(1)}, u32[]{:S(2)}, u32[]{:S(2)}) collective-permute-start(bf16[3584,128]{1,0:T(8,128)(2,1)} %get-tuple-element.60), channel_id=1, source_target_pairs={{0,2},{1,3},{2,0},{3,1},{4,6},{5,7},{6,4},{7,5},{8,10},{9,11},{10,... | collective-permute-start | bytes 2752520 | tf_op jit(solution)/shard_map/ppermute | solution.py:604
  141.2 6.2 %collective-permute-start.16 = (f32[384,128]{1,0:T(8,128)S(1)}, f32[384,128]{1,0:T(8,128)S(1)}, u32[]{:S(2)}, u32[]{:S(2)}) collective-permute-start(f32[384,128]{1,0:T(8,128)S(1)} %copy-done.23), channel_id=1, source_target_pairs={{0,4},{4,0},{8,12},{12,8},{1,5},{5,1},{9,13},{13,9},{2,6},{6,2},{1... | collective-permute-start | bytes 589832 | tf_op jit(solution)/shard_map/ppermute | solution.py:605
  145.5 5.9 %collective-permute-start.20 = (f32[128,192]{1,0:T(8,128)S(1)}, f32[128,192]{1,0:T(8,128)S(1)}, u32[]{:S(2)}, u32[]{:S(2)}) collective-permute-start(f32[128,192]{1,0:T(8,128)S(1)} %pad_maximum_fusion.3), channel_id=1, source_target_pairs={{0,4},{4,0},{8,12},{12,8},{1,5},{5,1},{9,13},{13,9},{2,6},{6,2},{1... | collective-permute-start | bytes 294920 | tf_op jit(solution)/shard_map/ppermute | solution.py:610
  147.4 30.5 %collective-permute-start.17 = (f32[384,128]{1,0:T(8,128)S(1)}, f32[384,128]{1,0:T(8,128)S(1)}, u32[]{:S(2)}, u32[]{:S(2)}) collective-permute-start(f32[384,128]{1,0:T(8,128)S(1)} %add.32), channel_id=1, source_target_pairs={{0,8},{4,12},{8,0},{12,4},{1,9},{5,13},{9,1},{13,5},{2,10},{6,14},... | collective-permute-start | bytes 589832 | tf_op jit(solution)/shard_map/ppermute | solution.py:616
  151.4 26.5 %collective-permute-start.24 = (f32[128,192]{1,0:T(8,128)S(1)}, f32[128,192]{1,0:T(8,128)S(1)}, u32[]{:S(2)}, u32[]{:S(2)}) collective-permute-start(f32[128,192]{1,0:T(8,128)S(1)} %fusion), channel_id=1, source_target_pairs={{0,8},{4,12},{8,0},{12,4},{1,9},{5,13},{9,1},{13,5},{2,10},{6,14},... | collective-permute-start | bytes 294920 | tf_op jit(solution)/shard_map/ppermute | solution.py:617
  157.4 20.6 %copy-start.25 = (s32[2]{0:T(128)S(1)}, s32[2]{0:T(128)}, u32[]{:S(2)}) copy-start(s32[2]{0:T(128)} %lengths.2) | copy-start | bytes 28
  157.4 27.9 %copy-start.3 = (bf16[4,64,3584]{2,1,0:T(8,128)(2,1)S(1)}, bf16[4,64,3584]{2,1,0:T(8,128)(2,1)}, u32[]{:S(2)}) copy-start(bf16[4,64,3584]{2,1,0:T(8,128)(2,1)} %param.18) | copy-start | bytes 5505028
  178.9 6.4 %collective-permute-start.26 = (f32[2,192,64]{2,1,0:T(8,128)S(1)}, f32[2,192,64]{2,1,0:T(8,128)S(1)}, u32[]{:S(2)}, u32[]{:S(2)}) collective-permute-start(f32[2,192,64]{2,1,0:T(8,128)S(1)} %shard_map.161.q0), channel_id=1, source_target_pairs={{0,2},{1,3},{2,0},{3,1},{4,6},{5,7},{6,4},{7,5},{8,10},{9,11},{10,... | collective-permute-start | bytes 294920 | tf_op jit(solution)/shard_map/ppermute | solution.py:619
  179.2 6.2 %collective-permute-start.23 = (f32[128,128]{1,0:T(8,128)}, f32[128,128]{1,0:T(8,128)S(1)}, u32[]{:S(2)}, u32[]{:S(2)}) collective-permute-start(f32[128,128]{1,0:T(8,128)} %get-tuple-element.68), channel_id=1, source_target_pairs={{0,2},{1,3},{2,0},{3,1},{4,6},{5,7},{6,4},{7,5},{8,10},{9,11},{10,... | collective-permute-start | bytes 196616 | tf_op jit(solution)/shard_map/ppermute | solution.py:615
  181.0 7.5 %collective-permute-start.25 = (f32[2,192,64]{2,1,0:T(8,128)S(1)}, f32[2,192,64]{2,1,0:T(8,128)S(1)}, u32[]{:S(2)}, u32[]{:S(2)}) collective-permute-start(f32[2,192,64]{2,1,0:T(8,128)S(1)} %shard_map.161.q0), channel_id=1, source_target_pairs={{0,1},{1,0},{2,3},{3,2},{4,5},{5,4},{6,7},{7,6},{8,9},{9,8},{10,11... | collective-permute-start | bytes 294920 | tf_op jit(solution)/shard_map/ppermute | solution.py:620
  185.3 3.2 %collective-permute-start.27 = (f32[2,192,64]{2,1,0:T(8,128)S(1)}, f32[2,192,64]{2,1,0:T(8,128)S(1)}, u32[]{:S(2)}, u32[]{:S(2)}) collective-permute-start(f32[2,192,64]{2,1,0:T(8,128)S(1)} %collective-permute-done.26.q2), channel_id=1, source_target_pairs={{0,1},{1,0},{2,3},{3,2},{4,5},{5,4},{6,7},{7,6},{8,9},{9,8},{10,11... | collective-permute-start | bytes 294920 | tf_op jit(solution)/shard_map/ppermute | solution.py:620
  189.9 5.4 %collective-permute-start.30 = (f32[4,8]{1,0:T(4,128)S(1)}, f32[4,8]{1,0:T(4,128)S(1)}, u32[]{:S(2)}, u32[]{:S(2)}) collective-permute-start(f32[4,8]{1,0:T(4,128)S(1)} %shard_map.162), channel_id=1, source_target_pairs={{0,12},{4,8},{8,4},{12,0},{1,13},{5,9},{9,5},{13,1},{2,14},{6,10},... | collective-permute-start | bytes 392 | tf_op jit(solution)/shard_map/ppermute | solution.py:626
  190.3 5.1 %collective-permute-start.29 = (f32[4,8]{1,0:T(4,128)S(1)}, f32[4,8]{1,0:T(4,128)S(1)}, u32[]{:S(2)}, u32[]{:S(2)}) collective-permute-start(f32[4,8]{1,0:T(4,128)S(1)} %shard_map.162), channel_id=1, source_target_pairs={{0,8},{4,12},{8,0},{12,4},{1,9},{5,13},{9,1},{13,5},{2,10},{6,14},... | collective-permute-start | bytes 392 | tf_op jit(solution)/shard_map/ppermute | solution.py:626
  191.2 4.7 %collective-permute-start.28 = (f32[4,8]{1,0:T(4,128)S(1)}, f32[4,8]{1,0:T(4,128)S(1)}, u32[]{:S(2)}, u32[]{:S(2)}) collective-permute-start(f32[4,8]{1,0:T(4,128)S(1)} %shard_map.162), channel_id=1, source_target_pairs={{0,4},{4,0},{8,12},{12,8},{1,5},{5,1},{9,13},{13,9},{2,6},{6,2},{1... | collective-permute-start | bytes 392 | tf_op jit(solution)/shard_map/ppermute | solution.py:626
  (20 other events, 41.3 us)

commit v20 on v18

--- a/solution.py
+++ b/solution.py
@@ -191,24 +191,31 @@
                 ]
                 for copy in copies:
                     copy.start()
-                for tile in range(2):
-                    for copy in weight_copies(tile):
-                        copy.start()
+                for copy in weight_copies(0):
+                    copy.start()
                 for copy in copies:
                     copy.wait()
 
         for copy in far_copies:
             copy.wait()
 
+    own_copy, sib_copy = weight_copies(step)
+    own_copy.wait()
+
+    @pl.when(step == 0)
+    def _():
+        for copy in weight_copies(1):
+            copy.start()
+
     @pl.when(step + 2 < tiles)
     def _():
         for copy in weight_copies(step + 2):
             copy.start()
 
-    for copy in weight_copies(step):
-        copy.wait()
     slot = lax.rem(step, 3)
-    return project(held[slot, 0], stacked[0]) + project(held[slot, 1], stacked[1])
+    own_product = project(held[slot, 0], stacked[0])
+    sib_copy.wait()
+    return own_product + project(held[slot, 1], stacked[1])
 
 
 def add_sides(hidden_grad, gate, up, proj_gate, proj_up, sides):

time: 194 us -> 194 us (level)
  transfers between devices with their start and end apart: 31 -> 31, of which waited for: 15 -> 14; matrix products, arithmetic and copies ran while one was open for 4% -> 4% of each run, Pallas kernels for 32% -> 33%
where the time goes in v20:
time: 194 us
  Pallas kernels  64.5 us (33%)
  waiting for transfers between devices  54.8 us (28%)
  starting transfers between devices  50.6 us (26%)
  local copies, waits for them, and re-layouts  17.9 us (9%)
  other arithmetic  5.39 us (3%)
    pallas_call x2, Pallas kernels, partial_sums(): pl.pallas_call(partial_kernel, grid=(units // TILE,), in_specs=[SCALARS]...  30.1 us
    ppermute x3, waiting for transfers between devices, last_hops(): return (own, one, mid, two, two, outer(after(two, one)))  28 us
    ppermute x6, waiting for transfers between devices, first_hops(): return (own, outer(own), across(own))  19.3 us
    pallas_call x1, Pallas kernels, lent_sides(): pl.pallas_call(lent_kernel, grid=(units // TILE,), in_specs=[SCALARS] + [...  18.6 us
    ppermute x6, starting transfers between devices, first_hops(): return (own, outer(own), across(own))  18.4 us
    unnamed x74, local copies, waits for them, and re-layouts  14.6 us
    ppermute x1, starting transfers between devices, moving_plan(): q_sums = q_sums + after(across(q_sums), b_near)  6.01 us
    ppermute x3, starting transfers between devices, last_hops(): return (own, one, mid, two, two, outer(after(two, one)))  5.81 us
  transfers between devices with their start and end apart: 31, of which 14 were waited for; matrix products, arithmetic and copies ran while one was open for 4% of the time, Pallas kernels for 33%

profile of v20, /device:TPU:0, one launch (start us, length us, event | category | flops | bytes accessed | tf_op | source)
XLA Modules:
  0.0 193.6 jit_solution(15209317545316295678)
XLA Ops:
  0.5 1.3 slice.40
  1.8 2.6 %collective-permute-start.1 = (bf16[128,3584]{1,0:T(8,128)(2,1)S(1)}, bf16[128,3584]{1,0:T(8,128)(2,1)S(1)}, u32[]{:S(2)}, u32[]{:S(2)}) collective-permute-start(bf16[128,3584]{1,0:T(8,128)(2,1)S(1)} %bitcast.46), channel_id=1, source_target_pairs={{0,2},{1,3},{2,0},{3,1},{4,6},{5,7},{6,4},{7,5},{8,10},{9,11},{10,... | collective-permute-start | bytes 2752520 | tf_op jit(solution)/shard_map/ppermute | solution.py:582
  4.4 2.6 %collective-permute-start = (bf16[128,2048]{1,0:T(8,128)(2,1)}, bf16[128,2048]{1,0:T(8,128)(2,1)}, u32[]{:S(2)}, u32[]{:S(2)}) collective-permute-start(bf16[128,2048]{1,0:T(8,128)(2,1)} %bitcast.4.q_outgrad.b0), channel_id=1, source_target_pairs={{0,8},{4,12},{8,0},{12,4},{1,9},{5,13},{9,1},{13,5},{2,10},{6,14},... | collective-permute-start | bytes 1572872 | tf_op jit(solution)/shard_map/ppermute | solution.py:565
  7.0 1.6 collective-permute-start.4
  8.6 1.5 copy-done.1
  10.1 1.2 copy-done.4
  11.3 1.2 copy-done.9
  12.5 1.2 copy-done.11
  13.7 1.2 copy-done.17
  14.9 1.0 copy-done.18
  15.9 1.0 copy-done.19
  18.8 4.9 %shard_map.154 = (f32[384,128]{1,0:T(8,128)S(1)}, f32[384,64]{1,0:T(8,128)S(1)}) custom-call(bf16[256,2048]{1,0:T(8,128)(2,1)S(1)} %bitcast.39, bf16[128,2048]{1,0:T(8,128)(2,1)S(1)} %bitcast.40, bf16[256,2048]{1,0:T(8,128)(2,1)S(1)} %bitcast.34, bf16[128,2048]{1,0:T(8,128)(2,1)} %bitcast.4.q_outgrad.b0, bf16[64,2048]{1,0:T(8,128)(2,1)S(1)} %copy-done.20, ...), custom_call_target="tpu_custom_call" | custom-call | flops 1024 | bytes 1024 | tf_op jit(solution)/shard_map/pallas_call | solution.py:403
  23.7 7.1 %collective-permute-done.b3.b4 = bf16[128,2048]{1,0:T(8,128)(2,1)} collective-permute-done((bf16[128,2048]{1,0:T(8,128)(2,1)}, bf16[128,2048]{1,0:T(8,128)(2,1)}, u32[]{:S(2)}, u32[]{:S(2)}) %collective-permute-start) | collective-permute-done | bytes 524320 | tf_op jit(solution)/shard_map/ppermute | solution.py:565
  31.0 1.9 collective-permute-start.6
  32.8 1.0 slice.42
  35.4 10.3 %collective-permute-start.2 = (bf16[128,2048]{1,0:T(8,128)(2,1)S(1)}, bf16[128,2048]{1,0:T(8,128)(2,1)S(1)}, u32[]{:S(2)}, u32[]{:S(2)}) collective-permute-start(bf16[128,2048]{1,0:T(8,128)(2,1)S(1)} %bitcast.42), channel_id=1, source_target_pairs={{0,8},{4,12},{8,0},{12,4},{1,9},{5,13},{9,1},{13,5},{2,10},{6,14},... | collective-permute-start | bytes 1572872 | tf_op jit(solution)/shard_map/ppermute | solution.py:565
  45.7 11.6 %collective-permute-done.6.b5 = bf16[128,2048]{1,0:T(8,128)(2,1)} collective-permute-done((bf16[128,2048]{1,0:T(8,128)(2,1)}, bf16[128,2048]{1,0:T(8,128)(2,1)}, u32[]{:S(2)}, u32[]{:S(2)}) %collective-permute-start.6) | collective-permute-done | bytes 524320 | tf_op jit(solution)/shard_map/ppermute | solution.py:569
  57.2 1.5 select_bitcast_fusion.5
  59.5 6.3 %collective-permute-done.2.b3.b4 = bf16[128,2048]{1,0:T(8,128)(2,1)S(1)} collective-permute-done((bf16[128,2048]{1,0:T(8,128)(2,1)S(1)}, bf16[128,2048]{1,0:T(8,128)(2,1)S(1)}, u32[]{:S(2)}, u32[]{:S(2)}) %collective-permute-start.2) | collective-permute-done | bytes 524320 | tf_op jit(solution)/shard_map/ppermute | solution.py:565
  65.8 2.1 %collective-permute-done.10.b1 = bf16[128,2048]{1,0:T(8,128)(2,1)S(1)} collective-permute-done((bf16[128,2048]{1,0:T(8,128)(2,1)S(1)}, bf16[128,2048]{1,0:T(8,128)(2,1)S(1)}, u32[]{:S(2)}, u32[]{:S(2)}) %collective-permute-start.10) | collective-permute-done | bytes 524320 | tf_op jit(solution)/shard_map/ppermute | solution.py:565
  68.0 2.2 %collective-permute-start.11 = (bf16[128,2048]{1,0:T(8,128)(2,1)S(1)}, bf16[128,2048]{1,0:T(8,128)(2,1)S(1)}, u32[]{:S(2)}, u32[]{:S(2)}) collective-permute-start(bf16[128,2048]{1,0:T(8,128)(2,1)S(1)} %collective-permute-done.2.b3.b4), channel_id=1, source_target_pairs={{0,4},{4,0},{8,12},{12,8},{1,5},{5,1},{9,13},{13,9},{2,6},{6,2},{1... | collective-permute-start | bytes 1572872 | tf_op jit(solution)/shard_map/ppermute | solution.py:569
  70.2 2.2 %collective-permute-start.14 = (bf16[128,2048]{1,0:T(8,128)(2,1)}, bf16[128,2048]{1,0:T(8,128)(2,1)}, u32[]{:S(2)}, u32[]{:S(2)}) collective-permute-start(bf16[128,2048]{1,0:T(8,128)(2,1)} %bitcast.9.b0), channel_id=1, source_target_pairs={{0,4},{4,0},{8,12},{12,8},{1,5},{5,1},{9,13},{13,9},{2,6},{6,2},{1... | collective-permute-start | bytes 1572872 | tf_op jit(solution)/shard_map/ppermute | solution.py:565
  72.4 4.6 %shard_map.155 = (bf16[3584,256]{1,0:T(8,128)(2,1)S(1)}, bf16[3584,256]{1,0:T(8,128)(2,1)S(1)}) custom-call(bf16[256,3584]{1,0:T(8,128)(2,1)S(1)} %bitcast.29, bf16[256,3584]{1,0:T(8,128)(2,1)S(1)} %bitcast.32, bf16[128,3584]{1,0:T(8,128)(2,1)S(1)} %collective-permute-done.1.far_gate, bf16[128,3584]{1,0:T(8,128)(2,1)} %collective-permute-done.7.far_up), custom_call_target="tpu_custom_call" | custom-call | flops 1024 | bytes 1024 | tf_op jit(solution)/shard_map/pallas_call | solution.py:302
  77.0 5.9 %collective-permute-done.11.b5 = bf16[128,2048]{1,0:T(8,128)(2,1)S(1)} collective-permute-done((bf16[128,2048]{1,0:T(8,128)(2,1)S(1)}, bf16[128,2048]{1,0:T(8,128)(2,1)S(1)}, u32[]{:S(2)}, u32[]{:S(2)}) %collective-permute-start.11) | collective-permute-done | bytes 524320 | tf_op jit(solution)/shard_map/ppermute | solution.py:569
  83.0 1.6 collective-permute-start.3
  85.5 1.1 pad_maximum_fusion.1
  87.7 15.0 %shard_map.156 = (f32[3584,128]{1,0:T(8,128)}, bf16[3584,128]{1,0:T(8,128)(2,1)}) custom-call(s32[2]{0:T(128)} %pad_add_fusion.flags, bf16[128,2048]{1,0:T(8,128)(2,1)} %bitcast.4.q_outgrad.b0, bf16[128,2048]{1,0:T(8,128)(2,1)} %copy-done.30, bf16[128,2048]{1,0:T(8,128)(2,1)} %collective-permute-done.5.b2, bf16[128,2048]{1,0:T(8,128)(2,1)} %collective-permute-done.b3.b4, ...), custom_call_target="tpu_custom_call" | custom-call | flops 1024 | bytes 1024 | tf_op jit(solution)/shard_map/pallas_call | solution.py:248
  102.8 3.6 %collective-permute-done.3.b3.b4 = bf16[128,2048]{1,0:T(8,128)(2,1)S(1)} collective-permute-done((bf16[128,2048]{1,0:T(8,128)(2,1)}, bf16[128,2048]{1,0:T(8,128)(2,1)S(1)}, u32[]{:S(2)}, u32[]{:S(2)}) %collective-permute-start.3) | collective-permute-done | bytes 524320 | tf_op jit(solution)/shard_map/ppermute | solution.py:565
  106.4 1.7 collective-permute-start.15
  108.1 1.6 collective-permute-done.18.far
  110.3 10.5 %collective-permute-done.15.b5 = bf16[128,2048]{1,0:T(8,128)(2,1)S(1)} collective-permute-done((bf16[128,2048]{1,0:T(8,128)(2,1)S(1)}, bf16[128,2048]{1,0:T(8,128)(2,1)S(1)}, u32[]{:S(2)}, u32[]{:S(2)}) %collective-permute-start.15) | collective-permute-done | bytes 524320 | tf_op jit(solution)/shard_map/ppermute | solution.py:569
  121.5 1.1 pad_maximum_fusion.2
  122.7 1.3 collective-permute-start.21
  124.0 15.1 %shard_map.157 = (f32[3584,128]{1,0:T(8,128)}, bf16[3584,128]{1,0:T(8,128)(2,1)}) custom-call(s32[2]{0:T(128)} %pad_add_fusion.flags, bf16[128,2048]{1,0:T(8,128)(2,1)} %bitcast.45, bf16[128,2048]{1,0:T(8,128)(2,1)} %copy-done.31, bf16[128,2048]{1,0:T(8,128)(2,1)} %copy-done.33, bf16[128,2048]{1,0:T(8,128)(2,1)} %copy-done.28, bf16[128,2048]{1,0:T(8,128)(2,1)} %copy-done.28, ...), custom_call_target="tpu_custom_call" | custom-call | flops 1024 | bytes 1024 | tf_op jit(solution)/shard_map/pallas_call | solution.py:248
  140.5 1.5 copy-done.16
  141.9 2.4 %shard_map.158 = f32[128,128]{1,0:T(8,128)S(1)} custom-call(f32[3584,128]{1,0:T(8,128)S(1)} %copy-done.16, bf16[3584,128]{1,0:T(8,128)(2,1)} %collective-permute-done.19.returned, bf16[128,3584]{1,0:T(8,128)(2,1)S(1)} %bitcast.36, bf16[128,3584]{1,0:T(8,128)(2,1)S(1)} %bitcast.38, bf16[64,3584]{1,0:T(8,128)(2,1)S(1)} %copy-done.5, bf16[64,3584]{1,0:T(8,128)(2,1)S(1)} %copy-done.7), custom_call_target="tpu_custom_call" | custom-call | flops 1024 | bytes 1024 | tf_op jit(solution)/shard_map/pallas_call | solution.py:275
  144.4 1.8 collective-permute-start.20
  146.3 4.0 %collective-permute-start.17 = (f32[384,128]{1,0:T(8,128)S(1)}, f32[384,128]{1,0:T(8,128)S(1)}, u32[]{:S(2)}, u32[]{:S(2)}) collective-permute-start(f32[384,128]{1,0:T(8,128)S(1)} %add.32), channel_id=1, source_target_pairs={{0,8},{4,12},{8,0},{12,4},{1,9},{5,13},{9,1},{13,5},{2,10},{6,14},... | collective-permute-start | bytes 589832 | tf_op jit(solution)/shard_map/ppermute | solution.py:621
  150.3 6.0 %collective-permute-start.24 = (f32[128,192]{1,0:T(8,128)S(1)}, f32[128,192]{1,0:T(8,128)S(1)}, u32[]{:S(2)}, u32[]{:S(2)}) collective-permute-start(f32[128,192]{1,0:T(8,128)S(1)} %fusion), channel_id=1, source_target_pairs={{0,8},{4,12},{8,0},{12,4},{1,9},{5,13},{9,1},{13,5},{2,10},{6,14},... | collective-permute-start | bytes 294920 | tf_op jit(solution)/shard_map/ppermute | solution.py:622
  156.3 18.6 %shard_map.159 = (f32[128,128]{1,0:T(8,128)}, f32[128,128]{1,0:T(8,128)}) custom-call(s32[2]{0:T(128)} %pad_add_fusion.flags, bf16[128,2048]{1,0:T(8,128)(2,1)} %bitcast.9.b0, bf16[128,2048]{1,0:T(8,128)(2,1)} %collective-permute-done.14.b1, bf16[128,2048]{1,0:T(8,128)(2,1)} %copy-done.34, bf16[128,2048]{1,0:T(8,128)(2,1)} %copy-done.27, ...), custom_call_target="tpu_custom_call" | custom-call | flops 1024 | bytes 1024 | tf_op jit(solution)/shard_map/pallas_call | solution.py:344
  176.2 1.8 collective-permute-start.23
  178.1 4.3 %collective-permute-done.23.far = f32[128,128]{1,0:T(8,128)S(1)} collective-permute-done((f32[128,128]{1,0:T(8,128)}, f32[128,128]{1,0:T(8,128)S(1)}, u32[]{:S(2)}, u32[]{:S(2)}) %collective-permute-start.23) | collective-permute-done | bytes 65568 | tf_op jit(solution)/shard_map/ppermute | solution.py:620
  182.5 1.5 copy-done.13
  184.0 1.6 shard_map.160.early
  185.6 1.4 shard_map.162
  187.0 1.4 collective-permute-start.30
  189.4 2.0 %collective-permute-start.28 = (f32[4,8]{1,0:T(4,128)S(1)}, f32[4,8]{1,0:T(4,128)S(1)}, u32[]{:S(2)}, u32[]{:S(2)}) collective-permute-start(f32[4,8]{1,0:T(4,128)S(1)} %shard_map.162), channel_id=1, source_target_pairs={{0,4},{4,0},{8,12},{12,8},{1,5},{5,1},{9,13},{13,9},{2,6},{6,2},{1... | collective-permute-start | bytes 392 | tf_op jit(solution)/shard_map/ppermute | solution.py:631
  191.5 1.0 collective-permute-done.30
  (117 shorter events, 13.0 us)
Async XLA Ops:
  0.0 8.6 %copy-start = (bf16[4,64,3584]{2,1,0:T(8,128)(2,1)S(1)}, bf16[4,64,3584]{2,1,0:T(8,128)(2,1)}, u32[]{:S(2)}) copy-start(bf16[4,64,3584]{2,1,0:T(8,128)(2,1)} %param.17) | copy-start | bytes 5505028
  0.0 87.7 %collective-permute-start.12 = (bf16[3584,2048]{1,0:T(8,128)(2,1)}, bf16[3584,2048]{1,0:T(8,128)(2,1)}, u32[]{:S(2)}, u32[]{:S(2)}) collective-permute-start(bf16[3584,2048]{1,0:T(8,128)(2,1)} %weight_own.5), channel_id=1, source_target_pairs={{0,1},{1,0},{2,3},{3,2},{4,5},{5,4},{6,7},{7,6},{8,9},{9,8},{10,11... | collective-permute-start | bytes 44040200 | tf_op jit(solution)/shard_map/ppermute | solution.py:580
  1.8 32.0 %collective-permute-start.1 = (bf16[128,3584]{1,0:T(8,128)(2,1)S(1)}, bf16[128,3584]{1,0:T(8,128)(2,1)S(1)}, u32[]{:S(2)}, u32[]{:S(2)}) collective-permute-start(bf16[128,3584]{1,0:T(8,128)(2,1)S(1)} %bitcast.46), channel_id=1, source_target_pairs={{0,2},{1,3},{2,0},{3,1},{4,6},{5,7},{6,4},{7,5},{8,10},{9,11},{10,... | collective-permute-start | bytes 2752520 | tf_op jit(solution)/shard_map/ppermute | solution.py:582
  4.4 26.5 %collective-permute-start = (bf16[128,2048]{1,0:T(8,128)(2,1)}, bf16[128,2048]{1,0:T(8,128)(2,1)}, u32[]{:S(2)}, u32[]{:S(2)}) collective-permute-start(bf16[128,2048]{1,0:T(8,128)(2,1)} %bitcast.4.q_outgrad.b0), channel_id=1, source_target_pairs={{0,8},{4,12},{8,0},{12,4},{1,9},{5,13},{9,1},{13,5},{2,10},{6,14},... | collective-permute-start | bytes 1572872 | tf_op jit(solution)/shard_map/ppermute | solution.py:565
  7.0 24.0 %collective-permute-start.4 = (bf16[128,2048]{1,0:T(8,128)(2,1)}, bf16[128,2048]{1,0:T(8,128)(2,1)S(1)}, u32[]{:S(2)}, u32[]{:S(2)}) collective-permute-start(bf16[128,2048]{1,0:T(8,128)(2,1)} %bitcast.4.q_outgrad.b0), channel_id=1, source_target_pairs={{0,4},{4,0},{8,12},{12,8},{1,5},{5,1},{9,13},{13,9},{2,6},{6,2},{1... | collective-permute-start | bytes 1572872 | tf_op jit(solution)/shard_map/ppermute | solution.py:565
  23.7 11.6 %copy-start.22 = (f32[384,128]{1,0:T(8,128)}, f32[384,128]{1,0:T(8,128)S(1)}, u32[]{:S(2)}) copy-start(f32[384,128]{1,0:T(8,128)S(1)} %get-tuple-element.56) | copy-start | bytes 589828
  31.0 4.4 %collective-permute-start.5 = (bf16[128,2048]{1,0:T(8,128)(2,1)}, bf16[128,2048]{1,0:T(8,128)(2,1)}, u32[]{:S(2)}, u32[]{:S(2)}) collective-permute-start(bf16[128,2048]{1,0:T(8,128)(2,1)} %bitcast.4.q_outgrad.b0), channel_id=1, source_target_pairs={{0,1},{1,0},{2,3},{3,2},{4,8},{5,9},{6,10},{7,11},{8,4},{9,5},{10,... | collective-permute-start | bytes 1572872 | tf_op jit(solution)/shard_map/ppermute | solution.py:568
  31.0 26.3 %collective-permute-start.6 = (bf16[128,2048]{1,0:T(8,128)(2,1)}, bf16[128,2048]{1,0:T(8,128)(2,1)}, u32[]{:S(2)}, u32[]{:S(2)}) collective-permute-start(bf16[128,2048]{1,0:T(8,128)(2,1)} %collective-permute-done.b3.b4), channel_id=1, source_target_pairs={{0,4},{4,0},{8,12},{12,8},{1,5},{5,1},{9,13},{13,9},{2,6},{6,2},{1... | collective-permute-start | bytes 1572872 | tf_op jit(solution)/shard_map/ppermute | solution.py:569
  33.8 25.0 %collective-permute-start.7 = (bf16[128,3584]{1,0:T(8,128)(2,1)}, bf16[128,3584]{1,0:T(8,128)(2,1)}, u32[]{:S(2)}, u32[]{:S(2)}) collective-permute-start(bf16[128,3584]{1,0:T(8,128)(2,1)} %bitcast.16), channel_id=1, source_target_pairs={{0,2},{1,3},{2,0},{3,1},{4,6},{5,7},{6,4},{7,5},{8,10},{9,11},{10,... | collective-permute-start | bytes 2752520 | tf_op jit(solution)/shard_map/ppermute | solution.py:590
  35.3 49.3 %copy-start.29 = (bf16[2,64,2048]{2,1,0:T(8,128)(2,1)}, bf16[2,64,2048]{2,1,0:T(8,128)(2,1)S(1)}, u32[]{:S(2)}) copy-start(bf16[2,64,2048]{2,1,0:T(8,128)(2,1)S(1)} %get-tuple-element.71) | copy-start | bytes 1572868
  35.3 32.7 %collective-permute-start.10 = (bf16[128,2048]{1,0:T(8,128)(2,1)S(1)}, bf16[128,2048]{1,0:T(8,128)(2,1)S(1)}, u32[]{:S(2)}, u32[]{:S(2)}) collective-permute-start(bf16[128,2048]{1,0:T(8,128)(2,1)S(1)} %bitcast.41), channel_id=1, source_target_pairs={{0,4},{4,0},{8,12},{12,8},{1,5},{5,1},{9,13},{13,9},{2,6},{6,2},{1... | collective-permute-start | bytes 1572872 | tf_op jit(solution)/shard_map/ppermute | solution.py:565
  35.4 30.5 %collective-permute-start.2 = (bf16[128,2048]{1,0:T(8,128)(2,1)S(1)}, bf16[128,2048]{1,0:T(8,128)(2,1)S(1)}, u32[]{:S(2)}, u32[]{:S(2)}) collective-permute-start(bf16[128,2048]{1,0:T(8,128)(2,1)S(1)} %bitcast.42), channel_id=1, source_target_pairs={{0,8},{4,12},{8,0},{12,4},{1,9},{5,13},{9,1},{13,5},{2,10},{6,14},... | collective-permute-start | bytes 1572872 | tf_op jit(solution)/shard_map/ppermute | solution.py:565
  58.7 13.7 %copy-start.2 = (bf16[4,64,3584]{2,1,0:T(8,128)(2,1)S(1)}, bf16[4,64,3584]{2,1,0:T(8,128)(2,1)}, u32[]{:S(2)}) copy-start(bf16[4,64,3584]{2,1,0:T(8,128)(2,1)} %param.18) | copy-start | bytes 5505028
  58.8 25.8 %collective-permute-start.8 = (bf16[2,128,2048]{2,1,0:T(8,128)(2,1)S(1)}, bf16[2,128,2048]{2,1,0:T(8,128)(2,1)S(1)}, u32[]{:S(2)}, u32[]{:S(2)}) collective-permute-start(bf16[2,128,2048]{2,1,0:T(8,128)(2,1)S(1)} %pad_maximum_fusion), channel_id=1, source_target_pairs={{0,2},{1,3},{2,0},{3,1},{4,6},{5,7},{6,4},{7,5},{8,10},{9,11},{10,... | collective-permute-start | bytes 3145736 | tf_op jit(solution)/shard_map/ppermute | solution.py:592
  65.8 18.8 %copy-start.28 = (bf16[128,2048]{1,0:T(8,128)(2,1)}, bf16[128,2048]{1,0:T(8,128)(2,1)S(1)}, u32[]{:S(2)}) copy-start(bf16[128,2048]{1,0:T(8,128)(2,1)S(1)} %collective-permute-done.2.b3.b4) | copy-start | bytes 1572868
  68.0 16.7 %copy-start.31 = (bf16[128,2048]{1,0:T(8,128)(2,1)}, bf16[128,2048]{1,0:T(8,128)(2,1)S(1)}, u32[]{:S(2)}) copy-start(bf16[128,2048]{1,0:T(8,128)(2,1)S(1)} %collective-permute-done.10.b1) | copy-start | bytes 1572868
  68.0 15.0 %collective-permute-start.11 = (bf16[128,2048]{1,0:T(8,128)(2,1)S(1)}, bf16[128,2048]{1,0:T(8,128)(2,1)S(1)}, u32[]{:S(2)}, u32[]{:S(2)}) collective-permute-start(bf16[128,2048]{1,0:T(8,128)(2,1)S(1)} %collective-permute-done.2.b3.b4), channel_id=1, source_target_pairs={{0,4},{4,0},{8,12},{12,8},{1,5},{5,1},{9,13},{13,9},{2,6},{6,2},{1... | collective-permute-start | bytes 1572872 | tf_op jit(solution)/shard_map/ppermute | solution.py:569
  70.2 14.5 %collective-permute-start.9 = (bf16[128,2048]{1,0:T(8,128)(2,1)S(1)}, bf16[128,2048]{1,0:T(8,128)(2,1)S(1)}, u32[]{:S(2)}, u32[]{:S(2)}) collective-permute-start(bf16[128,2048]{1,0:T(8,128)(2,1)S(1)} %bitcast.43), channel_id=1, source_target_pairs={{0,1},{1,0},{2,3},{3,2},{4,8},{5,9},{6,10},{7,11},{8,4},{9,5},{10,... | collective-permute-start | bytes 1572872 | tf_op jit(solution)/shard_map/ppermute | solution.py:568
  70.2 36.2 %collective-permute-start.14 = (bf16[128,2048]{1,0:T(8,128)(2,1)}, bf16[128,2048]{1,0:T(8,128)(2,1)}, u32[]{:S(2)}, u32[]{:S(2)}) collective-permute-start(bf16[128,2048]{1,0:T(8,128)(2,1)} %bitcast.9.b0), channel_id=1, source_target_pairs={{0,4},{4,0},{8,12},{12,8},{1,5},{5,1},{9,13},{13,9},{2,6},{6,2},{1... | collective-permute-start | bytes 1572872 | tf_op jit(solution)/shard_map/ppermute | solution.py:565
  77.0 7.8 %copy-start.14 = (bf16[3584,256]{1,0:T(8,128)(2,1)}, bf16[3584,256]{1,0:T(8,128)(2,1)S(1)}, u32[]{:S(2)}) copy-start(bf16[3584,256]{1,0:T(8,128)(2,1)S(1)} %get-tuple-element.49.gates) | copy-start | bytes 5505028
  77.0 7.8 %copy-start.15 = (bf16[3584,256]{1,0:T(8,128)(2,1)}, bf16[3584,256]{1,0:T(8,128)(2,1)S(1)}, u32[]{:S(2)}) copy-start(bf16[3584,256]{1,0:T(8,128)(2,1)S(1)} %get-tuple-element.64.ups) | copy-start | bytes 5505028
  83.0 23.4 %collective-permute-start.3 = (bf16[128,2048]{1,0:T(8,128)(2,1)}, bf16[128,2048]{1,0:T(8,128)(2,1)S(1)}, u32[]{:S(2)}, u32[]{:S(2)}) collective-permute-start(bf16[128,2048]{1,0:T(8,128)(2,1)} %bitcast.9.b0), channel_id=1, source_target_pairs={{0,8},{4,12},{8,0},{12,4},{1,9},{5,13},{9,1},{13,5},{2,10},{6,14},... | collective-permute-start | bytes 1572872 | tf_op jit(solution)/shard_map/ppermute | solution.py:565
  86.6 23.1 %collective-permute-start.18 = (bf16[2,128,2048]{2,1,0:T(8,128)(2,1)}, bf16[2,128,2048]{2,1,0:T(8,128)(2,1)}, u32[]{:S(2)}, u32[]{:S(2)}) collective-permute-start(bf16[2,128,2048]{2,1,0:T(8,128)(2,1)} %pad_maximum_fusion.1), channel_id=1, source_target_pairs={{0,2},{1,3},{2,0},{3,1},{4,6},{5,7},{6,4},{7,5},{8,10},{9,11},{10,... | collective-permute-start | bytes 3145736 | tf_op jit(solution)/shard_map/ppermute | solution.py:598
  106.4 14.5 %copy-start.27 = (bf16[128,2048]{1,0:T(8,128)(2,1)}, bf16[128,2048]{1,0:T(8,128)(2,1)S(1)}, u32[]{:S(2)}) copy-start(bf16[128,2048]{1,0:T(8,128)(2,1)S(1)} %collective-permute-done.3.b3.b4) | copy-start | bytes 1572868
  106.4 3.9 %collective-permute-start.13 = (bf16[128,2048]{1,0:T(8,128)(2,1)}, bf16[128,2048]{1,0:T(8,128)(2,1)S(1)}, u32[]{:S(2)}, u32[]{:S(2)}) collective-permute-start(bf16[128,2048]{1,0:T(8,128)(2,1)} %bitcast.9.b0), channel_id=1, source_target_pairs={{0,1},{1,0},{2,3},{3,2},{4,8},{5,9},{6,10},{7,11},{8,4},{9,5},{10,... | collective-permute-start | bytes 1572872 | tf_op jit(solution)/shard_map/ppermute | solution.py:568
  106.4 14.3 %collective-permute-start.15 = (bf16[128,2048]{1,0:T(8,128)(2,1)S(1)}, bf16[128,2048]{1,0:T(8,128)(2,1)S(1)}, u32[]{:S(2)}, u32[]{:S(2)}) collective-permute-start(bf16[128,2048]{1,0:T(8,128)(2,1)S(1)} %collective-permute-done.3.b3.b4), channel_id=1, source_target_pairs={{0,4},{4,0},{8,12},{12,8},{1,5},{5,1},{9,13},{13,9},{2,6},{6,2},{1... | collective-permute-start | bytes 1572872 | tf_op jit(solution)/shard_map/ppermute | solution.py:569
  109.7 30.7 %collective-permute-start.19 = (bf16[3584,128]{1,0:T(8,128)(2,1)}, bf16[3584,128]{1,0:T(8,128)(2,1)}, u32[]{:S(2)}, u32[]{:S(2)}) collective-permute-start(bf16[3584,128]{1,0:T(8,128)(2,1)} %get-tuple-element.58), channel_id=1, source_target_pairs={{0,2},{1,3},{2,0},{3,1},{4,6},{5,7},{6,4},{7,5},{8,10},{9,11},{10,... | collective-permute-start | bytes 2752520 | tf_op jit(solution)/shard_map/ppermute | solution.py:602
  110.3 10.7 %copy-start.34 = (bf16[128,2048]{1,0:T(8,128)(2,1)}, bf16[128,2048]{1,0:T(8,128)(2,1)S(1)}, u32[]{:S(2)}) copy-start(bf16[128,2048]{1,0:T(8,128)(2,1)S(1)} %collective-permute-done.13.b2) | copy-start | bytes 1572868
  122.7 17.4 %copy-start.23 = (f32[384,128]{1,0:T(8,128)S(1)}, f32[384,128]{1,0:T(8,128)}, u32[]{:S(2)}) copy-start(f32[384,128]{1,0:T(8,128)} %copy-done.22) | copy-start | bytes 589828
  122.7 17.7 %copy-start.5 = (bf16[64,3584]{1,0:T(8,128)(2,1)S(1)}, bf16[64,3584]{1,0:T(8,128)(2,1)}, u32[]{:S(2)}) copy-start(bf16[64,3584]{1,0:T(8,128)(2,1)} %proj_gate.5) | copy-start | bytes 1376260
  122.7 17.7 %copy-start.7 = (bf16[64,3584]{1,0:T(8,128)(2,1)S(1)}, bf16[64,3584]{1,0:T(8,128)(2,1)}, u32[]{:S(2)}) copy-start(bf16[64,3584]{1,0:T(8,128)(2,1)} %proj_up.5) | copy-start | bytes 1376260
  122.7 17.7 %copy-start.10 = (bf16[2,64,3584]{2,1,0:T(8,128)(2,1)S(1)}, bf16[2,64,3584]{2,1,0:T(8,128)(2,1)}, u32[]{:S(2)}) copy-start(bf16[2,64,3584]{2,1,0:T(8,128)(2,1)} %param.22) | copy-start | bytes 2752516
  122.7 17.8 %copy-start.12 = (bf16[2,64,3584]{2,1,0:T(8,128)(2,1)S(1)}, bf16[2,64,3584]{2,1,0:T(8,128)(2,1)}, u32[]{:S(2)}) copy-start(bf16[2,64,3584]{2,1,0:T(8,128)(2,1)} %param.23) | copy-start | bytes 2752516
  122.7 33.6 %collective-permute-start.21 = (bf16[2,128,2048]{2,1,0:T(8,128)(2,1)}, bf16[2,128,2048]{2,1,0:T(8,128)(2,1)}, u32[]{:S(2)}, u32[]{:S(2)}) collective-permute-start(bf16[2,128,2048]{2,1,0:T(8,128)(2,1)} %pad_maximum_fusion.2), channel_id=1, source_target_pairs={{0,2},{1,3},{2,0},{3,1},{4,6},{5,7},{6,4},{7,5},{8,10},{9,11},{10,... | collective-permute-start | bytes 3145736 | tf_op jit(solution)/shard_map/ppermute | solution.py:605
  139.1 43.4 %collective-permute-start.22 = (bf16[3584,128]{1,0:T(8,128)(2,1)}, bf16[3584,128]{1,0:T(8,128)(2,1)S(1)}, u32[]{:S(2)}, u32[]{:S(2)}) collective-permute-start(bf16[3584,128]{1,0:T(8,128)(2,1)} %get-tuple-element.60), channel_id=1, source_target_pairs={{0,2},{1,3},{2,0},{3,1},{4,6},{5,7},{6,4},{7,5},{8,10},{9,11},{10,... | collective-permute-start | bytes 2752520 | tf_op jit(solution)/shard_map/ppermute | solution.py:609
  140.1 6.2 %collective-permute-start.16 = (f32[384,128]{1,0:T(8,128)S(1)}, f32[384,128]{1,0:T(8,128)S(1)}, u32[]{:S(2)}, u32[]{:S(2)}) collective-permute-start(f32[384,128]{1,0:T(8,128)S(1)} %copy-done.23), channel_id=1, source_target_pairs={{0,4},{4,0},{8,12},{12,8},{1,5},{5,1},{9,13},{13,9},{2,6},{6,2},{1... | collective-permute-start | bytes 589832 | tf_op jit(solution)/shard_map/ppermute | solution.py:610
  144.4 5.9 %collective-permute-start.20 = (f32[128,192]{1,0:T(8,128)S(1)}, f32[128,192]{1,0:T(8,128)S(1)}, u32[]{:S(2)}, u32[]{:S(2)}) collective-permute-start(f32[128,192]{1,0:T(8,128)S(1)} %pad_maximum_fusion.3), channel_id=1, source_target_pairs={{0,4},{4,0},{8,12},{12,8},{1,5},{5,1},{9,13},{13,9},{2,6},{6,2},{1... | collective-permute-start | bytes 294920 | tf_op jit(solution)/shard_map/ppermute | solution.py:615
  146.3 28.7 %collective-permute-start.17 = (f32[384,128]{1,0:T(8,128)S(1)}, f32[384,128]{1,0:T(8,128)S(1)}, u32[]{:S(2)}, u32[]{:S(2)}) collective-permute-start(f32[384,128]{1,0:T(8,128)S(1)} %add.32), channel_id=1, source_target_pairs={{0,8},{4,12},{8,0},{12,4},{1,9},{5,13},{9,1},{13,5},{2,10},{6,14},... | collective-permute-start | bytes 589832 | tf_op jit(solution)/shard_map/ppermute | solution.py:621
  150.3 24.7 %collective-permute-start.24 = (f32[128,192]{1,0:T(8,128)S(1)}, f32[128,192]{1,0:T(8,128)S(1)}, u32[]{:S(2)}, u32[]{:S(2)}) collective-permute-start(f32[128,192]{1,0:T(8,128)S(1)} %fusion), channel_id=1, source_target_pairs={{0,8},{4,12},{8,0},{12,4},{1,9},{5,13},{9,1},{13,5},{2,10},{6,14},... | collective-permute-start | bytes 294920 | tf_op jit(solution)/shard_map/ppermute | solution.py:622
  156.3 18.7 %copy-start.25 = (s32[2]{0:T(128)S(1)}, s32[2]{0:T(128)}, u32[]{:S(2)}) copy-start(s32[2]{0:T(128)} %lengths.2) | copy-start | bytes 28
  156.3 26.1 %copy-start.3 = (bf16[4,64,3584]{2,1,0:T(8,128)(2,1)S(1)}, bf16[4,64,3584]{2,1,0:T(8,128)(2,1)}, u32[]{:S(2)}) copy-start(bf16[4,64,3584]{2,1,0:T(8,128)(2,1)} %param.18) | copy-start | bytes 5505028
  176.0 6.4 %collective-permute-start.26 = (f32[2,192,64]{2,1,0:T(8,128)S(1)}, f32[2,192,64]{2,1,0:T(8,128)S(1)}, u32[]{:S(2)}, u32[]{:S(2)}) collective-permute-start(f32[2,192,64]{2,1,0:T(8,128)S(1)} %shard_map.161.q0), channel_id=1, source_target_pairs={{0,2},{1,3},{2,0},{3,1},{4,6},{5,7},{6,4},{7,5},{8,10},{9,11},{10,... | collective-permute-start | bytes 294920 | tf_op jit(solution)/shard_map/ppermute | solution.py:624
  176.2 6.2 %collective-permute-start.23 = (f32[128,128]{1,0:T(8,128)}, f32[128,128]{1,0:T(8,128)S(1)}, u32[]{:S(2)}, u32[]{:S(2)}) collective-permute-start(f32[128,128]{1,0:T(8,128)} %get-tuple-element.68), channel_id=1, source_target_pairs={{0,2},{1,3},{2,0},{3,1},{4,6},{5,7},{6,4},{7,5},{8,10},{9,11},{10,... | collective-permute-start | bytes 196616 | tf_op jit(solution)/shard_map/ppermute | solution.py:620
  178.1 7.5 %collective-permute-start.25 = (f32[2,192,64]{2,1,0:T(8,128)S(1)}, f32[2,192,64]{2,1,0:T(8,128)S(1)}, u32[]{:S(2)}, u32[]{:S(2)}) collective-permute-start(f32[2,192,64]{2,1,0:T(8,128)S(1)} %shard_map.161.q0), channel_id=1, source_target_pairs={{0,1},{1,0},{2,3},{3,2},{4,5},{5,4},{6,7},{7,6},{8,9},{9,8},{10,11... | collective-permute-start | bytes 294920 | tf_op jit(solution)/shard_map/ppermute | solution.py:625
  182.4 3.2 %collective-permute-start.27 = (f32[2,192,64]{2,1,0:T(8,128)S(1)}, f32[2,192,64]{2,1,0:T(8,128)S(1)}, u32[]{:S(2)}, u32[]{:S(2)}) collective-permute-start(f32[2,192,64]{2,1,0:T(8,128)S(1)} %collective-permute-done.26.q2), channel_id=1, source_target_pairs={{0,1},{1,0},{2,3},{3,2},{4,5},{5,4},{6,7},{7,6},{8,9},{9,8},{10,11... | collective-permute-start | bytes 294920 | tf_op jit(solution)/shard_map/ppermute | solution.py:625
  187.0 5.4 %collective-permute-start.30 = (f32[4,8]{1,0:T(4,128)S(1)}, f32[4,8]{1,0:T(4,128)S(1)}, u32[]{:S(2)}, u32[]{:S(2)}) collective-permute-start(f32[4,8]{1,0:T(4,128)S(1)} %shard_map.162), channel_id=1, source_target_pairs={{0,12},{4,8},{8,4},{12,0},{1,13},{5,9},{9,5},{13,1},{2,14},{6,10},... | collective-permute-start | bytes 392 | tf_op jit(solution)/shard_map/ppermute | solution.py:631
  188.5 4.5 %collective-permute-start.29 = (f32[4,8]{1,0:T(4,128)S(1)}, f32[4,8]{1,0:T(4,128)S(1)}, u32[]{:S(2)}, u32[]{:S(2)}) collective-permute-start(f32[4,8]{1,0:T(4,128)S(1)} %shard_map.162), channel_id=1, source_target_pairs={{0,8},{4,12},{8,0},{12,4},{1,9},{5,13},{9,1},{13,5},{2,10},{6,14},... | collective-permute-start | bytes 392 | tf_op jit(solution)/shard_map/ppermute | solution.py:631
  189.4 3.6 %collective-permute-start.28 = (f32[4,8]{1,0:T(4,128)S(1)}, f32[4,8]{1,0:T(4,128)S(1)}, u32[]{:S(2)}, u32[]{:S(2)}) collective-permute-start(f32[4,8]{1,0:T(4,128)S(1)} %shard_map.162), channel_id=1, source_target_pairs={{0,4},{4,0},{8,12},{12,8},{1,5},{5,1},{9,13},{13,9},{2,6},{6,2},{1... | collective-permute-start | bytes 392 | tf_op jit(solution)/shard_map/ppermute | solution.py:631
  (20 other events, 41.3 us)

commit v21 on v18

--- a/solution.py
+++ b/solution.py
@@ -599,11 +599,11 @@
     a_near_sum, a_far_sum = partial_sums(
         flags, a_blocks, after(a_far, b_send), weight_own, weight_sib
     )
-    a_returned = to_chip(a_far_sum)
     in_out = own_in_out + outer(after(own_in_out, b_send))
     q_gradient = finished_sides(
         q_near_sum, after(q_returned, a_far_sum), q_gate, q_up, proj_gate, proj_up
     )
+    a_returned = to_chip(after(a_far_sum, q_gradient))
     q_sums = jnp.concatenate([q_gradient, hidden[2 * cut :]], axis=1)
     q_sums = q_sums + outer(q_sums)
     b_near, b_away = lent_sides(

time: 194 us -> 196 us (1.010)
  waiting for transfers between devices: 56.3 us -> 60.9 us
  starting transfers between devices: 50.6 us -> 47.3 us
    ppermute x1, waiting for transfers between devices: 0.06 us -> 5.43 us  [moving_plan(): in_out = own_in_out + outer(after(own_in_out, b_send))]
    ppermute x1, starting transfers between devices: 6 us -> 2.77 us  [moving_plan(): q_sums = q_sums + after(across(q_sums), b_near)]
    unnamed x74 -> x72, local copies, waits for them, and re-layouts: 14.6 us -> 15.6 us
  transfers between devices with their start and end apart: 31 -> 31, of which waited for: 15 -> 13; matrix products, arithmetic and copies ran while one was open for 4% -> 4% of each run, Pallas kernels for 32% -> 31%
where the time goes in v21:
time: 196 us
  Pallas kernels  62.6 us (32%)
  waiting for transfers between devices  60.9 us (31%)
  starting transfers between devices  47.3 us (24%)
  local copies, waits for them, and re-layouts  19.1 us (10%)
  other arithmetic  5.44 us (3%)
    pallas_call x2, Pallas kernels, partial_sums(): pl.pallas_call(partial_kernel, grid=(units // TILE,), in_specs=[SCALARS]...  28.7 us
    ppermute x3, waiting for transfers between devices, last_hops(): return (own, one, mid, two, two, outer(after(two, one)))  28 us
    ppermute x6, waiting for transfers between devices, first_hops(): return (own, outer(own), across(own))  19.9 us
    pallas_call x1, Pallas kernels, lent_sides(): pl.pallas_call(lent_kernel, grid=(units // TILE,), in_specs=[SCALARS] + [...  18.2 us
    ppermute x6, starting transfers between devices, first_hops(): return (own, outer(own), across(own))  18.2 us
    unnamed x72, local copies, waits for them, and re-layouts  15.6 us
    ppermute x3, starting transfers between devices, last_hops(): return (own, one, mid, two, two, outer(after(two, one)))  5.81 us
    ppermute x1, waiting for transfers between devices, moving_plan(): in_out = own_in_out + outer(after(own_in_out, b_send))  5.43 us
  transfers between devices with their start and end apart: 31, of which 13 were waited for; matrix products, arithmetic and copies ran while one was open for 4% of the time, Pallas kernels for 31%

profile of v21, /device:TPU:0, one launch (start us, length us, event | category | flops | bytes accessed | tf_op | source)
XLA Modules:
  0.0 195.7 jit_solution(14359677021307673428)
XLA Ops:
  0.5 1.3 slice.40
  1.8 2.6 %collective-permute-start.1 = (bf16[128,3584]{1,0:T(8,128)(2,1)S(1)}, bf16[128,3584]{1,0:T(8,128)(2,1)S(1)}, u32[]{:S(2)}, u32[]{:S(2)}) collective-permute-start(bf16[128,3584]{1,0:T(8,128)(2,1)S(1)} %bitcast.46), channel_id=1, source_target_pairs={{0,2},{1,3},{2,0},{3,1},{4,6},{5,7},{6,4},{7,5},{8,10},{9,11},{10,... | collective-permute-start | bytes 2752520 | tf_op jit(solution)/shard_map/ppermute | solution.py:575
  4.4 2.6 %collective-permute-start = (bf16[128,2048]{1,0:T(8,128)(2,1)}, bf16[128,2048]{1,0:T(8,128)(2,1)}, u32[]{:S(2)}, u32[]{:S(2)}) collective-permute-start(bf16[128,2048]{1,0:T(8,128)(2,1)} %bitcast.4.q_outgrad.b0), channel_id=1, source_target_pairs={{0,8},{4,12},{8,0},{12,4},{1,9},{5,13},{9,1},{13,5},{2,10},{6,14},... | collective-permute-start | bytes 1572872 | tf_op jit(solution)/shard_map/ppermute | solution.py:558
  7.0 1.6 collective-permute-start.4
  8.6 1.5 copy-done.1
  10.1 1.2 copy-done.4
  11.3 1.2 copy-done.9
  12.5 1.2 copy-done.11
  13.7 1.2 copy-done.17
  14.9 1.0 copy-done.18
  15.9 1.0 copy-done.19
  18.8 4.9 %shard_map.154 = (f32[384,128]{1,0:T(8,128)S(1)}, f32[384,64]{1,0:T(8,128)S(1)}) custom-call(bf16[256,2048]{1,0:T(8,128)(2,1)S(1)} %bitcast.39, bf16[128,2048]{1,0:T(8,128)(2,1)S(1)} %bitcast.40, bf16[256,2048]{1,0:T(8,128)(2,1)S(1)} %bitcast.34, bf16[128,2048]{1,0:T(8,128)(2,1)} %bitcast.4.q_outgrad.b0, bf16[64,2048]{1,0:T(8,128)(2,1)S(1)} %copy-done.20, ...), custom_call_target="tpu_custom_call" | custom-call | flops 1024 | bytes 1024 | tf_op jit(solution)/shard_map/pallas_call | solution.py:396
  23.7 7.2 %collective-permute-done.b3.b4 = bf16[128,2048]{1,0:T(8,128)(2,1)} collective-permute-done((bf16[128,2048]{1,0:T(8,128)(2,1)}, bf16[128,2048]{1,0:T(8,128)(2,1)}, u32[]{:S(2)}, u32[]{:S(2)}) %collective-permute-start) | collective-permute-done | bytes 524320 | tf_op jit(solution)/shard_map/ppermute | solution.py:558
  31.0 1.9 collective-permute-start.6
  34.4 1.1 fusion.1
  35.6 10.1 %collective-permute-start.2 = (bf16[128,2048]{1,0:T(8,128)(2,1)}, bf16[128,2048]{1,0:T(8,128)(2,1)S(1)}, u32[]{:S(2)}, u32[]{:S(2)}) collective-permute-start(bf16[128,2048]{1,0:T(8,128)(2,1)} %bitcast.42), channel_id=1, source_target_pairs={{0,8},{4,12},{8,0},{12,4},{1,9},{5,13},{9,1},{13,5},{2,10},{6,14},... | collective-permute-start | bytes 1572872 | tf_op jit(solution)/shard_map/ppermute | solution.py:558
  45.7 11.6 %collective-permute-done.6.b5 = bf16[128,2048]{1,0:T(8,128)(2,1)} collective-permute-done((bf16[128,2048]{1,0:T(8,128)(2,1)}, bf16[128,2048]{1,0:T(8,128)(2,1)}, u32[]{:S(2)}, u32[]{:S(2)}) %collective-permute-start.6) | collective-permute-done | bytes 524320 | tf_op jit(solution)/shard_map/ppermute | solution.py:562
  57.2 1.5 select_bitcast_fusion.5
  59.6 6.3 %collective-permute-done.2.b3.b4 = bf16[128,2048]{1,0:T(8,128)(2,1)S(1)} collective-permute-done((bf16[128,2048]{1,0:T(8,128)(2,1)}, bf16[128,2048]{1,0:T(8,128)(2,1)S(1)}, u32[]{:S(2)}, u32[]{:S(2)}) %collective-permute-start.2) | collective-permute-done | bytes 524320 | tf_op jit(solution)/shard_map/ppermute | solution.py:558
  65.9 2.0 %collective-permute-done.10.b1 = bf16[128,2048]{1,0:T(8,128)(2,1)S(1)} collective-permute-done((bf16[128,2048]{1,0:T(8,128)(2,1)}, bf16[128,2048]{1,0:T(8,128)(2,1)S(1)}, u32[]{:S(2)}, u32[]{:S(2)}) %collective-permute-start.10) | collective-permute-done | bytes 524320 | tf_op jit(solution)/shard_map/ppermute | solution.py:558
  68.0 2.2 %collective-permute-start.11 = (bf16[128,2048]{1,0:T(8,128)(2,1)S(1)}, bf16[128,2048]{1,0:T(8,128)(2,1)S(1)}, u32[]{:S(2)}, u32[]{:S(2)}) collective-permute-start(bf16[128,2048]{1,0:T(8,128)(2,1)S(1)} %collective-permute-done.2.b3.b4), channel_id=1, source_target_pairs={{0,4},{4,0},{8,12},{12,8},{1,5},{5,1},{9,13},{13,9},{2,6},{6,2},{1... | collective-permute-start | bytes 1572872 | tf_op jit(solution)/shard_map/ppermute | solution.py:562
  70.2 2.2 %collective-permute-start.14 = (bf16[128,2048]{1,0:T(8,128)(2,1)}, bf16[128,2048]{1,0:T(8,128)(2,1)}, u32[]{:S(2)}, u32[]{:S(2)}) collective-permute-start(bf16[128,2048]{1,0:T(8,128)(2,1)} %bitcast.9.b0), channel_id=1, source_target_pairs={{0,4},{4,0},{8,12},{12,8},{1,5},{5,1},{9,13},{13,9},{2,6},{6,2},{1... | collective-permute-start | bytes 1572872 | tf_op jit(solution)/shard_map/ppermute | solution.py:558
  72.4 4.6 %shard_map.155 = (bf16[3584,256]{1,0:T(8,128)(2,1)S(1)}, bf16[3584,256]{1,0:T(8,128)(2,1)S(1)}) custom-call(bf16[256,3584]{1,0:T(8,128)(2,1)S(1)} %bitcast.29, bf16[256,3584]{1,0:T(8,128)(2,1)S(1)} %bitcast.32, bf16[128,3584]{1,0:T(8,128)(2,1)S(1)} %collective-permute-done.1.far_gate, bf16[128,3584]{1,0:T(8,128)(2,1)} %collective-permute-done.7.far_up), custom_call_target="tpu_custom_call" | custom-call | flops 1024 | bytes 1024 | tf_op jit(solution)/shard_map/pallas_call | solution.py:295
  77.1 5.9 %collective-permute-done.11.b5 = bf16[128,2048]{1,0:T(8,128)(2,1)S(1)} collective-permute-done((bf16[128,2048]{1,0:T(8,128)(2,1)S(1)}, bf16[128,2048]{1,0:T(8,128)(2,1)S(1)}, u32[]{:S(2)}, u32[]{:S(2)}) %collective-permute-start.11) | collective-permute-done | bytes 524320 | tf_op jit(solution)/shard_map/ppermute | solution.py:562
  83.0 1.6 collective-permute-start.3
  85.5 1.1 pad_maximum_fusion.1
  87.7 14.3 %shard_map.156 = (f32[3584,128]{1,0:T(8,128)}, bf16[3584,128]{1,0:T(8,128)(2,1)}) custom-call(s32[2]{0:T(128)} %pad_add_fusion.flags, bf16[128,2048]{1,0:T(8,128)(2,1)} %bitcast.4.q_outgrad.b0, bf16[128,2048]{1,0:T(8,128)(2,1)} %copy-done.28, bf16[128,2048]{1,0:T(8,128)(2,1)} %collective-permute-done.5.b2, bf16[128,2048]{1,0:T(8,128)(2,1)} %collective-permute-done.b3.b4, ...), custom_call_target="tpu_custom_call" | custom-call | flops 1024 | bytes 1024 | tf_op jit(solution)/shard_map/pallas_call | solution.py:241
  102.1 4.3 %collective-permute-done.3.b3.b4 = bf16[128,2048]{1,0:T(8,128)(2,1)S(1)} collective-permute-done((bf16[128,2048]{1,0:T(8,128)(2,1)}, bf16[128,2048]{1,0:T(8,128)(2,1)S(1)}, u32[]{:S(2)}, u32[]{:S(2)}) %collective-permute-start.3) | collective-permute-done | bytes 524320 | tf_op jit(solution)/shard_map/ppermute | solution.py:558
  106.4 1.7 collective-permute-start.15
  108.1 1.5 collective-permute-done.18.far
  110.2 10.5 %collective-permute-done.15.b5 = bf16[128,2048]{1,0:T(8,128)(2,1)S(1)} collective-permute-done((bf16[128,2048]{1,0:T(8,128)(2,1)S(1)}, bf16[128,2048]{1,0:T(8,128)(2,1)S(1)}, u32[]{:S(2)}, u32[]{:S(2)}) %collective-permute-start.15) | collective-permute-done | bytes 524320 | tf_op jit(solution)/shard_map/ppermute | solution.py:562
  121.6 1.1 pad_maximum_fusion.2
  122.7 1.2 collective-permute-start.21
  123.9 14.3 %shard_map.157 = (f32[3584,128]{1,0:T(8,128)}, bf16[3584,128]{1,0:T(8,128)(2,1)}) custom-call(s32[2]{0:T(128)} %pad_add_fusion.flags, bf16[128,2048]{1,0:T(8,128)(2,1)} %bitcast.43, bf16[128,2048]{1,0:T(8,128)(2,1)} %copy-done.29, bf16[128,2048]{1,0:T(8,128)(2,1)} %copy-done.31, bf16[128,2048]{1,0:T(8,128)(2,1)} %copy-done.26, bf16[128,2048]{1,0:T(8,128)(2,1)} %copy-done.26, ...), custom_call_target="tpu_custom_call" | custom-call | flops 1024 | bytes 1024 | tf_op jit(solution)/shard_map/pallas_call | solution.py:241
  138.3 1.5 copy-done.16
  139.8 2.4 %shard_map.158 = f32[128,128]{1,0:T(8,128)S(1)} custom-call(f32[3584,128]{1,0:T(8,128)S(1)} %copy-done.16, bf16[3584,128]{1,0:T(8,128)(2,1)} %collective-permute-done.19.returned, bf16[128,3584]{1,0:T(8,128)(2,1)S(1)} %bitcast.36, bf16[128,3584]{1,0:T(8,128)(2,1)S(1)} %bitcast.38, bf16[64,3584]{1,0:T(8,128)(2,1)S(1)} %copy-done.5, bf16[64,3584]{1,0:T(8,128)(2,1)S(1)} %copy-done.7), custom_call_target="tpu_custom_call" | custom-call | flops 1024 | bytes 1024 | tf_op jit(solution)/shard_map/pallas_call | solution.py:268
  143.4 1.8 collective-permute-start.20
  145.2 5.4 %collective-permute-done.16 = f32[384,128]{1,0:T(8,128)S(1)} collective-permute-done((f32[384,128]{1,0:T(8,128)S(1)}, f32[384,128]{1,0:T(8,128)S(1)}, u32[]{:S(2)}, u32[]{:S(2)}) %collective-permute-start.16) | collective-permute-done | bytes 196640 | tf_op jit(solution)/shard_map/ppermute | solution.py:602
  150.7 4.3 %collective-permute-start.17 = (f32[384,128]{1,0:T(8,128)S(1)}, f32[384,128]{1,0:T(8,128)S(1)}, u32[]{:S(2)}, u32[]{:S(2)}) collective-permute-start(f32[384,128]{1,0:T(8,128)S(1)} %add.32), channel_id=1, source_target_pairs={{0,8},{4,12},{8,0},{12,4},{1,9},{5,13},{9,1},{13,5},{2,10},{6,14},... | collective-permute-start | bytes 589832 | tf_op jit(solution)/shard_map/ppermute | solution.py:614
  155.1 2.8 %collective-permute-start.24 = (f32[128,192]{1,0:T(8,128)S(1)}, f32[128,192]{1,0:T(8,128)S(1)}, u32[]{:S(2)}, u32[]{:S(2)}) collective-permute-start(f32[128,192]{1,0:T(8,128)S(1)} %fusion), channel_id=1, source_target_pairs={{0,8},{4,12},{8,0},{12,4},{1,9},{5,13},{9,1},{13,5},{2,10},{6,14},... | collective-permute-start | bytes 294920 | tf_op jit(solution)/shard_map/ppermute | solution.py:615
  158.8 18.2 %shard_map.159 = (f32[128,128]{1,0:T(8,128)}, f32[128,128]{1,0:T(8,128)}) custom-call(s32[2]{0:T(128)} %pad_add_fusion.flags, bf16[128,2048]{1,0:T(8,128)(2,1)} %bitcast.9.b0, bf16[128,2048]{1,0:T(8,128)(2,1)} %collective-permute-done.14.b1, bf16[128,2048]{1,0:T(8,128)(2,1)} %copy-done.32, bf16[128,2048]{1,0:T(8,128)(2,1)} %copy-done.25, ...), custom_call_target="tpu_custom_call" | custom-call | flops 1024 | bytes 1024 | tf_op jit(solution)/shard_map/pallas_call | solution.py:337
  178.2 2.0 %collective-permute-start.23 = (f32[128,128]{1,0:T(8,128)}, f32[128,128]{1,0:T(8,128)S(1)}, u32[]{:S(2)}, u32[]{:S(2)}) collective-permute-start(f32[128,128]{1,0:T(8,128)} %get-tuple-element.70), channel_id=1, source_target_pairs={{0,2},{1,3},{2,0},{3,1},{4,6},{5,7},{6,4},{7,5},{8,10},{9,11},{10,... | collective-permute-start | bytes 196616 | tf_op jit(solution)/shard_map/ppermute | solution.py:613
  180.2 4.3 %collective-permute-done.23.far = f32[128,128]{1,0:T(8,128)S(1)} collective-permute-done((f32[128,128]{1,0:T(8,128)}, f32[128,128]{1,0:T(8,128)S(1)}, u32[]{:S(2)}, u32[]{:S(2)}) %collective-permute-start.23) | collective-permute-done | bytes 65568 | tf_op jit(solution)/shard_map/ppermute | solution.py:613
  184.6 1.5 copy-done.13
  186.1 1.6 shard_map.160.early
  187.7 1.4 shard_map.162
  189.6 1.1 collective-permute-start.29
  190.7 2.9 %collective-permute-start.28 = (f32[4,8]{1,0:T(4,128)S(1)}, f32[4,8]{1,0:T(4,128)S(1)}, u32[]{:S(2)}, u32[]{:S(2)}) collective-permute-start(f32[4,8]{1,0:T(4,128)S(1)} %shard_map.162), channel_id=1, source_target_pairs={{0,4},{4,0},{8,12},{12,8},{1,5},{5,1},{9,13},{13,9},{2,6},{6,2},{1... | collective-permute-start | bytes 392 | tf_op jit(solution)/shard_map/ppermute | solution.py:624
  (115 shorter events, 14.2 us)
Async XLA Ops:
  0.0 8.6 %copy-start = (bf16[4,64,3584]{2,1,0:T(8,128)(2,1)S(1)}, bf16[4,64,3584]{2,1,0:T(8,128)(2,1)}, u32[]{:S(2)}) copy-start(bf16[4,64,3584]{2,1,0:T(8,128)(2,1)} %param.17) | copy-start | bytes 5505028
  0.0 87.7 %collective-permute-start.12 = (bf16[3584,2048]{1,0:T(8,128)(2,1)}, bf16[3584,2048]{1,0:T(8,128)(2,1)}, u32[]{:S(2)}, u32[]{:S(2)}) collective-permute-start(bf16[3584,2048]{1,0:T(8,128)(2,1)} %weight_own.5), channel_id=1, source_target_pairs={{0,1},{1,0},{2,3},{3,2},{4,5},{5,4},{6,7},{7,6},{8,9},{9,8},{10,11... | collective-permute-start | bytes 44040200 | tf_op jit(solution)/shard_map/ppermute | solution.py:573
  1.8 32.0 %collective-permute-start.1 = (bf16[128,3584]{1,0:T(8,128)(2,1)S(1)}, bf16[128,3584]{1,0:T(8,128)(2,1)S(1)}, u32[]{:S(2)}, u32[]{:S(2)}) collective-permute-start(bf16[128,3584]{1,0:T(8,128)(2,1)S(1)} %bitcast.46), channel_id=1, source_target_pairs={{0,2},{1,3},{2,0},{3,1},{4,6},{5,7},{6,4},{7,5},{8,10},{9,11},{10,... | collective-permute-start | bytes 2752520 | tf_op jit(solution)/shard_map/ppermute | solution.py:575
  4.4 26.5 %collective-permute-start = (bf16[128,2048]{1,0:T(8,128)(2,1)}, bf16[128,2048]{1,0:T(8,128)(2,1)}, u32[]{:S(2)}, u32[]{:S(2)}) collective-permute-start(bf16[128,2048]{1,0:T(8,128)(2,1)} %bitcast.4.q_outgrad.b0), channel_id=1, source_target_pairs={{0,8},{4,12},{8,0},{12,4},{1,9},{5,13},{9,1},{13,5},{2,10},{6,14},... | collective-permute-start | bytes 1572872 | tf_op jit(solution)/shard_map/ppermute | solution.py:558
  7.0 24.0 %collective-permute-start.4 = (bf16[128,2048]{1,0:T(8,128)(2,1)}, bf16[128,2048]{1,0:T(8,128)(2,1)S(1)}, u32[]{:S(2)}, u32[]{:S(2)}) collective-permute-start(bf16[128,2048]{1,0:T(8,128)(2,1)} %bitcast.4.q_outgrad.b0), channel_id=1, source_target_pairs={{0,4},{4,0},{8,12},{12,8},{1,5},{5,1},{9,13},{13,9},{2,6},{6,2},{1... | collective-permute-start | bytes 1572872 | tf_op jit(solution)/shard_map/ppermute | solution.py:558
  31.0 4.6 %collective-permute-start.5 = (bf16[128,2048]{1,0:T(8,128)(2,1)}, bf16[128,2048]{1,0:T(8,128)(2,1)}, u32[]{:S(2)}, u32[]{:S(2)}) collective-permute-start(bf16[128,2048]{1,0:T(8,128)(2,1)} %bitcast.4.q_outgrad.b0), channel_id=1, source_target_pairs={{0,1},{1,0},{2,3},{3,2},{4,8},{5,9},{6,10},{7,11},{8,4},{9,5},{10,... | collective-permute-start | bytes 1572872 | tf_op jit(solution)/shard_map/ppermute | solution.py:561
  31.0 26.3 %collective-permute-start.6 = (bf16[128,2048]{1,0:T(8,128)(2,1)}, bf16[128,2048]{1,0:T(8,128)(2,1)}, u32[]{:S(2)}, u32[]{:S(2)}) collective-permute-start(bf16[128,2048]{1,0:T(8,128)(2,1)} %collective-permute-done.b3.b4), channel_id=1, source_target_pairs={{0,4},{4,0},{8,12},{12,8},{1,5},{5,1},{9,13},{13,9},{2,6},{6,2},{1... | collective-permute-start | bytes 1572872 | tf_op jit(solution)/shard_map/ppermute | solution.py:562
  33.8 25.1 %collective-permute-start.7 = (bf16[128,3584]{1,0:T(8,128)(2,1)}, bf16[128,3584]{1,0:T(8,128)(2,1)}, u32[]{:S(2)}, u32[]{:S(2)}) collective-permute-start(bf16[128,3584]{1,0:T(8,128)(2,1)} %bitcast.16), channel_id=1, source_target_pairs={{0,2},{1,3},{2,0},{3,1},{4,6},{5,7},{6,4},{7,5},{8,10},{9,11},{10,... | collective-permute-start | bytes 2752520 | tf_op jit(solution)/shard_map/ppermute | solution.py:583
  35.5 32.5 %collective-permute-start.10 = (bf16[128,2048]{1,0:T(8,128)(2,1)}, bf16[128,2048]{1,0:T(8,128)(2,1)S(1)}, u32[]{:S(2)}, u32[]{:S(2)}) collective-permute-start(bf16[128,2048]{1,0:T(8,128)(2,1)} %bitcast.41), channel_id=1, source_target_pairs={{0,4},{4,0},{8,12},{12,8},{1,5},{5,1},{9,13},{13,9},{2,6},{6,2},{1... | collective-permute-start | bytes 1572872 | tf_op jit(solution)/shard_map/ppermute | solution.py:558
  35.6 30.4 %collective-permute-start.2 = (bf16[128,2048]{1,0:T(8,128)(2,1)}, bf16[128,2048]{1,0:T(8,128)(2,1)S(1)}, u32[]{:S(2)}, u32[]{:S(2)}) collective-permute-start(bf16[128,2048]{1,0:T(8,128)(2,1)} %bitcast.42), channel_id=1, source_target_pairs={{0,8},{4,12},{8,0},{12,4},{1,9},{5,13},{9,1},{13,5},{2,10},{6,14},... | collective-permute-start | bytes 1572872 | tf_op jit(solution)/shard_map/ppermute | solution.py:558
  57.2 12.9 %copy-start.27 = (bf16[2,64,2048]{2,1,0:T(8,128)(2,1)S(1)}, bf16[2,64,2048]{2,1,0:T(8,128)(2,1)}, u32[]{:S(2)}) copy-start(bf16[2,64,2048]{2,1,0:T(8,128)(2,1)} %get-tuple-element.73) | copy-start | bytes 1572868
  58.8 13.6 %copy-start.2 = (bf16[4,64,3584]{2,1,0:T(8,128)(2,1)S(1)}, bf16[4,64,3584]{2,1,0:T(8,128)(2,1)}, u32[]{:S(2)}) copy-start(bf16[4,64,3584]{2,1,0:T(8,128)(2,1)} %param.18) | copy-start | bytes 5505028
  58.9 25.7 %collective-permute-start.8 = (bf16[2,128,2048]{2,1,0:T(8,128)(2,1)S(1)}, bf16[2,128,2048]{2,1,0:T(8,128)(2,1)S(1)}, u32[]{:S(2)}, u32[]{:S(2)}) collective-permute-start(bf16[2,128,2048]{2,1,0:T(8,128)(2,1)S(1)} %pad_maximum_fusion), channel_id=1, source_target_pairs={{0,2},{1,3},{2,0},{3,1},{4,6},{5,7},{6,4},{7,5},{8,10},{9,11},{10,... | collective-permute-start | bytes 3145736 | tf_op jit(solution)/shard_map/ppermute | solution.py:585
  65.9 18.7 %copy-start.26 = (bf16[128,2048]{1,0:T(8,128)(2,1)}, bf16[128,2048]{1,0:T(8,128)(2,1)S(1)}, u32[]{:S(2)}) copy-start(bf16[128,2048]{1,0:T(8,128)(2,1)S(1)} %collective-permute-done.2.b3.b4) | copy-start | bytes 1572868
  68.0 16.7 %copy-start.29 = (bf16[128,2048]{1,0:T(8,128)(2,1)}, bf16[128,2048]{1,0:T(8,128)(2,1)S(1)}, u32[]{:S(2)}) copy-start(bf16[128,2048]{1,0:T(8,128)(2,1)S(1)} %collective-permute-done.10.b1) | copy-start | bytes 1572868
  68.0 15.0 %collective-permute-start.11 = (bf16[128,2048]{1,0:T(8,128)(2,1)S(1)}, bf16[128,2048]{1,0:T(8,128)(2,1)S(1)}, u32[]{:S(2)}, u32[]{:S(2)}) collective-permute-start(bf16[128,2048]{1,0:T(8,128)(2,1)S(1)} %collective-permute-done.2.b3.b4), channel_id=1, source_target_pairs={{0,4},{4,0},{8,12},{12,8},{1,5},{5,1},{9,13},{13,9},{2,6},{6,2},{1... | collective-permute-start | bytes 1572872 | tf_op jit(solution)/shard_map/ppermute | solution.py:562
  70.2 14.5 %collective-permute-start.9 = (bf16[128,2048]{1,0:T(8,128)(2,1)S(1)}, bf16[128,2048]{1,0:T(8,128)(2,1)S(1)}, u32[]{:S(2)}, u32[]{:S(2)}) collective-permute-start(bf16[128,2048]{1,0:T(8,128)(2,1)S(1)} %bitcast.44), channel_id=1, source_target_pairs={{0,1},{1,0},{2,3},{3,2},{4,8},{5,9},{6,10},{7,11},{8,4},{9,5},{10,... | collective-permute-start | bytes 1572872 | tf_op jit(solution)/shard_map/ppermute | solution.py:561
  70.2 36.2 %collective-permute-start.14 = (bf16[128,2048]{1,0:T(8,128)(2,1)}, bf16[128,2048]{1,0:T(8,128)(2,1)}, u32[]{:S(2)}, u32[]{:S(2)}) collective-permute-start(bf16[128,2048]{1,0:T(8,128)(2,1)} %bitcast.9.b0), channel_id=1, source_target_pairs={{0,4},{4,0},{8,12},{12,8},{1,5},{5,1},{9,13},{13,9},{2,6},{6,2},{1... | collective-permute-start | bytes 1572872 | tf_op jit(solution)/shard_map/ppermute | solution.py:558
  77.0 7.8 %copy-start.14 = (bf16[3584,256]{1,0:T(8,128)(2,1)}, bf16[3584,256]{1,0:T(8,128)(2,1)S(1)}, u32[]{:S(2)}) copy-start(bf16[3584,256]{1,0:T(8,128)(2,1)S(1)} %get-tuple-element.50.gates) | copy-start | bytes 5505028
  77.0 7.8 %copy-start.15 = (bf16[3584,256]{1,0:T(8,128)(2,1)}, bf16[3584,256]{1,0:T(8,128)(2,1)S(1)}, u32[]{:S(2)}) copy-start(bf16[3584,256]{1,0:T(8,128)(2,1)S(1)} %get-tuple-element.65.ups) | copy-start | bytes 5505028
  83.0 23.4 %collective-permute-start.3 = (bf16[128,2048]{1,0:T(8,128)(2,1)}, bf16[128,2048]{1,0:T(8,128)(2,1)S(1)}, u32[]{:S(2)}, u32[]{:S(2)}) collective-permute-start(bf16[128,2048]{1,0:T(8,128)(2,1)} %bitcast.9.b0), channel_id=1, source_target_pairs={{0,8},{4,12},{8,0},{12,4},{1,9},{5,13},{9,1},{13,5},{2,10},{6,14},... | collective-permute-start | bytes 1572872 | tf_op jit(solution)/shard_map/ppermute | solution.py:558
  86.6 23.1 %collective-permute-start.18 = (bf16[2,128,2048]{2,1,0:T(8,128)(2,1)}, bf16[2,128,2048]{2,1,0:T(8,128)(2,1)}, u32[]{:S(2)}, u32[]{:S(2)}) collective-permute-start(bf16[2,128,2048]{2,1,0:T(8,128)(2,1)} %pad_maximum_fusion.1), channel_id=1, source_target_pairs={{0,2},{1,3},{2,0},{3,1},{4,6},{5,7},{6,4},{7,5},{8,10},{9,11},{10,... | collective-permute-start | bytes 3145736 | tf_op jit(solution)/shard_map/ppermute | solution.py:591
  106.4 14.5 %copy-start.25 = (bf16[128,2048]{1,0:T(8,128)(2,1)}, bf16[128,2048]{1,0:T(8,128)(2,1)S(1)}, u32[]{:S(2)}) copy-start(bf16[128,2048]{1,0:T(8,128)(2,1)S(1)} %collective-permute-done.3.b3.b4) | copy-start | bytes 1572868
  106.4 3.8 %collective-permute-start.13 = (bf16[128,2048]{1,0:T(8,128)(2,1)}, bf16[128,2048]{1,0:T(8,128)(2,1)S(1)}, u32[]{:S(2)}, u32[]{:S(2)}) collective-permute-start(bf16[128,2048]{1,0:T(8,128)(2,1)} %bitcast.9.b0), channel_id=1, source_target_pairs={{0,1},{1,0},{2,3},{3,2},{4,8},{5,9},{6,10},{7,11},{8,4},{9,5},{10,... | collective-permute-start | bytes 1572872 | tf_op jit(solution)/shard_map/ppermute | solution.py:561
  106.4 14.3 %collective-permute-start.15 = (bf16[128,2048]{1,0:T(8,128)(2,1)S(1)}, bf16[128,2048]{1,0:T(8,128)(2,1)S(1)}, u32[]{:S(2)}, u32[]{:S(2)}) collective-permute-start(bf16[128,2048]{1,0:T(8,128)(2,1)S(1)} %collective-permute-done.3.b3.b4), channel_id=1, source_target_pairs={{0,4},{4,0},{8,12},{12,8},{1,5},{5,1},{9,13},{13,9},{2,6},{6,2},{1... | collective-permute-start | bytes 1572872 | tf_op jit(solution)/shard_map/ppermute | solution.py:562
  109.7 28.6 %collective-permute-start.19 = (bf16[3584,128]{1,0:T(8,128)(2,1)}, bf16[3584,128]{1,0:T(8,128)(2,1)}, u32[]{:S(2)}, u32[]{:S(2)}) collective-permute-start(bf16[3584,128]{1,0:T(8,128)(2,1)} %get-tuple-element.59), channel_id=1, source_target_pairs={{0,2},{1,3},{2,0},{3,1},{4,6},{5,7},{6,4},{7,5},{8,10},{9,11},{10,... | collective-permute-start | bytes 2752520 | tf_op jit(solution)/shard_map/ppermute | solution.py:595
  110.2 10.7 %copy-start.32 = (bf16[128,2048]{1,0:T(8,128)(2,1)}, bf16[128,2048]{1,0:T(8,128)(2,1)S(1)}, u32[]{:S(2)}) copy-start(bf16[128,2048]{1,0:T(8,128)(2,1)S(1)} %collective-permute-done.13.b2) | copy-start | bytes 1572868
  122.7 15.6 %copy-start.5 = (bf16[64,3584]{1,0:T(8,128)(2,1)S(1)}, bf16[64,3584]{1,0:T(8,128)(2,1)}, u32[]{:S(2)}) copy-start(bf16[64,3584]{1,0:T(8,128)(2,1)} %proj_gate.5) | copy-start | bytes 1376260
  122.7 15.6 %copy-start.7 = (bf16[64,3584]{1,0:T(8,128)(2,1)S(1)}, bf16[64,3584]{1,0:T(8,128)(2,1)}, u32[]{:S(2)}) copy-start(bf16[64,3584]{1,0:T(8,128)(2,1)} %proj_up.5) | copy-start | bytes 1376260
  122.7 15.6 %copy-start.10 = (bf16[2,64,3584]{2,1,0:T(8,128)(2,1)S(1)}, bf16[2,64,3584]{2,1,0:T(8,128)(2,1)}, u32[]{:S(2)}) copy-start(bf16[2,64,3584]{2,1,0:T(8,128)(2,1)} %param.22) | copy-start | bytes 2752516
  122.7 15.6 %copy-start.12 = (bf16[2,64,3584]{2,1,0:T(8,128)(2,1)S(1)}, bf16[2,64,3584]{2,1,0:T(8,128)(2,1)}, u32[]{:S(2)}) copy-start(bf16[2,64,3584]{2,1,0:T(8,128)(2,1)} %param.23) | copy-start | bytes 2752516
  122.7 35.2 %collective-permute-start.21 = (bf16[2,128,2048]{2,1,0:T(8,128)(2,1)}, bf16[2,128,2048]{2,1,0:T(8,128)(2,1)S(1)}, u32[]{:S(2)}, u32[]{:S(2)}) collective-permute-start(bf16[2,128,2048]{2,1,0:T(8,128)(2,1)} %pad_maximum_fusion.2), channel_id=1, source_target_pairs={{0,2},{1,3},{2,0},{3,1},{4,6},{5,7},{6,4},{7,5},{8,10},{9,11},{10,... | collective-permute-start | bytes 3145736 | tf_op jit(solution)/shard_map/ppermute | solution.py:598
  142.2 42.4 %collective-permute-start.22 = (bf16[3584,128]{1,0:T(8,128)(2,1)}, bf16[3584,128]{1,0:T(8,128)(2,1)S(1)}, u32[]{:S(2)}, u32[]{:S(2)}) collective-permute-start(bf16[3584,128]{1,0:T(8,128)(2,1)} %get-tuple-element.69), channel_id=1, source_target_pairs={{0,2},{1,3},{2,0},{3,1},{4,6},{5,7},{6,4},{7,5},{8,10},{9,11},{10,... | collective-permute-start | bytes 2752520 | tf_op jit(solution)/shard_map/ppermute | solution.py:606
  143.1 7.5 %collective-permute-start.16 = (f32[384,128]{1,0:T(8,128)S(1)}, f32[384,128]{1,0:T(8,128)S(1)}, u32[]{:S(2)}, u32[]{:S(2)}) collective-permute-start(f32[384,128]{1,0:T(8,128)S(1)} %get-tuple-element.57), channel_id=1, source_target_pairs={{0,4},{4,0},{8,12},{12,8},{1,5},{5,1},{9,13},{13,9},{2,6},{6,2},{1... | collective-permute-start | bytes 589832 | tf_op jit(solution)/shard_map/ppermute | solution.py:602
  143.4 11.6 %collective-permute-start.20 = (f32[128,192]{1,0:T(8,128)S(1)}, f32[128,192]{1,0:T(8,128)S(1)}, u32[]{:S(2)}, u32[]{:S(2)}) collective-permute-start(f32[128,192]{1,0:T(8,128)S(1)} %pad_maximum_fusion.3), channel_id=1, source_target_pairs={{0,4},{4,0},{8,12},{12,8},{1,5},{5,1},{9,13},{13,9},{2,6},{6,2},{1... | collective-permute-start | bytes 294920 | tf_op jit(solution)/shard_map/ppermute | solution.py:608
  150.7 26.4 %collective-permute-start.17 = (f32[384,128]{1,0:T(8,128)S(1)}, f32[384,128]{1,0:T(8,128)S(1)}, u32[]{:S(2)}, u32[]{:S(2)}) collective-permute-start(f32[384,128]{1,0:T(8,128)S(1)} %add.32), channel_id=1, source_target_pairs={{0,8},{4,12},{8,0},{12,4},{1,9},{5,13},{9,1},{13,5},{2,10},{6,14},... | collective-permute-start | bytes 589832 | tf_op jit(solution)/shard_map/ppermute | solution.py:614
  155.1 22.0 %collective-permute-start.24 = (f32[128,192]{1,0:T(8,128)S(1)}, f32[128,192]{1,0:T(8,128)S(1)}, u32[]{:S(2)}, u32[]{:S(2)}) collective-permute-start(f32[128,192]{1,0:T(8,128)S(1)} %fusion), channel_id=1, source_target_pairs={{0,8},{4,12},{8,0},{12,4},{1,9},{5,13},{9,1},{13,5},{2,10},{6,14},... | collective-permute-start | bytes 294920 | tf_op jit(solution)/shard_map/ppermute | solution.py:615
  158.8 18.3 %copy-start.23 = (s32[2]{0:T(128)S(1)}, s32[2]{0:T(128)}, u32[]{:S(2)}) copy-start(s32[2]{0:T(128)} %lengths.2) | copy-start | bytes 28
  158.8 25.7 %copy-start.6 = (bf16[64,3584]{1,0:T(8,128)(2,1)S(1)}, bf16[64,3584]{1,0:T(8,128)(2,1)}, u32[]{:S(2)}) copy-start(bf16[64,3584]{1,0:T(8,128)(2,1)} %proj_gate.5) | copy-start | bytes 1376260
  158.8 25.7 %copy-start.8 = (bf16[64,3584]{1,0:T(8,128)(2,1)S(1)}, bf16[64,3584]{1,0:T(8,128)(2,1)}, u32[]{:S(2)}) copy-start(bf16[64,3584]{1,0:T(8,128)(2,1)} %proj_up.5) | copy-start | bytes 1376260
  177.1 7.5 %copy-start.3 = (bf16[4,64,3584]{2,1,0:T(8,128)(2,1)S(1)}, bf16[4,64,3584]{2,1,0:T(8,128)(2,1)}, u32[]{:S(2)}) copy-start(bf16[4,64,3584]{2,1,0:T(8,128)(2,1)} %param.18) | copy-start | bytes 5505028
  178.1 6.4 %collective-permute-start.26 = (f32[2,192,64]{2,1,0:T(8,128)S(1)}, f32[2,192,64]{2,1,0:T(8,128)S(1)}, u32[]{:S(2)}, u32[]{:S(2)}) collective-permute-start(f32[2,192,64]{2,1,0:T(8,128)S(1)} %shard_map.161.q0), channel_id=1, source_target_pairs={{0,2},{1,3},{2,0},{3,1},{4,6},{5,7},{6,4},{7,5},{8,10},{9,11},{10,... | collective-permute-start | bytes 294920 | tf_op jit(solution)/shard_map/ppermute | solution.py:617
  178.2 6.4 %collective-permute-start.23 = (f32[128,128]{1,0:T(8,128)}, f32[128,128]{1,0:T(8,128)S(1)}, u32[]{:S(2)}, u32[]{:S(2)}) collective-permute-start(f32[128,128]{1,0:T(8,128)} %get-tuple-element.70), channel_id=1, source_target_pairs={{0,2},{1,3},{2,0},{3,1},{4,6},{5,7},{6,4},{7,5},{8,10},{9,11},{10,... | collective-permute-start | bytes 196616 | tf_op jit(solution)/shard_map/ppermute | solution.py:613
  180.2 7.5 %collective-permute-start.25 = (f32[2,192,64]{2,1,0:T(8,128)S(1)}, f32[2,192,64]{2,1,0:T(8,128)S(1)}, u32[]{:S(2)}, u32[]{:S(2)}) collective-permute-start(f32[2,192,64]{2,1,0:T(8,128)S(1)} %shard_map.161.q0), channel_id=1, source_target_pairs={{0,1},{1,0},{2,3},{3,2},{4,5},{5,4},{6,7},{7,6},{8,9},{9,8},{10,11... | collective-permute-start | bytes 294920 | tf_op jit(solution)/shard_map/ppermute | solution.py:618
  184.5 3.2 %collective-permute-start.27 = (f32[2,192,64]{2,1,0:T(8,128)S(1)}, f32[2,192,64]{2,1,0:T(8,128)S(1)}, u32[]{:S(2)}, u32[]{:S(2)}) collective-permute-start(f32[2,192,64]{2,1,0:T(8,128)S(1)} %collective-permute-done.26.q2), channel_id=1, source_target_pairs={{0,1},{1,0},{2,3},{3,2},{4,5},{5,4},{6,7},{7,6},{8,9},{9,8},{10,11... | collective-permute-start | bytes 294920 | tf_op jit(solution)/shard_map/ppermute | solution.py:618
  189.1 5.4 %collective-permute-start.30 = (f32[4,8]{1,0:T(4,128)S(1)}, f32[4,8]{1,0:T(4,128)S(1)}, u32[]{:S(2)}, u32[]{:S(2)}) collective-permute-start(f32[4,8]{1,0:T(4,128)S(1)} %shard_map.162), channel_id=1, source_target_pairs={{0,12},{4,8},{8,4},{12,0},{1,13},{5,9},{9,5},{13,1},{2,14},{6,10},... | collective-permute-start | bytes 392 | tf_op jit(solution)/shard_map/ppermute | solution.py:624
  189.6 5.0 %collective-permute-start.29 = (f32[4,8]{1,0:T(4,128)S(1)}, f32[4,8]{1,0:T(4,128)S(1)}, u32[]{:S(2)}, u32[]{:S(2)}) collective-permute-start(f32[4,8]{1,0:T(4,128)S(1)} %shard_map.162), channel_id=1, source_target_pairs={{0,8},{4,12},{8,0},{12,4},{1,9},{5,13},{9,1},{13,5},{2,10},{6,14},... | collective-permute-start | bytes 392 | tf_op jit(solution)/shard_map/ppermute | solution.py:624
  190.7 4.4 %collective-permute-start.28 = (f32[4,8]{1,0:T(4,128)S(1)}, f32[4,8]{1,0:T(4,128)S(1)}, u32[]{:S(2)}, u32[]{:S(2)}) collective-permute-start(f32[4,8]{1,0:T(4,128)S(1)} %shard_map.162), channel_id=1, source_target_pairs={{0,4},{4,0},{8,12},{12,8},{1,5},{5,1},{9,13},{13,9},{2,6},{6,2},{1... | collective-permute-start | bytes 392 | tf_op jit(solution)/shard_map/ppermute | solution.py:624
  (19 other events, 27.4 us)
